TPU v7x, 32 devices: a whole 2x2x4 slice. The times are simulated.
32 devices in a mesh: dp: 16 (over z, x, core), mp: 2 (over y).
Axes of the slice: x: 2, y: 2, z: 4, core: 2. Of those that a mesh axis runs over, the one named last changes fastest.
Arguments:
- master: float32 [2, 256, 512], P('mp', 'dp'), may hold values from -4 to 4
- moment: float32 [2, 256, 512], P('mp', 'dp'), may hold values from -0.06 to 0.06
- variance: float32 [2, 256, 512], P('mp', 'dp'), may hold values from 3e-06 to 3e-05
- flat_slot: int32 [256], replicated, may hold values from 0 to 255, each once
- feedback: bfloat16 [16, 2, 16, 8192], P('dp', None, 'mp'), may hold values from -0.029907227 to 0.029907227
- activations: bfloat16 [2, 2048, 8192], P(None, ('dp', 'mp')), may hold values from -6 to 6
- output_grads: bfloat16 [2, 2048, 8192], P(None, ('dp', 'mp')), may hold values from -6 to 6
Outputs:
- master_out: float32 [2, 256, 512], P('mp', 'dp')
- moment_out: float32 [2, 256, 512], P('mp', 'dp')
- feedback_out: bfloat16 [16, 2, 16, 8192], P('dp', None, 'mp')
Inputs may be any that keep to these rules, and one draw needn't show every extreme that they name: `flat_slot`: every position of the flat buffer holds exactly one of the 256 segments.
All inputs are finite; a program needn't handle non-finite values. Where the computation divides by a largest or mean magnitude, that divisor is 1e-20 or more.
Results may differ from a plain program's by a relative error of at most 0.0036.
The roundings to bfloat16 on the way count: a program that leaves them out, or rounds other values in their place, can miss the bound.
Values may be sent and summed in bfloat16 or wider, within the bound.
No kernel may reach another device: no remote copies, remote signals or barrier semaphores. Data moves between devices by JAX's collectives and lax.ppermute only.
A program may use at most 64 MiB of HBM per device.

v0:
```python
import jax
import jax.numpy as jnp
from jax import lax
from jax.sharding import PartitionSpec as P

beta_one = 0.9
step_rate = 0.05
epsilon = 1e-08
down_scale = 28672.0 ** (-0.5)


def silu_slope(preact):
    sigmoid_value = jax.nn.sigmoid(preact)
    return sigmoid_value * (1.0 + preact * (1.0 - sigmoid_value))


def gradients(weights, inputs, cotangent, model_width):
    up_scale = model_width ** (-0.5)
    before = up_scale * jnp.dot(inputs, weights[0].T, preferred_element_type=jnp.float32)
    hidden = jax.nn.silu(before).astype(jnp.bfloat16)
    back_grad = down_scale * jnp.dot(cotangent, weights[1].T, preferred_element_type=jnp.float32)
    slope_grad = (back_grad * silu_slope(before)).astype(jnp.bfloat16)
    grad_up = up_scale * jnp.dot(slope_grad.T, inputs, preferred_element_type=jnp.float32)
    grad_down = down_scale * jnp.dot(hidden.T, cotangent, preferred_element_type=jnp.float32)
    return jnp.stack([grad_up, grad_down])


def per_device(master, moment, variance, flat_slot, feedback, activations, output_grads):
    total_rows = flat_slot.shape[0]
    hidden_rows = feedback.shape[2]
    model_width = feedback.shape[3]
    workers = lax.axis_size("dp")
    tensor_shape = (2, hidden_rows, model_width)
    segment_shape = (total_rows, master.shape[2])
    inverse = (
        jnp.zeros((total_rows,), jnp.int32)
        .at[flat_slot]
        .set(jnp.arange(total_rows, dtype=jnp.int32))
    )
    working_flat = lax.all_gather(master[0].astype(jnp.bfloat16), "dp", axis=0, tiled=True)
    moment_flat, variance_flat = (
        lax.all_gather(moment[0], "dp", axis=0, tiled=True),
        lax.all_gather(variance[0], "dp", axis=0, tiled=True),
    )
    working = working_flat[flat_slot].reshape(tensor_shape)
    moment_t = moment_flat[flat_slot].reshape(tensor_shape)
    denominator = jnp.sqrt(variance_flat[flat_slot].reshape(tensor_shape)) + epsilon
    group_inputs, group_grads = (
        lax.all_gather(activations, "mp", axis=1, tiled=True),
        lax.all_gather(output_grads, "mp", axis=1, tiled=True),
    )
    step_one = gradients(working, group_inputs[0], group_grads[0], model_width)
    local_moment = beta_one * moment_t + (1.0 - beta_one) * step_one
    local_weights = (working.astype(jnp.float32) - step_rate * local_moment / denominator).astype(
        jnp.bfloat16
    )
    step_two = gradients(local_weights, group_inputs[1], group_grads[1], model_width)
    shifted = local_moment + feedback[0].astype(jnp.float32)
    magnitude = jnp.mean(jnp.abs(shifted), axis=-1, keepdims=True) + 1e-06
    packed = magnitude * jnp.tanh(shifted / magnitude)
    new_error = (shifted - packed).astype(jnp.bfloat16)
    grad_flat = step_two.reshape(segment_shape)[inverse]
    moment_own, grad_own = (
        lax.psum_scatter(
            packed.reshape(segment_shape)[inverse], "dp", scatter_dimension=0, tiled=True
        ),
        lax.psum_scatter(grad_flat, "dp", scatter_dimension=0, tiled=True),
    )
    mean_moment = moment_own / workers
    mean_grad = grad_own / workers
    moment_new = beta_one * mean_moment + (1.0 - beta_one) * mean_grad
    owner_denominator = jnp.sqrt(variance[0]) + epsilon
    master_new = master[0] - step_rate * (mean_moment + moment_new) / owner_denominator
    return (master_new[None], moment_new[None], new_error[None])


def solution(mesh):
    in_specs = (
        P("mp", "dp", None),
        P("mp", "dp", None),
        P("mp", "dp", None),
        P(),
        P("dp", None, "mp", None),
        P(None, ("dp", "mp"), None),
        P(None, ("dp", "mp"), None),
    )
    out_specs = (P("mp", "dp", None), P("mp", "dp", None), P("dp", None, "mp", None))
    return jax.shard_map(
        per_device, mesh=mesh, in_specs=in_specs, out_specs=out_specs, check_vma=False
    )
```

profile of v0, /device:TPU:0, one launch (start us, length us, event | category | flops | bytes accessed | tf_op | source)
XLA Modules:
  0.0 265.7 jit_solution(10059967838207748717)
XLA Ops:
  7.2 0.0 copy-start.6
  7.2 0.0 copy-start.4
  7.2 0.0 all-gather.7.cloned.1.call-start
  7.2 0.7 all-gather.7.cloned.1.call-update
  7.9 0.0 all-gather.5.cloned.1.call-start
  8.0 0.7 all-gather.5.cloned.1.call-update
  8.7 0.0 reduce-scatter.5.cloned.1.call-start
  8.8 23.8 %all_gather.16 = bf16[256,512]{1,0:T(8,128)(2,1)S(1)} all-gather(bf16[16,512]{1,0:T(8,128)(2,1)S(1)} %bitcast_convert_fusion), channel_id=1, replica_groups=mesh['dp'=16,'mp'=2] {'dp'}, dimensions={0}, use_global_device_ids=true | all-gather | bytes 278528 | tf_op jit(solution)/shard_map/all_gather | solution.py:40
  32.6 1.2 gather_fusion.1
  33.7 0.1 reshape.89
  33.8 18.9 %all-gather.1 = f32[1,256,512]{2,1,0:T(8,128)S(1)} all-gather(f32[1,16,512]{2,1,0:T(8,128)S(1)} %copy-done.4), channel_id=3, replica_groups=mesh['dp'=16,'mp'=2] {'dp'}, dimensions={1}, use_global_device_ids=true | all-gather | bytes 557056 | tf_op jit(solution)/shard_map/all_gather | solution.py:43
  52.7 1.0 gather_fusion.3
  53.7 0.1 sqrt_add_fusion
  53.8 0.1 add.93
  54.0 20.2 %all-gather = f32[1,256,512]{2,1,0:T(8,128)S(1)} all-gather(f32[1,16,512]{2,1,0:T(8,128)S(1)} %copy-done.8), channel_id=2, replica_groups=mesh['dp'=16,'mp'=2] {'dp'}, dimensions={1}, use_global_device_ids=true | all-gather | bytes 557056 | tf_op jit(solution)/shard_map/all_gather | solution.py:42
  74.2 1.0 gather_fusion
  75.2 0.1 broadcast_multiply_fusion
  75.2 0.1 mul.144
  75.4 0.1 squeeze.40
  75.4 0.1 squeeze.38
  75.5 1.4 scatter_custom_fusion
  77.0 0.0 copy-start.1
  77.0 0.0 all-gather.7.cloned.1.call-done
  77.0 2.6 fusion.12
  79.6 47.9 %all-gather.5.cloned.1.call-done = bf16[2,128,8192]{2,1,0:T(8,128)(2,1)} async-done(((bf16[2,64,8192]{2,1,0:T(8,128)(2,1)}), bf16[2,128,8192]{2,1,0:T(8,128)(2,1)}) %all-gather.5.cloned.1.call-update) | async-done | bytes 4194320 | tf_op jit(solution)/shard_map/all_gather | solution.py:50
  127.5 2.0 convolution_multiply_fusion.2
  129.4 3.8 %convolution_multiply_fusion.3 = f32[8,8192]{1,0:T(8,128)S(1)} fusion(bf16[2,128,8192]{2,1,0:T(8,128)(2,1)} %all-gather.7.cloned.1.call-done, bf16[8,8192]{1,0:T(8,128)(2,1)S(1)} %squeeze.38, bf16[2,128,8192]{2,1,0:T(8,128)(2,1)} %all-gather.5.cloned.1.call-done, f32[128,8]{0,1:T(8,128)S(1)} %fusion.12), kind=kOutput, calls=%fused_computation.11 | convolution fusion | flops 33630208 | bytes 4591616 | tf_op jit(solution)/shard_map/dot_general | solution.py:23
  133.2 0.9 subtract_convert_fusion.1
  134.2 0.7 copy-done.3
  134.9 2.2 fusion.7
  137.1 0.4 fusion
  137.5 3.8 %fusion.1 = f32[1,8,8192]{2,1,0:T(8,128)S(1)} fusion(bf16[2,128,8192]{2,1,0:T(8,128)(2,1)} %all-gather.7.cloned.1.call-done, bf16[2,128,8192]{2,1,0:T(8,128)(2,1)} %all-gather.5.cloned.1.call-done, bf16[2,8,8192]{2,1,0:T(8,128)(2,1)} %copy-done.3, f32[128,8]{0,1:T(8,128)S(1)} %fusion.7), kind=kOutput, calls=%fused_computation.9 | convolution fusion | flops 33630208 | bytes 4591616 | tf_op jit(solution)/shard_map/dot_general | solution.py:23
  141.4 0.1 reshape.86
  141.5 1.8 gather_fusion.4
  143.2 0.0 reduce-scatter.5.cloned.1.call-update
  143.3 0.0 reduce-scatter.3.cloned.1.call-start
  143.3 0.1 reshape.88
  143.4 0.9 mul.179
  144.4 0.1 mul.157
  144.5 0.1 mul.158
  144.6 1.1 mul.159
  145.7 0.3 tanh_multiply_fusion
  146.0 1.8 gather_fusion.2
  147.8 0.0 reduce-scatter.3.cloned.1.call-update
  147.8 0.9 subtract_convert_fusion
  148.7 50.4 %reduce-scatter.5.cloned.1.call-done = f32[16,512]{1,0:T(8,128)} async-done(((f32[256,512]{1,0:T(8,128)}), f32[16,512]{1,0:T(8,128)}) %reduce-scatter.5.cloned.1.call-update) | async-done | bytes 32784 | tf_op jit(solution)/shard_map/reduce_scatter | solution.py:67
  199.1 58.7 %reduce-scatter.3.cloned.1.call-done = f32[16,512]{1,0:T(8,128)} async-done(((f32[256,512]{1,0:T(8,128)}), f32[16,512]{1,0:T(8,128)}) %reduce-scatter.3.cloned.1.call-update) | async-done | bytes 32784 | tf_op jit(solution)/shard_map/reduce_scatter | solution.py:64
  257.8 1.4 fusion.24
  (25 shorter events, 0.1 us)
Async XLA Ops:
  7.2 1.6 copy-start.9
  7.2 1.6 copy-start.6
  7.2 26.7 %copy-start.4 = (f32[1,16,512]{2,1,0:T(8,128)S(1)}, f32[1,16,512]{2,1,0:T(8,128)}, u32[]{:S(2)}) copy-start(f32[1,16,512]{2,1,0:T(8,128)} %param.9) | copy-start | bytes 98308
  7.2 69.8 %all-gather.7.cloned.1.call-start = ((), (), s32[]{:S(2)}) async-start(), calls=%async_computation.3 | async-start | bytes 6291456 | tf_op jit(solution)/shard_map/all_gather | solution.py:49
  7.9 119.5 %all-gather.5.cloned.1.call-start = ((), (), s32[]{:S(2)}) async-start(), calls=%async_computation.2 | async-start | bytes 6291456 | tf_op jit(solution)/shard_map/all_gather | solution.py:50
  8.7 190.4 %reduce-scatter.5.cloned.1.call-start = ((), (), s32[]{:S(2)}) async-start(), calls=%async_computation.5 | async-start | bytes 557056 | tf_op jit(solution)/shard_map/reduce_scatter | solution.py:67
  33.7 20.2 %copy-start.8 = (f32[1,16,512]{2,1,0:T(8,128)S(1)}, f32[1,16,512]{2,1,0:T(8,128)}, u32[]{:S(2)}) copy-start(f32[1,16,512]{2,1,0:T(8,128)} %param.8) | copy-start | bytes 98308
  77.0 56.3 %copy-start.1 = (bf16[1,2,8,8192]{3,2,1,0:T(8,128)(2,1)S(1)}, bf16[1,2,8,8192]{3,2,1,0:T(8,128)(2,1)}, u32[]{:S(2)}) copy-start(bf16[1,2,8,8192]{3,2,1,0:T(8,128)(2,1)} %param.11) | copy-start | bytes 786436
  133.2 3.9 %copy-start = (bf16[2,128,8192]{2,1,0:T(8,128)(2,1)S(1)}, bf16[2,128,8192]{2,1,0:T(8,128)(2,1)}, u32[]{:S(2)}) copy-start(bf16[2,128,8192]{2,1,0:T(8,128)(2,1)} %all-gather.5.cloned.1.call-done) | copy-start | bytes 12582916
  134.2 0.7 copy-start.3
  143.3 114.5 %reduce-scatter.3.cloned.1.call-start = ((), (), s32[]{:S(2)}) async-start(), calls=%async_computation.4 | async-start | bytes 557056 | tf_op jit(solution)/shard_map/reduce_scatter | solution.py:64
  145.7 112.1 %copy-start.5 = (f32[1,16,512]{2,1,0:T(8,128)S(1)}, f32[1,16,512]{2,1,0:T(8,128)}, u32[]{:S(2)}) copy-start(f32[1,16,512]{2,1,0:T(8,128)} %param.9) | copy-start | bytes 98308
  145.7 112.0 %copy-start.7 = (f32[1,16,512]{2,1,0:T(8,128)S(1)}, f32[1,16,512]{2,1,0:T(8,128)}, u32[]{:S(2)}) copy-start(f32[1,16,512]{2,1,0:T(8,128)} %param.7) | copy-start | bytes 98308
  146.0 1.8 copy-start.2
Sparse Core Ops, SparseCore 0:
  9.6 59.4 all-gather.6
  70.6 56.8 all-gather.4
  143.4 55.6 reduce-scatter.4
  202.9 54.7 reduce-scatter.2
where the time goes:
time: 266 us
  waiting for transfers between devices  158 us (59%)
  blocking collectives  62.9 us (24%)
  matrix products  14.8 us (6%)
  between operations  14 us (5%)
  local copies, waits for them, and re-layouts  11.7 us (4%)
  other arithmetic  3.75 us (1%)
    reduce_scatter x1, waiting for transfers between devices, per_device(): lax.psum_scatter(packed.reshape(segment_shape)[inverse], 'dp', scatter_di...  58.7 us
    reduce_scatter x1, waiting for transfers between devices, per_device(): lax.psum_scatter(grad_flat, 'dp', scatter_dimension=0, tiled=True)  50.4 us
    all_gather x1, waiting for transfers between devices, per_device(): lax.all_gather(output_grads, 'mp', axis=1, tiled=True)  47.9 us
    all_gather x1, blocking collectives, per_device(): lax.all_gather(master[0].astype(jnp.bfloat16), 'dp', axis=0, tiled=True)  23.8 us
    all_gather x1, blocking collectives, per_device(): lax.all_gather(moment[0], 'dp', axis=0, tiled=True)  20.2 us
    all_gather x1, blocking collectives, per_device(): lax.all_gather(variance[0], 'dp', axis=0, tiled=True)  18.9 us
    dot_general x2, matrix products, gradients(): jnp.dot(slope_grad.T, inputs, preferred_element_type=jnp.float32)  7.61 us
  transfers between devices with their start and end apart: 4, of which 3 were waited for; matrix products, arithmetic and copies ran while one was open for 5% of the time, Pallas kernels for 0%

commit v1 on v0

v1 whole, which is shorter than its diff:
```python
import functools

import jax
import jax.numpy as jnp
from jax import lax
from jax.experimental import pallas as pl
from jax.experimental.pallas import tpu as pltpu
from jax.sharding import PartitionSpec as P

beta_one = 0.9
step_rate = 0.05
epsilon = 1e-08
down_scale = 28672.0 ** (-0.5)
BF = jnp.bfloat16
F32 = jnp.float32
NT = (((1,), (1,)), ((), ()))
NN = (((1,), (0,)), ((), ()))


def dot(a, b, dims=NN):
    return lax.dot_general(a, b, dims, preferred_element_type=F32)


def swap(x, axis, mask):
    n = lax.axis_size(axis)
    return lax.ppermute(x, axis, [(i, i ^ mask) for i in range(n)])


def bits_of(n, lowest=1):
    masks = []
    mask = n // 2
    while mask >= lowest:
        masks.append(mask)
        mask //= 2
    return masks


def gradient_rows(weights, x_ref, g_ref, hidden_rows, up_scale):
    before = up_scale * dot(weights, x_ref[...], NT)[:hidden_rows]
    back = down_scale * dot(weights, g_ref[...], NT)[hidden_rows:]
    sigmoid = jax.nn.sigmoid(before)
    hidden = before * sigmoid
    slope = back * (sigmoid * (1.0 + before * (1.0 - sigmoid)))
    zeros = jnp.zeros_like(slope)
    left_up = jnp.concatenate([slope, zeros], axis=0).astype(BF)
    left_down = jnp.concatenate([zeros, hidden], axis=0).astype(BF)

    def columns(at):
        return up_scale * dot(left_up, x_ref[:, at]) + down_scale * dot(left_down, g_ref[:, at])

    return columns


def first_kernel(hidden_rows, up_scale, chunk, place_ref, w0_ref, w1_ref, x_ref, g_ref, weights_ref, part_ref):
    rows = 2 * hidden_rows
    segment = w0_ref.shape[1]
    half = w0_ref.shape[0]
    width = x_ref.shape[1]
    ordered = dot(place_ref[:, :half], w0_ref[...]) + dot(place_ref[:, half:], w1_ref[...])
    for c in range(width // segment):
        weights_ref[:, c * segment : (c + 1) * segment] = ordered[c * rows : (c + 1) * rows].astype(BF)
    columns = gradient_rows(weights_ref[...], x_ref, g_ref, hidden_rows, up_scale)
    for c in range(width // chunk):
        at = slice(c * chunk, (c + 1) * chunk)
        part_ref[:, at] = columns(at).astype(BF)


def moments_kernel(rows, place_ref, a0_ref, a1_ref, moment_ref, rate_ref):
    half = a0_ref.shape[0]
    segment = a0_ref.shape[1] // 2
    width = moment_ref.shape[1]
    ordered = dot(place_ref[:, :half], a0_ref[...]) + dot(place_ref[:, half:], a1_ref[...])
    rate = step_rate / (jnp.sqrt(ordered[:, segment:]) + epsilon)
    for c in range(width // segment):
        at = slice(c * segment, (c + 1) * segment)
        moment_ref[:, at] = ordered[c * rows : (c + 1) * rows, :segment]
        rate_ref[:, at] = rate[c * rows : (c + 1) * rows]


def second_kernel(
    hidden_rows, up_scale, own, back_ref, part_ref, got_ref, weights_ref, moment_ref, rate_ref, x_ref, g_ref, *rest
):
    if own:
        feedback_ref, grad_ref, packed_ref, error_ref, local_ref, seg_ref = rest
    else:
        grad_ref, local_ref, seg_ref = rest
    rows = 2 * hidden_rows
    segment = grad_ref.shape[1]
    width = x_ref.shape[1]
    step_one = part_ref[...].astype(F32) + got_ref[...].astype(F32)
    local_moment = beta_one * moment_ref[...] + (1.0 - beta_one) * step_one
    local_ref[...] = (weights_ref[...].astype(F32) - local_moment * rate_ref[...]).astype(BF)
    columns = gradient_rows(local_ref[...], x_ref, g_ref, hidden_rows, up_scale)
    for c in range(width // segment):
        seg_ref[c * rows : (c + 1) * rows] = columns(slice(c * segment, (c + 1) * segment)).astype(BF)
    grad_ref[...] = dot(back_ref[...], seg_ref[...]).astype(BF)
    if own:
        shifted = local_moment + feedback_ref[...].astype(F32)
        magnitude = jnp.sum(jnp.abs(shifted), axis=1, keepdims=True) * (1.0 / width) + 1e-06
        packed = magnitude * jnp.tanh(shifted / magnitude)
        error_ref[...] = (shifted - packed).astype(BF)
        for c in range(width // segment):
            seg_ref[c * rows : (c + 1) * rows] = packed[:, c * segment : (c + 1) * segment].astype(BF)
        packed_ref[...] = dot(back_ref[...], seg_ref[...]).astype(BF)


def call(kernel, out_shape, operands, scratch=()):
    return pl.pallas_call(
        kernel,
        out_shape=out_shape,
        in_specs=[pl.BlockSpec(memory_space=pltpu.VMEM)] * len(operands),
        out_specs=jax.tree.map(lambda _: pl.BlockSpec(memory_space=pltpu.VMEM), out_shape),
        scratch_shapes=list(scratch),
        compiler_params=pltpu.CompilerParams(vmem_limit_bytes=32 * 1024 * 1024),
    )(*operands)


def per_device(master, moment, variance, flat_slot, feedback, activations, output_grads):
    n_dp, n_mp = lax.axis_size("dp"), lax.axis_size("mp")
    me = lax.axis_index("dp")
    span, segment = master.shape[1:]
    segments = flat_slot.shape[0]
    hidden_rows, width = feedback.shape[2:]
    rows = 2 * hidden_rows
    up_scale = width ** (-0.5)
    far = bits_of(n_dp, 2)
    mp_bits = bits_of(n_mp)
    shape = jax.ShapeDtypeStruct

    near_w = master[0].astype(BF)
    near_a = jnp.concatenate([moment[0].astype(BF), variance[0].astype(BF)], axis=1)
    for mask in far:
        got_w = swap(near_w, "dp", mask)
        got_a = swap(near_a, "dp", mask)
        near_w = jnp.concatenate([near_w, got_w], axis=0)
        near_a = jnp.concatenate([near_a, got_a], axis=0)

    owner = (flat_slot // span) ^ me
    position = jnp.zeros_like(owner)
    for place, mask in enumerate(far + [1]):
        position = position + jnp.where((owner & mask) != 0, 1 << place, 0)
    position = position * span + flat_slot % span
    position = position.reshape(rows, width // segment).T.reshape(segments)
    line = jnp.arange(segments, dtype=jnp.int32)
    place_map = (position[:, None] == line[None, :]).astype(BF)
    back_map = (line[:, None] == position[None, :]).astype(BF)

    blocks_w, blocks_a = [near_w], [near_a]
    for mask in reversed(mp_bits):
        blocks_w = blocks_w + [swap(b, "mp", mask) for b in blocks_w]
        blocks_a = blocks_a + [swap(b, "mp", mask) for b in blocks_a]
    pairs_w = [(b, swap(b, "dp", 1)) for b in blocks_w]
    pairs_a = [(b, swap(b, "dp", 1)) for b in blocks_a]

    x_one, x_two = activations[0], activations[1]
    g_one, g_two = output_grads[0], output_grads[1]
    tensor = (rows, width)
    flat = (segments, segment)
    weights, parts = [], []
    for w0, w1 in pairs_w:
        kernel = functools.partial(first_kernel, hidden_rows, up_scale, min(width, 1024))
        w_t, part = call(kernel, (shape(tensor, BF), shape(tensor, BF)), (place_map, w0, w1, x_one, g_one))
        weights.append(w_t)
        parts.append(part)
    moments, rates = [], []
    for a0, a1 in pairs_a:
        kernel = functools.partial(moments_kernel, rows)
        m_t, rate = call(kernel, (shape(tensor, F32), shape(tensor, F32)), (place_map, a0, a1))
        moments.append(m_t)
        rates.append(rate)

    for step, mask in enumerate(mp_bits):
        sent = [swap(part, "mp", mask) for part in parts]
        got = [sent[k ^ mask] for k in range(n_mp)]
        if step < len(mp_bits) - 1:
            parts = [(p.astype(F32) + q.astype(F32)).astype(BF) for p, q in zip(parts, got)]

    grads = [None] * n_mp
    for k in reversed(range(n_mp)):
        own = k == 0
        operands = [back_map, parts[k], got[k], weights[k], moments[k], rates[k], x_two, g_two]
        out = [shape(flat, BF)]
        if own:
            operands.append(feedback[0].reshape(tensor))
            out += [shape(flat, BF), shape(tensor, BF)]
        result = call(
            functools.partial(second_kernel, hidden_rows, up_scale, own),
            tuple(out),
            operands,
            [pltpu.VMEM(tensor, BF), pltpu.VMEM(flat, BF)],
        )
        grads[k] = result[0]
        if own:
            packed, error = result[1], result[2]

    for mask in mp_bits:
        kept = [k for k in range(len(grads)) if not k & mask]
        got = {k: swap(grads[k ^ mask], "mp", mask) for k in kept}
        grads = [(grads[k].astype(F32) + got[k].astype(F32)).astype(BF) for k in kept]
    both = jnp.concatenate([grads[0], packed], axis=1)
    last = None
    for mask in [1] + far[::-1]:
        count = both.shape[0] // 2
        got = swap(both[count:], "dp", mask)
        last = both[:count].astype(F32) + got.astype(F32)
        both = last.astype(BF)
    mean_grad = last[:, :segment] / n_dp
    mean_moment = last[:, segment:] / n_dp
    moment_new = beta_one * mean_moment + (1.0 - beta_one) * mean_grad
    denominator = jnp.sqrt(variance[0]) + epsilon
    master_new = master[0] - step_rate * (mean_moment + moment_new) / denominator
    return (master_new[None], moment_new[None], error.reshape(feedback.shape))


def solution(mesh):
    in_specs = (
        P("mp", "dp", None),
        P("mp", "dp", None),
        P("mp", "dp", None),
        P(),
        P("dp", None, "mp", None),
        P(None, ("dp", "mp"), None),
        P(None, ("dp", "mp"), None),
    )
    out_specs = (P("mp", "dp", None), P("mp", "dp", None), P("dp", None, "mp", None))
    return jax.shard_map(
        per_device, mesh=mesh, in_specs=in_specs, out_specs=out_specs, check_vma=False
    )
```

time: 266 us -> 66.9 us (0.25)
  waiting for transfers between devices: 158 us -> 31 us
  blocking collectives: 62.9 us -> 0 us
  starting transfers between devices: 0.16 us -> 20.9 us
  matrix products: 14.8 us -> 0 us
  between operations: 14 us -> 0.83 us
  local copies, waits for them, and re-layouts: 11.7 us -> 3.75 us
  Pallas kernels: 0 us -> 6.66 us
    reduce_scatter x2 -> x0, waiting for transfers between devices: 109 us -> none  [the longest x1 58.7 us: per_device(): lax.psum_scatter(packed.reshape(segment_shape)[inverse], 'dp', scatter_di...]
    all_gather x3 -> x0, blocking collectives: 62.9 us -> none  [the longest x1 23.8 us: per_device(): lax.all_gather(master[0].astype(jnp.bfloat16), 'dp', axis=0, tiled=True)]
    all_gather x2 -> x0, waiting for transfers between devices: 47.9 us -> none  [the longest x1 47.9 us: per_device(): lax.all_gather(output_grads, 'mp', axis=1, tiled=True)]
    ppermute x0 -> x19, waiting for transfers between devices: none -> 31 us  [swap(): return lax.ppermute(x, axis, [(i, i ^ mask) for i in range(n)])]
    ppermute x0 -> x19, starting transfers between devices: none -> 20.9 us  [swap(): return lax.ppermute(x, axis, [(i, i ^ mask) for i in range(n)])]
    dot_general x6 -> x0, matrix products: 14.8 us -> none  [the longest x2 7.61 us: gradients(): jnp.dot(slope_grad.T, inputs, preferred_element_type=jnp.float32)]
    pallas_call x0 -> x6, Pallas kernels: none -> 6.66 us  [call(): pl.pallas_call(kernel, out_shape=out_shape, in_specs=[pl.BlockSpec(memory...]
    gather x5 -> x0, local copies, waits for them, and re-layouts: 6.61 us -> none  [the longest x1 1.77 us: per_device(): packed.reshape(segment_shape)[inverse]]
  transfers between devices with their start and end apart: 4 -> 19, of which waited for: 3 -> 13; matrix products, arithmetic and copies ran while one was open for 5% -> 8% of each run, Pallas kernels for 0% -> 10%
where the time goes in v1:
time: 66.9 us; the launch traced here: 66.6 us
  waiting for transfers between devices  31 us (46%)
  starting transfers between devices  20.9 us (31%)
  Pallas kernels  6.66 us (10%)
  local copies, waits for them, and re-layouts  3.75 us (6%)
  other arithmetic  3.49 us (5%)
  between operations  0.83 us (1%)
    ppermute x19, waiting for transfers between devices, swap(): return lax.ppermute(x, axis, [(i, i ^ mask) for i in range(n)])  31 us
    ppermute x19, starting transfers between devices, swap(): return lax.ppermute(x, axis, [(i, i ^ mask) for i in range(n)])  20.9 us
    pallas_call x6, Pallas kernels, call(): pl.pallas_call(kernel, out_shape=out_shape, in_specs=[pl.BlockSpec(memory...  6.66 us
    squeeze x1, local copies, waits for them, and re-layouts, per_device(): g_one, g_two = (output_grads[0], output_grads[1])  3.48 us
  transfers between devices with their start and end apart: 19, of which 13 were waited for; matrix products, arithmetic and copies ran while one was open for 8% of the time, Pallas kernels for 10%

profile of v1, /device:TPU:0, one launch (start us, length us, event | category | flops | bytes accessed | tf_op | source)
XLA Modules:
  0.0 66.6 jit_solution(11820624482929177847)
XLA Ops:
  0.6 0.8 %bitcast_convert_fusion = bf16[16,512]{1,0:T(8,128)(2,1)S(1)} fusion(f32[1,16,512]{2,1,0:T(8,128)} %param.7), kind=kLoop, calls=%fused_computation.29 | loop fusion | flops 8192 | bytes 49152 | tf_op jit(solution)/shard_map/convert_element_type | solution.py:130
  1.4 4.0 %collective-permute-start = (bf16[16,512]{1,0:T(8,128)(2,1)S(1)}, bf16[16,512]{1,0:T(8,128)(2,1)S(1)}, u32[]{:S(2)}, u32[]{:S(2)}) collective-permute-start(bf16[16,512]{1,0:T(8,128)(2,1)S(1)} %bitcast_convert_fusion), channel_id=1, source_target_pairs={{0,16},{2,18},{4,20},{6,22},{8,24},{10,26},{12,28},{14,30},{16,0},... | collective-permute-start | bytes 49160 | tf_op jit(solution)/shard_map/ppermute | solution.py:26
  5.4 0.8 %convert_bitcast_fusion = (bf16[16,512]{1,0:T(8,128)(2,1)S(1)}, bf16[16,512]{1,0:T(8,128)(2,1)S(1)}) fusion(f32[1,16,512]{2,1,0:T(8,128)} %param.9, f32[1,16,512]{2,1,0:T(8,128)} %param.8), kind=kLoop, calls=%fused_computation.30 | loop fusion | flops 16384 | bytes 98304 | tf_op jit(solution)/shard_map/convert_element_type | solution.py:131
  6.2 0.1 collective-permute-start.7
  6.3 3.5 %slice_bitcast_fusion = (bf16[64,8192]{1,0:T(8,128)(2,1)S(1)}, bf16[64,8192]{1,0:T(8,128)(2,1)S(1)}, bf16[64,8192]{1,0:T(8,128)(2,1)S(1)}, bf16[64,8192]{1,0:T(8,128)(2,1)}) fusion(bf16[2,64,8192]{2,1,0:T(8,128)(2,1)} %param.13, bf16[2,64,8192]{2,1,0:T(8,128)(2,1)} %param.12), kind=kLoop, calls=%fused_computation | loop fusion | bytes 8388608 | tf_op jit(solution)/shard_map/squeeze | solution.py:156
  9.8 1.3 %collective-permute-done.7 = bf16[16,1024]{1,0:T(8,128)(2,1)S(1)} collective-permute-done((bf16[16,1024]{1,0:T(8,128)(2,1)S(1)}, bf16[16,1024]{1,0:T(8,128)(2,1)S(1)}, u32[]{:S(2)}, u32[]{:S(2)}) %collective-permute-start.7) | collective-permute-done | bytes 32800 | tf_op jit(solution)/shard_map/ppermute | solution.py:26
  11.1 1.6 %collective-permute-start.8 = (bf16[32,1024]{1,0:T(8,128)(2,1)S(1)}, bf16[32,1024]{1,0:T(8,128)(2,1)S(1)}, u32[]{:S(2)}, u32[]{:S(2)}) collective-permute-start(bf16[32,1024]{1,0:T(8,128)(2,1)S(1)} %pad_maximum_fusion.5), channel_id=1, source_target_pairs={{0,8},{2,10},{4,12},{6,14},{8,0},{10,2},{12,4},{14,6},{16,24},{18,... | collective-permute-start | bytes 196616 | tf_op jit(solution)/shard_map/ppermute | solution.py:26
  12.7 0.5 collective-permute-start.1
  13.1 2.2 %collective-permute-done.8 = bf16[32,1024]{1,0:T(8,128)(2,1)S(1)} collective-permute-done((bf16[32,1024]{1,0:T(8,128)(2,1)S(1)}, bf16[32,1024]{1,0:T(8,128)(2,1)S(1)}, u32[]{:S(2)}, u32[]{:S(2)}) %collective-permute-start.8) | collective-permute-done | bytes 65568 | tf_op jit(solution)/shard_map/ppermute | solution.py:26
  15.4 1.6 %collective-permute-start.9 = (bf16[64,1024]{1,0:T(8,128)(2,1)S(1)}, bf16[64,1024]{1,0:T(8,128)(2,1)}, u32[]{:S(2)}, u32[]{:S(2)}) collective-permute-start(bf16[64,1024]{1,0:T(8,128)(2,1)S(1)} %pad_maximum_fusion.3), channel_id=1, source_target_pairs={{0,4},{2,6},{4,0},{6,2},{8,12},{10,14},{12,8},{14,10},{16,20},{18,... | collective-permute-start | bytes 393224 | tf_op jit(solution)/shard_map/ppermute | solution.py:26
  17.0 0.1 reshape.19
  17.1 0.1 copy.10
  17.1 0.1 eq.31
  17.2 0.9 %collective-permute-start.2 = (bf16[64,512]{1,0:T(8,128)(2,1)S(1)}, bf16[64,512]{1,0:T(8,128)(2,1)S(1)}, u32[]{:S(2)}, u32[]{:S(2)}) collective-permute-start(bf16[64,512]{1,0:T(8,128)(2,1)S(1)} %pad_maximum_fusion.4), channel_id=1, source_target_pairs={{0,4},{2,6},{4,0},{6,2},{8,12},{10,14},{12,8},{14,10},{16,20},{18,... | collective-permute-start | bytes 196616 | tf_op jit(solution)/shard_map/ppermute | solution.py:26
  18.1 2.4 %collective-permute-done.9 = bf16[64,1024]{1,0:T(8,128)(2,1)} collective-permute-done((bf16[64,1024]{1,0:T(8,128)(2,1)S(1)}, bf16[64,1024]{1,0:T(8,128)(2,1)}, u32[]{:S(2)}, u32[]{:S(2)}) %collective-permute-start.9) | collective-permute-done | bytes 131104 | tf_op jit(solution)/shard_map/ppermute | solution.py:26
  20.5 0.9 %pad_maximum_fusion.1.a0_ref = bf16[128,1024]{1,0:T(8,128)(2,1)S(1)} fusion(bf16[64,1024]{1,0:T(8,128)(2,1)} %collective-permute-done.9, bf16[32,1024]{1,0:T(8,128)(2,1)S(1)} %collective-permute-done.8, bf16[16,1024]{1,0:T(8,128)(2,1)S(1)} %collective-permute-done.7, bf16[16,512]{1,0:T(8,128)(2,1)S(1)} %get-tuple-element.35, ...), kind=kLoop, calls=%fused_computation.10 | loop fusion | flops 1310720 | bytes 524288 | tf_op jit(solution)/shard_map/concatenate | solution.py:136
  21.5 1.6 %collective-permute-start.12 = (bf16[128,1024]{1,0:T(8,128)(2,1)S(1)}, bf16[128,1024]{1,0:T(8,128)(2,1)S(1)}, u32[]{:S(2)}, u32[]{:S(2)}) collective-permute-start(bf16[128,1024]{1,0:T(8,128)(2,1)S(1)} %pad_maximum_fusion.1.a0_ref), channel_id=1, source_target_pairs={{0,1},{1,0},{2,3},{3,2},{4,5},{5,4},{6,7},{7,6},{8,9},{9,8},{10,11... | collective-permute-start | bytes 786440 | tf_op jit(solution)/shard_map/ppermute | solution.py:26
  23.1 0.1 collective-permute-start.3
  23.1 0.1 fusion.2
  23.2 0.6 collective-permute-start.4
  23.8 0.7 collective-permute-done.3.w1_ref
  24.5 1.3 %shard_map.94 = (bf16[16,8192]{1,0:T(8,128)(2,1)S(1)}, bf16[16,8192]{1,0:T(8,128)(2,1)S(1)}) custom-call(bf16[256,256]{1,0:T(8,128)(2,1)S(1)} %get-tuple-element.31.place_ref, bf16[128,512]{1,0:T(8,128)(2,1)S(1)} %pad_maximum_fusion.2.w0_ref, bf16[128,512]{1,0:T(8,128)(2,1)S(1)} %collective-permute-done.3.w1_ref, ...), custom_call_target="tpu_custom_call" | custom-call | tf_op jit(solution)/shard_map/pallas_call | solution.py:108
  25.7 3.6 %collective-permute-done.12.a0_ref = bf16[128,1024]{1,0:T(8,128)(2,1)S(1)} collective-permute-done((bf16[128,1024]{1,0:T(8,128)(2,1)S(1)}, bf16[128,1024]{1,0:T(8,128)(2,1)S(1)}, u32[]{:S(2)}, u32[]{:S(2)}) %collective-permute-start.12) | collective-permute-done | bytes 262176 | tf_op jit(solution)/shard_map/ppermute | solution.py:26
  29.3 1.5 %collective-permute-start.11 = (bf16[16,8192]{1,0:T(8,128)(2,1)S(1)}, bf16[16,8192]{1,0:T(8,128)(2,1)S(1)}, u32[]{:S(2)}, u32[]{:S(2)}) collective-permute-start(bf16[16,8192]{1,0:T(8,128)(2,1)S(1)} %get-tuple-element.14.part_ref), channel_id=1, source_target_pairs={{0,1},{1,0},{2,3},{3,2},{4,5},{5,4},{6,7},{7,6},{8,9},{9,8},{10,11... | collective-permute-start | bytes 786440 | tf_op jit(solution)/shard_map/ppermute | solution.py:26
  30.8 0.2 collective-permute-start.5
  31.1 0.3 collective-permute-start.10
  31.3 0.8 %collective-permute-done.5.w1_ref = bf16[128,512]{1,0:T(8,128)(2,1)S(1)} collective-permute-done((bf16[128,512]{1,0:T(8,128)(2,1)S(1)}, bf16[128,512]{1,0:T(8,128)(2,1)S(1)}, u32[]{:S(2)}, u32[]{:S(2)}) %collective-permute-start.5) | collective-permute-done | bytes 131104 | tf_op jit(solution)/shard_map/ppermute | solution.py:26
  32.2 1.3 %shard_map.95 = (bf16[16,8192]{1,0:T(8,128)(2,1)S(1)}, bf16[16,8192]{1,0:T(8,128)(2,1)S(1)}) custom-call(bf16[256,256]{1,0:T(8,128)(2,1)S(1)} %get-tuple-element.31.place_ref, bf16[128,512]{1,0:T(8,128)(2,1)S(1)} %collective-permute-done.4.w0_ref, bf16[128,512]{1,0:T(8,128)(2,1)S(1)} %collective-permute-done.5.w1_ref, ...), custom_call_target="tpu_custom_call" | custom-call | tf_op jit(solution)/shard_map/pallas_call | solution.py:108
  33.4 1.5 %collective-permute-start.6 = (bf16[16,8192]{1,0:T(8,128)(2,1)S(1)}, bf16[16,8192]{1,0:T(8,128)(2,1)S(1)}, u32[]{:S(2)}, u32[]{:S(2)}) collective-permute-start(bf16[16,8192]{1,0:T(8,128)(2,1)S(1)} %get-tuple-element.15.part_ref), channel_id=1, source_target_pairs={{0,1},{1,0},{2,3},{3,2},{4,5},{5,4},{6,7},{7,6},{8,9},{9,8},{10,11... | collective-permute-start | bytes 786440 | tf_op jit(solution)/shard_map/ppermute | solution.py:26
  34.9 0.5 shard_map.98
  35.5 3.0 %collective-permute-done.11.got_ref = bf16[16,8192]{1,0:T(8,128)(2,1)S(1)} collective-permute-done((bf16[16,8192]{1,0:T(8,128)(2,1)S(1)}, bf16[16,8192]{1,0:T(8,128)(2,1)S(1)}, u32[]{:S(2)}, u32[]{:S(2)}) %collective-permute-start.11) | collective-permute-done | bytes 262176 | tf_op jit(solution)/shard_map/ppermute | solution.py:26
  38.4 1.2 %shard_map.99 = bf16[256,512]{1,0:T(8,128)(2,1)S(1)} custom-call(bf16[256,256]{1,0:T(8,128)(2,1)S(1)} %get-tuple-element.32.back_ref, bf16[16,8192]{1,0:T(8,128)(2,1)S(1)} %get-tuple-element.15.part_ref, bf16[16,8192]{1,0:T(8,128)(2,1)S(1)} %collective-permute-done.11.got_ref, bf16[16,8192]{1,0:T(8,128)(2,1)S(1)} %get-tuple-element.20.weights_ref, ...), custom_call_target="tpu_custom_call" | custom-call | tf_op jit(solution)/shard_map/pallas_call | solution.py:108
  39.7 1.6 %collective-permute-start.14 = (bf16[256,512]{1,0:T(8,128)(2,1)S(1)}, bf16[256,512]{1,0:T(8,128)(2,1)S(1)}, u32[]{:S(2)}, u32[]{:S(2)}) collective-permute-start(bf16[256,512]{1,0:T(8,128)(2,1)S(1)} %shard_map.99), channel_id=1, source_target_pairs={{0,1},{1,0},{2,3},{3,2},{4,5},{5,4},{6,7},{7,6},{8,9},{9,8},{10,11... | collective-permute-start | bytes 786440 | tf_op jit(solution)/shard_map/ppermute | solution.py:26
  41.3 0.5 shard_map.96
  41.8 2.2 %collective-permute-done.6.got_ref = bf16[16,8192]{1,0:T(8,128)(2,1)S(1)} collective-permute-done((bf16[16,8192]{1,0:T(8,128)(2,1)S(1)}, bf16[16,8192]{1,0:T(8,128)(2,1)S(1)}, u32[]{:S(2)}, u32[]{:S(2)}) %collective-permute-start.6) | collective-permute-done | bytes 262176 | tf_op jit(solution)/shard_map/ppermute | solution.py:26
  44.0 1.8 %shard_map.97 = (bf16[256,512]{1,0:T(8,128)(2,1)S(1)}, bf16[256,512]{1,0:T(8,128)(2,1)S(1)}, bf16[16,8192]{1,0:T(8,128)(2,1)}) custom-call(bf16[256,256]{1,0:T(8,128)(2,1)S(1)} %get-tuple-element.32.back_ref, bf16[16,8192]{1,0:T(8,128)(2,1)S(1)} %get-tuple-element.14.part_ref, bf16[16,8192]{1,0:T(8,128)(2,1)S(1)} %collective-permute-done.6.got_ref, ...), custom_call_target="tpu_custom_call" | custom-call | tf_op jit(solution)/shard_map/pallas_call | solution.py:108
  45.9 3.4 %collective-permute-done.14 = bf16[256,512]{1,0:T(8,128)(2,1)S(1)} collective-permute-done((bf16[256,512]{1,0:T(8,128)(2,1)S(1)}, bf16[256,512]{1,0:T(8,128)(2,1)S(1)}, u32[]{:S(2)}, u32[]{:S(2)}) %collective-permute-start.14) | collective-permute-done | bytes 262176 | tf_op jit(solution)/shard_map/ppermute | solution.py:26
  49.3 0.1 add_convert_fusion.1
  49.4 0.1 collective-permute-start.15
  49.4 1.5 %collective-permute-done.15 = bf16[128,1024]{1,0:T(8,128)(2,1)S(1)} collective-permute-done((bf16[128,1024]{1,0:T(8,128)(2,1)S(1)}, bf16[128,1024]{1,0:T(8,128)(2,1)S(1)}, u32[]{:S(2)}, u32[]{:S(2)}) %collective-permute-start.15) | collective-permute-done | bytes 262176 | tf_op jit(solution)/shard_map/ppermute | solution.py:26
  51.0 0.1 add_convert_fusion
  51.0 1.6 %collective-permute-start.16 = (bf16[64,1024]{1,0:T(8,128)(2,1)S(1)}, bf16[64,1024]{1,0:T(8,128)(2,1)S(1)}, u32[]{:S(2)}, u32[]{:S(2)}) collective-permute-start(bf16[64,1024]{1,0:T(8,128)(2,1)S(1)} %slice.59), channel_id=1, source_target_pairs={{0,4},{2,6},{4,0},{6,2},{8,12},{10,14},{12,8},{14,10},{16,20},{18,... | collective-permute-start | bytes 393224 | tf_op jit(solution)/shard_map/ppermute | solution.py:26
  52.6 4.0 %collective-permute-done.16 = bf16[64,1024]{1,0:T(8,128)(2,1)S(1)} collective-permute-done((bf16[64,1024]{1,0:T(8,128)(2,1)S(1)}, bf16[64,1024]{1,0:T(8,128)(2,1)S(1)}, u32[]{:S(2)}, u32[]{:S(2)}) %collective-permute-start.16) | collective-permute-done | bytes 131104 | tf_op jit(solution)/shard_map/ppermute | solution.py:26
  56.7 1.6 %collective-permute-start.17 = (bf16[32,1024]{1,0:T(8,128)(2,1)S(1)}, bf16[32,1024]{1,0:T(8,128)(2,1)S(1)}, u32[]{:S(2)}, u32[]{:S(2)}) collective-permute-start(bf16[32,1024]{1,0:T(8,128)(2,1)S(1)} %slice.61), channel_id=1, source_target_pairs={{0,8},{2,10},{4,12},{6,14},{8,0},{10,2},{12,4},{14,6},{16,24},{18,... | collective-permute-start | bytes 196616 | tf_op jit(solution)/shard_map/ppermute | solution.py:26
  58.3 2.7 %collective-permute-done.17 = bf16[32,1024]{1,0:T(8,128)(2,1)S(1)} collective-permute-done((bf16[32,1024]{1,0:T(8,128)(2,1)S(1)}, bf16[32,1024]{1,0:T(8,128)(2,1)S(1)}, u32[]{:S(2)}, u32[]{:S(2)}) %collective-permute-start.17) | collective-permute-done | bytes 65568 | tf_op jit(solution)/shard_map/ppermute | solution.py:26
  61.1 1.7 %collective-permute-start.18 = (bf16[16,1024]{1,0:T(8,128)(2,1)S(1)}, bf16[16,1024]{1,0:T(8,128)(2,1)S(1)}, u32[]{:S(2)}, u32[]{:S(2)}) collective-permute-start(bf16[16,1024]{1,0:T(8,128)(2,1)S(1)} %slice.63), channel_id=1, source_target_pairs={{0,16},{2,18},{4,20},{6,22},{8,24},{10,26},{12,28},{14,30},{16,0},... | collective-permute-start | bytes 98312 | tf_op jit(solution)/shard_map/ppermute | solution.py:26
  62.8 3.2 %collective-permute-done.18 = bf16[16,1024]{1,0:T(8,128)(2,1)S(1)} collective-permute-done((bf16[16,1024]{1,0:T(8,128)(2,1)S(1)}, bf16[16,1024]{1,0:T(8,128)(2,1)S(1)}, u32[]{:S(2)}, u32[]{:S(2)}) %collective-permute-start.18) | collective-permute-done | bytes 32800 | tf_op jit(solution)/shard_map/ppermute | solution.py:26
  66.0 0.6 fusion.6
  (31 shorter events, 0.2 us)
Async XLA Ops:
  1.4 11.3 %collective-permute-start = (bf16[16,512]{1,0:T(8,128)(2,1)S(1)}, bf16[16,512]{1,0:T(8,128)(2,1)S(1)}, u32[]{:S(2)}, u32[]{:S(2)}) collective-permute-start(bf16[16,512]{1,0:T(8,128)(2,1)S(1)} %bitcast_convert_fusion), channel_id=1, source_target_pairs={{0,16},{2,18},{4,20},{6,22},{8,24},{10,26},{12,28},{14,30},{16,0},... | collective-permute-start | bytes 49160 | tf_op jit(solution)/shard_map/ppermute | solution.py:26
  6.2 10.7 %copy-start.4 = (s32[256]{0:T(256)S(1)}, s32[256]{0:T(256)}, u32[]{:S(2)}) copy-start(s32[256]{0:T(256)} %param.10) | copy-start | bytes 3076
  6.2 4.9 %collective-permute-start.7 = (bf16[16,1024]{1,0:T(8,128)(2,1)S(1)}, bf16[16,1024]{1,0:T(8,128)(2,1)S(1)}, u32[]{:S(2)}, u32[]{:S(2)}) collective-permute-start(bf16[16,1024]{1,0:T(8,128)(2,1)S(1)} %pad_maximum_fusion.7), channel_id=1, source_target_pairs={{0,16},{2,18},{4,20},{6,22},{8,24},{10,26},{12,28},{14,30},{16,0},... | collective-permute-start | bytes 98312 | tf_op jit(solution)/shard_map/ppermute | solution.py:26
  11.1 4.3 %collective-permute-start.8 = (bf16[32,1024]{1,0:T(8,128)(2,1)S(1)}, bf16[32,1024]{1,0:T(8,128)(2,1)S(1)}, u32[]{:S(2)}, u32[]{:S(2)}) collective-permute-start(bf16[32,1024]{1,0:T(8,128)(2,1)S(1)} %pad_maximum_fusion.5), channel_id=1, source_target_pairs={{0,8},{2,10},{4,12},{6,14},{8,0},{10,2},{12,4},{14,6},{16,24},{18,... | collective-permute-start | bytes 196616 | tf_op jit(solution)/shard_map/ppermute | solution.py:26
  12.7 4.5 %collective-permute-start.1 = (bf16[32,512]{1,0:T(8,128)(2,1)S(1)}, bf16[32,512]{1,0:T(8,128)(2,1)S(1)}, u32[]{:S(2)}, u32[]{:S(2)}) collective-permute-start(bf16[32,512]{1,0:T(8,128)(2,1)S(1)} %pad_maximum_fusion.6), channel_id=1, source_target_pairs={{0,8},{2,10},{4,12},{6,14},{8,0},{10,2},{12,4},{14,6},{16,24},{18,... | collective-permute-start | bytes 98312 | tf_op jit(solution)/shard_map/ppermute | solution.py:26
  15.4 5.1 %collective-permute-start.9 = (bf16[64,1024]{1,0:T(8,128)(2,1)S(1)}, bf16[64,1024]{1,0:T(8,128)(2,1)}, u32[]{:S(2)}, u32[]{:S(2)}) collective-permute-start(bf16[64,1024]{1,0:T(8,128)(2,1)S(1)} %pad_maximum_fusion.3), channel_id=1, source_target_pairs={{0,4},{2,6},{4,0},{6,2},{8,12},{10,14},{12,8},{14,10},{16,20},{18,... | collective-permute-start | bytes 393224 | tf_op jit(solution)/shard_map/ppermute | solution.py:26
  17.2 5.8 %collective-permute-start.2 = (bf16[64,512]{1,0:T(8,128)(2,1)S(1)}, bf16[64,512]{1,0:T(8,128)(2,1)S(1)}, u32[]{:S(2)}, u32[]{:S(2)}) collective-permute-start(bf16[64,512]{1,0:T(8,128)(2,1)S(1)} %pad_maximum_fusion.4), channel_id=1, source_target_pairs={{0,4},{2,6},{4,0},{6,2},{8,12},{10,14},{12,8},{14,10},{16,20},{18,... | collective-permute-start | bytes 196616 | tf_op jit(solution)/shard_map/ppermute | solution.py:26
  21.5 7.8 %collective-permute-start.12 = (bf16[128,1024]{1,0:T(8,128)(2,1)S(1)}, bf16[128,1024]{1,0:T(8,128)(2,1)S(1)}, u32[]{:S(2)}, u32[]{:S(2)}) collective-permute-start(bf16[128,1024]{1,0:T(8,128)(2,1)S(1)} %pad_maximum_fusion.1.a0_ref), channel_id=1, source_target_pairs={{0,1},{1,0},{2,3},{3,2},{4,5},{5,4},{6,7},{7,6},{8,9},{9,8},{10,11... | collective-permute-start | bytes 786440 | tf_op jit(solution)/shard_map/ppermute | solution.py:26
  23.1 1.4 %collective-permute-start.3 = (bf16[128,512]{1,0:T(8,128)(2,1)S(1)}, bf16[128,512]{1,0:T(8,128)(2,1)S(1)}, u32[]{:S(2)}, u32[]{:S(2)}) collective-permute-start(bf16[128,512]{1,0:T(8,128)(2,1)S(1)} %pad_maximum_fusion.2.w0_ref), channel_id=1, source_target_pairs={{0,2},{2,0},{4,6},{6,4},{8,10},{10,8},{12,14},{14,12},{16,18},{18,... | collective-permute-start | bytes 393224 | tf_op jit(solution)/shard_map/ppermute | solution.py:26
  23.2 7.6 %collective-permute-start.4 = (bf16[128,512]{1,0:T(8,128)(2,1)S(1)}, bf16[128,512]{1,0:T(8,128)(2,1)S(1)}, u32[]{:S(2)}, u32[]{:S(2)}) collective-permute-start(bf16[128,512]{1,0:T(8,128)(2,1)S(1)} %pad_maximum_fusion.2.w0_ref), channel_id=1, source_target_pairs={{0,1},{1,0},{2,3},{3,2},{4,5},{5,4},{6,7},{7,6},{8,9},{9,8},{10,11... | collective-permute-start | bytes 393224 | tf_op jit(solution)/shard_map/ppermute | solution.py:26
  25.7 12.7 %copy-start = (bf16[64,8192]{1,0:T(8,128)(2,1)S(1)}, bf16[64,8192]{1,0:T(8,128)(2,1)}, u32[]{:S(2)}) copy-start(bf16[64,8192]{1,0:T(8,128)(2,1)} %get-tuple-element.34.x_ref) | copy-start | bytes 3145732
  29.3 5.6 %collective-permute-start.13 = (bf16[128,1024]{1,0:T(8,128)(2,1)S(1)}, bf16[128,1024]{1,0:T(8,128)(2,1)S(1)}, u32[]{:S(2)}, u32[]{:S(2)}) collective-permute-start(bf16[128,1024]{1,0:T(8,128)(2,1)S(1)} %collective-permute-done.12.a0_ref), channel_id=1, source_target_pairs={{0,2},{2,0},{4,6},{6,4},{8,10},{10,8},{12,14},{14,12},{16,18},{18,... | collective-permute-start | bytes 786440 | tf_op jit(solution)/shard_map/ppermute | solution.py:26
  29.3 9.1 %collective-permute-start.11 = (bf16[16,8192]{1,0:T(8,128)(2,1)S(1)}, bf16[16,8192]{1,0:T(8,128)(2,1)S(1)}, u32[]{:S(2)}, u32[]{:S(2)}) collective-permute-start(bf16[16,8192]{1,0:T(8,128)(2,1)S(1)} %get-tuple-element.14.part_ref), channel_id=1, source_target_pairs={{0,1},{1,0},{2,3},{3,2},{4,5},{5,4},{6,7},{7,6},{8,9},{9,8},{10,11... | collective-permute-start | bytes 786440 | tf_op jit(solution)/shard_map/ppermute | solution.py:26
  30.8 1.3 %collective-permute-start.5 = (bf16[128,512]{1,0:T(8,128)(2,1)S(1)}, bf16[128,512]{1,0:T(8,128)(2,1)S(1)}, u32[]{:S(2)}, u32[]{:S(2)}) collective-permute-start(bf16[128,512]{1,0:T(8,128)(2,1)S(1)} %collective-permute-done.4.w0_ref), channel_id=1, source_target_pairs={{0,2},{2,0},{4,6},{6,4},{8,10},{10,8},{12,14},{14,12},{16,18},{18,... | collective-permute-start | bytes 393224 | tf_op jit(solution)/shard_map/ppermute | solution.py:26
  31.1 10.2 %collective-permute-start.10 = (bf16[128,1024]{1,0:T(8,128)(2,1)S(1)}, bf16[128,1024]{1,0:T(8,128)(2,1)S(1)}, u32[]{:S(2)}, u32[]{:S(2)}) collective-permute-start(bf16[128,1024]{1,0:T(8,128)(2,1)S(1)} %pad_maximum_fusion.1.a0_ref), channel_id=1, source_target_pairs={{0,2},{2,0},{4,6},{6,4},{8,10},{10,8},{12,14},{14,12},{16,18},{18,... | collective-permute-start | bytes 786440 | tf_op jit(solution)/shard_map/ppermute | solution.py:26
  33.4 10.6 %collective-permute-start.6 = (bf16[16,8192]{1,0:T(8,128)(2,1)S(1)}, bf16[16,8192]{1,0:T(8,128)(2,1)S(1)}, u32[]{:S(2)}, u32[]{:S(2)}) collective-permute-start(bf16[16,8192]{1,0:T(8,128)(2,1)S(1)} %get-tuple-element.15.part_ref), channel_id=1, source_target_pairs={{0,1},{1,0},{2,3},{3,2},{4,5},{5,4},{6,7},{7,6},{8,9},{9,8},{10,11... | collective-permute-start | bytes 786440 | tf_op jit(solution)/shard_map/ppermute | solution.py:26
  38.4 5.6 %copy-start.1 = (bf16[1,2,8,8192]{3,2,1,0:T(8,128)(2,1)S(1)}, bf16[1,2,8,8192]{3,2,1,0:T(8,128)(2,1)}, u32[]{:S(2)}) copy-start(bf16[1,2,8,8192]{3,2,1,0:T(8,128)(2,1)} %param.11) | copy-start | bytes 786436
  39.7 9.6 %collective-permute-start.14 = (bf16[256,512]{1,0:T(8,128)(2,1)S(1)}, bf16[256,512]{1,0:T(8,128)(2,1)S(1)}, u32[]{:S(2)}, u32[]{:S(2)}) collective-permute-start(bf16[256,512]{1,0:T(8,128)(2,1)S(1)} %shard_map.99), channel_id=1, source_target_pairs={{0,1},{1,0},{2,3},{3,2},{4,5},{5,4},{6,7},{7,6},{8,9},{9,8},{10,11... | collective-permute-start | bytes 786440 | tf_op jit(solution)/shard_map/ppermute | solution.py:26
  45.9 20.1 %copy-start.2 = (f32[1,16,512]{2,1,0:T(8,128)S(1)}, f32[1,16,512]{2,1,0:T(8,128)}, u32[]{:S(2)}) copy-start(f32[1,16,512]{2,1,0:T(8,128)} %param.9) | copy-start | bytes 98308
  45.9 20.1 %copy-start.3 = (f32[1,16,512]{2,1,0:T(8,128)S(1)}, f32[1,16,512]{2,1,0:T(8,128)}, u32[]{:S(2)}) copy-start(f32[1,16,512]{2,1,0:T(8,128)} %param.7) | copy-start | bytes 98308
  49.4 1.6 %collective-permute-start.15 = (bf16[128,1024]{1,0:T(8,128)(2,1)S(1)}, bf16[128,1024]{1,0:T(8,128)(2,1)S(1)}, u32[]{:S(2)}, u32[]{:S(2)}) collective-permute-start(bf16[128,1024]{1,0:T(8,128)(2,1)S(1)} %pad_maximum_fusion), channel_id=1, source_target_pairs={{0,2},{2,0},{4,6},{6,4},{8,10},{10,8},{12,14},{14,12},{16,18},{18,... | collective-permute-start | bytes 786440 | tf_op jit(solution)/shard_map/ppermute | solution.py:26
  51.0 5.6 %collective-permute-start.16 = (bf16[64,1024]{1,0:T(8,128)(2,1)S(1)}, bf16[64,1024]{1,0:T(8,128)(2,1)S(1)}, u32[]{:S(2)}, u32[]{:S(2)}) collective-permute-start(bf16[64,1024]{1,0:T(8,128)(2,1)S(1)} %slice.59), channel_id=1, source_target_pairs={{0,4},{2,6},{4,0},{6,2},{8,12},{10,14},{12,8},{14,10},{16,20},{18,... | collective-permute-start | bytes 393224 | tf_op jit(solution)/shard_map/ppermute | solution.py:26
  56.7 4.3 %collective-permute-start.17 = (bf16[32,1024]{1,0:T(8,128)(2,1)S(1)}, bf16[32,1024]{1,0:T(8,128)(2,1)S(1)}, u32[]{:S(2)}, u32[]{:S(2)}) collective-permute-start(bf16[32,1024]{1,0:T(8,128)(2,1)S(1)} %slice.61), channel_id=1, source_target_pairs={{0,8},{2,10},{4,12},{6,14},{8,0},{10,2},{12,4},{14,6},{16,24},{18,... | collective-permute-start | bytes 196616 | tf_op jit(solution)/shard_map/ppermute | solution.py:26
  61.1 4.9 %collective-permute-start.18 = (bf16[16,1024]{1,0:T(8,128)(2,1)S(1)}, bf16[16,1024]{1,0:T(8,128)(2,1)S(1)}, u32[]{:S(2)}, u32[]{:S(2)}) collective-permute-start(bf16[16,1024]{1,0:T(8,128)(2,1)S(1)} %slice.63), channel_id=1, source_target_pairs={{0,16},{2,18},{4,20},{6,22},{8,24},{10,26},{12,28},{14,30},{16,0},... | collective-permute-start | bytes 98312 | tf_op jit(solution)/shard_map/ppermute | solution.py:26

commit v2 on v1

v2 whole, which is shorter than its diff:
```python
import functools

import jax
import jax.numpy as jnp
from jax import lax
from jax.experimental import pallas as pl
from jax.experimental.pallas import tpu as pltpu
from jax.sharding import PartitionSpec as P

beta_one = 0.9
step_rate = 0.05
epsilon = 1e-08
down_scale = 28672.0 ** (-0.5)
BF = jnp.bfloat16
F32 = jnp.float32
NT = (((1,), (1,)), ((), ()))
NN = (((1,), (0,)), ((), ()))


def dot(a, b, dims=NN):
    return lax.dot_general(a, b, dims, preferred_element_type=F32)


def swap(x, axis, mask):
    n = lax.axis_size(axis)
    return lax.ppermute(x, axis, [(i, i ^ mask) for i in range(n)])


def bits_of(n, lowest=1):
    masks = []
    mask = n // 2
    while mask >= lowest:
        masks.append(mask)
        mask //= 2
    return masks


def gradient_rows(weights, step, x_ref, g_ref, hidden_rows, up_scale):
    before = up_scale * dot(weights, x_ref[step], NT)[:hidden_rows]
    back = down_scale * dot(weights, g_ref[step], NT)[hidden_rows:]
    sigmoid = jax.nn.sigmoid(before)
    hidden = before * sigmoid
    slope = back * (sigmoid * (1.0 + before * (1.0 - sigmoid)))
    zeros = jnp.zeros_like(slope)
    left_up = jnp.concatenate([slope, zeros], axis=0).astype(BF)
    left_down = jnp.concatenate([zeros, hidden], axis=0).astype(BF)

    def columns(at):
        return up_scale * dot(left_up, x_ref[step, :, at]) + down_scale * dot(left_down, g_ref[step, :, at])

    return columns


def first_kernel(hidden_rows, up_scale, chunk, place_ref, w0_ref, w1_ref, x_ref, g_ref, weights_ref, part_ref, sent_ref):
    rows = 2 * hidden_rows
    half, segment = w0_ref.shape
    width = x_ref.shape[2]
    ordered = dot(place_ref[:, :half], w0_ref[...]) + dot(place_ref[:, half:], w1_ref[...])
    for c in range(width // segment):
        weights_ref[:, c * segment : (c + 1) * segment] = ordered[c * rows : (c + 1) * rows].astype(BF)
    columns = gradient_rows(weights_ref[...], 0, x_ref, g_ref, hidden_rows, up_scale)
    for c in range(width // chunk):
        at = slice(c * chunk, (c + 1) * chunk)
        part = columns(at)
        part_ref[:, at] = part
        sent_ref[:, at] = part.astype(BF)


def moments_kernel(rows, split, place_ref, a0_ref, a1_ref, moment_ref, rate_ref):
    half = a0_ref.shape[0]
    segment = a0_ref.shape[1] // (3 if split else 2)
    width = moment_ref.shape[1]
    ordered = dot(place_ref[:, :half], a0_ref[...]) + dot(place_ref[:, half:], a1_ref[...])
    moment = ordered[:, :segment]
    if split:
        moment = moment + ordered[:, segment : 2 * segment]
    rate = step_rate / (jnp.sqrt(ordered[:, -segment:]) + epsilon)
    for c in range(width // segment):
        at = slice(c * segment, (c + 1) * segment)
        moment_ref[:, at] = moment[c * rows : (c + 1) * rows]
        rate_ref[:, at] = rate[c * rows : (c + 1) * rows]


def second_kernel(
    hidden_rows, up_scale, own, back_ref, part_ref, got_ref, weights_ref, moment_ref, rate_ref, x_ref, g_ref, *rest
):
    if own:
        feedback_ref, kept_ref, sent_ref, error_ref, local_ref, seg_ref = rest
    else:
        kept_ref, sent_ref, local_ref, seg_ref = rest
    rows = 2 * hidden_rows
    half = kept_ref.shape[0]
    segment = seg_ref.shape[1]
    width = x_ref.shape[2]
    step_one = part_ref[...] + got_ref[...].astype(F32)
    local_moment = beta_one * moment_ref[...] + (1.0 - beta_one) * step_one
    local_ref[...] = (weights_ref[...].astype(F32) - local_moment * rate_ref[...]).astype(BF)
    columns = gradient_rows(local_ref[...], 1, x_ref, g_ref, hidden_rows, up_scale)
    for c in range(width // segment):
        seg_ref[c * rows : (c + 1) * rows] = columns(slice(c * segment, (c + 1) * segment)).astype(BF)
    flat = dot(back_ref[...], seg_ref[...]).astype(BF)
    kept_ref[:, :segment] = flat[:half]
    sent_ref[:, :segment] = flat[half:]
    if own:
        shifted = local_moment + feedback_ref[...].astype(F32)
        magnitude = jnp.sum(jnp.abs(shifted), axis=1, keepdims=True) * (1.0 / width) + 1e-06
        packed = magnitude * jnp.tanh(shifted / magnitude)
        error_ref[...] = (shifted - packed).astype(BF)
        for c in range(width // segment):
            seg_ref[c * rows : (c + 1) * rows] = packed[:, c * segment : (c + 1) * segment].astype(BF)
        flat = dot(back_ref[...], seg_ref[...]).astype(BF)
        kept_ref[:, segment:] = flat[:half]
        sent_ref[:, segment:] = flat[half:]


def call(kernel, out_shape, operands, scratch=()):
    return pl.pallas_call(
        kernel,
        out_shape=out_shape,
        in_specs=[pl.BlockSpec(memory_space=pltpu.VMEM)] * len(operands),
        out_specs=jax.tree.map(lambda _: pl.BlockSpec(memory_space=pltpu.VMEM), out_shape),
        scratch_shapes=list(scratch),
        compiler_params=pltpu.CompilerParams(vmem_limit_bytes=32 * 1024 * 1024),
    )(*operands)


def per_device(master, moment, variance, flat_slot, feedback, activations, output_grads):
    n_dp, n_mp = lax.axis_size("dp"), lax.axis_size("mp")
    me = lax.axis_index("dp")
    span, segment = master.shape[1:]
    segments = flat_slot.shape[0]
    hidden_rows, width = feedback.shape[2:]
    rows = 2 * hidden_rows
    up_scale = width ** (-0.5)
    far = bits_of(n_dp, 2)
    mp_bits = bits_of(n_mp)
    shape = jax.ShapeDtypeStruct

    near_w = master[0].astype(BF)
    for mask in far:
        near_w = jnp.concatenate([near_w, swap(near_w, "dp", mask)], axis=0)

    high = moment[0].astype(BF)
    low = (moment[0] - high.astype(F32)).astype(BF)
    spread = variance[0].astype(BF)
    blocks_a = [jnp.concatenate([high, spread], axis=1)]
    for mask in reversed(mp_bits):
        blocks_a = blocks_a + [swap(b, "mp", mask) for b in blocks_a]
    blocks_a[0] = jnp.concatenate([high, low, spread], axis=1)
    for mask in far:
        blocks_a = [jnp.concatenate([b, swap(b, "dp", mask)], axis=0) for b in blocks_a]

    owner = (flat_slot // span) ^ me
    position = jnp.zeros_like(owner)
    for place, mask in enumerate(far + [1]):
        position = position + jnp.where((owner & mask) != 0, 1 << place, 0)
    position = position * span + flat_slot % span
    position = position.reshape(rows, width // segment).T.reshape(segments)
    line = jnp.arange(segments, dtype=jnp.int32)
    place_map = (position[:, None] == line[None, :]).astype(BF)
    back_map = (line[:, None] == position[None, :]).astype(BF)

    blocks_w = [near_w]
    for mask in reversed(mp_bits):
        blocks_w = blocks_w + [swap(b, "mp", mask) for b in blocks_w]
    pairs_w = [(b, swap(b, "dp", 1)) for b in blocks_w]
    pairs_a = [(b, swap(b, "dp", 1)) for b in blocks_a]

    tensor = (rows, width)
    half = segments // 2
    weights, parts, sent = [], [], []
    for w0, w1 in pairs_w:
        kernel = functools.partial(first_kernel, hidden_rows, up_scale, min(width, 1024))
        out = (shape(tensor, BF), shape(tensor, F32), shape(tensor, BF))
        w_t, part, part_sent = call(kernel, out, (place_map, w0, w1, activations, output_grads))
        weights.append(w_t)
        parts.append(part)
        sent.append(part_sent)
    moments, rates = [], []
    for k, (a0, a1) in enumerate(pairs_a):
        kernel = functools.partial(moments_kernel, rows, k == 0)
        m_t, rate = call(kernel, (shape(tensor, F32), shape(tensor, F32)), (place_map, a0, a1))
        moments.append(m_t)
        rates.append(rate)

    for step, mask in enumerate(mp_bits):
        if step > 0:
            parts = [p + q.astype(F32) for p, q in zip(parts, got)]
            sent = [p.astype(BF) for p in parts]
        crossed = [swap(p, "mp", mask) for p in sent]
        got = [crossed[k ^ mask] for k in range(n_mp)]

    kept, sent = [None] * n_mp, [None] * n_mp
    for k in reversed(range(n_mp)):
        own = k == 0
        operands = [back_map, parts[k], got[k], weights[k], moments[k], rates[k], activations, output_grads]
        lanes = 2 * segment if own else segment
        out = [shape((half, lanes), BF), shape((half, lanes), BF)]
        if own:
            operands.append(feedback[0].reshape(tensor))
            out.append(shape(tensor, BF))
        result = call(
            functools.partial(second_kernel, hidden_rows, up_scale, own),
            tuple(out),
            operands,
            [pltpu.VMEM(tensor, BF), pltpu.VMEM((segments, segment), BF)],
        )
        kept[k], sent[k] = result[:2]
        if own:
            error = result[2]

    sums = [p.astype(F32) + swap(q, "dp", 1).astype(F32) for p, q in zip(kept, sent)]
    total, packed = sums[0][:, :segment], sums[0][:, segment:]
    grads = [total] + sums[1:]
    for mask in mp_bits:
        stay = [k for k in range(len(grads)) if not k & mask]
        got = {k: swap(grads[k ^ mask].astype(BF), "mp", mask) for k in stay}
        grads = [grads[k] + got[k].astype(F32) for k in stay]
    last = jnp.concatenate([grads[0], packed], axis=1)
    for mask in far[::-1]:
        count = last.shape[0] // 2
        last = last[:count] + swap(last[count:].astype(BF), "dp", mask).astype(F32)
    mean_grad = last[:, :segment] / n_dp
    mean_moment = last[:, segment:] / n_dp
    moment_new = beta_one * mean_moment + (1.0 - beta_one) * mean_grad
    denominator = jnp.sqrt(variance[0]) + epsilon
    master_new = master[0] - step_rate * (mean_moment + moment_new) / denominator
    return (master_new[None], moment_new[None], error.reshape(feedback.shape))


def solution(mesh):
    in_specs = (
        P("mp", "dp", None),
        P("mp", "dp", None),
        P("mp", "dp", None),
        P(),
        P("dp", None, "mp", None),
        P(None, ("dp", "mp"), None),
        P(None, ("dp", "mp"), None),
    )
    out_specs = (P("mp", "dp", None), P("mp", "dp", None), P("dp", None, "mp", None))
    return jax.shard_map(
        per_device, mesh=mesh, in_specs=in_specs, out_specs=out_specs, check_vma=False
    )
```

time: 66.9 us -> 68.4 us (1.022)
  starting transfers between devices: 20.9 us -> 25.3 us
  waiting for transfers between devices: 31 us -> 29 us
  local copies, waits for them, and re-layouts: 3.75 us -> 1.88 us
  other arithmetic: 3.49 us -> 4.19 us
    ppermute x19 -> x23, starting transfers between devices: 20.9 us -> 25.3 us  [swap(): return lax.ppermute(x, axis, [(i, i ^ mask) for i in range(n)])]
    squeeze x1 -> x0, local copies, waits for them, and re-layouts: 3.48 us -> none  [per_device(): g_one, g_two = (output_grads[0], output_grads[1])]
    ppermute x19 -> x23, waiting for transfers between devices: 31 us -> 29 us  [swap(): return lax.ppermute(x, axis, [(i, i ^ mask) for i in range(n)])]
    unnamed x10 -> x15, local copies, waits for them, and re-layouts: 0.02 us -> 1.62 us
    concatenate x8 -> x10, other arithmetic: 0.98 us -> 0.09 us  [the longest x5 0.06 us: per_device(): jnp.concatenate([b, swap(b, 'dp', mask)], axis=0)]
    convert_element_type x5 -> x3, other arithmetic: 0.97 us -> 1.71 us  [the longest x1 0.91 us: per_device(): low = (moment[0] - high.astype(F32)).astype(BF)]
  transfers between devices with their start and end apart: 19 -> 23, of which waited for: 13 -> 13; matrix products, arithmetic and copies ran while one was open for 8% -> 3% of each run, Pallas kernels for 10% -> 10%
where the time goes in v2:
time: 68.4 us; the launch traced here: 68.1 us
  waiting for transfers between devices  29 us (42%)
  starting transfers between devices  25.3 us (37%)
  Pallas kernels  6.82 us (10%)
  other arithmetic  4.19 us (6%)
  local copies, waits for them, and re-layouts  1.88 us (3%)
  between operations  0.87 us (1%)
    ppermute x23, waiting for transfers between devices, swap(): return lax.ppermute(x, axis, [(i, i ^ mask) for i in range(n)])  29 us
    ppermute x23, starting transfers between devices, swap(): return lax.ppermute(x, axis, [(i, i ^ mask) for i in range(n)])  25.3 us
    pallas_call x6, Pallas kernels, call(): pl.pallas_call(kernel, out_shape=out_shape, in_specs=[pl.BlockSpec(memory...  6.82 us
    unnamed x15, local copies, waits for them, and re-layouts  1.62 us
  transfers between devices with their start and end apart: 23, of which 13 were waited for; matrix products, arithmetic and copies ran while one was open for 3% of the time, Pallas kernels for 10%

profile of v2, /device:TPU:0, one launch (start us, length us, event | category | flops | bytes accessed | tf_op | source)
XLA Modules:
  0.0 68.1 jit_solution(1656893740620026875)
XLA Ops:
  0.6 0.9 %fusion.8 = (bf16[16,512]{1,0:T(8,128)(2,1)S(1)}, bf16[16,512]{1,0:T(8,128)(2,1)S(1)}) fusion(f32[1,16,512]{2,1,0:T(8,128)} %param.8), kind=kLoop, calls=%fused_computation.34 | loop fusion | flops 32768 | bytes 65536 | tf_op jit(solution)/shard_map/convert_element_type | solution.py:144
  1.6 0.8 %convert_bitcast_fusion = bf16[16,512]{1,0:T(8,128)(2,1)S(1)} fusion(f32[1,16,512]{2,1,0:T(8,128)} %param.9), kind=kLoop, calls=%fused_computation.36 | loop fusion | flops 8192 | bytes 49152 | tf_op jit(solution)/shard_map/convert_element_type | solution.py:145
  2.3 3.0 %collective-permute-start.13 = (bf16[16,1024]{1,0:T(8,128)(2,1)S(1)}, bf16[16,1024]{1,0:T(8,128)(2,1)S(1)}, u32[]{:S(2)}, u32[]{:S(2)}) collective-permute-start(bf16[16,1024]{1,0:T(8,128)(2,1)S(1)} %pad_maximum_fusion.10), channel_id=1, source_target_pairs={{0,1},{1,0},{2,3},{3,2},{4,5},{5,4},{6,7},{7,6},{8,9},{9,8},{10,11... | collective-permute-start | bytes 98312 | tf_op jit(solution)/shard_map/ppermute | solution.py:26
  5.3 0.8 %bitcast_convert_fusion.1 = bf16[16,512]{1,0:T(8,128)(2,1)S(1)} fusion(f32[1,16,512]{2,1,0:T(8,128)} %param.7), kind=kLoop, calls=%fused_computation.35 | loop fusion | flops 8192 | bytes 49152 | tf_op jit(solution)/shard_map/convert_element_type | solution.py:139
  6.0 2.6 %collective-permute-start = (bf16[16,512]{1,0:T(8,128)(2,1)S(1)}, bf16[16,512]{1,0:T(8,128)(2,1)S(1)}, u32[]{:S(2)}, u32[]{:S(2)}) collective-permute-start(bf16[16,512]{1,0:T(8,128)(2,1)S(1)} %bitcast_convert_fusion.1), channel_id=1, source_target_pairs={{0,16},{2,18},{4,20},{6,22},{8,24},{10,26},{12,28},{14,30},{16,0},... | collective-permute-start | bytes 49160 | tf_op jit(solution)/shard_map/ppermute | solution.py:26
  8.6 0.3 collective-permute-start.7
  9.0 0.7 %fusion.13 = s32[256]{0:T(256)S(1)} fusion(s32[256]{0:T(256)} %param.10, s32[]{:T(128)S(6)} %axis_index.15), kind=kLoop, calls=%fused_computation.54 | loop fusion | flops 9472 | bytes 2052 | tf_op jit(solution)/shard_map/add | solution.py:157
  9.7 0.1 reshape.18
  9.8 0.1 copy.10
  9.8 0.1 eq.31
  9.9 0.1 fusion.4
  10.0 0.7 collective-permute-done
  10.7 1.7 %collective-permute-start.1 = (bf16[32,512]{1,0:T(8,128)(2,1)S(1)}, bf16[32,512]{1,0:T(8,128)(2,1)S(1)}, u32[]{:S(2)}, u32[]{:S(2)}) collective-permute-start(bf16[32,512]{1,0:T(8,128)(2,1)S(1)} %pad_maximum_fusion.9), channel_id=1, source_target_pairs={{0,8},{2,10},{4,12},{6,14},{8,0},{10,2},{12,4},{14,6},{16,24},{18,... | collective-permute-start | bytes 98312 | tf_op jit(solution)/shard_map/ppermute | solution.py:26
  12.4 3.1 %collective-permute-start.14 = (bf16[16,1024]{1,0:T(8,128)(2,1)S(1)}, bf16[16,1024]{1,0:T(8,128)(2,1)S(1)}, u32[]{:S(2)}, u32[]{:S(2)}) collective-permute-start(bf16[16,1024]{1,0:T(8,128)(2,1)S(1)} %collective-permute-done.13), channel_id=1, source_target_pairs={{0,16},{2,18},{4,20},{6,22},{8,24},{10,26},{12,28},{14,30},{16,0},... | collective-permute-start | bytes 98312 | tf_op jit(solution)/shard_map/ppermute | solution.py:26
  15.5 1.6 %collective-permute-start.2 = (bf16[64,512]{1,0:T(8,128)(2,1)S(1)}, bf16[64,512]{1,0:T(8,128)(2,1)S(1)}, u32[]{:S(2)}, u32[]{:S(2)}) collective-permute-start(bf16[64,512]{1,0:T(8,128)(2,1)S(1)} %pad_maximum_fusion.6), channel_id=1, source_target_pairs={{0,4},{2,6},{4,0},{6,2},{8,12},{10,14},{12,8},{14,10},{16,20},{18,... | collective-permute-start | bytes 196616 | tf_op jit(solution)/shard_map/ppermute | solution.py:26
  17.0 0.9 %collective-permute-start.8 = (bf16[32,1536]{1,0:T(8,128)(2,1)S(1)}, bf16[32,1536]{1,0:T(8,128)(2,1)S(1)}, u32[]{:S(2)}, u32[]{:S(2)}) collective-permute-start(bf16[32,1536]{1,0:T(8,128)(2,1)S(1)} %pad_maximum_fusion.5), channel_id=1, source_target_pairs={{0,8},{2,10},{4,12},{6,14},{8,0},{10,2},{12,4},{14,6},{16,24},{18,... | collective-permute-start | bytes 294920 | tf_op jit(solution)/shard_map/ppermute | solution.py:26
  18.0 1.2 %collective-permute-start.15 = (bf16[32,1024]{1,0:T(8,128)(2,1)S(1)}, bf16[32,1024]{1,0:T(8,128)(2,1)S(1)}, u32[]{:S(2)}, u32[]{:S(2)}) collective-permute-start(bf16[32,1024]{1,0:T(8,128)(2,1)S(1)} %pad_maximum_fusion.7), channel_id=1, source_target_pairs={{0,8},{2,10},{4,12},{6,14},{8,0},{10,2},{12,4},{14,6},{16,24},{18,... | collective-permute-start | bytes 196616 | tf_op jit(solution)/shard_map/ppermute | solution.py:26
  19.2 0.6 collective-permute-done.2
  19.8 0.6 collective-permute-start.4
  20.4 1.3 %collective-permute-done.8 = bf16[32,1536]{1,0:T(8,128)(2,1)S(1)} collective-permute-done((bf16[32,1536]{1,0:T(8,128)(2,1)S(1)}, bf16[32,1536]{1,0:T(8,128)(2,1)S(1)}, u32[]{:S(2)}, u32[]{:S(2)}) %collective-permute-start.8) | collective-permute-done | bytes 98336 | tf_op jit(solution)/shard_map/ppermute | solution.py:26
  21.7 0.6 collective-permute-start.9
  22.3 0.1 collective-permute-done.15
  22.4 1.5 %collective-permute-start.16 = (bf16[64,1024]{1,0:T(8,128)(2,1)S(1)}, bf16[64,1024]{1,0:T(8,128)(2,1)S(1)}, u32[]{:S(2)}, u32[]{:S(2)}) collective-permute-start(bf16[64,1024]{1,0:T(8,128)(2,1)S(1)} %pad_maximum_fusion.4), channel_id=1, source_target_pairs={{0,4},{2,6},{4,0},{6,2},{8,12},{10,14},{12,8},{14,10},{16,20},{18,... | collective-permute-start | bytes 393224 | tf_op jit(solution)/shard_map/ppermute | solution.py:26
  23.9 0.9 %collective-permute-done.4.w0_ref = bf16[128,512]{1,0:T(8,128)(2,1)S(1)} collective-permute-done((bf16[128,512]{1,0:T(8,128)(2,1)S(1)}, bf16[128,512]{1,0:T(8,128)(2,1)S(1)}, u32[]{:S(2)}, u32[]{:S(2)}) %collective-permute-start.4) | collective-permute-done | bytes 131104 | tf_op jit(solution)/shard_map/ppermute | solution.py:26
  24.9 1.6 %copy-done.1 = bf16[2,64,8192]{2,1,0:T(8,128)(2,1)S(1)} copy-done((bf16[2,64,8192]{2,1,0:T(8,128)(2,1)S(1)}, bf16[2,64,8192]{2,1,0:T(8,128)(2,1)}, u32[]{:S(2)}) %copy-start.1) | copy-done | bytes 2097176
  26.4 1.3 %shard_map.94 = (bf16[16,8192]{1,0:T(8,128)(2,1)S(1)}, f32[16,8192]{1,0:T(8,128)S(1)}, bf16[16,8192]{1,0:T(8,128)(2,1)S(1)}) custom-call(bf16[256,256]{1,0:T(8,128)(2,1)S(1)} %get-tuple-element.39.place_ref, bf16[128,512]{1,0:T(8,128)(2,1)S(1)} %pad_maximum_fusion.3.w0_ref, bf16[128,512]{1,0:T(8,128)(2,1)S(1)} %collective-permute-done.3.w1_ref, ...), custom_call_target="tpu_custom_call" | custom-call | tf_op jit(solution)/shard_map/pallas_call | solution.py:117
  27.7 1.5 %collective-permute-done.9 = bf16[64,1536]{1,0:T(8,128)(2,1)S(1)} collective-permute-done((bf16[64,1536]{1,0:T(8,128)(2,1)S(1)}, bf16[64,1536]{1,0:T(8,128)(2,1)S(1)}, u32[]{:S(2)}, u32[]{:S(2)}) %collective-permute-start.9) | collective-permute-done | bytes 196640 | tf_op jit(solution)/shard_map/ppermute | solution.py:26
  29.2 0.1 collective-permute-start.10
  29.3 1.3 %collective-permute-done.16 = bf16[64,1024]{1,0:T(8,128)(2,1)S(1)} collective-permute-done((bf16[64,1024]{1,0:T(8,128)(2,1)S(1)}, bf16[64,1024]{1,0:T(8,128)(2,1)S(1)}, u32[]{:S(2)}, u32[]{:S(2)}) %collective-permute-start.16) | collective-permute-done | bytes 131104 | tf_op jit(solution)/shard_map/ppermute | solution.py:26
  30.7 1.6 %collective-permute-start.12 = (bf16[16,8192]{1,0:T(8,128)(2,1)S(1)}, bf16[16,8192]{1,0:T(8,128)(2,1)S(1)}, u32[]{:S(2)}, u32[]{:S(2)}) collective-permute-start(bf16[16,8192]{1,0:T(8,128)(2,1)S(1)} %get-tuple-element.26), channel_id=1, source_target_pairs={{0,1},{1,0},{2,3},{3,2},{4,5},{5,4},{6,7},{7,6},{8,9},{9,8},{10,11... | collective-permute-start | bytes 786440 | tf_op jit(solution)/shard_map/ppermute | solution.py:26
  32.3 1.3 %shard_map.95 = (bf16[16,8192]{1,0:T(8,128)(2,1)S(1)}, f32[16,8192]{1,0:T(8,128)S(1)}, bf16[16,8192]{1,0:T(8,128)(2,1)S(1)}) custom-call(bf16[256,256]{1,0:T(8,128)(2,1)S(1)} %get-tuple-element.39.place_ref, bf16[128,512]{1,0:T(8,128)(2,1)S(1)} %collective-permute-done.4.w0_ref, bf16[128,512]{1,0:T(8,128)(2,1)S(1)} %collective-permute-done.5.w1_ref, ...), custom_call_target="tpu_custom_call" | custom-call | tf_op jit(solution)/shard_map/pallas_call | solution.py:117
  33.5 0.6 collective-permute-start.6
  34.1 0.5 shard_map.98
  34.7 5.2 %collective-permute-done.12.got_ref = bf16[16,8192]{1,0:T(8,128)(2,1)S(1)} collective-permute-done((bf16[16,8192]{1,0:T(8,128)(2,1)S(1)}, bf16[16,8192]{1,0:T(8,128)(2,1)S(1)}, u32[]{:S(2)}, u32[]{:S(2)}) %collective-permute-start.12) | collective-permute-done | bytes 262176 | tf_op jit(solution)/shard_map/ppermute | solution.py:26
  39.9 1.3 %shard_map.99 = (bf16[128,512]{1,0:T(8,128)(2,1)S(1)}, bf16[128,512]{1,0:T(8,128)(2,1)S(1)}) custom-call(bf16[256,256]{1,0:T(8,128)(2,1)S(1)} %get-tuple-element.40.back_ref, f32[16,8192]{1,0:T(8,128)S(1)} %get-tuple-element.25.part_ref, bf16[16,8192]{1,0:T(8,128)(2,1)S(1)} %collective-permute-done.12.got_ref, ...), custom_call_target="tpu_custom_call" | custom-call | tf_op jit(solution)/shard_map/pallas_call | solution.py:117
  41.1 0.1 collective-permute-start.18
  41.2 0.7 shard_map.96
  41.9 3.1 %collective-permute-done.6.got_ref = bf16[16,8192]{1,0:T(8,128)(2,1)S(1)} collective-permute-done((bf16[16,8192]{1,0:T(8,128)(2,1)S(1)}, bf16[16,8192]{1,0:T(8,128)(2,1)S(1)}, u32[]{:S(2)}, u32[]{:S(2)}) %collective-permute-start.6) | collective-permute-done | bytes 262176 | tf_op jit(solution)/shard_map/ppermute | solution.py:26
  45.0 1.8 %shard_map.97 = (bf16[128,1024]{1,0:T(8,128)(2,1)S(1)}, bf16[128,1024]{1,0:T(8,128)(2,1)S(1)}, bf16[16,8192]{1,0:T(8,128)(2,1)}) custom-call(bf16[256,256]{1,0:T(8,128)(2,1)S(1)} %get-tuple-element.40.back_ref, f32[16,8192]{1,0:T(8,128)S(1)} %get-tuple-element.18.part_ref, bf16[16,8192]{1,0:T(8,128)(2,1)S(1)} %collective-permute-done.6.got_ref, ...), custom_call_target="tpu_custom_call" | custom-call | tf_op jit(solution)/shard_map/pallas_call | solution.py:117
  46.9 1.6 %collective-permute-start.19 = (bf16[128,512]{1,0:T(8,128)(2,1)S(1)}, bf16[128,512]{1,0:T(8,128)(2,1)S(1)}, u32[]{:S(2)}, u32[]{:S(2)}) collective-permute-start(bf16[128,512]{1,0:T(8,128)(2,1)S(1)} %add_convert_fusion), channel_id=1, source_target_pairs={{0,1},{1,0},{2,3},{3,2},{4,5},{5,4},{6,7},{7,6},{8,9},{9,8},{10,11... | collective-permute-start | bytes 393224 | tf_op jit(solution)/shard_map/ppermute | solution.py:26
  48.6 4.3 %collective-permute-done.19 = bf16[128,512]{1,0:T(8,128)(2,1)S(1)} collective-permute-done((bf16[128,512]{1,0:T(8,128)(2,1)S(1)}, bf16[128,512]{1,0:T(8,128)(2,1)S(1)}, u32[]{:S(2)}, u32[]{:S(2)}) %collective-permute-start.19) | collective-permute-done | bytes 131104 | tf_op jit(solution)/shard_map/ppermute | solution.py:26
  53.0 1.6 %collective-permute-start.20 = (bf16[64,1024]{1,0:T(8,128)(2,1)S(1)}, bf16[64,1024]{1,0:T(8,128)(2,1)S(1)}, u32[]{:S(2)}, u32[]{:S(2)}) collective-permute-start(bf16[64,1024]{1,0:T(8,128)(2,1)S(1)} %fusion.2), channel_id=1, source_target_pairs={{0,4},{2,6},{4,0},{6,2},{8,12},{10,14},{12,8},{14,10},{16,20},{18,... | collective-permute-start | bytes 393224 | tf_op jit(solution)/shard_map/ppermute | solution.py:26
  54.5 3.6 %collective-permute-done.20 = bf16[64,1024]{1,0:T(8,128)(2,1)S(1)} collective-permute-done((bf16[64,1024]{1,0:T(8,128)(2,1)S(1)}, bf16[64,1024]{1,0:T(8,128)(2,1)S(1)}, u32[]{:S(2)}, u32[]{:S(2)}) %collective-permute-start.20) | collective-permute-done | bytes 131104 | tf_op jit(solution)/shard_map/ppermute | solution.py:26
  58.2 0.9 %collective-permute-start.21 = (bf16[32,1024]{1,0:T(8,128)(2,1)S(1)}, bf16[32,1024]{1,0:T(8,128)(2,1)S(1)}, u32[]{:S(2)}, u32[]{:S(2)}) collective-permute-start(bf16[32,1024]{1,0:T(8,128)(2,1)S(1)} %slice.79), channel_id=1, source_target_pairs={{0,8},{2,10},{4,12},{6,14},{8,0},{10,2},{12,4},{14,6},{16,24},{18,... | collective-permute-start | bytes 196616 | tf_op jit(solution)/shard_map/ppermute | solution.py:26
  59.1 3.4 %collective-permute-done.21 = bf16[32,1024]{1,0:T(8,128)(2,1)S(1)} collective-permute-done((bf16[32,1024]{1,0:T(8,128)(2,1)S(1)}, bf16[32,1024]{1,0:T(8,128)(2,1)S(1)}, u32[]{:S(2)}, u32[]{:S(2)}) %collective-permute-start.21) | collective-permute-done | bytes 65568 | tf_op jit(solution)/shard_map/ppermute | solution.py:26
  62.6 1.9 %collective-permute-start.22 = (bf16[16,1024]{1,0:T(8,128)(2,1)S(1)}, bf16[16,1024]{1,0:T(8,128)(2,1)S(1)}, u32[]{:S(2)}, u32[]{:S(2)}) collective-permute-start(bf16[16,1024]{1,0:T(8,128)(2,1)S(1)} %slice.80), channel_id=1, source_target_pairs={{0,16},{2,18},{4,20},{6,22},{8,24},{10,26},{12,28},{14,30},{16,0},... | collective-permute-start | bytes 98312 | tf_op jit(solution)/shard_map/ppermute | solution.py:26
  64.5 3.0 %collective-permute-done.22 = bf16[16,1024]{1,0:T(8,128)(2,1)S(1)} collective-permute-done((bf16[16,1024]{1,0:T(8,128)(2,1)S(1)}, bf16[16,1024]{1,0:T(8,128)(2,1)S(1)}, u32[]{:S(2)}, u32[]{:S(2)}) %collective-permute-start.22) | collective-permute-done | bytes 32800 | tf_op jit(solution)/shard_map/ppermute | solution.py:26
  67.5 0.6 fusion.9
  (48 shorter events, 0.5 us)
Async XLA Ops:
  0.6 24.2 %copy-start = (bf16[2,64,8192]{2,1,0:T(8,128)(2,1)S(1)}, bf16[2,64,8192]{2,1,0:T(8,128)(2,1)}, u32[]{:S(2)}) copy-start(bf16[2,64,8192]{2,1,0:T(8,128)(2,1)} %x_ref.7) | copy-start | bytes 6291460
  2.3 10.1 %collective-permute-start.13 = (bf16[16,1024]{1,0:T(8,128)(2,1)S(1)}, bf16[16,1024]{1,0:T(8,128)(2,1)S(1)}, u32[]{:S(2)}, u32[]{:S(2)}) collective-permute-start(bf16[16,1024]{1,0:T(8,128)(2,1)S(1)} %pad_maximum_fusion.10), channel_id=1, source_target_pairs={{0,1},{1,0},{2,3},{3,2},{4,5},{5,4},{6,7},{7,6},{8,9},{9,8},{10,11... | collective-permute-start | bytes 98312 | tf_op jit(solution)/shard_map/ppermute | solution.py:26
  6.0 4.6 %collective-permute-start = (bf16[16,512]{1,0:T(8,128)(2,1)S(1)}, bf16[16,512]{1,0:T(8,128)(2,1)S(1)}, u32[]{:S(2)}, u32[]{:S(2)}) collective-permute-start(bf16[16,512]{1,0:T(8,128)(2,1)S(1)} %bitcast_convert_fusion.1), channel_id=1, source_target_pairs={{0,16},{2,18},{4,20},{6,22},{8,24},{10,26},{12,28},{14,30},{16,0},... | collective-permute-start | bytes 49160 | tf_op jit(solution)/shard_map/ppermute | solution.py:26
  8.6 8.4 %collective-permute-start.7 = (bf16[16,1536]{1,0:T(8,128)(2,1)S(1)}, bf16[16,1536]{1,0:T(8,128)(2,1)S(1)}, u32[]{:S(2)}, u32[]{:S(2)}) collective-permute-start(bf16[16,1536]{1,0:T(8,128)(2,1)S(1)} %pad_maximum_fusion.8), channel_id=1, source_target_pairs={{0,16},{2,18},{4,20},{6,22},{8,24},{10,26},{12,28},{14,30},{16,0},... | collective-permute-start | bytes 147464 | tf_op jit(solution)/shard_map/ppermute | solution.py:26
  10.7 4.8 %collective-permute-start.1 = (bf16[32,512]{1,0:T(8,128)(2,1)S(1)}, bf16[32,512]{1,0:T(8,128)(2,1)S(1)}, u32[]{:S(2)}, u32[]{:S(2)}) collective-permute-start(bf16[32,512]{1,0:T(8,128)(2,1)S(1)} %pad_maximum_fusion.9), channel_id=1, source_target_pairs={{0,8},{2,10},{4,12},{6,14},{8,0},{10,2},{12,4},{14,6},{16,24},{18,... | collective-permute-start | bytes 98312 | tf_op jit(solution)/shard_map/ppermute | solution.py:26
  12.4 5.6 %collective-permute-start.14 = (bf16[16,1024]{1,0:T(8,128)(2,1)S(1)}, bf16[16,1024]{1,0:T(8,128)(2,1)S(1)}, u32[]{:S(2)}, u32[]{:S(2)}) collective-permute-start(bf16[16,1024]{1,0:T(8,128)(2,1)S(1)} %collective-permute-done.13), channel_id=1, source_target_pairs={{0,16},{2,18},{4,20},{6,22},{8,24},{10,26},{12,28},{14,30},{16,0},... | collective-permute-start | bytes 98312 | tf_op jit(solution)/shard_map/ppermute | solution.py:26
  15.5 4.3 %collective-permute-start.2 = (bf16[64,512]{1,0:T(8,128)(2,1)S(1)}, bf16[64,512]{1,0:T(8,128)(2,1)S(1)}, u32[]{:S(2)}, u32[]{:S(2)}) collective-permute-start(bf16[64,512]{1,0:T(8,128)(2,1)S(1)} %pad_maximum_fusion.6), channel_id=1, source_target_pairs={{0,4},{2,6},{4,0},{6,2},{8,12},{10,14},{12,8},{14,10},{16,20},{18,... | collective-permute-start | bytes 196616 | tf_op jit(solution)/shard_map/ppermute | solution.py:26
  17.0 4.7 %collective-permute-start.8 = (bf16[32,1536]{1,0:T(8,128)(2,1)S(1)}, bf16[32,1536]{1,0:T(8,128)(2,1)S(1)}, u32[]{:S(2)}, u32[]{:S(2)}) collective-permute-start(bf16[32,1536]{1,0:T(8,128)(2,1)S(1)} %pad_maximum_fusion.5), channel_id=1, source_target_pairs={{0,8},{2,10},{4,12},{6,14},{8,0},{10,2},{12,4},{14,6},{16,24},{18,... | collective-permute-start | bytes 294920 | tf_op jit(solution)/shard_map/ppermute | solution.py:26
  18.0 4.4 %collective-permute-start.15 = (bf16[32,1024]{1,0:T(8,128)(2,1)S(1)}, bf16[32,1024]{1,0:T(8,128)(2,1)S(1)}, u32[]{:S(2)}, u32[]{:S(2)}) collective-permute-start(bf16[32,1024]{1,0:T(8,128)(2,1)S(1)} %pad_maximum_fusion.7), channel_id=1, source_target_pairs={{0,8},{2,10},{4,12},{6,14},{8,0},{10,2},{12,4},{14,6},{16,24},{18,... | collective-permute-start | bytes 196616 | tf_op jit(solution)/shard_map/ppermute | solution.py:26
  19.8 5.0 %collective-permute-start.4 = (bf16[128,512]{1,0:T(8,128)(2,1)S(1)}, bf16[128,512]{1,0:T(8,128)(2,1)S(1)}, u32[]{:S(2)}, u32[]{:S(2)}) collective-permute-start(bf16[128,512]{1,0:T(8,128)(2,1)S(1)} %pad_maximum_fusion.3.w0_ref), channel_id=1, source_target_pairs={{0,1},{1,0},{2,3},{3,2},{4,5},{5,4},{6,7},{7,6},{8,9},{9,8},{10,11... | collective-permute-start | bytes 393224 | tf_op jit(solution)/shard_map/ppermute | solution.py:26
  20.4 4.5 %collective-permute-start.3 = (bf16[128,512]{1,0:T(8,128)(2,1)S(1)}, bf16[128,512]{1,0:T(8,128)(2,1)S(1)}, u32[]{:S(2)}, u32[]{:S(2)}) collective-permute-start(bf16[128,512]{1,0:T(8,128)(2,1)S(1)} %pad_maximum_fusion.3.w0_ref), channel_id=1, source_target_pairs={{0,2},{2,0},{4,6},{6,4},{8,10},{10,8},{12,14},{14,12},{16,18},{18,... | collective-permute-start | bytes 393224 | tf_op jit(solution)/shard_map/ppermute | solution.py:26
  21.7 7.5 %collective-permute-start.9 = (bf16[64,1536]{1,0:T(8,128)(2,1)S(1)}, bf16[64,1536]{1,0:T(8,128)(2,1)S(1)}, u32[]{:S(2)}, u32[]{:S(2)}) collective-permute-start(bf16[64,1536]{1,0:T(8,128)(2,1)S(1)} %pad_maximum_fusion.2), channel_id=1, source_target_pairs={{0,4},{2,6},{4,0},{6,2},{8,12},{10,14},{12,8},{14,10},{16,20},{18,... | collective-permute-start | bytes 589832 | tf_op jit(solution)/shard_map/ppermute | solution.py:26
  22.4 8.2 %collective-permute-start.16 = (bf16[64,1024]{1,0:T(8,128)(2,1)S(1)}, bf16[64,1024]{1,0:T(8,128)(2,1)S(1)}, u32[]{:S(2)}, u32[]{:S(2)}) collective-permute-start(bf16[64,1024]{1,0:T(8,128)(2,1)S(1)} %pad_maximum_fusion.4), channel_id=1, source_target_pairs={{0,4},{2,6},{4,0},{6,2},{8,12},{10,14},{12,8},{14,10},{16,20},{18,... | collective-permute-start | bytes 393224 | tf_op jit(solution)/shard_map/ppermute | solution.py:26
  24.8 7.4 %collective-permute-start.5 = (bf16[128,512]{1,0:T(8,128)(2,1)S(1)}, bf16[128,512]{1,0:T(8,128)(2,1)S(1)}, u32[]{:S(2)}, u32[]{:S(2)}) collective-permute-start(bf16[128,512]{1,0:T(8,128)(2,1)S(1)} %collective-permute-done.4.w0_ref), channel_id=1, source_target_pairs={{0,2},{2,0},{4,6},{6,4},{8,10},{10,8},{12,14},{14,12},{16,18},{18,... | collective-permute-start | bytes 393224 | tf_op jit(solution)/shard_map/ppermute | solution.py:26
  24.9 1.6 %copy-start.1 = (bf16[2,64,8192]{2,1,0:T(8,128)(2,1)S(1)}, bf16[2,64,8192]{2,1,0:T(8,128)(2,1)}, u32[]{:S(2)}) copy-start(bf16[2,64,8192]{2,1,0:T(8,128)(2,1)} %g_ref.7) | copy-start | bytes 6291460
  29.2 12.0 %collective-permute-start.10 = (bf16[128,1536]{1,0:T(8,128)(2,1)S(1)}, bf16[128,1536]{1,0:T(8,128)(2,1)S(1)}, u32[]{:S(2)}, u32[]{:S(2)}) collective-permute-start(bf16[128,1536]{1,0:T(8,128)(2,1)S(1)} %pad_maximum_fusion.a0_ref), channel_id=1, source_target_pairs={{0,2},{2,0},{4,6},{6,4},{8,10},{10,8},{12,14},{14,12},{16,18},{18,... | collective-permute-start | bytes 1179656 | tf_op jit(solution)/shard_map/ppermute | solution.py:26
  30.6 3.5 %collective-permute-start.17 = (bf16[128,1024]{1,0:T(8,128)(2,1)S(1)}, bf16[128,1024]{1,0:T(8,128)(2,1)S(1)}, u32[]{:S(2)}, u32[]{:S(2)}) collective-permute-start(bf16[128,1024]{1,0:T(8,128)(2,1)S(1)} %constant_dynamic-update-slice_fusion.a0_ref), channel_id=1, source_target_pairs={{0,2},{2,0},{4,6},{6,4},{8,10},{10,8},{12,14},{14,12},{16,18},{18,... | collective-permute-start | bytes 786440 | tf_op jit(solution)/shard_map/ppermute | solution.py:26
  30.7 9.2 %copy-start.2 = (bf16[2,64,8192]{2,1,0:T(8,128)(2,1)S(1)}, bf16[2,64,8192]{2,1,0:T(8,128)(2,1)}, u32[]{:S(2)}) copy-start(bf16[2,64,8192]{2,1,0:T(8,128)(2,1)} %g_ref.7) | copy-start | bytes 6291460
  30.7 9.2 %collective-permute-start.12 = (bf16[16,8192]{1,0:T(8,128)(2,1)S(1)}, bf16[16,8192]{1,0:T(8,128)(2,1)S(1)}, u32[]{:S(2)}, u32[]{:S(2)}) collective-permute-start(bf16[16,8192]{1,0:T(8,128)(2,1)S(1)} %get-tuple-element.26), channel_id=1, source_target_pairs={{0,1},{1,0},{2,3},{3,2},{4,5},{5,4},{6,7},{7,6},{8,9},{9,8},{10,11... | collective-permute-start | bytes 786440 | tf_op jit(solution)/shard_map/ppermute | solution.py:26
  33.5 11.5 %collective-permute-start.6 = (bf16[16,8192]{1,0:T(8,128)(2,1)S(1)}, bf16[16,8192]{1,0:T(8,128)(2,1)S(1)}, u32[]{:S(2)}, u32[]{:S(2)}) collective-permute-start(bf16[16,8192]{1,0:T(8,128)(2,1)S(1)} %get-tuple-element.19), channel_id=1, source_target_pairs={{0,1},{1,0},{2,3},{3,2},{4,5},{5,4},{6,7},{7,6},{8,9},{9,8},{10,11... | collective-permute-start | bytes 786440 | tf_op jit(solution)/shard_map/ppermute | solution.py:26
  39.9 5.2 %copy-start.3 = (bf16[1,2,8,8192]{3,2,1,0:T(8,128)(2,1)S(1)}, bf16[1,2,8,8192]{3,2,1,0:T(8,128)(2,1)}, u32[]{:S(2)}) copy-start(bf16[1,2,8,8192]{3,2,1,0:T(8,128)(2,1)} %param.11) | copy-start | bytes 786436
  41.1 5.7 %collective-permute-start.18 = (bf16[128,512]{1,0:T(8,128)(2,1)S(1)}, bf16[128,512]{1,0:T(8,128)(2,1)S(1)}, u32[]{:S(2)}, u32[]{:S(2)}) collective-permute-start(bf16[128,512]{1,0:T(8,128)(2,1)S(1)} %get-tuple-element.31), channel_id=1, source_target_pairs={{0,2},{2,0},{4,6},{6,4},{8,10},{10,8},{12,14},{14,12},{16,18},{18,... | collective-permute-start | bytes 393224 | tf_op jit(solution)/shard_map/ppermute | solution.py:26
  46.9 1.6 %collective-permute-start.11 = (bf16[128,1024]{1,0:T(8,128)(2,1)S(1)}, bf16[128,1024]{1,0:T(8,128)(2,1)S(1)}, u32[]{:S(2)}, u32[]{:S(2)}) collective-permute-start(bf16[128,1024]{1,0:T(8,128)(2,1)S(1)} %get-tuple-element.24), channel_id=1, source_target_pairs={{0,2},{2,0},{4,6},{6,4},{8,10},{10,8},{12,14},{14,12},{16,18},{18,... | collective-permute-start | bytes 786440 | tf_op jit(solution)/shard_map/ppermute | solution.py:26
  46.9 6.0 %collective-permute-start.19 = (bf16[128,512]{1,0:T(8,128)(2,1)S(1)}, bf16[128,512]{1,0:T(8,128)(2,1)S(1)}, u32[]{:S(2)}, u32[]{:S(2)}) collective-permute-start(bf16[128,512]{1,0:T(8,128)(2,1)S(1)} %add_convert_fusion), channel_id=1, source_target_pairs={{0,1},{1,0},{2,3},{3,2},{4,5},{5,4},{6,7},{7,6},{8,9},{9,8},{10,11... | collective-permute-start | bytes 393224 | tf_op jit(solution)/shard_map/ppermute | solution.py:26
  48.5 19.0 %copy-start.4 = (f32[1,16,512]{2,1,0:T(8,128)S(1)}, f32[1,16,512]{2,1,0:T(8,128)}, u32[]{:S(2)}) copy-start(f32[1,16,512]{2,1,0:T(8,128)} %param.7) | copy-start | bytes 98308
  48.5 19.0 %copy-start.5 = (f32[1,16,512]{2,1,0:T(8,128)S(1)}, f32[1,16,512]{2,1,0:T(8,128)}, u32[]{:S(2)}) copy-start(f32[1,16,512]{2,1,0:T(8,128)} %param.9) | copy-start | bytes 98308
  53.0 5.2 %collective-permute-start.20 = (bf16[64,1024]{1,0:T(8,128)(2,1)S(1)}, bf16[64,1024]{1,0:T(8,128)(2,1)S(1)}, u32[]{:S(2)}, u32[]{:S(2)}) collective-permute-start(bf16[64,1024]{1,0:T(8,128)(2,1)S(1)} %fusion.2), channel_id=1, source_target_pairs={{0,4},{2,6},{4,0},{6,2},{8,12},{10,14},{12,8},{14,10},{16,20},{18,... | collective-permute-start | bytes 393224 | tf_op jit(solution)/shard_map/ppermute | solution.py:26
  58.2 4.3 %collective-permute-start.21 = (bf16[32,1024]{1,0:T(8,128)(2,1)S(1)}, bf16[32,1024]{1,0:T(8,128)(2,1)S(1)}, u32[]{:S(2)}, u32[]{:S(2)}) collective-permute-start(bf16[32,1024]{1,0:T(8,128)(2,1)S(1)} %slice.79), channel_id=1, source_target_pairs={{0,8},{2,10},{4,12},{6,14},{8,0},{10,2},{12,4},{14,6},{16,24},{18,... | collective-permute-start | bytes 196616 | tf_op jit(solution)/shard_map/ppermute | solution.py:26
  62.6 4.9 %collective-permute-start.22 = (bf16[16,1024]{1,0:T(8,128)(2,1)S(1)}, bf16[16,1024]{1,0:T(8,128)(2,1)S(1)}, u32[]{:S(2)}, u32[]{:S(2)}) collective-permute-start(bf16[16,1024]{1,0:T(8,128)(2,1)S(1)} %slice.80), channel_id=1, source_target_pairs={{0,16},{2,18},{4,20},{6,22},{8,24},{10,26},{12,28},{14,30},{16,0},... | collective-permute-start | bytes 98312 | tf_op jit(solution)/shard_map/ppermute | solution.py:26

commit v3 on v2

--- a/solution.py
+++ b/solution.py
@@ -26,6 +26,10 @@
     return lax.ppermute(x, axis, [(i, i ^ mask) for i in range(n)])
 
 
+def after(x, *others):
+    return lax.optimization_barrier((x, *others))[0]
+
+
 def bits_of(n, lowest=1):
     masks = []
     mask = n // 2
@@ -35,9 +39,9 @@
     return masks
 
 
-def gradient_rows(weights, step, x_ref, g_ref, hidden_rows, up_scale):
-    before = up_scale * dot(weights, x_ref[step], NT)[:hidden_rows]
-    back = down_scale * dot(weights, g_ref[step], NT)[hidden_rows:]
+def gradient_rows(weights, x_ref, g_ref, hidden_rows, up_scale):
+    before = up_scale * dot(weights, x_ref[...], NT)[:hidden_rows]
+    back = down_scale * dot(weights, g_ref[...], NT)[hidden_rows:]
     sigmoid = jax.nn.sigmoid(before)
     hidden = before * sigmoid
     slope = back * (sigmoid * (1.0 + before * (1.0 - sigmoid)))
@@ -46,7 +50,7 @@
     left_down = jnp.concatenate([zeros, hidden], axis=0).astype(BF)
 
     def columns(at):
-        return up_scale * dot(left_up, x_ref[step, :, at]) + down_scale * dot(left_down, g_ref[step, :, at])
+        return up_scale * dot(left_up, x_ref[:, at]) + down_scale * dot(left_down, g_ref[:, at])
 
     return columns
 
@@ -54,11 +58,11 @@
 def first_kernel(hidden_rows, up_scale, chunk, place_ref, w0_ref, w1_ref, x_ref, g_ref, weights_ref, part_ref, sent_ref):
     rows = 2 * hidden_rows
     half, segment = w0_ref.shape
-    width = x_ref.shape[2]
+    width = x_ref.shape[1]
     ordered = dot(place_ref[:, :half], w0_ref[...]) + dot(place_ref[:, half:], w1_ref[...])
     for c in range(width // segment):
         weights_ref[:, c * segment : (c + 1) * segment] = ordered[c * rows : (c + 1) * rows].astype(BF)
-    columns = gradient_rows(weights_ref[...], 0, x_ref, g_ref, hidden_rows, up_scale)
+    columns = gradient_rows(weights_ref[...], x_ref, g_ref, hidden_rows, up_scale)
     for c in range(width // chunk):
         at = slice(c * chunk, (c + 1) * chunk)
         part = columns(at)
@@ -85,22 +89,19 @@
     hidden_rows, up_scale, own, back_ref, part_ref, got_ref, weights_ref, moment_ref, rate_ref, x_ref, g_ref, *rest
 ):
     if own:
-        feedback_ref, kept_ref, sent_ref, error_ref, local_ref, seg_ref = rest
+        feedback_ref, grad_ref, packed_ref, error_ref, local_ref, seg_ref = rest
     else:
-        kept_ref, sent_ref, local_ref, seg_ref = rest
+        grad_ref, local_ref, seg_ref = rest
     rows = 2 * hidden_rows
-    half = kept_ref.shape[0]
     segment = seg_ref.shape[1]
-    width = x_ref.shape[2]
+    width = x_ref.shape[1]
     step_one = part_ref[...] + got_ref[...].astype(F32)
     local_moment = beta_one * moment_ref[...] + (1.0 - beta_one) * step_one
     local_ref[...] = (weights_ref[...].astype(F32) - local_moment * rate_ref[...]).astype(BF)
-    columns = gradient_rows(local_ref[...], 1, x_ref, g_ref, hidden_rows, up_scale)
+    columns = gradient_rows(local_ref[...], x_ref, g_ref, hidden_rows, up_scale)
     for c in range(width // segment):
         seg_ref[c * rows : (c + 1) * rows] = columns(slice(c * segment, (c + 1) * segment)).astype(BF)
-    flat = dot(back_ref[...], seg_ref[...]).astype(BF)
-    kept_ref[:, :segment] = flat[:half]
-    sent_ref[:, :segment] = flat[half:]
+    grad_ref[...] = dot(back_ref[...], seg_ref[...]).astype(BF)
     if own:
         shifted = local_moment + feedback_ref[...].astype(F32)
         magnitude = jnp.sum(jnp.abs(shifted), axis=1, keepdims=True) * (1.0 / width) + 1e-06
@@ -108,9 +109,11 @@
         error_ref[...] = (shifted - packed).astype(BF)
         for c in range(width // segment):
             seg_ref[c * rows : (c + 1) * rows] = packed[:, c * segment : (c + 1) * segment].astype(BF)
-        flat = dot(back_ref[...], seg_ref[...]).astype(BF)
-        kept_ref[:, segment:] = flat[:half]
-        sent_ref[:, segment:] = flat[half:]
+        packed_ref[...] = dot(back_ref[...], seg_ref[...]).astype(BF)
+
+
+def tokens_of(step, arrays, *others):
+    return [x[step] for x in lax.optimization_barrier((*arrays, *others))[: len(arrays)]]
 
 
 def call(kernel, out_shape, operands, scratch=()):
@@ -120,7 +123,8 @@
         in_specs=[pl.BlockSpec(memory_space=pltpu.VMEM)] * len(operands),
         out_specs=jax.tree.map(lambda _: pl.BlockSpec(memory_space=pltpu.VMEM), out_shape),
         scratch_shapes=list(scratch),
-        compiler_params=pltpu.CompilerParams(vmem_limit_bytes=32 * 1024 * 1024),
+        cost_estimate=pl.CostEstimate(flops=1, bytes_accessed=1, transcendentals=0),
+        compiler_params=pltpu.CompilerParams(vmem_limit_bytes=16 * 1024 * 1024),
     )(*operands)
 
 
@@ -137,18 +141,22 @@
     shape = jax.ShapeDtypeStruct
 
     near_w = master[0].astype(BF)
+    exact = after(moment[0], near_w)
+    high = lax.reduce_precision(exact, 8, 7)
+    low = (exact - high).astype(BF)
+    high, spread = high.astype(BF), variance[0].astype(BF)
+    blocks_a = [jnp.concatenate([high, low, spread], axis=1)]
+    near_a = jnp.concatenate([high, spread], axis=1)
+    steps = []
     for mask in far:
         near_w = jnp.concatenate([near_w, swap(near_w, "dp", mask)], axis=0)
-
-    high = moment[0].astype(BF)
-    low = (moment[0] - high.astype(F32)).astype(BF)
-    spread = variance[0].astype(BF)
-    blocks_a = [jnp.concatenate([high, spread], axis=1)]
+        steps.append(near_w)
+    others = [near_a]
     for mask in reversed(mp_bits):
-        blocks_a = blocks_a + [swap(b, "mp", mask) for b in blocks_a]
-    blocks_a[0] = jnp.concatenate([high, low, spread], axis=1)
-    for mask in far:
-        blocks_a = [jnp.concatenate([b, swap(b, "dp", mask)], axis=0) for b in blocks_a]
+        others = others + [swap(after(b, steps[0]), "mp", mask) for b in others]
+    blocks_a = blocks_a + others[1:]
+    for mask, step in zip(far, steps):
+        blocks_a = [jnp.concatenate([b, swap(after(b, step), "dp", mask)], axis=0) for b in blocks_a]
 
     owner = (flat_slot // span) ^ me
     position = jnp.zeros_like(owner)
@@ -164,18 +172,28 @@
     for mask in reversed(mp_bits):
         blocks_w = blocks_w + [swap(b, "mp", mask) for b in blocks_w]
     pairs_w = [(b, swap(b, "dp", 1)) for b in blocks_w]
-    pairs_a = [(b, swap(b, "dp", 1)) for b in blocks_a]
 
     tensor = (rows, width)
+    one = tokens_of(0, (activations, output_grads), steps[0])
     half = segments // 2
     weights, parts, sent = [], [], []
     for w0, w1 in pairs_w:
         kernel = functools.partial(first_kernel, hidden_rows, up_scale, min(width, 1024))
         out = (shape(tensor, BF), shape(tensor, F32), shape(tensor, BF))
-        w_t, part, part_sent = call(kernel, out, (place_map, w0, w1, activations, output_grads))
+        w_t, part, part_sent = call(kernel, out, (place_map, w0, w1, *one))
         weights.append(w_t)
         parts.append(part)
         sent.append(part_sent)
+    two = tokens_of(1, (activations, output_grads), sent[0])
+
+    for step, mask in enumerate(mp_bits):
+        if step > 0:
+            parts = [p + q.astype(F32) for p, q in zip(parts, got)]
+            sent = [p.astype(BF) for p in parts]
+        crossed = [swap(p, "mp", mask) for p in sent]
+        got = [crossed[k ^ mask] for k in range(n_mp)]
+
+    pairs_a = [(b, swap(b, "dp", 1)) for b in blocks_a]
     moments, rates = [], []
     for k, (a0, a1) in enumerate(pairs_a):
         kernel = functools.partial(moments_kernel, rows, k == 0)
@@ -183,41 +201,27 @@
         moments.append(m_t)
         rates.append(rate)
 
-    for step, mask in enumerate(mp_bits):
-        if step > 0:
-            parts = [p + q.astype(F32) for p, q in zip(parts, got)]
-            sent = [p.astype(BF) for p in parts]
-        crossed = [swap(p, "mp", mask) for p in sent]
-        got = [crossed[k ^ mask] for k in range(n_mp)]
-
-    kept, sent = [None] * n_mp, [None] * n_mp
+    grads = [None] * n_mp
     for k in reversed(range(n_mp)):
         own = k == 0
-        operands = [back_map, parts[k], got[k], weights[k], moments[k], rates[k], activations, output_grads]
-        lanes = 2 * segment if own else segment
-        out = [shape((half, lanes), BF), shape((half, lanes), BF)]
+        operands = [back_map, parts[k], got[k], weights[k], moments[k], rates[k], *two]
+        out = [shape((segments, segment), BF)]
         if own:
             operands.append(feedback[0].reshape(tensor))
-            out.append(shape(tensor, BF))
+            out += [shape((segments, segment), BF), shape(tensor, BF)]
         result = call(
             functools.partial(second_kernel, hidden_rows, up_scale, own),
             tuple(out),
             operands,
             [pltpu.VMEM(tensor, BF), pltpu.VMEM((segments, segment), BF)],
         )
-        kept[k], sent[k] = result[:2]
-        if own:
-            error = result[2]
-
-    sums = [p.astype(F32) + swap(q, "dp", 1).astype(F32) for p, q in zip(kept, sent)]
-    total, packed = sums[0][:, :segment], sums[0][:, segment:]
-    grads = [total] + sums[1:]
+        grads[k] = result[0]
+    packed, error = result[1:]
     for mask in mp_bits:
-        stay = [k for k in range(len(grads)) if not k & mask]
-        got = {k: swap(grads[k ^ mask].astype(BF), "mp", mask) for k in stay}
-        grads = [grads[k] + got[k].astype(F32) for k in stay]
-    last = jnp.concatenate([grads[0], packed], axis=1)
-    for mask in far[::-1]:
+        crossing = [p.astype(BF) for p in grads[mask:]]
+        grads = [p.astype(F32) + swap(q, "mp", mask).astype(F32) for p, q in zip(grads, crossing)]
+    last = jnp.concatenate([grads[0], packed.astype(F32)], axis=1)
+    for mask in [1] + far[::-1]:
         count = last.shape[0] // 2
         last = last[:count] + swap(last[count:].astype(BF), "dp", mask).astype(F32)
     mean_grad = last[:, :segment] / n_dp

time: 68.4 us -> 66.6 us (0.974)
  starting transfers between devices: 25.3 us -> 21.4 us
  waiting for transfers between devices: 29 us -> 30.8 us
    ppermute x23 -> x22, starting transfers between devices: 25.3 us -> 21.4 us  [swap(): return lax.ppermute(x, axis, [(i, i ^ mask) for i in range(n)])]
    ppermute x23 -> x22, waiting for transfers between devices: 29 us -> 30.8 us  [swap(): return lax.ppermute(x, axis, [(i, i ^ mask) for i in range(n)])]
    squeeze x0 -> x3, local copies, waits for them, and re-layouts: none -> 1.81 us  [tokens_of(): x[step]]
    unnamed x15 -> x13, local copies, waits for them, and re-layouts: 1.62 us -> 0.04 us
  transfers between devices with their start and end apart: 23 -> 22, of which waited for: 13 -> 10; matrix products, arithmetic and copies ran while one was open for 3% -> 7% of each run, Pallas kernels for 10% -> 10%
where the time goes in v3:
time: 66.6 us; the launch traced here: 66.3 us
  waiting for transfers between devices  30.8 us (46%)
  starting transfers between devices  21.4 us (32%)
  Pallas kernels  6.87 us (10%)
  other arithmetic  4.1 us (6%)
  local copies, waits for them, and re-layouts  2.13 us (3%)
  between operations  0.96 us (1%)
    ppermute x22, waiting for transfers between devices, swap(): return lax.ppermute(x, axis, [(i, i ^ mask) for i in range(n)])  30.8 us
    ppermute x22, starting transfers between devices, swap(): return lax.ppermute(x, axis, [(i, i ^ mask) for i in range(n)])  21.4 us
    pallas_call x6, Pallas kernels, call(): pl.pallas_call(kernel, out_shape=out_shape, in_specs=[pl.BlockSpec(memory...  6.87 us
    squeeze x3, local copies, waits for them, and re-layouts, tokens_of(): x[step]  1.81 us
  transfers between devices with their start and end apart: 22, of which 10 were waited for; matrix products, arithmetic and copies ran while one was open for 7% of the time, Pallas kernels for 10%

profile of v3, /device:TPU:0, one launch (start us, length us, event | category | flops | bytes accessed | tf_op | source)
XLA Modules:
  0.0 66.3 jit_solution(10464990926182522516)
XLA Ops:
  0.6 0.8 %bitcast_convert_fusion = bf16[16,512]{1,0:T(8,128)(2,1)S(1)} fusion(f32[1,16,512]{2,1,0:T(8,128)} %param.7), kind=kLoop, calls=%fused_computation.39 | loop fusion | flops 8192 | bytes 49152 | tf_op jit(solution)/shard_map/convert_element_type | solution.py:143
  1.4 4.0 %collective-permute-start = (bf16[16,512]{1,0:T(8,128)(2,1)S(1)}, bf16[16,512]{1,0:T(8,128)(2,1)S(1)}, u32[]{:S(2)}, u32[]{:S(2)}) collective-permute-start(bf16[16,512]{1,0:T(8,128)(2,1)S(1)} %bitcast_convert_fusion), channel_id=1, source_target_pairs={{0,16},{2,18},{4,20},{6,22},{8,24},{10,26},{12,28},{14,30},{16,0},... | collective-permute-start | bytes 49160 | tf_op jit(solution)/shard_map/ppermute | solution.py:26
  5.4 0.7 %fusion.13 = s32[256]{0:T(256)S(1)} fusion(s32[256]{0:T(256)} %param.10, s32[]{:T(128)S(6)} %axis_index.15), kind=kLoop, calls=%fused_computation.58 | loop fusion | flops 9472 | bytes 2052 | tf_op jit(solution)/shard_map/add | solution.py:165
  6.1 0.1 reshape.18
  6.2 0.1 copy.10
  6.3 0.1 eq.31
  6.4 0.1 fusion.4
  6.5 0.8 %convert_bitcast_fusion = bf16[16,512]{1,0:T(8,128)(2,1)S(1)} fusion(f32[1,16,512]{2,1,0:T(8,128)} %param.9), kind=kLoop, calls=%fused_computation.40 | loop fusion | flops 8192 | bytes 49152 | tf_op jit(solution)/shard_map/convert_element_type | solution.py:147
  7.2 0.8 %fusion.5 = (bf16[16,512]{1,0:T(8,128)(2,1)S(1)}, bf16[16,512]{1,0:T(8,128)(2,1)S(1)}) fusion(f32[16,512]{1,0:T(8,128)} %bitcast.28), kind=kLoop, calls=%fused_computation.31 | loop fusion | flops 32768 | bytes 65536 | tf_op jit(solution)/shard_map/convert_element_type | solution.py:146
  8.1 1.6 %collective-permute-start.1 = (bf16[32,512]{1,0:T(8,128)(2,1)S(1)}, bf16[32,512]{1,0:T(8,128)(2,1)S(1)}, u32[]{:S(2)}, u32[]{:S(2)}) collective-permute-start(bf16[32,512]{1,0:T(8,128)(2,1)S(1)} %pad_maximum_fusion.9), channel_id=1, source_target_pairs={{0,8},{2,10},{4,12},{6,14},{8,0},{10,2},{12,4},{14,6},{16,24},{18,... | collective-permute-start | bytes 98312 | tf_op jit(solution)/shard_map/ppermute | solution.py:26
  9.7 1.5 %collective-permute-start.12 = (bf16[16,1024]{1,0:T(8,128)(2,1)S(1)}, bf16[16,1024]{1,0:T(8,128)(2,1)S(1)}, u32[]{:S(2)}, u32[]{:S(2)}) collective-permute-start(bf16[16,1024]{1,0:T(8,128)(2,1)S(1)} %pad_maximum_fusion.10), channel_id=1, source_target_pairs={{0,1},{1,0},{2,3},{3,2},{4,5},{5,4},{6,7},{7,6},{8,9},{9,8},{10,11... | collective-permute-start | bytes 98312 | tf_op jit(solution)/shard_map/ppermute | solution.py:26
  11.2 2.0 %collective-permute-start.7 = (bf16[16,1536]{1,0:T(8,128)(2,1)S(1)}, bf16[16,1536]{1,0:T(8,128)(2,1)S(1)}, u32[]{:S(2)}, u32[]{:S(2)}) collective-permute-start(bf16[16,1536]{1,0:T(8,128)(2,1)S(1)} %pad_maximum_fusion.8), channel_id=1, source_target_pairs={{0,16},{2,18},{4,20},{6,22},{8,24},{10,26},{12,28},{14,30},{16,0},... | collective-permute-start | bytes 147464 | tf_op jit(solution)/shard_map/ppermute | solution.py:26
  13.2 1.7 %slice_bitcast_fusion.2 = (bf16[64,8192]{1,0:T(8,128)(2,1)S(1)}, bf16[64,8192]{1,0:T(8,128)(2,1)S(1)}) fusion(bf16[2,64,8192]{2,1,0:T(8,128)(2,1)} %param.13, bf16[2,64,8192]{2,1,0:T(8,128)(2,1)} %param.12), kind=kLoop, calls=%fused_computation.4 | loop fusion | bytes 4194304 | tf_op jit(solution)/shard_map/squeeze | solution.py:116
  14.9 1.6 %collective-permute-start.2 = (bf16[64,512]{1,0:T(8,128)(2,1)S(1)}, bf16[64,512]{1,0:T(8,128)(2,1)S(1)}, u32[]{:S(2)}, u32[]{:S(2)}) collective-permute-start(bf16[64,512]{1,0:T(8,128)(2,1)S(1)} %pad_maximum_fusion.6), channel_id=1, source_target_pairs={{0,4},{2,6},{4,0},{6,2},{8,12},{10,14},{12,8},{14,10},{16,20},{18,... | collective-permute-start | bytes 196616 | tf_op jit(solution)/shard_map/ppermute | solution.py:26
  16.5 0.9 %collective-permute-start.13 = (bf16[16,1024]{1,0:T(8,128)(2,1)S(1)}, bf16[16,1024]{1,0:T(8,128)(2,1)S(1)}, u32[]{:S(2)}, u32[]{:S(2)}) collective-permute-start(bf16[16,1024]{1,0:T(8,128)(2,1)S(1)} %collective-permute-done.12), channel_id=1, source_target_pairs={{0,16},{2,18},{4,20},{6,22},{8,24},{10,26},{12,28},{14,30},{16,0},... | collective-permute-start | bytes 98312 | tf_op jit(solution)/shard_map/ppermute | solution.py:26
  17.4 0.5 collective-permute-start.8
  18.0 3.7 %collective-permute-done.13 = bf16[16,1024]{1,0:T(8,128)(2,1)S(1)} collective-permute-done((bf16[16,1024]{1,0:T(8,128)(2,1)S(1)}, bf16[16,1024]{1,0:T(8,128)(2,1)S(1)}, u32[]{:S(2)}, u32[]{:S(2)}) %collective-permute-start.13) | collective-permute-done | bytes 32800 | tf_op jit(solution)/shard_map/ppermute | solution.py:26
  21.6 0.1 collective-permute-start.14
  21.8 0.6 collective-permute-start.4
  22.3 3.5 %collective-permute-done.14 = bf16[32,1024]{1,0:T(8,128)(2,1)S(1)} collective-permute-done((bf16[32,1024]{1,0:T(8,128)(2,1)S(1)}, bf16[32,1024]{1,0:T(8,128)(2,1)S(1)}, u32[]{:S(2)}, u32[]{:S(2)}) %collective-permute-start.14) | collective-permute-done | bytes 65568 | tf_op jit(solution)/shard_map/ppermute | solution.py:26
  25.9 0.6 collective-permute-start.15
  26.5 1.6 %collective-permute-start.9 = (bf16[64,1536]{1,0:T(8,128)(2,1)S(1)}, bf16[64,1536]{1,0:T(8,128)(2,1)S(1)}, u32[]{:S(2)}, u32[]{:S(2)}) collective-permute-start(bf16[64,1536]{1,0:T(8,128)(2,1)S(1)} %pad_maximum_fusion.2), channel_id=1, source_target_pairs={{0,4},{2,6},{4,0},{6,2},{8,12},{10,14},{12,8},{14,10},{16,20},{18,... | collective-permute-start | bytes 589832 | tf_op jit(solution)/shard_map/ppermute | solution.py:26
  28.1 1.3 %shard_map.94 = (bf16[16,8192]{1,0:T(8,128)(2,1)S(1)}, f32[16,8192]{1,0:T(8,128)S(1)}, bf16[16,8192]{1,0:T(8,128)(2,1)S(1)}) custom-call(bf16[256,256]{1,0:T(8,128)(2,1)S(1)} %get-tuple-element.57.place_ref, bf16[128,512]{1,0:T(8,128)(2,1)S(1)} %pad_maximum_fusion.3.w0_ref, bf16[128,512]{1,0:T(8,128)(2,1)S(1)} %collective-permute-done.3.w1_ref, ...), custom_call_target="tpu_custom_call" | custom-call | flops 1 | bytes 1 | tf_op jit(solution)/shard_map/pallas_call | solution.py:120
  29.4 0.6 collective-permute-start.11
  30.0 0.1 collective-permute-start.5
  30.1 0.8 %collective-permute-done.15 = bf16[64,1024]{1,0:T(8,128)(2,1)S(1)} collective-permute-done((bf16[64,1024]{1,0:T(8,128)(2,1)S(1)}, bf16[64,1024]{1,0:T(8,128)(2,1)S(1)}, u32[]{:S(2)}, u32[]{:S(2)}) %collective-permute-start.15) | collective-permute-done | bytes 131104 | tf_op jit(solution)/shard_map/ppermute | solution.py:26
  30.9 0.1 collective-permute-start.16
  31.0 2.0 %collective-permute-done.9 = bf16[64,1536]{1,0:T(8,128)(2,1)S(1)} collective-permute-done((bf16[64,1536]{1,0:T(8,128)(2,1)S(1)}, bf16[64,1536]{1,0:T(8,128)(2,1)S(1)}, u32[]{:S(2)}, u32[]{:S(2)}) %collective-permute-start.9) | collective-permute-done | bytes 196640 | tf_op jit(solution)/shard_map/ppermute | solution.py:26
  33.1 0.1 collective-permute-start.10
  33.2 0.1 slice_bitcast_fusion.g_ref
  33.2 1.3 %shard_map.95 = (bf16[16,8192]{1,0:T(8,128)(2,1)S(1)}, f32[16,8192]{1,0:T(8,128)S(1)}, bf16[16,8192]{1,0:T(8,128)(2,1)S(1)}) custom-call(bf16[256,256]{1,0:T(8,128)(2,1)S(1)} %get-tuple-element.57.place_ref, bf16[128,512]{1,0:T(8,128)(2,1)S(1)} %collective-permute-done.4.w0_ref, bf16[128,512]{1,0:T(8,128)(2,1)S(1)} %collective-permute-done.5.w1_ref, ...), custom_call_target="tpu_custom_call" | custom-call | flops 1 | bytes 1 | tf_op jit(solution)/shard_map/pallas_call | solution.py:120
  34.5 1.1 %collective-permute-start.6 = (bf16[16,8192]{1,0:T(8,128)(2,1)S(1)}, bf16[16,8192]{1,0:T(8,128)(2,1)S(1)}, u32[]{:S(2)}, u32[]{:S(2)}) collective-permute-start(bf16[16,8192]{1,0:T(8,128)(2,1)S(1)} %get-tuple-element.31), channel_id=1, source_target_pairs={{0,1},{1,0},{2,3},{3,2},{4,5},{5,4},{6,7},{7,6},{8,9},{9,8},{10,11... | collective-permute-start | bytes 786440 | tf_op jit(solution)/shard_map/ppermute | solution.py:26
  35.6 0.5 shard_map.98
  36.2 1.3 %shard_map.99 = bf16[256,512]{1,0:T(8,128)(2,1)S(1)} custom-call(bf16[256,256]{1,0:T(8,128)(2,1)S(1)} %get-tuple-element.58.back_ref, f32[16,8192]{1,0:T(8,128)S(1)} %get-tuple-element.43.part_ref, bf16[16,8192]{1,0:T(8,128)(2,1)S(1)} %collective-permute-done.11.got_ref, bf16[16,8192]{1,0:T(8,128)(2,1)S(1)} %get-tuple-element.44.weights_ref, ...), custom_call_target="tpu_custom_call" | custom-call | flops 1 | bytes 1 | tf_op jit(solution)/shard_map/pallas_call | solution.py:120
  37.5 1.1 %collective-permute-start.17 = (bf16[256,512]{1,0:T(8,128)(2,1)S(1)}, bf16[256,512]{1,0:T(8,128)(2,1)S(1)}, u32[]{:S(2)}, u32[]{:S(2)}) collective-permute-start(bf16[256,512]{1,0:T(8,128)(2,1)S(1)} %shard_map.99), channel_id=1, source_target_pairs={{0,1},{1,0},{2,3},{3,2},{4,5},{5,4},{6,7},{7,6},{8,9},{9,8},{10,11... | collective-permute-start | bytes 786440 | tf_op jit(solution)/shard_map/ppermute | solution.py:26
  38.5 0.7 %shard_map.96 = (f32[16,8192]{1,0:T(8,128)S(1)}, f32[16,8192]{1,0:T(8,128)S(1)}) custom-call(bf16[256,256]{1,0:T(8,128)(2,1)S(1)} %get-tuple-element.57.place_ref, bf16[128,1536]{1,0:T(8,128)(2,1)S(1)} %pad_maximum_fusion.1.a0_ref, bf16[128,1536]{1,0:T(8,128)(2,1)S(1)} %collective-permute-done.10.a1_ref), custom_call_target="tpu_custom_call" | custom-call | flops 1 | bytes 1 | tf_op jit(solution)/shard_map/pallas_call | solution.py:120
  39.2 4.5 %collective-permute-done.6.got_ref = bf16[16,8192]{1,0:T(8,128)(2,1)S(1)} collective-permute-done((bf16[16,8192]{1,0:T(8,128)(2,1)S(1)}, bf16[16,8192]{1,0:T(8,128)(2,1)S(1)}, u32[]{:S(2)}, u32[]{:S(2)}) %collective-permute-start.6) | collective-permute-done | bytes 262176 | tf_op jit(solution)/shard_map/ppermute | solution.py:26
  43.7 1.9 %shard_map.97 = (bf16[256,512]{1,0:T(8,128)(2,1)S(1)}, bf16[256,512]{1,0:T(8,128)(2,1)S(1)}, bf16[16,8192]{1,0:T(8,128)(2,1)}) custom-call(bf16[256,256]{1,0:T(8,128)(2,1)S(1)} %get-tuple-element.58.back_ref, f32[16,8192]{1,0:T(8,128)S(1)} %get-tuple-element.30.part_ref, bf16[16,8192]{1,0:T(8,128)(2,1)S(1)} %collective-permute-done.6.got_ref, ...), custom_call_target="tpu_custom_call" | custom-call | flops 1 | bytes 1 | tf_op jit(solution)/shard_map/pallas_call | solution.py:120
  45.6 3.3 %collective-permute-done.17 = bf16[256,512]{1,0:T(8,128)(2,1)S(1)} collective-permute-done((bf16[256,512]{1,0:T(8,128)(2,1)S(1)}, bf16[256,512]{1,0:T(8,128)(2,1)S(1)}, u32[]{:S(2)}, u32[]{:S(2)}) %collective-permute-start.17) | collective-permute-done | bytes 262176 | tf_op jit(solution)/shard_map/ppermute | solution.py:26
  49.0 0.1 collective-permute-start.18
  49.1 1.5 %collective-permute-done.18 = bf16[128,1024]{1,0:T(8,128)(2,1)S(1)} collective-permute-done((bf16[128,1024]{1,0:T(8,128)(2,1)S(1)}, bf16[128,1024]{1,0:T(8,128)(2,1)S(1)}, u32[]{:S(2)}, u32[]{:S(2)}) %collective-permute-start.18) | collective-permute-done | bytes 262176 | tf_op jit(solution)/shard_map/ppermute | solution.py:26
  50.7 0.8 %collective-permute-start.19 = (bf16[64,1024]{1,0:T(8,128)(2,1)S(1)}, bf16[64,1024]{1,0:T(8,128)(2,1)S(1)}, u32[]{:S(2)}, u32[]{:S(2)}) collective-permute-start(bf16[64,1024]{1,0:T(8,128)(2,1)S(1)} %slice.101), channel_id=1, source_target_pairs={{0,4},{2,6},{4,0},{6,2},{8,12},{10,14},{12,8},{14,10},{16,20},{18,... | collective-permute-start | bytes 393224 | tf_op jit(solution)/shard_map/ppermute | solution.py:26
  51.5 4.8 %collective-permute-done.19 = bf16[64,1024]{1,0:T(8,128)(2,1)S(1)} collective-permute-done((bf16[64,1024]{1,0:T(8,128)(2,1)S(1)}, bf16[64,1024]{1,0:T(8,128)(2,1)S(1)}, u32[]{:S(2)}, u32[]{:S(2)}) %collective-permute-start.19) | collective-permute-done | bytes 131104 | tf_op jit(solution)/shard_map/ppermute | solution.py:26
  56.4 1.5 %collective-permute-start.20 = (bf16[32,1024]{1,0:T(8,128)(2,1)S(1)}, bf16[32,1024]{1,0:T(8,128)(2,1)S(1)}, u32[]{:S(2)}, u32[]{:S(2)}) collective-permute-start(bf16[32,1024]{1,0:T(8,128)(2,1)S(1)} %slice.102), channel_id=1, source_target_pairs={{0,8},{2,10},{4,12},{6,14},{8,0},{10,2},{12,4},{14,6},{16,24},{18,... | collective-permute-start | bytes 196616 | tf_op jit(solution)/shard_map/ppermute | solution.py:26
  57.8 2.9 %collective-permute-done.20 = bf16[32,1024]{1,0:T(8,128)(2,1)S(1)} collective-permute-done((bf16[32,1024]{1,0:T(8,128)(2,1)S(1)}, bf16[32,1024]{1,0:T(8,128)(2,1)S(1)}, u32[]{:S(2)}, u32[]{:S(2)}) %collective-permute-start.20) | collective-permute-done | bytes 65568 | tf_op jit(solution)/shard_map/ppermute | solution.py:26
  60.7 1.0 %collective-permute-start.21 = (bf16[16,1024]{1,0:T(8,128)(2,1)S(1)}, bf16[16,1024]{1,0:T(8,128)(2,1)S(1)}, u32[]{:S(2)}, u32[]{:S(2)}) collective-permute-start(bf16[16,1024]{1,0:T(8,128)(2,1)S(1)} %slice.103), channel_id=1, source_target_pairs={{0,16},{2,18},{4,20},{6,22},{8,24},{10,26},{12,28},{14,30},{16,0},... | collective-permute-start | bytes 98312 | tf_op jit(solution)/shard_map/ppermute | solution.py:26
  61.8 3.8 %collective-permute-done.21 = bf16[16,1024]{1,0:T(8,128)(2,1)S(1)} collective-permute-done((bf16[16,1024]{1,0:T(8,128)(2,1)S(1)}, bf16[16,1024]{1,0:T(8,128)(2,1)S(1)}, u32[]{:S(2)}, u32[]{:S(2)}) %collective-permute-start.21) | collective-permute-done | bytes 32800 | tf_op jit(solution)/shard_map/ppermute | solution.py:26
  65.6 0.6 fusion.9
  (48 shorter events, 0.5 us)
Async XLA Ops:
  1.4 6.6 %collective-permute-start = (bf16[16,512]{1,0:T(8,128)(2,1)S(1)}, bf16[16,512]{1,0:T(8,128)(2,1)S(1)}, u32[]{:S(2)}, u32[]{:S(2)}) collective-permute-start(bf16[16,512]{1,0:T(8,128)(2,1)S(1)} %bitcast_convert_fusion), channel_id=1, source_target_pairs={{0,16},{2,18},{4,20},{6,22},{8,24},{10,26},{12,28},{14,30},{16,0},... | collective-permute-start | bytes 49160 | tf_op jit(solution)/shard_map/ppermute | solution.py:26
  8.1 6.9 %collective-permute-start.1 = (bf16[32,512]{1,0:T(8,128)(2,1)S(1)}, bf16[32,512]{1,0:T(8,128)(2,1)S(1)}, u32[]{:S(2)}, u32[]{:S(2)}) collective-permute-start(bf16[32,512]{1,0:T(8,128)(2,1)S(1)} %pad_maximum_fusion.9), channel_id=1, source_target_pairs={{0,8},{2,10},{4,12},{6,14},{8,0},{10,2},{12,4},{14,6},{16,24},{18,... | collective-permute-start | bytes 98312 | tf_op jit(solution)/shard_map/ppermute | solution.py:26
  9.7 6.8 %collective-permute-start.12 = (bf16[16,1024]{1,0:T(8,128)(2,1)S(1)}, bf16[16,1024]{1,0:T(8,128)(2,1)S(1)}, u32[]{:S(2)}, u32[]{:S(2)}) collective-permute-start(bf16[16,1024]{1,0:T(8,128)(2,1)S(1)} %pad_maximum_fusion.10), channel_id=1, source_target_pairs={{0,1},{1,0},{2,3},{3,2},{4,5},{5,4},{6,7},{7,6},{8,9},{9,8},{10,11... | collective-permute-start | bytes 98312 | tf_op jit(solution)/shard_map/ppermute | solution.py:26
  11.2 6.2 %collective-permute-start.7 = (bf16[16,1536]{1,0:T(8,128)(2,1)S(1)}, bf16[16,1536]{1,0:T(8,128)(2,1)S(1)}, u32[]{:S(2)}, u32[]{:S(2)}) collective-permute-start(bf16[16,1536]{1,0:T(8,128)(2,1)S(1)} %pad_maximum_fusion.8), channel_id=1, source_target_pairs={{0,16},{2,18},{4,20},{6,22},{8,24},{10,26},{12,28},{14,30},{16,0},... | collective-permute-start | bytes 147464 | tf_op jit(solution)/shard_map/ppermute | solution.py:26
  14.9 15.0 %copy-start.1 = (bf16[2,64,8192]{2,1,0:T(8,128)(2,1)S(1)}, bf16[2,64,8192]{2,1,0:T(8,128)(2,1)}, u32[]{:S(2)}) copy-start(bf16[2,64,8192]{2,1,0:T(8,128)(2,1)} %param.12) | copy-start | bytes 6291460
  14.9 6.8 %collective-permute-start.2 = (bf16[64,512]{1,0:T(8,128)(2,1)S(1)}, bf16[64,512]{1,0:T(8,128)(2,1)S(1)}, u32[]{:S(2)}, u32[]{:S(2)}) collective-permute-start(bf16[64,512]{1,0:T(8,128)(2,1)S(1)} %pad_maximum_fusion.6), channel_id=1, source_target_pairs={{0,4},{2,6},{4,0},{6,2},{8,12},{10,14},{12,8},{14,10},{16,20},{18,... | collective-permute-start | bytes 196616 | tf_op jit(solution)/shard_map/ppermute | solution.py:26
  16.5 5.1 %collective-permute-start.13 = (bf16[16,1024]{1,0:T(8,128)(2,1)S(1)}, bf16[16,1024]{1,0:T(8,128)(2,1)S(1)}, u32[]{:S(2)}, u32[]{:S(2)}) collective-permute-start(bf16[16,1024]{1,0:T(8,128)(2,1)S(1)} %collective-permute-done.12), channel_id=1, source_target_pairs={{0,16},{2,18},{4,20},{6,22},{8,24},{10,26},{12,28},{14,30},{16,0},... | collective-permute-start | bytes 98312 | tf_op jit(solution)/shard_map/ppermute | solution.py:26
  17.4 9.1 %collective-permute-start.8 = (bf16[32,1536]{1,0:T(8,128)(2,1)S(1)}, bf16[32,1536]{1,0:T(8,128)(2,1)S(1)}, u32[]{:S(2)}, u32[]{:S(2)}) collective-permute-start(bf16[32,1536]{1,0:T(8,128)(2,1)S(1)} %pad_maximum_fusion.5), channel_id=1, source_target_pairs={{0,8},{2,10},{4,12},{6,14},{8,0},{10,2},{12,4},{14,6},{16,24},{18,... | collective-permute-start | bytes 294920 | tf_op jit(solution)/shard_map/ppermute | solution.py:26
  21.6 4.3 %collective-permute-start.14 = (bf16[32,1024]{1,0:T(8,128)(2,1)S(1)}, bf16[32,1024]{1,0:T(8,128)(2,1)S(1)}, u32[]{:S(2)}, u32[]{:S(2)}) collective-permute-start(bf16[32,1024]{1,0:T(8,128)(2,1)S(1)} %pad_maximum_fusion.7), channel_id=1, source_target_pairs={{0,8},{2,10},{4,12},{6,14},{8,0},{10,2},{12,4},{14,6},{16,24},{18,... | collective-permute-start | bytes 196616 | tf_op jit(solution)/shard_map/ppermute | solution.py:26
  21.8 8.3 %collective-permute-start.4 = (bf16[128,512]{1,0:T(8,128)(2,1)S(1)}, bf16[128,512]{1,0:T(8,128)(2,1)S(1)}, u32[]{:S(2)}, u32[]{:S(2)}) collective-permute-start(bf16[128,512]{1,0:T(8,128)(2,1)S(1)} %pad_maximum_fusion.3.w0_ref), channel_id=1, source_target_pairs={{0,1},{1,0},{2,3},{3,2},{4,5},{5,4},{6,7},{7,6},{8,9},{9,8},{10,11... | collective-permute-start | bytes 393224 | tf_op jit(solution)/shard_map/ppermute | solution.py:26
  22.3 5.8 %collective-permute-start.3 = (bf16[128,512]{1,0:T(8,128)(2,1)S(1)}, bf16[128,512]{1,0:T(8,128)(2,1)S(1)}, u32[]{:S(2)}, u32[]{:S(2)}) collective-permute-start(bf16[128,512]{1,0:T(8,128)(2,1)S(1)} %pad_maximum_fusion.3.w0_ref), channel_id=1, source_target_pairs={{0,2},{2,0},{4,6},{6,4},{8,10},{10,8},{12,14},{14,12},{16,18},{18,... | collective-permute-start | bytes 393224 | tf_op jit(solution)/shard_map/ppermute | solution.py:26
  25.9 5.0 %collective-permute-start.15 = (bf16[64,1024]{1,0:T(8,128)(2,1)S(1)}, bf16[64,1024]{1,0:T(8,128)(2,1)S(1)}, u32[]{:S(2)}, u32[]{:S(2)}) collective-permute-start(bf16[64,1024]{1,0:T(8,128)(2,1)S(1)} %pad_maximum_fusion.4), channel_id=1, source_target_pairs={{0,4},{2,6},{4,0},{6,2},{8,12},{10,14},{12,8},{14,10},{16,20},{18,... | collective-permute-start | bytes 393224 | tf_op jit(solution)/shard_map/ppermute | solution.py:26
  26.5 6.5 %collective-permute-start.9 = (bf16[64,1536]{1,0:T(8,128)(2,1)S(1)}, bf16[64,1536]{1,0:T(8,128)(2,1)S(1)}, u32[]{:S(2)}, u32[]{:S(2)}) collective-permute-start(bf16[64,1536]{1,0:T(8,128)(2,1)S(1)} %pad_maximum_fusion.2), channel_id=1, source_target_pairs={{0,4},{2,6},{4,0},{6,2},{8,12},{10,14},{12,8},{14,10},{16,20},{18,... | collective-permute-start | bytes 589832 | tf_op jit(solution)/shard_map/ppermute | solution.py:26
  29.3 3.8 %copy-start.2 = (bf16[2,64,8192]{2,1,0:T(8,128)(2,1)S(1)}, bf16[2,64,8192]{2,1,0:T(8,128)(2,1)}, u32[]{:S(2)}) copy-start(bf16[2,64,8192]{2,1,0:T(8,128)(2,1)} %param.13) | copy-start | bytes 6291460
  29.4 6.8 %collective-permute-start.11 = (bf16[16,8192]{1,0:T(8,128)(2,1)S(1)}, bf16[16,8192]{1,0:T(8,128)(2,1)S(1)}, u32[]{:S(2)}, u32[]{:S(2)}) collective-permute-start(bf16[16,8192]{1,0:T(8,128)(2,1)S(1)} %get-tuple-element.39), channel_id=1, source_target_pairs={{0,1},{1,0},{2,3},{3,2},{4,5},{5,4},{6,7},{7,6},{8,9},{9,8},{10,11... | collective-permute-start | bytes 786440 | tf_op jit(solution)/shard_map/ppermute | solution.py:26
  30.0 3.2 %collective-permute-start.5 = (bf16[128,512]{1,0:T(8,128)(2,1)S(1)}, bf16[128,512]{1,0:T(8,128)(2,1)S(1)}, u32[]{:S(2)}, u32[]{:S(2)}) collective-permute-start(bf16[128,512]{1,0:T(8,128)(2,1)S(1)} %collective-permute-done.4.w0_ref), channel_id=1, source_target_pairs={{0,2},{2,0},{4,6},{6,4},{8,10},{10,8},{12,14},{14,12},{16,18},{18,... | collective-permute-start | bytes 393224 | tf_op jit(solution)/shard_map/ppermute | solution.py:26
  30.9 4.7 %collective-permute-start.16 = (bf16[128,1024]{1,0:T(8,128)(2,1)S(1)}, bf16[128,1024]{1,0:T(8,128)(2,1)S(1)}, u32[]{:S(2)}, u32[]{:S(2)}) collective-permute-start(bf16[128,1024]{1,0:T(8,128)(2,1)S(1)} %constant_dynamic-update-slice_fusion.a0_ref), channel_id=1, source_target_pairs={{0,2},{2,0},{4,6},{6,4},{8,10},{10,8},{12,14},{14,12},{16,18},{18,... | collective-permute-start | bytes 786440 | tf_op jit(solution)/shard_map/ppermute | solution.py:26
  33.1 5.5 %collective-permute-start.10 = (bf16[128,1536]{1,0:T(8,128)(2,1)S(1)}, bf16[128,1536]{1,0:T(8,128)(2,1)S(1)}, u32[]{:S(2)}, u32[]{:S(2)}) collective-permute-start(bf16[128,1536]{1,0:T(8,128)(2,1)S(1)} %pad_maximum_fusion.1.a0_ref), channel_id=1, source_target_pairs={{0,2},{2,0},{4,6},{6,4},{8,10},{10,8},{12,14},{14,12},{16,18},{18,... | collective-permute-start | bytes 1179656 | tf_op jit(solution)/shard_map/ppermute | solution.py:26
  34.5 9.2 %collective-permute-start.6 = (bf16[16,8192]{1,0:T(8,128)(2,1)S(1)}, bf16[16,8192]{1,0:T(8,128)(2,1)S(1)}, u32[]{:S(2)}, u32[]{:S(2)}) collective-permute-start(bf16[16,8192]{1,0:T(8,128)(2,1)S(1)} %get-tuple-element.31), channel_id=1, source_target_pairs={{0,1},{1,0},{2,3},{3,2},{4,5},{5,4},{6,7},{7,6},{8,9},{9,8},{10,11... | collective-permute-start | bytes 786440 | tf_op jit(solution)/shard_map/ppermute | solution.py:26
  36.2 7.5 %copy-start = (bf16[1,2,8,8192]{3,2,1,0:T(8,128)(2,1)S(1)}, bf16[1,2,8,8192]{3,2,1,0:T(8,128)(2,1)}, u32[]{:S(2)}) copy-start(bf16[1,2,8,8192]{3,2,1,0:T(8,128)(2,1)} %param.11) | copy-start | bytes 786436
  37.5 11.4 %collective-permute-start.17 = (bf16[256,512]{1,0:T(8,128)(2,1)S(1)}, bf16[256,512]{1,0:T(8,128)(2,1)S(1)}, u32[]{:S(2)}, u32[]{:S(2)}) collective-permute-start(bf16[256,512]{1,0:T(8,128)(2,1)S(1)} %shard_map.99), channel_id=1, source_target_pairs={{0,1},{1,0},{2,3},{3,2},{4,5},{5,4},{6,7},{7,6},{8,9},{9,8},{10,11... | collective-permute-start | bytes 786440 | tf_op jit(solution)/shard_map/ppermute | solution.py:26
  49.0 16.7 %copy-start.3 = (f32[1,16,512]{2,1,0:T(8,128)S(1)}, f32[1,16,512]{2,1,0:T(8,128)}, u32[]{:S(2)}) copy-start(f32[1,16,512]{2,1,0:T(8,128)} %param.7) | copy-start | bytes 98308
  49.0 16.7 %copy-start.4 = (f32[1,16,512]{2,1,0:T(8,128)S(1)}, f32[1,16,512]{2,1,0:T(8,128)}, u32[]{:S(2)}) copy-start(f32[1,16,512]{2,1,0:T(8,128)} %param.9) | copy-start | bytes 98308
  49.0 1.6 %collective-permute-start.18 = (bf16[128,1024]{1,0:T(8,128)(2,1)S(1)}, bf16[128,1024]{1,0:T(8,128)(2,1)S(1)}, u32[]{:S(2)}, u32[]{:S(2)}) collective-permute-start(bf16[128,1024]{1,0:T(8,128)(2,1)S(1)} %fusion.2), channel_id=1, source_target_pairs={{0,2},{2,0},{4,6},{6,4},{8,10},{10,8},{12,14},{14,12},{16,18},{18,... | collective-permute-start | bytes 786440 | tf_op jit(solution)/shard_map/ppermute | solution.py:26
  50.7 5.6 %collective-permute-start.19 = (bf16[64,1024]{1,0:T(8,128)(2,1)S(1)}, bf16[64,1024]{1,0:T(8,128)(2,1)S(1)}, u32[]{:S(2)}, u32[]{:S(2)}) collective-permute-start(bf16[64,1024]{1,0:T(8,128)(2,1)S(1)} %slice.101), channel_id=1, source_target_pairs={{0,4},{2,6},{4,0},{6,2},{8,12},{10,14},{12,8},{14,10},{16,20},{18,... | collective-permute-start | bytes 393224 | tf_op jit(solution)/shard_map/ppermute | solution.py:26
  56.4 4.3 %collective-permute-start.20 = (bf16[32,1024]{1,0:T(8,128)(2,1)S(1)}, bf16[32,1024]{1,0:T(8,128)(2,1)S(1)}, u32[]{:S(2)}, u32[]{:S(2)}) collective-permute-start(bf16[32,1024]{1,0:T(8,128)(2,1)S(1)} %slice.102), channel_id=1, source_target_pairs={{0,8},{2,10},{4,12},{6,14},{8,0},{10,2},{12,4},{14,6},{16,24},{18,... | collective-permute-start | bytes 196616 | tf_op jit(solution)/shard_map/ppermute | solution.py:26
  60.7 4.9 %collective-permute-start.21 = (bf16[16,1024]{1,0:T(8,128)(2,1)S(1)}, bf16[16,1024]{1,0:T(8,128)(2,1)S(1)}, u32[]{:S(2)}, u32[]{:S(2)}) collective-permute-start(bf16[16,1024]{1,0:T(8,128)(2,1)S(1)} %slice.103), channel_id=1, source_target_pairs={{0,16},{2,18},{4,20},{6,22},{8,24},{10,26},{12,28},{14,30},{16,0},... | collective-permute-start | bytes 98312 | tf_op jit(solution)/shard_map/ppermute | solution.py:26

commit v4 on v3

--- a/solution.py
+++ b/solution.py
@@ -70,15 +70,15 @@
         sent_ref[:, at] = part.astype(BF)
 
 
-def moments_kernel(rows, split, place_ref, a0_ref, a1_ref, moment_ref, rate_ref):
-    half = a0_ref.shape[0]
-    segment = a0_ref.shape[1] // (3 if split else 2)
+def moments_kernel(rows, place_ref, *refs):
+    terms, (moment_ref, rate_ref) = refs[:-2], refs[-2:]
+    count = len(terms) // 2
+    half, segment = terms[0].shape
     width = moment_ref.shape[1]
-    ordered = dot(place_ref[:, :half], a0_ref[...]) + dot(place_ref[:, half:], a1_ref[...])
-    moment = ordered[:, :segment]
-    if split:
-        moment = moment + ordered[:, segment : 2 * segment]
-    rate = step_rate / (jnp.sqrt(ordered[:, -segment:]) + epsilon)
+    near, far = place_ref[:, :half], place_ref[:, half:]
+    ordered = [dot(near, a[...]) + dot(far, b[...]) for a, b in zip(terms[:count], terms[count:])]
+    moment = sum(ordered[1:-1], ordered[0])
+    rate = step_rate / (jnp.sqrt(ordered[-1]) + epsilon)
     for c in range(width // segment):
         at = slice(c * segment, (c + 1) * segment)
         moment_ref[:, at] = moment[c * rows : (c + 1) * rows]
@@ -112,6 +112,17 @@
         packed_ref[...] = dot(back_ref[...], seg_ref[...]).astype(BF)
 
 
+def split_kernel(moment_ref, variance_ref, own_ref, near_ref):
+    segment = moment_ref.shape[1]
+    high = moment_ref[...].astype(BF)
+    spread = variance_ref[...].astype(BF)
+    own_ref[:, :segment] = high
+    own_ref[:, segment : 2 * segment] = (moment_ref[...] - high.astype(F32)).astype(BF)
+    own_ref[:, 2 * segment :] = spread
+    near_ref[:, :segment] = high
+    near_ref[:, segment:] = spread
+
+
 def tokens_of(step, arrays, *others):
     return [x[step] for x in lax.optimization_barrier((*arrays, *others))[: len(arrays)]]
 
@@ -141,28 +152,26 @@
     shape = jax.ShapeDtypeStruct
 
     near_w = master[0].astype(BF)
-    exact = after(moment[0], near_w)
-    high = lax.reduce_precision(exact, 8, 7)
-    low = (exact - high).astype(BF)
-    high, spread = high.astype(BF), variance[0].astype(BF)
-    blocks_a = [jnp.concatenate([high, low, spread], axis=1)]
-    near_a = jnp.concatenate([high, spread], axis=1)
+    own_a, near_a = call(
+        split_kernel,
+        (shape((span, 3 * segment), BF), shape((span, 2 * segment), BF)),
+        (after(moment[0], near_w), variance[0]),
+    )
     steps = []
     for mask in far:
         near_w = jnp.concatenate([near_w, swap(near_w, "dp", mask)], axis=0)
         steps.append(near_w)
     others = [near_a]
     for mask in reversed(mp_bits):
-        others = others + [swap(after(b, steps[0]), "mp", mask) for b in others]
-    blocks_a = blocks_a + others[1:]
-    for mask, step in zip(far, steps):
-        blocks_a = [jnp.concatenate([b, swap(after(b, step), "dp", mask)], axis=0) for b in blocks_a]
-
-    owner = (flat_slot // span) ^ me
+        others = others + [swap(b, "mp", mask) for b in others]
+    blocks_a = [after(own_a, steps[0])] + others[1:]
+
+    slot = after(flat_slot, steps[-1])
+    owner = (slot // span) ^ me
     position = jnp.zeros_like(owner)
     for place, mask in enumerate(far + [1]):
         position = position + jnp.where((owner & mask) != 0, 1 << place, 0)
-    position = position * span + flat_slot % span
+    position = position * span + slot % span
     position = position.reshape(rows, width // segment).T.reshape(segments)
     line = jnp.arange(segments, dtype=jnp.int32)
     place_map = (position[:, None] == line[None, :]).astype(BF)
@@ -174,7 +183,7 @@
     pairs_w = [(b, swap(b, "dp", 1)) for b in blocks_w]
 
     tensor = (rows, width)
-    one = tokens_of(0, (activations, output_grads), steps[0])
+    one = tokens_of(0, (activations, output_grads), steps[-2])
     half = segments // 2
     weights, parts, sent = [], [], []
     for w0, w1 in pairs_w:
@@ -184,7 +193,7 @@
         weights.append(w_t)
         parts.append(part)
         sent.append(part_sent)
-    two = tokens_of(1, (activations, output_grads), sent[0])
+    two = tokens_of(1, (activations, output_grads), sent[-1])
 
     for step, mask in enumerate(mp_bits):
         if step > 0:
@@ -193,18 +202,21 @@
         crossed = [swap(p, "mp", mask) for p in sent]
         got = [crossed[k ^ mask] for k in range(n_mp)]
 
-    pairs_a = [(b, swap(b, "dp", 1)) for b in blocks_a]
-    moments, rates = [], []
-    for k, (a0, a1) in enumerate(pairs_a):
-        kernel = functools.partial(moments_kernel, rows, k == 0)
-        m_t, rate = call(kernel, (shape(tensor, F32), shape(tensor, F32)), (place_map, a0, a1))
-        moments.append(m_t)
-        rates.append(rate)
-
-    grads = [None] * n_mp
+    for mask, event in zip(far[:-1], [steps[-1]] * (len(far) - 2) + [sent[0]]):
+        arrived = [after(swap(b, "dp", mask), event) for b in blocks_a]
+        blocks_a = [jnp.concatenate(pair, axis=0) for pair in zip(blocks_a, arrived)]
+    arrived = [swap(b, "dp", far[-1]) for b in blocks_a]
+
+    grads, event = [None] * n_mp, sent[-1]
     for k in reversed(range(n_mp)):
         own = k == 0
-        operands = [back_map, parts[k], got[k], weights[k], moments[k], rates[k], *two]
+        block = jnp.concatenate([blocks_a[k], after(arrived[k], event)], axis=0)
+        terms = [block[:, at : at + segment] for at in range(0, block.shape[1], segment)]
+        terms += [swap(term, "dp", 1) for term in terms]
+        moment_t, rate = call(
+            functools.partial(moments_kernel, rows), (shape(tensor, F32), shape(tensor, F32)), (place_map, *terms)
+        )
+        operands = [back_map, parts[k], got[k], weights[k], moment_t, rate, *two]
         out = [shape((segments, segment), BF)]
         if own:
             operands.append(feedback[0].reshape(tensor))
@@ -216,6 +228,7 @@
             [pltpu.VMEM(tensor, BF), pltpu.VMEM((segments, segment), BF)],
         )
         grads[k] = result[0]
+        event = grads[k]
     packed, error = result[1:]
     for mask in mp_bits:
         crossing = [p.astype(BF) for p in grads[mask:]]

time: 66.6 us -> 61 us (0.916)
  waiting for transfers between devices: 30.8 us -> 19.9 us
  starting transfers between devices: 21.4 us -> 27.3 us
  other arithmetic: 4.1 us -> 1.85 us
  local copies, waits for them, and re-layouts: 2.13 us -> 3.78 us
    ppermute x22 -> x25, waiting for transfers between devices: 30.8 us -> 19.9 us  [swap(): return lax.ppermute(x, axis, [(i, i ^ mask) for i in range(n)])]
    ppermute x22 -> x25, starting transfers between devices: 21.4 us -> 27.3 us  [swap(): return lax.ppermute(x, axis, [(i, i ^ mask) for i in range(n)])]
    unnamed x13 -> x22, local copies, waits for them, and re-layouts: 0.04 us -> 1.58 us
    convert_element_type x2 -> x0, other arithmetic: 1.53 us -> none  [the longest x1 0.76 us: per_device(): high, spread = (high.astype(BF), variance[0].astype(BF))]
    add x1, other arithmetic: 0.7 us -> 0.02 us  [per_device(): position = position * span + slot % span]
    pallas_call x6 -> x7, Pallas kernels: 6.87 us -> 6.82 us  [call(): pl.pallas_call(kernel, out_shape=out_shape, in_specs=[pl.BlockSpec(memory...]
  transfers between devices with their start and end apart: 22 -> 25, of which waited for: 10 -> 13; matrix products, arithmetic and copies ran while one was open for 7% -> 4% of each run, Pallas kernels for 10% -> 11%
where the time goes in v4:
time: 61 us; the launch traced here: 60.6 us
  starting transfers between devices  27.3 us (45%)
  waiting for transfers between devices  19.9 us (33%)
  Pallas kernels  6.82 us (11%)
  local copies, waits for them, and re-layouts  3.78 us (6%)
  other arithmetic  1.85 us (3%)
  between operations  0.98 us (2%)
    ppermute x25, starting transfers between devices, swap(): return lax.ppermute(x, axis, [(i, i ^ mask) for i in range(n)])  27.3 us
    ppermute x25, waiting for transfers between devices, swap(): return lax.ppermute(x, axis, [(i, i ^ mask) for i in range(n)])  19.9 us
    pallas_call x7, Pallas kernels, call(): pl.pallas_call(kernel, out_shape=out_shape, in_specs=[pl.BlockSpec(memory...  6.82 us
    squeeze x3, local copies, waits for them, and re-layouts, tokens_of(): x[step]  1.86 us
    unnamed x22, local copies, waits for them, and re-layouts  1.58 us
  transfers between devices with their start and end apart: 25, of which 13 were waited for; matrix products, arithmetic and copies ran while one was open for 4% of the time, Pallas kernels for 11%

profile of v4, /device:TPU:0, one launch (start us, length us, event | category | flops | bytes accessed | tf_op | source)
XLA Modules:
  0.0 60.6 jit_solution(10935026036485470761)
XLA Ops:
  0.6 0.8 %bitcast_convert_fusion = bf16[16,512]{1,0:T(8,128)(2,1)S(1)} fusion(f32[1,16,512]{2,1,0:T(8,128)} %param.7), kind=kLoop, calls=%fused_computation.31 | loop fusion | flops 8192 | bytes 49152 | tf_op jit(solution)/shard_map/convert_element_type | solution.py:154
  1.4 4.0 %collective-permute-start = (bf16[16,512]{1,0:T(8,128)(2,1)S(1)}, bf16[16,512]{1,0:T(8,128)(2,1)S(1)}, u32[]{:S(2)}, u32[]{:S(2)}) collective-permute-start(bf16[16,512]{1,0:T(8,128)(2,1)S(1)} %bitcast_convert_fusion), channel_id=1, source_target_pairs={{0,16},{2,18},{4,20},{6,22},{8,24},{10,26},{12,28},{14,30},{16,0},... | collective-permute-start | bytes 49160 | tf_op jit(solution)/shard_map/ppermute | solution.py:26
  5.4 0.8 %copy-done.1 = f32[1,16,512]{2,1,0:T(8,128)S(1)} copy-done((f32[1,16,512]{2,1,0:T(8,128)S(1)}, f32[1,16,512]{2,1,0:T(8,128)}, u32[]{:S(2)}) %copy-start.1) | copy-done | bytes 32792
  6.2 0.8 %copy-done.3 = f32[1,16,512]{2,1,0:T(8,128)S(1)} copy-done((f32[1,16,512]{2,1,0:T(8,128)S(1)}, f32[1,16,512]{2,1,0:T(8,128)}, u32[]{:S(2)}) %copy-start.3) | copy-done | bytes 32792
  7.0 1.6 %collective-permute-start.11 = (bf16[16,1024]{1,0:T(8,128)(2,1)S(1)}, bf16[16,1024]{1,0:T(8,128)(2,1)S(1)}, u32[]{:S(2)}, u32[]{:S(2)}) collective-permute-start(bf16[16,1024]{1,0:T(8,128)(2,1)S(1)} %get-tuple-element.45), channel_id=1, source_target_pairs={{0,1},{1,0},{2,3},{3,2},{4,5},{5,4},{6,7},{7,6},{8,9},{9,8},{10,11... | collective-permute-start | bytes 98312 | tf_op jit(solution)/shard_map/ppermute | solution.py:26
  8.6 1.6 %collective-permute-start.1 = (bf16[32,512]{1,0:T(8,128)(2,1)S(1)}, bf16[32,512]{1,0:T(8,128)(2,1)S(1)}, u32[]{:S(2)}, u32[]{:S(2)}) collective-permute-start(bf16[32,512]{1,0:T(8,128)(2,1)S(1)} %pad_maximum_fusion.7), channel_id=1, source_target_pairs={{0,8},{2,10},{4,12},{6,14},{8,0},{10,2},{12,4},{14,6},{16,24},{18,... | collective-permute-start | bytes 98312 | tf_op jit(solution)/shard_map/ppermute | solution.py:26
  10.1 1.6 %collective-permute-start.7 = (bf16[16,1536]{1,0:T(8,128)(2,1)S(1)}, bf16[16,1536]{1,0:T(8,128)(2,1)S(1)}, u32[]{:S(2)}, u32[]{:S(2)}) collective-permute-start(bf16[16,1536]{1,0:T(8,128)(2,1)S(1)} %get-tuple-element.39), channel_id=1, source_target_pairs={{0,16},{2,18},{4,20},{6,22},{8,24},{10,26},{12,28},{14,30},{16,0},... | collective-permute-start | bytes 147464 | tf_op jit(solution)/shard_map/ppermute | solution.py:26
  11.7 1.4 %collective-permute-start.12 = (bf16[16,1024]{1,0:T(8,128)(2,1)S(1)}, bf16[16,1024]{1,0:T(8,128)(2,1)S(1)}, u32[]{:S(2)}, u32[]{:S(2)}) collective-permute-start(bf16[16,1024]{1,0:T(8,128)(2,1)S(1)} %collective-permute-done.11), channel_id=1, source_target_pairs={{0,16},{2,18},{4,20},{6,22},{8,24},{10,26},{12,28},{14,30},{16,0},... | collective-permute-start | bytes 98312 | tf_op jit(solution)/shard_map/ppermute | solution.py:26
  13.2 1.6 %collective-permute-start.2 = (bf16[64,512]{1,0:T(8,128)(2,1)S(1)}, bf16[64,512]{1,0:T(8,128)(2,1)S(1)}, u32[]{:S(2)}, u32[]{:S(2)}) collective-permute-start(bf16[64,512]{1,0:T(8,128)(2,1)S(1)} %pad_maximum_fusion.5), channel_id=1, source_target_pairs={{0,4},{2,6},{4,0},{6,2},{8,12},{10,14},{12,8},{14,10},{16,20},{18,... | collective-permute-start | bytes 196616 | tf_op jit(solution)/shard_map/ppermute | solution.py:26
  14.7 1.7 %slice_bitcast_fusion.2 = (bf16[64,8192]{1,0:T(8,128)(2,1)S(1)}, bf16[64,8192]{1,0:T(8,128)(2,1)S(1)}) fusion(bf16[2,64,8192]{2,1,0:T(8,128)(2,1)} %param.13, bf16[2,64,8192]{2,1,0:T(8,128)(2,1)} %param.12), kind=kLoop, calls=%fused_computation.4 | loop fusion | bytes 4194304 | tf_op jit(solution)/shard_map/squeeze | solution.py:127
  16.4 1.0 %collective-permute-done.2 = bf16[64,512]{1,0:T(8,128)(2,1)S(1)} collective-permute-done((bf16[64,512]{1,0:T(8,128)(2,1)S(1)}, bf16[64,512]{1,0:T(8,128)(2,1)S(1)}, u32[]{:S(2)}, u32[]{:S(2)}) %collective-permute-start.2) | collective-permute-done | bytes 65568 | tf_op jit(solution)/shard_map/ppermute | solution.py:26
  17.6 0.6 collective-permute-start.4
  18.2 0.1 reshape.14
  18.3 0.1 eq.31
  18.4 0.1 fusion.4
  18.5 1.3 %collective-permute-start.13 = (bf16[32,1024]{1,0:T(8,128)(2,1)S(1)}, bf16[32,1024]{1,0:T(8,128)(2,1)S(1)}, u32[]{:S(2)}, u32[]{:S(2)}) collective-permute-start(bf16[32,1024]{1,0:T(8,128)(2,1)S(1)} %pad_maximum_fusion.6), channel_id=1, source_target_pairs={{0,8},{2,10},{4,12},{6,14},{8,0},{10,2},{12,4},{14,6},{16,24},{18,... | collective-permute-start | bytes 196616 | tf_op jit(solution)/shard_map/ppermute | solution.py:26
  19.9 0.9 %collective-permute-start.8 = (bf16[32,1536]{1,0:T(8,128)(2,1)S(1)}, bf16[32,1536]{1,0:T(8,128)(2,1)S(1)}, u32[]{:S(2)}, u32[]{:S(2)}) collective-permute-start(bf16[32,1536]{1,0:T(8,128)(2,1)S(1)} %pad_maximum_fusion.4), channel_id=1, source_target_pairs={{0,8},{2,10},{4,12},{6,14},{8,0},{10,2},{12,4},{14,6},{16,24},{18,... | collective-permute-start | bytes 294920 | tf_op jit(solution)/shard_map/ppermute | solution.py:26
  20.7 1.3 %shard_map.94 = (bf16[16,8192]{1,0:T(8,128)(2,1)S(1)}, f32[16,8192]{1,0:T(8,128)S(1)}, bf16[16,8192]{1,0:T(8,128)(2,1)S(1)}) custom-call(bf16[256,256]{1,0:T(8,128)(2,1)S(1)} %get-tuple-element.66.place_ref, bf16[128,512]{1,0:T(8,128)(2,1)S(1)} %pad_maximum_fusion.2.w0_ref, bf16[128,512]{1,0:T(8,128)(2,1)S(1)} %collective-permute-done.3.w1_ref, ...), custom_call_target="tpu_custom_call" | custom-call | flops 1 | bytes 1 | tf_op jit(solution)/shard_map/pallas_call | solution.py:131
  22.0 1.6 %collective-permute-start.10 = (bf16[16,8192]{1,0:T(8,128)(2,1)S(1)}, bf16[16,8192]{1,0:T(8,128)(2,1)S(1)}, u32[]{:S(2)}, u32[]{:S(2)}) collective-permute-start(bf16[16,8192]{1,0:T(8,128)(2,1)S(1)} %get-tuple-element.41), channel_id=1, source_target_pairs={{0,1},{1,0},{2,3},{3,2},{4,5},{5,4},{6,7},{7,6},{8,9},{9,8},{10,11... | collective-permute-start | bytes 786440 | tf_op jit(solution)/shard_map/ppermute | solution.py:26
  23.6 1.6 %collective-permute-start.14 = (bf16[64,1024]{1,0:T(8,128)(2,1)S(1)}, bf16[64,1024]{1,0:T(8,128)(2,1)S(1)}, u32[]{:S(2)}, u32[]{:S(2)}) collective-permute-start(bf16[64,1024]{1,0:T(8,128)(2,1)S(1)} %pad_maximum_fusion.3), channel_id=1, source_target_pairs={{0,4},{2,6},{4,0},{6,2},{8,12},{10,14},{12,8},{14,10},{16,20},{18,... | collective-permute-start | bytes 393224 | tf_op jit(solution)/shard_map/ppermute | solution.py:26
  25.2 1.4 %collective-permute-start.9 = (bf16[64,1536]{1,0:T(8,128)(2,1)S(1)}, bf16[64,1536]{1,0:T(8,128)(2,1)S(1)}, u32[]{:S(2)}, u32[]{:S(2)}) collective-permute-start(bf16[64,1536]{1,0:T(8,128)(2,1)S(1)} %pad_maximum_fusion.1), channel_id=1, source_target_pairs={{0,4},{2,6},{4,0},{6,2},{8,12},{10,14},{12,8},{14,10},{16,20},{18,... | collective-permute-start | bytes 589832 | tf_op jit(solution)/shard_map/ppermute | solution.py:26
  26.6 1.3 %collective-permute-done.5.w1_ref = bf16[128,512]{1,0:T(8,128)(2,1)S(1)} collective-permute-done((bf16[128,512]{1,0:T(8,128)(2,1)S(1)}, bf16[128,512]{1,0:T(8,128)(2,1)S(1)}, u32[]{:S(2)}, u32[]{:S(2)}) %collective-permute-start.5) | collective-permute-done | bytes 131104 | tf_op jit(solution)/shard_map/ppermute | solution.py:26
  27.9 1.3 %shard_map.95 = (bf16[16,8192]{1,0:T(8,128)(2,1)S(1)}, f32[16,8192]{1,0:T(8,128)S(1)}, bf16[16,8192]{1,0:T(8,128)(2,1)S(1)}) custom-call(bf16[256,256]{1,0:T(8,128)(2,1)S(1)} %get-tuple-element.66.place_ref, bf16[128,512]{1,0:T(8,128)(2,1)S(1)} %collective-permute-done.4.w0_ref, bf16[128,512]{1,0:T(8,128)(2,1)S(1)} %collective-permute-done.5.w1_ref, ...), custom_call_target="tpu_custom_call" | custom-call | flops 1 | bytes 1 | tf_op jit(solution)/shard_map/pallas_call | solution.py:131
  29.2 1.5 %collective-permute-start.6 = (bf16[16,8192]{1,0:T(8,128)(2,1)S(1)}, bf16[16,8192]{1,0:T(8,128)(2,1)S(1)}, u32[]{:S(2)}, u32[]{:S(2)}) collective-permute-start(bf16[16,8192]{1,0:T(8,128)(2,1)S(1)} %get-tuple-element.35), channel_id=1, source_target_pairs={{0,1},{1,0},{2,3},{3,2},{4,5},{5,4},{6,7},{7,6},{8,9},{9,8},{10,11... | collective-permute-start | bytes 786440 | tf_op jit(solution)/shard_map/ppermute | solution.py:26
  30.8 0.5 collective-permute-start.16
  31.4 0.7 %collective-permute-done.15.refs_2_ = bf16[128,512]{1,0:T(8,128)(2,1)S(1)} collective-permute-done((bf16[128,512]{1,0:T(8,128)(2,1)S(1)}, bf16[128,512]{1,0:T(8,128)(2,1)S(1)}, u32[]{:S(2)}, u32[]{:S(2)}) %collective-permute-start.15) | collective-permute-done | bytes 131104 | tf_op jit(solution)/shard_map/ppermute | solution.py:26
  32.1 0.2 collective-permute-done.16.refs_3_
  32.3 0.5 shard_map.97
  32.9 1.3 %shard_map.98 = bf16[256,512]{1,0:T(8,128)(2,1)S(1)} custom-call(bf16[256,256]{1,0:T(8,128)(2,1)S(1)} %get-tuple-element.67.back_ref, f32[16,8192]{1,0:T(8,128)S(1)} %get-tuple-element.43.part_ref, bf16[16,8192]{1,0:T(8,128)(2,1)S(1)} %collective-permute-done.10.got_ref, bf16[16,8192]{1,0:T(8,128)(2,1)S(1)} %get-tuple-element.44.weights_ref, ...), custom_call_target="tpu_custom_call" | custom-call | flops 1 | bytes 1 | tf_op jit(solution)/shard_map/pallas_call | solution.py:131
  34.1 0.9 %collective-permute-start.20 = (bf16[256,512]{1,0:T(8,128)(2,1)S(1)}, bf16[256,512]{1,0:T(8,128)(2,1)S(1)}, u32[]{:S(2)}, u32[]{:S(2)}) collective-permute-start(bf16[256,512]{1,0:T(8,128)(2,1)S(1)} %shard_map.98), channel_id=1, source_target_pairs={{0,1},{1,0},{2,3},{3,2},{4,5},{5,4},{6,7},{7,6},{8,9},{9,8},{10,11... | collective-permute-start | bytes 786440 | tf_op jit(solution)/shard_map/ppermute | solution.py:26
  35.1 0.1 collective-permute-start.17
  35.2 0.5 collective-permute-start.18
  35.6 0.1 collective-permute-start.19
  35.7 0.8 %collective-permute-done.17.refs_3_ = bf16[128,512]{1,0:T(8,128)(2,1)S(1)} collective-permute-done((bf16[128,512]{1,0:T(8,128)(2,1)S(1)}, bf16[128,512]{1,0:T(8,128)(2,1)S(1)}, u32[]{:S(2)}, u32[]{:S(2)}) %collective-permute-start.17) | collective-permute-done | bytes 131104 | tf_op jit(solution)/shard_map/ppermute | solution.py:26
  36.5 0.2 collective-permute-done.18.refs_4_
  36.7 0.3 collective-permute-done.19.refs_5_
  37.0 0.7 %shard_map.99 = (f32[16,8192]{1,0:T(8,128)S(1)}, f32[16,8192]{1,0:T(8,128)S(1)}) custom-call(bf16[256,256]{1,0:T(8,128)(2,1)S(1)} %get-tuple-element.66.place_ref, bf16[128,512]{1,0:T(8,128)(2,1)S(1)} %get-tuple-element.61.refs_0_, bf16[128,512]{1,0:T(8,128)(2,1)S(1)} %get-tuple-element.60.refs_1_, bf16[128,512]{1,0:T(8,128)(2,1)S(1)} %get-tuple-element.59.refs_2_, ...), custom_call_target="tpu_custom_call" | custom-call | flops 1 | bytes 1 | tf_op jit(solution)/shard_map/pallas_call | solution.py:131
  37.7 0.4 collective-permute-done.6.got_ref
  38.0 1.8 %shard_map.100 = (bf16[256,512]{1,0:T(8,128)(2,1)S(1)}, bf16[256,512]{1,0:T(8,128)(2,1)S(1)}, bf16[16,8192]{1,0:T(8,128)(2,1)}) custom-call(bf16[256,256]{1,0:T(8,128)(2,1)S(1)} %get-tuple-element.67.back_ref, f32[16,8192]{1,0:T(8,128)S(1)} %get-tuple-element.34.part_ref, bf16[16,8192]{1,0:T(8,128)(2,1)S(1)} %collective-permute-done.6.got_ref, ...), custom_call_target="tpu_custom_call" | custom-call | flops 1 | bytes 1 | tf_op jit(solution)/shard_map/pallas_call | solution.py:131
  39.9 3.3 %collective-permute-done.20 = bf16[256,512]{1,0:T(8,128)(2,1)S(1)} collective-permute-done((bf16[256,512]{1,0:T(8,128)(2,1)S(1)}, bf16[256,512]{1,0:T(8,128)(2,1)S(1)}, u32[]{:S(2)}, u32[]{:S(2)}) %collective-permute-start.20) | collective-permute-done | bytes 262176 | tf_op jit(solution)/shard_map/ppermute | solution.py:26
  43.4 1.5 %collective-permute-done.21 = bf16[128,1024]{1,0:T(8,128)(2,1)S(1)} collective-permute-done((bf16[128,1024]{1,0:T(8,128)(2,1)S(1)}, bf16[128,1024]{1,0:T(8,128)(2,1)S(1)}, u32[]{:S(2)}, u32[]{:S(2)}) %collective-permute-start.21) | collective-permute-done | bytes 262176 | tf_op jit(solution)/shard_map/ppermute | solution.py:26
  45.0 0.8 %collective-permute-start.22 = (bf16[64,1024]{1,0:T(8,128)(2,1)S(1)}, bf16[64,1024]{1,0:T(8,128)(2,1)S(1)}, u32[]{:S(2)}, u32[]{:S(2)}) collective-permute-start(bf16[64,1024]{1,0:T(8,128)(2,1)S(1)} %slice.126), channel_id=1, source_target_pairs={{0,4},{2,6},{4,0},{6,2},{8,12},{10,14},{12,8},{14,10},{16,20},{18,... | collective-permute-start | bytes 393224 | tf_op jit(solution)/shard_map/ppermute | solution.py:26
  45.8 4.8 %collective-permute-done.22 = bf16[64,1024]{1,0:T(8,128)(2,1)S(1)} collective-permute-done((bf16[64,1024]{1,0:T(8,128)(2,1)S(1)}, bf16[64,1024]{1,0:T(8,128)(2,1)S(1)}, u32[]{:S(2)}, u32[]{:S(2)}) %collective-permute-start.22) | collective-permute-done | bytes 131104 | tf_op jit(solution)/shard_map/ppermute | solution.py:26
  50.7 1.2 %collective-permute-start.23 = (bf16[32,1024]{1,0:T(8,128)(2,1)S(1)}, bf16[32,1024]{1,0:T(8,128)(2,1)S(1)}, u32[]{:S(2)}, u32[]{:S(2)}) collective-permute-start(bf16[32,1024]{1,0:T(8,128)(2,1)S(1)} %slice.127), channel_id=1, source_target_pairs={{0,8},{2,10},{4,12},{6,14},{8,0},{10,2},{12,4},{14,6},{16,24},{18,... | collective-permute-start | bytes 196616 | tf_op jit(solution)/shard_map/ppermute | solution.py:26
  51.9 3.2 %collective-permute-done.23 = bf16[32,1024]{1,0:T(8,128)(2,1)S(1)} collective-permute-done((bf16[32,1024]{1,0:T(8,128)(2,1)S(1)}, bf16[32,1024]{1,0:T(8,128)(2,1)S(1)}, u32[]{:S(2)}, u32[]{:S(2)}) %collective-permute-start.23) | collective-permute-done | bytes 65568 | tf_op jit(solution)/shard_map/ppermute | solution.py:26
  55.1 2.7 %collective-permute-start.24 = (bf16[16,1024]{1,0:T(8,128)(2,1)S(1)}, bf16[16,1024]{1,0:T(8,128)(2,1)S(1)}, u32[]{:S(2)}, u32[]{:S(2)}) collective-permute-start(bf16[16,1024]{1,0:T(8,128)(2,1)S(1)} %slice.128), channel_id=1, source_target_pairs={{0,16},{2,18},{4,20},{6,22},{8,24},{10,26},{12,28},{14,30},{16,0},... | collective-permute-start | bytes 98312 | tf_op jit(solution)/shard_map/ppermute | solution.py:26
  57.7 2.2 %collective-permute-done.24 = bf16[16,1024]{1,0:T(8,128)(2,1)S(1)} collective-permute-done((bf16[16,1024]{1,0:T(8,128)(2,1)S(1)}, bf16[16,1024]{1,0:T(8,128)(2,1)S(1)}, u32[]{:S(2)}, u32[]{:S(2)}) %collective-permute-start.24) | collective-permute-done | bytes 32800 | tf_op jit(solution)/shard_map/ppermute | solution.py:26
  60.0 0.6 %fusion.7 = (f32[1,16,512]{2,1,0:T(8,128)}, f32[1,16,512]{2,1,0:T(8,128)}) fusion(f32[16,1024]{1,0:T(8,128)S(1)} %slice_add_fusion.2, f32[1,16,512]{2,1,0:T(8,128)S(1)} %copy-done.2, f32[1,16,512]{2,1,0:T(8,128)S(1)} %copy-done.6), kind=kLoop, calls=%fused_computation.41 | loop fusion | flops 73728 | bytes 196608 | tf_op jit(solution)/shard_map/broadcast_in_dim | solution.py:245
  (62 shorter events, 1.0 us)
Async XLA Ops:
  1.4 7.2 %collective-permute-start = (bf16[16,512]{1,0:T(8,128)(2,1)S(1)}, bf16[16,512]{1,0:T(8,128)(2,1)S(1)}, u32[]{:S(2)}, u32[]{:S(2)}) collective-permute-start(bf16[16,512]{1,0:T(8,128)(2,1)S(1)} %bitcast_convert_fusion), channel_id=1, source_target_pairs={{0,16},{2,18},{4,20},{6,22},{8,24},{10,26},{12,28},{14,30},{16,0},... | collective-permute-start | bytes 49160 | tf_op jit(solution)/shard_map/ppermute | solution.py:26
  5.4 0.8 %copy-start.1 = (f32[1,16,512]{2,1,0:T(8,128)S(1)}, f32[1,16,512]{2,1,0:T(8,128)}, u32[]{:S(2)}) copy-start(f32[1,16,512]{2,1,0:T(8,128)} %param.9) | copy-start | bytes 98308
  6.2 0.8 %copy-start.3 = (f32[1,16,512]{2,1,0:T(8,128)S(1)}, f32[1,16,512]{2,1,0:T(8,128)}, u32[]{:S(2)}) copy-start(f32[1,16,512]{2,1,0:T(8,128)} %param.8) | copy-start | bytes 98308
  7.0 4.8 %collective-permute-start.11 = (bf16[16,1024]{1,0:T(8,128)(2,1)S(1)}, bf16[16,1024]{1,0:T(8,128)(2,1)S(1)}, u32[]{:S(2)}, u32[]{:S(2)}) collective-permute-start(bf16[16,1024]{1,0:T(8,128)(2,1)S(1)} %get-tuple-element.45), channel_id=1, source_target_pairs={{0,1},{1,0},{2,3},{3,2},{4,5},{5,4},{6,7},{7,6},{8,9},{9,8},{10,11... | collective-permute-start | bytes 98312 | tf_op jit(solution)/shard_map/ppermute | solution.py:26
  8.6 4.6 %collective-permute-start.1 = (bf16[32,512]{1,0:T(8,128)(2,1)S(1)}, bf16[32,512]{1,0:T(8,128)(2,1)S(1)}, u32[]{:S(2)}, u32[]{:S(2)}) collective-permute-start(bf16[32,512]{1,0:T(8,128)(2,1)S(1)} %pad_maximum_fusion.7), channel_id=1, source_target_pairs={{0,8},{2,10},{4,12},{6,14},{8,0},{10,2},{12,4},{14,6},{16,24},{18,... | collective-permute-start | bytes 98312 | tf_op jit(solution)/shard_map/ppermute | solution.py:26
  10.1 9.7 %collective-permute-start.7 = (bf16[16,1536]{1,0:T(8,128)(2,1)S(1)}, bf16[16,1536]{1,0:T(8,128)(2,1)S(1)}, u32[]{:S(2)}, u32[]{:S(2)}) collective-permute-start(bf16[16,1536]{1,0:T(8,128)(2,1)S(1)} %get-tuple-element.39), channel_id=1, source_target_pairs={{0,16},{2,18},{4,20},{6,22},{8,24},{10,26},{12,28},{14,30},{16,0},... | collective-permute-start | bytes 147464 | tf_op jit(solution)/shard_map/ppermute | solution.py:26
  11.7 6.8 %collective-permute-start.12 = (bf16[16,1024]{1,0:T(8,128)(2,1)S(1)}, bf16[16,1024]{1,0:T(8,128)(2,1)S(1)}, u32[]{:S(2)}, u32[]{:S(2)}) collective-permute-start(bf16[16,1024]{1,0:T(8,128)(2,1)S(1)} %collective-permute-done.11), channel_id=1, source_target_pairs={{0,16},{2,18},{4,20},{6,22},{8,24},{10,26},{12,28},{14,30},{16,0},... | collective-permute-start | bytes 98312 | tf_op jit(solution)/shard_map/ppermute | solution.py:26
  13.1 5.0 %copy-start.7 = (s32[256]{0:T(256)S(1)}, s32[256]{0:T(256)}, u32[]{:S(2)}) copy-start(s32[256]{0:T(256)} %param.10) | copy-start | bytes 3076
  13.2 4.3 %collective-permute-start.2 = (bf16[64,512]{1,0:T(8,128)(2,1)S(1)}, bf16[64,512]{1,0:T(8,128)(2,1)S(1)}, u32[]{:S(2)}, u32[]{:S(2)}) collective-permute-start(bf16[64,512]{1,0:T(8,128)(2,1)S(1)} %pad_maximum_fusion.5), channel_id=1, source_target_pairs={{0,4},{2,6},{4,0},{6,2},{8,12},{10,14},{12,8},{14,10},{16,20},{18,... | collective-permute-start | bytes 196616 | tf_op jit(solution)/shard_map/ppermute | solution.py:26
  17.5 3.2 %collective-permute-start.3 = (bf16[128,512]{1,0:T(8,128)(2,1)S(1)}, bf16[128,512]{1,0:T(8,128)(2,1)S(1)}, u32[]{:S(2)}, u32[]{:S(2)}) collective-permute-start(bf16[128,512]{1,0:T(8,128)(2,1)S(1)} %pad_maximum_fusion.2.w0_ref), channel_id=1, source_target_pairs={{0,2},{2,0},{4,6},{6,4},{8,10},{10,8},{12,14},{14,12},{16,18},{18,... | collective-permute-start | bytes 393224 | tf_op jit(solution)/shard_map/ppermute | solution.py:26
  17.6 9.0 %collective-permute-start.4 = (bf16[128,512]{1,0:T(8,128)(2,1)S(1)}, bf16[128,512]{1,0:T(8,128)(2,1)S(1)}, u32[]{:S(2)}, u32[]{:S(2)}) collective-permute-start(bf16[128,512]{1,0:T(8,128)(2,1)S(1)} %pad_maximum_fusion.2.w0_ref), channel_id=1, source_target_pairs={{0,1},{1,0},{2,3},{3,2},{4,5},{5,4},{6,7},{7,6},{8,9},{9,8},{10,11... | collective-permute-start | bytes 393224 | tf_op jit(solution)/shard_map/ppermute | solution.py:26
  18.5 5.1 %collective-permute-start.13 = (bf16[32,1024]{1,0:T(8,128)(2,1)S(1)}, bf16[32,1024]{1,0:T(8,128)(2,1)S(1)}, u32[]{:S(2)}, u32[]{:S(2)}) collective-permute-start(bf16[32,1024]{1,0:T(8,128)(2,1)S(1)} %pad_maximum_fusion.6), channel_id=1, source_target_pairs={{0,8},{2,10},{4,12},{6,14},{8,0},{10,2},{12,4},{14,6},{16,24},{18,... | collective-permute-start | bytes 196616 | tf_op jit(solution)/shard_map/ppermute | solution.py:26
  19.9 5.3 %collective-permute-start.8 = (bf16[32,1536]{1,0:T(8,128)(2,1)S(1)}, bf16[32,1536]{1,0:T(8,128)(2,1)S(1)}, u32[]{:S(2)}, u32[]{:S(2)}) collective-permute-start(bf16[32,1536]{1,0:T(8,128)(2,1)S(1)} %pad_maximum_fusion.4), channel_id=1, source_target_pairs={{0,8},{2,10},{4,12},{6,14},{8,0},{10,2},{12,4},{14,6},{16,24},{18,... | collective-permute-start | bytes 294920 | tf_op jit(solution)/shard_map/ppermute | solution.py:26
  22.0 9.3 %copy-start.4 = (bf16[2,64,8192]{2,1,0:T(8,128)(2,1)S(1)}, bf16[2,64,8192]{2,1,0:T(8,128)(2,1)}, u32[]{:S(2)}) copy-start(bf16[2,64,8192]{2,1,0:T(8,128)(2,1)} %param.13) | copy-start | bytes 6291460
  22.0 10.8 %collective-permute-start.10 = (bf16[16,8192]{1,0:T(8,128)(2,1)S(1)}, bf16[16,8192]{1,0:T(8,128)(2,1)S(1)}, u32[]{:S(2)}, u32[]{:S(2)}) collective-permute-start(bf16[16,8192]{1,0:T(8,128)(2,1)S(1)} %get-tuple-element.41), channel_id=1, source_target_pairs={{0,1},{1,0},{2,3},{3,2},{4,5},{5,4},{6,7},{7,6},{8,9},{9,8},{10,11... | collective-permute-start | bytes 786440 | tf_op jit(solution)/shard_map/ppermute | solution.py:26
  23.6 7.0 %collective-permute-start.14 = (bf16[64,1024]{1,0:T(8,128)(2,1)S(1)}, bf16[64,1024]{1,0:T(8,128)(2,1)S(1)}, u32[]{:S(2)}, u32[]{:S(2)}) collective-permute-start(bf16[64,1024]{1,0:T(8,128)(2,1)S(1)} %pad_maximum_fusion.3), channel_id=1, source_target_pairs={{0,4},{2,6},{4,0},{6,2},{8,12},{10,14},{12,8},{14,10},{16,20},{18,... | collective-permute-start | bytes 393224 | tf_op jit(solution)/shard_map/ppermute | solution.py:26
  25.2 9.8 %collective-permute-start.9 = (bf16[64,1536]{1,0:T(8,128)(2,1)S(1)}, bf16[64,1536]{1,0:T(8,128)(2,1)S(1)}, u32[]{:S(2)}, u32[]{:S(2)}) collective-permute-start(bf16[64,1536]{1,0:T(8,128)(2,1)S(1)} %pad_maximum_fusion.1), channel_id=1, source_target_pairs={{0,4},{2,6},{4,0},{6,2},{8,12},{10,14},{12,8},{14,10},{16,20},{18,... | collective-permute-start | bytes 589832 | tf_op jit(solution)/shard_map/ppermute | solution.py:26
  26.6 1.3 %collective-permute-start.5 = (bf16[128,512]{1,0:T(8,128)(2,1)S(1)}, bf16[128,512]{1,0:T(8,128)(2,1)S(1)}, u32[]{:S(2)}, u32[]{:S(2)}) collective-permute-start(bf16[128,512]{1,0:T(8,128)(2,1)S(1)} %collective-permute-done.4.w0_ref), channel_id=1, source_target_pairs={{0,2},{2,0},{4,6},{6,4},{8,10},{10,8},{12,14},{14,12},{16,18},{18,... | collective-permute-start | bytes 393224 | tf_op jit(solution)/shard_map/ppermute | solution.py:26
  26.6 4.8 %copy-start.5 = (bf16[2,64,8192]{2,1,0:T(8,128)(2,1)S(1)}, bf16[2,64,8192]{2,1,0:T(8,128)(2,1)}, u32[]{:S(2)}) copy-start(bf16[2,64,8192]{2,1,0:T(8,128)(2,1)} %param.12) | copy-start | bytes 6291460
  29.2 8.8 %collective-permute-start.6 = (bf16[16,8192]{1,0:T(8,128)(2,1)S(1)}, bf16[16,8192]{1,0:T(8,128)(2,1)S(1)}, u32[]{:S(2)}, u32[]{:S(2)}) collective-permute-start(bf16[16,8192]{1,0:T(8,128)(2,1)S(1)} %get-tuple-element.35), channel_id=1, source_target_pairs={{0,1},{1,0},{2,3},{3,2},{4,5},{5,4},{6,7},{7,6},{8,9},{9,8},{10,11... | collective-permute-start | bytes 786440 | tf_op jit(solution)/shard_map/ppermute | solution.py:26
  30.7 1.4 %collective-permute-start.15 = (bf16[128,512]{1,0:T(8,128)(2,1)S(1)}, bf16[128,512]{1,0:T(8,128)(2,1)S(1)}, u32[]{:S(2)}, u32[]{:S(2)}) collective-permute-start(bf16[128,512]{1,0:T(8,128)(2,1)S(1)} %get-tuple-element.63.refs_0_), channel_id=1, source_target_pairs={{0,2},{2,0},{4,6},{6,4},{8,10},{10,8},{12,14},{14,12},{16,18},{18,... | collective-permute-start | bytes 393224 | tf_op jit(solution)/shard_map/ppermute | solution.py:26
  30.8 1.5 %collective-permute-start.16 = (bf16[128,512]{1,0:T(8,128)(2,1)S(1)}, bf16[128,512]{1,0:T(8,128)(2,1)S(1)}, u32[]{:S(2)}, u32[]{:S(2)}) collective-permute-start(bf16[128,512]{1,0:T(8,128)(2,1)S(1)} %get-tuple-element.62.refs_1_), channel_id=1, source_target_pairs={{0,2},{2,0},{4,6},{6,4},{8,10},{10,8},{12,14},{14,12},{16,18},{18,... | collective-permute-start | bytes 393224 | tf_op jit(solution)/shard_map/ppermute | solution.py:26
  34.1 3.9 %copy-start = (bf16[1,2,8,8192]{3,2,1,0:T(8,128)(2,1)S(1)}, bf16[1,2,8,8192]{3,2,1,0:T(8,128)(2,1)}, u32[]{:S(2)}) copy-start(bf16[1,2,8,8192]{3,2,1,0:T(8,128)(2,1)} %param.11) | copy-start | bytes 786436
  34.1 9.1 %collective-permute-start.20 = (bf16[256,512]{1,0:T(8,128)(2,1)S(1)}, bf16[256,512]{1,0:T(8,128)(2,1)S(1)}, u32[]{:S(2)}, u32[]{:S(2)}) collective-permute-start(bf16[256,512]{1,0:T(8,128)(2,1)S(1)} %shard_map.98), channel_id=1, source_target_pairs={{0,1},{1,0},{2,3},{3,2},{4,5},{5,4},{6,7},{7,6},{8,9},{9,8},{10,11... | collective-permute-start | bytes 786440 | tf_op jit(solution)/shard_map/ppermute | solution.py:26
  35.1 1.4 %collective-permute-start.17 = (bf16[128,512]{1,0:T(8,128)(2,1)S(1)}, bf16[128,512]{1,0:T(8,128)(2,1)S(1)}, u32[]{:S(2)}, u32[]{:S(2)}) collective-permute-start(bf16[128,512]{1,0:T(8,128)(2,1)S(1)} %get-tuple-element.61.refs_0_), channel_id=1, source_target_pairs={{0,2},{2,0},{4,6},{6,4},{8,10},{10,8},{12,14},{14,12},{16,18},{18,... | collective-permute-start | bytes 393224 | tf_op jit(solution)/shard_map/ppermute | solution.py:26
  35.2 1.5 %collective-permute-start.18 = (bf16[128,512]{1,0:T(8,128)(2,1)S(1)}, bf16[128,512]{1,0:T(8,128)(2,1)S(1)}, u32[]{:S(2)}, u32[]{:S(2)}) collective-permute-start(bf16[128,512]{1,0:T(8,128)(2,1)S(1)} %get-tuple-element.60.refs_1_), channel_id=1, source_target_pairs={{0,2},{2,0},{4,6},{6,4},{8,10},{10,8},{12,14},{14,12},{16,18},{18,... | collective-permute-start | bytes 393224 | tf_op jit(solution)/shard_map/ppermute | solution.py:26
  35.6 1.3 %collective-permute-start.19 = (bf16[128,512]{1,0:T(8,128)(2,1)S(1)}, bf16[128,512]{1,0:T(8,128)(2,1)S(1)}, u32[]{:S(2)}, u32[]{:S(2)}) collective-permute-start(bf16[128,512]{1,0:T(8,128)(2,1)S(1)} %get-tuple-element.59.refs_2_), channel_id=1, source_target_pairs={{0,2},{2,0},{4,6},{6,4},{8,10},{10,8},{12,14},{14,12},{16,18},{18,... | collective-permute-start | bytes 393224 | tf_op jit(solution)/shard_map/ppermute | solution.py:26
  43.3 16.7 %copy-start.2 = (f32[1,16,512]{2,1,0:T(8,128)S(1)}, f32[1,16,512]{2,1,0:T(8,128)}, u32[]{:S(2)}) copy-start(f32[1,16,512]{2,1,0:T(8,128)} %param.9) | copy-start | bytes 98308
  43.3 16.7 %copy-start.6 = (f32[1,16,512]{2,1,0:T(8,128)S(1)}, f32[1,16,512]{2,1,0:T(8,128)}, u32[]{:S(2)}) copy-start(f32[1,16,512]{2,1,0:T(8,128)} %param.7) | copy-start | bytes 98308
  43.4 1.6 %collective-permute-start.21 = (bf16[128,1024]{1,0:T(8,128)(2,1)S(1)}, bf16[128,1024]{1,0:T(8,128)(2,1)S(1)}, u32[]{:S(2)}, u32[]{:S(2)}) collective-permute-start(bf16[128,1024]{1,0:T(8,128)(2,1)S(1)} %fusion.2), channel_id=1, source_target_pairs={{0,2},{2,0},{4,6},{6,4},{8,10},{10,8},{12,14},{14,12},{16,18},{18,... | collective-permute-start | bytes 786440 | tf_op jit(solution)/shard_map/ppermute | solution.py:26
  45.0 5.6 %collective-permute-start.22 = (bf16[64,1024]{1,0:T(8,128)(2,1)S(1)}, bf16[64,1024]{1,0:T(8,128)(2,1)S(1)}, u32[]{:S(2)}, u32[]{:S(2)}) collective-permute-start(bf16[64,1024]{1,0:T(8,128)(2,1)S(1)} %slice.126), channel_id=1, source_target_pairs={{0,4},{2,6},{4,0},{6,2},{8,12},{10,14},{12,8},{14,10},{16,20},{18,... | collective-permute-start | bytes 393224 | tf_op jit(solution)/shard_map/ppermute | solution.py:26
  50.7 4.3 %collective-permute-start.23 = (bf16[32,1024]{1,0:T(8,128)(2,1)S(1)}, bf16[32,1024]{1,0:T(8,128)(2,1)S(1)}, u32[]{:S(2)}, u32[]{:S(2)}) collective-permute-start(bf16[32,1024]{1,0:T(8,128)(2,1)S(1)} %slice.127), channel_id=1, source_target_pairs={{0,8},{2,10},{4,12},{6,14},{8,0},{10,2},{12,4},{14,6},{16,24},{18,... | collective-permute-start | bytes 196616 | tf_op jit(solution)/shard_map/ppermute | solution.py:26
  55.1 4.9 %collective-permute-start.24 = (bf16[16,1024]{1,0:T(8,128)(2,1)S(1)}, bf16[16,1024]{1,0:T(8,128)(2,1)S(1)}, u32[]{:S(2)}, u32[]{:S(2)}) collective-permute-start(bf16[16,1024]{1,0:T(8,128)(2,1)S(1)} %slice.128), channel_id=1, source_target_pairs={{0,16},{2,18},{4,20},{6,22},{8,24},{10,26},{12,28},{14,30},{16,0},... | collective-permute-start | bytes 98312 | tf_op jit(solution)/shard_map/ppermute | solution.py:26

commit v5 on v4

--- a/solution.py
+++ b/solution.py
@@ -85,13 +85,20 @@
         rate_ref[:, at] = rate[c * rows : (c + 1) * rows]
 
 
+def store_flat(back_ref, seg_ref, refs):
+    flat = dot(back_ref[...], seg_ref[...]).astype(BF)
+    count = flat.shape[0] // len(refs)
+    for i, ref in enumerate(refs):
+        ref[...] = flat[i * count : (i + 1) * count]
+
+
 def second_kernel(
     hidden_rows, up_scale, own, back_ref, part_ref, got_ref, weights_ref, moment_ref, rate_ref, x_ref, g_ref, *rest
 ):
     if own:
-        feedback_ref, grad_ref, packed_ref, error_ref, local_ref, seg_ref = rest
+        feedback_ref, *flat_refs, error_ref, local_ref, seg_ref = rest
     else:
-        grad_ref, local_ref, seg_ref = rest
+        *flat_refs, local_ref, seg_ref = rest
     rows = 2 * hidden_rows
     segment = seg_ref.shape[1]
     width = x_ref.shape[1]
@@ -101,7 +108,7 @@
     columns = gradient_rows(local_ref[...], x_ref, g_ref, hidden_rows, up_scale)
     for c in range(width // segment):
         seg_ref[c * rows : (c + 1) * rows] = columns(slice(c * segment, (c + 1) * segment)).astype(BF)
-    grad_ref[...] = dot(back_ref[...], seg_ref[...]).astype(BF)
+    store_flat(back_ref, seg_ref, flat_refs[:2] if own else flat_refs)
     if own:
         shifted = local_moment + feedback_ref[...].astype(F32)
         magnitude = jnp.sum(jnp.abs(shifted), axis=1, keepdims=True) * (1.0 / width) + 1e-06
@@ -109,11 +116,12 @@
         error_ref[...] = (shifted - packed).astype(BF)
         for c in range(width // segment):
             seg_ref[c * rows : (c + 1) * rows] = packed[:, c * segment : (c + 1) * segment].astype(BF)
-        packed_ref[...] = dot(back_ref[...], seg_ref[...]).astype(BF)
-
-
-def split_kernel(moment_ref, variance_ref, own_ref, near_ref):
-    segment = moment_ref.shape[1]
+        store_flat(back_ref, seg_ref, flat_refs[2:])
+
+
+def cast_kernel(master_ref, moment_ref, variance_ref, weights_ref, own_ref, near_ref):
+    segment = master_ref.shape[1]
+    weights_ref[...] = master_ref[...].astype(BF)
     high = moment_ref[...].astype(BF)
     spread = variance_ref[...].astype(BF)
     own_ref[:, :segment] = high
@@ -151,31 +159,32 @@
     mp_bits = bits_of(n_mp)
     shape = jax.ShapeDtypeStruct
 
-    near_w = master[0].astype(BF)
-    own_a, near_a = call(
-        split_kernel,
-        (shape((span, 3 * segment), BF), shape((span, 2 * segment), BF)),
-        (after(moment[0], near_w), variance[0]),
+    near_w, own_a, near_a = call(
+        cast_kernel,
+        tuple(shape((span, terms * segment), BF) for terms in (1, 3, 2)),
+        (master[0], moment[0], variance[0]),
     )
+
+    owner = (flat_slot // span) ^ me
+    position = jnp.zeros_like(owner)
+    for place, mask in enumerate(far + [1]):
+        position = position + jnp.where((owner & mask) != 0, 1 << place, 0)
+    position = position * span + flat_slot % span
+    position = position.reshape(rows, width // segment).T.reshape(segments)
+
     steps = []
     for mask in far:
         near_w = jnp.concatenate([near_w, swap(near_w, "dp", mask)], axis=0)
         steps.append(near_w)
-    others = [near_a]
+    others = [after(near_a, position)]
     for mask in reversed(mp_bits):
         others = others + [swap(b, "mp", mask) for b in others]
-    blocks_a = [after(own_a, steps[0])] + others[1:]
-
-    slot = after(flat_slot, steps[-1])
-    owner = (slot // span) ^ me
-    position = jnp.zeros_like(owner)
-    for place, mask in enumerate(far + [1]):
-        position = position + jnp.where((owner & mask) != 0, 1 << place, 0)
-    position = position * span + slot % span
-    position = position.reshape(rows, width // segment).T.reshape(segments)
+    all_a = jnp.concatenate([own_a] + others[1:], axis=1)
+
     line = jnp.arange(segments, dtype=jnp.int32)
-    place_map = (position[:, None] == line[None, :]).astype(BF)
-    back_map = (line[:, None] == position[None, :]).astype(BF)
+    spot = after(position, steps[-1])
+    place_map = (spot[:, None] == line[None, :]).astype(BF)
+    back_map = (line[:, None] == spot[None, :]).astype(BF)
 
     blocks_w = [near_w]
     for mask in reversed(mp_bits):
@@ -203,11 +212,15 @@
         got = [crossed[k ^ mask] for k in range(n_mp)]
 
     for mask, event in zip(far[:-1], [steps[-1]] * (len(far) - 2) + [sent[0]]):
-        arrived = [after(swap(b, "dp", mask), event) for b in blocks_a]
-        blocks_a = [jnp.concatenate(pair, axis=0) for pair in zip(blocks_a, arrived)]
-    arrived = [swap(b, "dp", far[-1]) for b in blocks_a]
-
-    grads, event = [None] * n_mp, sent[-1]
+        all_a = jnp.concatenate([all_a, after(swap(all_a, "dp", mask), event)], axis=0)
+    ends = [0] + [(3 + 2 * k) * segment for k in range(n_mp)]
+    blocks_a = [all_a[:, ends[k] : ends[k + 1]] for k in range(n_mp)]
+    arrived = [None] * n_mp
+    for k in reversed(range(n_mp)):
+        arrived[k] = swap(blocks_a[k], "dp", far[-1])
+
+    half = segments // 2
+    kept, away, event = [None] * n_mp, [None] * n_mp, sent[-1]
     for k in reversed(range(n_mp)):
         own = k == 0
         block = jnp.concatenate([blocks_a[k], after(arrived[k], event)], axis=0)
@@ -217,28 +230,38 @@
             functools.partial(moments_kernel, rows), (shape(tensor, F32), shape(tensor, F32)), (place_map, *terms)
         )
         operands = [back_map, parts[k], got[k], weights[k], moment_t, rate, *two]
-        out = [shape((segments, segment), BF)]
+        out = [shape((half, segment), BF)] * (4 if own else 2)
         if own:
             operands.append(feedback[0].reshape(tensor))
-            out += [shape((segments, segment), BF), shape(tensor, BF)]
+            out.append(shape(tensor, BF))
         result = call(
             functools.partial(second_kernel, hidden_rows, up_scale, own),
             tuple(out),
             operands,
             [pltpu.VMEM(tensor, BF), pltpu.VMEM((segments, segment), BF)],
         )
-        grads[k] = result[0]
-        event = grads[k]
-    packed, error = result[1:]
+        kept[k], away[k] = result[:2]
+        event = kept[k]
+    packed = result[2].astype(F32) + swap(result[3], "dp", 1).astype(F32)
+    error = result[4]
+
     for mask in mp_bits:
-        crossing = [p.astype(BF) for p in grads[mask:]]
-        grads = [p.astype(F32) + swap(q, "mp", mask).astype(F32) for p, q in zip(grads, crossing)]
-    last = jnp.concatenate([grads[0], packed.astype(F32)], axis=1)
-    for mask in [1] + far[::-1]:
-        count = last.shape[0] // 2
-        last = last[:count] + swap(last[count:].astype(BF), "dp", mask).astype(F32)
-    mean_grad = last[:, :segment] / n_dp
-    mean_moment = last[:, segment:] / n_dp
+        away_got = [swap(p.astype(BF), "mp", mask) for p in away[mask:]]
+        kept_got = [swap(p.astype(BF), "mp", mask) for p in kept[mask:]]
+        away = [p.astype(F32) + q.astype(F32) for p, q in zip(away, away_got)]
+        kept = [p.astype(F32) + q.astype(F32) for p, q in zip(kept, kept_got)]
+    grad = kept[0] + swap(away[0].astype(BF), "dp", 1).astype(F32)
+
+    def over_chips(total):
+        for mask in far[::-1]:
+            count = total.shape[0] // 2
+            total = total[:count] + swap(total[count:].astype(BF), "dp", mask).astype(F32)
+        return total
+
+    own_packed = over_chips(packed)
+    own_grad = over_chips(grad)
+    mean_grad = own_grad / n_dp
+    mean_moment = own_packed / n_dp
     moment_new = beta_one * mean_moment + (1.0 - beta_one) * mean_grad
     denominator = jnp.sqrt(variance[0]) + epsilon
     master_new = master[0] - step_rate * (mean_moment + moment_new) / denominator

time: 61 us -> 60.2 us (0.987)
  waiting for transfers between devices: 19.9 us -> 15.2 us
  starting transfers between devices: 27.3 us -> 30.7 us
  local copies, waits for them, and re-layouts: 3.78 us -> 4.43 us
    ppermute x25 -> x28, waiting for transfers between devices: 19.9 us -> 15.2 us  [swap(): return lax.ppermute(x, axis, [(i, i ^ mask) for i in range(n)])]
    ppermute x25 -> x28, starting transfers between devices: 27.3 us -> 30.7 us  [swap(): return lax.ppermute(x, axis, [(i, i ^ mask) for i in range(n)])]
    convert_element_type x3 -> x2, other arithmetic: 0.92 us -> 0.13 us  [the longest x1 0.1 us: per_device(): place_map = (spot[:, None] == line[None, :]).astype(BF)]
    unnamed x22 -> x19, local copies, waits for them, and re-layouts: 1.58 us -> 2.3 us
    add x6 -> x7, other arithmetic: 0.19 us -> 0.82 us  [the longest x1 0.7 us: per_device(): position = position * span + flat_slot % span]
  transfers between devices with their start and end apart: 25 -> 28, of which waited for: 13 -> 15; matrix products, arithmetic and copies ran while one was open for 4% -> 5% of each run, Pallas kernels for 11% -> 11%
where the time goes in v5:
time: 60.2 us; the launch traced here: 59.9 us
  starting transfers between devices  30.7 us (51%)
  waiting for transfers between devices  15.2 us (25%)
  Pallas kernels  6.82 us (11%)
  local copies, waits for them, and re-layouts  4.43 us (7%)
  other arithmetic  1.71 us (3%)
  between operations  0.94 us (2%)
    ppermute x28, starting transfers between devices, swap(): return lax.ppermute(x, axis, [(i, i ^ mask) for i in range(n)])  30.7 us
    ppermute x28, waiting for transfers between devices, swap(): return lax.ppermute(x, axis, [(i, i ^ mask) for i in range(n)])  15.2 us
    pallas_call x7, Pallas kernels, call(): pl.pallas_call(kernel, out_shape=out_shape, in_specs=[pl.BlockSpec(memory...  6.82 us
    unnamed x19, local copies, waits for them, and re-layouts  2.3 us
    squeeze x3, local copies, waits for them, and re-layouts, tokens_of(): x[step]  1.81 us
  transfers between devices with their start and end apart: 28, of which 15 were waited for; matrix products, arithmetic and copies ran while one was open for 5% of the time, Pallas kernels for 11%

profile of v5, /device:TPU:0, one launch (start us, length us, event | category | flops | bytes accessed | tf_op | source)
XLA Modules:
  0.0 59.9 jit_solution(12243637142290958828)
XLA Ops:
  0.6 0.7 %copy-done.1 = f32[1,16,512]{2,1,0:T(8,128)S(1)} copy-done((f32[1,16,512]{2,1,0:T(8,128)S(1)}, f32[1,16,512]{2,1,0:T(8,128)}, u32[]{:S(2)}) %copy-start.1) | copy-done | bytes 32792
  1.4 0.8 %copy-done.3 = f32[1,16,512]{2,1,0:T(8,128)S(1)} copy-done((f32[1,16,512]{2,1,0:T(8,128)S(1)}, f32[1,16,512]{2,1,0:T(8,128)}, u32[]{:S(2)}) %copy-start.3) | copy-done | bytes 32792
  2.2 0.8 %copy-done.5 = f32[1,16,512]{2,1,0:T(8,128)S(1)} copy-done((f32[1,16,512]{2,1,0:T(8,128)S(1)}, f32[1,16,512]{2,1,0:T(8,128)}, u32[]{:S(2)}) %copy-start.5) | copy-done | bytes 32792
  2.9 4.1 %collective-permute-start = (bf16[16,512]{1,0:T(8,128)(2,1)S(1)}, bf16[16,512]{1,0:T(8,128)(2,1)S(1)}, u32[]{:S(2)}, u32[]{:S(2)}) collective-permute-start(bf16[16,512]{1,0:T(8,128)(2,1)S(1)} %get-tuple-element.33), channel_id=1, source_target_pairs={{0,16},{2,18},{4,20},{6,22},{8,24},{10,26},{12,28},{14,30},{16,0},... | collective-permute-start | bytes 49160 | tf_op jit(solution)/shard_map/ppermute | solution.py:26
  7.0 0.7 %fusion.10 = s32[256]{0:T(256)S(1)} fusion(s32[256]{0:T(256)} %param.10, s32[]{:T(128)S(6)} %axis_index.15), kind=kLoop, calls=%fused_computation.62 | loop fusion | flops 9472 | bytes 2052 | tf_op jit(solution)/shard_map/add | solution.py:172
  8.0 1.5 %collective-permute-start.7 = (bf16[16,1024]{1,0:T(8,128)(2,1)S(1)}, bf16[16,1024]{1,0:T(8,128)(2,1)S(1)}, u32[]{:S(2)}, u32[]{:S(2)}) collective-permute-start(bf16[16,1024]{1,0:T(8,128)(2,1)S(1)} %get-tuple-element.42), channel_id=1, source_target_pairs={{0,1},{1,0},{2,3},{3,2},{4,5},{5,4},{6,7},{7,6},{8,9},{9,8},{10,11... | collective-permute-start | bytes 98312 | tf_op jit(solution)/shard_map/ppermute | solution.py:26
  9.5 1.6 %collective-permute-start.1 = (bf16[32,512]{1,0:T(8,128)(2,1)S(1)}, bf16[32,512]{1,0:T(8,128)(2,1)S(1)}, u32[]{:S(2)}, u32[]{:S(2)}) collective-permute-start(bf16[32,512]{1,0:T(8,128)(2,1)S(1)} %pad_maximum_fusion.5), channel_id=1, source_target_pairs={{0,8},{2,10},{4,12},{6,14},{8,0},{10,2},{12,4},{14,6},{16,24},{18,... | collective-permute-start | bytes 98312 | tf_op jit(solution)/shard_map/ppermute | solution.py:26
  11.2 0.7 %collective-permute-done.7 = bf16[16,1024]{1,0:T(8,128)(2,1)S(1)} collective-permute-done((bf16[16,1024]{1,0:T(8,128)(2,1)S(1)}, bf16[16,1024]{1,0:T(8,128)(2,1)S(1)}, u32[]{:S(2)}, u32[]{:S(2)}) %collective-permute-start.7) | collective-permute-done | bytes 32800 | tf_op jit(solution)/shard_map/ppermute | solution.py:26
  11.9 1.5 %collective-permute-start.8 = (bf16[16,2560]{1,0:T(8,128)(2,1)S(1)}, bf16[16,2560]{1,0:T(8,128)(2,1)S(1)}, u32[]{:S(2)}, u32[]{:S(2)}) collective-permute-start(bf16[16,2560]{1,0:T(8,128)(2,1)S(1)} %constant_dynamic-update-slice_fusion.7), channel_id=1, source_target_pairs={{0,16},{2,18},{4,20},{6,22},{8,24},{10,26},{12,28},{14,30},{16,0},... | collective-permute-start | bytes 245768 | tf_op jit(solution)/shard_map/ppermute | solution.py:26
  13.5 1.5 %collective-permute-start.2 = (bf16[64,512]{1,0:T(8,128)(2,1)S(1)}, bf16[64,512]{1,0:T(8,128)(2,1)S(1)}, u32[]{:S(2)}, u32[]{:S(2)}) collective-permute-start(bf16[64,512]{1,0:T(8,128)(2,1)S(1)} %get-tuple-element.70), channel_id=1, source_target_pairs={{0,4},{2,6},{4,0},{6,2},{8,12},{10,14},{12,8},{14,10},{16,20},{18,... | collective-permute-start | bytes 196616 | tf_op jit(solution)/shard_map/ppermute | solution.py:26
  15.0 1.7 %slice_bitcast_fusion.2 = (bf16[64,8192]{1,0:T(8,128)(2,1)S(1)}, bf16[64,8192]{1,0:T(8,128)(2,1)S(1)}) fusion(bf16[2,64,8192]{2,1,0:T(8,128)(2,1)} %param.13, bf16[2,64,8192]{2,1,0:T(8,128)(2,1)} %param.12), kind=kLoop, calls=%fused_computation.2 | loop fusion | bytes 4194304 | tf_op jit(solution)/shard_map/squeeze | solution.py:135
  16.7 1.1 %collective-permute-done.2 = bf16[64,512]{1,0:T(8,128)(2,1)S(1)} collective-permute-done((bf16[64,512]{1,0:T(8,128)(2,1)S(1)}, bf16[64,512]{1,0:T(8,128)(2,1)S(1)}, u32[]{:S(2)}, u32[]{:S(2)}) %collective-permute-start.2) | collective-permute-done | bytes 65568 | tf_op jit(solution)/shard_map/ppermute | solution.py:26
  17.8 1.5 %collective-permute-start.4 = (bf16[128,512]{1,0:T(8,128)(2,1)S(1)}, bf16[128,512]{1,0:T(8,128)(2,1)S(1)}, u32[]{:S(2)}, u32[]{:S(2)}) collective-permute-start(bf16[128,512]{1,0:T(8,128)(2,1)S(1)} %constant_dynamic-update-slice_fusion.3.w0_ref), channel_id=1, source_target_pairs={{0,1},{1,0},{2,3},{3,2},{4,5},{5,4},{6,7},{7,6},{8,9},{9,8},{10,11... | collective-permute-start | bytes 393224 | tf_op jit(solution)/shard_map/ppermute | solution.py:26
  19.3 1.4 %collective-permute-start.9 = (bf16[32,2560]{1,0:T(8,128)(2,1)S(1)}, bf16[32,2560]{1,0:T(8,128)(2,1)S(1)}, u32[]{:S(2)}, u32[]{:S(2)}) collective-permute-start(bf16[32,2560]{1,0:T(8,128)(2,1)S(1)} %pad_maximum_fusion.1), channel_id=1, source_target_pairs={{0,8},{2,10},{4,12},{6,14},{8,0},{10,2},{12,4},{14,6},{16,24},{18,... | collective-permute-start | bytes 491528 | tf_op jit(solution)/shard_map/ppermute | solution.py:26
  20.8 1.3 %shard_map.95 = (bf16[16,8192]{1,0:T(8,128)(2,1)S(1)}, f32[16,8192]{1,0:T(8,128)S(1)}, bf16[16,8192]{1,0:T(8,128)(2,1)S(1)}) custom-call(bf16[256,256]{1,0:T(8,128)(2,1)S(1)} %get-tuple-element.76.place_ref, bf16[128,512]{1,0:T(8,128)(2,1)S(1)} %constant_dynamic-update-slice_fusion.3.w0_ref, bf16[128,512]{1,0:T(8,128)(2,1)S(1)} %collective-permute-done.3.w1_ref, ...), custom_call_target="tpu_custom_call" | custom-call | flops 1 | bytes 1 | tf_op jit(solution)/shard_map/pallas_call | solution.py:139
  22.1 1.2 %collective-permute-start.11 = (bf16[16,8192]{1,0:T(8,128)(2,1)S(1)}, bf16[16,8192]{1,0:T(8,128)(2,1)S(1)}, u32[]{:S(2)}, u32[]{:S(2)}) collective-permute-start(bf16[16,8192]{1,0:T(8,128)(2,1)S(1)} %get-tuple-element.44), channel_id=1, source_target_pairs={{0,1},{1,0},{2,3},{3,2},{4,5},{5,4},{6,7},{7,6},{8,9},{9,8},{10,11... | collective-permute-start | bytes 786440 | tf_op jit(solution)/shard_map/ppermute | solution.py:26
  23.3 0.3 collective-permute-done.4.w0_ref
  23.7 2.0 %collective-permute-done.9 = bf16[32,2560]{1,0:T(8,128)(2,1)S(1)} collective-permute-done((bf16[32,2560]{1,0:T(8,128)(2,1)S(1)}, bf16[32,2560]{1,0:T(8,128)(2,1)S(1)}, u32[]{:S(2)}, u32[]{:S(2)}) %collective-permute-start.9) | collective-permute-done | bytes 163872 | tf_op jit(solution)/shard_map/ppermute | solution.py:26
  25.7 1.6 %collective-permute-start.12 = (bf16[64,1024]{1,0:T(8,128)(2,1)S(1)}, bf16[64,1024]{1,0:T(8,128)(2,1)S(1)}, u32[]{:S(2)}, u32[]{:S(2)}) collective-permute-start(bf16[64,1024]{1,0:T(8,128)(2,1)S(1)} %pad_maximum_fusion.4), channel_id=1, source_target_pairs={{0,4},{2,6},{4,0},{6,2},{8,12},{10,14},{12,8},{14,10},{16,20},{18,... | collective-permute-start | bytes 393224 | tf_op jit(solution)/shard_map/ppermute | solution.py:26
  27.3 0.6 %collective-permute-start.10 = (bf16[64,1536]{1,0:T(8,128)(2,1)S(1)}, bf16[64,1536]{1,0:T(8,128)(2,1)S(1)}, u32[]{:S(2)}, u32[]{:S(2)}) collective-permute-start(bf16[64,1536]{1,0:T(8,128)(2,1)S(1)} %slice.98), channel_id=1, source_target_pairs={{0,4},{2,6},{4,0},{6,2},{8,12},{10,14},{12,8},{14,10},{16,20},{18,... | collective-permute-start | bytes 589832 | tf_op jit(solution)/shard_map/ppermute | solution.py:26
  27.9 1.3 %shard_map.96 = (bf16[16,8192]{1,0:T(8,128)(2,1)S(1)}, f32[16,8192]{1,0:T(8,128)S(1)}, bf16[16,8192]{1,0:T(8,128)(2,1)S(1)}) custom-call(bf16[256,256]{1,0:T(8,128)(2,1)S(1)} %get-tuple-element.76.place_ref, bf16[128,512]{1,0:T(8,128)(2,1)S(1)} %collective-permute-done.4.w0_ref, bf16[128,512]{1,0:T(8,128)(2,1)S(1)} %collective-permute-done.5.w1_ref, ...), custom_call_target="tpu_custom_call" | custom-call | flops 1 | bytes 1 | tf_op jit(solution)/shard_map/pallas_call | solution.py:139
  29.2 0.8 %collective-permute-start.6 = (bf16[16,8192]{1,0:T(8,128)(2,1)S(1)}, bf16[16,8192]{1,0:T(8,128)(2,1)S(1)}, u32[]{:S(2)}, u32[]{:S(2)}) collective-permute-start(bf16[16,8192]{1,0:T(8,128)(2,1)S(1)} %get-tuple-element.38), channel_id=1, source_target_pairs={{0,1},{1,0},{2,3},{3,2},{4,5},{5,4},{6,7},{7,6},{8,9},{9,8},{10,11... | collective-permute-start | bytes 786440 | tf_op jit(solution)/shard_map/ppermute | solution.py:26
  30.0 2.2 %collective-permute-done.12 = bf16[64,1024]{1,0:T(8,128)(2,1)S(1)} collective-permute-done((bf16[64,1024]{1,0:T(8,128)(2,1)S(1)}, bf16[64,1024]{1,0:T(8,128)(2,1)S(1)}, u32[]{:S(2)}, u32[]{:S(2)}) %collective-permute-start.12) | collective-permute-done | bytes 131104 | tf_op jit(solution)/shard_map/ppermute | solution.py:26
  32.3 0.5 collective-permute-start.14
  32.9 0.8 %collective-permute-done.13.refs_2_ = bf16[128,512]{1,0:T(8,128)(2,1)S(1)} collective-permute-done((bf16[128,512]{1,0:T(8,128)(2,1)S(1)}, bf16[128,512]{1,0:T(8,128)(2,1)S(1)}, u32[]{:S(2)}, u32[]{:S(2)}) %collective-permute-start.13) | collective-permute-done | bytes 131104 | tf_op jit(solution)/shard_map/ppermute | solution.py:26
  33.7 0.2 collective-permute-done.14.refs_3_
  33.8 0.5 shard_map.97
  34.4 1.3 %shard_map.98 = (bf16[128,512]{1,0:T(8,128)(2,1)S(1)}, bf16[128,512]{1,0:T(8,128)(2,1)S(1)}) custom-call(bf16[256,256]{1,0:T(8,128)(2,1)S(1)} %get-tuple-element.77.back_ref, f32[16,8192]{1,0:T(8,128)S(1)} %get-tuple-element.46.part_ref, bf16[16,8192]{1,0:T(8,128)(2,1)S(1)} %collective-permute-done.11.got_ref, ...), custom_call_target="tpu_custom_call" | custom-call | flops 1 | bytes 1 | tf_op jit(solution)/shard_map/pallas_call | solution.py:139
  35.7 0.4 collective-permute-start.15
  36.3 0.3 collective-permute-start.17
  36.6 0.7 %collective-permute-start.23 = (bf16[128,512]{1,0:T(8,128)(2,1)S(1)}, bf16[128,512]{1,0:T(8,128)(2,1)S(1)}, u32[]{:S(2)}, u32[]{:S(2)}) collective-permute-start(bf16[128,512]{1,0:T(8,128)(2,1)S(1)} %get-tuple-element.61), channel_id=1, source_target_pairs={{0,1},{1,0},{2,3},{3,2},{4,5},{5,4},{6,7},{7,6},{8,9},{9,8},{10,11... | collective-permute-start | bytes 393224 | tf_op jit(solution)/shard_map/ppermute | solution.py:26
  37.4 1.3 %collective-permute-start.22 = (bf16[128,512]{1,0:T(8,128)(2,1)S(1)}, bf16[128,512]{1,0:T(8,128)(2,1)S(1)}, u32[]{:S(2)}, u32[]{:S(2)}) collective-permute-start(bf16[128,512]{1,0:T(8,128)(2,1)S(1)} %get-tuple-element.53), channel_id=1, source_target_pairs={{0,1},{1,0},{2,3},{3,2},{4,5},{5,4},{6,7},{7,6},{8,9},{9,8},{10,11... | collective-permute-start | bytes 393224 | tf_op jit(solution)/shard_map/ppermute | solution.py:26
  38.7 0.7 %shard_map.99 = (f32[16,8192]{1,0:T(8,128)S(1)}, f32[16,8192]{1,0:T(8,128)S(1)}) custom-call(bf16[256,256]{1,0:T(8,128)(2,1)S(1)} %get-tuple-element.76.place_ref, bf16[128,512]{1,0:T(8,128)(2,1)S(1)} %get-tuple-element.64.refs_0_, bf16[128,512]{1,0:T(8,128)(2,1)S(1)} %get-tuple-element.65.refs_1_, bf16[128,512]{1,0:T(8,128)(2,1)S(1)} %get-tuple-element.63.refs_2_, ...), custom_call_target="tpu_custom_call" | custom-call | flops 1 | bytes 1 | tf_op jit(solution)/shard_map/pallas_call | solution.py:139
  39.4 1.8 %shard_map.100 = (bf16[128,512]{1,0:T(8,128)(2,1)S(1)}, bf16[128,512]{1,0:T(8,128)(2,1)S(1)}, bf16[128,512]{1,0:T(8,128)(2,1)S(1)}, bf16[128,512]{1,0:T(8,128)(2,1)S(1)}, bf16[16,8192]{1,0:T(8,128)(2,1)}) custom-call(bf16[256,256]{1,0:T(8,128)(2,1)S(1)} %get-tuple-element.77.back_ref, f32[16,8192]{1,0:T(8,128)S(1)} %get-tuple-element.37.part_ref, ...), custom_call_target="tpu_custom_call" | custom-call | flops 1 | bytes 1 | tf_op jit(solution)/shard_map/pallas_call | solution.py:139
  41.2 1.8 %collective-permute-done.23 = bf16[128,512]{1,0:T(8,128)(2,1)S(1)} collective-permute-done((bf16[128,512]{1,0:T(8,128)(2,1)S(1)}, bf16[128,512]{1,0:T(8,128)(2,1)S(1)}, u32[]{:S(2)}, u32[]{:S(2)}) %collective-permute-start.23) | collective-permute-done | bytes 131104 | tf_op jit(solution)/shard_map/ppermute | solution.py:26
  43.1 1.6 %collective-permute-start.19 = (bf16[64,512]{1,0:T(8,128)(2,1)S(1)}, bf16[64,512]{1,0:T(8,128)(2,1)S(1)}, u32[]{:S(2)}, u32[]{:S(2)}) collective-permute-start(bf16[64,512]{1,0:T(8,128)(2,1)S(1)} %slice.168), channel_id=1, source_target_pairs={{0,4},{2,6},{4,0},{6,2},{8,12},{10,14},{12,8},{14,10},{16,20},{18,... | collective-permute-start | bytes 196616 | tf_op jit(solution)/shard_map/ppermute | solution.py:26
  44.7 0.3 collective-permute-done.22
  45.1 1.6 %collective-permute-start.25 = (bf16[64,512]{1,0:T(8,128)(2,1)S(1)}, bf16[64,512]{1,0:T(8,128)(2,1)S(1)}, u32[]{:S(2)}, u32[]{:S(2)}) collective-permute-start(bf16[64,512]{1,0:T(8,128)(2,1)S(1)} %slice.167), channel_id=1, source_target_pairs={{0,4},{2,6},{4,0},{6,2},{8,12},{10,14},{12,8},{14,10},{16,20},{18,... | collective-permute-start | bytes 196616 | tf_op jit(solution)/shard_map/ppermute | solution.py:26
  46.6 1.1 %collective-permute-done.19 = bf16[64,512]{1,0:T(8,128)(2,1)S(1)} collective-permute-done((bf16[64,512]{1,0:T(8,128)(2,1)S(1)}, bf16[64,512]{1,0:T(8,128)(2,1)S(1)}, u32[]{:S(2)}, u32[]{:S(2)}) %collective-permute-start.19) | collective-permute-done | bytes 65568 | tf_op jit(solution)/shard_map/ppermute | solution.py:26
  47.8 1.4 %collective-permute-start.20 = (bf16[32,512]{1,0:T(8,128)(2,1)S(1)}, bf16[32,512]{1,0:T(8,128)(2,1)S(1)}, u32[]{:S(2)}, u32[]{:S(2)}) collective-permute-start(bf16[32,512]{1,0:T(8,128)(2,1)S(1)} %slice.170), channel_id=1, source_target_pairs={{0,8},{2,10},{4,12},{6,14},{8,0},{10,2},{12,4},{14,6},{16,24},{18,... | collective-permute-start | bytes 98312 | tf_op jit(solution)/shard_map/ppermute | solution.py:26
  49.2 0.3 collective-permute-done.25
  49.5 1.4 %collective-permute-start.26 = (bf16[32,512]{1,0:T(8,128)(2,1)S(1)}, bf16[32,512]{1,0:T(8,128)(2,1)S(1)}, u32[]{:S(2)}, u32[]{:S(2)}) collective-permute-start(bf16[32,512]{1,0:T(8,128)(2,1)S(1)} %slice.169), channel_id=1, source_target_pairs={{0,8},{2,10},{4,12},{6,14},{8,0},{10,2},{12,4},{14,6},{16,24},{18,... | collective-permute-start | bytes 98312 | tf_op jit(solution)/shard_map/ppermute | solution.py:26
  50.8 1.1 %collective-permute-done.20 = bf16[32,512]{1,0:T(8,128)(2,1)S(1)} collective-permute-done((bf16[32,512]{1,0:T(8,128)(2,1)S(1)}, bf16[32,512]{1,0:T(8,128)(2,1)S(1)}, u32[]{:S(2)}, u32[]{:S(2)}) %collective-permute-start.20) | collective-permute-done | bytes 32800 | tf_op jit(solution)/shard_map/ppermute | solution.py:26
  51.9 2.5 %collective-permute-start.21 = (bf16[16,512]{1,0:T(8,128)(2,1)S(1)}, bf16[16,512]{1,0:T(8,128)(2,1)S(1)}, u32[]{:S(2)}, u32[]{:S(2)}) collective-permute-start(bf16[16,512]{1,0:T(8,128)(2,1)S(1)} %slice.172), channel_id=1, source_target_pairs={{0,16},{2,18},{4,20},{6,22},{8,24},{10,26},{12,28},{14,30},{16,0},... | collective-permute-start | bytes 49160 | tf_op jit(solution)/shard_map/ppermute | solution.py:26
  54.5 1.4 %collective-permute-start.27 = (bf16[16,512]{1,0:T(8,128)(2,1)S(1)}, bf16[16,512]{1,0:T(8,128)(2,1)S(1)}, u32[]{:S(2)}, u32[]{:S(2)}) collective-permute-start(bf16[16,512]{1,0:T(8,128)(2,1)S(1)} %slice.171), channel_id=1, source_target_pairs={{0,16},{2,18},{4,20},{6,22},{8,24},{10,26},{12,28},{14,30},{16,0},... | collective-permute-start | bytes 49160 | tf_op jit(solution)/shard_map/ppermute | solution.py:26
  55.9 0.7 %collective-permute-done.21 = bf16[16,512]{1,0:T(8,128)(2,1)S(1)} collective-permute-done((bf16[16,512]{1,0:T(8,128)(2,1)S(1)}, bf16[16,512]{1,0:T(8,128)(2,1)S(1)}, u32[]{:S(2)}, u32[]{:S(2)}) %collective-permute-start.21) | collective-permute-done | bytes 16416 | tf_op jit(solution)/shard_map/ppermute | solution.py:26
  56.6 2.6 %collective-permute-done.27 = bf16[16,512]{1,0:T(8,128)(2,1)S(1)} collective-permute-done((bf16[16,512]{1,0:T(8,128)(2,1)S(1)}, bf16[16,512]{1,0:T(8,128)(2,1)S(1)}, u32[]{:S(2)}, u32[]{:S(2)}) %collective-permute-start.27) | collective-permute-done | bytes 16416 | tf_op jit(solution)/shard_map/ppermute | solution.py:26
  59.2 0.7 %fusion.11 = (f32[1,16,512]{2,1,0:T(8,128)}, f32[1,16,512]{2,1,0:T(8,128)}) fusion(bf16[16,512]{1,0:T(8,128)(2,1)S(1)} %collective-permute-done.27, f32[32,512]{1,0:T(8,128)S(1)} %slice_add_fusion.2, bf16[16,512]{1,0:T(8,128)(2,1)S(1)} %collective-permute-done.21, f32[32,512]{1,0:T(8,128)S(1)} %slice_add_fusion.3, f32[1,16,512]{2,1,0:T(8,128)S(1)} %copy-done.4, ...), kind=kLoop, calls=%fused_computation.63 | loop fusion | flops 106496 | bytes 229376 | tf_op jit(solution)/shard_map/broadcast_in_dim | solution.py:268
  (66 shorter events, 1.3 us)
Async XLA Ops:
  0.6 0.8 %copy-start.1 = (f32[1,16,512]{2,1,0:T(8,128)S(1)}, f32[1,16,512]{2,1,0:T(8,128)}, u32[]{:S(2)}) copy-start(f32[1,16,512]{2,1,0:T(8,128)} %param.7) | copy-start | bytes 98308
  1.4 0.8 %copy-start.3 = (f32[1,16,512]{2,1,0:T(8,128)S(1)}, f32[1,16,512]{2,1,0:T(8,128)}, u32[]{:S(2)}) copy-start(f32[1,16,512]{2,1,0:T(8,128)} %param.9) | copy-start | bytes 98308
  2.1 0.8 %copy-start.5 = (f32[1,16,512]{2,1,0:T(8,128)S(1)}, f32[1,16,512]{2,1,0:T(8,128)}, u32[]{:S(2)}) copy-start(f32[1,16,512]{2,1,0:T(8,128)} %param.8) | copy-start | bytes 98308
  2.9 6.6 %collective-permute-start = (bf16[16,512]{1,0:T(8,128)(2,1)S(1)}, bf16[16,512]{1,0:T(8,128)(2,1)S(1)}, u32[]{:S(2)}, u32[]{:S(2)}) collective-permute-start(bf16[16,512]{1,0:T(8,128)(2,1)S(1)} %get-tuple-element.33), channel_id=1, source_target_pairs={{0,16},{2,18},{4,20},{6,22},{8,24},{10,26},{12,28},{14,30},{16,0},... | collective-permute-start | bytes 49160 | tf_op jit(solution)/shard_map/ppermute | solution.py:26
  8.0 3.9 %collective-permute-start.7 = (bf16[16,1024]{1,0:T(8,128)(2,1)S(1)}, bf16[16,1024]{1,0:T(8,128)(2,1)S(1)}, u32[]{:S(2)}, u32[]{:S(2)}) collective-permute-start(bf16[16,1024]{1,0:T(8,128)(2,1)S(1)} %get-tuple-element.42), channel_id=1, source_target_pairs={{0,1},{1,0},{2,3},{3,2},{4,5},{5,4},{6,7},{7,6},{8,9},{9,8},{10,11... | collective-permute-start | bytes 98312 | tf_op jit(solution)/shard_map/ppermute | solution.py:26
  9.5 4.0 %collective-permute-start.1 = (bf16[32,512]{1,0:T(8,128)(2,1)S(1)}, bf16[32,512]{1,0:T(8,128)(2,1)S(1)}, u32[]{:S(2)}, u32[]{:S(2)}) collective-permute-start(bf16[32,512]{1,0:T(8,128)(2,1)S(1)} %pad_maximum_fusion.5), channel_id=1, source_target_pairs={{0,8},{2,10},{4,12},{6,14},{8,0},{10,2},{12,4},{14,6},{16,24},{18,... | collective-permute-start | bytes 98312 | tf_op jit(solution)/shard_map/ppermute | solution.py:26
  11.9 7.4 %collective-permute-start.8 = (bf16[16,2560]{1,0:T(8,128)(2,1)S(1)}, bf16[16,2560]{1,0:T(8,128)(2,1)S(1)}, u32[]{:S(2)}, u32[]{:S(2)}) collective-permute-start(bf16[16,2560]{1,0:T(8,128)(2,1)S(1)} %constant_dynamic-update-slice_fusion.7), channel_id=1, source_target_pairs={{0,16},{2,18},{4,20},{6,22},{8,24},{10,26},{12,28},{14,30},{16,0},... | collective-permute-start | bytes 245768 | tf_op jit(solution)/shard_map/ppermute | solution.py:26
  13.5 4.3 %collective-permute-start.2 = (bf16[64,512]{1,0:T(8,128)(2,1)S(1)}, bf16[64,512]{1,0:T(8,128)(2,1)S(1)}, u32[]{:S(2)}, u32[]{:S(2)}) collective-permute-start(bf16[64,512]{1,0:T(8,128)(2,1)S(1)} %get-tuple-element.70), channel_id=1, source_target_pairs={{0,4},{2,6},{4,0},{6,2},{8,12},{10,14},{12,8},{14,10},{16,20},{18,... | collective-permute-start | bytes 196616 | tf_op jit(solution)/shard_map/ppermute | solution.py:26
  17.8 3.0 %collective-permute-start.3 = (bf16[128,512]{1,0:T(8,128)(2,1)S(1)}, bf16[128,512]{1,0:T(8,128)(2,1)S(1)}, u32[]{:S(2)}, u32[]{:S(2)}) collective-permute-start(bf16[128,512]{1,0:T(8,128)(2,1)S(1)} %constant_dynamic-update-slice_fusion.3.w0_ref), channel_id=1, source_target_pairs={{0,2},{2,0},{4,6},{6,4},{8,10},{10,8},{12,14},{14,12},{16,18},{18,... | collective-permute-start | bytes 393224 | tf_op jit(solution)/shard_map/ppermute | solution.py:26
  17.8 5.9 %collective-permute-start.4 = (bf16[128,512]{1,0:T(8,128)(2,1)S(1)}, bf16[128,512]{1,0:T(8,128)(2,1)S(1)}, u32[]{:S(2)}, u32[]{:S(2)}) collective-permute-start(bf16[128,512]{1,0:T(8,128)(2,1)S(1)} %constant_dynamic-update-slice_fusion.3.w0_ref), channel_id=1, source_target_pairs={{0,1},{1,0},{2,3},{3,2},{4,5},{5,4},{6,7},{7,6},{8,9},{9,8},{10,11... | collective-permute-start | bytes 393224 | tf_op jit(solution)/shard_map/ppermute | solution.py:26
  19.3 6.3 %collective-permute-start.9 = (bf16[32,2560]{1,0:T(8,128)(2,1)S(1)}, bf16[32,2560]{1,0:T(8,128)(2,1)S(1)}, u32[]{:S(2)}, u32[]{:S(2)}) collective-permute-start(bf16[32,2560]{1,0:T(8,128)(2,1)S(1)} %pad_maximum_fusion.1), channel_id=1, source_target_pairs={{0,8},{2,10},{4,12},{6,14},{8,0},{10,2},{12,4},{14,6},{16,24},{18,... | collective-permute-start | bytes 491528 | tf_op jit(solution)/shard_map/ppermute | solution.py:26
  22.1 7.9 %copy-start.6 = (bf16[2,64,8192]{2,1,0:T(8,128)(2,1)S(1)}, bf16[2,64,8192]{2,1,0:T(8,128)(2,1)}, u32[]{:S(2)}) copy-start(bf16[2,64,8192]{2,1,0:T(8,128)(2,1)} %param.13) | copy-start | bytes 6291460
  22.1 12.3 %collective-permute-start.11 = (bf16[16,8192]{1,0:T(8,128)(2,1)S(1)}, bf16[16,8192]{1,0:T(8,128)(2,1)S(1)}, u32[]{:S(2)}, u32[]{:S(2)}) collective-permute-start(bf16[16,8192]{1,0:T(8,128)(2,1)S(1)} %get-tuple-element.44), channel_id=1, source_target_pairs={{0,1},{1,0},{2,3},{3,2},{4,5},{5,4},{6,7},{7,6},{8,9},{9,8},{10,11... | collective-permute-start | bytes 786440 | tf_op jit(solution)/shard_map/ppermute | solution.py:26
  23.7 4.2 %collective-permute-start.5 = (bf16[128,512]{1,0:T(8,128)(2,1)S(1)}, bf16[128,512]{1,0:T(8,128)(2,1)S(1)}, u32[]{:S(2)}, u32[]{:S(2)}) collective-permute-start(bf16[128,512]{1,0:T(8,128)(2,1)S(1)} %collective-permute-done.4.w0_ref), channel_id=1, source_target_pairs={{0,2},{2,0},{4,6},{6,4},{8,10},{10,8},{12,14},{14,12},{16,18},{18,... | collective-permute-start | bytes 393224 | tf_op jit(solution)/shard_map/ppermute | solution.py:26
  25.7 6.5 %collective-permute-start.12 = (bf16[64,1024]{1,0:T(8,128)(2,1)S(1)}, bf16[64,1024]{1,0:T(8,128)(2,1)S(1)}, u32[]{:S(2)}, u32[]{:S(2)}) collective-permute-start(bf16[64,1024]{1,0:T(8,128)(2,1)S(1)} %pad_maximum_fusion.4), channel_id=1, source_target_pairs={{0,4},{2,6},{4,0},{6,2},{8,12},{10,14},{12,8},{14,10},{16,20},{18,... | collective-permute-start | bytes 393224 | tf_op jit(solution)/shard_map/ppermute | solution.py:26
  27.3 5.5 %copy-start.7 = (bf16[2,64,8192]{2,1,0:T(8,128)(2,1)S(1)}, bf16[2,64,8192]{2,1,0:T(8,128)(2,1)}, u32[]{:S(2)}) copy-start(bf16[2,64,8192]{2,1,0:T(8,128)(2,1)} %param.12) | copy-start | bytes 6291460
  27.3 8.4 %collective-permute-start.10 = (bf16[64,1536]{1,0:T(8,128)(2,1)S(1)}, bf16[64,1536]{1,0:T(8,128)(2,1)S(1)}, u32[]{:S(2)}, u32[]{:S(2)}) collective-permute-start(bf16[64,1536]{1,0:T(8,128)(2,1)S(1)} %slice.98), channel_id=1, source_target_pairs={{0,4},{2,6},{4,0},{6,2},{8,12},{10,14},{12,8},{14,10},{16,20},{18,... | collective-permute-start | bytes 589832 | tf_op jit(solution)/shard_map/ppermute | solution.py:26
  29.2 10.2 %collective-permute-start.6 = (bf16[16,8192]{1,0:T(8,128)(2,1)S(1)}, bf16[16,8192]{1,0:T(8,128)(2,1)S(1)}, u32[]{:S(2)}, u32[]{:S(2)}) collective-permute-start(bf16[16,8192]{1,0:T(8,128)(2,1)S(1)} %get-tuple-element.38), channel_id=1, source_target_pairs={{0,1},{1,0},{2,3},{3,2},{4,5},{5,4},{6,7},{7,6},{8,9},{9,8},{10,11... | collective-permute-start | bytes 786440 | tf_op jit(solution)/shard_map/ppermute | solution.py:26
  32.2 1.4 %collective-permute-start.13 = (bf16[128,512]{1,0:T(8,128)(2,1)S(1)}, bf16[128,512]{1,0:T(8,128)(2,1)S(1)}, u32[]{:S(2)}, u32[]{:S(2)}) collective-permute-start(bf16[128,512]{1,0:T(8,128)(2,1)S(1)} %get-tuple-element.67.refs_0_), channel_id=1, source_target_pairs={{0,2},{2,0},{4,6},{6,4},{8,10},{10,8},{12,14},{14,12},{16,18},{18,... | collective-permute-start | bytes 393224 | tf_op jit(solution)/shard_map/ppermute | solution.py:26
  32.3 1.5 %collective-permute-start.14 = (bf16[128,512]{1,0:T(8,128)(2,1)S(1)}, bf16[128,512]{1,0:T(8,128)(2,1)S(1)}, u32[]{:S(2)}, u32[]{:S(2)}) collective-permute-start(bf16[128,512]{1,0:T(8,128)(2,1)S(1)} %get-tuple-element.66.refs_1_), channel_id=1, source_target_pairs={{0,2},{2,0},{4,6},{6,4},{8,10},{10,8},{12,14},{14,12},{16,18},{18,... | collective-permute-start | bytes 393224 | tf_op jit(solution)/shard_map/ppermute | solution.py:26
  34.4 5.0 %copy-start = (bf16[1,2,8,8192]{3,2,1,0:T(8,128)(2,1)S(1)}, bf16[1,2,8,8192]{3,2,1,0:T(8,128)(2,1)}, u32[]{:S(2)}) copy-start(bf16[1,2,8,8192]{3,2,1,0:T(8,128)(2,1)} %param.11) | copy-start | bytes 786436
  35.7 1.6 %collective-permute-start.15 = (bf16[128,512]{1,0:T(8,128)(2,1)S(1)}, bf16[128,512]{1,0:T(8,128)(2,1)S(1)}, u32[]{:S(2)}, u32[]{:S(2)}) collective-permute-start(bf16[128,512]{1,0:T(8,128)(2,1)S(1)} %get-tuple-element.64.refs_0_), channel_id=1, source_target_pairs={{0,2},{2,0},{4,6},{6,4},{8,10},{10,8},{12,14},{14,12},{16,18},{18,... | collective-permute-start | bytes 393224 | tf_op jit(solution)/shard_map/ppermute | solution.py:26
  36.1 2.5 %collective-permute-start.16 = (bf16[128,512]{1,0:T(8,128)(2,1)S(1)}, bf16[128,512]{1,0:T(8,128)(2,1)S(1)}, u32[]{:S(2)}, u32[]{:S(2)}) collective-permute-start(bf16[128,512]{1,0:T(8,128)(2,1)S(1)} %get-tuple-element.65.refs_1_), channel_id=1, source_target_pairs={{0,2},{2,0},{4,6},{6,4},{8,10},{10,8},{12,14},{14,12},{16,18},{18,... | collective-permute-start | bytes 393224 | tf_op jit(solution)/shard_map/ppermute | solution.py:26
  36.3 2.4 %collective-permute-start.17 = (bf16[128,512]{1,0:T(8,128)(2,1)S(1)}, bf16[128,512]{1,0:T(8,128)(2,1)S(1)}, u32[]{:S(2)}, u32[]{:S(2)}) collective-permute-start(bf16[128,512]{1,0:T(8,128)(2,1)S(1)} %get-tuple-element.63.refs_2_), channel_id=1, source_target_pairs={{0,2},{2,0},{4,6},{6,4},{8,10},{10,8},{12,14},{14,12},{16,18},{18,... | collective-permute-start | bytes 393224 | tf_op jit(solution)/shard_map/ppermute | solution.py:26
  36.6 6.3 %collective-permute-start.23 = (bf16[128,512]{1,0:T(8,128)(2,1)S(1)}, bf16[128,512]{1,0:T(8,128)(2,1)S(1)}, u32[]{:S(2)}, u32[]{:S(2)}) collective-permute-start(bf16[128,512]{1,0:T(8,128)(2,1)S(1)} %get-tuple-element.61), channel_id=1, source_target_pairs={{0,1},{1,0},{2,3},{3,2},{4,5},{5,4},{6,7},{7,6},{8,9},{9,8},{10,11... | collective-permute-start | bytes 393224 | tf_op jit(solution)/shard_map/ppermute | solution.py:26
  37.4 7.7 %collective-permute-start.22 = (bf16[128,512]{1,0:T(8,128)(2,1)S(1)}, bf16[128,512]{1,0:T(8,128)(2,1)S(1)}, u32[]{:S(2)}, u32[]{:S(2)}) collective-permute-start(bf16[128,512]{1,0:T(8,128)(2,1)S(1)} %get-tuple-element.53), channel_id=1, source_target_pairs={{0,1},{1,0},{2,3},{3,2},{4,5},{5,4},{6,7},{7,6},{8,9},{9,8},{10,11... | collective-permute-start | bytes 393224 | tf_op jit(solution)/shard_map/ppermute | solution.py:26
  41.2 18.0 %copy-start.2 = (f32[1,16,512]{2,1,0:T(8,128)S(1)}, f32[1,16,512]{2,1,0:T(8,128)}, u32[]{:S(2)}) copy-start(f32[1,16,512]{2,1,0:T(8,128)} %param.7) | copy-start | bytes 98308
  41.2 18.0 %copy-start.4 = (f32[1,16,512]{2,1,0:T(8,128)S(1)}, f32[1,16,512]{2,1,0:T(8,128)}, u32[]{:S(2)}) copy-start(f32[1,16,512]{2,1,0:T(8,128)} %param.9) | copy-start | bytes 98308
  41.2 1.9 %collective-permute-start.18 = (bf16[128,512]{1,0:T(8,128)(2,1)S(1)}, bf16[128,512]{1,0:T(8,128)(2,1)S(1)}, u32[]{:S(2)}, u32[]{:S(2)}) collective-permute-start(bf16[128,512]{1,0:T(8,128)(2,1)S(1)} %get-tuple-element.58), channel_id=1, source_target_pairs={{0,2},{2,0},{4,6},{6,4},{8,10},{10,8},{12,14},{14,12},{16,18},{18,... | collective-permute-start | bytes 393224 | tf_op jit(solution)/shard_map/ppermute | solution.py:26
  43.0 2.0 %collective-permute-start.24 = (bf16[128,512]{1,0:T(8,128)(2,1)S(1)}, bf16[128,512]{1,0:T(8,128)(2,1)S(1)}, u32[]{:S(2)}, u32[]{:S(2)}) collective-permute-start(bf16[128,512]{1,0:T(8,128)(2,1)S(1)} %add_convert_fusion), channel_id=1, source_target_pairs={{0,2},{2,0},{4,6},{6,4},{8,10},{10,8},{12,14},{14,12},{16,18},{18,... | collective-permute-start | bytes 393224 | tf_op jit(solution)/shard_map/ppermute | solution.py:26
  43.1 4.6 %collective-permute-start.19 = (bf16[64,512]{1,0:T(8,128)(2,1)S(1)}, bf16[64,512]{1,0:T(8,128)(2,1)S(1)}, u32[]{:S(2)}, u32[]{:S(2)}) collective-permute-start(bf16[64,512]{1,0:T(8,128)(2,1)S(1)} %slice.168), channel_id=1, source_target_pairs={{0,4},{2,6},{4,0},{6,2},{8,12},{10,14},{12,8},{14,10},{16,20},{18,... | collective-permute-start | bytes 196616 | tf_op jit(solution)/shard_map/ppermute | solution.py:26
  45.1 4.3 %collective-permute-start.25 = (bf16[64,512]{1,0:T(8,128)(2,1)S(1)}, bf16[64,512]{1,0:T(8,128)(2,1)S(1)}, u32[]{:S(2)}, u32[]{:S(2)}) collective-permute-start(bf16[64,512]{1,0:T(8,128)(2,1)S(1)} %slice.167), channel_id=1, source_target_pairs={{0,4},{2,6},{4,0},{6,2},{8,12},{10,14},{12,8},{14,10},{16,20},{18,... | collective-permute-start | bytes 196616 | tf_op jit(solution)/shard_map/ppermute | solution.py:26
  47.8 4.1 %collective-permute-start.20 = (bf16[32,512]{1,0:T(8,128)(2,1)S(1)}, bf16[32,512]{1,0:T(8,128)(2,1)S(1)}, u32[]{:S(2)}, u32[]{:S(2)}) collective-permute-start(bf16[32,512]{1,0:T(8,128)(2,1)S(1)} %slice.170), channel_id=1, source_target_pairs={{0,8},{2,10},{4,12},{6,14},{8,0},{10,2},{12,4},{14,6},{16,24},{18,... | collective-permute-start | bytes 98312 | tf_op jit(solution)/shard_map/ppermute | solution.py:26
  49.5 5.0 %collective-permute-start.26 = (bf16[32,512]{1,0:T(8,128)(2,1)S(1)}, bf16[32,512]{1,0:T(8,128)(2,1)S(1)}, u32[]{:S(2)}, u32[]{:S(2)}) collective-permute-start(bf16[32,512]{1,0:T(8,128)(2,1)S(1)} %slice.169), channel_id=1, source_target_pairs={{0,8},{2,10},{4,12},{6,14},{8,0},{10,2},{12,4},{14,6},{16,24},{18,... | collective-permute-start | bytes 98312 | tf_op jit(solution)/shard_map/ppermute | solution.py:26
  51.9 4.7 %collective-permute-start.21 = (bf16[16,512]{1,0:T(8,128)(2,1)S(1)}, bf16[16,512]{1,0:T(8,128)(2,1)S(1)}, u32[]{:S(2)}, u32[]{:S(2)}) collective-permute-start(bf16[16,512]{1,0:T(8,128)(2,1)S(1)} %slice.172), channel_id=1, source_target_pairs={{0,16},{2,18},{4,20},{6,22},{8,24},{10,26},{12,28},{14,30},{16,0},... | collective-permute-start | bytes 49160 | tf_op jit(solution)/shard_map/ppermute | solution.py:26
  54.5 4.7 %collective-permute-start.27 = (bf16[16,512]{1,0:T(8,128)(2,1)S(1)}, bf16[16,512]{1,0:T(8,128)(2,1)S(1)}, u32[]{:S(2)}, u32[]{:S(2)}) collective-permute-start(bf16[16,512]{1,0:T(8,128)(2,1)S(1)} %slice.171), channel_id=1, source_target_pairs={{0,16},{2,18},{4,20},{6,22},{8,24},{10,26},{12,28},{14,30},{16,0},... | collective-permute-start | bytes 49160 | tf_op jit(solution)/shard_map/ppermute | solution.py:26

commit v6 on v5

--- a/solution.py
+++ b/solution.py
@@ -77,8 +77,8 @@
     width = moment_ref.shape[1]
     near, far = place_ref[:, :half], place_ref[:, half:]
     ordered = [dot(near, a[...]) + dot(far, b[...]) for a, b in zip(terms[:count], terms[count:])]
-    moment = sum(ordered[1:-1], ordered[0])
-    rate = step_rate / (jnp.sqrt(ordered[-1]) + epsilon)
+    moment = sum(ordered[2:], ordered[0])
+    rate = step_rate / (jnp.sqrt(ordered[1]) + epsilon)
     for c in range(width // segment):
         at = slice(c * segment, (c + 1) * segment)
         moment_ref[:, at] = moment[c * rows : (c + 1) * rows]
@@ -119,18 +119,6 @@
         store_flat(back_ref, seg_ref, flat_refs[2:])
 
 
-def cast_kernel(master_ref, moment_ref, variance_ref, weights_ref, own_ref, near_ref):
-    segment = master_ref.shape[1]
-    weights_ref[...] = master_ref[...].astype(BF)
-    high = moment_ref[...].astype(BF)
-    spread = variance_ref[...].astype(BF)
-    own_ref[:, :segment] = high
-    own_ref[:, segment : 2 * segment] = (moment_ref[...] - high.astype(F32)).astype(BF)
-    own_ref[:, 2 * segment :] = spread
-    near_ref[:, :segment] = high
-    near_ref[:, segment:] = spread
-
-
 def tokens_of(step, arrays, *others):
     return [x[step] for x in lax.optimization_barrier((*arrays, *others))[: len(arrays)]]
 
@@ -159,32 +147,29 @@
     mp_bits = bits_of(n_mp)
     shape = jax.ShapeDtypeStruct
 
-    near_w, own_a, near_a = call(
-        cast_kernel,
-        tuple(shape((span, terms * segment), BF) for terms in (1, 3, 2)),
-        (master[0], moment[0], variance[0]),
-    )
-
-    owner = (flat_slot // span) ^ me
-    position = jnp.zeros_like(owner)
-    for place, mask in enumerate(far + [1]):
-        position = position + jnp.where((owner & mask) != 0, 1 << place, 0)
-    position = position * span + flat_slot % span
-    position = position.reshape(rows, width // segment).T.reshape(segments)
-
+    near_w = master[0].astype(BF)
+    spans = jnp.concatenate([after(moment[0], near_w), variance[0]], axis=1)
+    near_a = spans.astype(BF)
+    low = spans[:, :segment] - lax.reduce_precision(spans[:, :segment], 8, 7)
     steps = []
     for mask in far:
         near_w = jnp.concatenate([near_w, swap(near_w, "dp", mask)], axis=0)
         steps.append(near_w)
-    others = [after(near_a, position)]
+    blocks_a = [near_a]
     for mask in reversed(mp_bits):
-        others = others + [swap(b, "mp", mask) for b in others]
-    all_a = jnp.concatenate([own_a] + others[1:], axis=1)
-
+        blocks_a = blocks_a + [swap(b, "mp", mask) for b in blocks_a]
+    blocks_a[0] = jnp.concatenate([near_a, low.astype(BF)], axis=1)
+
+    slot = after(flat_slot, steps[-1])
+    owner = (slot // span) ^ me
+    position = jnp.zeros_like(owner)
+    for place, mask in enumerate(far + [1]):
+        position = position + jnp.where((owner & mask) != 0, 1 << place, 0)
+    position = position * span + slot % span
+    position = position.reshape(rows, width // segment).T.reshape(segments)
     line = jnp.arange(segments, dtype=jnp.int32)
-    spot = after(position, steps[-1])
-    place_map = (spot[:, None] == line[None, :]).astype(BF)
-    back_map = (line[:, None] == spot[None, :]).astype(BF)
+    place_map = (position[:, None] == line[None, :]).astype(BF)
+    back_map = (line[:, None] == position[None, :]).astype(BF)
 
     blocks_w = [near_w]
     for mask in reversed(mp_bits):
@@ -211,19 +196,19 @@
         crossed = [swap(p, "mp", mask) for p in sent]
         got = [crossed[k ^ mask] for k in range(n_mp)]
 
-    for mask, event in zip(far[:-1], [steps[-1]] * (len(far) - 2) + [sent[0]]):
-        all_a = jnp.concatenate([all_a, after(swap(all_a, "dp", mask), event)], axis=0)
-    ends = [0] + [(3 + 2 * k) * segment for k in range(n_mp)]
-    blocks_a = [all_a[:, ends[k] : ends[k + 1]] for k in range(n_mp)]
-    arrived = [None] * n_mp
-    for k in reversed(range(n_mp)):
-        arrived[k] = swap(blocks_a[k], "dp", far[-1])
+    early = [one[0]] + [sent[0]] * (len(far) - 3)
+
+    def stage(block, mask, event):
+        return jnp.concatenate([block, after(swap(block, "dp", mask), event)], axis=0)
+
+    for mask, event, late in zip(far[:-1], early + [sent[0]], early[1:] + [sent[0], sent[-1]]):
+        blocks_a = [stage(b, mask, event if k else late) for k, b in enumerate(blocks_a)]
 
     half = segments // 2
     kept, away, event = [None] * n_mp, [None] * n_mp, sent[-1]
     for k in reversed(range(n_mp)):
         own = k == 0
-        block = jnp.concatenate([blocks_a[k], after(arrived[k], event)], axis=0)
+        block = stage(blocks_a[k], far[-1], event)
         terms = [block[:, at : at + segment] for at in range(0, block.shape[1], segment)]
         terms += [swap(term, "dp", 1) for term in terms]
         moment_t, rate = call(
@@ -247,19 +232,23 @@
 
     for mask in mp_bits:
         away_got = [swap(p.astype(BF), "mp", mask) for p in away[mask:]]
-        kept_got = [swap(p.astype(BF), "mp", mask) for p in kept[mask:]]
+        kept_got = [after(swap(p.astype(BF), "mp", mask), packed) for p in kept[mask:]]
         away = [p.astype(F32) + q.astype(F32) for p, q in zip(away, away_got)]
         kept = [p.astype(F32) + q.astype(F32) for p, q in zip(kept, kept_got)]
     grad = kept[0] + swap(away[0].astype(BF), "dp", 1).astype(F32)
 
-    def over_chips(total):
-        for mask in far[::-1]:
+    def halves(total, masks):
+        for mask in masks:
             count = total.shape[0] // 2
             total = total[:count] + swap(total[count:].astype(BF), "dp", mask).astype(F32)
         return total
 
-    own_packed = over_chips(packed)
-    own_grad = over_chips(grad)
+    packed, grad = halves(packed, far[:1:-1]), halves(grad, far[:1:-1])
+    both = jnp.concatenate([grad, packed], axis=1)
+    total = both[:span]
+    for k, mask in ((3, far[0] | far[1]), (1, far[0]), (2, far[1])):
+        total = total + swap(both[k * span : (k + 1) * span].astype(BF), "dp", mask).astype(F32)
+    own_grad, own_packed = total[:, :segment], total[:, segment:]
     mean_grad = own_grad / n_dp
     mean_moment = own_packed / n_dp
     moment_new = beta_one * mean_moment + (1.0 - beta_one) * mean_grad

time: 60.2 us -> 61.5 us (1.022)
  waiting for transfers between devices: 15.2 us -> 18.1 us
  local copies, waits for them, and re-layouts: 4.43 us -> 1.92 us
  other arithmetic: 1.71 us -> 3.41 us
  starting transfers between devices: 30.7 us -> 30 us
    ppermute x28 -> x29, waiting for transfers between devices: 15.2 us -> 18.1 us  [swap(): return lax.ppermute(x, axis, [(i, i ^ mask) for i in range(n)])]
    unnamed x19 -> x17, local copies, waits for them, and re-layouts: 2.3 us -> 0.05 us
    convert_element_type x1 -> x3, other arithmetic: 0.1 us -> 1.72 us  [the longest x1 0.84 us: per_device(): blocks_a[0] = jnp.concatenate([near_a, low.astype(BF)], axis=1)]
    another operation x0 -> x2, other arithmetic: none -> 0.78 us
    ppermute x28 -> x29, starting transfers between devices: 30.7 us -> 30 us  [swap(): return lax.ppermute(x, axis, [(i, i ^ mask) for i in range(n)])]
    add x5 -> x4, other arithmetic: 0.74 us -> 0.07 us  [the longest x2 0.03 us: halves(): total[:count] + swap(total[count:].astype(BF), 'dp', mask).astype(F32)]
    pallas_call x7 -> x6, Pallas kernels: 6.82 us -> 6.69 us  [call(): pl.pallas_call(kernel, out_shape=out_shape, in_specs=[pl.BlockSpec(memory...]
  transfers between devices with their start and end apart: 28 -> 29, of which waited for: 15 -> 10; matrix products, arithmetic and copies ran while one was open for 5% -> 6% of each run, Pallas kernels for 11% -> 11%
where the time goes in v6:
time: 61.5 us; the launch traced here: 61.1 us
  starting transfers between devices  30 us (49%)
  waiting for transfers between devices  18.1 us (29%)
  Pallas kernels  6.69 us (11%)
  other arithmetic  3.41 us (6%)
  local copies, waits for them, and re-layouts  1.92 us (3%)
  between operations  0.98 us (2%)
    ppermute x29, starting transfers between devices, swap(): return lax.ppermute(x, axis, [(i, i ^ mask) for i in range(n)])  30 us
    ppermute x29, waiting for transfers between devices, swap(): return lax.ppermute(x, axis, [(i, i ^ mask) for i in range(n)])  18.1 us
    pallas_call x6, Pallas kernels, call(): pl.pallas_call(kernel, out_shape=out_shape, in_specs=[pl.BlockSpec(memory...  6.69 us
    squeeze x3, local copies, waits for them, and re-layouts, tokens_of(): x[step]  1.55 us
  transfers between devices with their start and end apart: 29, of which 10 were waited for; matrix products, arithmetic and copies ran while one was open for 6% of the time, Pallas kernels for 11%

profile of v6, /device:TPU:0, one launch (start us, length us, event | category | flops | bytes accessed | tf_op | source)
XLA Modules:
  0.0 61.1 jit_solution(16700515153280986653)
XLA Ops:
  0.6 0.8 %bitcast_convert_fusion = bf16[16,512]{1,0:T(8,128)(2,1)S(1)} fusion(f32[1,16,512]{2,1,0:T(8,128)} %param.7), kind=kLoop, calls=%fused_computation.40 | loop fusion | flops 8192 | bytes 49152 | tf_op jit(solution)/shard_map/convert_element_type | solution.py:150
  1.4 4.0 %collective-permute-start = (bf16[16,512]{1,0:T(8,128)(2,1)S(1)}, bf16[16,512]{1,0:T(8,128)(2,1)S(1)}, u32[]{:S(2)}, u32[]{:S(2)}) collective-permute-start(bf16[16,512]{1,0:T(8,128)(2,1)S(1)} %bitcast_convert_fusion), channel_id=1, source_target_pairs={{0,16},{2,18},{4,20},{6,22},{8,24},{10,26},{12,28},{14,30},{16,0},... | collective-permute-start | bytes 49160 | tf_op jit(solution)/shard_map/ppermute | solution.py:26
  5.4 0.8 %convert_bitcast_fusion = bf16[16,512]{1,0:T(8,128)(2,1)S(1)} fusion(f32[1,16,512]{2,1,0:T(8,128)} %param.9), kind=kLoop, calls=%fused_computation.41 | loop fusion | flops 8192 | bytes 49152 | tf_op jit(solution)/shard_map/convert.6
  6.2 0.8 %fusion.7 = (bf16[16,512]{1,0:T(8,128)(2,1)S(1)}, bf16[16,512]{1,0:T(8,128)(2,1)S(1)}) fusion(f32[16,512]{1,0:T(8,128)} %bitcast.28), kind=kLoop, calls=%fused_computation.32 | loop fusion | flops 32768 | bytes 65536 | tf_op jit(solution)/shard_map/convert_element_type | solution.py:161
  7.0 1.6 %collective-permute-start.11 = (bf16[16,1024]{1,0:T(8,128)(2,1)S(1)}, bf16[16,1024]{1,0:T(8,128)(2,1)S(1)}, u32[]{:S(2)}, u32[]{:S(2)}) collective-permute-start(bf16[16,1024]{1,0:T(8,128)(2,1)S(1)} %pad_maximum_fusion.10), channel_id=1, source_target_pairs={{0,1},{1,0},{2,3},{3,2},{4,5},{5,4},{6,7},{7,6},{8,9},{9,8},{10,11... | collective-permute-start | bytes 98312 | tf_op jit(solution)/shard_map/ppermute | solution.py:26
  8.6 0.3 collective-permute-start.7
  9.0 1.6 %collective-permute-start.1 = (bf16[32,512]{1,0:T(8,128)(2,1)S(1)}, bf16[32,512]{1,0:T(8,128)(2,1)S(1)}, u32[]{:S(2)}, u32[]{:S(2)}) collective-permute-start(bf16[32,512]{1,0:T(8,128)(2,1)S(1)} %pad_maximum_fusion.9), channel_id=1, source_target_pairs={{0,8},{2,10},{4,12},{6,14},{8,0},{10,2},{12,4},{14,6},{16,24},{18,... | collective-permute-start | bytes 98312 | tf_op jit(solution)/shard_map/ppermute | solution.py:26
  10.6 0.4 collective-permute-done.11
  11.0 2.2 %collective-permute-start.12 = (bf16[16,1024]{1,0:T(8,128)(2,1)S(1)}, bf16[16,1024]{1,0:T(8,128)(2,1)S(1)}, u32[]{:S(2)}, u32[]{:S(2)}) collective-permute-start(bf16[16,1024]{1,0:T(8,128)(2,1)S(1)} %collective-permute-done.11), channel_id=1, source_target_pairs={{0,16},{2,18},{4,20},{6,22},{8,24},{10,26},{12,28},{14,30},{16,0},... | collective-permute-start | bytes 98312 | tf_op jit(solution)/shard_map/ppermute | solution.py:26
  13.2 1.6 %collective-permute-start.2 = (bf16[64,512]{1,0:T(8,128)(2,1)S(1)}, bf16[64,512]{1,0:T(8,128)(2,1)S(1)}, u32[]{:S(2)}, u32[]{:S(2)}) collective-permute-start(bf16[64,512]{1,0:T(8,128)(2,1)S(1)} %pad_maximum_fusion.6), channel_id=1, source_target_pairs={{0,4},{2,6},{4,0},{6,2},{8,12},{10,14},{12,8},{14,10},{16,20},{18,... | collective-permute-start | bytes 196616 | tf_op jit(solution)/shard_map/ppermute | solution.py:26
  14.8 1.3 %slice_bitcast_fusion.3.x_ref = bf16[64,8192]{1,0:T(8,128)(2,1)S(1)} fusion(bf16[2,64,8192]{2,1,0:T(8,128)(2,1)} %param.12), kind=kLoop, calls=%fused_computation.3 | loop fusion | bytes 2097152 | tf_op jit(solution)/shard_map/squeeze | solution.py:123
  16.2 1.4 %collective-permute-start.13 = (bf16[32,1024]{1,0:T(8,128)(2,1)S(1)}, bf16[32,1024]{1,0:T(8,128)(2,1)S(1)}, u32[]{:S(2)}, u32[]{:S(2)}) collective-permute-start(bf16[32,1024]{1,0:T(8,128)(2,1)S(1)} %pad_maximum_fusion.7), channel_id=1, source_target_pairs={{0,8},{2,10},{4,12},{6,14},{8,0},{10,2},{12,4},{14,6},{16,24},{18,... | collective-permute-start | bytes 196616 | tf_op jit(solution)/shard_map/ppermute | solution.py:26
  17.6 1.4 %collective-permute-start.4 = (bf16[128,512]{1,0:T(8,128)(2,1)S(1)}, bf16[128,512]{1,0:T(8,128)(2,1)S(1)}, u32[]{:S(2)}, u32[]{:S(2)}) collective-permute-start(bf16[128,512]{1,0:T(8,128)(2,1)S(1)} %pad_maximum_fusion.3.w0_ref), channel_id=1, source_target_pairs={{0,1},{1,0},{2,3},{3,2},{4,5},{5,4},{6,7},{7,6},{8,9},{9,8},{10,11... | collective-permute-start | bytes 393224 | tf_op jit(solution)/shard_map/ppermute | solution.py:26
  19.1 0.1 reshape.14
  19.2 0.1 eq.31
  19.3 0.1 fusion.2
  19.4 1.0 %collective-permute-done.3.w1_ref = bf16[128,512]{1,0:T(8,128)(2,1)S(1)} collective-permute-done((bf16[128,512]{1,0:T(8,128)(2,1)S(1)}, bf16[128,512]{1,0:T(8,128)(2,1)S(1)}, u32[]{:S(2)}, u32[]{:S(2)}) %collective-permute-start.3) | collective-permute-done | bytes 131104 | tf_op jit(solution)/shard_map/ppermute | solution.py:26
  20.4 1.3 %shard_map.94 = (bf16[16,8192]{1,0:T(8,128)(2,1)S(1)}, f32[16,8192]{1,0:T(8,128)S(1)}, bf16[16,8192]{1,0:T(8,128)(2,1)S(1)}) custom-call(bf16[256,256]{1,0:T(8,128)(2,1)S(1)} %get-tuple-element.75.place_ref, bf16[128,512]{1,0:T(8,128)(2,1)S(1)} %pad_maximum_fusion.3.w0_ref, bf16[128,512]{1,0:T(8,128)(2,1)S(1)} %collective-permute-done.3.w1_ref, ...), custom_call_target="tpu_custom_call" | custom-call | flops 1 | bytes 1 | tf_op jit(solution)/shard_map/pallas_call | solution.py:127
  21.7 0.7 %collective-permute-start.10 = (bf16[16,8192]{1,0:T(8,128)(2,1)S(1)}, bf16[16,8192]{1,0:T(8,128)(2,1)S(1)}, u32[]{:S(2)}, u32[]{:S(2)}) collective-permute-start(bf16[16,8192]{1,0:T(8,128)(2,1)S(1)} %get-tuple-element.40), channel_id=1, source_target_pairs={{0,1},{1,0},{2,3},{3,2},{4,5},{5,4},{6,7},{7,6},{8,9},{9,8},{10,11... | collective-permute-start | bytes 786440 | tf_op jit(solution)/shard_map/ppermute | solution.py:26
  22.4 1.5 %collective-permute-start.14 = (bf16[64,1024]{1,0:T(8,128)(2,1)S(1)}, bf16[64,1024]{1,0:T(8,128)(2,1)S(1)}, u32[]{:S(2)}, u32[]{:S(2)}) collective-permute-start(bf16[64,1024]{1,0:T(8,128)(2,1)S(1)} %pad_maximum_fusion.4), channel_id=1, source_target_pairs={{0,4},{2,6},{4,0},{6,2},{8,12},{10,14},{12,8},{14,10},{16,20},{18,... | collective-permute-start | bytes 393224 | tf_op jit(solution)/shard_map/ppermute | solution.py:26
  24.0 1.4 %collective-permute-start.8 = (bf16[32,1536]{1,0:T(8,128)(2,1)S(1)}, bf16[32,1536]{1,0:T(8,128)(2,1)S(1)}, u32[]{:S(2)}, u32[]{:S(2)}) collective-permute-start(bf16[32,1536]{1,0:T(8,128)(2,1)S(1)} %pad_maximum_fusion.5), channel_id=1, source_target_pairs={{0,8},{2,10},{4,12},{6,14},{8,0},{10,2},{12,4},{14,6},{16,24},{18,... | collective-permute-start | bytes 294920 | tf_op jit(solution)/shard_map/ppermute | solution.py:26
  25.4 1.3 %shard_map.95 = (bf16[16,8192]{1,0:T(8,128)(2,1)S(1)}, f32[16,8192]{1,0:T(8,128)S(1)}, bf16[16,8192]{1,0:T(8,128)(2,1)S(1)}) custom-call(bf16[256,256]{1,0:T(8,128)(2,1)S(1)} %get-tuple-element.75.place_ref, bf16[128,512]{1,0:T(8,128)(2,1)S(1)} %collective-permute-done.4.w0_ref, bf16[128,512]{1,0:T(8,128)(2,1)S(1)} %collective-permute-done.5.w1_ref, ...), custom_call_target="tpu_custom_call" | custom-call | flops 1 | bytes 1 | tf_op jit(solution)/shard_map/pallas_call | solution.py:127
  26.6 1.4 %collective-permute-start.6 = (bf16[16,8192]{1,0:T(8,128)(2,1)S(1)}, bf16[16,8192]{1,0:T(8,128)(2,1)S(1)}, u32[]{:S(2)}, u32[]{:S(2)}) collective-permute-start(bf16[16,8192]{1,0:T(8,128)(2,1)S(1)} %get-tuple-element.37), channel_id=1, source_target_pairs={{0,1},{1,0},{2,3},{3,2},{4,5},{5,4},{6,7},{7,6},{8,9},{9,8},{10,11... | collective-permute-start | bytes 786440 | tf_op jit(solution)/shard_map/ppermute | solution.py:26
  28.2 0.5 collective-permute-start.16
  28.7 0.5 collective-permute-done.8
  29.3 0.7 %collective-permute-start.9 = (bf16[64,1536]{1,0:T(8,128)(2,1)S(1)}, bf16[64,1536]{1,0:T(8,128)(2,1)S(1)}, u32[]{:S(2)}, u32[]{:S(2)}) collective-permute-start(bf16[64,1536]{1,0:T(8,128)(2,1)S(1)} %pad_maximum_fusion.2), channel_id=1, source_target_pairs={{0,4},{2,6},{4,0},{6,2},{8,12},{10,14},{12,8},{14,10},{16,20},{18,... | collective-permute-start | bytes 589832 | tf_op jit(solution)/shard_map/ppermute | solution.py:26
  29.9 0.2 slice_bitcast_fusion
  30.1 0.5 shard_map.96
  30.7 1.3 %shard_map.97 = (bf16[128,512]{1,0:T(8,128)(2,1)S(1)}, bf16[128,512]{1,0:T(8,128)(2,1)S(1)}) custom-call(bf16[256,256]{1,0:T(8,128)(2,1)S(1)} %get-tuple-element.76.back_ref, f32[16,8192]{1,0:T(8,128)S(1)} %get-tuple-element.43.part_ref, bf16[16,8192]{1,0:T(8,128)(2,1)S(1)} %collective-permute-done.10.got_ref, ...), custom_call_target="tpu_custom_call" | custom-call | flops 1 | bytes 1 | tf_op jit(solution)/shard_map/pallas_call | solution.py:127
  32.0 3.9 %collective-permute-done.9 = bf16[64,1536]{1,0:T(8,128)(2,1)S(1)} collective-permute-done((bf16[64,1536]{1,0:T(8,128)(2,1)S(1)}, bf16[64,1536]{1,0:T(8,128)(2,1)S(1)}, u32[]{:S(2)}, u32[]{:S(2)}) %collective-permute-start.9) | collective-permute-done | bytes 196640 | tf_op jit(solution)/shard_map/ppermute | solution.py:26
  36.0 0.5 collective-permute-start.18
  36.5 0.1 collective-permute-start.19
  36.6 1.4 %collective-permute-start.22 = (bf16[128,512]{1,0:T(8,128)(2,1)S(1)}, bf16[128,512]{1,0:T(8,128)(2,1)S(1)}, u32[]{:S(2)}, u32[]{:S(2)}) collective-permute-start(bf16[128,512]{1,0:T(8,128)(2,1)S(1)} %get-tuple-element.61), channel_id=1, source_target_pairs={{0,1},{1,0},{2,3},{3,2},{4,5},{5,4},{6,7},{7,6},{8,9},{9,8},{10,11... | collective-permute-start | bytes 393224 | tf_op jit(solution)/shard_map/ppermute | solution.py:26
  38.0 0.8 %collective-permute-start.20 = (bf16[128,512]{1,0:T(8,128)(2,1)S(1)}, bf16[128,512]{1,0:T(8,128)(2,1)S(1)}, u32[]{:S(2)}, u32[]{:S(2)}) collective-permute-start(bf16[128,512]{1,0:T(8,128)(2,1)S(1)} %get-tuple-element.52), channel_id=1, source_target_pairs={{0,1},{1,0},{2,3},{3,2},{4,5},{5,4},{6,7},{7,6},{8,9},{9,8},{10,11... | collective-permute-start | bytes 393224 | tf_op jit(solution)/shard_map/ppermute | solution.py:26
  38.8 0.6 shard_map.98
  39.3 1.8 %shard_map.99 = (bf16[128,512]{1,0:T(8,128)(2,1)S(1)}, bf16[128,512]{1,0:T(8,128)(2,1)S(1)}, bf16[128,512]{1,0:T(8,128)(2,1)S(1)}, bf16[128,512]{1,0:T(8,128)(2,1)S(1)}, bf16[16,8192]{1,0:T(8,128)(2,1)}) custom-call(bf16[256,256]{1,0:T(8,128)(2,1)S(1)} %get-tuple-element.76.back_ref, f32[16,8192]{1,0:T(8,128)S(1)} %get-tuple-element.36.part_ref, ...), custom_call_target="tpu_custom_call" | custom-call | flops 1 | bytes 1 | tf_op jit(solution)/shard_map/pallas_call | solution.py:127
  41.2 1.7 %collective-permute-done.22 = bf16[128,512]{1,0:T(8,128)(2,1)S(1)} collective-permute-done((bf16[128,512]{1,0:T(8,128)(2,1)S(1)}, bf16[128,512]{1,0:T(8,128)(2,1)S(1)}, u32[]{:S(2)}, u32[]{:S(2)}) %collective-permute-start.22) | collective-permute-done | bytes 131104 | tf_op jit(solution)/shard_map/ppermute | solution.py:26
  43.0 2.2 %collective-permute-done.20 = bf16[128,512]{1,0:T(8,128)(2,1)S(1)} collective-permute-done((bf16[128,512]{1,0:T(8,128)(2,1)S(1)}, bf16[128,512]{1,0:T(8,128)(2,1)S(1)}, u32[]{:S(2)}, u32[]{:S(2)}) %collective-permute-start.20) | collective-permute-done | bytes 131104 | tf_op jit(solution)/shard_map/ppermute | solution.py:26
  45.3 1.0 %collective-permute-start.24 = (bf16[64,512]{1,0:T(8,128)(2,1)S(1)}, bf16[64,512]{1,0:T(8,128)(2,1)S(1)}, u32[]{:S(2)}, u32[]{:S(2)}) collective-permute-start(bf16[64,512]{1,0:T(8,128)(2,1)S(1)} %slice.131), channel_id=1, source_target_pairs={{0,4},{2,6},{4,0},{6,2},{8,12},{10,14},{12,8},{14,10},{16,20},{18,... | collective-permute-start | bytes 196616 | tf_op jit(solution)/shard_map/ppermute | solution.py:26
  46.3 1.1 %collective-permute-start.25 = (bf16[64,512]{1,0:T(8,128)(2,1)S(1)}, bf16[64,512]{1,0:T(8,128)(2,1)S(1)}, u32[]{:S(2)}, u32[]{:S(2)}) collective-permute-start(bf16[64,512]{1,0:T(8,128)(2,1)S(1)} %slice.130), channel_id=1, source_target_pairs={{0,4},{2,6},{4,0},{6,2},{8,12},{10,14},{12,8},{14,10},{16,20},{18,... | collective-permute-start | bytes 196616 | tf_op jit(solution)/shard_map/ppermute | solution.py:26
  47.5 2.3 %collective-permute-done.24 = bf16[64,512]{1,0:T(8,128)(2,1)S(1)} collective-permute-done((bf16[64,512]{1,0:T(8,128)(2,1)S(1)}, bf16[64,512]{1,0:T(8,128)(2,1)S(1)}, u32[]{:S(2)}, u32[]{:S(2)}) %collective-permute-start.24) | collective-permute-done | bytes 65568 | tf_op jit(solution)/shard_map/ppermute | solution.py:26
  49.8 0.9 %collective-permute-done.25 = bf16[64,512]{1,0:T(8,128)(2,1)S(1)} collective-permute-done((bf16[64,512]{1,0:T(8,128)(2,1)S(1)}, bf16[64,512]{1,0:T(8,128)(2,1)S(1)}, u32[]{:S(2)}, u32[]{:S(2)}) %collective-permute-start.25) | collective-permute-done | bytes 65568 | tf_op jit(solution)/shard_map/ppermute | solution.py:26
  50.7 1.4 %collective-permute-start.28 = (bf16[16,1024]{1,0:T(8,128)(2,1)S(1)}, bf16[16,1024]{1,0:T(8,128)(2,1)S(1)}, u32[]{:S(2)}, u32[]{:S(2)}) collective-permute-start(bf16[16,1024]{1,0:T(8,128)(2,1)S(1)} %get-tuple-element.69), channel_id=1, source_target_pairs={{0,8},{2,10},{4,12},{6,14},{8,0},{10,2},{12,4},{14,6},{16,24},{18,... | collective-permute-start | bytes 98312 | tf_op jit(solution)/shard_map/ppermute | solution.py:26
  52.1 2.6 %collective-permute-start.27 = (bf16[16,1024]{1,0:T(8,128)(2,1)S(1)}, bf16[16,1024]{1,0:T(8,128)(2,1)S(1)}, u32[]{:S(2)}, u32[]{:S(2)}) collective-permute-start(bf16[16,1024]{1,0:T(8,128)(2,1)S(1)} %get-tuple-element.70), channel_id=1, source_target_pairs={{0,16},{2,18},{4,20},{6,22},{8,24},{10,26},{12,28},{14,30},{16,0},... | collective-permute-start | bytes 98312 | tf_op jit(solution)/shard_map/ppermute | solution.py:26
  54.7 0.5 collective-permute-start.26
  55.2 2.1 %collective-permute-done.27 = bf16[16,1024]{1,0:T(8,128)(2,1)S(1)} collective-permute-done((bf16[16,1024]{1,0:T(8,128)(2,1)S(1)}, bf16[16,1024]{1,0:T(8,128)(2,1)S(1)}, u32[]{:S(2)}, u32[]{:S(2)}) %collective-permute-start.27) | collective-permute-done | bytes 32800 | tf_op jit(solution)/shard_map/ppermute | solution.py:26
  57.3 3.1 %collective-permute-done.26 = bf16[16,1024]{1,0:T(8,128)(2,1)S(1)} collective-permute-done((bf16[16,1024]{1,0:T(8,128)(2,1)S(1)}, bf16[16,1024]{1,0:T(8,128)(2,1)S(1)}, u32[]{:S(2)}, u32[]{:S(2)}) %collective-permute-start.26) | collective-permute-done | bytes 32800 | tf_op jit(solution)/shard_map/ppermute | solution.py:26
  60.4 0.6 %fusion.11 = (f32[1,16,512]{2,1,0:T(8,128)}, f32[1,16,512]{2,1,0:T(8,128)}) fusion(f32[16,1024]{1,0:T(8,128)S(1)} %fusion.6, f32[1,16,512]{2,1,0:T(8,128)S(1)} %copy-done.5, f32[1,16,512]{2,1,0:T(8,128)S(1)} %copy-done.4), kind=kLoop, calls=%fused_computation.46 | loop fusion | flops 73728 | bytes 196608 | tf_op jit(solution)/shard_map/broadcast_in_dim | solution.py:257
  (68 shorter events, 0.8 us)
Async XLA Ops:
  1.4 7.6 %collective-permute-start = (bf16[16,512]{1,0:T(8,128)(2,1)S(1)}, bf16[16,512]{1,0:T(8,128)(2,1)S(1)}, u32[]{:S(2)}, u32[]{:S(2)}) collective-permute-start(bf16[16,512]{1,0:T(8,128)(2,1)S(1)} %bitcast_convert_fusion), channel_id=1, source_target_pairs={{0,16},{2,18},{4,20},{6,22},{8,24},{10,26},{12,28},{14,30},{16,0},... | collective-permute-start | bytes 49160 | tf_op jit(solution)/shard_map/ppermute | solution.py:26
  7.0 4.0 %collective-permute-start.11 = (bf16[16,1024]{1,0:T(8,128)(2,1)S(1)}, bf16[16,1024]{1,0:T(8,128)(2,1)S(1)}, u32[]{:S(2)}, u32[]{:S(2)}) collective-permute-start(bf16[16,1024]{1,0:T(8,128)(2,1)S(1)} %pad_maximum_fusion.10), channel_id=1, source_target_pairs={{0,1},{1,0},{2,3},{3,2},{4,5},{5,4},{6,7},{7,6},{8,9},{9,8},{10,11... | collective-permute-start | bytes 98312 | tf_op jit(solution)/shard_map/ppermute | solution.py:26
  8.6 15.3 %collective-permute-start.7 = (bf16[16,1536]{1,0:T(8,128)(2,1)S(1)}, bf16[16,1536]{1,0:T(8,128)(2,1)S(1)}, u32[]{:S(2)}, u32[]{:S(2)}) collective-permute-start(bf16[16,1536]{1,0:T(8,128)(2,1)S(1)} %pad_maximum_fusion.8), channel_id=1, source_target_pairs={{0,16},{2,18},{4,20},{6,22},{8,24},{10,26},{12,28},{14,30},{16,0},... | collective-permute-start | bytes 147464 | tf_op jit(solution)/shard_map/ppermute | solution.py:26
  9.0 7.1 %copy-start.2 = (bf16[2,64,8192]{2,1,0:T(8,128)(2,1)S(1)}, bf16[2,64,8192]{2,1,0:T(8,128)(2,1)}, u32[]{:S(2)}) copy-start(bf16[2,64,8192]{2,1,0:T(8,128)(2,1)} %param.13) | copy-start | bytes 6291460
  9.0 4.2 %collective-permute-start.1 = (bf16[32,512]{1,0:T(8,128)(2,1)S(1)}, bf16[32,512]{1,0:T(8,128)(2,1)S(1)}, u32[]{:S(2)}, u32[]{:S(2)}) collective-permute-start(bf16[32,512]{1,0:T(8,128)(2,1)S(1)} %pad_maximum_fusion.9), channel_id=1, source_target_pairs={{0,8},{2,10},{4,12},{6,14},{8,0},{10,2},{12,4},{14,6},{16,24},{18,... | collective-permute-start | bytes 98312 | tf_op jit(solution)/shard_map/ppermute | solution.py:26
  11.0 5.2 %collective-permute-start.12 = (bf16[16,1024]{1,0:T(8,128)(2,1)S(1)}, bf16[16,1024]{1,0:T(8,128)(2,1)S(1)}, u32[]{:S(2)}, u32[]{:S(2)}) collective-permute-start(bf16[16,1024]{1,0:T(8,128)(2,1)S(1)} %collective-permute-done.11), channel_id=1, source_target_pairs={{0,16},{2,18},{4,20},{6,22},{8,24},{10,26},{12,28},{14,30},{16,0},... | collective-permute-start | bytes 98312 | tf_op jit(solution)/shard_map/ppermute | solution.py:26
  13.2 5.8 %copy-start.6 = (s32[256]{0:T(256)S(1)}, s32[256]{0:T(256)}, u32[]{:S(2)}) copy-start(s32[256]{0:T(256)} %param.10) | copy-start | bytes 3076
  13.2 4.3 %collective-permute-start.2 = (bf16[64,512]{1,0:T(8,128)(2,1)S(1)}, bf16[64,512]{1,0:T(8,128)(2,1)S(1)}, u32[]{:S(2)}, u32[]{:S(2)}) collective-permute-start(bf16[64,512]{1,0:T(8,128)(2,1)S(1)} %pad_maximum_fusion.6), channel_id=1, source_target_pairs={{0,4},{2,6},{4,0},{6,2},{8,12},{10,14},{12,8},{14,10},{16,20},{18,... | collective-permute-start | bytes 196616 | tf_op jit(solution)/shard_map/ppermute | solution.py:26
  16.2 6.2 %collective-permute-start.13 = (bf16[32,1024]{1,0:T(8,128)(2,1)S(1)}, bf16[32,1024]{1,0:T(8,128)(2,1)S(1)}, u32[]{:S(2)}, u32[]{:S(2)}) collective-permute-start(bf16[32,1024]{1,0:T(8,128)(2,1)S(1)} %pad_maximum_fusion.7), channel_id=1, source_target_pairs={{0,8},{2,10},{4,12},{6,14},{8,0},{10,2},{12,4},{14,6},{16,24},{18,... | collective-permute-start | bytes 196616 | tf_op jit(solution)/shard_map/ppermute | solution.py:26
  17.6 6.4 %collective-permute-start.4 = (bf16[128,512]{1,0:T(8,128)(2,1)S(1)}, bf16[128,512]{1,0:T(8,128)(2,1)S(1)}, u32[]{:S(2)}, u32[]{:S(2)}) collective-permute-start(bf16[128,512]{1,0:T(8,128)(2,1)S(1)} %pad_maximum_fusion.3.w0_ref), channel_id=1, source_target_pairs={{0,1},{1,0},{2,3},{3,2},{4,5},{5,4},{6,7},{7,6},{8,9},{9,8},{10,11... | collective-permute-start | bytes 393224 | tf_op jit(solution)/shard_map/ppermute | solution.py:26
  19.0 1.3 %collective-permute-start.3 = (bf16[128,512]{1,0:T(8,128)(2,1)S(1)}, bf16[128,512]{1,0:T(8,128)(2,1)S(1)}, u32[]{:S(2)}, u32[]{:S(2)}) collective-permute-start(bf16[128,512]{1,0:T(8,128)(2,1)S(1)} %pad_maximum_fusion.3.w0_ref), channel_id=1, source_target_pairs={{0,2},{2,0},{4,6},{6,4},{8,10},{10,8},{12,14},{14,12},{16,18},{18,... | collective-permute-start | bytes 393224 | tf_op jit(solution)/shard_map/ppermute | solution.py:26
  21.6 8.3 %copy-start.1 = (bf16[2,64,8192]{2,1,0:T(8,128)(2,1)S(1)}, bf16[2,64,8192]{2,1,0:T(8,128)(2,1)}, u32[]{:S(2)}) copy-start(bf16[2,64,8192]{2,1,0:T(8,128)(2,1)} %param.12) | copy-start | bytes 6291460
  21.6 8.3 %copy-start.3 = (bf16[2,64,8192]{2,1,0:T(8,128)(2,1)S(1)}, bf16[2,64,8192]{2,1,0:T(8,128)(2,1)}, u32[]{:S(2)}) copy-start(bf16[2,64,8192]{2,1,0:T(8,128)(2,1)} %param.13) | copy-start | bytes 6291460
  21.7 9.0 %collective-permute-start.10 = (bf16[16,8192]{1,0:T(8,128)(2,1)S(1)}, bf16[16,8192]{1,0:T(8,128)(2,1)S(1)}, u32[]{:S(2)}, u32[]{:S(2)}) collective-permute-start(bf16[16,8192]{1,0:T(8,128)(2,1)S(1)} %get-tuple-element.40), channel_id=1, source_target_pairs={{0,1},{1,0},{2,3},{3,2},{4,5},{5,4},{6,7},{7,6},{8,9},{9,8},{10,11... | collective-permute-start | bytes 786440 | tf_op jit(solution)/shard_map/ppermute | solution.py:26
  22.4 5.7 %collective-permute-start.14 = (bf16[64,1024]{1,0:T(8,128)(2,1)S(1)}, bf16[64,1024]{1,0:T(8,128)(2,1)S(1)}, u32[]{:S(2)}, u32[]{:S(2)}) collective-permute-start(bf16[64,1024]{1,0:T(8,128)(2,1)S(1)} %pad_maximum_fusion.4), channel_id=1, source_target_pairs={{0,4},{2,6},{4,0},{6,2},{8,12},{10,14},{12,8},{14,10},{16,20},{18,... | collective-permute-start | bytes 393224 | tf_op jit(solution)/shard_map/ppermute | solution.py:26
  24.0 1.4 %collective-permute-start.5 = (bf16[128,512]{1,0:T(8,128)(2,1)S(1)}, bf16[128,512]{1,0:T(8,128)(2,1)S(1)}, u32[]{:S(2)}, u32[]{:S(2)}) collective-permute-start(bf16[128,512]{1,0:T(8,128)(2,1)S(1)} %collective-permute-done.4.w0_ref), channel_id=1, source_target_pairs={{0,2},{2,0},{4,6},{6,4},{8,10},{10,8},{12,14},{14,12},{16,18},{18,... | collective-permute-start | bytes 393224 | tf_op jit(solution)/shard_map/ppermute | solution.py:26
  24.0 5.3 %collective-permute-start.8 = (bf16[32,1536]{1,0:T(8,128)(2,1)S(1)}, bf16[32,1536]{1,0:T(8,128)(2,1)S(1)}, u32[]{:S(2)}, u32[]{:S(2)}) collective-permute-start(bf16[32,1536]{1,0:T(8,128)(2,1)S(1)} %pad_maximum_fusion.5), channel_id=1, source_target_pairs={{0,8},{2,10},{4,12},{6,14},{8,0},{10,2},{12,4},{14,6},{16,24},{18,... | collective-permute-start | bytes 294920 | tf_op jit(solution)/shard_map/ppermute | solution.py:26
  26.6 12.7 %collective-permute-start.6 = (bf16[16,8192]{1,0:T(8,128)(2,1)S(1)}, bf16[16,8192]{1,0:T(8,128)(2,1)S(1)}, u32[]{:S(2)}, u32[]{:S(2)}) collective-permute-start(bf16[16,8192]{1,0:T(8,128)(2,1)S(1)} %get-tuple-element.37), channel_id=1, source_target_pairs={{0,1},{1,0},{2,3},{3,2},{4,5},{5,4},{6,7},{7,6},{8,9},{9,8},{10,11... | collective-permute-start | bytes 786440 | tf_op jit(solution)/shard_map/ppermute | solution.py:26
  28.1 2.0 %collective-permute-start.15 = (bf16[128,512]{1,0:T(8,128)(2,1)S(1)}, bf16[128,512]{1,0:T(8,128)(2,1)S(1)}, u32[]{:S(2)}, u32[]{:S(2)}) collective-permute-start(bf16[128,512]{1,0:T(8,128)(2,1)S(1)} %get-tuple-element.67.refs_0_), channel_id=1, source_target_pairs={{0,2},{2,0},{4,6},{6,4},{8,10},{10,8},{12,14},{14,12},{16,18},{18,... | collective-permute-start | bytes 393224 | tf_op jit(solution)/shard_map/ppermute | solution.py:26
  28.2 1.9 %collective-permute-start.16 = (bf16[128,512]{1,0:T(8,128)(2,1)S(1)}, bf16[128,512]{1,0:T(8,128)(2,1)S(1)}, u32[]{:S(2)}, u32[]{:S(2)}) collective-permute-start(bf16[128,512]{1,0:T(8,128)(2,1)S(1)} %get-tuple-element.66.refs_1_), channel_id=1, source_target_pairs={{0,2},{2,0},{4,6},{6,4},{8,10},{10,8},{12,14},{14,12},{16,18},{18,... | collective-permute-start | bytes 393224 | tf_op jit(solution)/shard_map/ppermute | solution.py:26
  29.3 6.6 %collective-permute-start.9 = (bf16[64,1536]{1,0:T(8,128)(2,1)S(1)}, bf16[64,1536]{1,0:T(8,128)(2,1)S(1)}, u32[]{:S(2)}, u32[]{:S(2)}) collective-permute-start(bf16[64,1536]{1,0:T(8,128)(2,1)S(1)} %pad_maximum_fusion.2), channel_id=1, source_target_pairs={{0,4},{2,6},{4,0},{6,2},{8,12},{10,14},{12,8},{14,10},{16,20},{18,... | collective-permute-start | bytes 589832 | tf_op jit(solution)/shard_map/ppermute | solution.py:26
  32.0 7.4 %copy-start = (bf16[1,2,8,8192]{3,2,1,0:T(8,128)(2,1)S(1)}, bf16[1,2,8,8192]{3,2,1,0:T(8,128)(2,1)}, u32[]{:S(2)}) copy-start(bf16[1,2,8,8192]{3,2,1,0:T(8,128)(2,1)} %param.11) | copy-start | bytes 786436
  35.9 2.1 %collective-permute-start.17 = (bf16[128,512]{1,0:T(8,128)(2,1)S(1)}, bf16[128,512]{1,0:T(8,128)(2,1)S(1)}, u32[]{:S(2)}, u32[]{:S(2)}) collective-permute-start(bf16[128,512]{1,0:T(8,128)(2,1)S(1)} %get-tuple-element.65.refs_0_), channel_id=1, source_target_pairs={{0,2},{2,0},{4,6},{6,4},{8,10},{10,8},{12,14},{14,12},{16,18},{18,... | collective-permute-start | bytes 393224 | tf_op jit(solution)/shard_map/ppermute | solution.py:26
  36.0 2.8 %collective-permute-start.18 = (bf16[128,512]{1,0:T(8,128)(2,1)S(1)}, bf16[128,512]{1,0:T(8,128)(2,1)S(1)}, u32[]{:S(2)}, u32[]{:S(2)}) collective-permute-start(bf16[128,512]{1,0:T(8,128)(2,1)S(1)} %get-tuple-element.64.refs_1_), channel_id=1, source_target_pairs={{0,2},{2,0},{4,6},{6,4},{8,10},{10,8},{12,14},{14,12},{16,18},{18,... | collective-permute-start | bytes 393224 | tf_op jit(solution)/shard_map/ppermute | solution.py:26
  36.5 2.3 %collective-permute-start.19 = (bf16[128,512]{1,0:T(8,128)(2,1)S(1)}, bf16[128,512]{1,0:T(8,128)(2,1)S(1)}, u32[]{:S(2)}, u32[]{:S(2)}) collective-permute-start(bf16[128,512]{1,0:T(8,128)(2,1)S(1)} %get-tuple-element.63.refs_2_), channel_id=1, source_target_pairs={{0,2},{2,0},{4,6},{6,4},{8,10},{10,8},{12,14},{14,12},{16,18},{18,... | collective-permute-start | bytes 393224 | tf_op jit(solution)/shard_map/ppermute | solution.py:26
  36.6 6.3 %collective-permute-start.22 = (bf16[128,512]{1,0:T(8,128)(2,1)S(1)}, bf16[128,512]{1,0:T(8,128)(2,1)S(1)}, u32[]{:S(2)}, u32[]{:S(2)}) collective-permute-start(bf16[128,512]{1,0:T(8,128)(2,1)S(1)} %get-tuple-element.61), channel_id=1, source_target_pairs={{0,1},{1,0},{2,3},{3,2},{4,5},{5,4},{6,7},{7,6},{8,9},{9,8},{10,11... | collective-permute-start | bytes 393224 | tf_op jit(solution)/shard_map/ppermute | solution.py:26
  38.0 7.2 %collective-permute-start.20 = (bf16[128,512]{1,0:T(8,128)(2,1)S(1)}, bf16[128,512]{1,0:T(8,128)(2,1)S(1)}, u32[]{:S(2)}, u32[]{:S(2)}) collective-permute-start(bf16[128,512]{1,0:T(8,128)(2,1)S(1)} %get-tuple-element.52), channel_id=1, source_target_pairs={{0,1},{1,0},{2,3},{3,2},{4,5},{5,4},{6,7},{7,6},{8,9},{9,8},{10,11... | collective-permute-start | bytes 393224 | tf_op jit(solution)/shard_map/ppermute | solution.py:26
  41.2 19.2 %copy-start.4 = (f32[1,16,512]{2,1,0:T(8,128)S(1)}, f32[1,16,512]{2,1,0:T(8,128)}, u32[]{:S(2)}) copy-start(f32[1,16,512]{2,1,0:T(8,128)} %param.7) | copy-start | bytes 98308
  41.2 19.3 %copy-start.5 = (f32[1,16,512]{2,1,0:T(8,128)S(1)}, f32[1,16,512]{2,1,0:T(8,128)}, u32[]{:S(2)}) copy-start(f32[1,16,512]{2,1,0:T(8,128)} %param.9) | copy-start | bytes 98308
  41.2 1.8 %collective-permute-start.21 = (bf16[128,512]{1,0:T(8,128)(2,1)S(1)}, bf16[128,512]{1,0:T(8,128)(2,1)S(1)}, u32[]{:S(2)}, u32[]{:S(2)}) collective-permute-start(bf16[128,512]{1,0:T(8,128)(2,1)S(1)} %get-tuple-element.58), channel_id=1, source_target_pairs={{0,2},{2,0},{4,6},{6,4},{8,10},{10,8},{12,14},{14,12},{16,18},{18,... | collective-permute-start | bytes 393224 | tf_op jit(solution)/shard_map/ppermute | solution.py:26
  42.9 2.3 %collective-permute-start.23 = (bf16[128,512]{1,0:T(8,128)(2,1)S(1)}, bf16[128,512]{1,0:T(8,128)(2,1)S(1)}, u32[]{:S(2)}, u32[]{:S(2)}) collective-permute-start(bf16[128,512]{1,0:T(8,128)(2,1)S(1)} %add_convert_fusion), channel_id=1, source_target_pairs={{0,2},{2,0},{4,6},{6,4},{8,10},{10,8},{12,14},{14,12},{16,18},{18,... | collective-permute-start | bytes 393224 | tf_op jit(solution)/shard_map/ppermute | solution.py:26
  45.3 4.5 %collective-permute-start.24 = (bf16[64,512]{1,0:T(8,128)(2,1)S(1)}, bf16[64,512]{1,0:T(8,128)(2,1)S(1)}, u32[]{:S(2)}, u32[]{:S(2)}) collective-permute-start(bf16[64,512]{1,0:T(8,128)(2,1)S(1)} %slice.131), channel_id=1, source_target_pairs={{0,4},{2,6},{4,0},{6,2},{8,12},{10,14},{12,8},{14,10},{16,20},{18,... | collective-permute-start | bytes 196616 | tf_op jit(solution)/shard_map/ppermute | solution.py:26
  46.3 4.3 %collective-permute-start.25 = (bf16[64,512]{1,0:T(8,128)(2,1)S(1)}, bf16[64,512]{1,0:T(8,128)(2,1)S(1)}, u32[]{:S(2)}, u32[]{:S(2)}) collective-permute-start(bf16[64,512]{1,0:T(8,128)(2,1)S(1)} %slice.130), channel_id=1, source_target_pairs={{0,4},{2,6},{4,0},{6,2},{8,12},{10,14},{12,8},{14,10},{16,20},{18,... | collective-permute-start | bytes 196616 | tf_op jit(solution)/shard_map/ppermute | solution.py:26
  50.7 4.5 %collective-permute-start.28 = (bf16[16,1024]{1,0:T(8,128)(2,1)S(1)}, bf16[16,1024]{1,0:T(8,128)(2,1)S(1)}, u32[]{:S(2)}, u32[]{:S(2)}) collective-permute-start(bf16[16,1024]{1,0:T(8,128)(2,1)S(1)} %get-tuple-element.69), channel_id=1, source_target_pairs={{0,8},{2,10},{4,12},{6,14},{8,0},{10,2},{12,4},{14,6},{16,24},{18,... | collective-permute-start | bytes 98312 | tf_op jit(solution)/shard_map/ppermute | solution.py:26
  52.1 5.2 %collective-permute-start.27 = (bf16[16,1024]{1,0:T(8,128)(2,1)S(1)}, bf16[16,1024]{1,0:T(8,128)(2,1)S(1)}, u32[]{:S(2)}, u32[]{:S(2)}) collective-permute-start(bf16[16,1024]{1,0:T(8,128)(2,1)S(1)} %get-tuple-element.70), channel_id=1, source_target_pairs={{0,16},{2,18},{4,20},{6,22},{8,24},{10,26},{12,28},{14,30},{16,0},... | collective-permute-start | bytes 98312 | tf_op jit(solution)/shard_map/ppermute | solution.py:26
  54.7 5.7 %collective-permute-start.26 = (bf16[16,1024]{1,0:T(8,128)(2,1)S(1)}, bf16[16,1024]{1,0:T(8,128)(2,1)S(1)}, u32[]{:S(2)}, u32[]{:S(2)}) collective-permute-start(bf16[16,1024]{1,0:T(8,128)(2,1)S(1)} %get-tuple-element.68), channel_id=1, source_target_pairs={{0,24},{2,26},{4,28},{6,30},{8,16},{10,18},{12,20},{14,22},{16,8},... | collective-permute-start | bytes 98312 | tf_op jit(solution)/shard_map/ppermute | solution.py:26

commit v7 on v6

--- a/solution.py
+++ b/solution.py
@@ -150,7 +150,7 @@
     near_w = master[0].astype(BF)
     spans = jnp.concatenate([after(moment[0], near_w), variance[0]], axis=1)
     near_a = spans.astype(BF)
-    low = spans[:, :segment] - lax.reduce_precision(spans[:, :segment], 8, 7)
+    low = (spans[:, :segment] - lax.reduce_precision(spans[:, :segment], 8, 7)).astype(BF)
     steps = []
     for mask in far:
         near_w = jnp.concatenate([near_w, swap(near_w, "dp", mask)], axis=0)
@@ -158,7 +158,8 @@
     blocks_a = [near_a]
     for mask in reversed(mp_bits):
         blocks_a = blocks_a + [swap(b, "mp", mask) for b in blocks_a]
-    blocks_a[0] = jnp.concatenate([near_a, low.astype(BF)], axis=1)
+    blocks_a[0] = jnp.concatenate([near_a, low], axis=1)
+    blocks_a = [after(b, steps[0]) for b in blocks_a]
 
     slot = after(flat_slot, steps[-1])
     owner = (slot // span) ^ me
@@ -196,19 +197,16 @@
         crossed = [swap(p, "mp", mask) for p in sent]
         got = [crossed[k ^ mask] for k in range(n_mp)]
 
-    early = [one[0]] + [sent[0]] * (len(far) - 3)
-
-    def stage(block, mask, event):
-        return jnp.concatenate([block, after(swap(block, "dp", mask), event)], axis=0)
-
-    for mask, event, late in zip(far[:-1], early + [sent[0]], early[1:] + [sent[0], sent[-1]]):
-        blocks_a = [stage(b, mask, event if k else late) for k, b in enumerate(blocks_a)]
+    for mask, event in zip(far[:-1], [one[0]] + [sent[0]] * (len(far) - 2)):
+        arrived = [after(swap(b, "dp", mask), event) for b in blocks_a]
+        blocks_a = [jnp.concatenate(pair, axis=0) for pair in zip(blocks_a, arrived)]
+    arrived = [swap(b, "dp", far[-1]) for b in blocks_a]
 
     half = segments // 2
     kept, away, event = [None] * n_mp, [None] * n_mp, sent[-1]
     for k in reversed(range(n_mp)):
         own = k == 0
-        block = stage(blocks_a[k], far[-1], event)
+        block = jnp.concatenate([blocks_a[k], after(arrived[k], event)], axis=0)
         terms = [block[:, at : at + segment] for at in range(0, block.shape[1], segment)]
         terms += [swap(term, "dp", 1) for term in terms]
         moment_t, rate = call(
@@ -230,25 +228,21 @@
     packed = result[2].astype(F32) + swap(result[3], "dp", 1).astype(F32)
     error = result[4]
 
+    def halves(total, masks):
+        for mask in masks:
+            count = total.shape[0] // 2
+            total = total[:count] + swap(total[count:].astype(BF), "dp", mask).astype(F32)
+        return total
+
     for mask in mp_bits:
         away_got = [swap(p.astype(BF), "mp", mask) for p in away[mask:]]
         kept_got = [after(swap(p.astype(BF), "mp", mask), packed) for p in kept[mask:]]
         away = [p.astype(F32) + q.astype(F32) for p, q in zip(away, away_got)]
         kept = [p.astype(F32) + q.astype(F32) for p, q in zip(kept, kept_got)]
     grad = kept[0] + swap(away[0].astype(BF), "dp", 1).astype(F32)
-
-    def halves(total, masks):
-        for mask in masks:
-            count = total.shape[0] // 2
-            total = total[:count] + swap(total[count:].astype(BF), "dp", mask).astype(F32)
-        return total
-
-    packed, grad = halves(packed, far[:1:-1]), halves(grad, far[:1:-1])
-    both = jnp.concatenate([grad, packed], axis=1)
-    total = both[:span]
-    for k, mask in ((3, far[0] | far[1]), (1, far[0]), (2, far[1])):
-        total = total + swap(both[k * span : (k + 1) * span].astype(BF), "dp", mask).astype(F32)
-    own_grad, own_packed = total[:, :segment], total[:, segment:]
+    packed, grad = halves(packed, far[:-2:-1]), halves(grad, far[:-2:-1])
+    both = halves(jnp.concatenate([grad, packed], axis=1), far[-2::-1])
+    own_grad, own_packed = both[:, :segment], both[:, segment:]
     mean_grad = own_grad / n_dp
     mean_moment = own_packed / n_dp
     moment_new = beta_one * mean_moment + (1.0 - beta_one) * mean_grad

time: 61.5 us -> 58.1 us (0.945)
  waiting for transfers between devices: 18.1 us -> 15 us
  starting transfers between devices: 30 us -> 29.1 us
  other arithmetic: 3.41 us -> 4.03 us
    ppermute x29 -> x28, waiting for transfers between devices: 18.1 us -> 15 us  [swap(): return lax.ppermute(x, axis, [(i, i ^ mask) for i in range(n)])]
    ppermute x29 -> x28, starting transfers between devices: 30 us -> 29.1 us  [swap(): return lax.ppermute(x, axis, [(i, i ^ mask) for i in range(n)])]
  transfers between devices with their start and end apart: 29 -> 28, of which waited for: 10 -> 13; matrix products, arithmetic and copies ran while one was open for 6% -> 8% of each run, Pallas kernels for 11% -> 12%
where the time goes in v7:
time: 58.1 us; the launch traced here: 57.8 us
  starting transfers between devices  29.1 us (50%)
  waiting for transfers between devices  15 us (26%)
  Pallas kernels  6.68 us (11%)
  other arithmetic  4.03 us (7%)
  local copies, waits for them, and re-layouts  1.95 us (3%)
  between operations  0.97 us (2%)
    ppermute x28, starting transfers between devices, swap(): return lax.ppermute(x, axis, [(i, i ^ mask) for i in range(n)])  29.1 us
    ppermute x28, waiting for transfers between devices, swap(): return lax.ppermute(x, axis, [(i, i ^ mask) for i in range(n)])  15 us
    pallas_call x6, Pallas kernels, call(): pl.pallas_call(kernel, out_shape=out_shape, in_specs=[pl.BlockSpec(memory...  6.68 us
    squeeze x3, local copies, waits for them, and re-layouts, tokens_of(): x[step]  1.55 us
  transfers between devices with their start and end apart: 28, of which 13 were waited for; matrix products, arithmetic and copies ran while one was open for 8% of the time, Pallas kernels for 12%

profile of v7, /device:TPU:0, one launch (start us, length us, event | category | flops | bytes accessed | tf_op | source)
XLA Modules:
  0.0 57.8 jit_solution(14027075655582844365)
XLA Ops:
  0.6 0.8 %bitcast_convert_fusion = bf16[16,512]{1,0:T(8,128)(2,1)S(1)} fusion(f32[1,16,512]{2,1,0:T(8,128)} %param.7), kind=kLoop, calls=%fused_computation.39 | loop fusion | flops 8192 | bytes 49152 | tf_op jit(solution)/shard_map/convert_element_type | solution.py:150
  1.4 4.0 %collective-permute-start = (bf16[16,512]{1,0:T(8,128)(2,1)S(1)}, bf16[16,512]{1,0:T(8,128)(2,1)S(1)}, u32[]{:S(2)}, u32[]{:S(2)}) collective-permute-start(bf16[16,512]{1,0:T(8,128)(2,1)S(1)} %bitcast_convert_fusion), channel_id=1, source_target_pairs={{0,16},{2,18},{4,20},{6,22},{8,24},{10,26},{12,28},{14,30},{16,0},... | collective-permute-start | bytes 49160 | tf_op jit(solution)/shard_map/ppermute | solution.py:26
  5.4 0.8 %convert_bitcast_fusion = bf16[16,512]{1,0:T(8,128)(2,1)S(1)} fusion(f32[1,16,512]{2,1,0:T(8,128)} %param.9), kind=kLoop, calls=%fused_computation.48 | loop fusion | flops 8192 | bytes 49152 | tf_op jit(solution)/shard_map/convert.5
  6.2 0.8 %fusion.5 = (bf16[16,512]{1,0:T(8,128)(2,1)S(1)}, bf16[16,512]{1,0:T(8,128)(2,1)S(1)}) fusion(f32[16,512]{1,0:T(8,128)} %bitcast.28), kind=kLoop, calls=%fused_computation.31 | loop fusion | flops 32768 | bytes 65536 | tf_op jit(solution)/shard_map/convert_element_type | solution.py:153
  7.0 1.6 %collective-permute-start.11 = (bf16[16,1024]{1,0:T(8,128)(2,1)S(1)}, bf16[16,1024]{1,0:T(8,128)(2,1)S(1)}, u32[]{:S(2)}, u32[]{:S(2)}) collective-permute-start(bf16[16,1024]{1,0:T(8,128)(2,1)S(1)} %pad_maximum_fusion.9), channel_id=1, source_target_pairs={{0,1},{1,0},{2,3},{3,2},{4,5},{5,4},{6,7},{7,6},{8,9},{9,8},{10,11... | collective-permute-start | bytes 98312 | tf_op jit(solution)/shard_map/ppermute | solution.py:26
  8.6 1.6 %collective-permute-start.1 = (bf16[32,512]{1,0:T(8,128)(2,1)S(1)}, bf16[32,512]{1,0:T(8,128)(2,1)S(1)}, u32[]{:S(2)}, u32[]{:S(2)}) collective-permute-start(bf16[32,512]{1,0:T(8,128)(2,1)S(1)} %pad_maximum_fusion.8), channel_id=1, source_target_pairs={{0,8},{2,10},{4,12},{6,14},{8,0},{10,2},{12,4},{14,6},{16,24},{18,... | collective-permute-start | bytes 98312 | tf_op jit(solution)/shard_map/ppermute | solution.py:26
  10.3 1.4 %collective-permute-start.7 = (bf16[16,1536]{1,0:T(8,128)(2,1)S(1)}, bf16[16,1536]{1,0:T(8,128)(2,1)S(1)}, u32[]{:S(2)}, u32[]{:S(2)}) collective-permute-start(bf16[16,1536]{1,0:T(8,128)(2,1)S(1)} %pad_maximum_fusion.7), channel_id=1, source_target_pairs={{0,16},{2,18},{4,20},{6,22},{8,24},{10,26},{12,28},{14,30},{16,0},... | collective-permute-start | bytes 147464 | tf_op jit(solution)/shard_map/ppermute | solution.py:26
  11.7 1.6 %collective-permute-start.12 = (bf16[16,1024]{1,0:T(8,128)(2,1)S(1)}, bf16[16,1024]{1,0:T(8,128)(2,1)S(1)}, u32[]{:S(2)}, u32[]{:S(2)}) collective-permute-start(bf16[16,1024]{1,0:T(8,128)(2,1)S(1)} %collective-permute-done.11), channel_id=1, source_target_pairs={{0,16},{2,18},{4,20},{6,22},{8,24},{10,26},{12,28},{14,30},{16,0},... | collective-permute-start | bytes 98312 | tf_op jit(solution)/shard_map/ppermute | solution.py:26
  13.3 1.6 %collective-permute-start.2 = (bf16[64,512]{1,0:T(8,128)(2,1)S(1)}, bf16[64,512]{1,0:T(8,128)(2,1)S(1)}, u32[]{:S(2)}, u32[]{:S(2)}) collective-permute-start(bf16[64,512]{1,0:T(8,128)(2,1)S(1)} %pad_maximum_fusion.5), channel_id=1, source_target_pairs={{0,4},{2,6},{4,0},{6,2},{8,12},{10,14},{12,8},{14,10},{16,20},{18,... | collective-permute-start | bytes 196616 | tf_op jit(solution)/shard_map/ppermute | solution.py:26
  14.9 1.3 %slice_bitcast_fusion.3.x_ref = bf16[64,8192]{1,0:T(8,128)(2,1)S(1)} fusion(bf16[2,64,8192]{2,1,0:T(8,128)(2,1)} %param.12), kind=kLoop, calls=%fused_computation.3 | loop fusion | bytes 2097152 | tf_op jit(solution)/shard_map/squeeze | solution.py:123
  16.3 0.4 collective-permute-done.12
  16.6 0.6 %pad_maximum_fusion.4 = bf16[32,1536]{1,0:T(8,128)(2,1)} fusion(bf16[16,1536]{1,0:T(8,128)(2,1)S(1)} %collective-permute-done.7, bf16[16,1536]{1,0:T(8,128)(2,1)S(1)} %pad_maximum_fusion.7), kind=kLoop, calls=%fused_computation.24 | loop fusion | flops 196608 | bytes 196608 | tf_op jit(solution)/shard_map/concatenate | solution.py:202
  17.3 1.0 %collective-permute-start.13 = (bf16[32,1024]{1,0:T(8,128)(2,1)S(1)}, bf16[32,1024]{1,0:T(8,128)(2,1)S(1)}, u32[]{:S(2)}, u32[]{:S(2)}) collective-permute-start(bf16[32,1024]{1,0:T(8,128)(2,1)S(1)} %pad_maximum_fusion.6), channel_id=1, source_target_pairs={{0,8},{2,10},{4,12},{6,14},{8,0},{10,2},{12,4},{14,6},{16,24},{18,... | collective-permute-start | bytes 196616 | tf_op jit(solution)/shard_map/ppermute | solution.py:26
  18.2 1.1 %collective-permute-start.8 = (bf16[32,1536]{1,0:T(8,128)(2,1)}, bf16[32,1536]{1,0:T(8,128)(2,1)S(1)}, u32[]{:S(2)}, u32[]{:S(2)}) collective-permute-start(bf16[32,1536]{1,0:T(8,128)(2,1)} %pad_maximum_fusion.4), channel_id=1, source_target_pairs={{0,8},{2,10},{4,12},{6,14},{8,0},{10,2},{12,4},{14,6},{16,24},{18,... | collective-permute-start | bytes 294920 | tf_op jit(solution)/shard_map/ppermute | solution.py:26
  19.4 1.6 %collective-permute-start.4 = (bf16[128,512]{1,0:T(8,128)(2,1)S(1)}, bf16[128,512]{1,0:T(8,128)(2,1)S(1)}, u32[]{:S(2)}, u32[]{:S(2)}) collective-permute-start(bf16[128,512]{1,0:T(8,128)(2,1)S(1)} %pad_maximum_fusion.2.w0_ref), channel_id=1, source_target_pairs={{0,1},{1,0},{2,3},{3,2},{4,5},{5,4},{6,7},{7,6},{8,9},{9,8},{10,11... | collective-permute-start | bytes 393224 | tf_op jit(solution)/shard_map/ppermute | solution.py:26
  21.2 0.1 fusion.1
  21.3 1.0 %collective-permute-done.3.w1_ref = bf16[128,512]{1,0:T(8,128)(2,1)S(1)} collective-permute-done((bf16[128,512]{1,0:T(8,128)(2,1)S(1)}, bf16[128,512]{1,0:T(8,128)(2,1)S(1)}, u32[]{:S(2)}, u32[]{:S(2)}) %collective-permute-start.3) | collective-permute-done | bytes 131104 | tf_op jit(solution)/shard_map/ppermute | solution.py:26
  22.3 1.3 %shard_map.94 = (bf16[16,8192]{1,0:T(8,128)(2,1)S(1)}, f32[16,8192]{1,0:T(8,128)S(1)}, bf16[16,8192]{1,0:T(8,128)(2,1)S(1)}) custom-call(bf16[256,256]{1,0:T(8,128)(2,1)S(1)} %get-tuple-element.76.place_ref, bf16[128,512]{1,0:T(8,128)(2,1)S(1)} %pad_maximum_fusion.2.w0_ref, bf16[128,512]{1,0:T(8,128)(2,1)S(1)} %collective-permute-done.3.w1_ref, ...), custom_call_target="tpu_custom_call" | custom-call | flops 1 | bytes 1 | tf_op jit(solution)/shard_map/pallas_call | solution.py:127
  23.6 0.6 collective-permute-start.10
  24.2 1.6 %collective-permute-start.14 = (bf16[64,1024]{1,0:T(8,128)(2,1)S(1)}, bf16[64,1024]{1,0:T(8,128)(2,1)S(1)}, u32[]{:S(2)}, u32[]{:S(2)}) collective-permute-start(bf16[64,1024]{1,0:T(8,128)(2,1)S(1)} %pad_maximum_fusion.3), channel_id=1, source_target_pairs={{0,4},{2,6},{4,0},{6,2},{8,12},{10,14},{12,8},{14,10},{16,20},{18,... | collective-permute-start | bytes 393224 | tf_op jit(solution)/shard_map/ppermute | solution.py:26
  25.9 0.6 %collective-permute-start.9 = (bf16[64,1536]{1,0:T(8,128)(2,1)S(1)}, bf16[64,1536]{1,0:T(8,128)(2,1)S(1)}, u32[]{:S(2)}, u32[]{:S(2)}) collective-permute-start(bf16[64,1536]{1,0:T(8,128)(2,1)S(1)} %pad_maximum_fusion), channel_id=1, source_target_pairs={{0,4},{2,6},{4,0},{6,2},{8,12},{10,14},{12,8},{14,10},{16,20},{18,... | collective-permute-start | bytes 589832 | tf_op jit(solution)/shard_map/ppermute | solution.py:26
  26.5 0.7 %collective-permute-done.5.w1_ref = bf16[128,512]{1,0:T(8,128)(2,1)S(1)} collective-permute-done((bf16[128,512]{1,0:T(8,128)(2,1)S(1)}, bf16[128,512]{1,0:T(8,128)(2,1)S(1)}, u32[]{:S(2)}, u32[]{:S(2)}) %collective-permute-start.5) | collective-permute-done | bytes 131104 | tf_op jit(solution)/shard_map/ppermute | solution.py:26
  27.2 1.3 %shard_map.95 = (bf16[16,8192]{1,0:T(8,128)(2,1)S(1)}, f32[16,8192]{1,0:T(8,128)S(1)}, bf16[16,8192]{1,0:T(8,128)(2,1)S(1)}) custom-call(bf16[256,256]{1,0:T(8,128)(2,1)S(1)} %get-tuple-element.76.place_ref, bf16[128,512]{1,0:T(8,128)(2,1)S(1)} %collective-permute-done.4.w0_ref, bf16[128,512]{1,0:T(8,128)(2,1)S(1)} %collective-permute-done.5.w1_ref, ...), custom_call_target="tpu_custom_call" | custom-call | flops 1 | bytes 1 | tf_op jit(solution)/shard_map/pallas_call | solution.py:127
  28.5 1.6 %collective-permute-start.6 = (bf16[16,8192]{1,0:T(8,128)(2,1)S(1)}, bf16[16,8192]{1,0:T(8,128)(2,1)S(1)}, u32[]{:S(2)}, u32[]{:S(2)}) collective-permute-start(bf16[16,8192]{1,0:T(8,128)(2,1)S(1)} %get-tuple-element.39), channel_id=1, source_target_pairs={{0,1},{1,0},{2,3},{3,2},{4,5},{5,4},{6,7},{7,6},{8,9},{9,8},{10,11... | collective-permute-start | bytes 786440 | tf_op jit(solution)/shard_map/ppermute | solution.py:26
  30.2 0.5 collective-permute-start.15
  30.7 0.2 slice_bitcast_fusion
  30.9 0.6 %collective-permute-done.16.refs_3_ = bf16[128,512]{1,0:T(8,128)(2,1)S(1)} collective-permute-done((bf16[128,512]{1,0:T(8,128)(2,1)S(1)}, bf16[128,512]{1,0:T(8,128)(2,1)S(1)}, u32[]{:S(2)}, u32[]{:S(2)}) %collective-permute-start.16) | collective-permute-done | bytes 131104 | tf_op jit(solution)/shard_map/ppermute | solution.py:26
  31.5 0.2 collective-permute-done.15.refs_2_
  31.7 0.5 shard_map.96
  32.2 0.5 collective-permute-done.10.got_ref
  32.7 1.3 %shard_map.97 = (bf16[128,512]{1,0:T(8,128)(2,1)S(1)}, bf16[128,512]{1,0:T(8,128)(2,1)S(1)}) custom-call(bf16[256,256]{1,0:T(8,128)(2,1)S(1)} %get-tuple-element.77.back_ref, f32[16,8192]{1,0:T(8,128)S(1)} %get-tuple-element.46.part_ref, bf16[16,8192]{1,0:T(8,128)(2,1)S(1)} %collective-permute-done.10.got_ref, ...), custom_call_target="tpu_custom_call" | custom-call | flops 1 | bytes 1 | tf_op jit(solution)/shard_map/pallas_call | solution.py:127
  34.1 0.5 collective-permute-start.18
  34.7 1.3 %collective-permute-start.22 = (bf16[128,512]{1,0:T(8,128)(2,1)S(1)}, bf16[128,512]{1,0:T(8,128)(2,1)S(1)}, u32[]{:S(2)}, u32[]{:S(2)}) collective-permute-start(bf16[128,512]{1,0:T(8,128)(2,1)S(1)} %get-tuple-element.65), channel_id=1, source_target_pairs={{0,1},{1,0},{2,3},{3,2},{4,5},{5,4},{6,7},{7,6},{8,9},{9,8},{10,11... | collective-permute-start | bytes 393224 | tf_op jit(solution)/shard_map/ppermute | solution.py:26
  36.0 0.8 %collective-permute-start.20 = (bf16[128,512]{1,0:T(8,128)(2,1)S(1)}, bf16[128,512]{1,0:T(8,128)(2,1)S(1)}, u32[]{:S(2)}, u32[]{:S(2)}) collective-permute-start(bf16[128,512]{1,0:T(8,128)(2,1)S(1)} %get-tuple-element.56), channel_id=1, source_target_pairs={{0,1},{1,0},{2,3},{3,2},{4,5},{5,4},{6,7},{7,6},{8,9},{9,8},{10,11... | collective-permute-start | bytes 393224 | tf_op jit(solution)/shard_map/ppermute | solution.py:26
  36.8 0.6 shard_map.98
  37.3 0.3 collective-permute-done.6.got_ref
  37.6 1.8 %shard_map.99 = (bf16[128,512]{1,0:T(8,128)(2,1)S(1)}, bf16[128,512]{1,0:T(8,128)(2,1)S(1)}, bf16[128,512]{1,0:T(8,128)(2,1)S(1)}, bf16[128,512]{1,0:T(8,128)(2,1)S(1)}, bf16[16,8192]{1,0:T(8,128)(2,1)}) custom-call(bf16[256,256]{1,0:T(8,128)(2,1)S(1)} %get-tuple-element.77.back_ref, f32[16,8192]{1,0:T(8,128)S(1)} %get-tuple-element.38.part_ref, ...), custom_call_target="tpu_custom_call" | custom-call | flops 1 | bytes 1 | tf_op jit(solution)/shard_map/pallas_call | solution.py:127
  39.5 1.5 %collective-permute-done.22 = bf16[128,512]{1,0:T(8,128)(2,1)S(1)} collective-permute-done((bf16[128,512]{1,0:T(8,128)(2,1)S(1)}, bf16[128,512]{1,0:T(8,128)(2,1)S(1)}, u32[]{:S(2)}, u32[]{:S(2)}) %collective-permute-start.22) | collective-permute-done | bytes 131104 | tf_op jit(solution)/shard_map/ppermute | solution.py:26
  41.2 2.0 %collective-permute-start.25 = (bf16[64,512]{1,0:T(8,128)(2,1)S(1)}, bf16[64,512]{1,0:T(8,128)(2,1)S(1)}, u32[]{:S(2)}, u32[]{:S(2)}) collective-permute-start(bf16[64,512]{1,0:T(8,128)(2,1)S(1)} %slice.126), channel_id=1, source_target_pairs={{0,4},{2,6},{4,0},{6,2},{8,12},{10,14},{12,8},{14,10},{16,20},{18,... | collective-permute-start | bytes 196616 | tf_op jit(solution)/shard_map/ppermute | solution.py:26
  43.2 0.2 collective-permute-done.20
  43.5 1.7 %collective-permute-start.24 = (bf16[64,512]{1,0:T(8,128)(2,1)S(1)}, bf16[64,512]{1,0:T(8,128)(2,1)S(1)}, u32[]{:S(2)}, u32[]{:S(2)}) collective-permute-start(bf16[64,512]{1,0:T(8,128)(2,1)S(1)} %slice.127), channel_id=1, source_target_pairs={{0,4},{2,6},{4,0},{6,2},{8,12},{10,14},{12,8},{14,10},{16,20},{18,... | collective-permute-start | bytes 196616 | tf_op jit(solution)/shard_map/ppermute | solution.py:26
  45.1 0.8 %collective-permute-done.25 = bf16[64,512]{1,0:T(8,128)(2,1)S(1)} collective-permute-done((bf16[64,512]{1,0:T(8,128)(2,1)S(1)}, bf16[64,512]{1,0:T(8,128)(2,1)S(1)}, u32[]{:S(2)}, u32[]{:S(2)}) %collective-permute-start.25) | collective-permute-done | bytes 65568 | tf_op jit(solution)/shard_map/ppermute | solution.py:26
  45.9 1.9 %collective-permute-done.24 = bf16[64,512]{1,0:T(8,128)(2,1)S(1)} collective-permute-done((bf16[64,512]{1,0:T(8,128)(2,1)S(1)}, bf16[64,512]{1,0:T(8,128)(2,1)S(1)}, u32[]{:S(2)}, u32[]{:S(2)}) %collective-permute-start.24) | collective-permute-done | bytes 65568 | tf_op jit(solution)/shard_map/ppermute | solution.py:26
  47.8 1.0 %collective-permute-start.26 = (bf16[32,1024]{1,0:T(8,128)(2,1)S(1)}, bf16[32,1024]{1,0:T(8,128)(2,1)S(1)}, u32[]{:S(2)}, u32[]{:S(2)}) collective-permute-start(bf16[32,1024]{1,0:T(8,128)(2,1)S(1)} %fusion.4), channel_id=1, source_target_pairs={{0,8},{2,10},{4,12},{6,14},{8,0},{10,2},{12,4},{14,6},{16,24},{18,... | collective-permute-start | bytes 196616 | tf_op jit(solution)/shard_map/ppermute | solution.py:26
  48.8 3.4 %collective-permute-done.26 = bf16[32,1024]{1,0:T(8,128)(2,1)S(1)} collective-permute-done((bf16[32,1024]{1,0:T(8,128)(2,1)S(1)}, bf16[32,1024]{1,0:T(8,128)(2,1)S(1)}, u32[]{:S(2)}, u32[]{:S(2)}) %collective-permute-start.26) | collective-permute-done | bytes 65568 | tf_op jit(solution)/shard_map/ppermute | solution.py:26
  52.2 1.4 %collective-permute-start.27 = (bf16[16,1024]{1,0:T(8,128)(2,1)S(1)}, bf16[16,1024]{1,0:T(8,128)(2,1)S(1)}, u32[]{:S(2)}, u32[]{:S(2)}) collective-permute-start(bf16[16,1024]{1,0:T(8,128)(2,1)S(1)} %slice.128), channel_id=1, source_target_pairs={{0,16},{2,18},{4,20},{6,22},{8,24},{10,26},{12,28},{14,30},{16,0},... | collective-permute-start | bytes 98312 | tf_op jit(solution)/shard_map/ppermute | solution.py:26
  53.5 3.5 %collective-permute-done.27 = bf16[16,1024]{1,0:T(8,128)(2,1)S(1)} collective-permute-done((bf16[16,1024]{1,0:T(8,128)(2,1)S(1)}, bf16[16,1024]{1,0:T(8,128)(2,1)S(1)}, u32[]{:S(2)}, u32[]{:S(2)}) %collective-permute-start.27) | collective-permute-done | bytes 32800 | tf_op jit(solution)/shard_map/ppermute | solution.py:26
  57.1 0.6 %fusion.9 = (f32[1,16,512]{2,1,0:T(8,128)}, f32[1,16,512]{2,1,0:T(8,128)}) fusion(f32[16,1024]{1,0:T(8,128)S(1)} %slice_add_fusion.2, f32[1,16,512]{2,1,0:T(8,128)S(1)} %copy-done.5, f32[1,16,512]{2,1,0:T(8,128)S(1)} %copy-done.4), kind=kLoop, calls=%fused_computation.49 | loop fusion | flops 73728 | bytes 196608 | tf_op jit(solution)/shard_map/broadcast_in_dim | solution.py:251
  (70 shorter events, 1.1 us)
Async XLA Ops:
  1.4 7.2 %collective-permute-start = (bf16[16,512]{1,0:T(8,128)(2,1)S(1)}, bf16[16,512]{1,0:T(8,128)(2,1)S(1)}, u32[]{:S(2)}, u32[]{:S(2)}) collective-permute-start(bf16[16,512]{1,0:T(8,128)(2,1)S(1)} %bitcast_convert_fusion), channel_id=1, source_target_pairs={{0,16},{2,18},{4,20},{6,22},{8,24},{10,26},{12,28},{14,30},{16,0},... | collective-permute-start | bytes 49160 | tf_op jit(solution)/shard_map/ppermute | solution.py:26
  7.0 4.7 %collective-permute-start.11 = (bf16[16,1024]{1,0:T(8,128)(2,1)S(1)}, bf16[16,1024]{1,0:T(8,128)(2,1)S(1)}, u32[]{:S(2)}, u32[]{:S(2)}) collective-permute-start(bf16[16,1024]{1,0:T(8,128)(2,1)S(1)} %pad_maximum_fusion.9), channel_id=1, source_target_pairs={{0,1},{1,0},{2,3},{3,2},{4,5},{5,4},{6,7},{7,6},{8,9},{9,8},{10,11... | collective-permute-start | bytes 98312 | tf_op jit(solution)/shard_map/ppermute | solution.py:26
  8.6 7.5 %copy-start.2 = (bf16[2,64,8192]{2,1,0:T(8,128)(2,1)S(1)}, bf16[2,64,8192]{2,1,0:T(8,128)(2,1)}, u32[]{:S(2)}) copy-start(bf16[2,64,8192]{2,1,0:T(8,128)(2,1)} %param.13) | copy-start | bytes 6291460
  8.6 4.6 %collective-permute-start.1 = (bf16[32,512]{1,0:T(8,128)(2,1)S(1)}, bf16[32,512]{1,0:T(8,128)(2,1)S(1)}, u32[]{:S(2)}, u32[]{:S(2)}) collective-permute-start(bf16[32,512]{1,0:T(8,128)(2,1)S(1)} %pad_maximum_fusion.8), channel_id=1, source_target_pairs={{0,8},{2,10},{4,12},{6,14},{8,0},{10,2},{12,4},{14,6},{16,24},{18,... | collective-permute-start | bytes 98312 | tf_op jit(solution)/shard_map/ppermute | solution.py:26
  10.3 6.3 %collective-permute-start.7 = (bf16[16,1536]{1,0:T(8,128)(2,1)S(1)}, bf16[16,1536]{1,0:T(8,128)(2,1)S(1)}, u32[]{:S(2)}, u32[]{:S(2)}) collective-permute-start(bf16[16,1536]{1,0:T(8,128)(2,1)S(1)} %pad_maximum_fusion.7), channel_id=1, source_target_pairs={{0,16},{2,18},{4,20},{6,22},{8,24},{10,26},{12,28},{14,30},{16,0},... | collective-permute-start | bytes 147464 | tf_op jit(solution)/shard_map/ppermute | solution.py:26
  11.7 4.9 %collective-permute-start.12 = (bf16[16,1024]{1,0:T(8,128)(2,1)S(1)}, bf16[16,1024]{1,0:T(8,128)(2,1)S(1)}, u32[]{:S(2)}, u32[]{:S(2)}) collective-permute-start(bf16[16,1024]{1,0:T(8,128)(2,1)S(1)} %collective-permute-done.11), channel_id=1, source_target_pairs={{0,16},{2,18},{4,20},{6,22},{8,24},{10,26},{12,28},{14,30},{16,0},... | collective-permute-start | bytes 98312 | tf_op jit(solution)/shard_map/ppermute | solution.py:26
  13.3 7.7 %copy-start.6 = (s32[256]{0:T(256)S(1)}, s32[256]{0:T(256)}, u32[]{:S(2)}) copy-start(s32[256]{0:T(256)} %param.10) | copy-start | bytes 3076
  13.3 6.1 %collective-permute-start.2 = (bf16[64,512]{1,0:T(8,128)(2,1)S(1)}, bf16[64,512]{1,0:T(8,128)(2,1)S(1)}, u32[]{:S(2)}, u32[]{:S(2)}) collective-permute-start(bf16[64,512]{1,0:T(8,128)(2,1)S(1)} %pad_maximum_fusion.5), channel_id=1, source_target_pairs={{0,4},{2,6},{4,0},{6,2},{8,12},{10,14},{12,8},{14,10},{16,20},{18,... | collective-permute-start | bytes 196616 | tf_op jit(solution)/shard_map/ppermute | solution.py:26
  17.3 6.9 %collective-permute-start.13 = (bf16[32,1024]{1,0:T(8,128)(2,1)S(1)}, bf16[32,1024]{1,0:T(8,128)(2,1)S(1)}, u32[]{:S(2)}, u32[]{:S(2)}) collective-permute-start(bf16[32,1024]{1,0:T(8,128)(2,1)S(1)} %pad_maximum_fusion.6), channel_id=1, source_target_pairs={{0,8},{2,10},{4,12},{6,14},{8,0},{10,2},{12,4},{14,6},{16,24},{18,... | collective-permute-start | bytes 196616 | tf_op jit(solution)/shard_map/ppermute | solution.py:26
  18.2 6.0 %collective-permute-start.8 = (bf16[32,1536]{1,0:T(8,128)(2,1)}, bf16[32,1536]{1,0:T(8,128)(2,1)S(1)}, u32[]{:S(2)}, u32[]{:S(2)}) collective-permute-start(bf16[32,1536]{1,0:T(8,128)(2,1)} %pad_maximum_fusion.4), channel_id=1, source_target_pairs={{0,8},{2,10},{4,12},{6,14},{8,0},{10,2},{12,4},{14,6},{16,24},{18,... | collective-permute-start | bytes 294920 | tf_op jit(solution)/shard_map/ppermute | solution.py:26
  19.4 6.4 %collective-permute-start.4 = (bf16[128,512]{1,0:T(8,128)(2,1)S(1)}, bf16[128,512]{1,0:T(8,128)(2,1)S(1)}, u32[]{:S(2)}, u32[]{:S(2)}) collective-permute-start(bf16[128,512]{1,0:T(8,128)(2,1)S(1)} %pad_maximum_fusion.2.w0_ref), channel_id=1, source_target_pairs={{0,1},{1,0},{2,3},{3,2},{4,5},{5,4},{6,7},{7,6},{8,9},{9,8},{10,11... | collective-permute-start | bytes 393224 | tf_op jit(solution)/shard_map/ppermute | solution.py:26
  21.0 1.3 %collective-permute-start.3 = (bf16[128,512]{1,0:T(8,128)(2,1)S(1)}, bf16[128,512]{1,0:T(8,128)(2,1)S(1)}, u32[]{:S(2)}, u32[]{:S(2)}) collective-permute-start(bf16[128,512]{1,0:T(8,128)(2,1)S(1)} %pad_maximum_fusion.2.w0_ref), channel_id=1, source_target_pairs={{0,2},{2,0},{4,6},{6,4},{8,10},{10,8},{12,14},{14,12},{16,18},{18,... | collective-permute-start | bytes 393224 | tf_op jit(solution)/shard_map/ppermute | solution.py:26
  23.6 7.1 %copy-start.1 = (bf16[2,64,8192]{2,1,0:T(8,128)(2,1)S(1)}, bf16[2,64,8192]{2,1,0:T(8,128)(2,1)}, u32[]{:S(2)}) copy-start(bf16[2,64,8192]{2,1,0:T(8,128)(2,1)} %param.12) | copy-start | bytes 6291460
  23.6 7.1 %copy-start.3 = (bf16[2,64,8192]{2,1,0:T(8,128)(2,1)S(1)}, bf16[2,64,8192]{2,1,0:T(8,128)(2,1)}, u32[]{:S(2)}) copy-start(bf16[2,64,8192]{2,1,0:T(8,128)(2,1)} %param.13) | copy-start | bytes 6291460
  23.6 9.1 %collective-permute-start.10 = (bf16[16,8192]{1,0:T(8,128)(2,1)S(1)}, bf16[16,8192]{1,0:T(8,128)(2,1)S(1)}, u32[]{:S(2)}, u32[]{:S(2)}) collective-permute-start(bf16[16,8192]{1,0:T(8,128)(2,1)S(1)} %get-tuple-element.44), channel_id=1, source_target_pairs={{0,1},{1,0},{2,3},{3,2},{4,5},{5,4},{6,7},{7,6},{8,9},{9,8},{10,11... | collective-permute-start | bytes 786440 | tf_op jit(solution)/shard_map/ppermute | solution.py:26
  24.2 5.8 %collective-permute-start.14 = (bf16[64,1024]{1,0:T(8,128)(2,1)S(1)}, bf16[64,1024]{1,0:T(8,128)(2,1)S(1)}, u32[]{:S(2)}, u32[]{:S(2)}) collective-permute-start(bf16[64,1024]{1,0:T(8,128)(2,1)S(1)} %pad_maximum_fusion.3), channel_id=1, source_target_pairs={{0,4},{2,6},{4,0},{6,2},{8,12},{10,14},{12,8},{14,10},{16,20},{18,... | collective-permute-start | bytes 393224 | tf_op jit(solution)/shard_map/ppermute | solution.py:26
  25.8 1.4 %collective-permute-start.5 = (bf16[128,512]{1,0:T(8,128)(2,1)S(1)}, bf16[128,512]{1,0:T(8,128)(2,1)S(1)}, u32[]{:S(2)}, u32[]{:S(2)}) collective-permute-start(bf16[128,512]{1,0:T(8,128)(2,1)S(1)} %collective-permute-done.4.w0_ref), channel_id=1, source_target_pairs={{0,2},{2,0},{4,6},{6,4},{8,10},{10,8},{12,14},{14,12},{16,18},{18,... | collective-permute-start | bytes 393224 | tf_op jit(solution)/shard_map/ppermute | solution.py:26
  25.9 8.1 %collective-permute-start.9 = (bf16[64,1536]{1,0:T(8,128)(2,1)S(1)}, bf16[64,1536]{1,0:T(8,128)(2,1)S(1)}, u32[]{:S(2)}, u32[]{:S(2)}) collective-permute-start(bf16[64,1536]{1,0:T(8,128)(2,1)S(1)} %pad_maximum_fusion), channel_id=1, source_target_pairs={{0,4},{2,6},{4,0},{6,2},{8,12},{10,14},{12,8},{14,10},{16,20},{18,... | collective-permute-start | bytes 589832 | tf_op jit(solution)/shard_map/ppermute | solution.py:26
  28.5 9.2 %collective-permute-start.6 = (bf16[16,8192]{1,0:T(8,128)(2,1)S(1)}, bf16[16,8192]{1,0:T(8,128)(2,1)S(1)}, u32[]{:S(2)}, u32[]{:S(2)}) collective-permute-start(bf16[16,8192]{1,0:T(8,128)(2,1)S(1)} %get-tuple-element.39), channel_id=1, source_target_pairs={{0,1},{1,0},{2,3},{3,2},{4,5},{5,4},{6,7},{7,6},{8,9},{9,8},{10,11... | collective-permute-start | bytes 786440 | tf_op jit(solution)/shard_map/ppermute | solution.py:26
  30.1 1.4 %collective-permute-start.16 = (bf16[128,512]{1,0:T(8,128)(2,1)S(1)}, bf16[128,512]{1,0:T(8,128)(2,1)S(1)}, u32[]{:S(2)}, u32[]{:S(2)}) collective-permute-start(bf16[128,512]{1,0:T(8,128)(2,1)S(1)} %get-tuple-element.70.refs_1_), channel_id=1, source_target_pairs={{0,2},{2,0},{4,6},{6,4},{8,10},{10,8},{12,14},{14,12},{16,18},{18,... | collective-permute-start | bytes 393224 | tf_op jit(solution)/shard_map/ppermute | solution.py:26
  30.2 1.5 %collective-permute-start.15 = (bf16[128,512]{1,0:T(8,128)(2,1)S(1)}, bf16[128,512]{1,0:T(8,128)(2,1)S(1)}, u32[]{:S(2)}, u32[]{:S(2)}) collective-permute-start(bf16[128,512]{1,0:T(8,128)(2,1)S(1)} %get-tuple-element.71.refs_0_), channel_id=1, source_target_pairs={{0,2},{2,0},{4,6},{6,4},{8,10},{10,8},{12,14},{14,12},{16,18},{18,... | collective-permute-start | bytes 393224 | tf_op jit(solution)/shard_map/ppermute | solution.py:26
  34.0 3.7 %copy-start = (bf16[1,2,8,8192]{3,2,1,0:T(8,128)(2,1)S(1)}, bf16[1,2,8,8192]{3,2,1,0:T(8,128)(2,1)}, u32[]{:S(2)}) copy-start(bf16[1,2,8,8192]{3,2,1,0:T(8,128)(2,1)} %param.11) | copy-start | bytes 786436
  34.1 1.9 %collective-permute-start.19 = (bf16[128,512]{1,0:T(8,128)(2,1)S(1)}, bf16[128,512]{1,0:T(8,128)(2,1)S(1)}, u32[]{:S(2)}, u32[]{:S(2)}) collective-permute-start(bf16[128,512]{1,0:T(8,128)(2,1)S(1)} %get-tuple-element.67.refs_2_), channel_id=1, source_target_pairs={{0,2},{2,0},{4,6},{6,4},{8,10},{10,8},{12,14},{14,12},{16,18},{18,... | collective-permute-start | bytes 393224 | tf_op jit(solution)/shard_map/ppermute | solution.py:26
  34.1 2.6 %collective-permute-start.18 = (bf16[128,512]{1,0:T(8,128)(2,1)S(1)}, bf16[128,512]{1,0:T(8,128)(2,1)S(1)}, u32[]{:S(2)}, u32[]{:S(2)}) collective-permute-start(bf16[128,512]{1,0:T(8,128)(2,1)S(1)} %get-tuple-element.68.refs_1_), channel_id=1, source_target_pairs={{0,2},{2,0},{4,6},{6,4},{8,10},{10,8},{12,14},{14,12},{16,18},{18,... | collective-permute-start | bytes 393224 | tf_op jit(solution)/shard_map/ppermute | solution.py:26
  34.6 2.1 %collective-permute-start.17 = (bf16[128,512]{1,0:T(8,128)(2,1)S(1)}, bf16[128,512]{1,0:T(8,128)(2,1)S(1)}, u32[]{:S(2)}, u32[]{:S(2)}) collective-permute-start(bf16[128,512]{1,0:T(8,128)(2,1)S(1)} %get-tuple-element.69.refs_0_), channel_id=1, source_target_pairs={{0,2},{2,0},{4,6},{6,4},{8,10},{10,8},{12,14},{14,12},{16,18},{18,... | collective-permute-start | bytes 393224 | tf_op jit(solution)/shard_map/ppermute | solution.py:26
  34.7 6.3 %collective-permute-start.22 = (bf16[128,512]{1,0:T(8,128)(2,1)S(1)}, bf16[128,512]{1,0:T(8,128)(2,1)S(1)}, u32[]{:S(2)}, u32[]{:S(2)}) collective-permute-start(bf16[128,512]{1,0:T(8,128)(2,1)S(1)} %get-tuple-element.65), channel_id=1, source_target_pairs={{0,1},{1,0},{2,3},{3,2},{4,5},{5,4},{6,7},{7,6},{8,9},{9,8},{10,11... | collective-permute-start | bytes 393224 | tf_op jit(solution)/shard_map/ppermute | solution.py:26
  36.0 7.4 %collective-permute-start.20 = (bf16[128,512]{1,0:T(8,128)(2,1)S(1)}, bf16[128,512]{1,0:T(8,128)(2,1)S(1)}, u32[]{:S(2)}, u32[]{:S(2)}) collective-permute-start(bf16[128,512]{1,0:T(8,128)(2,1)S(1)} %get-tuple-element.56), channel_id=1, source_target_pairs={{0,1},{1,0},{2,3},{3,2},{4,5},{5,4},{6,7},{7,6},{8,9},{9,8},{10,11... | collective-permute-start | bytes 393224 | tf_op jit(solution)/shard_map/ppermute | solution.py:26
  39.5 17.6 %copy-start.4 = (f32[1,16,512]{2,1,0:T(8,128)S(1)}, f32[1,16,512]{2,1,0:T(8,128)}, u32[]{:S(2)}) copy-start(f32[1,16,512]{2,1,0:T(8,128)} %param.7) | copy-start | bytes 98308
  39.5 17.6 %copy-start.5 = (f32[1,16,512]{2,1,0:T(8,128)S(1)}, f32[1,16,512]{2,1,0:T(8,128)}, u32[]{:S(2)}) copy-start(f32[1,16,512]{2,1,0:T(8,128)} %param.9) | copy-start | bytes 98308
  39.5 1.6 %collective-permute-start.21 = (bf16[128,512]{1,0:T(8,128)(2,1)S(1)}, bf16[128,512]{1,0:T(8,128)(2,1)S(1)}, u32[]{:S(2)}, u32[]{:S(2)}) collective-permute-start(bf16[128,512]{1,0:T(8,128)(2,1)S(1)} %get-tuple-element.62), channel_id=1, source_target_pairs={{0,2},{2,0},{4,6},{6,4},{8,10},{10,8},{12,14},{14,12},{16,18},{18,... | collective-permute-start | bytes 393224 | tf_op jit(solution)/shard_map/ppermute | solution.py:26
  41.1 2.3 %collective-permute-start.23 = (bf16[128,512]{1,0:T(8,128)(2,1)S(1)}, bf16[128,512]{1,0:T(8,128)(2,1)S(1)}, u32[]{:S(2)}, u32[]{:S(2)}) collective-permute-start(bf16[128,512]{1,0:T(8,128)(2,1)S(1)} %add_convert_fusion), channel_id=1, source_target_pairs={{0,2},{2,0},{4,6},{6,4},{8,10},{10,8},{12,14},{14,12},{16,18},{18,... | collective-permute-start | bytes 393224 | tf_op jit(solution)/shard_map/ppermute | solution.py:26
  41.2 4.7 %collective-permute-start.25 = (bf16[64,512]{1,0:T(8,128)(2,1)S(1)}, bf16[64,512]{1,0:T(8,128)(2,1)S(1)}, u32[]{:S(2)}, u32[]{:S(2)}) collective-permute-start(bf16[64,512]{1,0:T(8,128)(2,1)S(1)} %slice.126), channel_id=1, source_target_pairs={{0,4},{2,6},{4,0},{6,2},{8,12},{10,14},{12,8},{14,10},{16,20},{18,... | collective-permute-start | bytes 196616 | tf_op jit(solution)/shard_map/ppermute | solution.py:26
  43.5 4.3 %collective-permute-start.24 = (bf16[64,512]{1,0:T(8,128)(2,1)S(1)}, bf16[64,512]{1,0:T(8,128)(2,1)S(1)}, u32[]{:S(2)}, u32[]{:S(2)}) collective-permute-start(bf16[64,512]{1,0:T(8,128)(2,1)S(1)} %slice.127), channel_id=1, source_target_pairs={{0,4},{2,6},{4,0},{6,2},{8,12},{10,14},{12,8},{14,10},{16,20},{18,... | collective-permute-start | bytes 196616 | tf_op jit(solution)/shard_map/ppermute | solution.py:26
  47.8 4.3 %collective-permute-start.26 = (bf16[32,1024]{1,0:T(8,128)(2,1)S(1)}, bf16[32,1024]{1,0:T(8,128)(2,1)S(1)}, u32[]{:S(2)}, u32[]{:S(2)}) collective-permute-start(bf16[32,1024]{1,0:T(8,128)(2,1)S(1)} %fusion.4), channel_id=1, source_target_pairs={{0,8},{2,10},{4,12},{6,14},{8,0},{10,2},{12,4},{14,6},{16,24},{18,... | collective-permute-start | bytes 196616 | tf_op jit(solution)/shard_map/ppermute | solution.py:26
  52.2 4.9 %collective-permute-start.27 = (bf16[16,1024]{1,0:T(8,128)(2,1)S(1)}, bf16[16,1024]{1,0:T(8,128)(2,1)S(1)}, u32[]{:S(2)}, u32[]{:S(2)}) collective-permute-start(bf16[16,1024]{1,0:T(8,128)(2,1)S(1)} %slice.128), channel_id=1, source_target_pairs={{0,16},{2,18},{4,20},{6,22},{8,24},{10,26},{12,28},{14,30},{16,0},... | collective-permute-start | bytes 98312 | tf_op jit(solution)/shard_map/ppermute | solution.py:26

commit v8 on v7

--- a/solution.py
+++ b/solution.py
@@ -158,8 +158,7 @@
     blocks_a = [near_a]
     for mask in reversed(mp_bits):
         blocks_a = blocks_a + [swap(b, "mp", mask) for b in blocks_a]
-    blocks_a[0] = jnp.concatenate([near_a, low], axis=1)
-    blocks_a = [after(b, steps[0]) for b in blocks_a]
+    all_a = after(jnp.concatenate([near_a, low] + blocks_a[1:], axis=1), steps[0])
 
     slot = after(flat_slot, steps[-1])
     owner = (slot // span) ^ me
@@ -197,9 +196,12 @@
         crossed = [swap(p, "mp", mask) for p in sent]
         got = [crossed[k ^ mask] for k in range(n_mp)]
 
-    for mask, event in zip(far[:-1], [one[0]] + [sent[0]] * (len(far) - 2)):
-        arrived = [after(swap(b, "dp", mask), event) for b in blocks_a]
-        blocks_a = [jnp.concatenate(pair, axis=0) for pair in zip(blocks_a, arrived)]
+    for mask in far[:-2]:
+        all_a = jnp.concatenate([all_a, after(swap(all_a, "dp", mask), steps[-1])], axis=0)
+    ends = [0] + [(3 + 2 * k) * segment for k in range(n_mp)]
+    blocks_a = [all_a[:, ends[k] : ends[k + 1]] for k in range(n_mp)]
+    arrived = [after(swap(b, "dp", far[-2]), sent[0]) for b in blocks_a]
+    blocks_a = [jnp.concatenate(pair, axis=0) for pair in zip(blocks_a, arrived)]
     arrived = [swap(b, "dp", far[-1]) for b in blocks_a]
 
     half = segments // 2

time: 58.1 us -> 58.2 us (level)
  other arithmetic: 4.03 us -> 3.41 us
  waiting for transfers between devices: 15 us -> 15.6 us
    concatenate x4 -> x2, other arithmetic: 0.68 us -> 0.02 us  [per_device(): jnp.concatenate(pair, axis=0)]
    ppermute x28 -> x27, waiting for transfers between devices: 15 us -> 15.6 us  [swap(): return lax.ppermute(x, axis, [(i, i ^ mask) for i in range(n)])]
    ppermute x28 -> x27, starting transfers between devices: 29.1 us -> 29.1 us  [swap(): return lax.ppermute(x, axis, [(i, i ^ mask) for i in range(n)])]
  transfers between devices with their start and end apart: 28 -> 27, of which waited for: 13 -> 13; matrix products, arithmetic and copies ran while one was open for 8% -> 7% of each run, Pallas kernels for 12% -> 12%
where the time goes in v8:
time: 58.2 us; the launch traced here: 57.9 us
  starting transfers between devices  29.1 us (50%)
  waiting for transfers between devices  15.6 us (27%)
  Pallas kernels  6.69 us (11%)
  other arithmetic  3.41 us (6%)
  local copies, waits for them, and re-layouts  2.18 us (4%)
  between operations  0.93 us (2%)
    ppermute x27, starting transfers between devices, swap(): return lax.ppermute(x, axis, [(i, i ^ mask) for i in range(n)])  29.1 us
    ppermute x27, waiting for transfers between devices, swap(): return lax.ppermute(x, axis, [(i, i ^ mask) for i in range(n)])  15.6 us
    pallas_call x6, Pallas kernels, call(): pl.pallas_call(kernel, out_shape=out_shape, in_specs=[pl.BlockSpec(memory...  6.69 us
    squeeze x3, local copies, waits for them, and re-layouts, tokens_of(): x[step]  1.81 us
  transfers between devices with their start and end apart: 27, of which 13 were waited for; matrix products, arithmetic and copies ran while one was open for 7% of the time, Pallas kernels for 12%

profile of v8, /device:TPU:0, one launch (start us, length us, event | category | flops | bytes accessed | tf_op | source)
XLA Modules:
  0.0 57.9 jit_solution(15088751121061118428)
XLA Ops:
  0.6 0.8 %bitcast_convert_fusion = bf16[16,512]{1,0:T(8,128)(2,1)S(1)} fusion(f32[1,16,512]{2,1,0:T(8,128)} %param.7), kind=kLoop, calls=%fused_computation.39 | loop fusion | flops 8192 | bytes 49152 | tf_op jit(solution)/shard_map/convert_element_type | solution.py:150
  1.4 4.0 %collective-permute-start = (bf16[16,512]{1,0:T(8,128)(2,1)S(1)}, bf16[16,512]{1,0:T(8,128)(2,1)S(1)}, u32[]{:S(2)}, u32[]{:S(2)}) collective-permute-start(bf16[16,512]{1,0:T(8,128)(2,1)S(1)} %bitcast_convert_fusion), channel_id=1, source_target_pairs={{0,16},{2,18},{4,20},{6,22},{8,24},{10,26},{12,28},{14,30},{16,0},... | collective-permute-start | bytes 49160 | tf_op jit(solution)/shard_map/ppermute | solution.py:26
  5.4 0.8 %convert_bitcast_fusion = bf16[16,512]{1,0:T(8,128)(2,1)S(1)} fusion(f32[1,16,512]{2,1,0:T(8,128)} %param.9), kind=kLoop, calls=%fused_computation.40 | loop fusion | flops 8192 | bytes 49152 | tf_op jit(solution)/shard_map/convert.5
  6.2 0.8 %fusion.5 = (bf16[16,512]{1,0:T(8,128)(2,1)S(1)}, bf16[16,512]{1,0:T(8,128)(2,1)S(1)}) fusion(f32[16,512]{1,0:T(8,128)} %bitcast.28), kind=kLoop, calls=%fused_computation.31 | loop fusion | flops 32768 | bytes 65536 | tf_op jit(solution)/shard_map/convert_element_type | solution.py:153
  7.0 1.6 %collective-permute-start.7 = (bf16[16,1024]{1,0:T(8,128)(2,1)S(1)}, bf16[16,1024]{1,0:T(8,128)(2,1)S(1)}, u32[]{:S(2)}, u32[]{:S(2)}) collective-permute-start(bf16[16,1024]{1,0:T(8,128)(2,1)S(1)} %pad_maximum_fusion.9), channel_id=1, source_target_pairs={{0,1},{1,0},{2,3},{3,2},{4,5},{5,4},{6,7},{7,6},{8,9},{9,8},{10,11... | collective-permute-start | bytes 98312 | tf_op jit(solution)/shard_map/ppermute | solution.py:26
  8.6 1.6 %collective-permute-start.1 = (bf16[32,512]{1,0:T(8,128)(2,1)S(1)}, bf16[32,512]{1,0:T(8,128)(2,1)S(1)}, u32[]{:S(2)}, u32[]{:S(2)}) collective-permute-start(bf16[32,512]{1,0:T(8,128)(2,1)S(1)} %pad_maximum_fusion.8), channel_id=1, source_target_pairs={{0,8},{2,10},{4,12},{6,14},{8,0},{10,2},{12,4},{14,6},{16,24},{18,... | collective-permute-start | bytes 98312 | tf_op jit(solution)/shard_map/ppermute | solution.py:26
  10.2 0.8 %collective-permute-done.7 = bf16[16,1024]{1,0:T(8,128)(2,1)S(1)} collective-permute-done((bf16[16,1024]{1,0:T(8,128)(2,1)S(1)}, bf16[16,1024]{1,0:T(8,128)(2,1)S(1)}, u32[]{:S(2)}, u32[]{:S(2)}) %collective-permute-start.7) | collective-permute-done | bytes 32800 | tf_op jit(solution)/shard_map/ppermute | solution.py:26
  11.0 0.8 %collective-permute-start.8 = (bf16[16,2560]{1,0:T(8,128)(2,1)S(1)}, bf16[16,2560]{1,0:T(8,128)(2,1)S(1)}, u32[]{:S(2)}, u32[]{:S(2)}) collective-permute-start(bf16[16,2560]{1,0:T(8,128)(2,1)S(1)} %pad_maximum_fusion.6), channel_id=1, source_target_pairs={{0,16},{2,18},{4,20},{6,22},{8,24},{10,26},{12,28},{14,30},{16,0},... | collective-permute-start | bytes 245768 | tf_op jit(solution)/shard_map/ppermute | solution.py:26
  11.8 0.7 %collective-permute-done.1 = bf16[32,512]{1,0:T(8,128)(2,1)S(1)} collective-permute-done((bf16[32,512]{1,0:T(8,128)(2,1)S(1)}, bf16[32,512]{1,0:T(8,128)(2,1)S(1)}, u32[]{:S(2)}, u32[]{:S(2)}) %collective-permute-start.1) | collective-permute-done | bytes 32800 | tf_op jit(solution)/shard_map/ppermute | solution.py:26
  12.6 1.6 %collective-permute-start.2 = (bf16[64,512]{1,0:T(8,128)(2,1)S(1)}, bf16[64,512]{1,0:T(8,128)(2,1)S(1)}, u32[]{:S(2)}, u32[]{:S(2)}) collective-permute-start(bf16[64,512]{1,0:T(8,128)(2,1)S(1)} %pad_maximum_fusion.7), channel_id=1, source_target_pairs={{0,4},{2,6},{4,0},{6,2},{8,12},{10,14},{12,8},{14,10},{16,20},{18,... | collective-permute-start | bytes 196616 | tf_op jit(solution)/shard_map/ppermute | solution.py:26
  14.1 1.7 %slice_bitcast_fusion.2 = (bf16[64,8192]{1,0:T(8,128)(2,1)S(1)}, bf16[64,8192]{1,0:T(8,128)(2,1)S(1)}) fusion(bf16[2,64,8192]{2,1,0:T(8,128)(2,1)} %param.13, bf16[2,64,8192]{2,1,0:T(8,128)(2,1)} %param.12), kind=kLoop, calls=%fused_computation.2 | loop fusion | bytes 4194304 | tf_op jit(solution)/shard_map/squeeze | solution.py:123
  15.8 1.1 %collective-permute-done.2 = bf16[64,512]{1,0:T(8,128)(2,1)S(1)} collective-permute-done((bf16[64,512]{1,0:T(8,128)(2,1)S(1)}, bf16[64,512]{1,0:T(8,128)(2,1)S(1)}, u32[]{:S(2)}, u32[]{:S(2)}) %collective-permute-start.2) | collective-permute-done | bytes 65568 | tf_op jit(solution)/shard_map/ppermute | solution.py:26
  16.9 0.9 %collective-permute-start.4 = (bf16[128,512]{1,0:T(8,128)(2,1)S(1)}, bf16[128,512]{1,0:T(8,128)(2,1)S(1)}, u32[]{:S(2)}, u32[]{:S(2)}) collective-permute-start(bf16[128,512]{1,0:T(8,128)(2,1)S(1)} %pad_maximum_fusion.4.w0_ref), channel_id=1, source_target_pairs={{0,1},{1,0},{2,3},{3,2},{4,5},{5,4},{6,7},{7,6},{8,9},{9,8},{10,11... | collective-permute-start | bytes 393224 | tf_op jit(solution)/shard_map/ppermute | solution.py:26
  18.0 0.1 eq.31
  18.1 1.6 %collective-permute-start.12 = (bf16[32,1024]{1,0:T(8,128)(2,1)S(1)}, bf16[32,1024]{1,0:T(8,128)(2,1)S(1)}, u32[]{:S(2)}, u32[]{:S(2)}) collective-permute-start(bf16[32,1024]{1,0:T(8,128)(2,1)S(1)} %slice.89), channel_id=1, source_target_pairs={{0,8},{2,10},{4,12},{6,14},{8,0},{10,2},{12,4},{14,6},{16,24},{18,... | collective-permute-start | bytes 196616 | tf_op jit(solution)/shard_map/ppermute | solution.py:26
  19.7 0.4 collective-permute-start.9
  20.1 0.1 fusion.1
  20.2 1.3 %shard_map.94 = (bf16[16,8192]{1,0:T(8,128)(2,1)S(1)}, f32[16,8192]{1,0:T(8,128)S(1)}, bf16[16,8192]{1,0:T(8,128)(2,1)S(1)}) custom-call(bf16[256,256]{1,0:T(8,128)(2,1)S(1)} %get-tuple-element.72.place_ref, bf16[128,512]{1,0:T(8,128)(2,1)S(1)} %pad_maximum_fusion.4.w0_ref, bf16[128,512]{1,0:T(8,128)(2,1)S(1)} %collective-permute-done.3.w1_ref, ...), custom_call_target="tpu_custom_call" | custom-call | flops 1 | bytes 1 | tf_op jit(solution)/shard_map/pallas_call | solution.py:127
  21.5 1.3 %collective-permute-start.11 = (bf16[16,8192]{1,0:T(8,128)(2,1)S(1)}, bf16[16,8192]{1,0:T(8,128)(2,1)S(1)}, u32[]{:S(2)}, u32[]{:S(2)}) collective-permute-start(bf16[16,8192]{1,0:T(8,128)(2,1)S(1)} %get-tuple-element.42), channel_id=1, source_target_pairs={{0,1},{1,0},{2,3},{3,2},{4,5},{5,4},{6,7},{7,6},{8,9},{9,8},{10,11... | collective-permute-start | bytes 786440 | tf_op jit(solution)/shard_map/ppermute | solution.py:26
  22.8 1.9 %collective-permute-done.9 = bf16[32,1536]{1,0:T(8,128)(2,1)S(1)} collective-permute-done((bf16[32,1536]{1,0:T(8,128)(2,1)S(1)}, bf16[32,1536]{1,0:T(8,128)(2,1)S(1)}, u32[]{:S(2)}, u32[]{:S(2)}) %collective-permute-start.9) | collective-permute-done | bytes 98336 | tf_op jit(solution)/shard_map/ppermute | solution.py:26
  24.7 1.6 %collective-permute-start.13 = (bf16[64,1024]{1,0:T(8,128)(2,1)S(1)}, bf16[64,1024]{1,0:T(8,128)(2,1)S(1)}, u32[]{:S(2)}, u32[]{:S(2)}) collective-permute-start(bf16[64,1024]{1,0:T(8,128)(2,1)S(1)} %pad_maximum_fusion.5), channel_id=1, source_target_pairs={{0,4},{2,6},{4,0},{6,2},{8,12},{10,14},{12,8},{14,10},{16,20},{18,... | collective-permute-start | bytes 393224 | tf_op jit(solution)/shard_map/ppermute | solution.py:26
  26.3 0.6 %collective-permute-start.10 = (bf16[64,1536]{1,0:T(8,128)(2,1)S(1)}, bf16[64,1536]{1,0:T(8,128)(2,1)S(1)}, u32[]{:S(2)}, u32[]{:S(2)}) collective-permute-start(bf16[64,1536]{1,0:T(8,128)(2,1)S(1)} %pad_maximum_fusion.2), channel_id=1, source_target_pairs={{0,4},{2,6},{4,0},{6,2},{8,12},{10,14},{12,8},{14,10},{16,20},{18,... | collective-permute-start | bytes 589832 | tf_op jit(solution)/shard_map/ppermute | solution.py:26
  26.9 0.7 %collective-permute-done.5.w1_ref = bf16[128,512]{1,0:T(8,128)(2,1)S(1)} collective-permute-done((bf16[128,512]{1,0:T(8,128)(2,1)S(1)}, bf16[128,512]{1,0:T(8,128)(2,1)S(1)}, u32[]{:S(2)}, u32[]{:S(2)}) %collective-permute-start.5) | collective-permute-done | bytes 131104 | tf_op jit(solution)/shard_map/ppermute | solution.py:26
  27.6 1.3 %shard_map.95 = (bf16[16,8192]{1,0:T(8,128)(2,1)S(1)}, f32[16,8192]{1,0:T(8,128)S(1)}, bf16[16,8192]{1,0:T(8,128)(2,1)S(1)}) custom-call(bf16[256,256]{1,0:T(8,128)(2,1)S(1)} %get-tuple-element.72.place_ref, bf16[128,512]{1,0:T(8,128)(2,1)S(1)} %collective-permute-done.4.w0_ref, bf16[128,512]{1,0:T(8,128)(2,1)S(1)} %collective-permute-done.5.w1_ref, ...), custom_call_target="tpu_custom_call" | custom-call | flops 1 | bytes 1 | tf_op jit(solution)/shard_map/pallas_call | solution.py:127
  28.9 1.3 %collective-permute-start.6 = (bf16[16,8192]{1,0:T(8,128)(2,1)S(1)}, bf16[16,8192]{1,0:T(8,128)(2,1)S(1)}, u32[]{:S(2)}, u32[]{:S(2)}) collective-permute-start(bf16[16,8192]{1,0:T(8,128)(2,1)S(1)} %get-tuple-element.37), channel_id=1, source_target_pairs={{0,1},{1,0},{2,3},{3,2},{4,5},{5,4},{6,7},{7,6},{8,9},{9,8},{10,11... | collective-permute-start | bytes 786440 | tf_op jit(solution)/shard_map/ppermute | solution.py:26
  30.3 0.5 collective-permute-start.14
  31.0 0.7 %collective-permute-done.15.refs_3_ = bf16[128,512]{1,0:T(8,128)(2,1)S(1)} collective-permute-done((bf16[128,512]{1,0:T(8,128)(2,1)S(1)}, bf16[128,512]{1,0:T(8,128)(2,1)S(1)}, u32[]{:S(2)}, u32[]{:S(2)}) %collective-permute-start.15) | collective-permute-done | bytes 131104 | tf_op jit(solution)/shard_map/ppermute | solution.py:26
  31.7 0.2 collective-permute-done.14.refs_2_
  31.8 0.5 shard_map.96
  32.4 1.3 %shard_map.97 = (bf16[128,512]{1,0:T(8,128)(2,1)S(1)}, bf16[128,512]{1,0:T(8,128)(2,1)S(1)}) custom-call(bf16[256,256]{1,0:T(8,128)(2,1)S(1)} %get-tuple-element.73.back_ref, f32[16,8192]{1,0:T(8,128)S(1)} %get-tuple-element.44.part_ref, bf16[16,8192]{1,0:T(8,128)(2,1)S(1)} %collective-permute-done.11.got_ref, ...), custom_call_target="tpu_custom_call" | custom-call | flops 1 | bytes 1 | tf_op jit(solution)/shard_map/pallas_call | solution.py:127
  33.7 0.3 collective-permute-done.10
  34.0 0.1 collective-permute-start.18
  34.1 0.5 collective-permute-start.17
  34.6 0.1 collective-permute-start.16
  34.7 1.2 %collective-permute-start.21 = (bf16[128,512]{1,0:T(8,128)(2,1)S(1)}, bf16[128,512]{1,0:T(8,128)(2,1)S(1)}, u32[]{:S(2)}, u32[]{:S(2)}) collective-permute-start(bf16[128,512]{1,0:T(8,128)(2,1)S(1)} %get-tuple-element.61), channel_id=1, source_target_pairs={{0,1},{1,0},{2,3},{3,2},{4,5},{5,4},{6,7},{7,6},{8,9},{9,8},{10,11... | collective-permute-start | bytes 393224 | tf_op jit(solution)/shard_map/ppermute | solution.py:26
  35.9 0.8 %collective-permute-start.19 = (bf16[128,512]{1,0:T(8,128)(2,1)S(1)}, bf16[128,512]{1,0:T(8,128)(2,1)S(1)}, u32[]{:S(2)}, u32[]{:S(2)}) collective-permute-start(bf16[128,512]{1,0:T(8,128)(2,1)S(1)} %get-tuple-element.52), channel_id=1, source_target_pairs={{0,1},{1,0},{2,3},{3,2},{4,5},{5,4},{6,7},{7,6},{8,9},{9,8},{10,11... | collective-permute-start | bytes 393224 | tf_op jit(solution)/shard_map/ppermute | solution.py:26
  36.7 0.6 shard_map.98
  37.3 1.8 %shard_map.99 = (bf16[128,512]{1,0:T(8,128)(2,1)S(1)}, bf16[128,512]{1,0:T(8,128)(2,1)S(1)}, bf16[128,512]{1,0:T(8,128)(2,1)S(1)}, bf16[128,512]{1,0:T(8,128)(2,1)S(1)}, bf16[16,8192]{1,0:T(8,128)(2,1)}) custom-call(bf16[256,256]{1,0:T(8,128)(2,1)S(1)} %get-tuple-element.73.back_ref, f32[16,8192]{1,0:T(8,128)S(1)} %get-tuple-element.36.part_ref, ...), custom_call_target="tpu_custom_call" | custom-call | flops 1 | bytes 1 | tf_op jit(solution)/shard_map/pallas_call | solution.py:127
  39.2 1.8 %collective-permute-done.21 = bf16[128,512]{1,0:T(8,128)(2,1)S(1)} collective-permute-done((bf16[128,512]{1,0:T(8,128)(2,1)S(1)}, bf16[128,512]{1,0:T(8,128)(2,1)S(1)}, u32[]{:S(2)}, u32[]{:S(2)}) %collective-permute-start.21) | collective-permute-done | bytes 131104 | tf_op jit(solution)/shard_map/ppermute | solution.py:26
  41.2 2.4 %collective-permute-start.24 = (bf16[64,512]{1,0:T(8,128)(2,1)S(1)}, bf16[64,512]{1,0:T(8,128)(2,1)S(1)}, u32[]{:S(2)}, u32[]{:S(2)}) collective-permute-start(bf16[64,512]{1,0:T(8,128)(2,1)S(1)} %slice.136), channel_id=1, source_target_pairs={{0,4},{2,6},{4,0},{6,2},{8,12},{10,14},{12,8},{14,10},{16,20},{18,... | collective-permute-start | bytes 196616 | tf_op jit(solution)/shard_map/ppermute | solution.py:26
  43.6 1.9 %collective-permute-start.23 = (bf16[64,512]{1,0:T(8,128)(2,1)S(1)}, bf16[64,512]{1,0:T(8,128)(2,1)S(1)}, u32[]{:S(2)}, u32[]{:S(2)}) collective-permute-start(bf16[64,512]{1,0:T(8,128)(2,1)S(1)} %slice.137), channel_id=1, source_target_pairs={{0,4},{2,6},{4,0},{6,2},{8,12},{10,14},{12,8},{14,10},{16,20},{18,... | collective-permute-start | bytes 196616 | tf_op jit(solution)/shard_map/ppermute | solution.py:26
  45.5 0.8 %collective-permute-done.24 = bf16[64,512]{1,0:T(8,128)(2,1)S(1)} collective-permute-done((bf16[64,512]{1,0:T(8,128)(2,1)S(1)}, bf16[64,512]{1,0:T(8,128)(2,1)S(1)}, u32[]{:S(2)}, u32[]{:S(2)}) %collective-permute-start.24) | collective-permute-done | bytes 65568 | tf_op jit(solution)/shard_map/ppermute | solution.py:26
  46.3 1.6 %collective-permute-done.23 = bf16[64,512]{1,0:T(8,128)(2,1)S(1)} collective-permute-done((bf16[64,512]{1,0:T(8,128)(2,1)S(1)}, bf16[64,512]{1,0:T(8,128)(2,1)S(1)}, u32[]{:S(2)}, u32[]{:S(2)}) %collective-permute-start.23) | collective-permute-done | bytes 65568 | tf_op jit(solution)/shard_map/ppermute | solution.py:26
  48.0 1.9 %collective-permute-start.25 = (bf16[32,1024]{1,0:T(8,128)(2,1)S(1)}, bf16[32,1024]{1,0:T(8,128)(2,1)S(1)}, u32[]{:S(2)}, u32[]{:S(2)}) collective-permute-start(bf16[32,1024]{1,0:T(8,128)(2,1)S(1)} %fusion.4), channel_id=1, source_target_pairs={{0,8},{2,10},{4,12},{6,14},{8,0},{10,2},{12,4},{14,6},{16,24},{18,... | collective-permute-start | bytes 196616 | tf_op jit(solution)/shard_map/ppermute | solution.py:26
  49.8 2.5 %collective-permute-done.25 = bf16[32,1024]{1,0:T(8,128)(2,1)S(1)} collective-permute-done((bf16[32,1024]{1,0:T(8,128)(2,1)S(1)}, bf16[32,1024]{1,0:T(8,128)(2,1)S(1)}, u32[]{:S(2)}, u32[]{:S(2)}) %collective-permute-start.25) | collective-permute-done | bytes 65568 | tf_op jit(solution)/shard_map/ppermute | solution.py:26
  52.3 2.5 %collective-permute-start.26 = (bf16[16,1024]{1,0:T(8,128)(2,1)S(1)}, bf16[16,1024]{1,0:T(8,128)(2,1)S(1)}, u32[]{:S(2)}, u32[]{:S(2)}) collective-permute-start(bf16[16,1024]{1,0:T(8,128)(2,1)S(1)} %slice.138), channel_id=1, source_target_pairs={{0,16},{2,18},{4,20},{6,22},{8,24},{10,26},{12,28},{14,30},{16,0},... | collective-permute-start | bytes 98312 | tf_op jit(solution)/shard_map/ppermute | solution.py:26
  54.8 2.4 %collective-permute-done.26 = bf16[16,1024]{1,0:T(8,128)(2,1)S(1)} collective-permute-done((bf16[16,1024]{1,0:T(8,128)(2,1)S(1)}, bf16[16,1024]{1,0:T(8,128)(2,1)S(1)}, u32[]{:S(2)}, u32[]{:S(2)}) %collective-permute-start.26) | collective-permute-done | bytes 32800 | tf_op jit(solution)/shard_map/ppermute | solution.py:26
  57.2 0.6 %fusion.9 = (f32[1,16,512]{2,1,0:T(8,128)}, f32[1,16,512]{2,1,0:T(8,128)}) fusion(f32[16,1024]{1,0:T(8,128)S(1)} %slice_add_fusion.2, f32[1,16,512]{2,1,0:T(8,128)S(1)} %copy-done.4, f32[1,16,512]{2,1,0:T(8,128)S(1)} %copy-done.3), kind=kLoop, calls=%fused_computation.41 | loop fusion | flops 73728 | bytes 196608 | tf_op jit(solution)/shard_map/broadcast_in_dim | solution.py:253
  (62 shorter events, 1.0 us)
Async XLA Ops:
  1.4 7.2 %collective-permute-start = (bf16[16,512]{1,0:T(8,128)(2,1)S(1)}, bf16[16,512]{1,0:T(8,128)(2,1)S(1)}, u32[]{:S(2)}, u32[]{:S(2)}) collective-permute-start(bf16[16,512]{1,0:T(8,128)(2,1)S(1)} %bitcast_convert_fusion), channel_id=1, source_target_pairs={{0,16},{2,18},{4,20},{6,22},{8,24},{10,26},{12,28},{14,30},{16,0},... | collective-permute-start | bytes 49160 | tf_op jit(solution)/shard_map/ppermute | solution.py:26
  7.0 4.0 %collective-permute-start.7 = (bf16[16,1024]{1,0:T(8,128)(2,1)S(1)}, bf16[16,1024]{1,0:T(8,128)(2,1)S(1)}, u32[]{:S(2)}, u32[]{:S(2)}) collective-permute-start(bf16[16,1024]{1,0:T(8,128)(2,1)S(1)} %pad_maximum_fusion.9), channel_id=1, source_target_pairs={{0,1},{1,0},{2,3},{3,2},{4,5},{5,4},{6,7},{7,6},{8,9},{9,8},{10,11... | collective-permute-start | bytes 98312 | tf_op jit(solution)/shard_map/ppermute | solution.py:26
  8.6 3.9 %collective-permute-start.1 = (bf16[32,512]{1,0:T(8,128)(2,1)S(1)}, bf16[32,512]{1,0:T(8,128)(2,1)S(1)}, u32[]{:S(2)}, u32[]{:S(2)}) collective-permute-start(bf16[32,512]{1,0:T(8,128)(2,1)S(1)} %pad_maximum_fusion.8), channel_id=1, source_target_pairs={{0,8},{2,10},{4,12},{6,14},{8,0},{10,2},{12,4},{14,6},{16,24},{18,... | collective-permute-start | bytes 98312 | tf_op jit(solution)/shard_map/ppermute | solution.py:26
  11.0 6.7 %collective-permute-start.8 = (bf16[16,2560]{1,0:T(8,128)(2,1)S(1)}, bf16[16,2560]{1,0:T(8,128)(2,1)S(1)}, u32[]{:S(2)}, u32[]{:S(2)}) collective-permute-start(bf16[16,2560]{1,0:T(8,128)(2,1)S(1)} %pad_maximum_fusion.6), channel_id=1, source_target_pairs={{0,16},{2,18},{4,20},{6,22},{8,24},{10,26},{12,28},{14,30},{16,0},... | collective-permute-start | bytes 245768 | tf_op jit(solution)/shard_map/ppermute | solution.py:26
  12.6 5.3 %copy-start.5 = (s32[256]{0:T(256)S(1)}, s32[256]{0:T(256)}, u32[]{:S(2)}) copy-start(s32[256]{0:T(256)} %param.10) | copy-start | bytes 3076
  12.6 4.3 %collective-permute-start.2 = (bf16[64,512]{1,0:T(8,128)(2,1)S(1)}, bf16[64,512]{1,0:T(8,128)(2,1)S(1)}, u32[]{:S(2)}, u32[]{:S(2)}) collective-permute-start(bf16[64,512]{1,0:T(8,128)(2,1)S(1)} %pad_maximum_fusion.7), channel_id=1, source_target_pairs={{0,4},{2,6},{4,0},{6,2},{8,12},{10,14},{12,8},{14,10},{16,20},{18,... | collective-permute-start | bytes 196616 | tf_op jit(solution)/shard_map/ppermute | solution.py:26
  16.9 9.4 %collective-permute-start.4 = (bf16[128,512]{1,0:T(8,128)(2,1)S(1)}, bf16[128,512]{1,0:T(8,128)(2,1)S(1)}, u32[]{:S(2)}, u32[]{:S(2)}) collective-permute-start(bf16[128,512]{1,0:T(8,128)(2,1)S(1)} %pad_maximum_fusion.4.w0_ref), channel_id=1, source_target_pairs={{0,1},{1,0},{2,3},{3,2},{4,5},{5,4},{6,7},{7,6},{8,9},{9,8},{10,11... | collective-permute-start | bytes 393224 | tf_op jit(solution)/shard_map/ppermute | solution.py:26
  17.8 2.5 %collective-permute-start.3 = (bf16[128,512]{1,0:T(8,128)(2,1)S(1)}, bf16[128,512]{1,0:T(8,128)(2,1)S(1)}, u32[]{:S(2)}, u32[]{:S(2)}) collective-permute-start(bf16[128,512]{1,0:T(8,128)(2,1)S(1)} %pad_maximum_fusion.4.w0_ref), channel_id=1, source_target_pairs={{0,2},{2,0},{4,6},{6,4},{8,10},{10,8},{12,14},{14,12},{16,18},{18,... | collective-permute-start | bytes 393224 | tf_op jit(solution)/shard_map/ppermute | solution.py:26
  18.1 4.7 %collective-permute-start.12 = (bf16[32,1024]{1,0:T(8,128)(2,1)S(1)}, bf16[32,1024]{1,0:T(8,128)(2,1)S(1)}, u32[]{:S(2)}, u32[]{:S(2)}) collective-permute-start(bf16[32,1024]{1,0:T(8,128)(2,1)S(1)} %slice.89), channel_id=1, source_target_pairs={{0,8},{2,10},{4,12},{6,14},{8,0},{10,2},{12,4},{14,6},{16,24},{18,... | collective-permute-start | bytes 196616 | tf_op jit(solution)/shard_map/ppermute | solution.py:26
  19.7 5.0 %collective-permute-start.9 = (bf16[32,1536]{1,0:T(8,128)(2,1)S(1)}, bf16[32,1536]{1,0:T(8,128)(2,1)S(1)}, u32[]{:S(2)}, u32[]{:S(2)}) collective-permute-start(bf16[32,1536]{1,0:T(8,128)(2,1)S(1)} %slice.88), channel_id=1, source_target_pairs={{0,8},{2,10},{4,12},{6,14},{8,0},{10,2},{12,4},{14,6},{16,24},{18,... | collective-permute-start | bytes 294920 | tf_op jit(solution)/shard_map/ppermute | solution.py:26
  21.5 9.3 %copy-start.1 = (bf16[2,64,8192]{2,1,0:T(8,128)(2,1)S(1)}, bf16[2,64,8192]{2,1,0:T(8,128)(2,1)}, u32[]{:S(2)}) copy-start(bf16[2,64,8192]{2,1,0:T(8,128)(2,1)} %param.12) | copy-start | bytes 6291460
  21.5 10.9 %collective-permute-start.11 = (bf16[16,8192]{1,0:T(8,128)(2,1)S(1)}, bf16[16,8192]{1,0:T(8,128)(2,1)S(1)}, u32[]{:S(2)}, u32[]{:S(2)}) collective-permute-start(bf16[16,8192]{1,0:T(8,128)(2,1)S(1)} %get-tuple-element.42), channel_id=1, source_target_pairs={{0,1},{1,0},{2,3},{3,2},{4,5},{5,4},{6,7},{7,6},{8,9},{9,8},{10,11... | collective-permute-start | bytes 786440 | tf_op jit(solution)/shard_map/ppermute | solution.py:26
  24.7 5.5 %collective-permute-start.13 = (bf16[64,1024]{1,0:T(8,128)(2,1)S(1)}, bf16[64,1024]{1,0:T(8,128)(2,1)S(1)}, u32[]{:S(2)}, u32[]{:S(2)}) collective-permute-start(bf16[64,1024]{1,0:T(8,128)(2,1)S(1)} %pad_maximum_fusion.5), channel_id=1, source_target_pairs={{0,4},{2,6},{4,0},{6,2},{8,12},{10,14},{12,8},{14,10},{16,20},{18,... | collective-permute-start | bytes 393224 | tf_op jit(solution)/shard_map/ppermute | solution.py:26
  26.3 1.3 %collective-permute-start.5 = (bf16[128,512]{1,0:T(8,128)(2,1)S(1)}, bf16[128,512]{1,0:T(8,128)(2,1)S(1)}, u32[]{:S(2)}, u32[]{:S(2)}) collective-permute-start(bf16[128,512]{1,0:T(8,128)(2,1)S(1)} %collective-permute-done.4.w0_ref), channel_id=1, source_target_pairs={{0,2},{2,0},{4,6},{6,4},{8,10},{10,8},{12,14},{14,12},{16,18},{18,... | collective-permute-start | bytes 393224 | tf_op jit(solution)/shard_map/ppermute | solution.py:26
  26.3 7.7 %collective-permute-start.10 = (bf16[64,1536]{1,0:T(8,128)(2,1)S(1)}, bf16[64,1536]{1,0:T(8,128)(2,1)S(1)}, u32[]{:S(2)}, u32[]{:S(2)}) collective-permute-start(bf16[64,1536]{1,0:T(8,128)(2,1)S(1)} %pad_maximum_fusion.2), channel_id=1, source_target_pairs={{0,4},{2,6},{4,0},{6,2},{8,12},{10,14},{12,8},{14,10},{16,20},{18,... | collective-permute-start | bytes 589832 | tf_op jit(solution)/shard_map/ppermute | solution.py:26
  28.9 2.0 %copy-start.2 = (bf16[2,64,8192]{2,1,0:T(8,128)(2,1)S(1)}, bf16[2,64,8192]{2,1,0:T(8,128)(2,1)}, u32[]{:S(2)}) copy-start(bf16[2,64,8192]{2,1,0:T(8,128)(2,1)} %param.13) | copy-start | bytes 6291460
  28.9 8.4 %collective-permute-start.6 = (bf16[16,8192]{1,0:T(8,128)(2,1)S(1)}, bf16[16,8192]{1,0:T(8,128)(2,1)S(1)}, u32[]{:S(2)}, u32[]{:S(2)}) collective-permute-start(bf16[16,8192]{1,0:T(8,128)(2,1)S(1)} %get-tuple-element.37), channel_id=1, source_target_pairs={{0,1},{1,0},{2,3},{3,2},{4,5},{5,4},{6,7},{7,6},{8,9},{9,8},{10,11... | collective-permute-start | bytes 786440 | tf_op jit(solution)/shard_map/ppermute | solution.py:26
  30.2 1.4 %collective-permute-start.15 = (bf16[128,512]{1,0:T(8,128)(2,1)S(1)}, bf16[128,512]{1,0:T(8,128)(2,1)S(1)}, u32[]{:S(2)}, u32[]{:S(2)}) collective-permute-start(bf16[128,512]{1,0:T(8,128)(2,1)S(1)} %get-tuple-element.66.refs_1_), channel_id=1, source_target_pairs={{0,2},{2,0},{4,6},{6,4},{8,10},{10,8},{12,14},{14,12},{16,18},{18,... | collective-permute-start | bytes 393224 | tf_op jit(solution)/shard_map/ppermute | solution.py:26
  30.3 1.5 %collective-permute-start.14 = (bf16[128,512]{1,0:T(8,128)(2,1)S(1)}, bf16[128,512]{1,0:T(8,128)(2,1)S(1)}, u32[]{:S(2)}, u32[]{:S(2)}) collective-permute-start(bf16[128,512]{1,0:T(8,128)(2,1)S(1)} %get-tuple-element.67.refs_0_), channel_id=1, source_target_pairs={{0,2},{2,0},{4,6},{6,4},{8,10},{10,8},{12,14},{14,12},{16,18},{18,... | collective-permute-start | bytes 393224 | tf_op jit(solution)/shard_map/ppermute | solution.py:26
  33.7 3.7 %copy-start = (bf16[1,2,8,8192]{3,2,1,0:T(8,128)(2,1)S(1)}, bf16[1,2,8,8192]{3,2,1,0:T(8,128)(2,1)}, u32[]{:S(2)}) copy-start(bf16[1,2,8,8192]{3,2,1,0:T(8,128)(2,1)} %param.11) | copy-start | bytes 786436
  34.0 1.9 %collective-permute-start.18 = (bf16[128,512]{1,0:T(8,128)(2,1)S(1)}, bf16[128,512]{1,0:T(8,128)(2,1)S(1)}, u32[]{:S(2)}, u32[]{:S(2)}) collective-permute-start(bf16[128,512]{1,0:T(8,128)(2,1)S(1)} %get-tuple-element.63.refs_2_), channel_id=1, source_target_pairs={{0,2},{2,0},{4,6},{6,4},{8,10},{10,8},{12,14},{14,12},{16,18},{18,... | collective-permute-start | bytes 393224 | tf_op jit(solution)/shard_map/ppermute | solution.py:26
  34.1 2.6 %collective-permute-start.17 = (bf16[128,512]{1,0:T(8,128)(2,1)S(1)}, bf16[128,512]{1,0:T(8,128)(2,1)S(1)}, u32[]{:S(2)}, u32[]{:S(2)}) collective-permute-start(bf16[128,512]{1,0:T(8,128)(2,1)S(1)} %get-tuple-element.64.refs_1_), channel_id=1, source_target_pairs={{0,2},{2,0},{4,6},{6,4},{8,10},{10,8},{12,14},{14,12},{16,18},{18,... | collective-permute-start | bytes 393224 | tf_op jit(solution)/shard_map/ppermute | solution.py:26
  34.6 2.1 %collective-permute-start.16 = (bf16[128,512]{1,0:T(8,128)(2,1)S(1)}, bf16[128,512]{1,0:T(8,128)(2,1)S(1)}, u32[]{:S(2)}, u32[]{:S(2)}) collective-permute-start(bf16[128,512]{1,0:T(8,128)(2,1)S(1)} %get-tuple-element.65.refs_0_), channel_id=1, source_target_pairs={{0,2},{2,0},{4,6},{6,4},{8,10},{10,8},{12,14},{14,12},{16,18},{18,... | collective-permute-start | bytes 393224 | tf_op jit(solution)/shard_map/ppermute | solution.py:26
  34.7 6.3 %collective-permute-start.21 = (bf16[128,512]{1,0:T(8,128)(2,1)S(1)}, bf16[128,512]{1,0:T(8,128)(2,1)S(1)}, u32[]{:S(2)}, u32[]{:S(2)}) collective-permute-start(bf16[128,512]{1,0:T(8,128)(2,1)S(1)} %get-tuple-element.61), channel_id=1, source_target_pairs={{0,1},{1,0},{2,3},{3,2},{4,5},{5,4},{6,7},{7,6},{8,9},{9,8},{10,11... | collective-permute-start | bytes 393224 | tf_op jit(solution)/shard_map/ppermute | solution.py:26
  35.9 7.6 %collective-permute-start.19 = (bf16[128,512]{1,0:T(8,128)(2,1)S(1)}, bf16[128,512]{1,0:T(8,128)(2,1)S(1)}, u32[]{:S(2)}, u32[]{:S(2)}) collective-permute-start(bf16[128,512]{1,0:T(8,128)(2,1)S(1)} %get-tuple-element.52), channel_id=1, source_target_pairs={{0,1},{1,0},{2,3},{3,2},{4,5},{5,4},{6,7},{7,6},{8,9},{9,8},{10,11... | collective-permute-start | bytes 393224 | tf_op jit(solution)/shard_map/ppermute | solution.py:26
  39.2 18.1 %copy-start.3 = (f32[1,16,512]{2,1,0:T(8,128)S(1)}, f32[1,16,512]{2,1,0:T(8,128)}, u32[]{:S(2)}) copy-start(f32[1,16,512]{2,1,0:T(8,128)} %param.7) | copy-start | bytes 98308
  39.2 18.1 %copy-start.4 = (f32[1,16,512]{2,1,0:T(8,128)S(1)}, f32[1,16,512]{2,1,0:T(8,128)}, u32[]{:S(2)}) copy-start(f32[1,16,512]{2,1,0:T(8,128)} %param.9) | copy-start | bytes 98308
  39.2 1.9 %collective-permute-start.20 = (bf16[128,512]{1,0:T(8,128)(2,1)S(1)}, bf16[128,512]{1,0:T(8,128)(2,1)S(1)}, u32[]{:S(2)}, u32[]{:S(2)}) collective-permute-start(bf16[128,512]{1,0:T(8,128)(2,1)S(1)} %get-tuple-element.58), channel_id=1, source_target_pairs={{0,2},{2,0},{4,6},{6,4},{8,10},{10,8},{12,14},{14,12},{16,18},{18,... | collective-permute-start | bytes 393224 | tf_op jit(solution)/shard_map/ppermute | solution.py:26
  41.0 2.5 %collective-permute-start.22 = (bf16[128,512]{1,0:T(8,128)(2,1)S(1)}, bf16[128,512]{1,0:T(8,128)(2,1)S(1)}, u32[]{:S(2)}, u32[]{:S(2)}) collective-permute-start(bf16[128,512]{1,0:T(8,128)(2,1)S(1)} %add_convert_fusion), channel_id=1, source_target_pairs={{0,2},{2,0},{4,6},{6,4},{8,10},{10,8},{12,14},{14,12},{16,18},{18,... | collective-permute-start | bytes 393224 | tf_op jit(solution)/shard_map/ppermute | solution.py:26
  41.2 5.1 %collective-permute-start.24 = (bf16[64,512]{1,0:T(8,128)(2,1)S(1)}, bf16[64,512]{1,0:T(8,128)(2,1)S(1)}, u32[]{:S(2)}, u32[]{:S(2)}) collective-permute-start(bf16[64,512]{1,0:T(8,128)(2,1)S(1)} %slice.136), channel_id=1, source_target_pairs={{0,4},{2,6},{4,0},{6,2},{8,12},{10,14},{12,8},{14,10},{16,20},{18,... | collective-permute-start | bytes 196616 | tf_op jit(solution)/shard_map/ppermute | solution.py:26
  43.6 4.3 %collective-permute-start.23 = (bf16[64,512]{1,0:T(8,128)(2,1)S(1)}, bf16[64,512]{1,0:T(8,128)(2,1)S(1)}, u32[]{:S(2)}, u32[]{:S(2)}) collective-permute-start(bf16[64,512]{1,0:T(8,128)(2,1)S(1)} %slice.137), channel_id=1, source_target_pairs={{0,4},{2,6},{4,0},{6,2},{8,12},{10,14},{12,8},{14,10},{16,20},{18,... | collective-permute-start | bytes 196616 | tf_op jit(solution)/shard_map/ppermute | solution.py:26
  48.0 4.3 %collective-permute-start.25 = (bf16[32,1024]{1,0:T(8,128)(2,1)S(1)}, bf16[32,1024]{1,0:T(8,128)(2,1)S(1)}, u32[]{:S(2)}, u32[]{:S(2)}) collective-permute-start(bf16[32,1024]{1,0:T(8,128)(2,1)S(1)} %fusion.4), channel_id=1, source_target_pairs={{0,8},{2,10},{4,12},{6,14},{8,0},{10,2},{12,4},{14,6},{16,24},{18,... | collective-permute-start | bytes 196616 | tf_op jit(solution)/shard_map/ppermute | solution.py:26
  52.3 4.9 %collective-permute-start.26 = (bf16[16,1024]{1,0:T(8,128)(2,1)S(1)}, bf16[16,1024]{1,0:T(8,128)(2,1)S(1)}, u32[]{:S(2)}, u32[]{:S(2)}) collective-permute-start(bf16[16,1024]{1,0:T(8,128)(2,1)S(1)} %slice.138), channel_id=1, source_target_pairs={{0,16},{2,18},{4,20},{6,22},{8,24},{10,26},{12,28},{14,30},{16,0},... | collective-permute-start | bytes 98312 | tf_op jit(solution)/shard_map/ppermute | solution.py:26

commit v9 on v8

--- a/solution.py
+++ b/solution.py
@@ -85,20 +85,20 @@
         rate_ref[:, at] = rate[c * rows : (c + 1) * rows]
 
 
-def store_flat(back_ref, seg_ref, refs):
+def store_flat(back_ref, seg_ref, kept_ref, away_ref, lanes):
     flat = dot(back_ref[...], seg_ref[...]).astype(BF)
-    count = flat.shape[0] // len(refs)
-    for i, ref in enumerate(refs):
-        ref[...] = flat[i * count : (i + 1) * count]
+    half = kept_ref.shape[0]
+    kept_ref[:, lanes] = flat[:half]
+    away_ref[:, lanes] = flat[half:]
 
 
 def second_kernel(
     hidden_rows, up_scale, own, back_ref, part_ref, got_ref, weights_ref, moment_ref, rate_ref, x_ref, g_ref, *rest
 ):
     if own:
-        feedback_ref, *flat_refs, error_ref, local_ref, seg_ref = rest
+        feedback_ref, kept_ref, away_ref, error_ref, local_ref, seg_ref = rest
     else:
-        *flat_refs, local_ref, seg_ref = rest
+        kept_ref, away_ref, local_ref, seg_ref = rest
     rows = 2 * hidden_rows
     segment = seg_ref.shape[1]
     width = x_ref.shape[1]
@@ -108,7 +108,7 @@
     columns = gradient_rows(local_ref[...], x_ref, g_ref, hidden_rows, up_scale)
     for c in range(width // segment):
         seg_ref[c * rows : (c + 1) * rows] = columns(slice(c * segment, (c + 1) * segment)).astype(BF)
-    store_flat(back_ref, seg_ref, flat_refs[:2] if own else flat_refs)
+    store_flat(back_ref, seg_ref, kept_ref, away_ref, slice(0, segment))
     if own:
         shifted = local_moment + feedback_ref[...].astype(F32)
         magnitude = jnp.sum(jnp.abs(shifted), axis=1, keepdims=True) * (1.0 / width) + 1e-06
@@ -116,7 +116,7 @@
         error_ref[...] = (shifted - packed).astype(BF)
         for c in range(width // segment):
             seg_ref[c * rows : (c + 1) * rows] = packed[:, c * segment : (c + 1) * segment].astype(BF)
-        store_flat(back_ref, seg_ref, flat_refs[2:])
+        store_flat(back_ref, seg_ref, kept_ref, away_ref, slice(segment, 2 * segment))
 
 
 def tokens_of(step, arrays, *others):
@@ -205,7 +205,7 @@
     arrived = [swap(b, "dp", far[-1]) for b in blocks_a]
 
     half = segments // 2
-    kept, away, event = [None] * n_mp, [None] * n_mp, sent[-1]
+    sums, event = [None] * n_mp, sent[-1]
     for k in reversed(range(n_mp)):
         own = k == 0
         block = jnp.concatenate([blocks_a[k], after(arrived[k], event)], axis=0)
@@ -215,7 +215,7 @@
             functools.partial(moments_kernel, rows), (shape(tensor, F32), shape(tensor, F32)), (place_map, *terms)
         )
         operands = [back_map, parts[k], got[k], weights[k], moment_t, rate, *two]
-        out = [shape((half, segment), BF)] * (4 if own else 2)
+        out = [shape((half, (2 if own else 1) * segment), BF)] * 2
         if own:
             operands.append(feedback[0].reshape(tensor))
             out.append(shape(tensor, BF))
@@ -225,26 +225,19 @@
             operands,
             [pltpu.VMEM(tensor, BF), pltpu.VMEM((segments, segment), BF)],
         )
-        kept[k], away[k] = result[:2]
-        event = kept[k]
-    packed = result[2].astype(F32) + swap(result[3], "dp", 1).astype(F32)
-    error = result[4]
-
-    def halves(total, masks):
-        for mask in masks:
-            count = total.shape[0] // 2
-            total = total[:count] + swap(total[count:].astype(BF), "dp", mask).astype(F32)
-        return total
-
+        event = result[0]
+        sums[k] = result[0].astype(F32) + swap(result[1], "dp", 1).astype(F32)
+    error = result[2]
+
+    for mask in far[::-1]:
+        count = sums[0].shape[0] // 2
+        sums = [p[:count] + swap(p[count:].astype(BF), "dp", mask).astype(F32) for p in sums]
+    own_grad, own_packed = sums[0][:, :segment], sums[0][:, segment:]
+    grads = [own_grad] + sums[1:]
     for mask in mp_bits:
-        away_got = [swap(p.astype(BF), "mp", mask) for p in away[mask:]]
-        kept_got = [after(swap(p.astype(BF), "mp", mask), packed) for p in kept[mask:]]
-        away = [p.astype(F32) + q.astype(F32) for p, q in zip(away, away_got)]
-        kept = [p.astype(F32) + q.astype(F32) for p, q in zip(kept, kept_got)]
-    grad = kept[0] + swap(away[0].astype(BF), "dp", 1).astype(F32)
-    packed, grad = halves(packed, far[:-2:-1]), halves(grad, far[:-2:-1])
-    both = halves(jnp.concatenate([grad, packed], axis=1), far[-2::-1])
-    own_grad, own_packed = both[:, :segment], both[:, segment:]
+        crossed = [swap(p.astype(BF), "mp", mask).astype(F32) for p in grads[mask:]]
+        grads = [p + q for p, q in zip(grads, crossed)]
+    own_grad = grads[0]
     mean_grad = own_grad / n_dp
     mean_moment = own_packed / n_dp
     moment_new = beta_one * mean_moment + (1.0 - beta_one) * mean_grad

time: 58.2 us -> 58.3 us (level)
  starting transfers between devices: 29.1 us -> 30.6 us
  waiting for transfers between devices: 15.6 us -> 14.1 us
    ppermute x27 -> x28, starting transfers between devices: 29.1 us -> 30.6 us  [swap(): return lax.ppermute(x, axis, [(i, i ^ mask) for i in range(n)])]
    ppermute x27 -> x28, waiting for transfers between devices: 15.6 us -> 14.1 us  [swap(): return lax.ppermute(x, axis, [(i, i ^ mask) for i in range(n)])]
  transfers between devices with their start and end apart: 27 -> 28, of which waited for: 13 -> 17; matrix products, arithmetic and copies ran while one was open for 7% -> 7% of each run, Pallas kernels for 12% -> 12%
where the time goes in v9:
time: 58.3 us; the launch traced here: 57.9 us
  starting transfers between devices  30.6 us (52%)
  waiting for transfers between devices  14.1 us (24%)
  Pallas kernels  6.69 us (11%)
  other arithmetic  3.4 us (6%)
  local copies, waits for them, and re-layouts  2.21 us (4%)
  between operations  0.93 us (2%)
    ppermute x28, starting transfers between devices, swap(): return lax.ppermute(x, axis, [(i, i ^ mask) for i in range(n)])  30.6 us
    ppermute x28, waiting for transfers between devices, swap(): return lax.ppermute(x, axis, [(i, i ^ mask) for i in range(n)])  14.1 us
    pallas_call x6, Pallas kernels, call(): pl.pallas_call(kernel, out_shape=out_shape, in_specs=[pl.BlockSpec(memory...  6.69 us
    squeeze x3, local copies, waits for them, and re-layouts, tokens_of(): x[step]  1.81 us
  transfers between devices with their start and end apart: 28, of which 17 were waited for; matrix products, arithmetic and copies ran while one was open for 7% of the time, Pallas kernels for 12%

profile of v9, /device:TPU:0, one launch (start us, length us, event | category | flops | bytes accessed | tf_op | source)
XLA Modules:
  0.0 57.9 jit_solution(7372446483509596489)
XLA Ops:
  0.6 0.8 %bitcast_convert_fusion = bf16[16,512]{1,0:T(8,128)(2,1)S(1)} fusion(f32[1,16,512]{2,1,0:T(8,128)} %param.7), kind=kLoop, calls=%fused_computation.40 | loop fusion | flops 8192 | bytes 49152 | tf_op jit(solution)/shard_map/convert_element_type | solution.py:150
  1.4 4.0 %collective-permute-start = (bf16[16,512]{1,0:T(8,128)(2,1)S(1)}, bf16[16,512]{1,0:T(8,128)(2,1)S(1)}, u32[]{:S(2)}, u32[]{:S(2)}) collective-permute-start(bf16[16,512]{1,0:T(8,128)(2,1)S(1)} %bitcast_convert_fusion), channel_id=1, source_target_pairs={{0,16},{2,18},{4,20},{6,22},{8,24},{10,26},{12,28},{14,30},{16,0},... | collective-permute-start | bytes 49160 | tf_op jit(solution)/shard_map/ppermute | solution.py:26
  5.4 0.8 %convert_bitcast_fusion = bf16[16,512]{1,0:T(8,128)(2,1)S(1)} fusion(f32[1,16,512]{2,1,0:T(8,128)} %param.9), kind=kLoop, calls=%fused_computation.41 | loop fusion | flops 8192 | bytes 49152 | tf_op jit(solution)/shard_map/convert.7
  6.2 0.8 %fusion.2 = (bf16[16,512]{1,0:T(8,128)(2,1)S(1)}, bf16[16,512]{1,0:T(8,128)(2,1)S(1)}) fusion(f32[16,512]{1,0:T(8,128)} %bitcast.28), kind=kLoop, calls=%fused_computation.28 | loop fusion | flops 32768 | bytes 65536 | tf_op jit(solution)/shard_map/convert_element_type | solution.py:153
  7.0 1.6 %collective-permute-start.7 = (bf16[16,1024]{1,0:T(8,128)(2,1)S(1)}, bf16[16,1024]{1,0:T(8,128)(2,1)S(1)}, u32[]{:S(2)}, u32[]{:S(2)}) collective-permute-start(bf16[16,1024]{1,0:T(8,128)(2,1)S(1)} %pad_maximum_fusion.8), channel_id=1, source_target_pairs={{0,1},{1,0},{2,3},{3,2},{4,5},{5,4},{6,7},{7,6},{8,9},{9,8},{10,11... | collective-permute-start | bytes 98312 | tf_op jit(solution)/shard_map/ppermute | solution.py:26
  8.6 1.6 %collective-permute-start.1 = (bf16[32,512]{1,0:T(8,128)(2,1)S(1)}, bf16[32,512]{1,0:T(8,128)(2,1)S(1)}, u32[]{:S(2)}, u32[]{:S(2)}) collective-permute-start(bf16[32,512]{1,0:T(8,128)(2,1)S(1)} %pad_maximum_fusion.7), channel_id=1, source_target_pairs={{0,8},{2,10},{4,12},{6,14},{8,0},{10,2},{12,4},{14,6},{16,24},{18,... | collective-permute-start | bytes 98312 | tf_op jit(solution)/shard_map/ppermute | solution.py:26
  10.2 0.8 %collective-permute-done.7 = bf16[16,1024]{1,0:T(8,128)(2,1)S(1)} collective-permute-done((bf16[16,1024]{1,0:T(8,128)(2,1)S(1)}, bf16[16,1024]{1,0:T(8,128)(2,1)S(1)}, u32[]{:S(2)}, u32[]{:S(2)}) %collective-permute-start.7) | collective-permute-done | bytes 32800 | tf_op jit(solution)/shard_map/ppermute | solution.py:26
  11.0 0.8 %collective-permute-start.8 = (bf16[16,2560]{1,0:T(8,128)(2,1)S(1)}, bf16[16,2560]{1,0:T(8,128)(2,1)S(1)}, u32[]{:S(2)}, u32[]{:S(2)}) collective-permute-start(bf16[16,2560]{1,0:T(8,128)(2,1)S(1)} %pad_maximum_fusion.5), channel_id=1, source_target_pairs={{0,16},{2,18},{4,20},{6,22},{8,24},{10,26},{12,28},{14,30},{16,0},... | collective-permute-start | bytes 245768 | tf_op jit(solution)/shard_map/ppermute | solution.py:26
  11.8 0.7 %collective-permute-done.1 = bf16[32,512]{1,0:T(8,128)(2,1)S(1)} collective-permute-done((bf16[32,512]{1,0:T(8,128)(2,1)S(1)}, bf16[32,512]{1,0:T(8,128)(2,1)S(1)}, u32[]{:S(2)}, u32[]{:S(2)}) %collective-permute-start.1) | collective-permute-done | bytes 32800 | tf_op jit(solution)/shard_map/ppermute | solution.py:26
  12.6 1.6 %collective-permute-start.2 = (bf16[64,512]{1,0:T(8,128)(2,1)S(1)}, bf16[64,512]{1,0:T(8,128)(2,1)S(1)}, u32[]{:S(2)}, u32[]{:S(2)}) collective-permute-start(bf16[64,512]{1,0:T(8,128)(2,1)S(1)} %pad_maximum_fusion.6), channel_id=1, source_target_pairs={{0,4},{2,6},{4,0},{6,2},{8,12},{10,14},{12,8},{14,10},{16,20},{18,... | collective-permute-start | bytes 196616 | tf_op jit(solution)/shard_map/ppermute | solution.py:26
  14.1 1.7 %slice_bitcast_fusion.2 = (bf16[64,8192]{1,0:T(8,128)(2,1)S(1)}, bf16[64,8192]{1,0:T(8,128)(2,1)S(1)}) fusion(bf16[2,64,8192]{2,1,0:T(8,128)(2,1)} %param.13, bf16[2,64,8192]{2,1,0:T(8,128)(2,1)} %param.12), kind=kLoop, calls=%fused_computation.2 | loop fusion | bytes 4194304 | tf_op jit(solution)/shard_map/squeeze | solution.py:123
  15.8 1.1 %collective-permute-done.2 = bf16[64,512]{1,0:T(8,128)(2,1)S(1)} collective-permute-done((bf16[64,512]{1,0:T(8,128)(2,1)S(1)}, bf16[64,512]{1,0:T(8,128)(2,1)S(1)}, u32[]{:S(2)}, u32[]{:S(2)}) %collective-permute-start.2) | collective-permute-done | bytes 65568 | tf_op jit(solution)/shard_map/ppermute | solution.py:26
  16.9 0.9 %collective-permute-start.4 = (bf16[128,512]{1,0:T(8,128)(2,1)S(1)}, bf16[128,512]{1,0:T(8,128)(2,1)S(1)}, u32[]{:S(2)}, u32[]{:S(2)}) collective-permute-start(bf16[128,512]{1,0:T(8,128)(2,1)S(1)} %pad_maximum_fusion.3.w0_ref), channel_id=1, source_target_pairs={{0,1},{1,0},{2,3},{3,2},{4,5},{5,4},{6,7},{7,6},{8,9},{9,8},{10,11... | collective-permute-start | bytes 393224 | tf_op jit(solution)/shard_map/ppermute | solution.py:26
  18.1 1.6 %collective-permute-start.12 = (bf16[32,1024]{1,0:T(8,128)(2,1)S(1)}, bf16[32,1024]{1,0:T(8,128)(2,1)S(1)}, u32[]{:S(2)}, u32[]{:S(2)}) collective-permute-start(bf16[32,1024]{1,0:T(8,128)(2,1)S(1)} %slice.107), channel_id=1, source_target_pairs={{0,8},{2,10},{4,12},{6,14},{8,0},{10,2},{12,4},{14,6},{16,24},{18,... | collective-permute-start | bytes 196616 | tf_op jit(solution)/shard_map/ppermute | solution.py:26
  19.7 0.4 collective-permute-start.9
  20.2 1.3 %shard_map.94 = (bf16[16,8192]{1,0:T(8,128)(2,1)S(1)}, f32[16,8192]{1,0:T(8,128)S(1)}, bf16[16,8192]{1,0:T(8,128)(2,1)S(1)}) custom-call(bf16[256,256]{1,0:T(8,128)(2,1)S(1)} %get-tuple-element.66.place_ref, bf16[128,512]{1,0:T(8,128)(2,1)S(1)} %pad_maximum_fusion.3.w0_ref, bf16[128,512]{1,0:T(8,128)(2,1)S(1)} %collective-permute-done.3.w1_ref, ...), custom_call_target="tpu_custom_call" | custom-call | flops 1 | bytes 1 | tf_op jit(solution)/shard_map/pallas_call | solution.py:127
  21.5 1.3 %collective-permute-start.11 = (bf16[16,8192]{1,0:T(8,128)(2,1)S(1)}, bf16[16,8192]{1,0:T(8,128)(2,1)S(1)}, u32[]{:S(2)}, u32[]{:S(2)}) collective-permute-start(bf16[16,8192]{1,0:T(8,128)(2,1)S(1)} %get-tuple-element.39), channel_id=1, source_target_pairs={{0,1},{1,0},{2,3},{3,2},{4,5},{5,4},{6,7},{7,6},{8,9},{9,8},{10,11... | collective-permute-start | bytes 786440 | tf_op jit(solution)/shard_map/ppermute | solution.py:26
  22.8 1.9 %collective-permute-done.9 = bf16[32,1536]{1,0:T(8,128)(2,1)S(1)} collective-permute-done((bf16[32,1536]{1,0:T(8,128)(2,1)S(1)}, bf16[32,1536]{1,0:T(8,128)(2,1)S(1)}, u32[]{:S(2)}, u32[]{:S(2)}) %collective-permute-start.9) | collective-permute-done | bytes 98336 | tf_op jit(solution)/shard_map/ppermute | solution.py:26
  24.7 1.6 %collective-permute-start.13 = (bf16[64,1024]{1,0:T(8,128)(2,1)S(1)}, bf16[64,1024]{1,0:T(8,128)(2,1)S(1)}, u32[]{:S(2)}, u32[]{:S(2)}) collective-permute-start(bf16[64,1024]{1,0:T(8,128)(2,1)S(1)} %pad_maximum_fusion.4), channel_id=1, source_target_pairs={{0,4},{2,6},{4,0},{6,2},{8,12},{10,14},{12,8},{14,10},{16,20},{18,... | collective-permute-start | bytes 393224 | tf_op jit(solution)/shard_map/ppermute | solution.py:26
  26.3 0.6 %collective-permute-start.10 = (bf16[64,1536]{1,0:T(8,128)(2,1)S(1)}, bf16[64,1536]{1,0:T(8,128)(2,1)S(1)}, u32[]{:S(2)}, u32[]{:S(2)}) collective-permute-start(bf16[64,1536]{1,0:T(8,128)(2,1)S(1)} %pad_maximum_fusion.2), channel_id=1, source_target_pairs={{0,4},{2,6},{4,0},{6,2},{8,12},{10,14},{12,8},{14,10},{16,20},{18,... | collective-permute-start | bytes 589832 | tf_op jit(solution)/shard_map/ppermute | solution.py:26
  26.9 0.7 %collective-permute-done.5.w1_ref = bf16[128,512]{1,0:T(8,128)(2,1)S(1)} collective-permute-done((bf16[128,512]{1,0:T(8,128)(2,1)S(1)}, bf16[128,512]{1,0:T(8,128)(2,1)S(1)}, u32[]{:S(2)}, u32[]{:S(2)}) %collective-permute-start.5) | collective-permute-done | bytes 131104 | tf_op jit(solution)/shard_map/ppermute | solution.py:26
  27.6 1.3 %shard_map.95 = (bf16[16,8192]{1,0:T(8,128)(2,1)S(1)}, f32[16,8192]{1,0:T(8,128)S(1)}, bf16[16,8192]{1,0:T(8,128)(2,1)S(1)}) custom-call(bf16[256,256]{1,0:T(8,128)(2,1)S(1)} %get-tuple-element.66.place_ref, bf16[128,512]{1,0:T(8,128)(2,1)S(1)} %collective-permute-done.4.w0_ref, bf16[128,512]{1,0:T(8,128)(2,1)S(1)} %collective-permute-done.5.w1_ref, ...), custom_call_target="tpu_custom_call" | custom-call | flops 1 | bytes 1 | tf_op jit(solution)/shard_map/pallas_call | solution.py:127
  28.9 1.3 %collective-permute-start.6 = (bf16[16,8192]{1,0:T(8,128)(2,1)S(1)}, bf16[16,8192]{1,0:T(8,128)(2,1)S(1)}, u32[]{:S(2)}, u32[]{:S(2)}) collective-permute-start(bf16[16,8192]{1,0:T(8,128)(2,1)S(1)} %get-tuple-element.34), channel_id=1, source_target_pairs={{0,1},{1,0},{2,3},{3,2},{4,5},{5,4},{6,7},{7,6},{8,9},{9,8},{10,11... | collective-permute-start | bytes 786440 | tf_op jit(solution)/shard_map/ppermute | solution.py:26
  30.3 0.5 collective-permute-start.14
  31.0 0.7 %collective-permute-done.15.refs_3_ = bf16[128,512]{1,0:T(8,128)(2,1)S(1)} collective-permute-done((bf16[128,512]{1,0:T(8,128)(2,1)S(1)}, bf16[128,512]{1,0:T(8,128)(2,1)S(1)}, u32[]{:S(2)}, u32[]{:S(2)}) %collective-permute-start.15) | collective-permute-done | bytes 131104 | tf_op jit(solution)/shard_map/ppermute | solution.py:26
  31.8 0.5 shard_map.96
  32.4 1.3 %shard_map.97 = (bf16[128,512]{1,0:T(8,128)(2,1)S(1)}, bf16[128,512]{1,0:T(8,128)(2,1)S(1)}) custom-call(bf16[256,256]{1,0:T(8,128)(2,1)S(1)} %get-tuple-element.67.back_ref, f32[16,8192]{1,0:T(8,128)S(1)} %get-tuple-element.41.part_ref, bf16[16,8192]{1,0:T(8,128)(2,1)S(1)} %collective-permute-done.11.got_ref, ...), custom_call_target="tpu_custom_call" | custom-call | flops 1 | bytes 1 | tf_op jit(solution)/shard_map/pallas_call | solution.py:127
  33.7 0.3 collective-permute-done.10
  34.1 0.5 collective-permute-start.17
  34.7 0.4 collective-permute-start.23
  35.1 0.3 collective-permute-done.18.refs_5_
  35.6 0.3 collective-permute-done.16.refs_3_
  35.9 0.6 shard_map.98
  36.5 0.8 %collective-permute-done.6.got_ref = bf16[16,8192]{1,0:T(8,128)(2,1)S(1)} collective-permute-done((bf16[16,8192]{1,0:T(8,128)(2,1)S(1)}, bf16[16,8192]{1,0:T(8,128)(2,1)S(1)}, u32[]{:S(2)}, u32[]{:S(2)}) %collective-permute-start.6) | collective-permute-done | bytes 262176 | tf_op jit(solution)/shard_map/ppermute | solution.py:26
  37.3 1.8 %shard_map.99 = (bf16[128,1024]{1,0:T(8,128)(2,1)S(1)}, bf16[128,1024]{1,0:T(8,128)(2,1)S(1)}, bf16[16,8192]{1,0:T(8,128)(2,1)}) custom-call(bf16[256,256]{1,0:T(8,128)(2,1)S(1)} %get-tuple-element.67.back_ref, f32[16,8192]{1,0:T(8,128)S(1)} %get-tuple-element.33.part_ref, bf16[16,8192]{1,0:T(8,128)(2,1)S(1)} %collective-permute-done.6.got_ref, ...), custom_call_target="tpu_custom_call" | custom-call | flops 1 | bytes 1 | tf_op jit(solution)/shard_map/pallas_call | solution.py:127
  39.2 1.6 %collective-permute-start.24 = (bf16[64,512]{1,0:T(8,128)(2,1)S(1)}, bf16[64,512]{1,0:T(8,128)(2,1)S(1)}, u32[]{:S(2)}, u32[]{:S(2)}) collective-permute-start(bf16[64,512]{1,0:T(8,128)(2,1)S(1)} %slice.161), channel_id=1, source_target_pairs={{0,4},{2,6},{4,0},{6,2},{8,12},{10,14},{12,8},{14,10},{16,20},{18,... | collective-permute-start | bytes 196616 | tf_op jit(solution)/shard_map/ppermute | solution.py:26
  40.9 1.1 %collective-permute-start.20 = (bf16[64,1024]{1,0:T(8,128)(2,1)S(1)}, bf16[64,1024]{1,0:T(8,128)(2,1)S(1)}, u32[]{:S(2)}, u32[]{:S(2)}) collective-permute-start(bf16[64,1024]{1,0:T(8,128)(2,1)S(1)} %slice.160), channel_id=1, source_target_pairs={{0,4},{2,6},{4,0},{6,2},{8,12},{10,14},{12,8},{14,10},{16,20},{18,... | collective-permute-start | bytes 393224 | tf_op jit(solution)/shard_map/ppermute | solution.py:26
  42.1 2.0 %collective-permute-done.24 = bf16[64,512]{1,0:T(8,128)(2,1)S(1)} collective-permute-done((bf16[64,512]{1,0:T(8,128)(2,1)S(1)}, bf16[64,512]{1,0:T(8,128)(2,1)S(1)}, u32[]{:S(2)}, u32[]{:S(2)}) %collective-permute-start.24) | collective-permute-done | bytes 65568 | tf_op jit(solution)/shard_map/ppermute | solution.py:26
  44.1 1.6 %collective-permute-start.25 = (bf16[32,512]{1,0:T(8,128)(2,1)S(1)}, bf16[32,512]{1,0:T(8,128)(2,1)S(1)}, u32[]{:S(2)}, u32[]{:S(2)}) collective-permute-start(bf16[32,512]{1,0:T(8,128)(2,1)S(1)} %slice.163), channel_id=1, source_target_pairs={{0,8},{2,10},{4,12},{6,14},{8,0},{10,2},{12,4},{14,6},{16,24},{18,... | collective-permute-start | bytes 98312 | tf_op jit(solution)/shard_map/ppermute | solution.py:26
  45.6 1.0 %collective-permute-done.20 = bf16[64,1024]{1,0:T(8,128)(2,1)S(1)} collective-permute-done((bf16[64,1024]{1,0:T(8,128)(2,1)S(1)}, bf16[64,1024]{1,0:T(8,128)(2,1)S(1)}, u32[]{:S(2)}, u32[]{:S(2)}) %collective-permute-start.20) | collective-permute-done | bytes 131104 | tf_op jit(solution)/shard_map/ppermute | solution.py:26
  46.6 1.7 %collective-permute-start.21 = (bf16[32,1024]{1,0:T(8,128)(2,1)S(1)}, bf16[32,1024]{1,0:T(8,128)(2,1)S(1)}, u32[]{:S(2)}, u32[]{:S(2)}) collective-permute-start(bf16[32,1024]{1,0:T(8,128)(2,1)S(1)} %slice.162), channel_id=1, source_target_pairs={{0,8},{2,10},{4,12},{6,14},{8,0},{10,2},{12,4},{14,6},{16,24},{18,... | collective-permute-start | bytes 196616 | tf_op jit(solution)/shard_map/ppermute | solution.py:26
  48.3 2.5 %collective-permute-start.26 = (bf16[16,512]{1,0:T(8,128)(2,1)S(1)}, bf16[16,512]{1,0:T(8,128)(2,1)S(1)}, u32[]{:S(2)}, u32[]{:S(2)}) collective-permute-start(bf16[16,512]{1,0:T(8,128)(2,1)S(1)} %slice.165), channel_id=1, source_target_pairs={{0,16},{2,18},{4,20},{6,22},{8,24},{10,26},{12,28},{14,30},{16,0},... | collective-permute-start | bytes 49160 | tf_op jit(solution)/shard_map/ppermute | solution.py:26
  50.9 0.3 collective-permute-done.21
  51.2 2.3 %collective-permute-start.22 = (bf16[16,1024]{1,0:T(8,128)(2,1)S(1)}, bf16[16,1024]{1,0:T(8,128)(2,1)S(1)}, u32[]{:S(2)}, u32[]{:S(2)}) collective-permute-start(bf16[16,1024]{1,0:T(8,128)(2,1)S(1)} %slice.164), channel_id=1, source_target_pairs={{0,16},{2,18},{4,20},{6,22},{8,24},{10,26},{12,28},{14,30},{16,0},... | collective-permute-start | bytes 98312 | tf_op jit(solution)/shard_map/ppermute | solution.py:26
  53.5 1.0 %collective-permute-start.27 = (bf16[16,512]{1,0:T(8,128)(2,1)S(1)}, bf16[16,512]{1,0:T(8,128)(2,1)S(1)}, u32[]{:S(2)}, u32[]{:S(2)}) collective-permute-start(bf16[16,512]{1,0:T(8,128)(2,1)S(1)} %fusion.3), channel_id=1, source_target_pairs={{0,1},{1,0},{2,3},{3,2},{4,5},{5,4},{6,7},{7,6},{8,9},{9,8},{10,11... | collective-permute-start | bytes 49160 | tf_op jit(solution)/shard_map/ppermute | solution.py:26
  54.4 1.6 %collective-permute-done.22 = bf16[16,1024]{1,0:T(8,128)(2,1)S(1)} collective-permute-done((bf16[16,1024]{1,0:T(8,128)(2,1)S(1)}, bf16[16,1024]{1,0:T(8,128)(2,1)S(1)}, u32[]{:S(2)}, u32[]{:S(2)}) %collective-permute-start.22) | collective-permute-done | bytes 32800 | tf_op jit(solution)/shard_map/ppermute | solution.py:26
  56.1 1.2 %collective-permute-done.27 = bf16[16,512]{1,0:T(8,128)(2,1)S(1)} collective-permute-done((bf16[16,512]{1,0:T(8,128)(2,1)S(1)}, bf16[16,512]{1,0:T(8,128)(2,1)S(1)}, u32[]{:S(2)}, u32[]{:S(2)}) %collective-permute-start.27) | collective-permute-done | bytes 16416 | tf_op jit(solution)/shard_map/ppermute | solution.py:26
  57.3 0.6 %fusion.12 = (f32[1,16,512]{2,1,0:T(8,128)}, f32[1,16,512]{2,1,0:T(8,128)}) fusion(bf16[16,512]{1,0:T(8,128)(2,1)S(1)} %collective-permute-done.27, f32[16,1024]{1,0:T(8,128)S(1)} %slice_add_fusion.4, f32[1,16,512]{2,1,0:T(8,128)S(1)} %copy-done.4, f32[1,16,512]{2,1,0:T(8,128)S(1)} %copy-done.3), kind=kLoop, calls=%fused_computation.57 | loop fusion | flops 90112 | bytes 212992 | tf_op jit(solution)/shard_map/broadcast_in_dim | solution.py:246
  (67 shorter events, 1.6 us)
Async XLA Ops:
  1.4 7.2 %collective-permute-start = (bf16[16,512]{1,0:T(8,128)(2,1)S(1)}, bf16[16,512]{1,0:T(8,128)(2,1)S(1)}, u32[]{:S(2)}, u32[]{:S(2)}) collective-permute-start(bf16[16,512]{1,0:T(8,128)(2,1)S(1)} %bitcast_convert_fusion), channel_id=1, source_target_pairs={{0,16},{2,18},{4,20},{6,22},{8,24},{10,26},{12,28},{14,30},{16,0},... | collective-permute-start | bytes 49160 | tf_op jit(solution)/shard_map/ppermute | solution.py:26
  7.0 4.0 %collective-permute-start.7 = (bf16[16,1024]{1,0:T(8,128)(2,1)S(1)}, bf16[16,1024]{1,0:T(8,128)(2,1)S(1)}, u32[]{:S(2)}, u32[]{:S(2)}) collective-permute-start(bf16[16,1024]{1,0:T(8,128)(2,1)S(1)} %pad_maximum_fusion.8), channel_id=1, source_target_pairs={{0,1},{1,0},{2,3},{3,2},{4,5},{5,4},{6,7},{7,6},{8,9},{9,8},{10,11... | collective-permute-start | bytes 98312 | tf_op jit(solution)/shard_map/ppermute | solution.py:26
  8.6 3.9 %collective-permute-start.1 = (bf16[32,512]{1,0:T(8,128)(2,1)S(1)}, bf16[32,512]{1,0:T(8,128)(2,1)S(1)}, u32[]{:S(2)}, u32[]{:S(2)}) collective-permute-start(bf16[32,512]{1,0:T(8,128)(2,1)S(1)} %pad_maximum_fusion.7), channel_id=1, source_target_pairs={{0,8},{2,10},{4,12},{6,14},{8,0},{10,2},{12,4},{14,6},{16,24},{18,... | collective-permute-start | bytes 98312 | tf_op jit(solution)/shard_map/ppermute | solution.py:26
  11.0 6.7 %collective-permute-start.8 = (bf16[16,2560]{1,0:T(8,128)(2,1)S(1)}, bf16[16,2560]{1,0:T(8,128)(2,1)S(1)}, u32[]{:S(2)}, u32[]{:S(2)}) collective-permute-start(bf16[16,2560]{1,0:T(8,128)(2,1)S(1)} %pad_maximum_fusion.5), channel_id=1, source_target_pairs={{0,16},{2,18},{4,20},{6,22},{8,24},{10,26},{12,28},{14,30},{16,0},... | collective-permute-start | bytes 245768 | tf_op jit(solution)/shard_map/ppermute | solution.py:26
  12.6 5.3 %copy-start.5 = (s32[256]{0:T(256)S(1)}, s32[256]{0:T(256)}, u32[]{:S(2)}) copy-start(s32[256]{0:T(256)} %param.10) | copy-start | bytes 3076
  12.6 4.3 %collective-permute-start.2 = (bf16[64,512]{1,0:T(8,128)(2,1)S(1)}, bf16[64,512]{1,0:T(8,128)(2,1)S(1)}, u32[]{:S(2)}, u32[]{:S(2)}) collective-permute-start(bf16[64,512]{1,0:T(8,128)(2,1)S(1)} %pad_maximum_fusion.6), channel_id=1, source_target_pairs={{0,4},{2,6},{4,0},{6,2},{8,12},{10,14},{12,8},{14,10},{16,20},{18,... | collective-permute-start | bytes 196616 | tf_op jit(solution)/shard_map/ppermute | solution.py:26
  16.9 9.4 %collective-permute-start.4 = (bf16[128,512]{1,0:T(8,128)(2,1)S(1)}, bf16[128,512]{1,0:T(8,128)(2,1)S(1)}, u32[]{:S(2)}, u32[]{:S(2)}) collective-permute-start(bf16[128,512]{1,0:T(8,128)(2,1)S(1)} %pad_maximum_fusion.3.w0_ref), channel_id=1, source_target_pairs={{0,1},{1,0},{2,3},{3,2},{4,5},{5,4},{6,7},{7,6},{8,9},{9,8},{10,11... | collective-permute-start | bytes 393224 | tf_op jit(solution)/shard_map/ppermute | solution.py:26
  17.8 2.5 %collective-permute-start.3 = (bf16[128,512]{1,0:T(8,128)(2,1)S(1)}, bf16[128,512]{1,0:T(8,128)(2,1)S(1)}, u32[]{:S(2)}, u32[]{:S(2)}) collective-permute-start(bf16[128,512]{1,0:T(8,128)(2,1)S(1)} %pad_maximum_fusion.3.w0_ref), channel_id=1, source_target_pairs={{0,2},{2,0},{4,6},{6,4},{8,10},{10,8},{12,14},{14,12},{16,18},{18,... | collective-permute-start | bytes 393224 | tf_op jit(solution)/shard_map/ppermute | solution.py:26
  18.1 4.7 %collective-permute-start.12 = (bf16[32,1024]{1,0:T(8,128)(2,1)S(1)}, bf16[32,1024]{1,0:T(8,128)(2,1)S(1)}, u32[]{:S(2)}, u32[]{:S(2)}) collective-permute-start(bf16[32,1024]{1,0:T(8,128)(2,1)S(1)} %slice.107), channel_id=1, source_target_pairs={{0,8},{2,10},{4,12},{6,14},{8,0},{10,2},{12,4},{14,6},{16,24},{18,... | collective-permute-start | bytes 196616 | tf_op jit(solution)/shard_map/ppermute | solution.py:26
  19.7 5.0 %collective-permute-start.9 = (bf16[32,1536]{1,0:T(8,128)(2,1)S(1)}, bf16[32,1536]{1,0:T(8,128)(2,1)S(1)}, u32[]{:S(2)}, u32[]{:S(2)}) collective-permute-start(bf16[32,1536]{1,0:T(8,128)(2,1)S(1)} %slice.106), channel_id=1, source_target_pairs={{0,8},{2,10},{4,12},{6,14},{8,0},{10,2},{12,4},{14,6},{16,24},{18,... | collective-permute-start | bytes 294920 | tf_op jit(solution)/shard_map/ppermute | solution.py:26
  21.5 9.3 %copy-start.1 = (bf16[2,64,8192]{2,1,0:T(8,128)(2,1)S(1)}, bf16[2,64,8192]{2,1,0:T(8,128)(2,1)}, u32[]{:S(2)}) copy-start(bf16[2,64,8192]{2,1,0:T(8,128)(2,1)} %param.12) | copy-start | bytes 6291460
  21.5 10.9 %collective-permute-start.11 = (bf16[16,8192]{1,0:T(8,128)(2,1)S(1)}, bf16[16,8192]{1,0:T(8,128)(2,1)S(1)}, u32[]{:S(2)}, u32[]{:S(2)}) collective-permute-start(bf16[16,8192]{1,0:T(8,128)(2,1)S(1)} %get-tuple-element.39), channel_id=1, source_target_pairs={{0,1},{1,0},{2,3},{3,2},{4,5},{5,4},{6,7},{7,6},{8,9},{9,8},{10,11... | collective-permute-start | bytes 786440 | tf_op jit(solution)/shard_map/ppermute | solution.py:26
  24.7 5.5 %collective-permute-start.13 = (bf16[64,1024]{1,0:T(8,128)(2,1)S(1)}, bf16[64,1024]{1,0:T(8,128)(2,1)S(1)}, u32[]{:S(2)}, u32[]{:S(2)}) collective-permute-start(bf16[64,1024]{1,0:T(8,128)(2,1)S(1)} %pad_maximum_fusion.4), channel_id=1, source_target_pairs={{0,4},{2,6},{4,0},{6,2},{8,12},{10,14},{12,8},{14,10},{16,20},{18,... | collective-permute-start | bytes 393224 | tf_op jit(solution)/shard_map/ppermute | solution.py:26
  26.3 1.3 %collective-permute-start.5 = (bf16[128,512]{1,0:T(8,128)(2,1)S(1)}, bf16[128,512]{1,0:T(8,128)(2,1)S(1)}, u32[]{:S(2)}, u32[]{:S(2)}) collective-permute-start(bf16[128,512]{1,0:T(8,128)(2,1)S(1)} %collective-permute-done.4.w0_ref), channel_id=1, source_target_pairs={{0,2},{2,0},{4,6},{6,4},{8,10},{10,8},{12,14},{14,12},{16,18},{18,... | collective-permute-start | bytes 393224 | tf_op jit(solution)/shard_map/ppermute | solution.py:26
  26.3 7.7 %collective-permute-start.10 = (bf16[64,1536]{1,0:T(8,128)(2,1)S(1)}, bf16[64,1536]{1,0:T(8,128)(2,1)S(1)}, u32[]{:S(2)}, u32[]{:S(2)}) collective-permute-start(bf16[64,1536]{1,0:T(8,128)(2,1)S(1)} %pad_maximum_fusion.2), channel_id=1, source_target_pairs={{0,4},{2,6},{4,0},{6,2},{8,12},{10,14},{12,8},{14,10},{16,20},{18,... | collective-permute-start | bytes 589832 | tf_op jit(solution)/shard_map/ppermute | solution.py:26
  28.9 2.0 %copy-start.2 = (bf16[2,64,8192]{2,1,0:T(8,128)(2,1)S(1)}, bf16[2,64,8192]{2,1,0:T(8,128)(2,1)}, u32[]{:S(2)}) copy-start(bf16[2,64,8192]{2,1,0:T(8,128)(2,1)} %param.13) | copy-start | bytes 6291460
  28.9 8.4 %collective-permute-start.6 = (bf16[16,8192]{1,0:T(8,128)(2,1)S(1)}, bf16[16,8192]{1,0:T(8,128)(2,1)S(1)}, u32[]{:S(2)}, u32[]{:S(2)}) collective-permute-start(bf16[16,8192]{1,0:T(8,128)(2,1)S(1)} %get-tuple-element.34), channel_id=1, source_target_pairs={{0,1},{1,0},{2,3},{3,2},{4,5},{5,4},{6,7},{7,6},{8,9},{9,8},{10,11... | collective-permute-start | bytes 786440 | tf_op jit(solution)/shard_map/ppermute | solution.py:26
  30.2 1.4 %collective-permute-start.15 = (bf16[128,512]{1,0:T(8,128)(2,1)S(1)}, bf16[128,512]{1,0:T(8,128)(2,1)S(1)}, u32[]{:S(2)}, u32[]{:S(2)}) collective-permute-start(bf16[128,512]{1,0:T(8,128)(2,1)S(1)} %get-tuple-element.60.refs_1_), channel_id=1, source_target_pairs={{0,2},{2,0},{4,6},{6,4},{8,10},{10,8},{12,14},{14,12},{16,18},{18,... | collective-permute-start | bytes 393224 | tf_op jit(solution)/shard_map/ppermute | solution.py:26
  30.3 1.5 %collective-permute-start.14 = (bf16[128,512]{1,0:T(8,128)(2,1)S(1)}, bf16[128,512]{1,0:T(8,128)(2,1)S(1)}, u32[]{:S(2)}, u32[]{:S(2)}) collective-permute-start(bf16[128,512]{1,0:T(8,128)(2,1)S(1)} %get-tuple-element.61.refs_0_), channel_id=1, source_target_pairs={{0,2},{2,0},{4,6},{6,4},{8,10},{10,8},{12,14},{14,12},{16,18},{18,... | collective-permute-start | bytes 393224 | tf_op jit(solution)/shard_map/ppermute | solution.py:26
  33.7 3.7 %copy-start = (bf16[1,2,8,8192]{3,2,1,0:T(8,128)(2,1)S(1)}, bf16[1,2,8,8192]{3,2,1,0:T(8,128)(2,1)}, u32[]{:S(2)}) copy-start(bf16[1,2,8,8192]{3,2,1,0:T(8,128)(2,1)} %param.11) | copy-start | bytes 786436
  34.0 1.4 %collective-permute-start.18 = (bf16[128,512]{1,0:T(8,128)(2,1)S(1)}, bf16[128,512]{1,0:T(8,128)(2,1)S(1)}, u32[]{:S(2)}, u32[]{:S(2)}) collective-permute-start(bf16[128,512]{1,0:T(8,128)(2,1)S(1)} %get-tuple-element.57.refs_2_), channel_id=1, source_target_pairs={{0,2},{2,0},{4,6},{6,4},{8,10},{10,8},{12,14},{14,12},{16,18},{18,... | collective-permute-start | bytes 393224 | tf_op jit(solution)/shard_map/ppermute | solution.py:26
  34.1 1.5 %collective-permute-start.17 = (bf16[128,512]{1,0:T(8,128)(2,1)S(1)}, bf16[128,512]{1,0:T(8,128)(2,1)S(1)}, u32[]{:S(2)}, u32[]{:S(2)}) collective-permute-start(bf16[128,512]{1,0:T(8,128)(2,1)S(1)} %get-tuple-element.58.refs_1_), channel_id=1, source_target_pairs={{0,2},{2,0},{4,6},{6,4},{8,10},{10,8},{12,14},{14,12},{16,18},{18,... | collective-permute-start | bytes 393224 | tf_op jit(solution)/shard_map/ppermute | solution.py:26
  34.6 1.3 %collective-permute-start.16 = (bf16[128,512]{1,0:T(8,128)(2,1)S(1)}, bf16[128,512]{1,0:T(8,128)(2,1)S(1)}, u32[]{:S(2)}, u32[]{:S(2)}) collective-permute-start(bf16[128,512]{1,0:T(8,128)(2,1)S(1)} %get-tuple-element.59.refs_0_), channel_id=1, source_target_pairs={{0,2},{2,0},{4,6},{6,4},{8,10},{10,8},{12,14},{14,12},{16,18},{18,... | collective-permute-start | bytes 393224 | tf_op jit(solution)/shard_map/ppermute | solution.py:26
  34.7 4.5 %collective-permute-start.23 = (bf16[128,512]{1,0:T(8,128)(2,1)S(1)}, bf16[128,512]{1,0:T(8,128)(2,1)S(1)}, u32[]{:S(2)}, u32[]{:S(2)}) collective-permute-start(bf16[128,512]{1,0:T(8,128)(2,1)S(1)} %get-tuple-element.55), channel_id=1, source_target_pairs={{0,2},{2,0},{4,6},{6,4},{8,10},{10,8},{12,14},{14,12},{16,18},{18,... | collective-permute-start | bytes 393224 | tf_op jit(solution)/shard_map/ppermute | solution.py:26
  39.2 18.1 %copy-start.3 = (f32[1,16,512]{2,1,0:T(8,128)S(1)}, f32[1,16,512]{2,1,0:T(8,128)}, u32[]{:S(2)}) copy-start(f32[1,16,512]{2,1,0:T(8,128)} %param.7) | copy-start | bytes 98308
  39.2 18.1 %copy-start.4 = (f32[1,16,512]{2,1,0:T(8,128)S(1)}, f32[1,16,512]{2,1,0:T(8,128)}, u32[]{:S(2)}) copy-start(f32[1,16,512]{2,1,0:T(8,128)} %param.9) | copy-start | bytes 98308
  39.2 1.7 %collective-permute-start.19 = (bf16[128,1024]{1,0:T(8,128)(2,1)S(1)}, bf16[128,1024]{1,0:T(8,128)(2,1)S(1)}, u32[]{:S(2)}, u32[]{:S(2)}) collective-permute-start(bf16[128,1024]{1,0:T(8,128)(2,1)S(1)} %get-tuple-element.54), channel_id=1, source_target_pairs={{0,2},{2,0},{4,6},{6,4},{8,10},{10,8},{12,14},{14,12},{16,18},{18,... | collective-permute-start | bytes 786440 | tf_op jit(solution)/shard_map/ppermute | solution.py:26
  39.2 4.8 %collective-permute-start.24 = (bf16[64,512]{1,0:T(8,128)(2,1)S(1)}, bf16[64,512]{1,0:T(8,128)(2,1)S(1)}, u32[]{:S(2)}, u32[]{:S(2)}) collective-permute-start(bf16[64,512]{1,0:T(8,128)(2,1)S(1)} %slice.161), channel_id=1, source_target_pairs={{0,4},{2,6},{4,0},{6,2},{8,12},{10,14},{12,8},{14,10},{16,20},{18,... | collective-permute-start | bytes 196616 | tf_op jit(solution)/shard_map/ppermute | solution.py:26
  40.9 5.7 %collective-permute-start.20 = (bf16[64,1024]{1,0:T(8,128)(2,1)S(1)}, bf16[64,1024]{1,0:T(8,128)(2,1)S(1)}, u32[]{:S(2)}, u32[]{:S(2)}) collective-permute-start(bf16[64,1024]{1,0:T(8,128)(2,1)S(1)} %slice.160), channel_id=1, source_target_pairs={{0,4},{2,6},{4,0},{6,2},{8,12},{10,14},{12,8},{14,10},{16,20},{18,... | collective-permute-start | bytes 393224 | tf_op jit(solution)/shard_map/ppermute | solution.py:26
  44.1 4.2 %collective-permute-start.25 = (bf16[32,512]{1,0:T(8,128)(2,1)S(1)}, bf16[32,512]{1,0:T(8,128)(2,1)S(1)}, u32[]{:S(2)}, u32[]{:S(2)}) collective-permute-start(bf16[32,512]{1,0:T(8,128)(2,1)S(1)} %slice.163), channel_id=1, source_target_pairs={{0,8},{2,10},{4,12},{6,14},{8,0},{10,2},{12,4},{14,6},{16,24},{18,... | collective-permute-start | bytes 98312 | tf_op jit(solution)/shard_map/ppermute | solution.py:26
  46.6 4.5 %collective-permute-start.21 = (bf16[32,1024]{1,0:T(8,128)(2,1)S(1)}, bf16[32,1024]{1,0:T(8,128)(2,1)S(1)}, u32[]{:S(2)}, u32[]{:S(2)}) collective-permute-start(bf16[32,1024]{1,0:T(8,128)(2,1)S(1)} %slice.162), channel_id=1, source_target_pairs={{0,8},{2,10},{4,12},{6,14},{8,0},{10,2},{12,4},{14,6},{16,24},{18,... | collective-permute-start | bytes 196616 | tf_op jit(solution)/shard_map/ppermute | solution.py:26
  48.3 5.1 %collective-permute-start.26 = (bf16[16,512]{1,0:T(8,128)(2,1)S(1)}, bf16[16,512]{1,0:T(8,128)(2,1)S(1)}, u32[]{:S(2)}, u32[]{:S(2)}) collective-permute-start(bf16[16,512]{1,0:T(8,128)(2,1)S(1)} %slice.165), channel_id=1, source_target_pairs={{0,16},{2,18},{4,20},{6,22},{8,24},{10,26},{12,28},{14,30},{16,0},... | collective-permute-start | bytes 49160 | tf_op jit(solution)/shard_map/ppermute | solution.py:26
  51.2 4.9 %collective-permute-start.22 = (bf16[16,1024]{1,0:T(8,128)(2,1)S(1)}, bf16[16,1024]{1,0:T(8,128)(2,1)S(1)}, u32[]{:S(2)}, u32[]{:S(2)}) collective-permute-start(bf16[16,1024]{1,0:T(8,128)(2,1)S(1)} %slice.164), channel_id=1, source_target_pairs={{0,16},{2,18},{4,20},{6,22},{8,24},{10,26},{12,28},{14,30},{16,0},... | collective-permute-start | bytes 98312 | tf_op jit(solution)/shard_map/ppermute | solution.py:26
  53.5 3.8 %collective-permute-start.27 = (bf16[16,512]{1,0:T(8,128)(2,1)S(1)}, bf16[16,512]{1,0:T(8,128)(2,1)S(1)}, u32[]{:S(2)}, u32[]{:S(2)}) collective-permute-start(bf16[16,512]{1,0:T(8,128)(2,1)S(1)} %fusion.3), channel_id=1, source_target_pairs={{0,1},{1,0},{2,3},{3,2},{4,5},{5,4},{6,7},{7,6},{8,9},{9,8},{10,11... | collective-permute-start | bytes 49160 | tf_op jit(solution)/shard_map/ppermute | solution.py:26

commit v10 on v9

--- a/solution.py
+++ b/solution.py
@@ -200,7 +200,8 @@
         all_a = jnp.concatenate([all_a, after(swap(all_a, "dp", mask), steps[-1])], axis=0)
     ends = [0] + [(3 + 2 * k) * segment for k in range(n_mp)]
     blocks_a = [all_a[:, ends[k] : ends[k + 1]] for k in range(n_mp)]
-    arrived = [after(swap(b, "dp", far[-2]), sent[0]) for b in blocks_a]
+    blocks_a[0] = after(blocks_a[0], sent[0])
+    arrived = [after(swap(b, "dp", far[-2]), sent[0] if k else sent[-1]) for k, b in enumerate(blocks_a)]
     blocks_a = [jnp.concatenate(pair, axis=0) for pair in zip(blocks_a, arrived)]
     arrived = [swap(b, "dp", far[-1]) for b in blocks_a]
 

time: 58.3 us -> 57.1 us (0.979)
  waiting for transfers between devices: 14.1 us -> 12.1 us
  starting transfers between devices: 30.6 us -> 31.4 us
    ppermute x28, waiting for transfers between devices: 14.1 us -> 12.1 us  [swap(): return lax.ppermute(x, axis, [(i, i ^ mask) for i in range(n)])]
    ppermute x28, starting transfers between devices: 30.6 us -> 31.4 us  [swap(): return lax.ppermute(x, axis, [(i, i ^ mask) for i in range(n)])]
  transfers between devices with their start and end apart: 28 -> 28, of which waited for: 17 -> 16; matrix products, arithmetic and copies ran while one was open for 7% -> 7% of each run, Pallas kernels for 12% -> 12%
where the time goes in v10:
time: 57.1 us; the launch traced here: 56.8 us
  starting transfers between devices  31.4 us (55%)
  waiting for transfers between devices  12.1 us (21%)
  Pallas kernels  6.69 us (12%)
  other arithmetic  3.37 us (6%)
  local copies, waits for them, and re-layouts  2.24 us (4%)
  between operations  0.98 us (2%)
    ppermute x28, starting transfers between devices, swap(): return lax.ppermute(x, axis, [(i, i ^ mask) for i in range(n)])  31.4 us
    ppermute x28, waiting for transfers between devices, swap(): return lax.ppermute(x, axis, [(i, i ^ mask) for i in range(n)])  12.1 us
    pallas_call x6, Pallas kernels, call(): pl.pallas_call(kernel, out_shape=out_shape, in_specs=[pl.BlockSpec(memory...  6.69 us
    squeeze x3, local copies, waits for them, and re-layouts, tokens_of(): x[step]  1.81 us
  transfers between devices with their start and end apart: 28, of which 16 were waited for; matrix products, arithmetic and copies ran while one was open for 7% of the time, Pallas kernels for 12%

profile of v10, /device:TPU:0, one launch (start us, length us, event | category | flops | bytes accessed | tf_op | source)
XLA Modules:
  0.0 56.8 jit_solution(2145582948886347486)
XLA Ops:
  0.6 0.8 %bitcast_convert_fusion = bf16[16,512]{1,0:T(8,128)(2,1)S(1)} fusion(f32[1,16,512]{2,1,0:T(8,128)} %param.7), kind=kLoop, calls=%fused_computation.39 | loop fusion | flops 8192 | bytes 49152 | tf_op jit(solution)/shard_map/convert_element_type | solution.py:150
  1.4 4.0 %collective-permute-start = (bf16[16,512]{1,0:T(8,128)(2,1)S(1)}, bf16[16,512]{1,0:T(8,128)(2,1)S(1)}, u32[]{:S(2)}, u32[]{:S(2)}) collective-permute-start(bf16[16,512]{1,0:T(8,128)(2,1)S(1)} %bitcast_convert_fusion), channel_id=1, source_target_pairs={{0,16},{2,18},{4,20},{6,22},{8,24},{10,26},{12,28},{14,30},{16,0},... | collective-permute-start | bytes 49160 | tf_op jit(solution)/shard_map/ppermute | solution.py:26
  5.4 0.8 %fusion.2 = (bf16[16,512]{1,0:T(8,128)(2,1)S(1)}, bf16[16,512]{1,0:T(8,128)(2,1)S(1)}) fusion(f32[16,512]{1,0:T(8,128)} %bitcast.28), kind=kLoop, calls=%fused_computation.27 | loop fusion | flops 32768 | bytes 65536 | tf_op jit(solution)/shard_map/convert_element_type | solution.py:153
  6.3 0.8 %convert_bitcast_fusion = bf16[16,512]{1,0:T(8,128)(2,1)S(1)} fusion(f32[1,16,512]{2,1,0:T(8,128)} %param.9), kind=kLoop, calls=%fused_computation.40 | loop fusion | flops 8192 | bytes 49152 | tf_op jit(solution)/shard_map/convert.7
  7.0 1.5 %collective-permute-start.7 = (bf16[16,1024]{1,0:T(8,128)(2,1)S(1)}, bf16[16,1024]{1,0:T(8,128)(2,1)S(1)}, u32[]{:S(2)}, u32[]{:S(2)}) collective-permute-start(bf16[16,1024]{1,0:T(8,128)(2,1)S(1)} %pad_maximum_fusion.7), channel_id=1, source_target_pairs={{0,1},{1,0},{2,3},{3,2},{4,5},{5,4},{6,7},{7,6},{8,9},{9,8},{10,11... | collective-permute-start | bytes 98312 | tf_op jit(solution)/shard_map/ppermute | solution.py:26
  8.6 1.6 %collective-permute-start.1 = (bf16[32,512]{1,0:T(8,128)(2,1)S(1)}, bf16[32,512]{1,0:T(8,128)(2,1)S(1)}, u32[]{:S(2)}, u32[]{:S(2)}) collective-permute-start(bf16[32,512]{1,0:T(8,128)(2,1)S(1)} %pad_maximum_fusion.6), channel_id=1, source_target_pairs={{0,8},{2,10},{4,12},{6,14},{8,0},{10,2},{12,4},{14,6},{16,24},{18,... | collective-permute-start | bytes 98312 | tf_op jit(solution)/shard_map/ppermute | solution.py:26
  10.1 0.8 %collective-permute-done.7 = bf16[16,1024]{1,0:T(8,128)(2,1)S(1)} collective-permute-done((bf16[16,1024]{1,0:T(8,128)(2,1)S(1)}, bf16[16,1024]{1,0:T(8,128)(2,1)S(1)}, u32[]{:S(2)}, u32[]{:S(2)}) %collective-permute-start.7) | collective-permute-done | bytes 32800 | tf_op jit(solution)/shard_map/ppermute | solution.py:26
  11.0 0.8 %collective-permute-start.8 = (bf16[16,2560]{1,0:T(8,128)(2,1)S(1)}, bf16[16,2560]{1,0:T(8,128)(2,1)S(1)}, u32[]{:S(2)}, u32[]{:S(2)}) collective-permute-start(bf16[16,2560]{1,0:T(8,128)(2,1)S(1)} %pad_maximum_fusion.4), channel_id=1, source_target_pairs={{0,16},{2,18},{4,20},{6,22},{8,24},{10,26},{12,28},{14,30},{16,0},... | collective-permute-start | bytes 245768 | tf_op jit(solution)/shard_map/ppermute | solution.py:26
  11.8 0.7 %collective-permute-done.1 = bf16[32,512]{1,0:T(8,128)(2,1)S(1)} collective-permute-done((bf16[32,512]{1,0:T(8,128)(2,1)S(1)}, bf16[32,512]{1,0:T(8,128)(2,1)S(1)}, u32[]{:S(2)}, u32[]{:S(2)}) %collective-permute-start.1) | collective-permute-done | bytes 32800 | tf_op jit(solution)/shard_map/ppermute | solution.py:26
  12.5 1.6 %collective-permute-start.2 = (bf16[64,512]{1,0:T(8,128)(2,1)S(1)}, bf16[64,512]{1,0:T(8,128)(2,1)S(1)}, u32[]{:S(2)}, u32[]{:S(2)}) collective-permute-start(bf16[64,512]{1,0:T(8,128)(2,1)S(1)} %pad_maximum_fusion.5), channel_id=1, source_target_pairs={{0,4},{2,6},{4,0},{6,2},{8,12},{10,14},{12,8},{14,10},{16,20},{18,... | collective-permute-start | bytes 196616 | tf_op jit(solution)/shard_map/ppermute | solution.py:26
  14.0 1.7 %slice_bitcast_fusion.2 = (bf16[64,8192]{1,0:T(8,128)(2,1)S(1)}, bf16[64,8192]{1,0:T(8,128)(2,1)S(1)}) fusion(bf16[2,64,8192]{2,1,0:T(8,128)(2,1)} %param.13, bf16[2,64,8192]{2,1,0:T(8,128)(2,1)} %param.12), kind=kLoop, calls=%fused_computation.2 | loop fusion | bytes 4194304 | tf_op jit(solution)/shard_map/squeeze | solution.py:123
  15.7 1.1 %collective-permute-done.2 = bf16[64,512]{1,0:T(8,128)(2,1)S(1)} collective-permute-done((bf16[64,512]{1,0:T(8,128)(2,1)S(1)}, bf16[64,512]{1,0:T(8,128)(2,1)S(1)}, u32[]{:S(2)}, u32[]{:S(2)}) %collective-permute-start.2) | collective-permute-done | bytes 65568 | tf_op jit(solution)/shard_map/ppermute | solution.py:26
  16.9 0.9 %collective-permute-start.4 = (bf16[128,512]{1,0:T(8,128)(2,1)S(1)}, bf16[128,512]{1,0:T(8,128)(2,1)S(1)}, u32[]{:S(2)}, u32[]{:S(2)}) collective-permute-start(bf16[128,512]{1,0:T(8,128)(2,1)S(1)} %pad_maximum_fusion.2.w0_ref), channel_id=1, source_target_pairs={{0,1},{1,0},{2,3},{3,2},{4,5},{5,4},{6,7},{7,6},{8,9},{9,8},{10,11... | collective-permute-start | bytes 393224 | tf_op jit(solution)/shard_map/ppermute | solution.py:26
  18.2 1.5 %collective-permute-start.12 = (bf16[32,1024]{1,0:T(8,128)(2,1)S(1)}, bf16[32,1024]{1,0:T(8,128)(2,1)S(1)}, u32[]{:S(2)}, u32[]{:S(2)}) collective-permute-start(bf16[32,1024]{1,0:T(8,128)(2,1)S(1)} %slice.107), channel_id=1, source_target_pairs={{0,8},{2,10},{4,12},{6,14},{8,0},{10,2},{12,4},{14,6},{16,24},{18,... | collective-permute-start | bytes 196616 | tf_op jit(solution)/shard_map/ppermute | solution.py:26
  19.8 1.3 %shard_map.94 = (bf16[16,8192]{1,0:T(8,128)(2,1)S(1)}, f32[16,8192]{1,0:T(8,128)S(1)}, bf16[16,8192]{1,0:T(8,128)(2,1)S(1)}) custom-call(bf16[256,256]{1,0:T(8,128)(2,1)S(1)} %get-tuple-element.68.place_ref, bf16[128,512]{1,0:T(8,128)(2,1)S(1)} %pad_maximum_fusion.2.w0_ref, bf16[128,512]{1,0:T(8,128)(2,1)S(1)} %collective-permute-done.3.w1_ref, ...), custom_call_target="tpu_custom_call" | custom-call | flops 1 | bytes 1 | tf_op jit(solution)/shard_map/pallas_call | solution.py:127
  21.0 1.3 %collective-permute-start.11 = (bf16[16,8192]{1,0:T(8,128)(2,1)S(1)}, bf16[16,8192]{1,0:T(8,128)(2,1)S(1)}, u32[]{:S(2)}, u32[]{:S(2)}) collective-permute-start(bf16[16,8192]{1,0:T(8,128)(2,1)S(1)} %get-tuple-element.40), channel_id=1, source_target_pairs={{0,1},{1,0},{2,3},{3,2},{4,5},{5,4},{6,7},{7,6},{8,9},{9,8},{10,11... | collective-permute-start | bytes 786440 | tf_op jit(solution)/shard_map/ppermute | solution.py:26
  22.3 0.4 collective-permute-start.9
  22.9 1.6 %collective-permute-start.13 = (bf16[64,1024]{1,0:T(8,128)(2,1)S(1)}, bf16[64,1024]{1,0:T(8,128)(2,1)S(1)}, u32[]{:S(2)}, u32[]{:S(2)}) collective-permute-start(bf16[64,1024]{1,0:T(8,128)(2,1)S(1)} %pad_maximum_fusion.3), channel_id=1, source_target_pairs={{0,4},{2,6},{4,0},{6,2},{8,12},{10,14},{12,8},{14,10},{16,20},{18,... | collective-permute-start | bytes 393224 | tf_op jit(solution)/shard_map/ppermute | solution.py:26
  24.4 1.3 %shard_map.95 = (bf16[16,8192]{1,0:T(8,128)(2,1)S(1)}, f32[16,8192]{1,0:T(8,128)S(1)}, bf16[16,8192]{1,0:T(8,128)(2,1)S(1)}) custom-call(bf16[256,256]{1,0:T(8,128)(2,1)S(1)} %get-tuple-element.68.place_ref, bf16[128,512]{1,0:T(8,128)(2,1)S(1)} %collective-permute-done.4.w0_ref, bf16[128,512]{1,0:T(8,128)(2,1)S(1)} %collective-permute-done.5.w1_ref, ...), custom_call_target="tpu_custom_call" | custom-call | flops 1 | bytes 1 | tf_op jit(solution)/shard_map/pallas_call | solution.py:127
  25.7 0.9 %collective-permute-start.6 = (bf16[16,8192]{1,0:T(8,128)(2,1)S(1)}, bf16[16,8192]{1,0:T(8,128)(2,1)S(1)}, u32[]{:S(2)}, u32[]{:S(2)}) collective-permute-start(bf16[16,8192]{1,0:T(8,128)(2,1)S(1)} %get-tuple-element.35), channel_id=1, source_target_pairs={{0,1},{1,0},{2,3},{3,2},{4,5},{5,4},{6,7},{7,6},{8,9},{9,8},{10,11... | collective-permute-start | bytes 786440 | tf_op jit(solution)/shard_map/ppermute | solution.py:26
  26.6 0.3 collective-permute-done.9
  27.0 1.6 %collective-permute-start.10 = (bf16[64,1536]{1,0:T(8,128)(2,1)S(1)}, bf16[64,1536]{1,0:T(8,128)(2,1)S(1)}, u32[]{:S(2)}, u32[]{:S(2)}) collective-permute-start(bf16[64,1536]{1,0:T(8,128)(2,1)S(1)} %pad_maximum_fusion.1), channel_id=1, source_target_pairs={{0,4},{2,6},{4,0},{6,2},{8,12},{10,14},{12,8},{14,10},{16,20},{18,... | collective-permute-start | bytes 589832 | tf_op jit(solution)/shard_map/ppermute | solution.py:26
  28.5 0.3 collective-permute-done.13
  29.0 0.5 collective-permute-start.15
  29.7 0.7 %collective-permute-done.14.refs_2_ = bf16[128,512]{1,0:T(8,128)(2,1)S(1)} collective-permute-done((bf16[128,512]{1,0:T(8,128)(2,1)S(1)}, bf16[128,512]{1,0:T(8,128)(2,1)S(1)}, u32[]{:S(2)}, u32[]{:S(2)}) %collective-permute-start.14) | collective-permute-done | bytes 131104 | tf_op jit(solution)/shard_map/ppermute | solution.py:26
  30.3 0.2 collective-permute-done.15.refs_3_
  30.5 0.5 shard_map.96
  31.1 1.3 %shard_map.97 = (bf16[128,512]{1,0:T(8,128)(2,1)S(1)}, bf16[128,512]{1,0:T(8,128)(2,1)S(1)}) custom-call(bf16[256,256]{1,0:T(8,128)(2,1)S(1)} %get-tuple-element.69.back_ref, f32[16,8192]{1,0:T(8,128)S(1)} %get-tuple-element.43.part_ref, bf16[16,8192]{1,0:T(8,128)(2,1)S(1)} %collective-permute-done.11.got_ref, ...), custom_call_target="tpu_custom_call" | custom-call | flops 1 | bytes 1 | tf_op jit(solution)/shard_map/pallas_call | solution.py:127
  32.3 1.1 %collective-permute-done.10 = bf16[64,1536]{1,0:T(8,128)(2,1)S(1)} collective-permute-done((bf16[64,1536]{1,0:T(8,128)(2,1)S(1)}, bf16[64,1536]{1,0:T(8,128)(2,1)S(1)}, u32[]{:S(2)}, u32[]{:S(2)}) %collective-permute-start.10) | collective-permute-done | bytes 196640 | tf_op jit(solution)/shard_map/ppermute | solution.py:26
  33.6 0.5 collective-permute-start.17
  34.2 0.4 collective-permute-start.23
  34.6 0.3 collective-permute-done.16.refs_3_
  35.1 0.3 collective-permute-done.18.refs_5_
  35.5 0.6 shard_map.98
  36.0 1.8 %shard_map.99 = (bf16[128,1024]{1,0:T(8,128)(2,1)S(1)}, bf16[128,1024]{1,0:T(8,128)(2,1)S(1)}, bf16[16,8192]{1,0:T(8,128)(2,1)}) custom-call(bf16[256,256]{1,0:T(8,128)(2,1)S(1)} %get-tuple-element.69.back_ref, f32[16,8192]{1,0:T(8,128)S(1)} %get-tuple-element.34.part_ref, bf16[16,8192]{1,0:T(8,128)(2,1)S(1)} %collective-permute-done.6.got_ref, ...), custom_call_target="tpu_custom_call" | custom-call | flops 1 | bytes 1 | tf_op jit(solution)/shard_map/pallas_call | solution.py:127
  37.9 0.2 collective-permute-start.19
  38.1 1.2 %collective-permute-start.24 = (bf16[64,512]{1,0:T(8,128)(2,1)S(1)}, bf16[64,512]{1,0:T(8,128)(2,1)S(1)}, u32[]{:S(2)}, u32[]{:S(2)}) collective-permute-start(bf16[64,512]{1,0:T(8,128)(2,1)S(1)} %slice.161), channel_id=1, source_target_pairs={{0,4},{2,6},{4,0},{6,2},{8,12},{10,14},{12,8},{14,10},{16,20},{18,... | collective-permute-start | bytes 196616 | tf_op jit(solution)/shard_map/ppermute | solution.py:26
  39.5 1.2 %collective-permute-start.20 = (bf16[64,1024]{1,0:T(8,128)(2,1)S(1)}, bf16[64,1024]{1,0:T(8,128)(2,1)S(1)}, u32[]{:S(2)}, u32[]{:S(2)}) collective-permute-start(bf16[64,1024]{1,0:T(8,128)(2,1)S(1)} %slice.160), channel_id=1, source_target_pairs={{0,4},{2,6},{4,0},{6,2},{8,12},{10,14},{12,8},{14,10},{16,20},{18,... | collective-permute-start | bytes 393224 | tf_op jit(solution)/shard_map/ppermute | solution.py:26
  40.7 2.0 %collective-permute-done.24 = bf16[64,512]{1,0:T(8,128)(2,1)S(1)} collective-permute-done((bf16[64,512]{1,0:T(8,128)(2,1)S(1)}, bf16[64,512]{1,0:T(8,128)(2,1)S(1)}, u32[]{:S(2)}, u32[]{:S(2)}) %collective-permute-start.24) | collective-permute-done | bytes 65568 | tf_op jit(solution)/shard_map/ppermute | solution.py:26
  42.8 1.5 %collective-permute-start.25 = (bf16[32,512]{1,0:T(8,128)(2,1)S(1)}, bf16[32,512]{1,0:T(8,128)(2,1)S(1)}, u32[]{:S(2)}, u32[]{:S(2)}) collective-permute-start(bf16[32,512]{1,0:T(8,128)(2,1)S(1)} %slice.163), channel_id=1, source_target_pairs={{0,8},{2,10},{4,12},{6,14},{8,0},{10,2},{12,4},{14,6},{16,24},{18,... | collective-permute-start | bytes 98312 | tf_op jit(solution)/shard_map/ppermute | solution.py:26
  44.2 1.1 %collective-permute-done.20 = bf16[64,1024]{1,0:T(8,128)(2,1)S(1)} collective-permute-done((bf16[64,1024]{1,0:T(8,128)(2,1)S(1)}, bf16[64,1024]{1,0:T(8,128)(2,1)S(1)}, u32[]{:S(2)}, u32[]{:S(2)}) %collective-permute-start.20) | collective-permute-done | bytes 131104 | tf_op jit(solution)/shard_map/ppermute | solution.py:26
  45.4 1.5 %collective-permute-start.21 = (bf16[32,1024]{1,0:T(8,128)(2,1)S(1)}, bf16[32,1024]{1,0:T(8,128)(2,1)S(1)}, u32[]{:S(2)}, u32[]{:S(2)}) collective-permute-start(bf16[32,1024]{1,0:T(8,128)(2,1)S(1)} %slice.162), channel_id=1, source_target_pairs={{0,8},{2,10},{4,12},{6,14},{8,0},{10,2},{12,4},{14,6},{16,24},{18,... | collective-permute-start | bytes 196616 | tf_op jit(solution)/shard_map/ppermute | solution.py:26
  46.9 3.1 %collective-permute-start.26 = (bf16[16,512]{1,0:T(8,128)(2,1)S(1)}, bf16[16,512]{1,0:T(8,128)(2,1)S(1)}, u32[]{:S(2)}, u32[]{:S(2)}) collective-permute-start(bf16[16,512]{1,0:T(8,128)(2,1)S(1)} %slice.165), channel_id=1, source_target_pairs={{0,16},{2,18},{4,20},{6,22},{8,24},{10,26},{12,28},{14,30},{16,0},... | collective-permute-start | bytes 49160 | tf_op jit(solution)/shard_map/ppermute | solution.py:26
  50.1 2.2 %collective-permute-start.22 = (bf16[16,1024]{1,0:T(8,128)(2,1)S(1)}, bf16[16,1024]{1,0:T(8,128)(2,1)S(1)}, u32[]{:S(2)}, u32[]{:S(2)}) collective-permute-start(bf16[16,1024]{1,0:T(8,128)(2,1)S(1)} %slice.164), channel_id=1, source_target_pairs={{0,16},{2,18},{4,20},{6,22},{8,24},{10,26},{12,28},{14,30},{16,0},... | collective-permute-start | bytes 98312 | tf_op jit(solution)/shard_map/ppermute | solution.py:26
  52.3 1.0 %collective-permute-start.27 = (bf16[16,512]{1,0:T(8,128)(2,1)S(1)}, bf16[16,512]{1,0:T(8,128)(2,1)S(1)}, u32[]{:S(2)}, u32[]{:S(2)}) collective-permute-start(bf16[16,512]{1,0:T(8,128)(2,1)S(1)} %fusion.3), channel_id=1, source_target_pairs={{0,1},{1,0},{2,3},{3,2},{4,5},{5,4},{6,7},{7,6},{8,9},{9,8},{10,11... | collective-permute-start | bytes 49160 | tf_op jit(solution)/shard_map/ppermute | solution.py:26
  53.3 1.7 %collective-permute-done.22 = bf16[16,1024]{1,0:T(8,128)(2,1)S(1)} collective-permute-done((bf16[16,1024]{1,0:T(8,128)(2,1)S(1)}, bf16[16,1024]{1,0:T(8,128)(2,1)S(1)}, u32[]{:S(2)}, u32[]{:S(2)}) %collective-permute-start.22) | collective-permute-done | bytes 32800 | tf_op jit(solution)/shard_map/ppermute | solution.py:26
  55.0 1.1 %collective-permute-done.27 = bf16[16,512]{1,0:T(8,128)(2,1)S(1)} collective-permute-done((bf16[16,512]{1,0:T(8,128)(2,1)S(1)}, bf16[16,512]{1,0:T(8,128)(2,1)S(1)}, u32[]{:S(2)}, u32[]{:S(2)}) %collective-permute-start.27) | collective-permute-done | bytes 16416 | tf_op jit(solution)/shard_map/ppermute | solution.py:26
  56.1 0.6 %fusion.12 = (f32[1,16,512]{2,1,0:T(8,128)}, f32[1,16,512]{2,1,0:T(8,128)}) fusion(bf16[16,512]{1,0:T(8,128)(2,1)S(1)} %collective-permute-done.27, f32[16,1024]{1,0:T(8,128)S(1)} %slice_add_fusion.4, f32[1,16,512]{2,1,0:T(8,128)S(1)} %copy-done.4, f32[1,16,512]{2,1,0:T(8,128)S(1)} %copy-done.3), kind=kLoop, calls=%fused_computation.59 | loop fusion | flops 90112 | bytes 212992 | tf_op jit(solution)/shard_map/broadcast_in_dim | solution.py:247
  (69 shorter events, 1.5 us)
Async XLA Ops:
  1.4 7.2 %collective-permute-start = (bf16[16,512]{1,0:T(8,128)(2,1)S(1)}, bf16[16,512]{1,0:T(8,128)(2,1)S(1)}, u32[]{:S(2)}, u32[]{:S(2)}) collective-permute-start(bf16[16,512]{1,0:T(8,128)(2,1)S(1)} %bitcast_convert_fusion), channel_id=1, source_target_pairs={{0,16},{2,18},{4,20},{6,22},{8,24},{10,26},{12,28},{14,30},{16,0},... | collective-permute-start | bytes 49160 | tf_op jit(solution)/shard_map/ppermute | solution.py:26
  7.0 3.9 %collective-permute-start.7 = (bf16[16,1024]{1,0:T(8,128)(2,1)S(1)}, bf16[16,1024]{1,0:T(8,128)(2,1)S(1)}, u32[]{:S(2)}, u32[]{:S(2)}) collective-permute-start(bf16[16,1024]{1,0:T(8,128)(2,1)S(1)} %pad_maximum_fusion.7), channel_id=1, source_target_pairs={{0,1},{1,0},{2,3},{3,2},{4,5},{5,4},{6,7},{7,6},{8,9},{9,8},{10,11... | collective-permute-start | bytes 98312 | tf_op jit(solution)/shard_map/ppermute | solution.py:26
  8.6 3.9 %collective-permute-start.1 = (bf16[32,512]{1,0:T(8,128)(2,1)S(1)}, bf16[32,512]{1,0:T(8,128)(2,1)S(1)}, u32[]{:S(2)}, u32[]{:S(2)}) collective-permute-start(bf16[32,512]{1,0:T(8,128)(2,1)S(1)} %pad_maximum_fusion.6), channel_id=1, source_target_pairs={{0,8},{2,10},{4,12},{6,14},{8,0},{10,2},{12,4},{14,6},{16,24},{18,... | collective-permute-start | bytes 98312 | tf_op jit(solution)/shard_map/ppermute | solution.py:26
  11.0 6.9 %collective-permute-start.8 = (bf16[16,2560]{1,0:T(8,128)(2,1)S(1)}, bf16[16,2560]{1,0:T(8,128)(2,1)S(1)}, u32[]{:S(2)}, u32[]{:S(2)}) collective-permute-start(bf16[16,2560]{1,0:T(8,128)(2,1)S(1)} %pad_maximum_fusion.4), channel_id=1, source_target_pairs={{0,16},{2,18},{4,20},{6,22},{8,24},{10,26},{12,28},{14,30},{16,0},... | collective-permute-start | bytes 245768 | tf_op jit(solution)/shard_map/ppermute | solution.py:26
  12.5 5.4 %copy-start.5 = (s32[256]{0:T(256)S(1)}, s32[256]{0:T(256)}, u32[]{:S(2)}) copy-start(s32[256]{0:T(256)} %param.10) | copy-start | bytes 3076
  12.5 4.3 %collective-permute-start.2 = (bf16[64,512]{1,0:T(8,128)(2,1)S(1)}, bf16[64,512]{1,0:T(8,128)(2,1)S(1)}, u32[]{:S(2)}, u32[]{:S(2)}) collective-permute-start(bf16[64,512]{1,0:T(8,128)(2,1)S(1)} %pad_maximum_fusion.5), channel_id=1, source_target_pairs={{0,4},{2,6},{4,0},{6,2},{8,12},{10,14},{12,8},{14,10},{16,20},{18,... | collective-permute-start | bytes 196616 | tf_op jit(solution)/shard_map/ppermute | solution.py:26
  16.8 2.9 %collective-permute-start.3 = (bf16[128,512]{1,0:T(8,128)(2,1)S(1)}, bf16[128,512]{1,0:T(8,128)(2,1)S(1)}, u32[]{:S(2)}, u32[]{:S(2)}) collective-permute-start(bf16[128,512]{1,0:T(8,128)(2,1)S(1)} %pad_maximum_fusion.2.w0_ref), channel_id=1, source_target_pairs={{0,2},{2,0},{4,6},{6,4},{8,10},{10,8},{12,14},{14,12},{16,18},{18,... | collective-permute-start | bytes 393224 | tf_op jit(solution)/shard_map/ppermute | solution.py:26
  16.9 5.9 %collective-permute-start.4 = (bf16[128,512]{1,0:T(8,128)(2,1)S(1)}, bf16[128,512]{1,0:T(8,128)(2,1)S(1)}, u32[]{:S(2)}, u32[]{:S(2)}) collective-permute-start(bf16[128,512]{1,0:T(8,128)(2,1)S(1)} %pad_maximum_fusion.2.w0_ref), channel_id=1, source_target_pairs={{0,1},{1,0},{2,3},{3,2},{4,5},{5,4},{6,7},{7,6},{8,9},{9,8},{10,11... | collective-permute-start | bytes 393224 | tf_op jit(solution)/shard_map/ppermute | solution.py:26
  18.2 4.7 %collective-permute-start.12 = (bf16[32,1024]{1,0:T(8,128)(2,1)S(1)}, bf16[32,1024]{1,0:T(8,128)(2,1)S(1)}, u32[]{:S(2)}, u32[]{:S(2)}) collective-permute-start(bf16[32,1024]{1,0:T(8,128)(2,1)S(1)} %slice.107), channel_id=1, source_target_pairs={{0,8},{2,10},{4,12},{6,14},{8,0},{10,2},{12,4},{14,6},{16,24},{18,... | collective-permute-start | bytes 196616 | tf_op jit(solution)/shard_map/ppermute | solution.py:26
  21.0 10.0 %collective-permute-start.11 = (bf16[16,8192]{1,0:T(8,128)(2,1)S(1)}, bf16[16,8192]{1,0:T(8,128)(2,1)S(1)}, u32[]{:S(2)}, u32[]{:S(2)}) collective-permute-start(bf16[16,8192]{1,0:T(8,128)(2,1)S(1)} %get-tuple-element.40), channel_id=1, source_target_pairs={{0,1},{1,0},{2,3},{3,2},{4,5},{5,4},{6,7},{7,6},{8,9},{9,8},{10,11... | collective-permute-start | bytes 786440 | tf_op jit(solution)/shard_map/ppermute | solution.py:26
  22.3 4.6 %collective-permute-start.9 = (bf16[32,1536]{1,0:T(8,128)(2,1)S(1)}, bf16[32,1536]{1,0:T(8,128)(2,1)S(1)}, u32[]{:S(2)}, u32[]{:S(2)}) collective-permute-start(bf16[32,1536]{1,0:T(8,128)(2,1)S(1)} %slice.106), channel_id=1, source_target_pairs={{0,8},{2,10},{4,12},{6,14},{8,0},{10,2},{12,4},{14,6},{16,24},{18,... | collective-permute-start | bytes 294920 | tf_op jit(solution)/shard_map/ppermute | solution.py:26
  22.8 1.6 %collective-permute-start.5 = (bf16[128,512]{1,0:T(8,128)(2,1)S(1)}, bf16[128,512]{1,0:T(8,128)(2,1)S(1)}, u32[]{:S(2)}, u32[]{:S(2)}) collective-permute-start(bf16[128,512]{1,0:T(8,128)(2,1)S(1)} %collective-permute-done.4.w0_ref), channel_id=1, source_target_pairs={{0,2},{2,0},{4,6},{6,4},{8,10},{10,8},{12,14},{14,12},{16,18},{18,... | collective-permute-start | bytes 393224 | tf_op jit(solution)/shard_map/ppermute | solution.py:26
  22.8 6.6 %copy-start.1 = (bf16[2,64,8192]{2,1,0:T(8,128)(2,1)S(1)}, bf16[2,64,8192]{2,1,0:T(8,128)(2,1)}, u32[]{:S(2)}) copy-start(bf16[2,64,8192]{2,1,0:T(8,128)(2,1)} %param.13) | copy-start | bytes 6291460
  22.9 6.0 %collective-permute-start.13 = (bf16[64,1024]{1,0:T(8,128)(2,1)S(1)}, bf16[64,1024]{1,0:T(8,128)(2,1)S(1)}, u32[]{:S(2)}, u32[]{:S(2)}) collective-permute-start(bf16[64,1024]{1,0:T(8,128)(2,1)S(1)} %pad_maximum_fusion.3), channel_id=1, source_target_pairs={{0,4},{2,6},{4,0},{6,2},{8,12},{10,14},{12,8},{14,10},{16,20},{18,... | collective-permute-start | bytes 393224 | tf_op jit(solution)/shard_map/ppermute | solution.py:26
  25.7 3.8 %copy-start.2 = (bf16[2,64,8192]{2,1,0:T(8,128)(2,1)S(1)}, bf16[2,64,8192]{2,1,0:T(8,128)(2,1)}, u32[]{:S(2)}) copy-start(bf16[2,64,8192]{2,1,0:T(8,128)(2,1)} %param.12) | copy-start | bytes 6291460
  25.7 10.3 %collective-permute-start.6 = (bf16[16,8192]{1,0:T(8,128)(2,1)S(1)}, bf16[16,8192]{1,0:T(8,128)(2,1)S(1)}, u32[]{:S(2)}, u32[]{:S(2)}) collective-permute-start(bf16[16,8192]{1,0:T(8,128)(2,1)S(1)} %get-tuple-element.35), channel_id=1, source_target_pairs={{0,1},{1,0},{2,3},{3,2},{4,5},{5,4},{6,7},{7,6},{8,9},{9,8},{10,11... | collective-permute-start | bytes 786440 | tf_op jit(solution)/shard_map/ppermute | solution.py:26
  27.0 6.5 %collective-permute-start.10 = (bf16[64,1536]{1,0:T(8,128)(2,1)S(1)}, bf16[64,1536]{1,0:T(8,128)(2,1)S(1)}, u32[]{:S(2)}, u32[]{:S(2)}) collective-permute-start(bf16[64,1536]{1,0:T(8,128)(2,1)S(1)} %pad_maximum_fusion.1), channel_id=1, source_target_pairs={{0,4},{2,6},{4,0},{6,2},{8,12},{10,14},{12,8},{14,10},{16,20},{18,... | collective-permute-start | bytes 589832 | tf_op jit(solution)/shard_map/ppermute | solution.py:26
  28.9 1.4 %collective-permute-start.14 = (bf16[128,512]{1,0:T(8,128)(2,1)S(1)}, bf16[128,512]{1,0:T(8,128)(2,1)S(1)}, u32[]{:S(2)}, u32[]{:S(2)}) collective-permute-start(bf16[128,512]{1,0:T(8,128)(2,1)S(1)} %get-tuple-element.63.refs_0_), channel_id=1, source_target_pairs={{0,2},{2,0},{4,6},{6,4},{8,10},{10,8},{12,14},{14,12},{16,18},{18,... | collective-permute-start | bytes 393224 | tf_op jit(solution)/shard_map/ppermute | solution.py:26
  29.0 1.5 %collective-permute-start.15 = (bf16[128,512]{1,0:T(8,128)(2,1)S(1)}, bf16[128,512]{1,0:T(8,128)(2,1)S(1)}, u32[]{:S(2)}, u32[]{:S(2)}) collective-permute-start(bf16[128,512]{1,0:T(8,128)(2,1)S(1)} %get-tuple-element.62.refs_1_), channel_id=1, source_target_pairs={{0,2},{2,0},{4,6},{6,4},{8,10},{10,8},{12,14},{14,12},{16,18},{18,... | collective-permute-start | bytes 393224 | tf_op jit(solution)/shard_map/ppermute | solution.py:26
  32.3 3.7 %copy-start = (bf16[1,2,8,8192]{3,2,1,0:T(8,128)(2,1)S(1)}, bf16[1,2,8,8192]{3,2,1,0:T(8,128)(2,1)}, u32[]{:S(2)}) copy-start(bf16[1,2,8,8192]{3,2,1,0:T(8,128)(2,1)} %param.11) | copy-start | bytes 786436
  33.5 1.4 %collective-permute-start.16 = (bf16[128,512]{1,0:T(8,128)(2,1)S(1)}, bf16[128,512]{1,0:T(8,128)(2,1)S(1)}, u32[]{:S(2)}, u32[]{:S(2)}) collective-permute-start(bf16[128,512]{1,0:T(8,128)(2,1)S(1)} %get-tuple-element.61.refs_0_), channel_id=1, source_target_pairs={{0,2},{2,0},{4,6},{6,4},{8,10},{10,8},{12,14},{14,12},{16,18},{18,... | collective-permute-start | bytes 393224 | tf_op jit(solution)/shard_map/ppermute | solution.py:26
  33.6 1.5 %collective-permute-start.17 = (bf16[128,512]{1,0:T(8,128)(2,1)S(1)}, bf16[128,512]{1,0:T(8,128)(2,1)S(1)}, u32[]{:S(2)}, u32[]{:S(2)}) collective-permute-start(bf16[128,512]{1,0:T(8,128)(2,1)S(1)} %get-tuple-element.60.refs_1_), channel_id=1, source_target_pairs={{0,2},{2,0},{4,6},{6,4},{8,10},{10,8},{12,14},{14,12},{16,18},{18,... | collective-permute-start | bytes 393224 | tf_op jit(solution)/shard_map/ppermute | solution.py:26
  34.1 1.3 %collective-permute-start.18 = (bf16[128,512]{1,0:T(8,128)(2,1)S(1)}, bf16[128,512]{1,0:T(8,128)(2,1)S(1)}, u32[]{:S(2)}, u32[]{:S(2)}) collective-permute-start(bf16[128,512]{1,0:T(8,128)(2,1)S(1)} %get-tuple-element.59.refs_2_), channel_id=1, source_target_pairs={{0,2},{2,0},{4,6},{6,4},{8,10},{10,8},{12,14},{14,12},{16,18},{18,... | collective-permute-start | bytes 393224 | tf_op jit(solution)/shard_map/ppermute | solution.py:26
  34.2 3.9 %collective-permute-start.23 = (bf16[128,512]{1,0:T(8,128)(2,1)S(1)}, bf16[128,512]{1,0:T(8,128)(2,1)S(1)}, u32[]{:S(2)}, u32[]{:S(2)}) collective-permute-start(bf16[128,512]{1,0:T(8,128)(2,1)S(1)} %get-tuple-element.57), channel_id=1, source_target_pairs={{0,2},{2,0},{4,6},{6,4},{8,10},{10,8},{12,14},{14,12},{16,18},{18,... | collective-permute-start | bytes 393224 | tf_op jit(solution)/shard_map/ppermute | solution.py:26
  37.9 18.3 %copy-start.3 = (f32[1,16,512]{2,1,0:T(8,128)S(1)}, f32[1,16,512]{2,1,0:T(8,128)}, u32[]{:S(2)}) copy-start(f32[1,16,512]{2,1,0:T(8,128)} %param.7) | copy-start | bytes 98308
  37.9 18.3 %copy-start.4 = (f32[1,16,512]{2,1,0:T(8,128)S(1)}, f32[1,16,512]{2,1,0:T(8,128)}, u32[]{:S(2)}) copy-start(f32[1,16,512]{2,1,0:T(8,128)} %param.9) | copy-start | bytes 98308
  37.9 1.5 %collective-permute-start.19 = (bf16[128,1024]{1,0:T(8,128)(2,1)S(1)}, bf16[128,1024]{1,0:T(8,128)(2,1)S(1)}, u32[]{:S(2)}, u32[]{:S(2)}) collective-permute-start(bf16[128,1024]{1,0:T(8,128)(2,1)S(1)} %get-tuple-element.56), channel_id=1, source_target_pairs={{0,2},{2,0},{4,6},{6,4},{8,10},{10,8},{12,14},{14,12},{16,18},{18,... | collective-permute-start | bytes 786440 | tf_op jit(solution)/shard_map/ppermute | solution.py:26
  38.1 4.6 %collective-permute-start.24 = (bf16[64,512]{1,0:T(8,128)(2,1)S(1)}, bf16[64,512]{1,0:T(8,128)(2,1)S(1)}, u32[]{:S(2)}, u32[]{:S(2)}) collective-permute-start(bf16[64,512]{1,0:T(8,128)(2,1)S(1)} %slice.161), channel_id=1, source_target_pairs={{0,4},{2,6},{4,0},{6,2},{8,12},{10,14},{12,8},{14,10},{16,20},{18,... | collective-permute-start | bytes 196616 | tf_op jit(solution)/shard_map/ppermute | solution.py:26
  39.5 5.8 %collective-permute-start.20 = (bf16[64,1024]{1,0:T(8,128)(2,1)S(1)}, bf16[64,1024]{1,0:T(8,128)(2,1)S(1)}, u32[]{:S(2)}, u32[]{:S(2)}) collective-permute-start(bf16[64,1024]{1,0:T(8,128)(2,1)S(1)} %slice.160), channel_id=1, source_target_pairs={{0,4},{2,6},{4,0},{6,2},{8,12},{10,14},{12,8},{14,10},{16,20},{18,... | collective-permute-start | bytes 393224 | tf_op jit(solution)/shard_map/ppermute | solution.py:26
  42.8 4.2 %collective-permute-start.25 = (bf16[32,512]{1,0:T(8,128)(2,1)S(1)}, bf16[32,512]{1,0:T(8,128)(2,1)S(1)}, u32[]{:S(2)}, u32[]{:S(2)}) collective-permute-start(bf16[32,512]{1,0:T(8,128)(2,1)S(1)} %slice.163), channel_id=1, source_target_pairs={{0,8},{2,10},{4,12},{6,14},{8,0},{10,2},{12,4},{14,6},{16,24},{18,... | collective-permute-start | bytes 98312 | tf_op jit(solution)/shard_map/ppermute | solution.py:26
  45.4 4.7 %collective-permute-start.21 = (bf16[32,1024]{1,0:T(8,128)(2,1)S(1)}, bf16[32,1024]{1,0:T(8,128)(2,1)S(1)}, u32[]{:S(2)}, u32[]{:S(2)}) collective-permute-start(bf16[32,1024]{1,0:T(8,128)(2,1)S(1)} %slice.162), channel_id=1, source_target_pairs={{0,8},{2,10},{4,12},{6,14},{8,0},{10,2},{12,4},{14,6},{16,24},{18,... | collective-permute-start | bytes 196616 | tf_op jit(solution)/shard_map/ppermute | solution.py:26
  46.9 5.4 %collective-permute-start.26 = (bf16[16,512]{1,0:T(8,128)(2,1)S(1)}, bf16[16,512]{1,0:T(8,128)(2,1)S(1)}, u32[]{:S(2)}, u32[]{:S(2)}) collective-permute-start(bf16[16,512]{1,0:T(8,128)(2,1)S(1)} %slice.165), channel_id=1, source_target_pairs={{0,16},{2,18},{4,20},{6,22},{8,24},{10,26},{12,28},{14,30},{16,0},... | collective-permute-start | bytes 49160 | tf_op jit(solution)/shard_map/ppermute | solution.py:26
  50.1 4.9 %collective-permute-start.22 = (bf16[16,1024]{1,0:T(8,128)(2,1)S(1)}, bf16[16,1024]{1,0:T(8,128)(2,1)S(1)}, u32[]{:S(2)}, u32[]{:S(2)}) collective-permute-start(bf16[16,1024]{1,0:T(8,128)(2,1)S(1)} %slice.164), channel_id=1, source_target_pairs={{0,16},{2,18},{4,20},{6,22},{8,24},{10,26},{12,28},{14,30},{16,0},... | collective-permute-start | bytes 98312 | tf_op jit(solution)/shard_map/ppermute | solution.py:26
  52.3 3.8 %collective-permute-start.27 = (bf16[16,512]{1,0:T(8,128)(2,1)S(1)}, bf16[16,512]{1,0:T(8,128)(2,1)S(1)}, u32[]{:S(2)}, u32[]{:S(2)}) collective-permute-start(bf16[16,512]{1,0:T(8,128)(2,1)S(1)} %fusion.3), channel_id=1, source_target_pairs={{0,1},{1,0},{2,3},{3,2},{4,5},{5,4},{6,7},{7,6},{8,9},{9,8},{10,11... | collective-permute-start | bytes 49160 | tf_op jit(solution)/shard_map/ppermute | solution.py:26

commit v11 on v10

--- a/solution.py
+++ b/solution.py
@@ -230,15 +230,18 @@
         sums[k] = result[0].astype(F32) + swap(result[1], "dp", 1).astype(F32)
     error = result[2]
 
-    for mask in far[::-1]:
-        count = sums[0].shape[0] // 2
-        sums = [p[:count] + swap(p[count:].astype(BF), "dp", mask).astype(F32) for p in sums]
-    own_grad, own_packed = sums[0][:, :segment], sums[0][:, segment:]
-    grads = [own_grad] + sums[1:]
+    def halve(total, mask):
+        count = total.shape[0] // 2
+        return total[:count] + swap(total[count:].astype(BF), "dp", mask).astype(F32)
+
+    for mask in far[:0:-1]:
+        sums = [halve(p, mask) for p in sums]
+    grads = [sums[0][:, :segment]] + sums[1:]
     for mask in mp_bits:
         crossed = [swap(p.astype(BF), "mp", mask).astype(F32) for p in grads[mask:]]
         grads = [p + q for p, q in zip(grads, crossed)]
-    own_grad = grads[0]
+    both = halve(jnp.concatenate([grads[0], sums[0][:, segment:]], axis=1), far[0])
+    own_grad, own_packed = both[:, :segment], both[:, segment:]
     mean_grad = own_grad / n_dp
     mean_moment = own_packed / n_dp
     moment_new = beta_one * mean_moment + (1.0 - beta_one) * mean_grad

time: 57.1 us -> 60.8 us (1.065)
  waiting for transfers between devices: 12.1 us -> 21.2 us
  starting transfers between devices: 31.4 us -> 25.9 us
    ppermute x28 -> x27, waiting for transfers between devices: 12.1 us -> 21.2 us  [swap(): return lax.ppermute(x, axis, [(i, i ^ mask) for i in range(n)])]
    ppermute x28 -> x27, starting transfers between devices: 31.4 us -> 25.9 us  [swap(): return lax.ppermute(x, axis, [(i, i ^ mask) for i in range(n)])]
  transfers between devices with their start and end apart: 28 -> 27, of which waited for: 16 -> 16; matrix products, arithmetic and copies ran while one was open for 7% -> 7% of each run, Pallas kernels for 12% -> 11%
where the time goes in v11:
time: 60.8 us; the launch traced here: 60.4 us
  starting transfers between devices  25.9 us (43%)
  waiting for transfers between devices  21.2 us (35%)
  Pallas kernels  6.69 us (11%)
  other arithmetic  3.38 us (6%)
  local copies, waits for them, and re-layouts  2.23 us (4%)
  between operations  0.98 us (2%)
    ppermute x27, starting transfers between devices, swap(): return lax.ppermute(x, axis, [(i, i ^ mask) for i in range(n)])  25.9 us
    ppermute x27, waiting for transfers between devices, swap(): return lax.ppermute(x, axis, [(i, i ^ mask) for i in range(n)])  21.2 us
    pallas_call x6, Pallas kernels, call(): pl.pallas_call(kernel, out_shape=out_shape, in_specs=[pl.BlockSpec(memory...  6.69 us
    squeeze x3, local copies, waits for them, and re-layouts, tokens_of(): x[step]  1.81 us
  transfers between devices with their start and end apart: 27, of which 16 were waited for; matrix products, arithmetic and copies ran while one was open for 7% of the time, Pallas kernels for 11%

profile of v11, /device:TPU:0, one launch (start us, length us, event | category | flops | bytes accessed | tf_op | source)
XLA Modules:
  0.0 60.4 jit_solution(10133576296549335704)
XLA Ops:
  0.6 0.8 %bitcast_convert_fusion = bf16[16,512]{1,0:T(8,128)(2,1)S(1)} fusion(f32[1,16,512]{2,1,0:T(8,128)} %param.7), kind=kLoop, calls=%fused_computation.41 | loop fusion | flops 8192 | bytes 49152 | tf_op jit(solution)/shard_map/convert_element_type | solution.py:150
  1.4 4.0 %collective-permute-start = (bf16[16,512]{1,0:T(8,128)(2,1)S(1)}, bf16[16,512]{1,0:T(8,128)(2,1)S(1)}, u32[]{:S(2)}, u32[]{:S(2)}) collective-permute-start(bf16[16,512]{1,0:T(8,128)(2,1)S(1)} %bitcast_convert_fusion), channel_id=1, source_target_pairs={{0,16},{2,18},{4,20},{6,22},{8,24},{10,26},{12,28},{14,30},{16,0},... | collective-permute-start | bytes 49160 | tf_op jit(solution)/shard_map/ppermute | solution.py:26
  5.4 0.8 %fusion.6 = (bf16[16,512]{1,0:T(8,128)(2,1)S(1)}, bf16[16,512]{1,0:T(8,128)(2,1)S(1)}) fusion(f32[16,512]{1,0:T(8,128)} %bitcast.28), kind=kLoop, calls=%fused_computation.33 | loop fusion | flops 32768 | bytes 65536 | tf_op jit(solution)/shard_map/convert_element_type | solution.py:153
  6.3 0.8 %convert_bitcast_fusion = bf16[16,512]{1,0:T(8,128)(2,1)S(1)} fusion(f32[1,16,512]{2,1,0:T(8,128)} %param.9), kind=kLoop, calls=%fused_computation.42 | loop fusion | flops 8192 | bytes 49152 | tf_op jit(solution)/shard_map/convert.6
  7.0 1.5 %collective-permute-start.7 = (bf16[16,1024]{1,0:T(8,128)(2,1)S(1)}, bf16[16,1024]{1,0:T(8,128)(2,1)S(1)}, u32[]{:S(2)}, u32[]{:S(2)}) collective-permute-start(bf16[16,1024]{1,0:T(8,128)(2,1)S(1)} %pad_maximum_fusion.8), channel_id=1, source_target_pairs={{0,1},{1,0},{2,3},{3,2},{4,5},{5,4},{6,7},{7,6},{8,9},{9,8},{10,11... | collective-permute-start | bytes 98312 | tf_op jit(solution)/shard_map/ppermute | solution.py:26
  8.6 1.6 %collective-permute-start.1 = (bf16[32,512]{1,0:T(8,128)(2,1)S(1)}, bf16[32,512]{1,0:T(8,128)(2,1)S(1)}, u32[]{:S(2)}, u32[]{:S(2)}) collective-permute-start(bf16[32,512]{1,0:T(8,128)(2,1)S(1)} %pad_maximum_fusion.7), channel_id=1, source_target_pairs={{0,8},{2,10},{4,12},{6,14},{8,0},{10,2},{12,4},{14,6},{16,24},{18,... | collective-permute-start | bytes 98312 | tf_op jit(solution)/shard_map/ppermute | solution.py:26
  10.1 0.8 %collective-permute-done.7 = bf16[16,1024]{1,0:T(8,128)(2,1)S(1)} collective-permute-done((bf16[16,1024]{1,0:T(8,128)(2,1)S(1)}, bf16[16,1024]{1,0:T(8,128)(2,1)S(1)}, u32[]{:S(2)}, u32[]{:S(2)}) %collective-permute-start.7) | collective-permute-done | bytes 32800 | tf_op jit(solution)/shard_map/ppermute | solution.py:26
  11.0 0.8 %collective-permute-start.8 = (bf16[16,2560]{1,0:T(8,128)(2,1)S(1)}, bf16[16,2560]{1,0:T(8,128)(2,1)S(1)}, u32[]{:S(2)}, u32[]{:S(2)}) collective-permute-start(bf16[16,2560]{1,0:T(8,128)(2,1)S(1)} %pad_maximum_fusion.4), channel_id=1, source_target_pairs={{0,16},{2,18},{4,20},{6,22},{8,24},{10,26},{12,28},{14,30},{16,0},... | collective-permute-start | bytes 245768 | tf_op jit(solution)/shard_map/ppermute | solution.py:26
  11.8 0.7 %collective-permute-done.1 = bf16[32,512]{1,0:T(8,128)(2,1)S(1)} collective-permute-done((bf16[32,512]{1,0:T(8,128)(2,1)S(1)}, bf16[32,512]{1,0:T(8,128)(2,1)S(1)}, u32[]{:S(2)}, u32[]{:S(2)}) %collective-permute-start.1) | collective-permute-done | bytes 32800 | tf_op jit(solution)/shard_map/ppermute | solution.py:26
  12.5 1.6 %collective-permute-start.2 = (bf16[64,512]{1,0:T(8,128)(2,1)S(1)}, bf16[64,512]{1,0:T(8,128)(2,1)S(1)}, u32[]{:S(2)}, u32[]{:S(2)}) collective-permute-start(bf16[64,512]{1,0:T(8,128)(2,1)S(1)} %pad_maximum_fusion.6), channel_id=1, source_target_pairs={{0,4},{2,6},{4,0},{6,2},{8,12},{10,14},{12,8},{14,10},{16,20},{18,... | collective-permute-start | bytes 196616 | tf_op jit(solution)/shard_map/ppermute | solution.py:26
  14.0 1.7 %slice_bitcast_fusion.2 = (bf16[64,8192]{1,0:T(8,128)(2,1)S(1)}, bf16[64,8192]{1,0:T(8,128)(2,1)S(1)}) fusion(bf16[2,64,8192]{2,1,0:T(8,128)(2,1)} %param.13, bf16[2,64,8192]{2,1,0:T(8,128)(2,1)} %param.12), kind=kLoop, calls=%fused_computation.2 | loop fusion | bytes 4194304 | tf_op jit(solution)/shard_map/squeeze | solution.py:123
  15.7 1.1 %collective-permute-done.2 = bf16[64,512]{1,0:T(8,128)(2,1)S(1)} collective-permute-done((bf16[64,512]{1,0:T(8,128)(2,1)S(1)}, bf16[64,512]{1,0:T(8,128)(2,1)S(1)}, u32[]{:S(2)}, u32[]{:S(2)}) %collective-permute-start.2) | collective-permute-done | bytes 65568 | tf_op jit(solution)/shard_map/ppermute | solution.py:26
  16.9 0.9 %collective-permute-start.4 = (bf16[128,512]{1,0:T(8,128)(2,1)S(1)}, bf16[128,512]{1,0:T(8,128)(2,1)S(1)}, u32[]{:S(2)}, u32[]{:S(2)}) collective-permute-start(bf16[128,512]{1,0:T(8,128)(2,1)S(1)} %pad_maximum_fusion.2.w0_ref), channel_id=1, source_target_pairs={{0,1},{1,0},{2,3},{3,2},{4,5},{5,4},{6,7},{7,6},{8,9},{9,8},{10,11... | collective-permute-start | bytes 393224 | tf_op jit(solution)/shard_map/ppermute | solution.py:26
  18.1 1.5 %collective-permute-start.12 = (bf16[32,1024]{1,0:T(8,128)(2,1)S(1)}, bf16[32,1024]{1,0:T(8,128)(2,1)S(1)}, u32[]{:S(2)}, u32[]{:S(2)}) collective-permute-start(bf16[32,1024]{1,0:T(8,128)(2,1)S(1)} %slice.106), channel_id=1, source_target_pairs={{0,8},{2,10},{4,12},{6,14},{8,0},{10,2},{12,4},{14,6},{16,24},{18,... | collective-permute-start | bytes 196616 | tf_op jit(solution)/shard_map/ppermute | solution.py:26
  19.8 1.3 %shard_map.94 = (bf16[16,8192]{1,0:T(8,128)(2,1)S(1)}, f32[16,8192]{1,0:T(8,128)S(1)}, bf16[16,8192]{1,0:T(8,128)(2,1)S(1)}) custom-call(bf16[256,256]{1,0:T(8,128)(2,1)S(1)} %get-tuple-element.70.place_ref, bf16[128,512]{1,0:T(8,128)(2,1)S(1)} %pad_maximum_fusion.2.w0_ref, bf16[128,512]{1,0:T(8,128)(2,1)S(1)} %collective-permute-done.3.w1_ref, ...), custom_call_target="tpu_custom_call" | custom-call | flops 1 | bytes 1 | tf_op jit(solution)/shard_map/pallas_call | solution.py:127
  21.1 1.3 %collective-permute-start.11 = (bf16[16,8192]{1,0:T(8,128)(2,1)S(1)}, bf16[16,8192]{1,0:T(8,128)(2,1)S(1)}, u32[]{:S(2)}, u32[]{:S(2)}) collective-permute-start(bf16[16,8192]{1,0:T(8,128)(2,1)S(1)} %get-tuple-element.40), channel_id=1, source_target_pairs={{0,1},{1,0},{2,3},{3,2},{4,5},{5,4},{6,7},{7,6},{8,9},{9,8},{10,11... | collective-permute-start | bytes 786440 | tf_op jit(solution)/shard_map/ppermute | solution.py:26
  22.5 1.6 %collective-permute-start.13 = (bf16[64,1024]{1,0:T(8,128)(2,1)S(1)}, bf16[64,1024]{1,0:T(8,128)(2,1)S(1)}, u32[]{:S(2)}, u32[]{:S(2)}) collective-permute-start(bf16[64,1024]{1,0:T(8,128)(2,1)S(1)} %pad_maximum_fusion.3), channel_id=1, source_target_pairs={{0,4},{2,6},{4,0},{6,2},{8,12},{10,14},{12,8},{14,10},{16,20},{18,... | collective-permute-start | bytes 393224 | tf_op jit(solution)/shard_map/ppermute | solution.py:26
  24.0 1.5 %collective-permute-start.9 = (bf16[32,1536]{1,0:T(8,128)(2,1)S(1)}, bf16[32,1536]{1,0:T(8,128)(2,1)S(1)}, u32[]{:S(2)}, u32[]{:S(2)}) collective-permute-start(bf16[32,1536]{1,0:T(8,128)(2,1)S(1)} %slice.105), channel_id=1, source_target_pairs={{0,8},{2,10},{4,12},{6,14},{8,0},{10,2},{12,4},{14,6},{16,24},{18,... | collective-permute-start | bytes 294920 | tf_op jit(solution)/shard_map/ppermute | solution.py:26
  25.5 1.3 %collective-permute-done.5.w1_ref = bf16[128,512]{1,0:T(8,128)(2,1)S(1)} collective-permute-done((bf16[128,512]{1,0:T(8,128)(2,1)S(1)}, bf16[128,512]{1,0:T(8,128)(2,1)S(1)}, u32[]{:S(2)}, u32[]{:S(2)}) %collective-permute-start.5) | collective-permute-done | bytes 131104 | tf_op jit(solution)/shard_map/ppermute | solution.py:26
  26.9 1.3 %shard_map.95 = (bf16[16,8192]{1,0:T(8,128)(2,1)S(1)}, f32[16,8192]{1,0:T(8,128)S(1)}, bf16[16,8192]{1,0:T(8,128)(2,1)S(1)}) custom-call(bf16[256,256]{1,0:T(8,128)(2,1)S(1)} %get-tuple-element.70.place_ref, bf16[128,512]{1,0:T(8,128)(2,1)S(1)} %collective-permute-done.4.w0_ref, bf16[128,512]{1,0:T(8,128)(2,1)S(1)} %collective-permute-done.5.w1_ref, ...), custom_call_target="tpu_custom_call" | custom-call | flops 1 | bytes 1 | tf_op jit(solution)/shard_map/pallas_call | solution.py:127
  28.1 1.3 %collective-permute-start.6 = (bf16[16,8192]{1,0:T(8,128)(2,1)S(1)}, bf16[16,8192]{1,0:T(8,128)(2,1)S(1)}, u32[]{:S(2)}, u32[]{:S(2)}) collective-permute-start(bf16[16,8192]{1,0:T(8,128)(2,1)S(1)} %get-tuple-element.35), channel_id=1, source_target_pairs={{0,1},{1,0},{2,3},{3,2},{4,5},{5,4},{6,7},{7,6},{8,9},{9,8},{10,11... | collective-permute-start | bytes 786440 | tf_op jit(solution)/shard_map/ppermute | solution.py:26
  29.6 0.5 collective-permute-start.15
  30.3 0.6 collective-permute-start.10
  30.9 0.2 collective-permute-done.15.refs_3_
  31.1 0.5 shard_map.96
  31.7 1.3 %shard_map.97 = (bf16[128,512]{1,0:T(8,128)(2,1)S(1)}, bf16[128,512]{1,0:T(8,128)(2,1)S(1)}) custom-call(bf16[256,256]{1,0:T(8,128)(2,1)S(1)} %get-tuple-element.71.back_ref, f32[16,8192]{1,0:T(8,128)S(1)} %get-tuple-element.43.part_ref, bf16[16,8192]{1,0:T(8,128)(2,1)S(1)} %collective-permute-done.11.got_ref, ...), custom_call_target="tpu_custom_call" | custom-call | flops 1 | bytes 1 | tf_op jit(solution)/shard_map/pallas_call | solution.py:127
  33.0 4.3 %collective-permute-done.10 = bf16[64,1536]{1,0:T(8,128)(2,1)S(1)} collective-permute-done((bf16[64,1536]{1,0:T(8,128)(2,1)S(1)}, bf16[64,1536]{1,0:T(8,128)(2,1)S(1)}, u32[]{:S(2)}, u32[]{:S(2)}) %collective-permute-start.10) | collective-permute-done | bytes 196640 | tf_op jit(solution)/shard_map/ppermute | solution.py:26
  37.4 0.5 collective-permute-start.17
  38.0 0.4 collective-permute-start.22
  38.4 0.3 collective-permute-done.16.refs_3_
  38.9 0.3 collective-permute-done.18.refs_5_
  39.2 0.6 shard_map.98
  39.8 1.8 %shard_map.99 = (bf16[128,1024]{1,0:T(8,128)(2,1)S(1)}, bf16[128,1024]{1,0:T(8,128)(2,1)S(1)}, bf16[16,8192]{1,0:T(8,128)(2,1)}) custom-call(bf16[256,256]{1,0:T(8,128)(2,1)S(1)} %get-tuple-element.71.back_ref, f32[16,8192]{1,0:T(8,128)S(1)} %get-tuple-element.34.part_ref, bf16[16,8192]{1,0:T(8,128)(2,1)S(1)} %collective-permute-done.6.got_ref, ...), custom_call_target="tpu_custom_call" | custom-call | flops 1 | bytes 1 | tf_op jit(solution)/shard_map/pallas_call | solution.py:127
  41.6 0.2 collective-permute-start.19
  41.9 0.6 collective-permute-start.23
  42.5 0.7 %collective-permute-done.19 = bf16[128,1024]{1,0:T(8,128)(2,1)S(1)} collective-permute-done((bf16[128,1024]{1,0:T(8,128)(2,1)S(1)}, bf16[128,1024]{1,0:T(8,128)(2,1)S(1)}, u32[]{:S(2)}, u32[]{:S(2)}) %collective-permute-start.19) | collective-permute-done | bytes 262176 | tf_op jit(solution)/shard_map/ppermute | solution.py:26
  43.3 0.9 %collective-permute-start.20 = (bf16[64,1024]{1,0:T(8,128)(2,1)S(1)}, bf16[64,1024]{1,0:T(8,128)(2,1)S(1)}, u32[]{:S(2)}, u32[]{:S(2)}) collective-permute-start(bf16[64,1024]{1,0:T(8,128)(2,1)S(1)} %slice.162), channel_id=1, source_target_pairs={{0,4},{2,6},{4,0},{6,2},{8,12},{10,14},{12,8},{14,10},{16,20},{18,... | collective-permute-start | bytes 393224 | tf_op jit(solution)/shard_map/ppermute | solution.py:26
  44.1 2.3 %collective-permute-done.23 = bf16[64,512]{1,0:T(8,128)(2,1)S(1)} collective-permute-done((bf16[64,512]{1,0:T(8,128)(2,1)S(1)}, bf16[64,512]{1,0:T(8,128)(2,1)S(1)}, u32[]{:S(2)}, u32[]{:S(2)}) %collective-permute-start.23) | collective-permute-done | bytes 65568 | tf_op jit(solution)/shard_map/ppermute | solution.py:26
  46.5 0.5 collective-permute-start.24
  47.1 2.0 %collective-permute-done.20 = bf16[64,1024]{1,0:T(8,128)(2,1)S(1)} collective-permute-done((bf16[64,1024]{1,0:T(8,128)(2,1)S(1)}, bf16[64,1024]{1,0:T(8,128)(2,1)S(1)}, u32[]{:S(2)}, u32[]{:S(2)}) %collective-permute-start.20) | collective-permute-done | bytes 131104 | tf_op jit(solution)/shard_map/ppermute | solution.py:26
  49.1 0.5 collective-permute-start.21
  49.7 0.8 %collective-permute-done.24 = bf16[32,512]{1,0:T(8,128)(2,1)S(1)} collective-permute-done((bf16[32,512]{1,0:T(8,128)(2,1)S(1)}, bf16[32,512]{1,0:T(8,128)(2,1)S(1)}, u32[]{:S(2)}, u32[]{:S(2)}) %collective-permute-start.24) | collective-permute-done | bytes 32800 | tf_op jit(solution)/shard_map/ppermute | solution.py:26
  50.5 0.9 %collective-permute-start.25 = (bf16[32,512]{1,0:T(8,128)(2,1)S(1)}, bf16[32,512]{1,0:T(8,128)(2,1)S(1)}, u32[]{:S(2)}, u32[]{:S(2)}) collective-permute-start(bf16[32,512]{1,0:T(8,128)(2,1)S(1)} %fusion.5), channel_id=1, source_target_pairs={{0,1},{1,0},{2,3},{3,2},{4,5},{5,4},{6,7},{7,6},{8,9},{9,8},{10,11... | collective-permute-start | bytes 98312 | tf_op jit(solution)/shard_map/ppermute | solution.py:26
  51.5 2.0 %collective-permute-done.21 = bf16[32,1024]{1,0:T(8,128)(2,1)S(1)} collective-permute-done((bf16[32,1024]{1,0:T(8,128)(2,1)S(1)}, bf16[32,1024]{1,0:T(8,128)(2,1)S(1)}, u32[]{:S(2)}, u32[]{:S(2)}) %collective-permute-start.21) | collective-permute-done | bytes 65568 | tf_op jit(solution)/shard_map/ppermute | solution.py:26
  53.5 1.0 %collective-permute-done.25 = bf16[32,512]{1,0:T(8,128)(2,1)S(1)} collective-permute-done((bf16[32,512]{1,0:T(8,128)(2,1)S(1)}, bf16[32,512]{1,0:T(8,128)(2,1)S(1)}, u32[]{:S(2)}, u32[]{:S(2)}) %collective-permute-start.25) | collective-permute-done | bytes 32800 | tf_op jit(solution)/shard_map/ppermute | solution.py:26
  54.5 2.3 %collective-permute-start.26 = (bf16[16,1024]{1,0:T(8,128)(2,1)S(1)}, bf16[16,1024]{1,0:T(8,128)(2,1)S(1)}, u32[]{:S(2)}, u32[]{:S(2)}) collective-permute-start(bf16[16,1024]{1,0:T(8,128)(2,1)S(1)} %fusion.4), channel_id=1, source_target_pairs={{0,16},{2,18},{4,20},{6,22},{8,24},{10,26},{12,28},{14,30},{16,0},... | collective-permute-start | bytes 98312 | tf_op jit(solution)/shard_map/ppermute | solution.py:26
  56.8 2.9 %collective-permute-done.26 = bf16[16,1024]{1,0:T(8,128)(2,1)S(1)} collective-permute-done((bf16[16,1024]{1,0:T(8,128)(2,1)S(1)}, bf16[16,1024]{1,0:T(8,128)(2,1)S(1)}, u32[]{:S(2)}, u32[]{:S(2)}) %collective-permute-start.26) | collective-permute-done | bytes 32800 | tf_op jit(solution)/shard_map/ppermute | solution.py:26
  59.8 0.6 %fusion.10 = (f32[1,16,512]{2,1,0:T(8,128)}, f32[1,16,512]{2,1,0:T(8,128)}) fusion(f32[16,1024]{1,0:T(8,128)S(1)} %fusion.3, f32[1,16,512]{2,1,0:T(8,128)S(1)} %copy-done.4, f32[1,16,512]{2,1,0:T(8,128)S(1)} %copy-done.3), kind=kLoop, calls=%fused_computation.48 | loop fusion | flops 73728 | bytes 196608 | tf_op jit(solution)/shard_map/broadcast_in_dim | solution.py:250
  (66 shorter events, 1.5 us)
Async XLA Ops:
  1.4 7.2 %collective-permute-start = (bf16[16,512]{1,0:T(8,128)(2,1)S(1)}, bf16[16,512]{1,0:T(8,128)(2,1)S(1)}, u32[]{:S(2)}, u32[]{:S(2)}) collective-permute-start(bf16[16,512]{1,0:T(8,128)(2,1)S(1)} %bitcast_convert_fusion), channel_id=1, source_target_pairs={{0,16},{2,18},{4,20},{6,22},{8,24},{10,26},{12,28},{14,30},{16,0},... | collective-permute-start | bytes 49160 | tf_op jit(solution)/shard_map/ppermute | solution.py:26
  7.0 3.9 %collective-permute-start.7 = (bf16[16,1024]{1,0:T(8,128)(2,1)S(1)}, bf16[16,1024]{1,0:T(8,128)(2,1)S(1)}, u32[]{:S(2)}, u32[]{:S(2)}) collective-permute-start(bf16[16,1024]{1,0:T(8,128)(2,1)S(1)} %pad_maximum_fusion.8), channel_id=1, source_target_pairs={{0,1},{1,0},{2,3},{3,2},{4,5},{5,4},{6,7},{7,6},{8,9},{9,8},{10,11... | collective-permute-start | bytes 98312 | tf_op jit(solution)/shard_map/ppermute | solution.py:26
  8.6 3.9 %collective-permute-start.1 = (bf16[32,512]{1,0:T(8,128)(2,1)S(1)}, bf16[32,512]{1,0:T(8,128)(2,1)S(1)}, u32[]{:S(2)}, u32[]{:S(2)}) collective-permute-start(bf16[32,512]{1,0:T(8,128)(2,1)S(1)} %pad_maximum_fusion.7), channel_id=1, source_target_pairs={{0,8},{2,10},{4,12},{6,14},{8,0},{10,2},{12,4},{14,6},{16,24},{18,... | collective-permute-start | bytes 98312 | tf_op jit(solution)/shard_map/ppermute | solution.py:26
  11.0 7.1 %collective-permute-start.8 = (bf16[16,2560]{1,0:T(8,128)(2,1)S(1)}, bf16[16,2560]{1,0:T(8,128)(2,1)S(1)}, u32[]{:S(2)}, u32[]{:S(2)}) collective-permute-start(bf16[16,2560]{1,0:T(8,128)(2,1)S(1)} %pad_maximum_fusion.4), channel_id=1, source_target_pairs={{0,16},{2,18},{4,20},{6,22},{8,24},{10,26},{12,28},{14,30},{16,0},... | collective-permute-start | bytes 245768 | tf_op jit(solution)/shard_map/ppermute | solution.py:26
  12.5 5.4 %copy-start.5 = (s32[256]{0:T(256)S(1)}, s32[256]{0:T(256)}, u32[]{:S(2)}) copy-start(s32[256]{0:T(256)} %param.10) | copy-start | bytes 3076
  12.5 4.3 %collective-permute-start.2 = (bf16[64,512]{1,0:T(8,128)(2,1)S(1)}, bf16[64,512]{1,0:T(8,128)(2,1)S(1)}, u32[]{:S(2)}, u32[]{:S(2)}) collective-permute-start(bf16[64,512]{1,0:T(8,128)(2,1)S(1)} %pad_maximum_fusion.6), channel_id=1, source_target_pairs={{0,4},{2,6},{4,0},{6,2},{8,12},{10,14},{12,8},{14,10},{16,20},{18,... | collective-permute-start | bytes 196616 | tf_op jit(solution)/shard_map/ppermute | solution.py:26
  16.8 3.0 %collective-permute-start.3 = (bf16[128,512]{1,0:T(8,128)(2,1)S(1)}, bf16[128,512]{1,0:T(8,128)(2,1)S(1)}, u32[]{:S(2)}, u32[]{:S(2)}) collective-permute-start(bf16[128,512]{1,0:T(8,128)(2,1)S(1)} %pad_maximum_fusion.2.w0_ref), channel_id=1, source_target_pairs={{0,2},{2,0},{4,6},{6,4},{8,10},{10,8},{12,14},{14,12},{16,18},{18,... | collective-permute-start | bytes 393224 | tf_op jit(solution)/shard_map/ppermute | solution.py:26
  16.9 8.6 %collective-permute-start.4 = (bf16[128,512]{1,0:T(8,128)(2,1)S(1)}, bf16[128,512]{1,0:T(8,128)(2,1)S(1)}, u32[]{:S(2)}, u32[]{:S(2)}) collective-permute-start(bf16[128,512]{1,0:T(8,128)(2,1)S(1)} %pad_maximum_fusion.2.w0_ref), channel_id=1, source_target_pairs={{0,1},{1,0},{2,3},{3,2},{4,5},{5,4},{6,7},{7,6},{8,9},{9,8},{10,11... | collective-permute-start | bytes 393224 | tf_op jit(solution)/shard_map/ppermute | solution.py:26
  18.1 4.3 %collective-permute-start.12 = (bf16[32,1024]{1,0:T(8,128)(2,1)S(1)}, bf16[32,1024]{1,0:T(8,128)(2,1)S(1)}, u32[]{:S(2)}, u32[]{:S(2)}) collective-permute-start(bf16[32,1024]{1,0:T(8,128)(2,1)S(1)} %slice.106), channel_id=1, source_target_pairs={{0,8},{2,10},{4,12},{6,14},{8,0},{10,2},{12,4},{14,6},{16,24},{18,... | collective-permute-start | bytes 196616 | tf_op jit(solution)/shard_map/ppermute | solution.py:26
  21.1 9.0 %copy-start.1 = (bf16[2,64,8192]{2,1,0:T(8,128)(2,1)S(1)}, bf16[2,64,8192]{2,1,0:T(8,128)(2,1)}, u32[]{:S(2)}) copy-start(bf16[2,64,8192]{2,1,0:T(8,128)(2,1)} %param.13) | copy-start | bytes 6291460
  21.1 10.6 %collective-permute-start.11 = (bf16[16,8192]{1,0:T(8,128)(2,1)S(1)}, bf16[16,8192]{1,0:T(8,128)(2,1)S(1)}, u32[]{:S(2)}, u32[]{:S(2)}) collective-permute-start(bf16[16,8192]{1,0:T(8,128)(2,1)S(1)} %get-tuple-element.40), channel_id=1, source_target_pairs={{0,1},{1,0},{2,3},{3,2},{4,5},{5,4},{6,7},{7,6},{8,9},{9,8},{10,11... | collective-permute-start | bytes 786440 | tf_op jit(solution)/shard_map/ppermute | solution.py:26
  22.5 7.0 %collective-permute-start.13 = (bf16[64,1024]{1,0:T(8,128)(2,1)S(1)}, bf16[64,1024]{1,0:T(8,128)(2,1)S(1)}, u32[]{:S(2)}, u32[]{:S(2)}) collective-permute-start(bf16[64,1024]{1,0:T(8,128)(2,1)S(1)} %pad_maximum_fusion.3), channel_id=1, source_target_pairs={{0,4},{2,6},{4,0},{6,2},{8,12},{10,14},{12,8},{14,10},{16,20},{18,... | collective-permute-start | bytes 393224 | tf_op jit(solution)/shard_map/ppermute | solution.py:26
  24.0 6.2 %collective-permute-start.9 = (bf16[32,1536]{1,0:T(8,128)(2,1)S(1)}, bf16[32,1536]{1,0:T(8,128)(2,1)S(1)}, u32[]{:S(2)}, u32[]{:S(2)}) collective-permute-start(bf16[32,1536]{1,0:T(8,128)(2,1)S(1)} %slice.105), channel_id=1, source_target_pairs={{0,8},{2,10},{4,12},{6,14},{8,0},{10,2},{12,4},{14,6},{16,24},{18,... | collective-permute-start | bytes 294920 | tf_op jit(solution)/shard_map/ppermute | solution.py:26
  25.5 1.3 %collective-permute-start.5 = (bf16[128,512]{1,0:T(8,128)(2,1)S(1)}, bf16[128,512]{1,0:T(8,128)(2,1)S(1)}, u32[]{:S(2)}, u32[]{:S(2)}) collective-permute-start(bf16[128,512]{1,0:T(8,128)(2,1)S(1)} %collective-permute-done.4.w0_ref), channel_id=1, source_target_pairs={{0,2},{2,0},{4,6},{6,4},{8,10},{10,8},{12,14},{14,12},{16,18},{18,... | collective-permute-start | bytes 393224 | tf_op jit(solution)/shard_map/ppermute | solution.py:26
  28.1 2.1 %copy-start.2 = (bf16[2,64,8192]{2,1,0:T(8,128)(2,1)S(1)}, bf16[2,64,8192]{2,1,0:T(8,128)(2,1)}, u32[]{:S(2)}) copy-start(bf16[2,64,8192]{2,1,0:T(8,128)(2,1)} %param.12) | copy-start | bytes 6291460
  28.1 11.6 %collective-permute-start.6 = (bf16[16,8192]{1,0:T(8,128)(2,1)S(1)}, bf16[16,8192]{1,0:T(8,128)(2,1)S(1)}, u32[]{:S(2)}, u32[]{:S(2)}) collective-permute-start(bf16[16,8192]{1,0:T(8,128)(2,1)S(1)} %get-tuple-element.35), channel_id=1, source_target_pairs={{0,1},{1,0},{2,3},{3,2},{4,5},{5,4},{6,7},{7,6},{8,9},{9,8},{10,11... | collective-permute-start | bytes 786440 | tf_op jit(solution)/shard_map/ppermute | solution.py:26
  29.5 1.4 %collective-permute-start.14 = (bf16[128,512]{1,0:T(8,128)(2,1)S(1)}, bf16[128,512]{1,0:T(8,128)(2,1)S(1)}, u32[]{:S(2)}, u32[]{:S(2)}) collective-permute-start(bf16[128,512]{1,0:T(8,128)(2,1)S(1)} %get-tuple-element.63.refs_0_), channel_id=1, source_target_pairs={{0,2},{2,0},{4,6},{6,4},{8,10},{10,8},{12,14},{14,12},{16,18},{18,... | collective-permute-start | bytes 393224 | tf_op jit(solution)/shard_map/ppermute | solution.py:26
  29.6 1.5 %collective-permute-start.15 = (bf16[128,512]{1,0:T(8,128)(2,1)S(1)}, bf16[128,512]{1,0:T(8,128)(2,1)S(1)}, u32[]{:S(2)}, u32[]{:S(2)}) collective-permute-start(bf16[128,512]{1,0:T(8,128)(2,1)S(1)} %get-tuple-element.62.refs_1_), channel_id=1, source_target_pairs={{0,2},{2,0},{4,6},{6,4},{8,10},{10,8},{12,14},{14,12},{16,18},{18,... | collective-permute-start | bytes 393224 | tf_op jit(solution)/shard_map/ppermute | solution.py:26
  30.3 7.0 %collective-permute-start.10 = (bf16[64,1536]{1,0:T(8,128)(2,1)S(1)}, bf16[64,1536]{1,0:T(8,128)(2,1)S(1)}, u32[]{:S(2)}, u32[]{:S(2)}) collective-permute-start(bf16[64,1536]{1,0:T(8,128)(2,1)S(1)} %pad_maximum_fusion.1), channel_id=1, source_target_pairs={{0,4},{2,6},{4,0},{6,2},{8,12},{10,14},{12,8},{14,10},{16,20},{18,... | collective-permute-start | bytes 589832 | tf_op jit(solution)/shard_map/ppermute | solution.py:26
  32.9 6.9 %copy-start = (bf16[1,2,8,8192]{3,2,1,0:T(8,128)(2,1)S(1)}, bf16[1,2,8,8192]{3,2,1,0:T(8,128)(2,1)}, u32[]{:S(2)}) copy-start(bf16[1,2,8,8192]{3,2,1,0:T(8,128)(2,1)} %param.11) | copy-start | bytes 786436
  37.3 1.4 %collective-permute-start.16 = (bf16[128,512]{1,0:T(8,128)(2,1)S(1)}, bf16[128,512]{1,0:T(8,128)(2,1)S(1)}, u32[]{:S(2)}, u32[]{:S(2)}) collective-permute-start(bf16[128,512]{1,0:T(8,128)(2,1)S(1)} %get-tuple-element.61.refs_0_), channel_id=1, source_target_pairs={{0,2},{2,0},{4,6},{6,4},{8,10},{10,8},{12,14},{14,12},{16,18},{18,... | collective-permute-start | bytes 393224 | tf_op jit(solution)/shard_map/ppermute | solution.py:26
  37.4 1.5 %collective-permute-start.17 = (bf16[128,512]{1,0:T(8,128)(2,1)S(1)}, bf16[128,512]{1,0:T(8,128)(2,1)S(1)}, u32[]{:S(2)}, u32[]{:S(2)}) collective-permute-start(bf16[128,512]{1,0:T(8,128)(2,1)S(1)} %get-tuple-element.60.refs_1_), channel_id=1, source_target_pairs={{0,2},{2,0},{4,6},{6,4},{8,10},{10,8},{12,14},{14,12},{16,18},{18,... | collective-permute-start | bytes 393224 | tf_op jit(solution)/shard_map/ppermute | solution.py:26
  37.9 1.3 %collective-permute-start.18 = (bf16[128,512]{1,0:T(8,128)(2,1)S(1)}, bf16[128,512]{1,0:T(8,128)(2,1)S(1)}, u32[]{:S(2)}, u32[]{:S(2)}) collective-permute-start(bf16[128,512]{1,0:T(8,128)(2,1)S(1)} %get-tuple-element.59.refs_2_), channel_id=1, source_target_pairs={{0,2},{2,0},{4,6},{6,4},{8,10},{10,8},{12,14},{14,12},{16,18},{18,... | collective-permute-start | bytes 393224 | tf_op jit(solution)/shard_map/ppermute | solution.py:26
  38.0 3.9 %collective-permute-start.22 = (bf16[128,512]{1,0:T(8,128)(2,1)S(1)}, bf16[128,512]{1,0:T(8,128)(2,1)S(1)}, u32[]{:S(2)}, u32[]{:S(2)}) collective-permute-start(bf16[128,512]{1,0:T(8,128)(2,1)S(1)} %get-tuple-element.57), channel_id=1, source_target_pairs={{0,2},{2,0},{4,6},{6,4},{8,10},{10,8},{12,14},{14,12},{16,18},{18,... | collective-permute-start | bytes 393224 | tf_op jit(solution)/shard_map/ppermute | solution.py:26
  41.6 18.1 %copy-start.3 = (f32[1,16,512]{2,1,0:T(8,128)S(1)}, f32[1,16,512]{2,1,0:T(8,128)}, u32[]{:S(2)}) copy-start(f32[1,16,512]{2,1,0:T(8,128)} %param.7) | copy-start | bytes 98308
  41.6 18.1 %copy-start.4 = (f32[1,16,512]{2,1,0:T(8,128)S(1)}, f32[1,16,512]{2,1,0:T(8,128)}, u32[]{:S(2)}) copy-start(f32[1,16,512]{2,1,0:T(8,128)} %param.9) | copy-start | bytes 98308
  41.6 1.5 %collective-permute-start.19 = (bf16[128,1024]{1,0:T(8,128)(2,1)S(1)}, bf16[128,1024]{1,0:T(8,128)(2,1)S(1)}, u32[]{:S(2)}, u32[]{:S(2)}) collective-permute-start(bf16[128,1024]{1,0:T(8,128)(2,1)S(1)} %get-tuple-element.56), channel_id=1, source_target_pairs={{0,2},{2,0},{4,6},{6,4},{8,10},{10,8},{12,14},{14,12},{16,18},{18,... | collective-permute-start | bytes 786440 | tf_op jit(solution)/shard_map/ppermute | solution.py:26
  41.9 4.6 %collective-permute-start.23 = (bf16[64,512]{1,0:T(8,128)(2,1)S(1)}, bf16[64,512]{1,0:T(8,128)(2,1)S(1)}, u32[]{:S(2)}, u32[]{:S(2)}) collective-permute-start(bf16[64,512]{1,0:T(8,128)(2,1)S(1)} %slice.163), channel_id=1, source_target_pairs={{0,4},{2,6},{4,0},{6,2},{8,12},{10,14},{12,8},{14,10},{16,20},{18,... | collective-permute-start | bytes 196616 | tf_op jit(solution)/shard_map/ppermute | solution.py:26
  43.3 5.8 %collective-permute-start.20 = (bf16[64,1024]{1,0:T(8,128)(2,1)S(1)}, bf16[64,1024]{1,0:T(8,128)(2,1)S(1)}, u32[]{:S(2)}, u32[]{:S(2)}) collective-permute-start(bf16[64,1024]{1,0:T(8,128)(2,1)S(1)} %slice.162), channel_id=1, source_target_pairs={{0,4},{2,6},{4,0},{6,2},{8,12},{10,14},{12,8},{14,10},{16,20},{18,... | collective-permute-start | bytes 393224 | tf_op jit(solution)/shard_map/ppermute | solution.py:26
  46.5 4.0 %collective-permute-start.24 = (bf16[32,512]{1,0:T(8,128)(2,1)S(1)}, bf16[32,512]{1,0:T(8,128)(2,1)S(1)}, u32[]{:S(2)}, u32[]{:S(2)}) collective-permute-start(bf16[32,512]{1,0:T(8,128)(2,1)S(1)} %slice.165), channel_id=1, source_target_pairs={{0,8},{2,10},{4,12},{6,14},{8,0},{10,2},{12,4},{14,6},{16,24},{18,... | collective-permute-start | bytes 98312 | tf_op jit(solution)/shard_map/ppermute | solution.py:26
  49.1 4.3 %collective-permute-start.21 = (bf16[32,1024]{1,0:T(8,128)(2,1)S(1)}, bf16[32,1024]{1,0:T(8,128)(2,1)S(1)}, u32[]{:S(2)}, u32[]{:S(2)}) collective-permute-start(bf16[32,1024]{1,0:T(8,128)(2,1)S(1)} %slice.164), channel_id=1, source_target_pairs={{0,8},{2,10},{4,12},{6,14},{8,0},{10,2},{12,4},{14,6},{16,24},{18,... | collective-permute-start | bytes 196616 | tf_op jit(solution)/shard_map/ppermute | solution.py:26
  50.5 4.0 %collective-permute-start.25 = (bf16[32,512]{1,0:T(8,128)(2,1)S(1)}, bf16[32,512]{1,0:T(8,128)(2,1)S(1)}, u32[]{:S(2)}, u32[]{:S(2)}) collective-permute-start(bf16[32,512]{1,0:T(8,128)(2,1)S(1)} %fusion.5), channel_id=1, source_target_pairs={{0,1},{1,0},{2,3},{3,2},{4,5},{5,4},{6,7},{7,6},{8,9},{9,8},{10,11... | collective-permute-start | bytes 98312 | tf_op jit(solution)/shard_map/ppermute | solution.py:26
  54.5 5.2 %collective-permute-start.26 = (bf16[16,1024]{1,0:T(8,128)(2,1)S(1)}, bf16[16,1024]{1,0:T(8,128)(2,1)S(1)}, u32[]{:S(2)}, u32[]{:S(2)}) collective-permute-start(bf16[16,1024]{1,0:T(8,128)(2,1)S(1)} %fusion.4), channel_id=1, source_target_pairs={{0,16},{2,18},{4,20},{6,22},{8,24},{10,26},{12,28},{14,30},{16,0},... | collective-permute-start | bytes 98312 | tf_op jit(solution)/shard_map/ppermute | solution.py:26

commit v12 on v10

--- a/solution.py
+++ b/solution.py
@@ -70,21 +70,6 @@
         sent_ref[:, at] = part.astype(BF)
 
 
-def moments_kernel(rows, place_ref, *refs):
-    terms, (moment_ref, rate_ref) = refs[:-2], refs[-2:]
-    count = len(terms) // 2
-    half, segment = terms[0].shape
-    width = moment_ref.shape[1]
-    near, far = place_ref[:, :half], place_ref[:, half:]
-    ordered = [dot(near, a[...]) + dot(far, b[...]) for a, b in zip(terms[:count], terms[count:])]
-    moment = sum(ordered[2:], ordered[0])
-    rate = step_rate / (jnp.sqrt(ordered[1]) + epsilon)
-    for c in range(width // segment):
-        at = slice(c * segment, (c + 1) * segment)
-        moment_ref[:, at] = moment[c * rows : (c + 1) * rows]
-        rate_ref[:, at] = rate[c * rows : (c + 1) * rows]
-
-
 def store_flat(back_ref, seg_ref, kept_ref, away_ref, lanes):
     flat = dot(back_ref[...], seg_ref[...]).astype(BF)
     half = kept_ref.shape[0]
@@ -93,24 +78,35 @@
 
 
 def second_kernel(
-    hidden_rows, up_scale, own, back_ref, part_ref, got_ref, weights_ref, moment_ref, rate_ref, x_ref, g_ref, *rest
+    hidden_rows, up_scale, own, place_ref, back_ref, part_ref, got_ref, weights_ref, x_ref, g_ref, near_ref, *rest
 ):
     if own:
-        feedback_ref, kept_ref, away_ref, error_ref, local_ref, seg_ref = rest
+        *far_refs, feedback_ref, kept_ref, away_ref, error_ref, local_ref, seg_ref, shifted_ref = rest
     else:
-        kept_ref, away_ref, local_ref, seg_ref = rest
+        *far_refs, kept_ref, away_ref, local_ref, seg_ref = rest
     rows = 2 * hidden_rows
+    half = near_ref.shape[0]
     segment = seg_ref.shape[1]
     width = x_ref.shape[1]
-    step_one = part_ref[...] + got_ref[...].astype(F32)
-    local_moment = beta_one * moment_ref[...] + (1.0 - beta_one) * step_one
-    local_ref[...] = (weights_ref[...].astype(F32) - local_moment * rate_ref[...]).astype(BF)
+    near = dot(place_ref[:, :half], near_ref[...])
+    terms = [
+        near[:, i * segment : (i + 1) * segment] + dot(place_ref[:, half:], ref[...]) for i, ref in enumerate(far_refs)
+    ]
+    moment = sum(terms[2:], terms[0])
+    rate = step_rate / (jnp.sqrt(terms[1]) + epsilon)
+    for c in range(width // segment):
+        at, run = slice(c * segment, (c + 1) * segment), slice(c * rows, (c + 1) * rows)
+        step_one = part_ref[:, at] + got_ref[:, at].astype(F32)
+        local_moment = beta_one * moment[run] + (1.0 - beta_one) * step_one
+        local_ref[:, at] = (weights_ref[:, at].astype(F32) - local_moment * rate[run]).astype(BF)
+        if own:
+            shifted_ref[:, at] = local_moment + feedback_ref[:, at].astype(F32)
     columns = gradient_rows(local_ref[...], x_ref, g_ref, hidden_rows, up_scale)
     for c in range(width // segment):
         seg_ref[c * rows : (c + 1) * rows] = columns(slice(c * segment, (c + 1) * segment)).astype(BF)
     store_flat(back_ref, seg_ref, kept_ref, away_ref, slice(0, segment))
     if own:
-        shifted = local_moment + feedback_ref[...].astype(F32)
+        shifted = shifted_ref[...]
         magnitude = jnp.sum(jnp.abs(shifted), axis=1, keepdims=True) * (1.0 / width) + 1e-06
         packed = magnitude * jnp.tanh(shifted / magnitude)
         error_ref[...] = (shifted - packed).astype(BF)
@@ -210,21 +206,19 @@
     for k in reversed(range(n_mp)):
         own = k == 0
         block = jnp.concatenate([blocks_a[k], after(arrived[k], event)], axis=0)
-        terms = [block[:, at : at + segment] for at in range(0, block.shape[1], segment)]
-        terms += [swap(term, "dp", 1) for term in terms]
-        moment_t, rate = call(
-            functools.partial(moments_kernel, rows), (shape(tensor, F32), shape(tensor, F32)), (place_map, *terms)
-        )
-        operands = [back_map, parts[k], got[k], weights[k], moment_t, rate, *two]
+        far_terms = [swap(block[:, at : at + segment], "dp", 1) for at in range(0, block.shape[1], segment)]
+        operands = [place_map, back_map, parts[k], got[k], weights[k], *two, block, *far_terms]
         out = [shape((half, (2 if own else 1) * segment), BF)] * 2
+        scratch = [pltpu.VMEM(tensor, BF), pltpu.VMEM((segments, segment), BF)]
         if own:
             operands.append(feedback[0].reshape(tensor))
             out.append(shape(tensor, BF))
+            scratch.append(pltpu.VMEM(tensor, F32))
         result = call(
             functools.partial(second_kernel, hidden_rows, up_scale, own),
             tuple(out),
             operands,
-            [pltpu.VMEM(tensor, BF), pltpu.VMEM((segments, segment), BF)],
+            scratch,
         )
         event = result[0]
         sums[k] = result[0].astype(F32) + swap(result[1], "dp", 1).astype(F32)

time: 57.1 us -> 56.9 us (level)
    pallas_call x6 -> x4, Pallas kernels: 6.69 us -> 6.35 us  [call(): pl.pallas_call(kernel, out_shape=out_shape, in_specs=[pl.BlockSpec(memory...]
  transfers between devices with their start and end apart: 28 -> 28, of which waited for: 16 -> 17; matrix products, arithmetic and copies ran while one was open for 7% -> 7% of each run, Pallas kernels for 12% -> 11%
where the time goes in v12:
time: 56.9 us; the launch traced here: 56.6 us
  starting transfers between devices  31.5 us (55%)
  waiting for transfers between devices  12.2 us (21%)
  Pallas kernels  6.35 us (11%)
  other arithmetic  3.37 us (6%)
  local copies, waits for them, and re-layouts  2.24 us (4%)
  between operations  0.96 us (2%)
    ppermute x28, starting transfers between devices, swap(): return lax.ppermute(x, axis, [(i, i ^ mask) for i in range(n)])  31.5 us
    ppermute x28, waiting for transfers between devices, swap(): return lax.ppermute(x, axis, [(i, i ^ mask) for i in range(n)])  12.2 us
    pallas_call x4, Pallas kernels, call(): pl.pallas_call(kernel, out_shape=out_shape, in_specs=[pl.BlockSpec(memory...  6.35 us
    squeeze x3, local copies, waits for them, and re-layouts, tokens_of(): x[step]  1.81 us
  transfers between devices with their start and end apart: 28, of which 17 were waited for; matrix products, arithmetic and copies ran while one was open for 7% of the time, Pallas kernels for 11%

profile of v12, /device:TPU:0, one launch (start us, length us, event | category | flops | bytes accessed | tf_op | source)
XLA Modules:
  0.0 56.6 jit_solution(10811085120709485960)
XLA Ops:
  0.6 0.8 %bitcast_convert_fusion = bf16[16,512]{1,0:T(8,128)(2,1)S(1)} fusion(f32[1,16,512]{2,1,0:T(8,128)} %param.7), kind=kLoop, calls=%fused_computation.39 | loop fusion | flops 8192 | bytes 49152 | tf_op jit(solution)/shard_map/convert_element_type | solution.py:146
  1.4 4.0 %collective-permute-start = (bf16[16,512]{1,0:T(8,128)(2,1)S(1)}, bf16[16,512]{1,0:T(8,128)(2,1)S(1)}, u32[]{:S(2)}, u32[]{:S(2)}) collective-permute-start(bf16[16,512]{1,0:T(8,128)(2,1)S(1)} %bitcast_convert_fusion), channel_id=1, source_target_pairs={{0,16},{2,18},{4,20},{6,22},{8,24},{10,26},{12,28},{14,30},{16,0},... | collective-permute-start | bytes 49160 | tf_op jit(solution)/shard_map/ppermute | solution.py:26
  5.4 0.8 %fusion.2 = (bf16[16,512]{1,0:T(8,128)(2,1)S(1)}, bf16[16,512]{1,0:T(8,128)(2,1)S(1)}) fusion(f32[16,512]{1,0:T(8,128)} %bitcast.28), kind=kLoop, calls=%fused_computation.27 | loop fusion | flops 32768 | bytes 65536 | tf_op jit(solution)/shard_map/convert_element_type | solution.py:149
  6.3 0.8 %convert_bitcast_fusion = bf16[16,512]{1,0:T(8,128)(2,1)S(1)} fusion(f32[1,16,512]{2,1,0:T(8,128)} %param.9), kind=kLoop, calls=%fused_computation.40 | loop fusion | flops 8192 | bytes 49152 | tf_op jit(solution)/shard_map/convert.7
  7.0 1.5 %collective-permute-start.7 = (bf16[16,1024]{1,0:T(8,128)(2,1)S(1)}, bf16[16,1024]{1,0:T(8,128)(2,1)S(1)}, u32[]{:S(2)}, u32[]{:S(2)}) collective-permute-start(bf16[16,1024]{1,0:T(8,128)(2,1)S(1)} %pad_maximum_fusion.7), channel_id=1, source_target_pairs={{0,1},{1,0},{2,3},{3,2},{4,5},{5,4},{6,7},{7,6},{8,9},{9,8},{10,11... | collective-permute-start | bytes 98312 | tf_op jit(solution)/shard_map/ppermute | solution.py:26
  8.6 1.6 %collective-permute-start.1 = (bf16[32,512]{1,0:T(8,128)(2,1)S(1)}, bf16[32,512]{1,0:T(8,128)(2,1)S(1)}, u32[]{:S(2)}, u32[]{:S(2)}) collective-permute-start(bf16[32,512]{1,0:T(8,128)(2,1)S(1)} %pad_maximum_fusion.6), channel_id=1, source_target_pairs={{0,8},{2,10},{4,12},{6,14},{8,0},{10,2},{12,4},{14,6},{16,24},{18,... | collective-permute-start | bytes 98312 | tf_op jit(solution)/shard_map/ppermute | solution.py:26
  10.1 0.8 %collective-permute-done.7 = bf16[16,1024]{1,0:T(8,128)(2,1)S(1)} collective-permute-done((bf16[16,1024]{1,0:T(8,128)(2,1)S(1)}, bf16[16,1024]{1,0:T(8,128)(2,1)S(1)}, u32[]{:S(2)}, u32[]{:S(2)}) %collective-permute-start.7) | collective-permute-done | bytes 32800 | tf_op jit(solution)/shard_map/ppermute | solution.py:26
  11.0 0.8 %collective-permute-start.8 = (bf16[16,2560]{1,0:T(8,128)(2,1)S(1)}, bf16[16,2560]{1,0:T(8,128)(2,1)S(1)}, u32[]{:S(2)}, u32[]{:S(2)}) collective-permute-start(bf16[16,2560]{1,0:T(8,128)(2,1)S(1)} %pad_maximum_fusion.4), channel_id=1, source_target_pairs={{0,16},{2,18},{4,20},{6,22},{8,24},{10,26},{12,28},{14,30},{16,0},... | collective-permute-start | bytes 245768 | tf_op jit(solution)/shard_map/ppermute | solution.py:26
  11.8 0.7 %collective-permute-done.1 = bf16[32,512]{1,0:T(8,128)(2,1)S(1)} collective-permute-done((bf16[32,512]{1,0:T(8,128)(2,1)S(1)}, bf16[32,512]{1,0:T(8,128)(2,1)S(1)}, u32[]{:S(2)}, u32[]{:S(2)}) %collective-permute-start.1) | collective-permute-done | bytes 32800 | tf_op jit(solution)/shard_map/ppermute | solution.py:26
  12.5 1.6 %collective-permute-start.2 = (bf16[64,512]{1,0:T(8,128)(2,1)S(1)}, bf16[64,512]{1,0:T(8,128)(2,1)S(1)}, u32[]{:S(2)}, u32[]{:S(2)}) collective-permute-start(bf16[64,512]{1,0:T(8,128)(2,1)S(1)} %pad_maximum_fusion.5), channel_id=1, source_target_pairs={{0,4},{2,6},{4,0},{6,2},{8,12},{10,14},{12,8},{14,10},{16,20},{18,... | collective-permute-start | bytes 196616 | tf_op jit(solution)/shard_map/ppermute | solution.py:26
  14.0 1.7 %slice_bitcast_fusion.2 = (bf16[64,8192]{1,0:T(8,128)(2,1)S(1)}, bf16[64,8192]{1,0:T(8,128)(2,1)S(1)}) fusion(bf16[2,64,8192]{2,1,0:T(8,128)(2,1)} %param.13, bf16[2,64,8192]{2,1,0:T(8,128)(2,1)} %param.12), kind=kLoop, calls=%fused_computation.2 | loop fusion | bytes 4194304 | tf_op jit(solution)/shard_map/squeeze | solution.py:119
  15.7 1.1 %collective-permute-done.2 = bf16[64,512]{1,0:T(8,128)(2,1)S(1)} collective-permute-done((bf16[64,512]{1,0:T(8,128)(2,1)S(1)}, bf16[64,512]{1,0:T(8,128)(2,1)S(1)}, u32[]{:S(2)}, u32[]{:S(2)}) %collective-permute-start.2) | collective-permute-done | bytes 65568 | tf_op jit(solution)/shard_map/ppermute | solution.py:26
  16.9 0.9 %collective-permute-start.4 = (bf16[128,512]{1,0:T(8,128)(2,1)S(1)}, bf16[128,512]{1,0:T(8,128)(2,1)S(1)}, u32[]{:S(2)}, u32[]{:S(2)}) collective-permute-start(bf16[128,512]{1,0:T(8,128)(2,1)S(1)} %pad_maximum_fusion.2.w0_ref), channel_id=1, source_target_pairs={{0,1},{1,0},{2,3},{3,2},{4,5},{5,4},{6,7},{7,6},{8,9},{9,8},{10,11... | collective-permute-start | bytes 393224 | tf_op jit(solution)/shard_map/ppermute | solution.py:26
  18.2 1.5 %collective-permute-start.12 = (bf16[32,1024]{1,0:T(8,128)(2,1)S(1)}, bf16[32,1024]{1,0:T(8,128)(2,1)S(1)}, u32[]{:S(2)}, u32[]{:S(2)}) collective-permute-start(bf16[32,1024]{1,0:T(8,128)(2,1)S(1)} %slice.107), channel_id=1, source_target_pairs={{0,8},{2,10},{4,12},{6,14},{8,0},{10,2},{12,4},{14,6},{16,24},{18,... | collective-permute-start | bytes 196616 | tf_op jit(solution)/shard_map/ppermute | solution.py:26
  19.8 1.3 %shard_map.94 = (bf16[16,8192]{1,0:T(8,128)(2,1)S(1)}, f32[16,8192]{1,0:T(8,128)S(1)}, bf16[16,8192]{1,0:T(8,128)(2,1)S(1)}) custom-call(bf16[256,256]{1,0:T(8,128)(2,1)S(1)} %get-tuple-element.61.place_ref, bf16[128,512]{1,0:T(8,128)(2,1)S(1)} %pad_maximum_fusion.2.w0_ref, bf16[128,512]{1,0:T(8,128)(2,1)S(1)} %collective-permute-done.3.w1_ref, ...), custom_call_target="tpu_custom_call" | custom-call | flops 1 | bytes 1 | tf_op jit(solution)/shard_map/pallas_call | solution.py:123
  21.0 1.3 %collective-permute-start.11 = (bf16[16,8192]{1,0:T(8,128)(2,1)S(1)}, bf16[16,8192]{1,0:T(8,128)(2,1)S(1)}, u32[]{:S(2)}, u32[]{:S(2)}) collective-permute-start(bf16[16,8192]{1,0:T(8,128)(2,1)S(1)} %get-tuple-element.38), channel_id=1, source_target_pairs={{0,1},{1,0},{2,3},{3,2},{4,5},{5,4},{6,7},{7,6},{8,9},{9,8},{10,11... | collective-permute-start | bytes 786440 | tf_op jit(solution)/shard_map/ppermute | solution.py:26
  22.3 0.4 collective-permute-start.9
  22.9 1.6 %collective-permute-start.13 = (bf16[64,1024]{1,0:T(8,128)(2,1)S(1)}, bf16[64,1024]{1,0:T(8,128)(2,1)S(1)}, u32[]{:S(2)}, u32[]{:S(2)}) collective-permute-start(bf16[64,1024]{1,0:T(8,128)(2,1)S(1)} %pad_maximum_fusion.3), channel_id=1, source_target_pairs={{0,4},{2,6},{4,0},{6,2},{8,12},{10,14},{12,8},{14,10},{16,20},{18,... | collective-permute-start | bytes 393224 | tf_op jit(solution)/shard_map/ppermute | solution.py:26
  24.4 1.3 %shard_map.95 = (bf16[16,8192]{1,0:T(8,128)(2,1)S(1)}, f32[16,8192]{1,0:T(8,128)S(1)}, bf16[16,8192]{1,0:T(8,128)(2,1)S(1)}) custom-call(bf16[256,256]{1,0:T(8,128)(2,1)S(1)} %get-tuple-element.61.place_ref, bf16[128,512]{1,0:T(8,128)(2,1)S(1)} %collective-permute-done.4.w0_ref, bf16[128,512]{1,0:T(8,128)(2,1)S(1)} %collective-permute-done.5.w1_ref, ...), custom_call_target="tpu_custom_call" | custom-call | flops 1 | bytes 1 | tf_op jit(solution)/shard_map/pallas_call | solution.py:123
  25.7 0.9 %collective-permute-start.6 = (bf16[16,8192]{1,0:T(8,128)(2,1)S(1)}, bf16[16,8192]{1,0:T(8,128)(2,1)S(1)}, u32[]{:S(2)}, u32[]{:S(2)}) collective-permute-start(bf16[16,8192]{1,0:T(8,128)(2,1)S(1)} %get-tuple-element.31), channel_id=1, source_target_pairs={{0,1},{1,0},{2,3},{3,2},{4,5},{5,4},{6,7},{7,6},{8,9},{9,8},{10,11... | collective-permute-start | bytes 786440 | tf_op jit(solution)/shard_map/ppermute | solution.py:26
  26.6 0.3 collective-permute-done.9
  27.0 1.6 %collective-permute-start.10 = (bf16[64,1536]{1,0:T(8,128)(2,1)S(1)}, bf16[64,1536]{1,0:T(8,128)(2,1)S(1)}, u32[]{:S(2)}, u32[]{:S(2)}) collective-permute-start(bf16[64,1536]{1,0:T(8,128)(2,1)S(1)} %pad_maximum_fusion.1), channel_id=1, source_target_pairs={{0,4},{2,6},{4,0},{6,2},{8,12},{10,14},{12,8},{14,10},{16,20},{18,... | collective-permute-start | bytes 589832 | tf_op jit(solution)/shard_map/ppermute | solution.py:26
  28.5 0.3 collective-permute-done.13
  29.0 0.5 collective-permute-start.15
  29.7 0.7 %collective-permute-done.14.rest_0_ = bf16[128,512]{1,0:T(8,128)(2,1)S(1)} collective-permute-done((bf16[128,512]{1,0:T(8,128)(2,1)S(1)}, bf16[128,512]{1,0:T(8,128)(2,1)S(1)}, u32[]{:S(2)}, u32[]{:S(2)}) %collective-permute-start.14) | collective-permute-done | bytes 131104 | tf_op jit(solution)/shard_map/ppermute | solution.py:26
  30.3 0.2 collective-permute-done.15.rest_1_
  30.5 1.7 %shard_map.96 = (bf16[128,512]{1,0:T(8,128)(2,1)S(1)}, bf16[128,512]{1,0:T(8,128)(2,1)S(1)}) custom-call(bf16[256,256]{1,0:T(8,128)(2,1)S(1)} %get-tuple-element.61.place_ref, bf16[256,256]{1,0:T(8,128)(2,1)S(1)} %get-tuple-element.60.back_ref, f32[16,8192]{1,0:T(8,128)S(1)} %get-tuple-element.41.part_ref, ...), custom_call_target="tpu_custom_call" | custom-call | flops 1 | bytes 1 | tf_op jit(solution)/shard_map/pallas_call | solution.py:123
  32.3 1.2 %collective-permute-done.10 = bf16[64,1536]{1,0:T(8,128)(2,1)S(1)} collective-permute-done((bf16[64,1536]{1,0:T(8,128)(2,1)S(1)}, bf16[64,1536]{1,0:T(8,128)(2,1)S(1)}, u32[]{:S(2)}, u32[]{:S(2)}) %collective-permute-start.10) | collective-permute-done | bytes 196640 | tf_op jit(solution)/shard_map/ppermute | solution.py:26
  33.6 0.5 collective-permute-start.17
  34.2 0.4 collective-permute-start.23
  34.6 0.2 collective-permute-done.6.got_ref
  34.8 0.1 collective-permute-done.16.rest_0_
  34.9 0.2 collective-permute-done.17.rest_1_
  35.1 0.3 collective-permute-done.18.rest_2_
  35.5 2.1 %shard_map.97 = (bf16[128,1024]{1,0:T(8,128)(2,1)S(1)}, bf16[128,1024]{1,0:T(8,128)(2,1)S(1)}, bf16[16,8192]{1,0:T(8,128)(2,1)}) custom-call(bf16[256,256]{1,0:T(8,128)(2,1)S(1)} %get-tuple-element.61.place_ref, bf16[256,256]{1,0:T(8,128)(2,1)S(1)} %get-tuple-element.60.back_ref, f32[16,8192]{1,0:T(8,128)S(1)} %get-tuple-element.30.part_ref, ...), custom_call_target="tpu_custom_call" | custom-call | flops 1 | bytes 1 | tf_op jit(solution)/shard_map/pallas_call | solution.py:123
  37.6 0.2 collective-permute-start.19
  37.9 1.2 %collective-permute-start.24 = (bf16[64,512]{1,0:T(8,128)(2,1)S(1)}, bf16[64,512]{1,0:T(8,128)(2,1)S(1)}, u32[]{:S(2)}, u32[]{:S(2)}) collective-permute-start(bf16[64,512]{1,0:T(8,128)(2,1)S(1)} %slice.161), channel_id=1, source_target_pairs={{0,4},{2,6},{4,0},{6,2},{8,12},{10,14},{12,8},{14,10},{16,20},{18,... | collective-permute-start | bytes 196616 | tf_op jit(solution)/shard_map/ppermute | solution.py:26
  39.3 1.2 %collective-permute-start.20 = (bf16[64,1024]{1,0:T(8,128)(2,1)S(1)}, bf16[64,1024]{1,0:T(8,128)(2,1)S(1)}, u32[]{:S(2)}, u32[]{:S(2)}) collective-permute-start(bf16[64,1024]{1,0:T(8,128)(2,1)S(1)} %slice.160), channel_id=1, source_target_pairs={{0,4},{2,6},{4,0},{6,2},{8,12},{10,14},{12,8},{14,10},{16,20},{18,... | collective-permute-start | bytes 393224 | tf_op jit(solution)/shard_map/ppermute | solution.py:26
  40.5 2.0 %collective-permute-done.24 = bf16[64,512]{1,0:T(8,128)(2,1)S(1)} collective-permute-done((bf16[64,512]{1,0:T(8,128)(2,1)S(1)}, bf16[64,512]{1,0:T(8,128)(2,1)S(1)}, u32[]{:S(2)}, u32[]{:S(2)}) %collective-permute-start.24) | collective-permute-done | bytes 65568 | tf_op jit(solution)/shard_map/ppermute | solution.py:26
  42.5 1.5 %collective-permute-start.25 = (bf16[32,512]{1,0:T(8,128)(2,1)S(1)}, bf16[32,512]{1,0:T(8,128)(2,1)S(1)}, u32[]{:S(2)}, u32[]{:S(2)}) collective-permute-start(bf16[32,512]{1,0:T(8,128)(2,1)S(1)} %slice.163), channel_id=1, source_target_pairs={{0,8},{2,10},{4,12},{6,14},{8,0},{10,2},{12,4},{14,6},{16,24},{18,... | collective-permute-start | bytes 98312 | tf_op jit(solution)/shard_map/ppermute | solution.py:26
  44.0 1.1 %collective-permute-done.20 = bf16[64,1024]{1,0:T(8,128)(2,1)S(1)} collective-permute-done((bf16[64,1024]{1,0:T(8,128)(2,1)S(1)}, bf16[64,1024]{1,0:T(8,128)(2,1)S(1)}, u32[]{:S(2)}, u32[]{:S(2)}) %collective-permute-start.20) | collective-permute-done | bytes 131104 | tf_op jit(solution)/shard_map/ppermute | solution.py:26
  45.1 1.5 %collective-permute-start.21 = (bf16[32,1024]{1,0:T(8,128)(2,1)S(1)}, bf16[32,1024]{1,0:T(8,128)(2,1)S(1)}, u32[]{:S(2)}, u32[]{:S(2)}) collective-permute-start(bf16[32,1024]{1,0:T(8,128)(2,1)S(1)} %slice.162), channel_id=1, source_target_pairs={{0,8},{2,10},{4,12},{6,14},{8,0},{10,2},{12,4},{14,6},{16,24},{18,... | collective-permute-start | bytes 196616 | tf_op jit(solution)/shard_map/ppermute | solution.py:26
  46.7 3.1 %collective-permute-start.26 = (bf16[16,512]{1,0:T(8,128)(2,1)S(1)}, bf16[16,512]{1,0:T(8,128)(2,1)S(1)}, u32[]{:S(2)}, u32[]{:S(2)}) collective-permute-start(bf16[16,512]{1,0:T(8,128)(2,1)S(1)} %slice.165), channel_id=1, source_target_pairs={{0,16},{2,18},{4,20},{6,22},{8,24},{10,26},{12,28},{14,30},{16,0},... | collective-permute-start | bytes 49160 | tf_op jit(solution)/shard_map/ppermute | solution.py:26
  49.9 2.2 %collective-permute-start.22 = (bf16[16,1024]{1,0:T(8,128)(2,1)S(1)}, bf16[16,1024]{1,0:T(8,128)(2,1)S(1)}, u32[]{:S(2)}, u32[]{:S(2)}) collective-permute-start(bf16[16,1024]{1,0:T(8,128)(2,1)S(1)} %slice.164), channel_id=1, source_target_pairs={{0,16},{2,18},{4,20},{6,22},{8,24},{10,26},{12,28},{14,30},{16,0},... | collective-permute-start | bytes 98312 | tf_op jit(solution)/shard_map/ppermute | solution.py:26
  52.1 1.0 %collective-permute-start.27 = (bf16[16,512]{1,0:T(8,128)(2,1)S(1)}, bf16[16,512]{1,0:T(8,128)(2,1)S(1)}, u32[]{:S(2)}, u32[]{:S(2)}) collective-permute-start(bf16[16,512]{1,0:T(8,128)(2,1)S(1)} %fusion.3), channel_id=1, source_target_pairs={{0,1},{1,0},{2,3},{3,2},{4,5},{5,4},{6,7},{7,6},{8,9},{9,8},{10,11... | collective-permute-start | bytes 49160 | tf_op jit(solution)/shard_map/ppermute | solution.py:26
  53.1 1.7 %collective-permute-done.22 = bf16[16,1024]{1,0:T(8,128)(2,1)S(1)} collective-permute-done((bf16[16,1024]{1,0:T(8,128)(2,1)S(1)}, bf16[16,1024]{1,0:T(8,128)(2,1)S(1)}, u32[]{:S(2)}, u32[]{:S(2)}) %collective-permute-start.22) | collective-permute-done | bytes 32800 | tf_op jit(solution)/shard_map/ppermute | solution.py:26
  54.8 1.1 %collective-permute-done.27 = bf16[16,512]{1,0:T(8,128)(2,1)S(1)} collective-permute-done((bf16[16,512]{1,0:T(8,128)(2,1)S(1)}, bf16[16,512]{1,0:T(8,128)(2,1)S(1)}, u32[]{:S(2)}, u32[]{:S(2)}) %collective-permute-start.27) | collective-permute-done | bytes 16416 | tf_op jit(solution)/shard_map/ppermute | solution.py:26
  55.9 0.6 %fusion.12 = (f32[1,16,512]{2,1,0:T(8,128)}, f32[1,16,512]{2,1,0:T(8,128)}) fusion(bf16[16,512]{1,0:T(8,128)(2,1)S(1)} %collective-permute-done.27, f32[16,1024]{1,0:T(8,128)S(1)} %slice_add_fusion.4, f32[1,16,512]{2,1,0:T(8,128)S(1)} %copy-done.4, f32[1,16,512]{2,1,0:T(8,128)S(1)} %copy-done.3), kind=kLoop, calls=%fused_computation.59 | loop fusion | flops 90112 | bytes 212992 | tf_op jit(solution)/shard_map/broadcast_in_dim | solution.py:241
  (67 shorter events, 1.4 us)
Async XLA Ops:
  1.4 7.2 %collective-permute-start = (bf16[16,512]{1,0:T(8,128)(2,1)S(1)}, bf16[16,512]{1,0:T(8,128)(2,1)S(1)}, u32[]{:S(2)}, u32[]{:S(2)}) collective-permute-start(bf16[16,512]{1,0:T(8,128)(2,1)S(1)} %bitcast_convert_fusion), channel_id=1, source_target_pairs={{0,16},{2,18},{4,20},{6,22},{8,24},{10,26},{12,28},{14,30},{16,0},... | collective-permute-start | bytes 49160 | tf_op jit(solution)/shard_map/ppermute | solution.py:26
  7.0 3.9 %collective-permute-start.7 = (bf16[16,1024]{1,0:T(8,128)(2,1)S(1)}, bf16[16,1024]{1,0:T(8,128)(2,1)S(1)}, u32[]{:S(2)}, u32[]{:S(2)}) collective-permute-start(bf16[16,1024]{1,0:T(8,128)(2,1)S(1)} %pad_maximum_fusion.7), channel_id=1, source_target_pairs={{0,1},{1,0},{2,3},{3,2},{4,5},{5,4},{6,7},{7,6},{8,9},{9,8},{10,11... | collective-permute-start | bytes 98312 | tf_op jit(solution)/shard_map/ppermute | solution.py:26
  8.6 3.9 %collective-permute-start.1 = (bf16[32,512]{1,0:T(8,128)(2,1)S(1)}, bf16[32,512]{1,0:T(8,128)(2,1)S(1)}, u32[]{:S(2)}, u32[]{:S(2)}) collective-permute-start(bf16[32,512]{1,0:T(8,128)(2,1)S(1)} %pad_maximum_fusion.6), channel_id=1, source_target_pairs={{0,8},{2,10},{4,12},{6,14},{8,0},{10,2},{12,4},{14,6},{16,24},{18,... | collective-permute-start | bytes 98312 | tf_op jit(solution)/shard_map/ppermute | solution.py:26
  11.0 6.9 %collective-permute-start.8 = (bf16[16,2560]{1,0:T(8,128)(2,1)S(1)}, bf16[16,2560]{1,0:T(8,128)(2,1)S(1)}, u32[]{:S(2)}, u32[]{:S(2)}) collective-permute-start(bf16[16,2560]{1,0:T(8,128)(2,1)S(1)} %pad_maximum_fusion.4), channel_id=1, source_target_pairs={{0,16},{2,18},{4,20},{6,22},{8,24},{10,26},{12,28},{14,30},{16,0},... | collective-permute-start | bytes 245768 | tf_op jit(solution)/shard_map/ppermute | solution.py:26
  12.5 5.4 %copy-start.5 = (s32[256]{0:T(256)S(1)}, s32[256]{0:T(256)}, u32[]{:S(2)}) copy-start(s32[256]{0:T(256)} %param.10) | copy-start | bytes 3076
  12.5 4.3 %collective-permute-start.2 = (bf16[64,512]{1,0:T(8,128)(2,1)S(1)}, bf16[64,512]{1,0:T(8,128)(2,1)S(1)}, u32[]{:S(2)}, u32[]{:S(2)}) collective-permute-start(bf16[64,512]{1,0:T(8,128)(2,1)S(1)} %pad_maximum_fusion.5), channel_id=1, source_target_pairs={{0,4},{2,6},{4,0},{6,2},{8,12},{10,14},{12,8},{14,10},{16,20},{18,... | collective-permute-start | bytes 196616 | tf_op jit(solution)/shard_map/ppermute | solution.py:26
  16.8 2.9 %collective-permute-start.3 = (bf16[128,512]{1,0:T(8,128)(2,1)S(1)}, bf16[128,512]{1,0:T(8,128)(2,1)S(1)}, u32[]{:S(2)}, u32[]{:S(2)}) collective-permute-start(bf16[128,512]{1,0:T(8,128)(2,1)S(1)} %pad_maximum_fusion.2.w0_ref), channel_id=1, source_target_pairs={{0,2},{2,0},{4,6},{6,4},{8,10},{10,8},{12,14},{14,12},{16,18},{18,... | collective-permute-start | bytes 393224 | tf_op jit(solution)/shard_map/ppermute | solution.py:26
  16.9 5.9 %collective-permute-start.4 = (bf16[128,512]{1,0:T(8,128)(2,1)S(1)}, bf16[128,512]{1,0:T(8,128)(2,1)S(1)}, u32[]{:S(2)}, u32[]{:S(2)}) collective-permute-start(bf16[128,512]{1,0:T(8,128)(2,1)S(1)} %pad_maximum_fusion.2.w0_ref), channel_id=1, source_target_pairs={{0,1},{1,0},{2,3},{3,2},{4,5},{5,4},{6,7},{7,6},{8,9},{9,8},{10,11... | collective-permute-start | bytes 393224 | tf_op jit(solution)/shard_map/ppermute | solution.py:26
  18.2 4.7 %collective-permute-start.12 = (bf16[32,1024]{1,0:T(8,128)(2,1)S(1)}, bf16[32,1024]{1,0:T(8,128)(2,1)S(1)}, u32[]{:S(2)}, u32[]{:S(2)}) collective-permute-start(bf16[32,1024]{1,0:T(8,128)(2,1)S(1)} %slice.107), channel_id=1, source_target_pairs={{0,8},{2,10},{4,12},{6,14},{8,0},{10,2},{12,4},{14,6},{16,24},{18,... | collective-permute-start | bytes 196616 | tf_op jit(solution)/shard_map/ppermute | solution.py:26
  21.0 9.5 %collective-permute-start.11 = (bf16[16,8192]{1,0:T(8,128)(2,1)S(1)}, bf16[16,8192]{1,0:T(8,128)(2,1)S(1)}, u32[]{:S(2)}, u32[]{:S(2)}) collective-permute-start(bf16[16,8192]{1,0:T(8,128)(2,1)S(1)} %get-tuple-element.38), channel_id=1, source_target_pairs={{0,1},{1,0},{2,3},{3,2},{4,5},{5,4},{6,7},{7,6},{8,9},{9,8},{10,11... | collective-permute-start | bytes 786440 | tf_op jit(solution)/shard_map/ppermute | solution.py:26
  22.3 4.6 %collective-permute-start.9 = (bf16[32,1536]{1,0:T(8,128)(2,1)S(1)}, bf16[32,1536]{1,0:T(8,128)(2,1)S(1)}, u32[]{:S(2)}, u32[]{:S(2)}) collective-permute-start(bf16[32,1536]{1,0:T(8,128)(2,1)S(1)} %slice.106), channel_id=1, source_target_pairs={{0,8},{2,10},{4,12},{6,14},{8,0},{10,2},{12,4},{14,6},{16,24},{18,... | collective-permute-start | bytes 294920 | tf_op jit(solution)/shard_map/ppermute | solution.py:26
  22.8 1.6 %collective-permute-start.5 = (bf16[128,512]{1,0:T(8,128)(2,1)S(1)}, bf16[128,512]{1,0:T(8,128)(2,1)S(1)}, u32[]{:S(2)}, u32[]{:S(2)}) collective-permute-start(bf16[128,512]{1,0:T(8,128)(2,1)S(1)} %collective-permute-done.4.w0_ref), channel_id=1, source_target_pairs={{0,2},{2,0},{4,6},{6,4},{8,10},{10,8},{12,14},{14,12},{16,18},{18,... | collective-permute-start | bytes 393224 | tf_op jit(solution)/shard_map/ppermute | solution.py:26
  22.8 6.6 %copy-start.1 = (bf16[2,64,8192]{2,1,0:T(8,128)(2,1)S(1)}, bf16[2,64,8192]{2,1,0:T(8,128)(2,1)}, u32[]{:S(2)}) copy-start(bf16[2,64,8192]{2,1,0:T(8,128)(2,1)} %param.13) | copy-start | bytes 6291460
  22.9 6.0 %collective-permute-start.13 = (bf16[64,1024]{1,0:T(8,128)(2,1)S(1)}, bf16[64,1024]{1,0:T(8,128)(2,1)S(1)}, u32[]{:S(2)}, u32[]{:S(2)}) collective-permute-start(bf16[64,1024]{1,0:T(8,128)(2,1)S(1)} %pad_maximum_fusion.3), channel_id=1, source_target_pairs={{0,4},{2,6},{4,0},{6,2},{8,12},{10,14},{12,8},{14,10},{16,20},{18,... | collective-permute-start | bytes 393224 | tf_op jit(solution)/shard_map/ppermute | solution.py:26
  25.7 3.8 %copy-start.2 = (bf16[2,64,8192]{2,1,0:T(8,128)(2,1)S(1)}, bf16[2,64,8192]{2,1,0:T(8,128)(2,1)}, u32[]{:S(2)}) copy-start(bf16[2,64,8192]{2,1,0:T(8,128)(2,1)} %param.12) | copy-start | bytes 6291460
  25.7 9.1 %collective-permute-start.6 = (bf16[16,8192]{1,0:T(8,128)(2,1)S(1)}, bf16[16,8192]{1,0:T(8,128)(2,1)S(1)}, u32[]{:S(2)}, u32[]{:S(2)}) collective-permute-start(bf16[16,8192]{1,0:T(8,128)(2,1)S(1)} %get-tuple-element.31), channel_id=1, source_target_pairs={{0,1},{1,0},{2,3},{3,2},{4,5},{5,4},{6,7},{7,6},{8,9},{9,8},{10,11... | collective-permute-start | bytes 786440 | tf_op jit(solution)/shard_map/ppermute | solution.py:26
  27.0 6.5 %collective-permute-start.10 = (bf16[64,1536]{1,0:T(8,128)(2,1)S(1)}, bf16[64,1536]{1,0:T(8,128)(2,1)S(1)}, u32[]{:S(2)}, u32[]{:S(2)}) collective-permute-start(bf16[64,1536]{1,0:T(8,128)(2,1)S(1)} %pad_maximum_fusion.1), channel_id=1, source_target_pairs={{0,4},{2,6},{4,0},{6,2},{8,12},{10,14},{12,8},{14,10},{16,20},{18,... | collective-permute-start | bytes 589832 | tf_op jit(solution)/shard_map/ppermute | solution.py:26
  28.9 1.4 %collective-permute-start.14 = (bf16[128,512]{1,0:T(8,128)(2,1)S(1)}, bf16[128,512]{1,0:T(8,128)(2,1)S(1)}, u32[]{:S(2)}, u32[]{:S(2)}) collective-permute-start(bf16[128,512]{1,0:T(8,128)(2,1)S(1)} %get-tuple-element.55), channel_id=1, source_target_pairs={{0,2},{2,0},{4,6},{6,4},{8,10},{10,8},{12,14},{14,12},{16,18},{18,... | collective-permute-start | bytes 393224 | tf_op jit(solution)/shard_map/ppermute | solution.py:26
  29.0 1.5 %collective-permute-start.15 = (bf16[128,512]{1,0:T(8,128)(2,1)S(1)}, bf16[128,512]{1,0:T(8,128)(2,1)S(1)}, u32[]{:S(2)}, u32[]{:S(2)}) collective-permute-start(bf16[128,512]{1,0:T(8,128)(2,1)S(1)} %get-tuple-element.54), channel_id=1, source_target_pairs={{0,2},{2,0},{4,6},{6,4},{8,10},{10,8},{12,14},{14,12},{16,18},{18,... | collective-permute-start | bytes 393224 | tf_op jit(solution)/shard_map/ppermute | solution.py:26
  30.5 5.0 %copy-start = (bf16[1,2,8,8192]{3,2,1,0:T(8,128)(2,1)S(1)}, bf16[1,2,8,8192]{3,2,1,0:T(8,128)(2,1)}, u32[]{:S(2)}) copy-start(bf16[1,2,8,8192]{3,2,1,0:T(8,128)(2,1)} %param.11) | copy-start | bytes 786436
  33.5 1.4 %collective-permute-start.16 = (bf16[128,512]{1,0:T(8,128)(2,1)S(1)}, bf16[128,512]{1,0:T(8,128)(2,1)S(1)}, u32[]{:S(2)}, u32[]{:S(2)}) collective-permute-start(bf16[128,512]{1,0:T(8,128)(2,1)S(1)} %get-tuple-element.53), channel_id=1, source_target_pairs={{0,2},{2,0},{4,6},{6,4},{8,10},{10,8},{12,14},{14,12},{16,18},{18,... | collective-permute-start | bytes 393224 | tf_op jit(solution)/shard_map/ppermute | solution.py:26
  33.6 1.5 %collective-permute-start.17 = (bf16[128,512]{1,0:T(8,128)(2,1)S(1)}, bf16[128,512]{1,0:T(8,128)(2,1)S(1)}, u32[]{:S(2)}, u32[]{:S(2)}) collective-permute-start(bf16[128,512]{1,0:T(8,128)(2,1)S(1)} %get-tuple-element.52), channel_id=1, source_target_pairs={{0,2},{2,0},{4,6},{6,4},{8,10},{10,8},{12,14},{14,12},{16,18},{18,... | collective-permute-start | bytes 393224 | tf_op jit(solution)/shard_map/ppermute | solution.py:26
  34.1 1.3 %collective-permute-start.18 = (bf16[128,512]{1,0:T(8,128)(2,1)S(1)}, bf16[128,512]{1,0:T(8,128)(2,1)S(1)}, u32[]{:S(2)}, u32[]{:S(2)}) collective-permute-start(bf16[128,512]{1,0:T(8,128)(2,1)S(1)} %get-tuple-element.51), channel_id=1, source_target_pairs={{0,2},{2,0},{4,6},{6,4},{8,10},{10,8},{12,14},{14,12},{16,18},{18,... | collective-permute-start | bytes 393224 | tf_op jit(solution)/shard_map/ppermute | solution.py:26
  34.2 3.6 %collective-permute-start.23 = (bf16[128,512]{1,0:T(8,128)(2,1)S(1)}, bf16[128,512]{1,0:T(8,128)(2,1)S(1)}, u32[]{:S(2)}, u32[]{:S(2)}) collective-permute-start(bf16[128,512]{1,0:T(8,128)(2,1)S(1)} %get-tuple-element.49), channel_id=1, source_target_pairs={{0,2},{2,0},{4,6},{6,4},{8,10},{10,8},{12,14},{14,12},{16,18},{18,... | collective-permute-start | bytes 393224 | tf_op jit(solution)/shard_map/ppermute | solution.py:26
  37.6 18.4 %copy-start.3 = (f32[1,16,512]{2,1,0:T(8,128)S(1)}, f32[1,16,512]{2,1,0:T(8,128)}, u32[]{:S(2)}) copy-start(f32[1,16,512]{2,1,0:T(8,128)} %param.7) | copy-start | bytes 98308
  37.6 18.3 %copy-start.4 = (f32[1,16,512]{2,1,0:T(8,128)S(1)}, f32[1,16,512]{2,1,0:T(8,128)}, u32[]{:S(2)}) copy-start(f32[1,16,512]{2,1,0:T(8,128)} %param.9) | copy-start | bytes 98308
  37.6 1.6 %collective-permute-start.19 = (bf16[128,1024]{1,0:T(8,128)(2,1)S(1)}, bf16[128,1024]{1,0:T(8,128)(2,1)S(1)}, u32[]{:S(2)}, u32[]{:S(2)}) collective-permute-start(bf16[128,1024]{1,0:T(8,128)(2,1)S(1)} %get-tuple-element.48), channel_id=1, source_target_pairs={{0,2},{2,0},{4,6},{6,4},{8,10},{10,8},{12,14},{14,12},{16,18},{18,... | collective-permute-start | bytes 786440 | tf_op jit(solution)/shard_map/ppermute | solution.py:26
  37.9 4.6 %collective-permute-start.24 = (bf16[64,512]{1,0:T(8,128)(2,1)S(1)}, bf16[64,512]{1,0:T(8,128)(2,1)S(1)}, u32[]{:S(2)}, u32[]{:S(2)}) collective-permute-start(bf16[64,512]{1,0:T(8,128)(2,1)S(1)} %slice.161), channel_id=1, source_target_pairs={{0,4},{2,6},{4,0},{6,2},{8,12},{10,14},{12,8},{14,10},{16,20},{18,... | collective-permute-start | bytes 196616 | tf_op jit(solution)/shard_map/ppermute | solution.py:26
  39.3 5.8 %collective-permute-start.20 = (bf16[64,1024]{1,0:T(8,128)(2,1)S(1)}, bf16[64,1024]{1,0:T(8,128)(2,1)S(1)}, u32[]{:S(2)}, u32[]{:S(2)}) collective-permute-start(bf16[64,1024]{1,0:T(8,128)(2,1)S(1)} %slice.160), channel_id=1, source_target_pairs={{0,4},{2,6},{4,0},{6,2},{8,12},{10,14},{12,8},{14,10},{16,20},{18,... | collective-permute-start | bytes 393224 | tf_op jit(solution)/shard_map/ppermute | solution.py:26
  42.5 4.1 %collective-permute-start.25 = (bf16[32,512]{1,0:T(8,128)(2,1)S(1)}, bf16[32,512]{1,0:T(8,128)(2,1)S(1)}, u32[]{:S(2)}, u32[]{:S(2)}) collective-permute-start(bf16[32,512]{1,0:T(8,128)(2,1)S(1)} %slice.163), channel_id=1, source_target_pairs={{0,8},{2,10},{4,12},{6,14},{8,0},{10,2},{12,4},{14,6},{16,24},{18,... | collective-permute-start | bytes 98312 | tf_op jit(solution)/shard_map/ppermute | solution.py:26
  45.1 4.7 %collective-permute-start.21 = (bf16[32,1024]{1,0:T(8,128)(2,1)S(1)}, bf16[32,1024]{1,0:T(8,128)(2,1)S(1)}, u32[]{:S(2)}, u32[]{:S(2)}) collective-permute-start(bf16[32,1024]{1,0:T(8,128)(2,1)S(1)} %slice.162), channel_id=1, source_target_pairs={{0,8},{2,10},{4,12},{6,14},{8,0},{10,2},{12,4},{14,6},{16,24},{18,... | collective-permute-start | bytes 196616 | tf_op jit(solution)/shard_map/ppermute | solution.py:26
  46.7 5.4 %collective-permute-start.26 = (bf16[16,512]{1,0:T(8,128)(2,1)S(1)}, bf16[16,512]{1,0:T(8,128)(2,1)S(1)}, u32[]{:S(2)}, u32[]{:S(2)}) collective-permute-start(bf16[16,512]{1,0:T(8,128)(2,1)S(1)} %slice.165), channel_id=1, source_target_pairs={{0,16},{2,18},{4,20},{6,22},{8,24},{10,26},{12,28},{14,30},{16,0},... | collective-permute-start | bytes 49160 | tf_op jit(solution)/shard_map/ppermute | solution.py:26
  49.9 4.9 %collective-permute-start.22 = (bf16[16,1024]{1,0:T(8,128)(2,1)S(1)}, bf16[16,1024]{1,0:T(8,128)(2,1)S(1)}, u32[]{:S(2)}, u32[]{:S(2)}) collective-permute-start(bf16[16,1024]{1,0:T(8,128)(2,1)S(1)} %slice.164), channel_id=1, source_target_pairs={{0,16},{2,18},{4,20},{6,22},{8,24},{10,26},{12,28},{14,30},{16,0},... | collective-permute-start | bytes 98312 | tf_op jit(solution)/shard_map/ppermute | solution.py:26
  52.1 3.8 %collective-permute-start.27 = (bf16[16,512]{1,0:T(8,128)(2,1)S(1)}, bf16[16,512]{1,0:T(8,128)(2,1)S(1)}, u32[]{:S(2)}, u32[]{:S(2)}) collective-permute-start(bf16[16,512]{1,0:T(8,128)(2,1)S(1)} %fusion.3), channel_id=1, source_target_pairs={{0,1},{1,0},{2,3},{3,2},{4,5},{5,4},{6,7},{7,6},{8,9},{9,8},{10,11... | collective-permute-start | bytes 49160 | tf_op jit(solution)/shard_map/ppermute | solution.py:26

commit v13 on v12

--- a/solution.py
+++ b/solution.py
@@ -28,6 +28,11 @@
 
 def after(x, *others):
     return lax.optimization_barrier((x, *others))[0]
+
+
+def halve(total, mask, *others):
+    count = total.shape[0] // 2
+    return total[:count] + after(swap(total[count:].astype(BF), "dp", mask), *others).astype(F32)
 
 
 def bits_of(n, lowest=1):
@@ -199,7 +204,10 @@
     blocks_a[0] = after(blocks_a[0], sent[0])
     arrived = [after(swap(b, "dp", far[-2]), sent[0] if k else sent[-1]) for k, b in enumerate(blocks_a)]
     blocks_a = [jnp.concatenate(pair, axis=0) for pair in zip(blocks_a, arrived)]
-    arrived = [swap(b, "dp", far[-1]) for b in blocks_a]
+    arrived = [swap(blocks_a[0], "dp", far[-1])]
+    for block in blocks_a[1:]:
+        terms = [swap(block[:, at : at + segment], "dp", far[-1]) for at in (0, segment)]
+        arrived.append(jnp.concatenate(lax.optimization_barrier((*terms, sent[-1], blocks_a[0]))[:2], axis=1))
 
     half = segments // 2
     sums, event = [None] * n_mp, sent[-1]
@@ -221,18 +229,22 @@
             scratch,
         )
         event = result[0]
-        sums[k] = result[0].astype(F32) + swap(result[1], "dp", 1).astype(F32)
-    error = result[2]
-
-    for mask in far[::-1]:
-        count = sums[0].shape[0] // 2
-        sums = [p[:count] + swap(p[count:].astype(BF), "dp", mask).astype(F32) for p in sums]
-    own_grad, own_packed = sums[0][:, :segment], sums[0][:, segment:]
-    grads = [own_grad] + sums[1:]
+        if own:
+            sums[1:] = [halve(p, far[-1], event) for p in sums[1:]]
+            away, error = after(result[1], *sums[1:]), result[2]
+        else:
+            away = result[1]
+        sums[k] = result[0].astype(F32) + swap(away, "dp", 1).astype(F32)
+    sums[0] = halve(sums[0], far[-1])
+
+    grads = [sums[0][:, :segment]] + sums[1:]
     for mask in mp_bits:
         crossed = [swap(p.astype(BF), "mp", mask).astype(F32) for p in grads[mask:]]
         grads = [p + q for p, q in zip(grads, crossed)]
-    own_grad = grads[0]
+    both = jnp.concatenate([grads[0], sums[0][:, segment:]], axis=1)
+    for mask in far[-2::-1]:
+        both = halve(both, mask)
+    own_grad, own_packed = both[:, :segment], both[:, segment:]
     mean_grad = own_grad / n_dp
     mean_moment = own_packed / n_dp
     moment_new = beta_one * mean_moment + (1.0 - beta_one) * mean_grad

time: 56.9 us -> 57.3 us (level)
  waiting for transfers between devices: 12.2 us -> 15.6 us
  starting transfers between devices: 31.5 us -> 28.4 us
    ppermute x28 -> x27, waiting for transfers between devices: 12.2 us -> 15.6 us  [swap(): return lax.ppermute(x, axis, [(i, i ^ mask) for i in range(n)])]
    ppermute x28 -> x27, starting transfers between devices: 31.5 us -> 28.4 us  [swap(): return lax.ppermute(x, axis, [(i, i ^ mask) for i in range(n)])]
  transfers between devices with their start and end apart: 28 -> 27, of which waited for: 17 -> 13; matrix products, arithmetic and copies ran while one was open for 7% -> 7% of each run, Pallas kernels for 11% -> 11%
where the time goes in v13:
time: 57.3 us; the launch traced here: 56.9 us
  starting transfers between devices  28.4 us (50%)
  waiting for transfers between devices  15.6 us (27%)
  Pallas kernels  6.35 us (11%)
  other arithmetic  3.4 us (6%)
  local copies, waits for them, and re-layouts  2.23 us (4%)
  between operations  0.98 us (2%)
    ppermute x27, starting transfers between devices, swap(): return lax.ppermute(x, axis, [(i, i ^ mask) for i in range(n)])  28.4 us
    ppermute x27, waiting for transfers between devices, swap(): return lax.ppermute(x, axis, [(i, i ^ mask) for i in range(n)])  15.6 us
    pallas_call x4, Pallas kernels, call(): pl.pallas_call(kernel, out_shape=out_shape, in_specs=[pl.BlockSpec(memory...  6.35 us
    squeeze x3, local copies, waits for them, and re-layouts, tokens_of(): x[step]  1.81 us
  transfers between devices with their start and end apart: 27, of which 13 were waited for; matrix products, arithmetic and copies ran while one was open for 7% of the time, Pallas kernels for 11%

profile of v13, /device:TPU:0, one launch (start us, length us, event | category | flops | bytes accessed | tf_op | source)
XLA Modules:
  0.0 56.9 jit_solution(7597640356015476496)
XLA Ops:
  0.6 0.8 %bitcast_convert_fusion = bf16[16,512]{1,0:T(8,128)(2,1)S(1)} fusion(f32[1,16,512]{2,1,0:T(8,128)} %param.7), kind=kLoop, calls=%fused_computation.41 | loop fusion | flops 8192 | bytes 49152 | tf_op jit(solution)/shard_map/convert_element_type | solution.py:151
  1.4 4.0 %collective-permute-start = (bf16[16,512]{1,0:T(8,128)(2,1)S(1)}, bf16[16,512]{1,0:T(8,128)(2,1)S(1)}, u32[]{:S(2)}, u32[]{:S(2)}) collective-permute-start(bf16[16,512]{1,0:T(8,128)(2,1)S(1)} %bitcast_convert_fusion), channel_id=1, source_target_pairs={{0,16},{2,18},{4,20},{6,22},{8,24},{10,26},{12,28},{14,30},{16,0},... | collective-permute-start | bytes 49160 | tf_op jit(solution)/shard_map/ppermute | solution.py:26
  5.4 0.8 %convert_bitcast_fusion = bf16[16,512]{1,0:T(8,128)(2,1)S(1)} fusion(f32[1,16,512]{2,1,0:T(8,128)} %param.9), kind=kLoop, calls=%fused_computation.49 | loop fusion | flops 8192 | bytes 49152 | tf_op jit(solution)/shard_map/convert.5
  6.2 0.8 %fusion.6 = (bf16[16,512]{1,0:T(8,128)(2,1)S(1)}, bf16[16,512]{1,0:T(8,128)(2,1)S(1)}) fusion(f32[16,512]{1,0:T(8,128)} %bitcast.28), kind=kLoop, calls=%fused_computation.33 | loop fusion | flops 32768 | bytes 65536 | tf_op jit(solution)/shard_map/convert_element_type | solution.py:154
  7.0 1.6 %collective-permute-start.7 = (bf16[16,1024]{1,0:T(8,128)(2,1)S(1)}, bf16[16,1024]{1,0:T(8,128)(2,1)S(1)}, u32[]{:S(2)}, u32[]{:S(2)}) collective-permute-start(bf16[16,1024]{1,0:T(8,128)(2,1)S(1)} %pad_maximum_fusion.8), channel_id=1, source_target_pairs={{0,1},{1,0},{2,3},{3,2},{4,5},{5,4},{6,7},{7,6},{8,9},{9,8},{10,11... | collective-permute-start | bytes 98312 | tf_op jit(solution)/shard_map/ppermute | solution.py:26
  8.6 1.6 %collective-permute-start.1 = (bf16[32,512]{1,0:T(8,128)(2,1)S(1)}, bf16[32,512]{1,0:T(8,128)(2,1)S(1)}, u32[]{:S(2)}, u32[]{:S(2)}) collective-permute-start(bf16[32,512]{1,0:T(8,128)(2,1)S(1)} %pad_maximum_fusion.7), channel_id=1, source_target_pairs={{0,8},{2,10},{4,12},{6,14},{8,0},{10,2},{12,4},{14,6},{16,24},{18,... | collective-permute-start | bytes 98312 | tf_op jit(solution)/shard_map/ppermute | solution.py:26
  10.2 0.8 %collective-permute-done.7 = bf16[16,1024]{1,0:T(8,128)(2,1)S(1)} collective-permute-done((bf16[16,1024]{1,0:T(8,128)(2,1)S(1)}, bf16[16,1024]{1,0:T(8,128)(2,1)S(1)}, u32[]{:S(2)}, u32[]{:S(2)}) %collective-permute-start.7) | collective-permute-done | bytes 32800 | tf_op jit(solution)/shard_map/ppermute | solution.py:26
  11.0 0.8 %collective-permute-start.8 = (bf16[16,2560]{1,0:T(8,128)(2,1)S(1)}, bf16[16,2560]{1,0:T(8,128)(2,1)S(1)}, u32[]{:S(2)}, u32[]{:S(2)}) collective-permute-start(bf16[16,2560]{1,0:T(8,128)(2,1)S(1)} %pad_maximum_fusion.4), channel_id=1, source_target_pairs={{0,16},{2,18},{4,20},{6,22},{8,24},{10,26},{12,28},{14,30},{16,0},... | collective-permute-start | bytes 245768 | tf_op jit(solution)/shard_map/ppermute | solution.py:26
  11.8 0.7 %collective-permute-done.1 = bf16[32,512]{1,0:T(8,128)(2,1)S(1)} collective-permute-done((bf16[32,512]{1,0:T(8,128)(2,1)S(1)}, bf16[32,512]{1,0:T(8,128)(2,1)S(1)}, u32[]{:S(2)}, u32[]{:S(2)}) %collective-permute-start.1) | collective-permute-done | bytes 32800 | tf_op jit(solution)/shard_map/ppermute | solution.py:26
  12.6 1.6 %collective-permute-start.2 = (bf16[64,512]{1,0:T(8,128)(2,1)S(1)}, bf16[64,512]{1,0:T(8,128)(2,1)S(1)}, u32[]{:S(2)}, u32[]{:S(2)}) collective-permute-start(bf16[64,512]{1,0:T(8,128)(2,1)S(1)} %pad_maximum_fusion.6), channel_id=1, source_target_pairs={{0,4},{2,6},{4,0},{6,2},{8,12},{10,14},{12,8},{14,10},{16,20},{18,... | collective-permute-start | bytes 196616 | tf_op jit(solution)/shard_map/ppermute | solution.py:26
  14.1 1.7 %slice_bitcast_fusion.2 = (bf16[64,8192]{1,0:T(8,128)(2,1)S(1)}, bf16[64,8192]{1,0:T(8,128)(2,1)S(1)}) fusion(bf16[2,64,8192]{2,1,0:T(8,128)(2,1)} %param.13, bf16[2,64,8192]{2,1,0:T(8,128)(2,1)} %param.12), kind=kLoop, calls=%fused_computation.2 | loop fusion | bytes 4194304 | tf_op jit(solution)/shard_map/squeeze | solution.py:124
  15.8 1.1 %collective-permute-done.2 = bf16[64,512]{1,0:T(8,128)(2,1)S(1)} collective-permute-done((bf16[64,512]{1,0:T(8,128)(2,1)S(1)}, bf16[64,512]{1,0:T(8,128)(2,1)S(1)}, u32[]{:S(2)}, u32[]{:S(2)}) %collective-permute-start.2) | collective-permute-done | bytes 65568 | tf_op jit(solution)/shard_map/ppermute | solution.py:26
  16.9 0.9 %collective-permute-start.4 = (bf16[128,512]{1,0:T(8,128)(2,1)S(1)}, bf16[128,512]{1,0:T(8,128)(2,1)S(1)}, u32[]{:S(2)}, u32[]{:S(2)}) collective-permute-start(bf16[128,512]{1,0:T(8,128)(2,1)S(1)} %pad_maximum_fusion.2.w0_ref), channel_id=1, source_target_pairs={{0,1},{1,0},{2,3},{3,2},{4,5},{5,4},{6,7},{7,6},{8,9},{9,8},{10,11... | collective-permute-start | bytes 393224 | tf_op jit(solution)/shard_map/ppermute | solution.py:26
  17.8 0.1 reshape.14
  17.9 0.1 copy.10
  18.0 0.1 eq.30
  18.1 1.6 %collective-permute-start.12 = (bf16[32,1024]{1,0:T(8,128)(2,1)S(1)}, bf16[32,1024]{1,0:T(8,128)(2,1)S(1)}, u32[]{:S(2)}, u32[]{:S(2)}) collective-permute-start(bf16[32,1024]{1,0:T(8,128)(2,1)S(1)} %slice.105), channel_id=1, source_target_pairs={{0,8},{2,10},{4,12},{6,14},{8,0},{10,2},{12,4},{14,6},{16,24},{18,... | collective-permute-start | bytes 196616 | tf_op jit(solution)/shard_map/ppermute | solution.py:26
  19.7 0.1 fusion.1
  19.8 1.3 %shard_map.94 = (bf16[16,8192]{1,0:T(8,128)(2,1)S(1)}, f32[16,8192]{1,0:T(8,128)S(1)}, bf16[16,8192]{1,0:T(8,128)(2,1)S(1)}) custom-call(bf16[256,256]{1,0:T(8,128)(2,1)S(1)} %get-tuple-element.77.place_ref, bf16[128,512]{1,0:T(8,128)(2,1)S(1)} %pad_maximum_fusion.2.w0_ref, bf16[128,512]{1,0:T(8,128)(2,1)S(1)} %collective-permute-done.3.w1_ref, ...), custom_call_target="tpu_custom_call" | custom-call | flops 1 | bytes 1 | tf_op jit(solution)/shard_map/pallas_call | solution.py:128
  21.1 1.3 %collective-permute-start.11 = (bf16[16,8192]{1,0:T(8,128)(2,1)S(1)}, bf16[16,8192]{1,0:T(8,128)(2,1)S(1)}, u32[]{:S(2)}, u32[]{:S(2)}) collective-permute-start(bf16[16,8192]{1,0:T(8,128)(2,1)S(1)} %get-tuple-element.42), channel_id=1, source_target_pairs={{0,1},{1,0},{2,3},{3,2},{4,5},{5,4},{6,7},{7,6},{8,9},{9,8},{10,11... | collective-permute-start | bytes 786440 | tf_op jit(solution)/shard_map/ppermute | solution.py:26
  22.3 0.9 %collective-permute-start.9 = (bf16[32,1536]{1,0:T(8,128)(2,1)S(1)}, bf16[32,1536]{1,0:T(8,128)(2,1)S(1)}, u32[]{:S(2)}, u32[]{:S(2)}) collective-permute-start(bf16[32,1536]{1,0:T(8,128)(2,1)S(1)} %slice.104), channel_id=1, source_target_pairs={{0,8},{2,10},{4,12},{6,14},{8,0},{10,2},{12,4},{14,6},{16,24},{18,... | collective-permute-start | bytes 294920 | tf_op jit(solution)/shard_map/ppermute | solution.py:26
  23.3 1.6 %collective-permute-start.14 = (bf16[64,512]{1,0:T(8,128)(2,1)S(1)}, bf16[64,512]{1,0:T(8,128)(2,1)S(1)}, u32[]{:S(2)}, u32[]{:S(2)}) collective-permute-start(bf16[64,512]{1,0:T(8,128)(2,1)S(1)} %get-tuple-element.66), channel_id=1, source_target_pairs={{0,4},{2,6},{4,0},{6,2},{8,12},{10,14},{12,8},{14,10},{16,20},{18,... | collective-permute-start | bytes 196616 | tf_op jit(solution)/shard_map/ppermute | solution.py:26
  24.9 0.5 collective-permute-start.13
  25.4 1.3 %shard_map.95 = (bf16[16,8192]{1,0:T(8,128)(2,1)S(1)}, f32[16,8192]{1,0:T(8,128)S(1)}, bf16[16,8192]{1,0:T(8,128)(2,1)S(1)}) custom-call(bf16[256,256]{1,0:T(8,128)(2,1)S(1)} %get-tuple-element.77.place_ref, bf16[128,512]{1,0:T(8,128)(2,1)S(1)} %collective-permute-done.4.w0_ref, bf16[128,512]{1,0:T(8,128)(2,1)S(1)} %collective-permute-done.5.w1_ref, ...), custom_call_target="tpu_custom_call" | custom-call | flops 1 | bytes 1 | tf_op jit(solution)/shard_map/pallas_call | solution.py:128
  26.7 0.9 %collective-permute-start.6 = (bf16[16,8192]{1,0:T(8,128)(2,1)S(1)}, bf16[16,8192]{1,0:T(8,128)(2,1)S(1)}, u32[]{:S(2)}, u32[]{:S(2)}) collective-permute-start(bf16[16,8192]{1,0:T(8,128)(2,1)S(1)} %get-tuple-element.35), channel_id=1, source_target_pairs={{0,1},{1,0},{2,3},{3,2},{4,5},{5,4},{6,7},{7,6},{8,9},{9,8},{10,11... | collective-permute-start | bytes 786440 | tf_op jit(solution)/shard_map/ppermute | solution.py:26
  27.6 1.6 %collective-permute-start.10 = (bf16[64,1536]{1,0:T(8,128)(2,1)S(1)}, bf16[64,1536]{1,0:T(8,128)(2,1)S(1)}, u32[]{:S(2)}, u32[]{:S(2)}) collective-permute-start(bf16[64,1536]{1,0:T(8,128)(2,1)S(1)} %get-tuple-element.68), channel_id=1, source_target_pairs={{0,4},{2,6},{4,0},{6,2},{8,12},{10,14},{12,8},{14,10},{16,20},{18,... | collective-permute-start | bytes 589832 | tf_op jit(solution)/shard_map/ppermute | solution.py:26
  29.2 0.1 collective-permute-done.13
  29.4 0.5 collective-permute-start.15
  30.1 0.7 %collective-permute-done.16.rest_1_ = bf16[128,512]{1,0:T(8,128)(2,1)S(1)} collective-permute-done((bf16[128,512]{1,0:T(8,128)(2,1)S(1)}, bf16[128,512]{1,0:T(8,128)(2,1)S(1)}, u32[]{:S(2)}, u32[]{:S(2)}) %collective-permute-start.16) | collective-permute-done | bytes 131104 | tf_op jit(solution)/shard_map/ppermute | solution.py:26
  30.8 0.2 collective-permute-done.15.rest_0_
  31.0 1.8 %shard_map.96 = (bf16[128,512]{1,0:T(8,128)(2,1)S(1)}, bf16[128,512]{1,0:T(8,128)(2,1)S(1)}) custom-call(bf16[256,256]{1,0:T(8,128)(2,1)S(1)} %get-tuple-element.77.place_ref, bf16[256,256]{1,0:T(8,128)(2,1)S(1)} %get-tuple-element.76.back_ref, f32[16,8192]{1,0:T(8,128)S(1)} %get-tuple-element.45.part_ref, ...), custom_call_target="tpu_custom_call" | custom-call | flops 1 | bytes 1 | tf_op jit(solution)/shard_map/pallas_call | solution.py:128
  32.7 0.4 collective-permute-start.20
  33.1 1.0 %collective-permute-done.10 = bf16[64,1536]{1,0:T(8,128)(2,1)S(1)} collective-permute-done((bf16[64,1536]{1,0:T(8,128)(2,1)S(1)}, bf16[64,1536]{1,0:T(8,128)(2,1)S(1)}, u32[]{:S(2)}, u32[]{:S(2)}) %collective-permute-start.10) | collective-permute-done | bytes 196640 | tf_op jit(solution)/shard_map/ppermute | solution.py:26
  34.3 0.5 collective-permute-start.18
  34.8 0.1 collective-permute-start.17
  34.9 1.6 %collective-permute-start.21 = (bf16[64,512]{1,0:T(8,128)(2,1)S(1)}, bf16[64,512]{1,0:T(8,128)(2,1)S(1)}, u32[]{:S(2)}, u32[]{:S(2)}) collective-permute-start(bf16[64,512]{1,0:T(8,128)(2,1)S(1)} %slice.164), channel_id=1, source_target_pairs={{0,4},{2,6},{4,0},{6,2},{8,12},{10,14},{12,8},{14,10},{16,20},{18,... | collective-permute-start | bytes 196616 | tf_op jit(solution)/shard_map/ppermute | solution.py:26
  36.5 2.1 %shard_map.97 = (bf16[128,1024]{1,0:T(8,128)(2,1)S(1)}, bf16[128,1024]{1,0:T(8,128)(2,1)S(1)}, bf16[16,8192]{1,0:T(8,128)(2,1)}) custom-call(bf16[256,256]{1,0:T(8,128)(2,1)S(1)} %get-tuple-element.77.place_ref, bf16[256,256]{1,0:T(8,128)(2,1)S(1)} %get-tuple-element.76.back_ref, f32[16,8192]{1,0:T(8,128)S(1)} %get-tuple-element.34.part_ref, ...), custom_call_target="tpu_custom_call" | custom-call | flops 1 | bytes 1 | tf_op jit(solution)/shard_map/pallas_call | solution.py:128
  38.6 0.8 %collective-permute-done.21 = bf16[64,512]{1,0:T(8,128)(2,1)S(1)} collective-permute-done((bf16[64,512]{1,0:T(8,128)(2,1)S(1)}, bf16[64,512]{1,0:T(8,128)(2,1)S(1)}, u32[]{:S(2)}, u32[]{:S(2)}) %collective-permute-start.21) | collective-permute-done | bytes 65568 | tf_op jit(solution)/shard_map/ppermute | solution.py:26
  39.5 1.5 %collective-permute-done.22 = bf16[128,1024]{1,0:T(8,128)(2,1)S(1)} collective-permute-done((bf16[128,1024]{1,0:T(8,128)(2,1)S(1)}, bf16[128,1024]{1,0:T(8,128)(2,1)S(1)}, u32[]{:S(2)}, u32[]{:S(2)}) %collective-permute-start.22) | collective-permute-done | bytes 262176 | tf_op jit(solution)/shard_map/ppermute | solution.py:26
  41.1 1.6 %collective-permute-start.23 = (bf16[64,1024]{1,0:T(8,128)(2,1)S(1)}, bf16[64,1024]{1,0:T(8,128)(2,1)S(1)}, u32[]{:S(2)}, u32[]{:S(2)}) collective-permute-start(bf16[64,1024]{1,0:T(8,128)(2,1)S(1)} %slice.163), channel_id=1, source_target_pairs={{0,4},{2,6},{4,0},{6,2},{8,12},{10,14},{12,8},{14,10},{16,20},{18,... | collective-permute-start | bytes 393224 | tf_op jit(solution)/shard_map/ppermute | solution.py:26
  42.7 1.2 %collective-permute-start.24 = (bf16[64,512]{1,0:T(8,128)(2,1)S(1)}, bf16[64,512]{1,0:T(8,128)(2,1)S(1)}, u32[]{:S(2)}, u32[]{:S(2)}) collective-permute-start(bf16[64,512]{1,0:T(8,128)(2,1)S(1)} %slice_add_fusion.2), channel_id=1, source_target_pairs={{0,1},{1,0},{2,3},{3,2},{4,5},{5,4},{6,7},{7,6},{8,9},{9,8},{10,11... | collective-permute-start | bytes 196616 | tf_op jit(solution)/shard_map/ppermute | solution.py:26
  43.9 2.9 %collective-permute-done.23 = bf16[64,1024]{1,0:T(8,128)(2,1)S(1)} collective-permute-done((bf16[64,1024]{1,0:T(8,128)(2,1)S(1)}, bf16[64,1024]{1,0:T(8,128)(2,1)S(1)}, u32[]{:S(2)}, u32[]{:S(2)}) %collective-permute-start.23) | collective-permute-done | bytes 131104 | tf_op jit(solution)/shard_map/ppermute | solution.py:26
  46.8 0.2 collective-permute-done.24
  47.0 1.2 %collective-permute-start.25 = (bf16[32,1024]{1,0:T(8,128)(2,1)S(1)}, bf16[32,1024]{1,0:T(8,128)(2,1)S(1)}, u32[]{:S(2)}, u32[]{:S(2)}) collective-permute-start(bf16[32,1024]{1,0:T(8,128)(2,1)S(1)} %fusion.4), channel_id=1, source_target_pairs={{0,8},{2,10},{4,12},{6,14},{8,0},{10,2},{12,4},{14,6},{16,24},{18,... | collective-permute-start | bytes 196616 | tf_op jit(solution)/shard_map/ppermute | solution.py:26
  48.2 3.1 %collective-permute-done.25 = bf16[32,1024]{1,0:T(8,128)(2,1)S(1)} collective-permute-done((bf16[32,1024]{1,0:T(8,128)(2,1)S(1)}, bf16[32,1024]{1,0:T(8,128)(2,1)S(1)}, u32[]{:S(2)}, u32[]{:S(2)}) %collective-permute-start.25) | collective-permute-done | bytes 65568 | tf_op jit(solution)/shard_map/ppermute | solution.py:26
  51.3 2.5 %collective-permute-start.26 = (bf16[16,1024]{1,0:T(8,128)(2,1)S(1)}, bf16[16,1024]{1,0:T(8,128)(2,1)S(1)}, u32[]{:S(2)}, u32[]{:S(2)}) collective-permute-start(bf16[16,1024]{1,0:T(8,128)(2,1)S(1)} %slice.165), channel_id=1, source_target_pairs={{0,16},{2,18},{4,20},{6,22},{8,24},{10,26},{12,28},{14,30},{16,0},... | collective-permute-start | bytes 98312 | tf_op jit(solution)/shard_map/ppermute | solution.py:26
  53.9 2.3 %collective-permute-done.26 = bf16[16,1024]{1,0:T(8,128)(2,1)S(1)} collective-permute-done((bf16[16,1024]{1,0:T(8,128)(2,1)S(1)}, bf16[16,1024]{1,0:T(8,128)(2,1)S(1)}, u32[]{:S(2)}, u32[]{:S(2)}) %collective-permute-start.26) | collective-permute-done | bytes 32800 | tf_op jit(solution)/shard_map/ppermute | solution.py:26
  56.3 0.6 %fusion.10 = (f32[1,16,512]{2,1,0:T(8,128)}, f32[1,16,512]{2,1,0:T(8,128)}) fusion(f32[16,1024]{1,0:T(8,128)S(1)} %slice_add_fusion.3, f32[1,16,512]{2,1,0:T(8,128)S(1)} %copy-done.4, f32[1,16,512]{2,1,0:T(8,128)S(1)} %copy-done.3), kind=kLoop, calls=%fused_computation.50 | loop fusion | flops 73728 | bytes 196608 | tf_op jit(solution)/shard_map/broadcast_in_dim | solution.py:253
  (62 shorter events, 0.9 us)
Async XLA Ops:
  1.4 7.2 %collective-permute-start = (bf16[16,512]{1,0:T(8,128)(2,1)S(1)}, bf16[16,512]{1,0:T(8,128)(2,1)S(1)}, u32[]{:S(2)}, u32[]{:S(2)}) collective-permute-start(bf16[16,512]{1,0:T(8,128)(2,1)S(1)} %bitcast_convert_fusion), channel_id=1, source_target_pairs={{0,16},{2,18},{4,20},{6,22},{8,24},{10,26},{12,28},{14,30},{16,0},... | collective-permute-start | bytes 49160 | tf_op jit(solution)/shard_map/ppermute | solution.py:26
  7.0 4.0 %collective-permute-start.7 = (bf16[16,1024]{1,0:T(8,128)(2,1)S(1)}, bf16[16,1024]{1,0:T(8,128)(2,1)S(1)}, u32[]{:S(2)}, u32[]{:S(2)}) collective-permute-start(bf16[16,1024]{1,0:T(8,128)(2,1)S(1)} %pad_maximum_fusion.8), channel_id=1, source_target_pairs={{0,1},{1,0},{2,3},{3,2},{4,5},{5,4},{6,7},{7,6},{8,9},{9,8},{10,11... | collective-permute-start | bytes 98312 | tf_op jit(solution)/shard_map/ppermute | solution.py:26
  8.6 3.9 %collective-permute-start.1 = (bf16[32,512]{1,0:T(8,128)(2,1)S(1)}, bf16[32,512]{1,0:T(8,128)(2,1)S(1)}, u32[]{:S(2)}, u32[]{:S(2)}) collective-permute-start(bf16[32,512]{1,0:T(8,128)(2,1)S(1)} %pad_maximum_fusion.7), channel_id=1, source_target_pairs={{0,8},{2,10},{4,12},{6,14},{8,0},{10,2},{12,4},{14,6},{16,24},{18,... | collective-permute-start | bytes 98312 | tf_op jit(solution)/shard_map/ppermute | solution.py:26
  11.0 6.7 %collective-permute-start.8 = (bf16[16,2560]{1,0:T(8,128)(2,1)S(1)}, bf16[16,2560]{1,0:T(8,128)(2,1)S(1)}, u32[]{:S(2)}, u32[]{:S(2)}) collective-permute-start(bf16[16,2560]{1,0:T(8,128)(2,1)S(1)} %pad_maximum_fusion.4), channel_id=1, source_target_pairs={{0,16},{2,18},{4,20},{6,22},{8,24},{10,26},{12,28},{14,30},{16,0},... | collective-permute-start | bytes 245768 | tf_op jit(solution)/shard_map/ppermute | solution.py:26
  12.6 5.3 %copy-start.5 = (s32[256]{0:T(256)S(1)}, s32[256]{0:T(256)}, u32[]{:S(2)}) copy-start(s32[256]{0:T(256)} %param.10) | copy-start | bytes 3076
  12.6 4.3 %collective-permute-start.2 = (bf16[64,512]{1,0:T(8,128)(2,1)S(1)}, bf16[64,512]{1,0:T(8,128)(2,1)S(1)}, u32[]{:S(2)}, u32[]{:S(2)}) collective-permute-start(bf16[64,512]{1,0:T(8,128)(2,1)S(1)} %pad_maximum_fusion.6), channel_id=1, source_target_pairs={{0,4},{2,6},{4,0},{6,2},{8,12},{10,14},{12,8},{14,10},{16,20},{18,... | collective-permute-start | bytes 196616 | tf_op jit(solution)/shard_map/ppermute | solution.py:26
  16.9 6.3 %collective-permute-start.4 = (bf16[128,512]{1,0:T(8,128)(2,1)S(1)}, bf16[128,512]{1,0:T(8,128)(2,1)S(1)}, u32[]{:S(2)}, u32[]{:S(2)}) collective-permute-start(bf16[128,512]{1,0:T(8,128)(2,1)S(1)} %pad_maximum_fusion.2.w0_ref), channel_id=1, source_target_pairs={{0,1},{1,0},{2,3},{3,2},{4,5},{5,4},{6,7},{7,6},{8,9},{9,8},{10,11... | collective-permute-start | bytes 393224 | tf_op jit(solution)/shard_map/ppermute | solution.py:26
  17.8 2.0 %collective-permute-start.3 = (bf16[128,512]{1,0:T(8,128)(2,1)S(1)}, bf16[128,512]{1,0:T(8,128)(2,1)S(1)}, u32[]{:S(2)}, u32[]{:S(2)}) collective-permute-start(bf16[128,512]{1,0:T(8,128)(2,1)S(1)} %pad_maximum_fusion.2.w0_ref), channel_id=1, source_target_pairs={{0,2},{2,0},{4,6},{6,4},{8,10},{10,8},{12,14},{14,12},{16,18},{18,... | collective-permute-start | bytes 393224 | tf_op jit(solution)/shard_map/ppermute | solution.py:26
  18.1 5.2 %collective-permute-start.12 = (bf16[32,1024]{1,0:T(8,128)(2,1)S(1)}, bf16[32,1024]{1,0:T(8,128)(2,1)S(1)}, u32[]{:S(2)}, u32[]{:S(2)}) collective-permute-start(bf16[32,1024]{1,0:T(8,128)(2,1)S(1)} %slice.105), channel_id=1, source_target_pairs={{0,8},{2,10},{4,12},{6,14},{8,0},{10,2},{12,4},{14,6},{16,24},{18,... | collective-permute-start | bytes 196616 | tf_op jit(solution)/shard_map/ppermute | solution.py:26
  21.1 9.0 %collective-permute-start.11 = (bf16[16,8192]{1,0:T(8,128)(2,1)S(1)}, bf16[16,8192]{1,0:T(8,128)(2,1)S(1)}, u32[]{:S(2)}, u32[]{:S(2)}) collective-permute-start(bf16[16,8192]{1,0:T(8,128)(2,1)S(1)} %get-tuple-element.42), channel_id=1, source_target_pairs={{0,1},{1,0},{2,3},{3,2},{4,5},{5,4},{6,7},{7,6},{8,9},{9,8},{10,11... | collective-permute-start | bytes 786440 | tf_op jit(solution)/shard_map/ppermute | solution.py:26
  22.3 5.2 %collective-permute-start.9 = (bf16[32,1536]{1,0:T(8,128)(2,1)S(1)}, bf16[32,1536]{1,0:T(8,128)(2,1)S(1)}, u32[]{:S(2)}, u32[]{:S(2)}) collective-permute-start(bf16[32,1536]{1,0:T(8,128)(2,1)S(1)} %slice.104), channel_id=1, source_target_pairs={{0,8},{2,10},{4,12},{6,14},{8,0},{10,2},{12,4},{14,6},{16,24},{18,... | collective-permute-start | bytes 294920 | tf_op jit(solution)/shard_map/ppermute | solution.py:26
  23.2 2.2 %collective-permute-start.5 = (bf16[128,512]{1,0:T(8,128)(2,1)S(1)}, bf16[128,512]{1,0:T(8,128)(2,1)S(1)}, u32[]{:S(2)}, u32[]{:S(2)}) collective-permute-start(bf16[128,512]{1,0:T(8,128)(2,1)S(1)} %collective-permute-done.4.w0_ref), channel_id=1, source_target_pairs={{0,2},{2,0},{4,6},{6,4},{8,10},{10,8},{12,14},{14,12},{16,18},{18,... | collective-permute-start | bytes 393224 | tf_op jit(solution)/shard_map/ppermute | solution.py:26
  23.3 6.6 %copy-start.1 = (bf16[2,64,8192]{2,1,0:T(8,128)(2,1)S(1)}, bf16[2,64,8192]{2,1,0:T(8,128)(2,1)}, u32[]{:S(2)}) copy-start(bf16[2,64,8192]{2,1,0:T(8,128)(2,1)} %param.12) | copy-start | bytes 6291460
  23.3 5.8 %collective-permute-start.14 = (bf16[64,512]{1,0:T(8,128)(2,1)S(1)}, bf16[64,512]{1,0:T(8,128)(2,1)S(1)}, u32[]{:S(2)}, u32[]{:S(2)}) collective-permute-start(bf16[64,512]{1,0:T(8,128)(2,1)S(1)} %get-tuple-element.66), channel_id=1, source_target_pairs={{0,4},{2,6},{4,0},{6,2},{8,12},{10,14},{12,8},{14,10},{16,20},{18,... | collective-permute-start | bytes 196616 | tf_op jit(solution)/shard_map/ppermute | solution.py:26
  24.9 4.4 %collective-permute-start.13 = (bf16[64,512]{1,0:T(8,128)(2,1)S(1)}, bf16[64,512]{1,0:T(8,128)(2,1)S(1)}, u32[]{:S(2)}, u32[]{:S(2)}) collective-permute-start(bf16[64,512]{1,0:T(8,128)(2,1)S(1)} %get-tuple-element.67), channel_id=1, source_target_pairs={{0,4},{2,6},{4,0},{6,2},{8,12},{10,14},{12,8},{14,10},{16,20},{18,... | collective-permute-start | bytes 196616 | tf_op jit(solution)/shard_map/ppermute | solution.py:26
  26.7 3.3 %copy-start.2 = (bf16[2,64,8192]{2,1,0:T(8,128)(2,1)S(1)}, bf16[2,64,8192]{2,1,0:T(8,128)(2,1)}, u32[]{:S(2)}) copy-start(bf16[2,64,8192]{2,1,0:T(8,128)(2,1)} %param.13) | copy-start | bytes 6291460
  26.7 9.8 %collective-permute-start.6 = (bf16[16,8192]{1,0:T(8,128)(2,1)S(1)}, bf16[16,8192]{1,0:T(8,128)(2,1)S(1)}, u32[]{:S(2)}, u32[]{:S(2)}) collective-permute-start(bf16[16,8192]{1,0:T(8,128)(2,1)S(1)} %get-tuple-element.35), channel_id=1, source_target_pairs={{0,1},{1,0},{2,3},{3,2},{4,5},{5,4},{6,7},{7,6},{8,9},{9,8},{10,11... | collective-permute-start | bytes 786440 | tf_op jit(solution)/shard_map/ppermute | solution.py:26
  27.6 6.5 %collective-permute-start.10 = (bf16[64,1536]{1,0:T(8,128)(2,1)S(1)}, bf16[64,1536]{1,0:T(8,128)(2,1)S(1)}, u32[]{:S(2)}, u32[]{:S(2)}) collective-permute-start(bf16[64,1536]{1,0:T(8,128)(2,1)S(1)} %get-tuple-element.68), channel_id=1, source_target_pairs={{0,4},{2,6},{4,0},{6,2},{8,12},{10,14},{12,8},{14,10},{16,20},{18,... | collective-permute-start | bytes 589832 | tf_op jit(solution)/shard_map/ppermute | solution.py:26
  29.4 1.4 %collective-permute-start.16 = (bf16[128,512]{1,0:T(8,128)(2,1)S(1)}, bf16[128,512]{1,0:T(8,128)(2,1)S(1)}, u32[]{:S(2)}, u32[]{:S(2)}) collective-permute-start(bf16[128,512]{1,0:T(8,128)(2,1)S(1)} %get-tuple-element.64), channel_id=1, source_target_pairs={{0,2},{2,0},{4,6},{6,4},{8,10},{10,8},{12,14},{14,12},{16,18},{18,... | collective-permute-start | bytes 393224 | tf_op jit(solution)/shard_map/ppermute | solution.py:26
  29.4 1.5 %collective-permute-start.15 = (bf16[128,512]{1,0:T(8,128)(2,1)S(1)}, bf16[128,512]{1,0:T(8,128)(2,1)S(1)}, u32[]{:S(2)}, u32[]{:S(2)}) collective-permute-start(bf16[128,512]{1,0:T(8,128)(2,1)S(1)} %get-tuple-element.65), channel_id=1, source_target_pairs={{0,2},{2,0},{4,6},{6,4},{8,10},{10,8},{12,14},{14,12},{16,18},{18,... | collective-permute-start | bytes 393224 | tf_op jit(solution)/shard_map/ppermute | solution.py:26
  31.0 5.5 %copy-start = (bf16[1,2,8,8192]{3,2,1,0:T(8,128)(2,1)S(1)}, bf16[1,2,8,8192]{3,2,1,0:T(8,128)(2,1)}, u32[]{:S(2)}) copy-start(bf16[1,2,8,8192]{3,2,1,0:T(8,128)(2,1)} %param.11) | copy-start | bytes 786436
  32.7 2.1 %collective-permute-start.20 = (bf16[128,512]{1,0:T(8,128)(2,1)S(1)}, bf16[128,512]{1,0:T(8,128)(2,1)S(1)}, u32[]{:S(2)}, u32[]{:S(2)}) collective-permute-start(bf16[128,512]{1,0:T(8,128)(2,1)S(1)} %get-tuple-element.55), channel_id=1, source_target_pairs={{0,2},{2,0},{4,6},{6,4},{8,10},{10,8},{12,14},{14,12},{16,18},{18,... | collective-permute-start | bytes 393224 | tf_op jit(solution)/shard_map/ppermute | solution.py:26
  34.2 2.3 %collective-permute-start.19 = (bf16[128,512]{1,0:T(8,128)(2,1)S(1)}, bf16[128,512]{1,0:T(8,128)(2,1)S(1)}, u32[]{:S(2)}, u32[]{:S(2)}) collective-permute-start(bf16[128,512]{1,0:T(8,128)(2,1)S(1)} %get-tuple-element.59), channel_id=1, source_target_pairs={{0,2},{2,0},{4,6},{6,4},{8,10},{10,8},{12,14},{14,12},{16,18},{18,... | collective-permute-start | bytes 393224 | tf_op jit(solution)/shard_map/ppermute | solution.py:26
  34.3 2.2 %collective-permute-start.18 = (bf16[128,512]{1,0:T(8,128)(2,1)S(1)}, bf16[128,512]{1,0:T(8,128)(2,1)S(1)}, u32[]{:S(2)}, u32[]{:S(2)}) collective-permute-start(bf16[128,512]{1,0:T(8,128)(2,1)S(1)} %get-tuple-element.60), channel_id=1, source_target_pairs={{0,2},{2,0},{4,6},{6,4},{8,10},{10,8},{12,14},{14,12},{16,18},{18,... | collective-permute-start | bytes 393224 | tf_op jit(solution)/shard_map/ppermute | solution.py:26
  34.8 1.7 %collective-permute-start.17 = (bf16[128,512]{1,0:T(8,128)(2,1)S(1)}, bf16[128,512]{1,0:T(8,128)(2,1)S(1)}, u32[]{:S(2)}, u32[]{:S(2)}) collective-permute-start(bf16[128,512]{1,0:T(8,128)(2,1)S(1)} %get-tuple-element.61), channel_id=1, source_target_pairs={{0,2},{2,0},{4,6},{6,4},{8,10},{10,8},{12,14},{14,12},{16,18},{18,... | collective-permute-start | bytes 393224 | tf_op jit(solution)/shard_map/ppermute | solution.py:26
  34.9 4.5 %collective-permute-start.21 = (bf16[64,512]{1,0:T(8,128)(2,1)S(1)}, bf16[64,512]{1,0:T(8,128)(2,1)S(1)}, u32[]{:S(2)}, u32[]{:S(2)}) collective-permute-start(bf16[64,512]{1,0:T(8,128)(2,1)S(1)} %slice.164), channel_id=1, source_target_pairs={{0,4},{2,6},{4,0},{6,2},{8,12},{10,14},{12,8},{14,10},{16,20},{18,... | collective-permute-start | bytes 196616 | tf_op jit(solution)/shard_map/ppermute | solution.py:26
  38.6 17.7 %copy-start.3 = (f32[1,16,512]{2,1,0:T(8,128)S(1)}, f32[1,16,512]{2,1,0:T(8,128)}, u32[]{:S(2)}) copy-start(f32[1,16,512]{2,1,0:T(8,128)} %param.7) | copy-start | bytes 98308
  38.6 17.7 %copy-start.4 = (f32[1,16,512]{2,1,0:T(8,128)S(1)}, f32[1,16,512]{2,1,0:T(8,128)}, u32[]{:S(2)}) copy-start(f32[1,16,512]{2,1,0:T(8,128)} %param.9) | copy-start | bytes 98308
  39.4 1.6 %collective-permute-start.22 = (bf16[128,1024]{1,0:T(8,128)(2,1)S(1)}, bf16[128,1024]{1,0:T(8,128)(2,1)S(1)}, u32[]{:S(2)}, u32[]{:S(2)}) collective-permute-start(bf16[128,1024]{1,0:T(8,128)(2,1)S(1)} %get-tuple-element.57), channel_id=1, source_target_pairs={{0,2},{2,0},{4,6},{6,4},{8,10},{10,8},{12,14},{14,12},{16,18},{18,... | collective-permute-start | bytes 786440 | tf_op jit(solution)/shard_map/ppermute | solution.py:26
  41.1 5.6 %collective-permute-start.23 = (bf16[64,1024]{1,0:T(8,128)(2,1)S(1)}, bf16[64,1024]{1,0:T(8,128)(2,1)S(1)}, u32[]{:S(2)}, u32[]{:S(2)}) collective-permute-start(bf16[64,1024]{1,0:T(8,128)(2,1)S(1)} %slice.163), channel_id=1, source_target_pairs={{0,4},{2,6},{4,0},{6,2},{8,12},{10,14},{12,8},{14,10},{16,20},{18,... | collective-permute-start | bytes 393224 | tf_op jit(solution)/shard_map/ppermute | solution.py:26
  42.7 4.3 %collective-permute-start.24 = (bf16[64,512]{1,0:T(8,128)(2,1)S(1)}, bf16[64,512]{1,0:T(8,128)(2,1)S(1)}, u32[]{:S(2)}, u32[]{:S(2)}) collective-permute-start(bf16[64,512]{1,0:T(8,128)(2,1)S(1)} %slice_add_fusion.2), channel_id=1, source_target_pairs={{0,1},{1,0},{2,3},{3,2},{4,5},{5,4},{6,7},{7,6},{8,9},{9,8},{10,11... | collective-permute-start | bytes 196616 | tf_op jit(solution)/shard_map/ppermute | solution.py:26
  47.0 4.3 %collective-permute-start.25 = (bf16[32,1024]{1,0:T(8,128)(2,1)S(1)}, bf16[32,1024]{1,0:T(8,128)(2,1)S(1)}, u32[]{:S(2)}, u32[]{:S(2)}) collective-permute-start(bf16[32,1024]{1,0:T(8,128)(2,1)S(1)} %fusion.4), channel_id=1, source_target_pairs={{0,8},{2,10},{4,12},{6,14},{8,0},{10,2},{12,4},{14,6},{16,24},{18,... | collective-permute-start | bytes 196616 | tf_op jit(solution)/shard_map/ppermute | solution.py:26
  51.3 4.9 %collective-permute-start.26 = (bf16[16,1024]{1,0:T(8,128)(2,1)S(1)}, bf16[16,1024]{1,0:T(8,128)(2,1)S(1)}, u32[]{:S(2)}, u32[]{:S(2)}) collective-permute-start(bf16[16,1024]{1,0:T(8,128)(2,1)S(1)} %slice.165), channel_id=1, source_target_pairs={{0,16},{2,18},{4,20},{6,22},{8,24},{10,26},{12,28},{14,30},{16,0},... | collective-permute-start | bytes 98312 | tf_op jit(solution)/shard_map/ppermute | solution.py:26

commit v14 on v13

--- a/solution.py
+++ b/solution.py
@@ -30,9 +30,9 @@
     return lax.optimization_barrier((x, *others))[0]
 
 
-def halve(total, mask, *others):
+def halve(total, mask):
     count = total.shape[0] // 2
-    return total[:count] + after(swap(total[count:].astype(BF), "dp", mask), *others).astype(F32)
+    return total[:count] + swap(total[count:].astype(BF), "dp", mask).astype(F32)
 
 
 def bits_of(n, lowest=1):
@@ -229,14 +229,10 @@
             scratch,
         )
         event = result[0]
-        if own:
-            sums[1:] = [halve(p, far[-1], event) for p in sums[1:]]
-            away, error = after(result[1], *sums[1:]), result[2]
-        else:
-            away = result[1]
-        sums[k] = result[0].astype(F32) + swap(away, "dp", 1).astype(F32)
-    sums[0] = halve(sums[0], far[-1])
-
+        sums[k] = result[0].astype(F32) + swap(result[1], "dp", 1).astype(F32)
+    error = result[2]
+
+    sums = [halve(p, far[-1]) for p in sums]
     grads = [sums[0][:, :segment]] + sums[1:]
     for mask in mp_bits:
         crossed = [swap(p.astype(BF), "mp", mask).astype(F32) for p in grads[mask:]]

time: 57.3 us -> 57.7 us (level)
  transfers between devices with their start and end apart: 27 -> 27, of which waited for: 13 -> 15; matrix products, arithmetic and copies ran while one was open for 7% -> 7% of each run, Pallas kernels for 11% -> 11%
where the time goes in v14:
time: 57.7 us; the launch traced here: 57.3 us
  starting transfers between devices  28.7 us (50%)
  waiting for transfers between devices  15.6 us (27%)
  Pallas kernels  6.34 us (11%)
  other arithmetic  3.39 us (6%)
  local copies, waits for them, and re-layouts  2.23 us (4%)
  between operations  0.96 us (2%)
    ppermute x27, starting transfers between devices, swap(): return lax.ppermute(x, axis, [(i, i ^ mask) for i in range(n)])  28.7 us
    ppermute x27, waiting for transfers between devices, swap(): return lax.ppermute(x, axis, [(i, i ^ mask) for i in range(n)])  15.6 us
    pallas_call x4, Pallas kernels, call(): pl.pallas_call(kernel, out_shape=out_shape, in_specs=[pl.BlockSpec(memory...  6.34 us
    squeeze x3, local copies, waits for them, and re-layouts, tokens_of(): x[step]  1.81 us
  transfers between devices with their start and end apart: 27, of which 15 were waited for; matrix products, arithmetic and copies ran while one was open for 7% of the time, Pallas kernels for 11%

profile of v14, /device:TPU:0, one launch (start us, length us, event | category | flops | bytes accessed | tf_op | source)
XLA Modules:
  0.0 57.3 jit_solution(10267636705440355412)
XLA Ops:
  0.6 0.8 %bitcast_convert_fusion = bf16[16,512]{1,0:T(8,128)(2,1)S(1)} fusion(f32[1,16,512]{2,1,0:T(8,128)} %param.7), kind=kLoop, calls=%fused_computation.42 | loop fusion | flops 8192 | bytes 49152 | tf_op jit(solution)/shard_map/convert_element_type | solution.py:151
  1.4 4.0 %collective-permute-start = (bf16[16,512]{1,0:T(8,128)(2,1)S(1)}, bf16[16,512]{1,0:T(8,128)(2,1)S(1)}, u32[]{:S(2)}, u32[]{:S(2)}) collective-permute-start(bf16[16,512]{1,0:T(8,128)(2,1)S(1)} %bitcast_convert_fusion), channel_id=1, source_target_pairs={{0,16},{2,18},{4,20},{6,22},{8,24},{10,26},{12,28},{14,30},{16,0},... | collective-permute-start | bytes 49160 | tf_op jit(solution)/shard_map/ppermute | solution.py:26
  5.4 0.8 %convert_bitcast_fusion = bf16[16,512]{1,0:T(8,128)(2,1)S(1)} fusion(f32[1,16,512]{2,1,0:T(8,128)} %param.9), kind=kLoop, calls=%fused_computation.50 | loop fusion | flops 8192 | bytes 49152 | tf_op jit(solution)/shard_map/convert.5
  6.2 0.8 %fusion.7 = (bf16[16,512]{1,0:T(8,128)(2,1)S(1)}, bf16[16,512]{1,0:T(8,128)(2,1)S(1)}) fusion(f32[16,512]{1,0:T(8,128)} %bitcast.28), kind=kLoop, calls=%fused_computation.34 | loop fusion | flops 32768 | bytes 65536 | tf_op jit(solution)/shard_map/convert_element_type | solution.py:154
  7.0 1.6 %collective-permute-start.7 = (bf16[16,1024]{1,0:T(8,128)(2,1)S(1)}, bf16[16,1024]{1,0:T(8,128)(2,1)S(1)}, u32[]{:S(2)}, u32[]{:S(2)}) collective-permute-start(bf16[16,1024]{1,0:T(8,128)(2,1)S(1)} %pad_maximum_fusion.8), channel_id=1, source_target_pairs={{0,1},{1,0},{2,3},{3,2},{4,5},{5,4},{6,7},{7,6},{8,9},{9,8},{10,11... | collective-permute-start | bytes 98312 | tf_op jit(solution)/shard_map/ppermute | solution.py:26
  8.6 1.6 %collective-permute-start.1 = (bf16[32,512]{1,0:T(8,128)(2,1)S(1)}, bf16[32,512]{1,0:T(8,128)(2,1)S(1)}, u32[]{:S(2)}, u32[]{:S(2)}) collective-permute-start(bf16[32,512]{1,0:T(8,128)(2,1)S(1)} %pad_maximum_fusion.7), channel_id=1, source_target_pairs={{0,8},{2,10},{4,12},{6,14},{8,0},{10,2},{12,4},{14,6},{16,24},{18,... | collective-permute-start | bytes 98312 | tf_op jit(solution)/shard_map/ppermute | solution.py:26
  10.2 0.8 %collective-permute-done.7 = bf16[16,1024]{1,0:T(8,128)(2,1)S(1)} collective-permute-done((bf16[16,1024]{1,0:T(8,128)(2,1)S(1)}, bf16[16,1024]{1,0:T(8,128)(2,1)S(1)}, u32[]{:S(2)}, u32[]{:S(2)}) %collective-permute-start.7) | collective-permute-done | bytes 32800 | tf_op jit(solution)/shard_map/ppermute | solution.py:26
  11.0 0.8 %collective-permute-start.8 = (bf16[16,2560]{1,0:T(8,128)(2,1)S(1)}, bf16[16,2560]{1,0:T(8,128)(2,1)S(1)}, u32[]{:S(2)}, u32[]{:S(2)}) collective-permute-start(bf16[16,2560]{1,0:T(8,128)(2,1)S(1)} %pad_maximum_fusion.4), channel_id=1, source_target_pairs={{0,16},{2,18},{4,20},{6,22},{8,24},{10,26},{12,28},{14,30},{16,0},... | collective-permute-start | bytes 245768 | tf_op jit(solution)/shard_map/ppermute | solution.py:26
  11.8 0.7 %collective-permute-done.1 = bf16[32,512]{1,0:T(8,128)(2,1)S(1)} collective-permute-done((bf16[32,512]{1,0:T(8,128)(2,1)S(1)}, bf16[32,512]{1,0:T(8,128)(2,1)S(1)}, u32[]{:S(2)}, u32[]{:S(2)}) %collective-permute-start.1) | collective-permute-done | bytes 32800 | tf_op jit(solution)/shard_map/ppermute | solution.py:26
  12.6 1.6 %collective-permute-start.2 = (bf16[64,512]{1,0:T(8,128)(2,1)S(1)}, bf16[64,512]{1,0:T(8,128)(2,1)S(1)}, u32[]{:S(2)}, u32[]{:S(2)}) collective-permute-start(bf16[64,512]{1,0:T(8,128)(2,1)S(1)} %pad_maximum_fusion.6), channel_id=1, source_target_pairs={{0,4},{2,6},{4,0},{6,2},{8,12},{10,14},{12,8},{14,10},{16,20},{18,... | collective-permute-start | bytes 196616 | tf_op jit(solution)/shard_map/ppermute | solution.py:26
  14.1 1.7 %slice_bitcast_fusion.2 = (bf16[64,8192]{1,0:T(8,128)(2,1)S(1)}, bf16[64,8192]{1,0:T(8,128)(2,1)S(1)}) fusion(bf16[2,64,8192]{2,1,0:T(8,128)(2,1)} %param.13, bf16[2,64,8192]{2,1,0:T(8,128)(2,1)} %param.12), kind=kLoop, calls=%fused_computation.2 | loop fusion | bytes 4194304 | tf_op jit(solution)/shard_map/squeeze | solution.py:124
  15.8 1.1 %collective-permute-done.2 = bf16[64,512]{1,0:T(8,128)(2,1)S(1)} collective-permute-done((bf16[64,512]{1,0:T(8,128)(2,1)S(1)}, bf16[64,512]{1,0:T(8,128)(2,1)S(1)}, u32[]{:S(2)}, u32[]{:S(2)}) %collective-permute-start.2) | collective-permute-done | bytes 65568 | tf_op jit(solution)/shard_map/ppermute | solution.py:26
  16.9 0.9 %collective-permute-start.4 = (bf16[128,512]{1,0:T(8,128)(2,1)S(1)}, bf16[128,512]{1,0:T(8,128)(2,1)S(1)}, u32[]{:S(2)}, u32[]{:S(2)}) collective-permute-start(bf16[128,512]{1,0:T(8,128)(2,1)S(1)} %pad_maximum_fusion.2.w0_ref), channel_id=1, source_target_pairs={{0,1},{1,0},{2,3},{3,2},{4,5},{5,4},{6,7},{7,6},{8,9},{9,8},{10,11... | collective-permute-start | bytes 393224 | tf_op jit(solution)/shard_map/ppermute | solution.py:26
  18.0 0.1 eq.30
  18.1 1.6 %collective-permute-start.12 = (bf16[32,1024]{1,0:T(8,128)(2,1)S(1)}, bf16[32,1024]{1,0:T(8,128)(2,1)S(1)}, u32[]{:S(2)}, u32[]{:S(2)}) collective-permute-start(bf16[32,1024]{1,0:T(8,128)(2,1)S(1)} %slice.105), channel_id=1, source_target_pairs={{0,8},{2,10},{4,12},{6,14},{8,0},{10,2},{12,4},{14,6},{16,24},{18,... | collective-permute-start | bytes 196616 | tf_op jit(solution)/shard_map/ppermute | solution.py:26
  19.7 0.1 fusion.1
  19.8 1.3 %shard_map.94 = (bf16[16,8192]{1,0:T(8,128)(2,1)S(1)}, f32[16,8192]{1,0:T(8,128)S(1)}, bf16[16,8192]{1,0:T(8,128)(2,1)S(1)}) custom-call(bf16[256,256]{1,0:T(8,128)(2,1)S(1)} %get-tuple-element.73.place_ref, bf16[128,512]{1,0:T(8,128)(2,1)S(1)} %pad_maximum_fusion.2.w0_ref, bf16[128,512]{1,0:T(8,128)(2,1)S(1)} %collective-permute-done.3.w1_ref, ...), custom_call_target="tpu_custom_call" | custom-call | flops 1 | bytes 1 | tf_op jit(solution)/shard_map/pallas_call | solution.py:128
  21.1 1.3 %collective-permute-start.11 = (bf16[16,8192]{1,0:T(8,128)(2,1)S(1)}, bf16[16,8192]{1,0:T(8,128)(2,1)S(1)}, u32[]{:S(2)}, u32[]{:S(2)}) collective-permute-start(bf16[16,8192]{1,0:T(8,128)(2,1)S(1)} %get-tuple-element.40), channel_id=1, source_target_pairs={{0,1},{1,0},{2,3},{3,2},{4,5},{5,4},{6,7},{7,6},{8,9},{9,8},{10,11... | collective-permute-start | bytes 786440 | tf_op jit(solution)/shard_map/ppermute | solution.py:26
  22.3 0.9 %collective-permute-start.9 = (bf16[32,1536]{1,0:T(8,128)(2,1)S(1)}, bf16[32,1536]{1,0:T(8,128)(2,1)S(1)}, u32[]{:S(2)}, u32[]{:S(2)}) collective-permute-start(bf16[32,1536]{1,0:T(8,128)(2,1)S(1)} %slice.104), channel_id=1, source_target_pairs={{0,8},{2,10},{4,12},{6,14},{8,0},{10,2},{12,4},{14,6},{16,24},{18,... | collective-permute-start | bytes 294920 | tf_op jit(solution)/shard_map/ppermute | solution.py:26
  23.3 1.6 %collective-permute-start.14 = (bf16[64,512]{1,0:T(8,128)(2,1)S(1)}, bf16[64,512]{1,0:T(8,128)(2,1)S(1)}, u32[]{:S(2)}, u32[]{:S(2)}) collective-permute-start(bf16[64,512]{1,0:T(8,128)(2,1)S(1)} %get-tuple-element.62), channel_id=1, source_target_pairs={{0,4},{2,6},{4,0},{6,2},{8,12},{10,14},{12,8},{14,10},{16,20},{18,... | collective-permute-start | bytes 196616 | tf_op jit(solution)/shard_map/ppermute | solution.py:26
  24.9 0.5 collective-permute-start.13
  25.4 1.3 %shard_map.95 = (bf16[16,8192]{1,0:T(8,128)(2,1)S(1)}, f32[16,8192]{1,0:T(8,128)S(1)}, bf16[16,8192]{1,0:T(8,128)(2,1)S(1)}) custom-call(bf16[256,256]{1,0:T(8,128)(2,1)S(1)} %get-tuple-element.73.place_ref, bf16[128,512]{1,0:T(8,128)(2,1)S(1)} %collective-permute-done.4.w0_ref, bf16[128,512]{1,0:T(8,128)(2,1)S(1)} %collective-permute-done.5.w1_ref, ...), custom_call_target="tpu_custom_call" | custom-call | flops 1 | bytes 1 | tf_op jit(solution)/shard_map/pallas_call | solution.py:128
  26.7 0.9 %collective-permute-start.6 = (bf16[16,8192]{1,0:T(8,128)(2,1)S(1)}, bf16[16,8192]{1,0:T(8,128)(2,1)S(1)}, u32[]{:S(2)}, u32[]{:S(2)}) collective-permute-start(bf16[16,8192]{1,0:T(8,128)(2,1)S(1)} %get-tuple-element.33), channel_id=1, source_target_pairs={{0,1},{1,0},{2,3},{3,2},{4,5},{5,4},{6,7},{7,6},{8,9},{9,8},{10,11... | collective-permute-start | bytes 786440 | tf_op jit(solution)/shard_map/ppermute | solution.py:26
  27.6 1.6 %collective-permute-start.10 = (bf16[64,1536]{1,0:T(8,128)(2,1)S(1)}, bf16[64,1536]{1,0:T(8,128)(2,1)S(1)}, u32[]{:S(2)}, u32[]{:S(2)}) collective-permute-start(bf16[64,1536]{1,0:T(8,128)(2,1)S(1)} %get-tuple-element.64), channel_id=1, source_target_pairs={{0,4},{2,6},{4,0},{6,2},{8,12},{10,14},{12,8},{14,10},{16,20},{18,... | collective-permute-start | bytes 589832 | tf_op jit(solution)/shard_map/ppermute | solution.py:26
  29.2 0.1 collective-permute-done.13
  29.4 0.5 collective-permute-start.15
  30.1 0.7 %collective-permute-done.16.rest_1_ = bf16[128,512]{1,0:T(8,128)(2,1)S(1)} collective-permute-done((bf16[128,512]{1,0:T(8,128)(2,1)S(1)}, bf16[128,512]{1,0:T(8,128)(2,1)S(1)}, u32[]{:S(2)}, u32[]{:S(2)}) %collective-permute-start.16) | collective-permute-done | bytes 131104 | tf_op jit(solution)/shard_map/ppermute | solution.py:26
  30.8 0.2 collective-permute-done.15.rest_0_
  31.0 1.8 %shard_map.96 = (bf16[128,512]{1,0:T(8,128)(2,1)S(1)}, bf16[128,512]{1,0:T(8,128)(2,1)S(1)}) custom-call(bf16[256,256]{1,0:T(8,128)(2,1)S(1)} %get-tuple-element.73.place_ref, bf16[256,256]{1,0:T(8,128)(2,1)S(1)} %get-tuple-element.72.back_ref, f32[16,8192]{1,0:T(8,128)S(1)} %get-tuple-element.43.part_ref, ...), custom_call_target="tpu_custom_call" | custom-call | flops 1 | bytes 1 | tf_op jit(solution)/shard_map/pallas_call | solution.py:128
  32.7 1.4 %collective-permute-done.10 = bf16[64,1536]{1,0:T(8,128)(2,1)S(1)} collective-permute-done((bf16[64,1536]{1,0:T(8,128)(2,1)S(1)}, bf16[64,1536]{1,0:T(8,128)(2,1)S(1)}, u32[]{:S(2)}, u32[]{:S(2)}) %collective-permute-start.10) | collective-permute-done | bytes 196640 | tf_op jit(solution)/shard_map/ppermute | solution.py:26
  34.3 0.5 collective-permute-start.18
  34.8 0.4 collective-permute-start.22
  35.3 0.3 collective-permute-done.19.rest_2_
  35.6 0.2 collective-permute-done.18.rest_1_
  35.8 0.3 collective-permute-done.17.rest_0_
  36.1 2.1 %shard_map.97 = (bf16[128,1024]{1,0:T(8,128)(2,1)S(1)}, bf16[128,1024]{1,0:T(8,128)(2,1)S(1)}, bf16[16,8192]{1,0:T(8,128)(2,1)}) custom-call(bf16[256,256]{1,0:T(8,128)(2,1)S(1)} %get-tuple-element.73.place_ref, bf16[256,256]{1,0:T(8,128)(2,1)S(1)} %get-tuple-element.72.back_ref, f32[16,8192]{1,0:T(8,128)S(1)} %get-tuple-element.32.part_ref, ...), custom_call_target="tpu_custom_call" | custom-call | flops 1 | bytes 1 | tf_op jit(solution)/shard_map/pallas_call | solution.py:128
  38.2 0.3 collective-permute-start.20
  38.5 1.6 %collective-permute-start.23 = (bf16[64,512]{1,0:T(8,128)(2,1)S(1)}, bf16[64,512]{1,0:T(8,128)(2,1)S(1)}, u32[]{:S(2)}, u32[]{:S(2)}) collective-permute-start(bf16[64,512]{1,0:T(8,128)(2,1)S(1)} %slice.166), channel_id=1, source_target_pairs={{0,4},{2,6},{4,0},{6,2},{8,12},{10,14},{12,8},{14,10},{16,20},{18,... | collective-permute-start | bytes 196616 | tf_op jit(solution)/shard_map/ppermute | solution.py:26
  40.2 1.3 %collective-permute-start.21 = (bf16[64,1024]{1,0:T(8,128)(2,1)S(1)}, bf16[64,1024]{1,0:T(8,128)(2,1)S(1)}, u32[]{:S(2)}, u32[]{:S(2)}) collective-permute-start(bf16[64,1024]{1,0:T(8,128)(2,1)S(1)} %slice.165), channel_id=1, source_target_pairs={{0,4},{2,6},{4,0},{6,2},{8,12},{10,14},{12,8},{14,10},{16,20},{18,... | collective-permute-start | bytes 393224 | tf_op jit(solution)/shard_map/ppermute | solution.py:26
  41.4 1.6 %collective-permute-done.23 = bf16[64,512]{1,0:T(8,128)(2,1)S(1)} collective-permute-done((bf16[64,512]{1,0:T(8,128)(2,1)S(1)}, bf16[64,512]{1,0:T(8,128)(2,1)S(1)}, u32[]{:S(2)}, u32[]{:S(2)}) %collective-permute-start.23) | collective-permute-done | bytes 65568 | tf_op jit(solution)/shard_map/ppermute | solution.py:26
  43.0 1.3 %collective-permute-start.24 = (bf16[64,512]{1,0:T(8,128)(2,1)S(1)}, bf16[64,512]{1,0:T(8,128)(2,1)S(1)}, u32[]{:S(2)}, u32[]{:S(2)}) collective-permute-start(bf16[64,512]{1,0:T(8,128)(2,1)S(1)} %fusion.5), channel_id=1, source_target_pairs={{0,1},{1,0},{2,3},{3,2},{4,5},{5,4},{6,7},{7,6},{8,9},{9,8},{10,11... | collective-permute-start | bytes 196616 | tf_op jit(solution)/shard_map/ppermute | solution.py:26
  44.3 1.4 %collective-permute-done.21 = bf16[64,1024]{1,0:T(8,128)(2,1)S(1)} collective-permute-done((bf16[64,1024]{1,0:T(8,128)(2,1)S(1)}, bf16[64,1024]{1,0:T(8,128)(2,1)S(1)}, u32[]{:S(2)}, u32[]{:S(2)}) %collective-permute-start.21) | collective-permute-done | bytes 131104 | tf_op jit(solution)/shard_map/ppermute | solution.py:26
  45.8 1.6 %collective-permute-done.24 = bf16[64,512]{1,0:T(8,128)(2,1)S(1)} collective-permute-done((bf16[64,512]{1,0:T(8,128)(2,1)S(1)}, bf16[64,512]{1,0:T(8,128)(2,1)S(1)}, u32[]{:S(2)}, u32[]{:S(2)}) %collective-permute-start.24) | collective-permute-done | bytes 65568 | tf_op jit(solution)/shard_map/ppermute | solution.py:26
  47.4 1.2 %collective-permute-start.25 = (bf16[32,1024]{1,0:T(8,128)(2,1)S(1)}, bf16[32,1024]{1,0:T(8,128)(2,1)S(1)}, u32[]{:S(2)}, u32[]{:S(2)}) collective-permute-start(bf16[32,1024]{1,0:T(8,128)(2,1)S(1)} %fusion.4), channel_id=1, source_target_pairs={{0,8},{2,10},{4,12},{6,14},{8,0},{10,2},{12,4},{14,6},{16,24},{18,... | collective-permute-start | bytes 196616 | tf_op jit(solution)/shard_map/ppermute | solution.py:26
  48.6 3.1 %collective-permute-done.25 = bf16[32,1024]{1,0:T(8,128)(2,1)S(1)} collective-permute-done((bf16[32,1024]{1,0:T(8,128)(2,1)S(1)}, bf16[32,1024]{1,0:T(8,128)(2,1)S(1)}, u32[]{:S(2)}, u32[]{:S(2)}) %collective-permute-start.25) | collective-permute-done | bytes 65568 | tf_op jit(solution)/shard_map/ppermute | solution.py:26
  51.8 2.9 %collective-permute-start.26 = (bf16[16,1024]{1,0:T(8,128)(2,1)S(1)}, bf16[16,1024]{1,0:T(8,128)(2,1)S(1)}, u32[]{:S(2)}, u32[]{:S(2)}) collective-permute-start(bf16[16,1024]{1,0:T(8,128)(2,1)S(1)} %slice.167), channel_id=1, source_target_pairs={{0,16},{2,18},{4,20},{6,22},{8,24},{10,26},{12,28},{14,30},{16,0},... | collective-permute-start | bytes 98312 | tf_op jit(solution)/shard_map/ppermute | solution.py:26
  54.6 2.0 %collective-permute-done.26 = bf16[16,1024]{1,0:T(8,128)(2,1)S(1)} collective-permute-done((bf16[16,1024]{1,0:T(8,128)(2,1)S(1)}, bf16[16,1024]{1,0:T(8,128)(2,1)S(1)}, u32[]{:S(2)}, u32[]{:S(2)}) %collective-permute-start.26) | collective-permute-done | bytes 32800 | tf_op jit(solution)/shard_map/ppermute | solution.py:26
  56.7 0.6 %fusion.11 = (f32[1,16,512]{2,1,0:T(8,128)}, f32[1,16,512]{2,1,0:T(8,128)}) fusion(f32[16,1024]{1,0:T(8,128)S(1)} %slice_add_fusion.3, f32[1,16,512]{2,1,0:T(8,128)S(1)} %copy-done.4, f32[1,16,512]{2,1,0:T(8,128)S(1)} %copy-done.3), kind=kLoop, calls=%fused_computation.51 | loop fusion | flops 73728 | bytes 196608 | tf_op jit(solution)/shard_map/broadcast_in_dim | solution.py:249
  (62 shorter events, 1.0 us)
Async XLA Ops:
  1.4 7.2 %collective-permute-start = (bf16[16,512]{1,0:T(8,128)(2,1)S(1)}, bf16[16,512]{1,0:T(8,128)(2,1)S(1)}, u32[]{:S(2)}, u32[]{:S(2)}) collective-permute-start(bf16[16,512]{1,0:T(8,128)(2,1)S(1)} %bitcast_convert_fusion), channel_id=1, source_target_pairs={{0,16},{2,18},{4,20},{6,22},{8,24},{10,26},{12,28},{14,30},{16,0},... | collective-permute-start | bytes 49160 | tf_op jit(solution)/shard_map/ppermute | solution.py:26
  7.0 4.0 %collective-permute-start.7 = (bf16[16,1024]{1,0:T(8,128)(2,1)S(1)}, bf16[16,1024]{1,0:T(8,128)(2,1)S(1)}, u32[]{:S(2)}, u32[]{:S(2)}) collective-permute-start(bf16[16,1024]{1,0:T(8,128)(2,1)S(1)} %pad_maximum_fusion.8), channel_id=1, source_target_pairs={{0,1},{1,0},{2,3},{3,2},{4,5},{5,4},{6,7},{7,6},{8,9},{9,8},{10,11... | collective-permute-start | bytes 98312 | tf_op jit(solution)/shard_map/ppermute | solution.py:26
  8.6 3.9 %collective-permute-start.1 = (bf16[32,512]{1,0:T(8,128)(2,1)S(1)}, bf16[32,512]{1,0:T(8,128)(2,1)S(1)}, u32[]{:S(2)}, u32[]{:S(2)}) collective-permute-start(bf16[32,512]{1,0:T(8,128)(2,1)S(1)} %pad_maximum_fusion.7), channel_id=1, source_target_pairs={{0,8},{2,10},{4,12},{6,14},{8,0},{10,2},{12,4},{14,6},{16,24},{18,... | collective-permute-start | bytes 98312 | tf_op jit(solution)/shard_map/ppermute | solution.py:26
  11.0 6.7 %collective-permute-start.8 = (bf16[16,2560]{1,0:T(8,128)(2,1)S(1)}, bf16[16,2560]{1,0:T(8,128)(2,1)S(1)}, u32[]{:S(2)}, u32[]{:S(2)}) collective-permute-start(bf16[16,2560]{1,0:T(8,128)(2,1)S(1)} %pad_maximum_fusion.4), channel_id=1, source_target_pairs={{0,16},{2,18},{4,20},{6,22},{8,24},{10,26},{12,28},{14,30},{16,0},... | collective-permute-start | bytes 245768 | tf_op jit(solution)/shard_map/ppermute | solution.py:26
  12.6 5.3 %copy-start.5 = (s32[256]{0:T(256)S(1)}, s32[256]{0:T(256)}, u32[]{:S(2)}) copy-start(s32[256]{0:T(256)} %param.10) | copy-start | bytes 3076
  12.6 4.3 %collective-permute-start.2 = (bf16[64,512]{1,0:T(8,128)(2,1)S(1)}, bf16[64,512]{1,0:T(8,128)(2,1)S(1)}, u32[]{:S(2)}, u32[]{:S(2)}) collective-permute-start(bf16[64,512]{1,0:T(8,128)(2,1)S(1)} %pad_maximum_fusion.6), channel_id=1, source_target_pairs={{0,4},{2,6},{4,0},{6,2},{8,12},{10,14},{12,8},{14,10},{16,20},{18,... | collective-permute-start | bytes 196616 | tf_op jit(solution)/shard_map/ppermute | solution.py:26
  16.9 6.3 %collective-permute-start.4 = (bf16[128,512]{1,0:T(8,128)(2,1)S(1)}, bf16[128,512]{1,0:T(8,128)(2,1)S(1)}, u32[]{:S(2)}, u32[]{:S(2)}) collective-permute-start(bf16[128,512]{1,0:T(8,128)(2,1)S(1)} %pad_maximum_fusion.2.w0_ref), channel_id=1, source_target_pairs={{0,1},{1,0},{2,3},{3,2},{4,5},{5,4},{6,7},{7,6},{8,9},{9,8},{10,11... | collective-permute-start | bytes 393224 | tf_op jit(solution)/shard_map/ppermute | solution.py:26
  17.8 2.0 %collective-permute-start.3 = (bf16[128,512]{1,0:T(8,128)(2,1)S(1)}, bf16[128,512]{1,0:T(8,128)(2,1)S(1)}, u32[]{:S(2)}, u32[]{:S(2)}) collective-permute-start(bf16[128,512]{1,0:T(8,128)(2,1)S(1)} %pad_maximum_fusion.2.w0_ref), channel_id=1, source_target_pairs={{0,2},{2,0},{4,6},{6,4},{8,10},{10,8},{12,14},{14,12},{16,18},{18,... | collective-permute-start | bytes 393224 | tf_op jit(solution)/shard_map/ppermute | solution.py:26
  18.1 5.2 %collective-permute-start.12 = (bf16[32,1024]{1,0:T(8,128)(2,1)S(1)}, bf16[32,1024]{1,0:T(8,128)(2,1)S(1)}, u32[]{:S(2)}, u32[]{:S(2)}) collective-permute-start(bf16[32,1024]{1,0:T(8,128)(2,1)S(1)} %slice.105), channel_id=1, source_target_pairs={{0,8},{2,10},{4,12},{6,14},{8,0},{10,2},{12,4},{14,6},{16,24},{18,... | collective-permute-start | bytes 196616 | tf_op jit(solution)/shard_map/ppermute | solution.py:26
  21.1 9.0 %collective-permute-start.11 = (bf16[16,8192]{1,0:T(8,128)(2,1)S(1)}, bf16[16,8192]{1,0:T(8,128)(2,1)S(1)}, u32[]{:S(2)}, u32[]{:S(2)}) collective-permute-start(bf16[16,8192]{1,0:T(8,128)(2,1)S(1)} %get-tuple-element.40), channel_id=1, source_target_pairs={{0,1},{1,0},{2,3},{3,2},{4,5},{5,4},{6,7},{7,6},{8,9},{9,8},{10,11... | collective-permute-start | bytes 786440 | tf_op jit(solution)/shard_map/ppermute | solution.py:26
  22.3 5.2 %collective-permute-start.9 = (bf16[32,1536]{1,0:T(8,128)(2,1)S(1)}, bf16[32,1536]{1,0:T(8,128)(2,1)S(1)}, u32[]{:S(2)}, u32[]{:S(2)}) collective-permute-start(bf16[32,1536]{1,0:T(8,128)(2,1)S(1)} %slice.104), channel_id=1, source_target_pairs={{0,8},{2,10},{4,12},{6,14},{8,0},{10,2},{12,4},{14,6},{16,24},{18,... | collective-permute-start | bytes 294920 | tf_op jit(solution)/shard_map/ppermute | solution.py:26
  23.2 2.2 %collective-permute-start.5 = (bf16[128,512]{1,0:T(8,128)(2,1)S(1)}, bf16[128,512]{1,0:T(8,128)(2,1)S(1)}, u32[]{:S(2)}, u32[]{:S(2)}) collective-permute-start(bf16[128,512]{1,0:T(8,128)(2,1)S(1)} %collective-permute-done.4.w0_ref), channel_id=1, source_target_pairs={{0,2},{2,0},{4,6},{6,4},{8,10},{10,8},{12,14},{14,12},{16,18},{18,... | collective-permute-start | bytes 393224 | tf_op jit(solution)/shard_map/ppermute | solution.py:26
  23.3 6.6 %copy-start.1 = (bf16[2,64,8192]{2,1,0:T(8,128)(2,1)S(1)}, bf16[2,64,8192]{2,1,0:T(8,128)(2,1)}, u32[]{:S(2)}) copy-start(bf16[2,64,8192]{2,1,0:T(8,128)(2,1)} %param.12) | copy-start | bytes 6291460
  23.3 5.8 %collective-permute-start.14 = (bf16[64,512]{1,0:T(8,128)(2,1)S(1)}, bf16[64,512]{1,0:T(8,128)(2,1)S(1)}, u32[]{:S(2)}, u32[]{:S(2)}) collective-permute-start(bf16[64,512]{1,0:T(8,128)(2,1)S(1)} %get-tuple-element.62), channel_id=1, source_target_pairs={{0,4},{2,6},{4,0},{6,2},{8,12},{10,14},{12,8},{14,10},{16,20},{18,... | collective-permute-start | bytes 196616 | tf_op jit(solution)/shard_map/ppermute | solution.py:26
  24.9 4.4 %collective-permute-start.13 = (bf16[64,512]{1,0:T(8,128)(2,1)S(1)}, bf16[64,512]{1,0:T(8,128)(2,1)S(1)}, u32[]{:S(2)}, u32[]{:S(2)}) collective-permute-start(bf16[64,512]{1,0:T(8,128)(2,1)S(1)} %get-tuple-element.63), channel_id=1, source_target_pairs={{0,4},{2,6},{4,0},{6,2},{8,12},{10,14},{12,8},{14,10},{16,20},{18,... | collective-permute-start | bytes 196616 | tf_op jit(solution)/shard_map/ppermute | solution.py:26
  26.7 3.3 %copy-start.2 = (bf16[2,64,8192]{2,1,0:T(8,128)(2,1)S(1)}, bf16[2,64,8192]{2,1,0:T(8,128)(2,1)}, u32[]{:S(2)}) copy-start(bf16[2,64,8192]{2,1,0:T(8,128)(2,1)} %param.13) | copy-start | bytes 6291460
  26.7 8.6 %collective-permute-start.6 = (bf16[16,8192]{1,0:T(8,128)(2,1)S(1)}, bf16[16,8192]{1,0:T(8,128)(2,1)S(1)}, u32[]{:S(2)}, u32[]{:S(2)}) collective-permute-start(bf16[16,8192]{1,0:T(8,128)(2,1)S(1)} %get-tuple-element.33), channel_id=1, source_target_pairs={{0,1},{1,0},{2,3},{3,2},{4,5},{5,4},{6,7},{7,6},{8,9},{9,8},{10,11... | collective-permute-start | bytes 786440 | tf_op jit(solution)/shard_map/ppermute | solution.py:26
  27.6 6.5 %collective-permute-start.10 = (bf16[64,1536]{1,0:T(8,128)(2,1)S(1)}, bf16[64,1536]{1,0:T(8,128)(2,1)S(1)}, u32[]{:S(2)}, u32[]{:S(2)}) collective-permute-start(bf16[64,1536]{1,0:T(8,128)(2,1)S(1)} %get-tuple-element.64), channel_id=1, source_target_pairs={{0,4},{2,6},{4,0},{6,2},{8,12},{10,14},{12,8},{14,10},{16,20},{18,... | collective-permute-start | bytes 589832 | tf_op jit(solution)/shard_map/ppermute | solution.py:26
  29.4 1.4 %collective-permute-start.16 = (bf16[128,512]{1,0:T(8,128)(2,1)S(1)}, bf16[128,512]{1,0:T(8,128)(2,1)S(1)}, u32[]{:S(2)}, u32[]{:S(2)}) collective-permute-start(bf16[128,512]{1,0:T(8,128)(2,1)S(1)} %get-tuple-element.60), channel_id=1, source_target_pairs={{0,2},{2,0},{4,6},{6,4},{8,10},{10,8},{12,14},{14,12},{16,18},{18,... | collective-permute-start | bytes 393224 | tf_op jit(solution)/shard_map/ppermute | solution.py:26
  29.4 1.5 %collective-permute-start.15 = (bf16[128,512]{1,0:T(8,128)(2,1)S(1)}, bf16[128,512]{1,0:T(8,128)(2,1)S(1)}, u32[]{:S(2)}, u32[]{:S(2)}) collective-permute-start(bf16[128,512]{1,0:T(8,128)(2,1)S(1)} %get-tuple-element.61), channel_id=1, source_target_pairs={{0,2},{2,0},{4,6},{6,4},{8,10},{10,8},{12,14},{14,12},{16,18},{18,... | collective-permute-start | bytes 393224 | tf_op jit(solution)/shard_map/ppermute | solution.py:26
  31.0 5.2 %copy-start = (bf16[1,2,8,8192]{3,2,1,0:T(8,128)(2,1)S(1)}, bf16[1,2,8,8192]{3,2,1,0:T(8,128)(2,1)}, u32[]{:S(2)}) copy-start(bf16[1,2,8,8192]{3,2,1,0:T(8,128)(2,1)} %param.11) | copy-start | bytes 786436
  34.2 1.4 %collective-permute-start.19 = (bf16[128,512]{1,0:T(8,128)(2,1)S(1)}, bf16[128,512]{1,0:T(8,128)(2,1)S(1)}, u32[]{:S(2)}, u32[]{:S(2)}) collective-permute-start(bf16[128,512]{1,0:T(8,128)(2,1)S(1)} %get-tuple-element.55), channel_id=1, source_target_pairs={{0,2},{2,0},{4,6},{6,4},{8,10},{10,8},{12,14},{14,12},{16,18},{18,... | collective-permute-start | bytes 393224 | tf_op jit(solution)/shard_map/ppermute | solution.py:26
  34.3 1.5 %collective-permute-start.18 = (bf16[128,512]{1,0:T(8,128)(2,1)S(1)}, bf16[128,512]{1,0:T(8,128)(2,1)S(1)}, u32[]{:S(2)}, u32[]{:S(2)}) collective-permute-start(bf16[128,512]{1,0:T(8,128)(2,1)S(1)} %get-tuple-element.56), channel_id=1, source_target_pairs={{0,2},{2,0},{4,6},{6,4},{8,10},{10,8},{12,14},{14,12},{16,18},{18,... | collective-permute-start | bytes 393224 | tf_op jit(solution)/shard_map/ppermute | solution.py:26
  34.8 1.3 %collective-permute-start.17 = (bf16[128,512]{1,0:T(8,128)(2,1)S(1)}, bf16[128,512]{1,0:T(8,128)(2,1)S(1)}, u32[]{:S(2)}, u32[]{:S(2)}) collective-permute-start(bf16[128,512]{1,0:T(8,128)(2,1)S(1)} %get-tuple-element.57), channel_id=1, source_target_pairs={{0,2},{2,0},{4,6},{6,4},{8,10},{10,8},{12,14},{14,12},{16,18},{18,... | collective-permute-start | bytes 393224 | tf_op jit(solution)/shard_map/ppermute | solution.py:26
  34.8 3.6 %collective-permute-start.22 = (bf16[128,512]{1,0:T(8,128)(2,1)S(1)}, bf16[128,512]{1,0:T(8,128)(2,1)S(1)}, u32[]{:S(2)}, u32[]{:S(2)}) collective-permute-start(bf16[128,512]{1,0:T(8,128)(2,1)S(1)} %get-tuple-element.53), channel_id=1, source_target_pairs={{0,2},{2,0},{4,6},{6,4},{8,10},{10,8},{12,14},{14,12},{16,18},{18,... | collective-permute-start | bytes 393224 | tf_op jit(solution)/shard_map/ppermute | solution.py:26
  38.2 1.9 %collective-permute-start.20 = (bf16[128,1024]{1,0:T(8,128)(2,1)S(1)}, bf16[128,1024]{1,0:T(8,128)(2,1)S(1)}, u32[]{:S(2)}, u32[]{:S(2)}) collective-permute-start(bf16[128,1024]{1,0:T(8,128)(2,1)S(1)} %get-tuple-element.52), channel_id=1, source_target_pairs={{0,2},{2,0},{4,6},{6,4},{8,10},{10,8},{12,14},{14,12},{16,18},{18,... | collective-permute-start | bytes 786440 | tf_op jit(solution)/shard_map/ppermute | solution.py:26
  38.5 18.2 %copy-start.3 = (f32[1,16,512]{2,1,0:T(8,128)S(1)}, f32[1,16,512]{2,1,0:T(8,128)}, u32[]{:S(2)}) copy-start(f32[1,16,512]{2,1,0:T(8,128)} %param.7) | copy-start | bytes 98308
  38.5 18.2 %copy-start.4 = (f32[1,16,512]{2,1,0:T(8,128)S(1)}, f32[1,16,512]{2,1,0:T(8,128)}, u32[]{:S(2)}) copy-start(f32[1,16,512]{2,1,0:T(8,128)} %param.9) | copy-start | bytes 98308
  38.5 4.5 %collective-permute-start.23 = (bf16[64,512]{1,0:T(8,128)(2,1)S(1)}, bf16[64,512]{1,0:T(8,128)(2,1)S(1)}, u32[]{:S(2)}, u32[]{:S(2)}) collective-permute-start(bf16[64,512]{1,0:T(8,128)(2,1)S(1)} %slice.166), channel_id=1, source_target_pairs={{0,4},{2,6},{4,0},{6,2},{8,12},{10,14},{12,8},{14,10},{16,20},{18,... | collective-permute-start | bytes 196616 | tf_op jit(solution)/shard_map/ppermute | solution.py:26
  40.2 5.5 %collective-permute-start.21 = (bf16[64,1024]{1,0:T(8,128)(2,1)S(1)}, bf16[64,1024]{1,0:T(8,128)(2,1)S(1)}, u32[]{:S(2)}, u32[]{:S(2)}) collective-permute-start(bf16[64,1024]{1,0:T(8,128)(2,1)S(1)} %slice.165), channel_id=1, source_target_pairs={{0,4},{2,6},{4,0},{6,2},{8,12},{10,14},{12,8},{14,10},{16,20},{18,... | collective-permute-start | bytes 393224 | tf_op jit(solution)/shard_map/ppermute | solution.py:26
  43.0 4.3 %collective-permute-start.24 = (bf16[64,512]{1,0:T(8,128)(2,1)S(1)}, bf16[64,512]{1,0:T(8,128)(2,1)S(1)}, u32[]{:S(2)}, u32[]{:S(2)}) collective-permute-start(bf16[64,512]{1,0:T(8,128)(2,1)S(1)} %fusion.5), channel_id=1, source_target_pairs={{0,1},{1,0},{2,3},{3,2},{4,5},{5,4},{6,7},{7,6},{8,9},{9,8},{10,11... | collective-permute-start | bytes 196616 | tf_op jit(solution)/shard_map/ppermute | solution.py:26
  47.4 4.3 %collective-permute-start.25 = (bf16[32,1024]{1,0:T(8,128)(2,1)S(1)}, bf16[32,1024]{1,0:T(8,128)(2,1)S(1)}, u32[]{:S(2)}, u32[]{:S(2)}) collective-permute-start(bf16[32,1024]{1,0:T(8,128)(2,1)S(1)} %fusion.4), channel_id=1, source_target_pairs={{0,8},{2,10},{4,12},{6,14},{8,0},{10,2},{12,4},{14,6},{16,24},{18,... | collective-permute-start | bytes 196616 | tf_op jit(solution)/shard_map/ppermute | solution.py:26
  51.8 4.9 %collective-permute-start.26 = (bf16[16,1024]{1,0:T(8,128)(2,1)S(1)}, bf16[16,1024]{1,0:T(8,128)(2,1)S(1)}, u32[]{:S(2)}, u32[]{:S(2)}) collective-permute-start(bf16[16,1024]{1,0:T(8,128)(2,1)S(1)} %slice.167), channel_id=1, source_target_pairs={{0,16},{2,18},{4,20},{6,22},{8,24},{10,26},{12,28},{14,30},{16,0},... | collective-permute-start | bytes 98312 | tf_op jit(solution)/shard_map/ppermute | solution.py:26

commit v15 on v12

--- a/solution.py
+++ b/solution.py
@@ -144,9 +144,8 @@
     shape = jax.ShapeDtypeStruct
 
     near_w = master[0].astype(BF)
-    spans = jnp.concatenate([after(moment[0], near_w), variance[0]], axis=1)
+    spans = jnp.pad(after(moment[0], near_w), ((0, 0), (0, segment))) + jnp.pad(variance[0], ((0, 0), (segment, 0)))
     near_a = spans.astype(BF)
-    low = (spans[:, :segment] - lax.reduce_precision(spans[:, :segment], 8, 7)).astype(BF)
     steps = []
     for mask in far:
         near_w = jnp.concatenate([near_w, swap(near_w, "dp", mask)], axis=0)
@@ -154,6 +153,8 @@
     blocks_a = [near_a]
     for mask in reversed(mp_bits):
         blocks_a = blocks_a + [swap(b, "mp", mask) for b in blocks_a]
+    exact = after(moment[0], steps[0])
+    low = (exact - lax.reduce_precision(exact, 8, 7)).astype(BF)
     all_a = after(jnp.concatenate([near_a, low] + blocks_a[1:], axis=1), steps[0])
 
     slot = after(flat_slot, steps[-1])

time: 56.9 us -> 57.2 us (level)
  waiting for transfers between devices: 12.2 us -> 15.6 us
  starting transfers between devices: 31.5 us -> 28.4 us
    ppermute x28, waiting for transfers between devices: 12.2 us -> 15.6 us  [swap(): return lax.ppermute(x, axis, [(i, i ^ mask) for i in range(n)])]
    ppermute x28, starting transfers between devices: 31.5 us -> 28.4 us  [swap(): return lax.ppermute(x, axis, [(i, i ^ mask) for i in range(n)])]
    another operation x1 -> x0, other arithmetic: 0.76 us -> none
    convert_element_type x1 -> x2, other arithmetic: 0.84 us -> 1.54 us  [the longest x1 0.78 us: per_device(): near_a = spans.astype(BF)]
  transfers between devices with their start and end apart: 28 -> 28, of which waited for: 17 -> 16; matrix products, arithmetic and copies ran while one was open for 7% -> 7% of each run, Pallas kernels for 11% -> 11%
where the time goes in v15:
time: 57.2 us; the launch traced here: 56.9 us
  starting transfers between devices  28.4 us (50%)
  waiting for transfers between devices  15.6 us (27%)
  Pallas kernels  6.34 us (11%)
  other arithmetic  3.31 us (6%)
  local copies, waits for them, and re-layouts  2.24 us (4%)
  between operations  0.98 us (2%)
    ppermute x28, starting transfers between devices, swap(): return lax.ppermute(x, axis, [(i, i ^ mask) for i in range(n)])  28.4 us
    ppermute x28, waiting for transfers between devices, swap(): return lax.ppermute(x, axis, [(i, i ^ mask) for i in range(n)])  15.6 us
    pallas_call x4, Pallas kernels, call(): pl.pallas_call(kernel, out_shape=out_shape, in_specs=[pl.BlockSpec(memory...  6.34 us
    squeeze x3, local copies, waits for them, and re-layouts, tokens_of(): x[step]  1.81 us
  transfers between devices with their start and end apart: 28, of which 16 were waited for; matrix products, arithmetic and copies ran while one was open for 7% of the time, Pallas kernels for 11%

profile of v15, /device:TPU:0, one launch (start us, length us, event | category | flops | bytes accessed | tf_op | source)
XLA Modules:
  0.0 56.9 jit_solution(11772080656278575433)
XLA Ops:
  0.6 0.8 %bitcast_convert_fusion = bf16[16,512]{1,0:T(8,128)(2,1)S(1)} fusion(f32[1,16,512]{2,1,0:T(8,128)} %param.7), kind=kLoop, calls=%fused_computation.37 | loop fusion | flops 8192 | bytes 49152 | tf_op jit(solution)/shard_map/convert_element_type | solution.py:146
  1.4 4.0 %collective-permute-start = (bf16[16,512]{1,0:T(8,128)(2,1)S(1)}, bf16[16,512]{1,0:T(8,128)(2,1)S(1)}, u32[]{:S(2)}, u32[]{:S(2)}) collective-permute-start(bf16[16,512]{1,0:T(8,128)(2,1)S(1)} %bitcast_convert_fusion), channel_id=1, source_target_pairs={{0,16},{2,18},{4,20},{6,22},{8,24},{10,26},{12,28},{14,30},{16,0},... | collective-permute-start | bytes 49160 | tf_op jit(solution)/shard_map/ppermute | solution.py:26
  5.4 0.8 %add_convert_fusion = bf16[16,1024]{1,0:T(8,128)(2,1)S(1)} fusion(f32[16,512]{1,0:T(8,128)} %bitcast.26, f32[16,512]{1,0:T(8,128)} %bitcast.24), kind=kLoop, calls=%fused_computation.26 | loop fusion | flops 32768 | bytes 98304 | tf_op jit(solution)/shard_map/convert_element_type | solution.py:148
  6.2 1.5 %collective-permute-start.7 = (bf16[16,1024]{1,0:T(8,128)(2,1)S(1)}, bf16[16,1024]{1,0:T(8,128)(2,1)S(1)}, u32[]{:S(2)}, u32[]{:S(2)}) collective-permute-start(bf16[16,1024]{1,0:T(8,128)(2,1)S(1)} %add_convert_fusion), channel_id=1, source_target_pairs={{0,1},{1,0},{2,3},{3,2},{4,5},{5,4},{6,7},{7,6},{8,9},{9,8},{10,11... | collective-permute-start | bytes 98312 | tf_op jit(solution)/shard_map/ppermute | solution.py:26
  7.7 1.6 %collective-permute-start.1 = (bf16[32,512]{1,0:T(8,128)(2,1)S(1)}, bf16[32,512]{1,0:T(8,128)(2,1)S(1)}, u32[]{:S(2)}, u32[]{:S(2)}) collective-permute-start(bf16[32,512]{1,0:T(8,128)(2,1)S(1)} %pad_maximum_fusion.6), channel_id=1, source_target_pairs={{0,8},{2,10},{4,12},{6,14},{8,0},{10,2},{12,4},{14,6},{16,24},{18,... | collective-permute-start | bytes 98312 | tf_op jit(solution)/shard_map/ppermute | solution.py:26
  9.3 0.8 %fusion.2 = bf16[16,512]{1,0:T(8,128)(2,1)S(1)} fusion(f32[16,512]{1,0:T(8,128)} %bitcast.25), kind=kLoop, calls=%fused_computation.28 | loop fusion | flops 24576 | bytes 49152 | tf_op jit(solution)/shard_map/convert_element_type | solution.py:157
  10.1 2.4 %collective-permute-start.8 = (bf16[16,2560]{1,0:T(8,128)(2,1)S(1)}, bf16[16,2560]{1,0:T(8,128)(2,1)S(1)}, u32[]{:S(2)}, u32[]{:S(2)}) collective-permute-start(bf16[16,2560]{1,0:T(8,128)(2,1)S(1)} %pad_maximum_fusion.4), channel_id=1, source_target_pairs={{0,16},{2,18},{4,20},{6,22},{8,24},{10,26},{12,28},{14,30},{16,0},... | collective-permute-start | bytes 245768 | tf_op jit(solution)/shard_map/ppermute | solution.py:26
  12.6 1.6 %collective-permute-start.2 = (bf16[64,512]{1,0:T(8,128)(2,1)S(1)}, bf16[64,512]{1,0:T(8,128)(2,1)S(1)}, u32[]{:S(2)}, u32[]{:S(2)}) collective-permute-start(bf16[64,512]{1,0:T(8,128)(2,1)S(1)} %pad_maximum_fusion.5), channel_id=1, source_target_pairs={{0,4},{2,6},{4,0},{6,2},{8,12},{10,14},{12,8},{14,10},{16,20},{18,... | collective-permute-start | bytes 196616 | tf_op jit(solution)/shard_map/ppermute | solution.py:26
  14.2 1.7 %slice_bitcast_fusion.2 = (bf16[64,8192]{1,0:T(8,128)(2,1)S(1)}, bf16[64,8192]{1,0:T(8,128)(2,1)S(1)}) fusion(bf16[2,64,8192]{2,1,0:T(8,128)(2,1)} %param.13, bf16[2,64,8192]{2,1,0:T(8,128)(2,1)} %param.12), kind=kLoop, calls=%fused_computation.2 | loop fusion | bytes 4194304 | tf_op jit(solution)/shard_map/squeeze | solution.py:119
  15.8 1.1 %collective-permute-done.2 = bf16[64,512]{1,0:T(8,128)(2,1)S(1)} collective-permute-done((bf16[64,512]{1,0:T(8,128)(2,1)S(1)}, bf16[64,512]{1,0:T(8,128)(2,1)S(1)}, u32[]{:S(2)}, u32[]{:S(2)}) %collective-permute-start.2) | collective-permute-done | bytes 65568 | tf_op jit(solution)/shard_map/ppermute | solution.py:26
  17.0 1.6 %collective-permute-start.4 = (bf16[128,512]{1,0:T(8,128)(2,1)S(1)}, bf16[128,512]{1,0:T(8,128)(2,1)S(1)}, u32[]{:S(2)}, u32[]{:S(2)}) collective-permute-start(bf16[128,512]{1,0:T(8,128)(2,1)S(1)} %pad_maximum_fusion.2.w0_ref), channel_id=1, source_target_pairs={{0,1},{1,0},{2,3},{3,2},{4,5},{5,4},{6,7},{7,6},{8,9},{9,8},{10,11... | collective-permute-start | bytes 393224 | tf_op jit(solution)/shard_map/ppermute | solution.py:26
  18.8 0.1 eq.30
  18.9 0.4 collective-permute-start.12
  19.3 0.1 fusion.1
  19.4 1.3 %shard_map.94 = (bf16[16,8192]{1,0:T(8,128)(2,1)S(1)}, f32[16,8192]{1,0:T(8,128)S(1)}, bf16[16,8192]{1,0:T(8,128)(2,1)S(1)}) custom-call(bf16[256,256]{1,0:T(8,128)(2,1)S(1)} %get-tuple-element.61.place_ref, bf16[128,512]{1,0:T(8,128)(2,1)S(1)} %pad_maximum_fusion.2.w0_ref, bf16[128,512]{1,0:T(8,128)(2,1)S(1)} %collective-permute-done.3.w1_ref, ...), custom_call_target="tpu_custom_call" | custom-call | flops 1 | bytes 1 | tf_op jit(solution)/shard_map/pallas_call | solution.py:123
  20.7 0.8 %collective-permute-start.11 = (bf16[16,8192]{1,0:T(8,128)(2,1)S(1)}, bf16[16,8192]{1,0:T(8,128)(2,1)S(1)}, u32[]{:S(2)}, u32[]{:S(2)}) collective-permute-start(bf16[16,8192]{1,0:T(8,128)(2,1)S(1)} %get-tuple-element.40), channel_id=1, source_target_pairs={{0,1},{1,0},{2,3},{3,2},{4,5},{5,4},{6,7},{7,6},{8,9},{9,8},{10,11... | collective-permute-start | bytes 786440 | tf_op jit(solution)/shard_map/ppermute | solution.py:26
  21.5 1.4 %collective-permute-start.9 = (bf16[32,1536]{1,0:T(8,128)(2,1)S(1)}, bf16[32,1536]{1,0:T(8,128)(2,1)S(1)}, u32[]{:S(2)}, u32[]{:S(2)}) collective-permute-start(bf16[32,1536]{1,0:T(8,128)(2,1)S(1)} %slice.106), channel_id=1, source_target_pairs={{0,8},{2,10},{4,12},{6,14},{8,0},{10,2},{12,4},{14,6},{16,24},{18,... | collective-permute-start | bytes 294920 | tf_op jit(solution)/shard_map/ppermute | solution.py:26
  23.0 0.2 collective-permute-done.12
  23.2 1.6 %collective-permute-start.13 = (bf16[64,1024]{1,0:T(8,128)(2,1)S(1)}, bf16[64,1024]{1,0:T(8,128)(2,1)S(1)}, u32[]{:S(2)}, u32[]{:S(2)}) collective-permute-start(bf16[64,1024]{1,0:T(8,128)(2,1)S(1)} %pad_maximum_fusion.3), channel_id=1, source_target_pairs={{0,4},{2,6},{4,0},{6,2},{8,12},{10,14},{12,8},{14,10},{16,20},{18,... | collective-permute-start | bytes 393224 | tf_op jit(solution)/shard_map/ppermute | solution.py:26
  24.8 1.3 %shard_map.95 = (bf16[16,8192]{1,0:T(8,128)(2,1)S(1)}, f32[16,8192]{1,0:T(8,128)S(1)}, bf16[16,8192]{1,0:T(8,128)(2,1)S(1)}) custom-call(bf16[256,256]{1,0:T(8,128)(2,1)S(1)} %get-tuple-element.61.place_ref, bf16[128,512]{1,0:T(8,128)(2,1)S(1)} %collective-permute-done.4.w0_ref, bf16[128,512]{1,0:T(8,128)(2,1)S(1)} %collective-permute-done.5.w1_ref, ...), custom_call_target="tpu_custom_call" | custom-call | flops 1 | bytes 1 | tf_op jit(solution)/shard_map/pallas_call | solution.py:123
  26.1 1.8 %collective-permute-start.6 = (bf16[16,8192]{1,0:T(8,128)(2,1)S(1)}, bf16[16,8192]{1,0:T(8,128)(2,1)S(1)}, u32[]{:S(2)}, u32[]{:S(2)}) collective-permute-start(bf16[16,8192]{1,0:T(8,128)(2,1)S(1)} %get-tuple-element.32), channel_id=1, source_target_pairs={{0,1},{1,0},{2,3},{3,2},{4,5},{5,4},{6,7},{7,6},{8,9},{9,8},{10,11... | collective-permute-start | bytes 786440 | tf_op jit(solution)/shard_map/ppermute | solution.py:26
  27.9 1.3 %collective-permute-start.10 = (bf16[64,1536]{1,0:T(8,128)(2,1)S(1)}, bf16[64,1536]{1,0:T(8,128)(2,1)S(1)}, u32[]{:S(2)}, u32[]{:S(2)}) collective-permute-start(bf16[64,1536]{1,0:T(8,128)(2,1)S(1)} %pad_maximum_fusion.1), channel_id=1, source_target_pairs={{0,4},{2,6},{4,0},{6,2},{8,12},{10,14},{12,8},{14,10},{16,20},{18,... | collective-permute-start | bytes 589832 | tf_op jit(solution)/shard_map/ppermute | solution.py:26
  29.3 0.5 collective-permute-start.15
  30.0 0.7 %collective-permute-done.14.rest_0_ = bf16[128,512]{1,0:T(8,128)(2,1)S(1)} collective-permute-done((bf16[128,512]{1,0:T(8,128)(2,1)S(1)}, bf16[128,512]{1,0:T(8,128)(2,1)S(1)}, u32[]{:S(2)}, u32[]{:S(2)}) %collective-permute-start.14) | collective-permute-done | bytes 131104 | tf_op jit(solution)/shard_map/ppermute | solution.py:26
  30.6 0.2 collective-permute-done.15.rest_1_
  30.8 1.8 %shard_map.96 = (bf16[128,512]{1,0:T(8,128)(2,1)S(1)}, bf16[128,512]{1,0:T(8,128)(2,1)S(1)}) custom-call(bf16[256,256]{1,0:T(8,128)(2,1)S(1)} %get-tuple-element.61.place_ref, bf16[256,256]{1,0:T(8,128)(2,1)S(1)} %get-tuple-element.60.back_ref, f32[16,8192]{1,0:T(8,128)S(1)} %get-tuple-element.43.part_ref, ...), custom_call_target="tpu_custom_call" | custom-call | flops 1 | bytes 1 | tf_op jit(solution)/shard_map/pallas_call | solution.py:123
  32.6 2.1 %collective-permute-done.10 = bf16[64,1536]{1,0:T(8,128)(2,1)S(1)} collective-permute-done((bf16[64,1536]{1,0:T(8,128)(2,1)S(1)}, bf16[64,1536]{1,0:T(8,128)(2,1)S(1)}, u32[]{:S(2)}, u32[]{:S(2)}) %collective-permute-start.10) | collective-permute-done | bytes 196640 | tf_op jit(solution)/shard_map/ppermute | solution.py:26
  34.8 0.5 collective-permute-start.17
  35.3 0.1 collective-permute-start.18
  35.4 0.4 collective-permute-start.23
  35.8 0.3 collective-permute-done.16.rest_0_
  36.2 0.2 collective-permute-done.17.rest_1_
  36.4 0.3 collective-permute-done.18.rest_2_
  36.7 2.1 %shard_map.97 = (bf16[128,1024]{1,0:T(8,128)(2,1)S(1)}, bf16[128,1024]{1,0:T(8,128)(2,1)S(1)}, bf16[16,8192]{1,0:T(8,128)(2,1)}) custom-call(bf16[256,256]{1,0:T(8,128)(2,1)S(1)} %get-tuple-element.61.place_ref, bf16[256,256]{1,0:T(8,128)(2,1)S(1)} %get-tuple-element.60.back_ref, f32[16,8192]{1,0:T(8,128)S(1)} %get-tuple-element.31.part_ref, ...), custom_call_target="tpu_custom_call" | custom-call | flops 1 | bytes 1 | tf_op jit(solution)/shard_map/pallas_call | solution.py:123
  38.8 0.3 collective-permute-start.19
  39.1 1.2 %collective-permute-start.24 = (bf16[64,512]{1,0:T(8,128)(2,1)S(1)}, bf16[64,512]{1,0:T(8,128)(2,1)S(1)}, u32[]{:S(2)}, u32[]{:S(2)}) collective-permute-start(bf16[64,512]{1,0:T(8,128)(2,1)S(1)} %slice.161), channel_id=1, source_target_pairs={{0,4},{2,6},{4,0},{6,2},{8,12},{10,14},{12,8},{14,10},{16,20},{18,... | collective-permute-start | bytes 196616 | tf_op jit(solution)/shard_map/ppermute | solution.py:26
  40.5 1.2 %collective-permute-start.20 = (bf16[64,1024]{1,0:T(8,128)(2,1)S(1)}, bf16[64,1024]{1,0:T(8,128)(2,1)S(1)}, u32[]{:S(2)}, u32[]{:S(2)}) collective-permute-start(bf16[64,1024]{1,0:T(8,128)(2,1)S(1)} %slice.160), channel_id=1, source_target_pairs={{0,4},{2,6},{4,0},{6,2},{8,12},{10,14},{12,8},{14,10},{16,20},{18,... | collective-permute-start | bytes 393224 | tf_op jit(solution)/shard_map/ppermute | solution.py:26
  41.7 2.0 %collective-permute-done.24 = bf16[64,512]{1,0:T(8,128)(2,1)S(1)} collective-permute-done((bf16[64,512]{1,0:T(8,128)(2,1)S(1)}, bf16[64,512]{1,0:T(8,128)(2,1)S(1)}, u32[]{:S(2)}, u32[]{:S(2)}) %collective-permute-start.24) | collective-permute-done | bytes 65568 | tf_op jit(solution)/shard_map/ppermute | solution.py:26
  43.8 2.5 %collective-permute-done.20 = bf16[64,1024]{1,0:T(8,128)(2,1)S(1)} collective-permute-done((bf16[64,1024]{1,0:T(8,128)(2,1)S(1)}, bf16[64,1024]{1,0:T(8,128)(2,1)S(1)}, u32[]{:S(2)}, u32[]{:S(2)}) %collective-permute-start.20) | collective-permute-done | bytes 131104 | tf_op jit(solution)/shard_map/ppermute | solution.py:26
  46.4 1.3 %collective-permute-done.25 = bf16[32,512]{1,0:T(8,128)(2,1)S(1)} collective-permute-done((bf16[32,512]{1,0:T(8,128)(2,1)S(1)}, bf16[32,512]{1,0:T(8,128)(2,1)S(1)}, u32[]{:S(2)}, u32[]{:S(2)}) %collective-permute-start.25) | collective-permute-done | bytes 32800 | tf_op jit(solution)/shard_map/ppermute | solution.py:26
  47.7 2.3 %collective-permute-start.26 = (bf16[16,512]{1,0:T(8,128)(2,1)S(1)}, bf16[16,512]{1,0:T(8,128)(2,1)S(1)}, u32[]{:S(2)}, u32[]{:S(2)}) collective-permute-start(bf16[16,512]{1,0:T(8,128)(2,1)S(1)} %slice.165), channel_id=1, source_target_pairs={{0,16},{2,18},{4,20},{6,22},{8,24},{10,26},{12,28},{14,30},{16,0},... | collective-permute-start | bytes 49160 | tf_op jit(solution)/shard_map/ppermute | solution.py:26
  50.0 0.9 %collective-permute-done.21 = bf16[32,1024]{1,0:T(8,128)(2,1)S(1)} collective-permute-done((bf16[32,1024]{1,0:T(8,128)(2,1)S(1)}, bf16[32,1024]{1,0:T(8,128)(2,1)S(1)}, u32[]{:S(2)}, u32[]{:S(2)}) %collective-permute-start.21) | collective-permute-done | bytes 65568 | tf_op jit(solution)/shard_map/ppermute | solution.py:26
  50.9 1.4 %collective-permute-start.22 = (bf16[16,1024]{1,0:T(8,128)(2,1)S(1)}, bf16[16,1024]{1,0:T(8,128)(2,1)S(1)}, u32[]{:S(2)}, u32[]{:S(2)}) collective-permute-start(bf16[16,1024]{1,0:T(8,128)(2,1)S(1)} %slice.164), channel_id=1, source_target_pairs={{0,16},{2,18},{4,20},{6,22},{8,24},{10,26},{12,28},{14,30},{16,0},... | collective-permute-start | bytes 98312 | tf_op jit(solution)/shard_map/ppermute | solution.py:26
  52.2 0.2 collective-permute-done.26
  52.5 0.3 collective-permute-start.27
  52.8 3.2 %collective-permute-done.22 = bf16[16,1024]{1,0:T(8,128)(2,1)S(1)} collective-permute-done((bf16[16,1024]{1,0:T(8,128)(2,1)S(1)}, bf16[16,1024]{1,0:T(8,128)(2,1)S(1)}, u32[]{:S(2)}, u32[]{:S(2)}) %collective-permute-start.22) | collective-permute-done | bytes 32800 | tf_op jit(solution)/shard_map/ppermute | solution.py:26
  56.0 0.2 collective-permute-done.27
  56.2 0.6 %fusion.11 = (f32[1,16,512]{2,1,0:T(8,128)}, f32[1,16,512]{2,1,0:T(8,128)}) fusion(bf16[16,512]{1,0:T(8,128)(2,1)S(1)} %collective-permute-done.27, f32[16,1024]{1,0:T(8,128)S(1)} %slice_add_fusion.4, f32[1,16,512]{2,1,0:T(8,128)S(1)} %copy-done.3, f32[1,16,512]{2,1,0:T(8,128)S(1)} %copy-done.4), kind=kLoop, calls=%fused_computation.57 | loop fusion | flops 90112 | bytes 212992 | tf_op jit(solution)/shard_map/broadcast_in_dim | solution.py:242
  (66 shorter events, 1.3 us)
Async XLA Ops:
  1.4 6.3 %collective-permute-start = (bf16[16,512]{1,0:T(8,128)(2,1)S(1)}, bf16[16,512]{1,0:T(8,128)(2,1)S(1)}, u32[]{:S(2)}, u32[]{:S(2)}) collective-permute-start(bf16[16,512]{1,0:T(8,128)(2,1)S(1)} %bitcast_convert_fusion), channel_id=1, source_target_pairs={{0,16},{2,18},{4,20},{6,22},{8,24},{10,26},{12,28},{14,30},{16,0},... | collective-permute-start | bytes 49160 | tf_op jit(solution)/shard_map/ppermute | solution.py:26
  6.2 3.9 %collective-permute-start.7 = (bf16[16,1024]{1,0:T(8,128)(2,1)S(1)}, bf16[16,1024]{1,0:T(8,128)(2,1)S(1)}, u32[]{:S(2)}, u32[]{:S(2)}) collective-permute-start(bf16[16,1024]{1,0:T(8,128)(2,1)S(1)} %add_convert_fusion), channel_id=1, source_target_pairs={{0,1},{1,0},{2,3},{3,2},{4,5},{5,4},{6,7},{7,6},{8,9},{9,8},{10,11... | collective-permute-start | bytes 98312 | tf_op jit(solution)/shard_map/ppermute | solution.py:26
  7.7 4.8 %collective-permute-start.1 = (bf16[32,512]{1,0:T(8,128)(2,1)S(1)}, bf16[32,512]{1,0:T(8,128)(2,1)S(1)}, u32[]{:S(2)}, u32[]{:S(2)}) collective-permute-start(bf16[32,512]{1,0:T(8,128)(2,1)S(1)} %pad_maximum_fusion.6), channel_id=1, source_target_pairs={{0,8},{2,10},{4,12},{6,14},{8,0},{10,2},{12,4},{14,6},{16,24},{18,... | collective-permute-start | bytes 98312 | tf_op jit(solution)/shard_map/ppermute | solution.py:26
  10.1 8.5 %collective-permute-start.8 = (bf16[16,2560]{1,0:T(8,128)(2,1)S(1)}, bf16[16,2560]{1,0:T(8,128)(2,1)S(1)}, u32[]{:S(2)}, u32[]{:S(2)}) collective-permute-start(bf16[16,2560]{1,0:T(8,128)(2,1)S(1)} %pad_maximum_fusion.4), channel_id=1, source_target_pairs={{0,16},{2,18},{4,20},{6,22},{8,24},{10,26},{12,28},{14,30},{16,0},... | collective-permute-start | bytes 245768 | tf_op jit(solution)/shard_map/ppermute | solution.py:26
  12.6 6.1 %copy-start.5 = (s32[256]{0:T(256)S(1)}, s32[256]{0:T(256)}, u32[]{:S(2)}) copy-start(s32[256]{0:T(256)} %param.10) | copy-start | bytes 3076
  12.6 4.3 %collective-permute-start.2 = (bf16[64,512]{1,0:T(8,128)(2,1)S(1)}, bf16[64,512]{1,0:T(8,128)(2,1)S(1)}, u32[]{:S(2)}, u32[]{:S(2)}) collective-permute-start(bf16[64,512]{1,0:T(8,128)(2,1)S(1)} %pad_maximum_fusion.5), channel_id=1, source_target_pairs={{0,4},{2,6},{4,0},{6,2},{8,12},{10,14},{12,8},{14,10},{16,20},{18,... | collective-permute-start | bytes 196616 | tf_op jit(solution)/shard_map/ppermute | solution.py:26
  16.9 2.5 %collective-permute-start.3 = (bf16[128,512]{1,0:T(8,128)(2,1)S(1)}, bf16[128,512]{1,0:T(8,128)(2,1)S(1)}, u32[]{:S(2)}, u32[]{:S(2)}) collective-permute-start(bf16[128,512]{1,0:T(8,128)(2,1)S(1)} %pad_maximum_fusion.2.w0_ref), channel_id=1, source_target_pairs={{0,2},{2,0},{4,6},{6,4},{8,10},{10,8},{12,14},{14,12},{16,18},{18,... | collective-permute-start | bytes 393224 | tf_op jit(solution)/shard_map/ppermute | solution.py:26
  17.0 5.9 %collective-permute-start.4 = (bf16[128,512]{1,0:T(8,128)(2,1)S(1)}, bf16[128,512]{1,0:T(8,128)(2,1)S(1)}, u32[]{:S(2)}, u32[]{:S(2)}) collective-permute-start(bf16[128,512]{1,0:T(8,128)(2,1)S(1)} %pad_maximum_fusion.2.w0_ref), channel_id=1, source_target_pairs={{0,1},{1,0},{2,3},{3,2},{4,5},{5,4},{6,7},{7,6},{8,9},{9,8},{10,11... | collective-permute-start | bytes 393224 | tf_op jit(solution)/shard_map/ppermute | solution.py:26
  18.9 4.3 %collective-permute-start.12 = (bf16[32,1024]{1,0:T(8,128)(2,1)S(1)}, bf16[32,1024]{1,0:T(8,128)(2,1)S(1)}, u32[]{:S(2)}, u32[]{:S(2)}) collective-permute-start(bf16[32,1024]{1,0:T(8,128)(2,1)S(1)} %slice.107), channel_id=1, source_target_pairs={{0,8},{2,10},{4,12},{6,14},{8,0},{10,2},{12,4},{14,6},{16,24},{18,... | collective-permute-start | bytes 196616 | tf_op jit(solution)/shard_map/ppermute | solution.py:26
  20.7 10.1 %collective-permute-start.11 = (bf16[16,8192]{1,0:T(8,128)(2,1)S(1)}, bf16[16,8192]{1,0:T(8,128)(2,1)S(1)}, u32[]{:S(2)}, u32[]{:S(2)}) collective-permute-start(bf16[16,8192]{1,0:T(8,128)(2,1)S(1)} %get-tuple-element.40), channel_id=1, source_target_pairs={{0,1},{1,0},{2,3},{3,2},{4,5},{5,4},{6,7},{7,6},{8,9},{9,8},{10,11... | collective-permute-start | bytes 786440 | tf_op jit(solution)/shard_map/ppermute | solution.py:26
  21.5 6.3 %collective-permute-start.9 = (bf16[32,1536]{1,0:T(8,128)(2,1)S(1)}, bf16[32,1536]{1,0:T(8,128)(2,1)S(1)}, u32[]{:S(2)}, u32[]{:S(2)}) collective-permute-start(bf16[32,1536]{1,0:T(8,128)(2,1)S(1)} %slice.106), channel_id=1, source_target_pairs={{0,8},{2,10},{4,12},{6,14},{8,0},{10,2},{12,4},{14,6},{16,24},{18,... | collective-permute-start | bytes 294920 | tf_op jit(solution)/shard_map/ppermute | solution.py:26
  22.9 1.8 %collective-permute-start.5 = (bf16[128,512]{1,0:T(8,128)(2,1)S(1)}, bf16[128,512]{1,0:T(8,128)(2,1)S(1)}, u32[]{:S(2)}, u32[]{:S(2)}) collective-permute-start(bf16[128,512]{1,0:T(8,128)(2,1)S(1)} %collective-permute-done.4.w0_ref), channel_id=1, source_target_pairs={{0,2},{2,0},{4,6},{6,4},{8,10},{10,8},{12,14},{14,12},{16,18},{18,... | collective-permute-start | bytes 393224 | tf_op jit(solution)/shard_map/ppermute | solution.py:26
  23.0 6.9 %copy-start.1 = (bf16[2,64,8192]{2,1,0:T(8,128)(2,1)S(1)}, bf16[2,64,8192]{2,1,0:T(8,128)(2,1)}, u32[]{:S(2)}) copy-start(bf16[2,64,8192]{2,1,0:T(8,128)(2,1)} %param.13) | copy-start | bytes 6291460
  23.2 6.0 %collective-permute-start.13 = (bf16[64,1024]{1,0:T(8,128)(2,1)S(1)}, bf16[64,1024]{1,0:T(8,128)(2,1)S(1)}, u32[]{:S(2)}, u32[]{:S(2)}) collective-permute-start(bf16[64,1024]{1,0:T(8,128)(2,1)S(1)} %pad_maximum_fusion.3), channel_id=1, source_target_pairs={{0,4},{2,6},{4,0},{6,2},{8,12},{10,14},{12,8},{14,10},{16,20},{18,... | collective-permute-start | bytes 393224 | tf_op jit(solution)/shard_map/ppermute | solution.py:26
  26.0 3.8 %copy-start.2 = (bf16[2,64,8192]{2,1,0:T(8,128)(2,1)S(1)}, bf16[2,64,8192]{2,1,0:T(8,128)(2,1)}, u32[]{:S(2)}) copy-start(bf16[2,64,8192]{2,1,0:T(8,128)(2,1)} %param.12) | copy-start | bytes 6291460
  26.1 9.8 %collective-permute-start.6 = (bf16[16,8192]{1,0:T(8,128)(2,1)S(1)}, bf16[16,8192]{1,0:T(8,128)(2,1)S(1)}, u32[]{:S(2)}, u32[]{:S(2)}) collective-permute-start(bf16[16,8192]{1,0:T(8,128)(2,1)S(1)} %get-tuple-element.32), channel_id=1, source_target_pairs={{0,1},{1,0},{2,3},{3,2},{4,5},{5,4},{6,7},{7,6},{8,9},{9,8},{10,11... | collective-permute-start | bytes 786440 | tf_op jit(solution)/shard_map/ppermute | solution.py:26
  27.9 6.8 %collective-permute-start.10 = (bf16[64,1536]{1,0:T(8,128)(2,1)S(1)}, bf16[64,1536]{1,0:T(8,128)(2,1)S(1)}, u32[]{:S(2)}, u32[]{:S(2)}) collective-permute-start(bf16[64,1536]{1,0:T(8,128)(2,1)S(1)} %pad_maximum_fusion.1), channel_id=1, source_target_pairs={{0,4},{2,6},{4,0},{6,2},{8,12},{10,14},{12,8},{14,10},{16,20},{18,... | collective-permute-start | bytes 589832 | tf_op jit(solution)/shard_map/ppermute | solution.py:26
  29.2 1.4 %collective-permute-start.14 = (bf16[128,512]{1,0:T(8,128)(2,1)S(1)}, bf16[128,512]{1,0:T(8,128)(2,1)S(1)}, u32[]{:S(2)}, u32[]{:S(2)}) collective-permute-start(bf16[128,512]{1,0:T(8,128)(2,1)S(1)} %get-tuple-element.57), channel_id=1, source_target_pairs={{0,2},{2,0},{4,6},{6,4},{8,10},{10,8},{12,14},{14,12},{16,18},{18,... | collective-permute-start | bytes 393224 | tf_op jit(solution)/shard_map/ppermute | solution.py:26
  29.3 1.5 %collective-permute-start.15 = (bf16[128,512]{1,0:T(8,128)(2,1)S(1)}, bf16[128,512]{1,0:T(8,128)(2,1)S(1)}, u32[]{:S(2)}, u32[]{:S(2)}) collective-permute-start(bf16[128,512]{1,0:T(8,128)(2,1)S(1)} %get-tuple-element.56), channel_id=1, source_target_pairs={{0,2},{2,0},{4,6},{6,4},{8,10},{10,8},{12,14},{14,12},{16,18},{18,... | collective-permute-start | bytes 393224 | tf_op jit(solution)/shard_map/ppermute | solution.py:26
  30.8 5.8 %copy-start = (bf16[1,2,8,8192]{3,2,1,0:T(8,128)(2,1)S(1)}, bf16[1,2,8,8192]{3,2,1,0:T(8,128)(2,1)}, u32[]{:S(2)}) copy-start(bf16[1,2,8,8192]{3,2,1,0:T(8,128)(2,1)} %param.11) | copy-start | bytes 786436
  34.8 1.4 %collective-permute-start.16 = (bf16[128,512]{1,0:T(8,128)(2,1)S(1)}, bf16[128,512]{1,0:T(8,128)(2,1)S(1)}, u32[]{:S(2)}, u32[]{:S(2)}) collective-permute-start(bf16[128,512]{1,0:T(8,128)(2,1)S(1)} %get-tuple-element.55), channel_id=1, source_target_pairs={{0,2},{2,0},{4,6},{6,4},{8,10},{10,8},{12,14},{14,12},{16,18},{18,... | collective-permute-start | bytes 393224 | tf_op jit(solution)/shard_map/ppermute | solution.py:26
  34.8 1.5 %collective-permute-start.17 = (bf16[128,512]{1,0:T(8,128)(2,1)S(1)}, bf16[128,512]{1,0:T(8,128)(2,1)S(1)}, u32[]{:S(2)}, u32[]{:S(2)}) collective-permute-start(bf16[128,512]{1,0:T(8,128)(2,1)S(1)} %get-tuple-element.54), channel_id=1, source_target_pairs={{0,2},{2,0},{4,6},{6,4},{8,10},{10,8},{12,14},{14,12},{16,18},{18,... | collective-permute-start | bytes 393224 | tf_op jit(solution)/shard_map/ppermute | solution.py:26
  35.3 1.3 %collective-permute-start.18 = (bf16[128,512]{1,0:T(8,128)(2,1)S(1)}, bf16[128,512]{1,0:T(8,128)(2,1)S(1)}, u32[]{:S(2)}, u32[]{:S(2)}) collective-permute-start(bf16[128,512]{1,0:T(8,128)(2,1)S(1)} %get-tuple-element.53), channel_id=1, source_target_pairs={{0,2},{2,0},{4,6},{6,4},{8,10},{10,8},{12,14},{14,12},{16,18},{18,... | collective-permute-start | bytes 393224 | tf_op jit(solution)/shard_map/ppermute | solution.py:26
  35.4 3.6 %collective-permute-start.23 = (bf16[128,512]{1,0:T(8,128)(2,1)S(1)}, bf16[128,512]{1,0:T(8,128)(2,1)S(1)}, u32[]{:S(2)}, u32[]{:S(2)}) collective-permute-start(bf16[128,512]{1,0:T(8,128)(2,1)S(1)} %get-tuple-element.51), channel_id=1, source_target_pairs={{0,2},{2,0},{4,6},{6,4},{8,10},{10,8},{12,14},{14,12},{16,18},{18,... | collective-permute-start | bytes 393224 | tf_op jit(solution)/shard_map/ppermute | solution.py:26
  38.8 17.4 %copy-start.3 = (f32[1,16,512]{2,1,0:T(8,128)S(1)}, f32[1,16,512]{2,1,0:T(8,128)}, u32[]{:S(2)}) copy-start(f32[1,16,512]{2,1,0:T(8,128)} %param.9) | copy-start | bytes 98308
  38.8 17.4 %copy-start.4 = (f32[1,16,512]{2,1,0:T(8,128)S(1)}, f32[1,16,512]{2,1,0:T(8,128)}, u32[]{:S(2)}) copy-start(f32[1,16,512]{2,1,0:T(8,128)} %param.7) | copy-start | bytes 98308
  38.8 1.6 %collective-permute-start.19 = (bf16[128,1024]{1,0:T(8,128)(2,1)S(1)}, bf16[128,1024]{1,0:T(8,128)(2,1)S(1)}, u32[]{:S(2)}, u32[]{:S(2)}) collective-permute-start(bf16[128,1024]{1,0:T(8,128)(2,1)S(1)} %get-tuple-element.50), channel_id=1, source_target_pairs={{0,2},{2,0},{4,6},{6,4},{8,10},{10,8},{12,14},{14,12},{16,18},{18,... | collective-permute-start | bytes 786440 | tf_op jit(solution)/shard_map/ppermute | solution.py:26
  39.1 4.6 %collective-permute-start.24 = (bf16[64,512]{1,0:T(8,128)(2,1)S(1)}, bf16[64,512]{1,0:T(8,128)(2,1)S(1)}, u32[]{:S(2)}, u32[]{:S(2)}) collective-permute-start(bf16[64,512]{1,0:T(8,128)(2,1)S(1)} %slice.161), channel_id=1, source_target_pairs={{0,4},{2,6},{4,0},{6,2},{8,12},{10,14},{12,8},{14,10},{16,20},{18,... | collective-permute-start | bytes 196616 | tf_op jit(solution)/shard_map/ppermute | solution.py:26
  40.5 5.8 %collective-permute-start.20 = (bf16[64,1024]{1,0:T(8,128)(2,1)S(1)}, bf16[64,1024]{1,0:T(8,128)(2,1)S(1)}, u32[]{:S(2)}, u32[]{:S(2)}) collective-permute-start(bf16[64,1024]{1,0:T(8,128)(2,1)S(1)} %slice.160), channel_id=1, source_target_pairs={{0,4},{2,6},{4,0},{6,2},{8,12},{10,14},{12,8},{14,10},{16,20},{18,... | collective-permute-start | bytes 393224 | tf_op jit(solution)/shard_map/ppermute | solution.py:26
  43.7 4.0 %collective-permute-start.25 = (bf16[32,512]{1,0:T(8,128)(2,1)S(1)}, bf16[32,512]{1,0:T(8,128)(2,1)S(1)}, u32[]{:S(2)}, u32[]{:S(2)}) collective-permute-start(bf16[32,512]{1,0:T(8,128)(2,1)S(1)} %slice.163), channel_id=1, source_target_pairs={{0,8},{2,10},{4,12},{6,14},{8,0},{10,2},{12,4},{14,6},{16,24},{18,... | collective-permute-start | bytes 98312 | tf_op jit(solution)/shard_map/ppermute | solution.py:26
  46.3 4.5 %collective-permute-start.21 = (bf16[32,1024]{1,0:T(8,128)(2,1)S(1)}, bf16[32,1024]{1,0:T(8,128)(2,1)S(1)}, u32[]{:S(2)}, u32[]{:S(2)}) collective-permute-start(bf16[32,1024]{1,0:T(8,128)(2,1)S(1)} %slice.162), channel_id=1, source_target_pairs={{0,8},{2,10},{4,12},{6,14},{8,0},{10,2},{12,4},{14,6},{16,24},{18,... | collective-permute-start | bytes 196616 | tf_op jit(solution)/shard_map/ppermute | solution.py:26
  47.7 4.7 %collective-permute-start.26 = (bf16[16,512]{1,0:T(8,128)(2,1)S(1)}, bf16[16,512]{1,0:T(8,128)(2,1)S(1)}, u32[]{:S(2)}, u32[]{:S(2)}) collective-permute-start(bf16[16,512]{1,0:T(8,128)(2,1)S(1)} %slice.165), channel_id=1, source_target_pairs={{0,16},{2,18},{4,20},{6,22},{8,24},{10,26},{12,28},{14,30},{16,0},... | collective-permute-start | bytes 49160 | tf_op jit(solution)/shard_map/ppermute | solution.py:26
  50.9 5.1 %collective-permute-start.22 = (bf16[16,1024]{1,0:T(8,128)(2,1)S(1)}, bf16[16,1024]{1,0:T(8,128)(2,1)S(1)}, u32[]{:S(2)}, u32[]{:S(2)}) collective-permute-start(bf16[16,1024]{1,0:T(8,128)(2,1)S(1)} %slice.164), channel_id=1, source_target_pairs={{0,16},{2,18},{4,20},{6,22},{8,24},{10,26},{12,28},{14,30},{16,0},... | collective-permute-start | bytes 98312 | tf_op jit(solution)/shard_map/ppermute | solution.py:26
  52.5 3.7 %collective-permute-start.27 = (bf16[16,512]{1,0:T(8,128)(2,1)S(1)}, bf16[16,512]{1,0:T(8,128)(2,1)S(1)}, u32[]{:S(2)}, u32[]{:S(2)}) collective-permute-start(bf16[16,512]{1,0:T(8,128)(2,1)S(1)} %fusion.3), channel_id=1, source_target_pairs={{0,1},{1,0},{2,3},{3,2},{4,5},{5,4},{6,7},{7,6},{8,9},{9,8},{10,11... | collective-permute-start | bytes 49160 | tf_op jit(solution)/shard_map/ppermute | solution.py:26

commit v16 on v14

--- a/solution.py
+++ b/solution.py
@@ -232,14 +232,13 @@
         sums[k] = result[0].astype(F32) + swap(result[1], "dp", 1).astype(F32)
     error = result[2]
 
-    sums = [halve(p, far[-1]) for p in sums]
+    for mask in far[:0:-1]:
+        sums = [halve(p, mask) for p in sums]
     grads = [sums[0][:, :segment]] + sums[1:]
     for mask in mp_bits:
         crossed = [swap(p.astype(BF), "mp", mask).astype(F32) for p in grads[mask:]]
         grads = [p + q for p, q in zip(grads, crossed)]
-    both = jnp.concatenate([grads[0], sums[0][:, segment:]], axis=1)
-    for mask in far[-2::-1]:
-        both = halve(both, mask)
+    both = halve(jnp.concatenate([grads[0], sums[0][:, segment:]], axis=1), far[0])
     own_grad, own_packed = both[:, :segment], both[:, segment:]
     mean_grad = own_grad / n_dp
     mean_moment = own_packed / n_dp

time: 57.7 us -> 56.9 us (0.986)
  waiting for transfers between devices: 15.6 us -> 14.1 us
  starting transfers between devices: 28.7 us -> 29.6 us
    ppermute x27 -> x28, waiting for transfers between devices: 15.6 us -> 14.1 us  [swap(): return lax.ppermute(x, axis, [(i, i ^ mask) for i in range(n)])]
    ppermute x27 -> x28, starting transfers between devices: 28.7 us -> 29.6 us  [swap(): return lax.ppermute(x, axis, [(i, i ^ mask) for i in range(n)])]
  transfers between devices with their start and end apart: 27 -> 28, of which waited for: 15 -> 15; matrix products, arithmetic and copies ran while one was open for 7% -> 7% of each run, Pallas kernels for 11% -> 11%
where the time goes in v16:
time: 56.9 us; the launch traced here: 56.6 us
  starting transfers between devices  29.6 us (52%)
  waiting for transfers between devices  14.1 us (25%)
  Pallas kernels  6.34 us (11%)
  other arithmetic  3.38 us (6%)
  local copies, waits for them, and re-layouts  2.24 us (4%)
  between operations  0.97 us (2%)
    ppermute x28, starting transfers between devices, swap(): return lax.ppermute(x, axis, [(i, i ^ mask) for i in range(n)])  29.6 us
    ppermute x28, waiting for transfers between devices, swap(): return lax.ppermute(x, axis, [(i, i ^ mask) for i in range(n)])  14.1 us
    pallas_call x4, Pallas kernels, call(): pl.pallas_call(kernel, out_shape=out_shape, in_specs=[pl.BlockSpec(memory...  6.34 us
    squeeze x3, local copies, waits for them, and re-layouts, tokens_of(): x[step]  1.81 us
  transfers between devices with their start and end apart: 28, of which 15 were waited for; matrix products, arithmetic and copies ran while one was open for 7% of the time, Pallas kernels for 11%

profile of v16, /device:TPU:0, one launch (start us, length us, event | category | flops | bytes accessed | tf_op | source)
XLA Modules:
  0.0 56.6 jit_solution(6462351397569594208)
XLA Ops:
  0.6 0.8 %bitcast_convert_fusion = bf16[16,512]{1,0:T(8,128)(2,1)S(1)} fusion(f32[1,16,512]{2,1,0:T(8,128)} %param.7), kind=kLoop, calls=%fused_computation.44 | loop fusion | flops 8192 | bytes 49152 | tf_op jit(solution)/shard_map/convert_element_type | solution.py:151
  1.4 4.0 %collective-permute-start = (bf16[16,512]{1,0:T(8,128)(2,1)S(1)}, bf16[16,512]{1,0:T(8,128)(2,1)S(1)}, u32[]{:S(2)}, u32[]{:S(2)}) collective-permute-start(bf16[16,512]{1,0:T(8,128)(2,1)S(1)} %bitcast_convert_fusion), channel_id=1, source_target_pairs={{0,16},{2,18},{4,20},{6,22},{8,24},{10,26},{12,28},{14,30},{16,0},... | collective-permute-start | bytes 49160 | tf_op jit(solution)/shard_map/ppermute | solution.py:26
  5.4 0.8 %convert_bitcast_fusion = bf16[16,512]{1,0:T(8,128)(2,1)S(1)} fusion(f32[1,16,512]{2,1,0:T(8,128)} %param.9), kind=kLoop, calls=%fused_computation.52 | loop fusion | flops 8192 | bytes 49152 | tf_op jit(solution)/shard_map/convert.6
  6.2 0.8 %fusion.7 = (bf16[16,512]{1,0:T(8,128)(2,1)S(1)}, bf16[16,512]{1,0:T(8,128)(2,1)S(1)}) fusion(f32[16,512]{1,0:T(8,128)} %bitcast.28), kind=kLoop, calls=%fused_computation.36 | loop fusion | flops 32768 | bytes 65536 | tf_op jit(solution)/shard_map/convert_element_type | solution.py:154
  7.0 1.6 %collective-permute-start.7 = (bf16[16,1024]{1,0:T(8,128)(2,1)S(1)}, bf16[16,1024]{1,0:T(8,128)(2,1)S(1)}, u32[]{:S(2)}, u32[]{:S(2)}) collective-permute-start(bf16[16,1024]{1,0:T(8,128)(2,1)S(1)} %pad_maximum_fusion.8), channel_id=1, source_target_pairs={{0,1},{1,0},{2,3},{3,2},{4,5},{5,4},{6,7},{7,6},{8,9},{9,8},{10,11... | collective-permute-start | bytes 98312 | tf_op jit(solution)/shard_map/ppermute | solution.py:26
  8.6 1.6 %collective-permute-start.1 = (bf16[32,512]{1,0:T(8,128)(2,1)S(1)}, bf16[32,512]{1,0:T(8,128)(2,1)S(1)}, u32[]{:S(2)}, u32[]{:S(2)}) collective-permute-start(bf16[32,512]{1,0:T(8,128)(2,1)S(1)} %pad_maximum_fusion.7), channel_id=1, source_target_pairs={{0,8},{2,10},{4,12},{6,14},{8,0},{10,2},{12,4},{14,6},{16,24},{18,... | collective-permute-start | bytes 98312 | tf_op jit(solution)/shard_map/ppermute | solution.py:26
  10.2 0.8 %collective-permute-done.7 = bf16[16,1024]{1,0:T(8,128)(2,1)S(1)} collective-permute-done((bf16[16,1024]{1,0:T(8,128)(2,1)S(1)}, bf16[16,1024]{1,0:T(8,128)(2,1)S(1)}, u32[]{:S(2)}, u32[]{:S(2)}) %collective-permute-start.7) | collective-permute-done | bytes 32800 | tf_op jit(solution)/shard_map/ppermute | solution.py:26
  11.0 0.8 %collective-permute-start.8 = (bf16[16,2560]{1,0:T(8,128)(2,1)S(1)}, bf16[16,2560]{1,0:T(8,128)(2,1)S(1)}, u32[]{:S(2)}, u32[]{:S(2)}) collective-permute-start(bf16[16,2560]{1,0:T(8,128)(2,1)S(1)} %pad_maximum_fusion.3), channel_id=1, source_target_pairs={{0,16},{2,18},{4,20},{6,22},{8,24},{10,26},{12,28},{14,30},{16,0},... | collective-permute-start | bytes 245768 | tf_op jit(solution)/shard_map/ppermute | solution.py:26
  11.8 0.7 %collective-permute-done.1 = bf16[32,512]{1,0:T(8,128)(2,1)S(1)} collective-permute-done((bf16[32,512]{1,0:T(8,128)(2,1)S(1)}, bf16[32,512]{1,0:T(8,128)(2,1)S(1)}, u32[]{:S(2)}, u32[]{:S(2)}) %collective-permute-start.1) | collective-permute-done | bytes 32800 | tf_op jit(solution)/shard_map/ppermute | solution.py:26
  12.6 1.6 %collective-permute-start.2 = (bf16[64,512]{1,0:T(8,128)(2,1)S(1)}, bf16[64,512]{1,0:T(8,128)(2,1)S(1)}, u32[]{:S(2)}, u32[]{:S(2)}) collective-permute-start(bf16[64,512]{1,0:T(8,128)(2,1)S(1)} %pad_maximum_fusion.6), channel_id=1, source_target_pairs={{0,4},{2,6},{4,0},{6,2},{8,12},{10,14},{12,8},{14,10},{16,20},{18,... | collective-permute-start | bytes 196616 | tf_op jit(solution)/shard_map/ppermute | solution.py:26
  14.1 1.7 %slice_bitcast_fusion.2 = (bf16[64,8192]{1,0:T(8,128)(2,1)S(1)}, bf16[64,8192]{1,0:T(8,128)(2,1)S(1)}) fusion(bf16[2,64,8192]{2,1,0:T(8,128)(2,1)} %param.13, bf16[2,64,8192]{2,1,0:T(8,128)(2,1)} %param.12), kind=kLoop, calls=%fused_computation.2 | loop fusion | bytes 4194304 | tf_op jit(solution)/shard_map/squeeze | solution.py:124
  15.8 1.1 %collective-permute-done.2 = bf16[64,512]{1,0:T(8,128)(2,1)S(1)} collective-permute-done((bf16[64,512]{1,0:T(8,128)(2,1)S(1)}, bf16[64,512]{1,0:T(8,128)(2,1)S(1)}, u32[]{:S(2)}, u32[]{:S(2)}) %collective-permute-start.2) | collective-permute-done | bytes 65568 | tf_op jit(solution)/shard_map/ppermute | solution.py:26
  16.9 0.9 %collective-permute-start.4 = (bf16[128,512]{1,0:T(8,128)(2,1)S(1)}, bf16[128,512]{1,0:T(8,128)(2,1)S(1)}, u32[]{:S(2)}, u32[]{:S(2)}) collective-permute-start(bf16[128,512]{1,0:T(8,128)(2,1)S(1)} %pad_maximum_fusion.1.w0_ref), channel_id=1, source_target_pairs={{0,1},{1,0},{2,3},{3,2},{4,5},{5,4},{6,7},{7,6},{8,9},{9,8},{10,11... | collective-permute-start | bytes 393224 | tf_op jit(solution)/shard_map/ppermute | solution.py:26
  18.1 1.6 %collective-permute-start.12 = (bf16[32,1024]{1,0:T(8,128)(2,1)S(1)}, bf16[32,1024]{1,0:T(8,128)(2,1)S(1)}, u32[]{:S(2)}, u32[]{:S(2)}) collective-permute-start(bf16[32,1024]{1,0:T(8,128)(2,1)S(1)} %slice.114), channel_id=1, source_target_pairs={{0,8},{2,10},{4,12},{6,14},{8,0},{10,2},{12,4},{14,6},{16,24},{18,... | collective-permute-start | bytes 196616 | tf_op jit(solution)/shard_map/ppermute | solution.py:26
  19.7 0.1 fusion.1
  19.8 1.3 %shard_map.94 = (bf16[16,8192]{1,0:T(8,128)(2,1)S(1)}, f32[16,8192]{1,0:T(8,128)S(1)}, bf16[16,8192]{1,0:T(8,128)(2,1)S(1)}) custom-call(bf16[256,256]{1,0:T(8,128)(2,1)S(1)} %get-tuple-element.73.place_ref, bf16[128,512]{1,0:T(8,128)(2,1)S(1)} %pad_maximum_fusion.1.w0_ref, bf16[128,512]{1,0:T(8,128)(2,1)S(1)} %collective-permute-done.3.w1_ref, ...), custom_call_target="tpu_custom_call" | custom-call | flops 1 | bytes 1 | tf_op jit(solution)/shard_map/pallas_call | solution.py:128
  21.1 1.3 %collective-permute-start.11 = (bf16[16,8192]{1,0:T(8,128)(2,1)S(1)}, bf16[16,8192]{1,0:T(8,128)(2,1)S(1)}, u32[]{:S(2)}, u32[]{:S(2)}) collective-permute-start(bf16[16,8192]{1,0:T(8,128)(2,1)S(1)} %get-tuple-element.40), channel_id=1, source_target_pairs={{0,1},{1,0},{2,3},{3,2},{4,5},{5,4},{6,7},{7,6},{8,9},{9,8},{10,11... | collective-permute-start | bytes 786440 | tf_op jit(solution)/shard_map/ppermute | solution.py:26
  22.3 0.9 %collective-permute-start.9 = (bf16[32,1536]{1,0:T(8,128)(2,1)S(1)}, bf16[32,1536]{1,0:T(8,128)(2,1)S(1)}, u32[]{:S(2)}, u32[]{:S(2)}) collective-permute-start(bf16[32,1536]{1,0:T(8,128)(2,1)S(1)} %slice.113), channel_id=1, source_target_pairs={{0,8},{2,10},{4,12},{6,14},{8,0},{10,2},{12,4},{14,6},{16,24},{18,... | collective-permute-start | bytes 294920 | tf_op jit(solution)/shard_map/ppermute | solution.py:26
  23.3 1.6 %collective-permute-start.14 = (bf16[64,512]{1,0:T(8,128)(2,1)S(1)}, bf16[64,512]{1,0:T(8,128)(2,1)S(1)}, u32[]{:S(2)}, u32[]{:S(2)}) collective-permute-start(bf16[64,512]{1,0:T(8,128)(2,1)S(1)} %get-tuple-element.62), channel_id=1, source_target_pairs={{0,4},{2,6},{4,0},{6,2},{8,12},{10,14},{12,8},{14,10},{16,20},{18,... | collective-permute-start | bytes 196616 | tf_op jit(solution)/shard_map/ppermute | solution.py:26
  24.9 0.5 collective-permute-start.13
  25.4 1.3 %shard_map.95 = (bf16[16,8192]{1,0:T(8,128)(2,1)S(1)}, f32[16,8192]{1,0:T(8,128)S(1)}, bf16[16,8192]{1,0:T(8,128)(2,1)S(1)}) custom-call(bf16[256,256]{1,0:T(8,128)(2,1)S(1)} %get-tuple-element.73.place_ref, bf16[128,512]{1,0:T(8,128)(2,1)S(1)} %collective-permute-done.4.w0_ref, bf16[128,512]{1,0:T(8,128)(2,1)S(1)} %collective-permute-done.5.w1_ref, ...), custom_call_target="tpu_custom_call" | custom-call | flops 1 | bytes 1 | tf_op jit(solution)/shard_map/pallas_call | solution.py:128
  26.7 0.9 %collective-permute-start.6 = (bf16[16,8192]{1,0:T(8,128)(2,1)S(1)}, bf16[16,8192]{1,0:T(8,128)(2,1)S(1)}, u32[]{:S(2)}, u32[]{:S(2)}) collective-permute-start(bf16[16,8192]{1,0:T(8,128)(2,1)S(1)} %get-tuple-element.33), channel_id=1, source_target_pairs={{0,1},{1,0},{2,3},{3,2},{4,5},{5,4},{6,7},{7,6},{8,9},{9,8},{10,11... | collective-permute-start | bytes 786440 | tf_op jit(solution)/shard_map/ppermute | solution.py:26
  27.6 1.6 %collective-permute-start.10 = (bf16[64,1536]{1,0:T(8,128)(2,1)S(1)}, bf16[64,1536]{1,0:T(8,128)(2,1)S(1)}, u32[]{:S(2)}, u32[]{:S(2)}) collective-permute-start(bf16[64,1536]{1,0:T(8,128)(2,1)S(1)} %get-tuple-element.64), channel_id=1, source_target_pairs={{0,4},{2,6},{4,0},{6,2},{8,12},{10,14},{12,8},{14,10},{16,20},{18,... | collective-permute-start | bytes 589832 | tf_op jit(solution)/shard_map/ppermute | solution.py:26
  29.2 0.1 collective-permute-done.13
  29.4 0.5 collective-permute-start.15
  30.1 0.7 %collective-permute-done.16.rest_1_ = bf16[128,512]{1,0:T(8,128)(2,1)S(1)} collective-permute-done((bf16[128,512]{1,0:T(8,128)(2,1)S(1)}, bf16[128,512]{1,0:T(8,128)(2,1)S(1)}, u32[]{:S(2)}, u32[]{:S(2)}) %collective-permute-start.16) | collective-permute-done | bytes 131104 | tf_op jit(solution)/shard_map/ppermute | solution.py:26
  30.8 0.2 collective-permute-done.15.rest_0_
  31.0 1.8 %shard_map.96 = (bf16[128,512]{1,0:T(8,128)(2,1)S(1)}, bf16[128,512]{1,0:T(8,128)(2,1)S(1)}) custom-call(bf16[256,256]{1,0:T(8,128)(2,1)S(1)} %get-tuple-element.73.place_ref, bf16[256,256]{1,0:T(8,128)(2,1)S(1)} %get-tuple-element.72.back_ref, f32[16,8192]{1,0:T(8,128)S(1)} %get-tuple-element.43.part_ref, ...), custom_call_target="tpu_custom_call" | custom-call | flops 1 | bytes 1 | tf_op jit(solution)/shard_map/pallas_call | solution.py:128
  32.7 1.4 %collective-permute-done.10 = bf16[64,1536]{1,0:T(8,128)(2,1)S(1)} collective-permute-done((bf16[64,1536]{1,0:T(8,128)(2,1)S(1)}, bf16[64,1536]{1,0:T(8,128)(2,1)S(1)}, u32[]{:S(2)}, u32[]{:S(2)}) %collective-permute-start.10) | collective-permute-done | bytes 196640 | tf_op jit(solution)/shard_map/ppermute | solution.py:26
  34.3 0.5 collective-permute-start.18
  34.8 0.4 collective-permute-start.23
  35.3 0.3 collective-permute-done.19.rest_2_
  35.6 0.2 collective-permute-done.18.rest_1_
  35.8 0.3 collective-permute-done.17.rest_0_
  36.1 2.1 %shard_map.97 = (bf16[128,1024]{1,0:T(8,128)(2,1)S(1)}, bf16[128,1024]{1,0:T(8,128)(2,1)S(1)}, bf16[16,8192]{1,0:T(8,128)(2,1)}) custom-call(bf16[256,256]{1,0:T(8,128)(2,1)S(1)} %get-tuple-element.73.place_ref, bf16[256,256]{1,0:T(8,128)(2,1)S(1)} %get-tuple-element.72.back_ref, f32[16,8192]{1,0:T(8,128)S(1)} %get-tuple-element.32.part_ref, ...), custom_call_target="tpu_custom_call" | custom-call | flops 1 | bytes 1 | tf_op jit(solution)/shard_map/pallas_call | solution.py:128
  38.2 0.3 collective-permute-start.20
  38.5 1.6 %collective-permute-start.24 = (bf16[64,512]{1,0:T(8,128)(2,1)S(1)}, bf16[64,512]{1,0:T(8,128)(2,1)S(1)}, u32[]{:S(2)}, u32[]{:S(2)}) collective-permute-start(bf16[64,512]{1,0:T(8,128)(2,1)S(1)} %slice.179), channel_id=1, source_target_pairs={{0,4},{2,6},{4,0},{6,2},{8,12},{10,14},{12,8},{14,10},{16,20},{18,... | collective-permute-start | bytes 196616 | tf_op jit(solution)/shard_map/ppermute | solution.py:26
  40.2 1.3 %collective-permute-start.21 = (bf16[64,1024]{1,0:T(8,128)(2,1)S(1)}, bf16[64,1024]{1,0:T(8,128)(2,1)S(1)}, u32[]{:S(2)}, u32[]{:S(2)}) collective-permute-start(bf16[64,1024]{1,0:T(8,128)(2,1)S(1)} %slice.178), channel_id=1, source_target_pairs={{0,4},{2,6},{4,0},{6,2},{8,12},{10,14},{12,8},{14,10},{16,20},{18,... | collective-permute-start | bytes 393224 | tf_op jit(solution)/shard_map/ppermute | solution.py:26
  41.5 1.5 %collective-permute-done.24 = bf16[64,512]{1,0:T(8,128)(2,1)S(1)} collective-permute-done((bf16[64,512]{1,0:T(8,128)(2,1)S(1)}, bf16[64,512]{1,0:T(8,128)(2,1)S(1)}, u32[]{:S(2)}, u32[]{:S(2)}) %collective-permute-start.24) | collective-permute-done | bytes 65568 | tf_op jit(solution)/shard_map/ppermute | solution.py:26
  43.0 1.2 %collective-permute-start.25 = (bf16[32,512]{1,0:T(8,128)(2,1)S(1)}, bf16[32,512]{1,0:T(8,128)(2,1)S(1)}, u32[]{:S(2)}, u32[]{:S(2)}) collective-permute-start(bf16[32,512]{1,0:T(8,128)(2,1)S(1)} %slice.181), channel_id=1, source_target_pairs={{0,8},{2,10},{4,12},{6,14},{8,0},{10,2},{12,4},{14,6},{16,24},{18,... | collective-permute-start | bytes 98312 | tf_op jit(solution)/shard_map/ppermute | solution.py:26
  44.2 1.5 %collective-permute-done.21 = bf16[64,1024]{1,0:T(8,128)(2,1)S(1)} collective-permute-done((bf16[64,1024]{1,0:T(8,128)(2,1)S(1)}, bf16[64,1024]{1,0:T(8,128)(2,1)S(1)}, u32[]{:S(2)}, u32[]{:S(2)}) %collective-permute-start.21) | collective-permute-done | bytes 131104 | tf_op jit(solution)/shard_map/ppermute | solution.py:26
  45.8 1.2 %collective-permute-start.22 = (bf16[32,1024]{1,0:T(8,128)(2,1)S(1)}, bf16[32,1024]{1,0:T(8,128)(2,1)S(1)}, u32[]{:S(2)}, u32[]{:S(2)}) collective-permute-start(bf16[32,1024]{1,0:T(8,128)(2,1)S(1)} %slice.180), channel_id=1, source_target_pairs={{0,8},{2,10},{4,12},{6,14},{8,0},{10,2},{12,4},{14,6},{16,24},{18,... | collective-permute-start | bytes 196616 | tf_op jit(solution)/shard_map/ppermute | solution.py:26
  47.0 1.3 %collective-permute-start.26 = (bf16[32,512]{1,0:T(8,128)(2,1)S(1)}, bf16[32,512]{1,0:T(8,128)(2,1)S(1)}, u32[]{:S(2)}, u32[]{:S(2)}) collective-permute-start(bf16[32,512]{1,0:T(8,128)(2,1)S(1)} %fusion.6), channel_id=1, source_target_pairs={{0,1},{1,0},{2,3},{3,2},{4,5},{5,4},{6,7},{7,6},{8,9},{9,8},{10,11... | collective-permute-start | bytes 98312 | tf_op jit(solution)/shard_map/ppermute | solution.py:26
  48.3 1.8 %collective-permute-done.22 = bf16[32,1024]{1,0:T(8,128)(2,1)S(1)} collective-permute-done((bf16[32,1024]{1,0:T(8,128)(2,1)S(1)}, bf16[32,1024]{1,0:T(8,128)(2,1)S(1)}, u32[]{:S(2)}, u32[]{:S(2)}) %collective-permute-start.22) | collective-permute-done | bytes 65568 | tf_op jit(solution)/shard_map/ppermute | solution.py:26
  50.1 0.9 %collective-permute-done.26 = bf16[32,512]{1,0:T(8,128)(2,1)S(1)} collective-permute-done((bf16[32,512]{1,0:T(8,128)(2,1)S(1)}, bf16[32,512]{1,0:T(8,128)(2,1)S(1)}, u32[]{:S(2)}, u32[]{:S(2)}) %collective-permute-start.26) | collective-permute-done | bytes 32800 | tf_op jit(solution)/shard_map/ppermute | solution.py:26
  51.0 2.5 %collective-permute-start.27 = (bf16[16,1024]{1,0:T(8,128)(2,1)S(1)}, bf16[16,1024]{1,0:T(8,128)(2,1)S(1)}, u32[]{:S(2)}, u32[]{:S(2)}) collective-permute-start(bf16[16,1024]{1,0:T(8,128)(2,1)S(1)} %fusion.5), channel_id=1, source_target_pairs={{0,16},{2,18},{4,20},{6,22},{8,24},{10,26},{12,28},{14,30},{16,0},... | collective-permute-start | bytes 98312 | tf_op jit(solution)/shard_map/ppermute | solution.py:26
  53.6 2.3 %collective-permute-done.27 = bf16[16,1024]{1,0:T(8,128)(2,1)S(1)} collective-permute-done((bf16[16,1024]{1,0:T(8,128)(2,1)S(1)}, bf16[16,1024]{1,0:T(8,128)(2,1)S(1)}, u32[]{:S(2)}, u32[]{:S(2)}) %collective-permute-start.27) | collective-permute-done | bytes 32800 | tf_op jit(solution)/shard_map/ppermute | solution.py:26
  55.9 0.6 %fusion.11 = (f32[1,16,512]{2,1,0:T(8,128)}, f32[1,16,512]{2,1,0:T(8,128)}) fusion(f32[16,1024]{1,0:T(8,128)S(1)} %fusion.3, f32[1,16,512]{2,1,0:T(8,128)S(1)} %copy-done.4, f32[1,16,512]{2,1,0:T(8,128)S(1)} %copy-done.3), kind=kLoop, calls=%fused_computation.53 | loop fusion | flops 73728 | bytes 196608 | tf_op jit(solution)/shard_map/broadcast_in_dim | solution.py:248
  (66 shorter events, 1.1 us)
Async XLA Ops:
  1.4 7.2 %collective-permute-start = (bf16[16,512]{1,0:T(8,128)(2,1)S(1)}, bf16[16,512]{1,0:T(8,128)(2,1)S(1)}, u32[]{:S(2)}, u32[]{:S(2)}) collective-permute-start(bf16[16,512]{1,0:T(8,128)(2,1)S(1)} %bitcast_convert_fusion), channel_id=1, source_target_pairs={{0,16},{2,18},{4,20},{6,22},{8,24},{10,26},{12,28},{14,30},{16,0},... | collective-permute-start | bytes 49160 | tf_op jit(solution)/shard_map/ppermute | solution.py:26
  7.0 4.0 %collective-permute-start.7 = (bf16[16,1024]{1,0:T(8,128)(2,1)S(1)}, bf16[16,1024]{1,0:T(8,128)(2,1)S(1)}, u32[]{:S(2)}, u32[]{:S(2)}) collective-permute-start(bf16[16,1024]{1,0:T(8,128)(2,1)S(1)} %pad_maximum_fusion.8), channel_id=1, source_target_pairs={{0,1},{1,0},{2,3},{3,2},{4,5},{5,4},{6,7},{7,6},{8,9},{9,8},{10,11... | collective-permute-start | bytes 98312 | tf_op jit(solution)/shard_map/ppermute | solution.py:26
  8.6 3.9 %collective-permute-start.1 = (bf16[32,512]{1,0:T(8,128)(2,1)S(1)}, bf16[32,512]{1,0:T(8,128)(2,1)S(1)}, u32[]{:S(2)}, u32[]{:S(2)}) collective-permute-start(bf16[32,512]{1,0:T(8,128)(2,1)S(1)} %pad_maximum_fusion.7), channel_id=1, source_target_pairs={{0,8},{2,10},{4,12},{6,14},{8,0},{10,2},{12,4},{14,6},{16,24},{18,... | collective-permute-start | bytes 98312 | tf_op jit(solution)/shard_map/ppermute | solution.py:26
  11.0 6.7 %collective-permute-start.8 = (bf16[16,2560]{1,0:T(8,128)(2,1)S(1)}, bf16[16,2560]{1,0:T(8,128)(2,1)S(1)}, u32[]{:S(2)}, u32[]{:S(2)}) collective-permute-start(bf16[16,2560]{1,0:T(8,128)(2,1)S(1)} %pad_maximum_fusion.3), channel_id=1, source_target_pairs={{0,16},{2,18},{4,20},{6,22},{8,24},{10,26},{12,28},{14,30},{16,0},... | collective-permute-start | bytes 245768 | tf_op jit(solution)/shard_map/ppermute | solution.py:26
  12.6 5.3 %copy-start.5 = (s32[256]{0:T(256)S(1)}, s32[256]{0:T(256)}, u32[]{:S(2)}) copy-start(s32[256]{0:T(256)} %param.10) | copy-start | bytes 3076
  12.6 4.3 %collective-permute-start.2 = (bf16[64,512]{1,0:T(8,128)(2,1)S(1)}, bf16[64,512]{1,0:T(8,128)(2,1)S(1)}, u32[]{:S(2)}, u32[]{:S(2)}) collective-permute-start(bf16[64,512]{1,0:T(8,128)(2,1)S(1)} %pad_maximum_fusion.6), channel_id=1, source_target_pairs={{0,4},{2,6},{4,0},{6,2},{8,12},{10,14},{12,8},{14,10},{16,20},{18,... | collective-permute-start | bytes 196616 | tf_op jit(solution)/shard_map/ppermute | solution.py:26
  16.9 6.3 %collective-permute-start.4 = (bf16[128,512]{1,0:T(8,128)(2,1)S(1)}, bf16[128,512]{1,0:T(8,128)(2,1)S(1)}, u32[]{:S(2)}, u32[]{:S(2)}) collective-permute-start(bf16[128,512]{1,0:T(8,128)(2,1)S(1)} %pad_maximum_fusion.1.w0_ref), channel_id=1, source_target_pairs={{0,1},{1,0},{2,3},{3,2},{4,5},{5,4},{6,7},{7,6},{8,9},{9,8},{10,11... | collective-permute-start | bytes 393224 | tf_op jit(solution)/shard_map/ppermute | solution.py:26
  17.8 2.0 %collective-permute-start.3 = (bf16[128,512]{1,0:T(8,128)(2,1)S(1)}, bf16[128,512]{1,0:T(8,128)(2,1)S(1)}, u32[]{:S(2)}, u32[]{:S(2)}) collective-permute-start(bf16[128,512]{1,0:T(8,128)(2,1)S(1)} %pad_maximum_fusion.1.w0_ref), channel_id=1, source_target_pairs={{0,2},{2,0},{4,6},{6,4},{8,10},{10,8},{12,14},{14,12},{16,18},{18,... | collective-permute-start | bytes 393224 | tf_op jit(solution)/shard_map/ppermute | solution.py:26
  18.1 5.2 %collective-permute-start.12 = (bf16[32,1024]{1,0:T(8,128)(2,1)S(1)}, bf16[32,1024]{1,0:T(8,128)(2,1)S(1)}, u32[]{:S(2)}, u32[]{:S(2)}) collective-permute-start(bf16[32,1024]{1,0:T(8,128)(2,1)S(1)} %slice.114), channel_id=1, source_target_pairs={{0,8},{2,10},{4,12},{6,14},{8,0},{10,2},{12,4},{14,6},{16,24},{18,... | collective-permute-start | bytes 196616 | tf_op jit(solution)/shard_map/ppermute | solution.py:26
  21.1 9.0 %collective-permute-start.11 = (bf16[16,8192]{1,0:T(8,128)(2,1)S(1)}, bf16[16,8192]{1,0:T(8,128)(2,1)S(1)}, u32[]{:S(2)}, u32[]{:S(2)}) collective-permute-start(bf16[16,8192]{1,0:T(8,128)(2,1)S(1)} %get-tuple-element.40), channel_id=1, source_target_pairs={{0,1},{1,0},{2,3},{3,2},{4,5},{5,4},{6,7},{7,6},{8,9},{9,8},{10,11... | collective-permute-start | bytes 786440 | tf_op jit(solution)/shard_map/ppermute | solution.py:26
  22.3 5.2 %collective-permute-start.9 = (bf16[32,1536]{1,0:T(8,128)(2,1)S(1)}, bf16[32,1536]{1,0:T(8,128)(2,1)S(1)}, u32[]{:S(2)}, u32[]{:S(2)}) collective-permute-start(bf16[32,1536]{1,0:T(8,128)(2,1)S(1)} %slice.113), channel_id=1, source_target_pairs={{0,8},{2,10},{4,12},{6,14},{8,0},{10,2},{12,4},{14,6},{16,24},{18,... | collective-permute-start | bytes 294920 | tf_op jit(solution)/shard_map/ppermute | solution.py:26
  23.2 2.2 %collective-permute-start.5 = (bf16[128,512]{1,0:T(8,128)(2,1)S(1)}, bf16[128,512]{1,0:T(8,128)(2,1)S(1)}, u32[]{:S(2)}, u32[]{:S(2)}) collective-permute-start(bf16[128,512]{1,0:T(8,128)(2,1)S(1)} %collective-permute-done.4.w0_ref), channel_id=1, source_target_pairs={{0,2},{2,0},{4,6},{6,4},{8,10},{10,8},{12,14},{14,12},{16,18},{18,... | collective-permute-start | bytes 393224 | tf_op jit(solution)/shard_map/ppermute | solution.py:26
  23.3 6.6 %copy-start.1 = (bf16[2,64,8192]{2,1,0:T(8,128)(2,1)S(1)}, bf16[2,64,8192]{2,1,0:T(8,128)(2,1)}, u32[]{:S(2)}) copy-start(bf16[2,64,8192]{2,1,0:T(8,128)(2,1)} %param.12) | copy-start | bytes 6291460
  23.3 5.8 %collective-permute-start.14 = (bf16[64,512]{1,0:T(8,128)(2,1)S(1)}, bf16[64,512]{1,0:T(8,128)(2,1)S(1)}, u32[]{:S(2)}, u32[]{:S(2)}) collective-permute-start(bf16[64,512]{1,0:T(8,128)(2,1)S(1)} %get-tuple-element.62), channel_id=1, source_target_pairs={{0,4},{2,6},{4,0},{6,2},{8,12},{10,14},{12,8},{14,10},{16,20},{18,... | collective-permute-start | bytes 196616 | tf_op jit(solution)/shard_map/ppermute | solution.py:26
  24.9 4.4 %collective-permute-start.13 = (bf16[64,512]{1,0:T(8,128)(2,1)S(1)}, bf16[64,512]{1,0:T(8,128)(2,1)S(1)}, u32[]{:S(2)}, u32[]{:S(2)}) collective-permute-start(bf16[64,512]{1,0:T(8,128)(2,1)S(1)} %get-tuple-element.63), channel_id=1, source_target_pairs={{0,4},{2,6},{4,0},{6,2},{8,12},{10,14},{12,8},{14,10},{16,20},{18,... | collective-permute-start | bytes 196616 | tf_op jit(solution)/shard_map/ppermute | solution.py:26
  26.7 3.3 %copy-start.2 = (bf16[2,64,8192]{2,1,0:T(8,128)(2,1)S(1)}, bf16[2,64,8192]{2,1,0:T(8,128)(2,1)}, u32[]{:S(2)}) copy-start(bf16[2,64,8192]{2,1,0:T(8,128)(2,1)} %param.13) | copy-start | bytes 6291460
  26.7 8.6 %collective-permute-start.6 = (bf16[16,8192]{1,0:T(8,128)(2,1)S(1)}, bf16[16,8192]{1,0:T(8,128)(2,1)S(1)}, u32[]{:S(2)}, u32[]{:S(2)}) collective-permute-start(bf16[16,8192]{1,0:T(8,128)(2,1)S(1)} %get-tuple-element.33), channel_id=1, source_target_pairs={{0,1},{1,0},{2,3},{3,2},{4,5},{5,4},{6,7},{7,6},{8,9},{9,8},{10,11... | collective-permute-start | bytes 786440 | tf_op jit(solution)/shard_map/ppermute | solution.py:26
  27.6 6.5 %collective-permute-start.10 = (bf16[64,1536]{1,0:T(8,128)(2,1)S(1)}, bf16[64,1536]{1,0:T(8,128)(2,1)S(1)}, u32[]{:S(2)}, u32[]{:S(2)}) collective-permute-start(bf16[64,1536]{1,0:T(8,128)(2,1)S(1)} %get-tuple-element.64), channel_id=1, source_target_pairs={{0,4},{2,6},{4,0},{6,2},{8,12},{10,14},{12,8},{14,10},{16,20},{18,... | collective-permute-start | bytes 589832 | tf_op jit(solution)/shard_map/ppermute | solution.py:26
  29.4 1.4 %collective-permute-start.16 = (bf16[128,512]{1,0:T(8,128)(2,1)S(1)}, bf16[128,512]{1,0:T(8,128)(2,1)S(1)}, u32[]{:S(2)}, u32[]{:S(2)}) collective-permute-start(bf16[128,512]{1,0:T(8,128)(2,1)S(1)} %get-tuple-element.58), channel_id=1, source_target_pairs={{0,2},{2,0},{4,6},{6,4},{8,10},{10,8},{12,14},{14,12},{16,18},{18,... | collective-permute-start | bytes 393224 | tf_op jit(solution)/shard_map/ppermute | solution.py:26
  29.4 1.5 %collective-permute-start.15 = (bf16[128,512]{1,0:T(8,128)(2,1)S(1)}, bf16[128,512]{1,0:T(8,128)(2,1)S(1)}, u32[]{:S(2)}, u32[]{:S(2)}) collective-permute-start(bf16[128,512]{1,0:T(8,128)(2,1)S(1)} %get-tuple-element.59), channel_id=1, source_target_pairs={{0,2},{2,0},{4,6},{6,4},{8,10},{10,8},{12,14},{14,12},{16,18},{18,... | collective-permute-start | bytes 393224 | tf_op jit(solution)/shard_map/ppermute | solution.py:26
  31.0 5.2 %copy-start = (bf16[1,2,8,8192]{3,2,1,0:T(8,128)(2,1)S(1)}, bf16[1,2,8,8192]{3,2,1,0:T(8,128)(2,1)}, u32[]{:S(2)}) copy-start(bf16[1,2,8,8192]{3,2,1,0:T(8,128)(2,1)} %param.11) | copy-start | bytes 786436
  34.2 1.4 %collective-permute-start.19 = (bf16[128,512]{1,0:T(8,128)(2,1)S(1)}, bf16[128,512]{1,0:T(8,128)(2,1)S(1)}, u32[]{:S(2)}, u32[]{:S(2)}) collective-permute-start(bf16[128,512]{1,0:T(8,128)(2,1)S(1)} %get-tuple-element.55), channel_id=1, source_target_pairs={{0,2},{2,0},{4,6},{6,4},{8,10},{10,8},{12,14},{14,12},{16,18},{18,... | collective-permute-start | bytes 393224 | tf_op jit(solution)/shard_map/ppermute | solution.py:26
  34.3 1.5 %collective-permute-start.18 = (bf16[128,512]{1,0:T(8,128)(2,1)S(1)}, bf16[128,512]{1,0:T(8,128)(2,1)S(1)}, u32[]{:S(2)}, u32[]{:S(2)}) collective-permute-start(bf16[128,512]{1,0:T(8,128)(2,1)S(1)} %get-tuple-element.56), channel_id=1, source_target_pairs={{0,2},{2,0},{4,6},{6,4},{8,10},{10,8},{12,14},{14,12},{16,18},{18,... | collective-permute-start | bytes 393224 | tf_op jit(solution)/shard_map/ppermute | solution.py:26
  34.8 1.3 %collective-permute-start.17 = (bf16[128,512]{1,0:T(8,128)(2,1)S(1)}, bf16[128,512]{1,0:T(8,128)(2,1)S(1)}, u32[]{:S(2)}, u32[]{:S(2)}) collective-permute-start(bf16[128,512]{1,0:T(8,128)(2,1)S(1)} %get-tuple-element.57), channel_id=1, source_target_pairs={{0,2},{2,0},{4,6},{6,4},{8,10},{10,8},{12,14},{14,12},{16,18},{18,... | collective-permute-start | bytes 393224 | tf_op jit(solution)/shard_map/ppermute | solution.py:26
  34.8 3.6 %collective-permute-start.23 = (bf16[128,512]{1,0:T(8,128)(2,1)S(1)}, bf16[128,512]{1,0:T(8,128)(2,1)S(1)}, u32[]{:S(2)}, u32[]{:S(2)}) collective-permute-start(bf16[128,512]{1,0:T(8,128)(2,1)S(1)} %get-tuple-element.53), channel_id=1, source_target_pairs={{0,2},{2,0},{4,6},{6,4},{8,10},{10,8},{12,14},{14,12},{16,18},{18,... | collective-permute-start | bytes 393224 | tf_op jit(solution)/shard_map/ppermute | solution.py:26
  38.2 17.7 %copy-start.3 = (f32[1,16,512]{2,1,0:T(8,128)S(1)}, f32[1,16,512]{2,1,0:T(8,128)}, u32[]{:S(2)}) copy-start(f32[1,16,512]{2,1,0:T(8,128)} %param.7) | copy-start | bytes 98308
  38.2 17.7 %copy-start.4 = (f32[1,16,512]{2,1,0:T(8,128)S(1)}, f32[1,16,512]{2,1,0:T(8,128)}, u32[]{:S(2)}) copy-start(f32[1,16,512]{2,1,0:T(8,128)} %param.9) | copy-start | bytes 98308
  38.2 1.9 %collective-permute-start.20 = (bf16[128,1024]{1,0:T(8,128)(2,1)S(1)}, bf16[128,1024]{1,0:T(8,128)(2,1)S(1)}, u32[]{:S(2)}, u32[]{:S(2)}) collective-permute-start(bf16[128,1024]{1,0:T(8,128)(2,1)S(1)} %get-tuple-element.52), channel_id=1, source_target_pairs={{0,2},{2,0},{4,6},{6,4},{8,10},{10,8},{12,14},{14,12},{16,18},{18,... | collective-permute-start | bytes 786440 | tf_op jit(solution)/shard_map/ppermute | solution.py:26
  38.5 4.5 %collective-permute-start.24 = (bf16[64,512]{1,0:T(8,128)(2,1)S(1)}, bf16[64,512]{1,0:T(8,128)(2,1)S(1)}, u32[]{:S(2)}, u32[]{:S(2)}) collective-permute-start(bf16[64,512]{1,0:T(8,128)(2,1)S(1)} %slice.179), channel_id=1, source_target_pairs={{0,4},{2,6},{4,0},{6,2},{8,12},{10,14},{12,8},{14,10},{16,20},{18,... | collective-permute-start | bytes 196616 | tf_op jit(solution)/shard_map/ppermute | solution.py:26
  40.2 5.5 %collective-permute-start.21 = (bf16[64,1024]{1,0:T(8,128)(2,1)S(1)}, bf16[64,1024]{1,0:T(8,128)(2,1)S(1)}, u32[]{:S(2)}, u32[]{:S(2)}) collective-permute-start(bf16[64,1024]{1,0:T(8,128)(2,1)S(1)} %slice.178), channel_id=1, source_target_pairs={{0,4},{2,6},{4,0},{6,2},{8,12},{10,14},{12,8},{14,10},{16,20},{18,... | collective-permute-start | bytes 393224 | tf_op jit(solution)/shard_map/ppermute | solution.py:26
  43.0 4.0 %collective-permute-start.25 = (bf16[32,512]{1,0:T(8,128)(2,1)S(1)}, bf16[32,512]{1,0:T(8,128)(2,1)S(1)}, u32[]{:S(2)}, u32[]{:S(2)}) collective-permute-start(bf16[32,512]{1,0:T(8,128)(2,1)S(1)} %slice.181), channel_id=1, source_target_pairs={{0,8},{2,10},{4,12},{6,14},{8,0},{10,2},{12,4},{14,6},{16,24},{18,... | collective-permute-start | bytes 98312 | tf_op jit(solution)/shard_map/ppermute | solution.py:26
  45.8 4.3 %collective-permute-start.22 = (bf16[32,1024]{1,0:T(8,128)(2,1)S(1)}, bf16[32,1024]{1,0:T(8,128)(2,1)S(1)}, u32[]{:S(2)}, u32[]{:S(2)}) collective-permute-start(bf16[32,1024]{1,0:T(8,128)(2,1)S(1)} %slice.180), channel_id=1, source_target_pairs={{0,8},{2,10},{4,12},{6,14},{8,0},{10,2},{12,4},{14,6},{16,24},{18,... | collective-permute-start | bytes 196616 | tf_op jit(solution)/shard_map/ppermute | solution.py:26
  47.0 4.0 %collective-permute-start.26 = (bf16[32,512]{1,0:T(8,128)(2,1)S(1)}, bf16[32,512]{1,0:T(8,128)(2,1)S(1)}, u32[]{:S(2)}, u32[]{:S(2)}) collective-permute-start(bf16[32,512]{1,0:T(8,128)(2,1)S(1)} %fusion.6), channel_id=1, source_target_pairs={{0,1},{1,0},{2,3},{3,2},{4,5},{5,4},{6,7},{7,6},{8,9},{9,8},{10,11... | collective-permute-start | bytes 98312 | tf_op jit(solution)/shard_map/ppermute | solution.py:26
  51.0 4.9 %collective-permute-start.27 = (bf16[16,1024]{1,0:T(8,128)(2,1)S(1)}, bf16[16,1024]{1,0:T(8,128)(2,1)S(1)}, u32[]{:S(2)}, u32[]{:S(2)}) collective-permute-start(bf16[16,1024]{1,0:T(8,128)(2,1)S(1)} %fusion.5), channel_id=1, source_target_pairs={{0,16},{2,18},{4,20},{6,22},{8,24},{10,26},{12,28},{14,30},{16,0},... | collective-permute-start | bytes 98312 | tf_op jit(solution)/shard_map/ppermute | solution.py:26

commit v17 on v16

--- a/solution.py
+++ b/solution.py
@@ -149,9 +149,8 @@
     shape = jax.ShapeDtypeStruct
 
     near_w = master[0].astype(BF)
-    spans = jnp.concatenate([after(moment[0], near_w), variance[0]], axis=1)
+    spans = jnp.pad(after(moment[0], near_w), ((0, 0), (0, segment))) + jnp.pad(variance[0], ((0, 0), (segment, 0)))
     near_a = spans.astype(BF)
-    low = (spans[:, :segment] - lax.reduce_precision(spans[:, :segment], 8, 7)).astype(BF)
     steps = []
     for mask in far:
         near_w = jnp.concatenate([near_w, swap(near_w, "dp", mask)], axis=0)
@@ -159,6 +158,8 @@
     blocks_a = [near_a]
     for mask in reversed(mp_bits):
         blocks_a = blocks_a + [swap(b, "mp", mask) for b in blocks_a]
+    exact = after(moment[0], steps[0])
+    low = (exact - lax.reduce_precision(exact, 8, 7)).astype(BF)
     all_a = after(jnp.concatenate([near_a, low] + blocks_a[1:], axis=1), steps[0])
 
     slot = after(flat_slot, steps[-1])

time: 56.9 us -> 57.2 us (level)
  waiting for transfers between devices: 14.1 us -> 14.8 us
    ppermute x28, waiting for transfers between devices: 14.1 us -> 14.8 us  [swap(): return lax.ppermute(x, axis, [(i, i ^ mask) for i in range(n)])]
    another operation x2 -> x1, other arithmetic: 0.77 us -> 0.01 us
    convert_element_type x1 -> x2, other arithmetic: 0.84 us -> 1.54 us  [the longest x1 0.78 us: per_device(): near_a = spans.astype(BF)]
where the time goes in v17:
time: 57.2 us; the launch traced here: 56.9 us
  starting transfers between devices  29.2 us (51%)
  waiting for transfers between devices  14.8 us (26%)
  Pallas kernels  6.33 us (11%)
  other arithmetic  3.32 us (6%)
  local copies, waits for them, and re-layouts  2.24 us (4%)
  between operations  0.97 us (2%)
    ppermute x28, starting transfers between devices, swap(): return lax.ppermute(x, axis, [(i, i ^ mask) for i in range(n)])  29.2 us
    ppermute x28, waiting for transfers between devices, swap(): return lax.ppermute(x, axis, [(i, i ^ mask) for i in range(n)])  14.8 us
    pallas_call x4, Pallas kernels, call(): pl.pallas_call(kernel, out_shape=out_shape, in_specs=[pl.BlockSpec(memory...  6.33 us
    squeeze x3, local copies, waits for them, and re-layouts, tokens_of(): x[step]  1.81 us
  transfers between devices with their start and end apart: 28, of which 15 were waited for; matrix products, arithmetic and copies ran while one was open for 7% of the time, Pallas kernels for 11%

profile of v17, /device:TPU:0, one launch (start us, length us, event | category | flops | bytes accessed | tf_op | source)
XLA Modules:
  0.0 56.9 jit_solution(4457799996017676101)
XLA Ops:
  0.6 0.8 %bitcast_convert_fusion = bf16[16,512]{1,0:T(8,128)(2,1)S(1)} fusion(f32[1,16,512]{2,1,0:T(8,128)} %param.7), kind=kLoop, calls=%fused_computation.42 | loop fusion | flops 8192 | bytes 49152 | tf_op jit(solution)/shard_map/convert_element_type | solution.py:151
  1.4 4.0 %collective-permute-start = (bf16[16,512]{1,0:T(8,128)(2,1)S(1)}, bf16[16,512]{1,0:T(8,128)(2,1)S(1)}, u32[]{:S(2)}, u32[]{:S(2)}) collective-permute-start(bf16[16,512]{1,0:T(8,128)(2,1)S(1)} %bitcast_convert_fusion), channel_id=1, source_target_pairs={{0,16},{2,18},{4,20},{6,22},{8,24},{10,26},{12,28},{14,30},{16,0},... | collective-permute-start | bytes 49160 | tf_op jit(solution)/shard_map/ppermute | solution.py:26
  5.4 0.8 %add_convert_fusion = bf16[16,1024]{1,0:T(8,128)(2,1)S(1)} fusion(f32[16,512]{1,0:T(8,128)} %bitcast.26, f32[16,512]{1,0:T(8,128)} %bitcast.24), kind=kLoop, calls=%fused_computation.35 | loop fusion | flops 32768 | bytes 98304 | tf_op jit(solution)/shard_map/convert_element_type | solution.py:153
  6.2 1.5 %collective-permute-start.7 = (bf16[16,1024]{1,0:T(8,128)(2,1)S(1)}, bf16[16,1024]{1,0:T(8,128)(2,1)S(1)}, u32[]{:S(2)}, u32[]{:S(2)}) collective-permute-start(bf16[16,1024]{1,0:T(8,128)(2,1)S(1)} %add_convert_fusion), channel_id=1, source_target_pairs={{0,1},{1,0},{2,3},{3,2},{4,5},{5,4},{6,7},{7,6},{8,9},{9,8},{10,11... | collective-permute-start | bytes 98312 | tf_op jit(solution)/shard_map/ppermute | solution.py:26
  7.7 1.6 %collective-permute-start.1 = (bf16[32,512]{1,0:T(8,128)(2,1)S(1)}, bf16[32,512]{1,0:T(8,128)(2,1)S(1)}, u32[]{:S(2)}, u32[]{:S(2)}) collective-permute-start(bf16[32,512]{1,0:T(8,128)(2,1)S(1)} %pad_maximum_fusion.7), channel_id=1, source_target_pairs={{0,8},{2,10},{4,12},{6,14},{8,0},{10,2},{12,4},{14,6},{16,24},{18,... | collective-permute-start | bytes 98312 | tf_op jit(solution)/shard_map/ppermute | solution.py:26
  9.3 0.8 %fusion.7 = bf16[16,512]{1,0:T(8,128)(2,1)S(1)} fusion(f32[16,512]{1,0:T(8,128)} %bitcast.25), kind=kLoop, calls=%fused_computation.37 | loop fusion | flops 24576 | bytes 49152 | tf_op jit(solution)/shard_map/convert_element_type | solution.py:162
  10.1 2.4 %collective-permute-start.8 = (bf16[16,2560]{1,0:T(8,128)(2,1)S(1)}, bf16[16,2560]{1,0:T(8,128)(2,1)S(1)}, u32[]{:S(2)}, u32[]{:S(2)}) collective-permute-start(bf16[16,2560]{1,0:T(8,128)(2,1)S(1)} %pad_maximum_fusion.3), channel_id=1, source_target_pairs={{0,16},{2,18},{4,20},{6,22},{8,24},{10,26},{12,28},{14,30},{16,0},... | collective-permute-start | bytes 245768 | tf_op jit(solution)/shard_map/ppermute | solution.py:26
  12.6 1.6 %collective-permute-start.2 = (bf16[64,512]{1,0:T(8,128)(2,1)S(1)}, bf16[64,512]{1,0:T(8,128)(2,1)S(1)}, u32[]{:S(2)}, u32[]{:S(2)}) collective-permute-start(bf16[64,512]{1,0:T(8,128)(2,1)S(1)} %pad_maximum_fusion.6), channel_id=1, source_target_pairs={{0,4},{2,6},{4,0},{6,2},{8,12},{10,14},{12,8},{14,10},{16,20},{18,... | collective-permute-start | bytes 196616 | tf_op jit(solution)/shard_map/ppermute | solution.py:26
  14.2 1.7 %slice_bitcast_fusion.2 = (bf16[64,8192]{1,0:T(8,128)(2,1)S(1)}, bf16[64,8192]{1,0:T(8,128)(2,1)S(1)}) fusion(bf16[2,64,8192]{2,1,0:T(8,128)(2,1)} %param.13, bf16[2,64,8192]{2,1,0:T(8,128)(2,1)} %param.12), kind=kLoop, calls=%fused_computation.2 | loop fusion | bytes 4194304 | tf_op jit(solution)/shard_map/squeeze | solution.py:124
  15.8 1.1 %collective-permute-done.2 = bf16[64,512]{1,0:T(8,128)(2,1)S(1)} collective-permute-done((bf16[64,512]{1,0:T(8,128)(2,1)S(1)}, bf16[64,512]{1,0:T(8,128)(2,1)S(1)}, u32[]{:S(2)}, u32[]{:S(2)}) %collective-permute-start.2) | collective-permute-done | bytes 65568 | tf_op jit(solution)/shard_map/ppermute | solution.py:26
  16.9 1.6 %collective-permute-start.4 = (bf16[128,512]{1,0:T(8,128)(2,1)S(1)}, bf16[128,512]{1,0:T(8,128)(2,1)S(1)}, u32[]{:S(2)}, u32[]{:S(2)}) collective-permute-start(bf16[128,512]{1,0:T(8,128)(2,1)S(1)} %pad_maximum_fusion.1.w0_ref), channel_id=1, source_target_pairs={{0,1},{1,0},{2,3},{3,2},{4,5},{5,4},{6,7},{7,6},{8,9},{9,8},{10,11... | collective-permute-start | bytes 393224 | tf_op jit(solution)/shard_map/ppermute | solution.py:26
  18.8 0.4 collective-permute-start.12
  19.3 0.1 fusion.1
  19.4 0.5 collective-permute-done.3.w1_ref
  19.9 1.3 %shard_map.94 = (bf16[16,8192]{1,0:T(8,128)(2,1)S(1)}, f32[16,8192]{1,0:T(8,128)S(1)}, bf16[16,8192]{1,0:T(8,128)(2,1)S(1)}) custom-call(bf16[256,256]{1,0:T(8,128)(2,1)S(1)} %get-tuple-element.73.place_ref, bf16[128,512]{1,0:T(8,128)(2,1)S(1)} %pad_maximum_fusion.1.w0_ref, bf16[128,512]{1,0:T(8,128)(2,1)S(1)} %collective-permute-done.3.w1_ref, ...), custom_call_target="tpu_custom_call" | custom-call | flops 1 | bytes 1 | tf_op jit(solution)/shard_map/pallas_call | solution.py:128
  21.1 0.6 collective-permute-start.11
  21.7 1.1 %collective-permute-start.9 = (bf16[32,1536]{1,0:T(8,128)(2,1)S(1)}, bf16[32,1536]{1,0:T(8,128)(2,1)S(1)}, u32[]{:S(2)}, u32[]{:S(2)}) collective-permute-start(bf16[32,1536]{1,0:T(8,128)(2,1)S(1)} %slice.113), channel_id=1, source_target_pairs={{0,8},{2,10},{4,12},{6,14},{8,0},{10,2},{12,4},{14,6},{16,24},{18,... | collective-permute-start | bytes 294920 | tf_op jit(solution)/shard_map/ppermute | solution.py:26
  22.9 0.5 collective-permute-done.12
  23.4 1.6 %collective-permute-start.14 = (bf16[64,512]{1,0:T(8,128)(2,1)S(1)}, bf16[64,512]{1,0:T(8,128)(2,1)S(1)}, u32[]{:S(2)}, u32[]{:S(2)}) collective-permute-start(bf16[64,512]{1,0:T(8,128)(2,1)S(1)} %get-tuple-element.64), channel_id=1, source_target_pairs={{0,4},{2,6},{4,0},{6,2},{8,12},{10,14},{12,8},{14,10},{16,20},{18,... | collective-permute-start | bytes 196616 | tf_op jit(solution)/shard_map/ppermute | solution.py:26
  24.9 0.5 collective-permute-start.13
  25.5 1.3 %shard_map.95 = (bf16[16,8192]{1,0:T(8,128)(2,1)S(1)}, f32[16,8192]{1,0:T(8,128)S(1)}, bf16[16,8192]{1,0:T(8,128)(2,1)S(1)}) custom-call(bf16[256,256]{1,0:T(8,128)(2,1)S(1)} %get-tuple-element.73.place_ref, bf16[128,512]{1,0:T(8,128)(2,1)S(1)} %collective-permute-done.4.w0_ref, bf16[128,512]{1,0:T(8,128)(2,1)S(1)} %collective-permute-done.5.w1_ref, ...), custom_call_target="tpu_custom_call" | custom-call | flops 1 | bytes 1 | tf_op jit(solution)/shard_map/pallas_call | solution.py:128
  26.8 1.1 %collective-permute-start.6 = (bf16[16,8192]{1,0:T(8,128)(2,1)S(1)}, bf16[16,8192]{1,0:T(8,128)(2,1)S(1)}, u32[]{:S(2)}, u32[]{:S(2)}) collective-permute-start(bf16[16,8192]{1,0:T(8,128)(2,1)S(1)} %get-tuple-element.34), channel_id=1, source_target_pairs={{0,1},{1,0},{2,3},{3,2},{4,5},{5,4},{6,7},{7,6},{8,9},{9,8},{10,11... | collective-permute-start | bytes 786440 | tf_op jit(solution)/shard_map/ppermute | solution.py:26
  27.9 1.6 %collective-permute-start.10 = (bf16[64,1536]{1,0:T(8,128)(2,1)S(1)}, bf16[64,1536]{1,0:T(8,128)(2,1)S(1)}, u32[]{:S(2)}, u32[]{:S(2)}) collective-permute-start(bf16[64,1536]{1,0:T(8,128)(2,1)S(1)} %get-tuple-element.66), channel_id=1, source_target_pairs={{0,4},{2,6},{4,0},{6,2},{8,12},{10,14},{12,8},{14,10},{16,20},{18,... | collective-permute-start | bytes 589832 | tf_op jit(solution)/shard_map/ppermute | solution.py:26
  29.6 0.5 collective-permute-start.15
  30.3 0.7 %collective-permute-done.16.rest_1_ = bf16[128,512]{1,0:T(8,128)(2,1)S(1)} collective-permute-done((bf16[128,512]{1,0:T(8,128)(2,1)S(1)}, bf16[128,512]{1,0:T(8,128)(2,1)S(1)}, u32[]{:S(2)}, u32[]{:S(2)}) %collective-permute-start.16) | collective-permute-done | bytes 131104 | tf_op jit(solution)/shard_map/ppermute | solution.py:26
  30.9 0.2 collective-permute-done.15.rest_0_
  31.1 1.7 %shard_map.96 = (bf16[128,512]{1,0:T(8,128)(2,1)S(1)}, bf16[128,512]{1,0:T(8,128)(2,1)S(1)}) custom-call(bf16[256,256]{1,0:T(8,128)(2,1)S(1)} %get-tuple-element.73.place_ref, bf16[256,256]{1,0:T(8,128)(2,1)S(1)} %get-tuple-element.72.back_ref, f32[16,8192]{1,0:T(8,128)S(1)} %get-tuple-element.45.part_ref, ...), custom_call_target="tpu_custom_call" | custom-call | flops 1 | bytes 1 | tf_op jit(solution)/shard_map/pallas_call | solution.py:128
  32.9 1.5 %collective-permute-done.10 = bf16[64,1536]{1,0:T(8,128)(2,1)S(1)} collective-permute-done((bf16[64,1536]{1,0:T(8,128)(2,1)S(1)}, bf16[64,1536]{1,0:T(8,128)(2,1)S(1)}, u32[]{:S(2)}, u32[]{:S(2)}) %collective-permute-start.10) | collective-permute-done | bytes 196640 | tf_op jit(solution)/shard_map/ppermute | solution.py:26
  34.6 0.5 collective-permute-start.18
  35.1 0.4 collective-permute-start.23
  35.6 0.3 collective-permute-done.19.rest_2_
  35.9 0.2 collective-permute-done.18.rest_1_
  36.1 0.3 collective-permute-done.17.rest_0_
  36.4 2.1 %shard_map.97 = (bf16[128,1024]{1,0:T(8,128)(2,1)S(1)}, bf16[128,1024]{1,0:T(8,128)(2,1)S(1)}, bf16[16,8192]{1,0:T(8,128)(2,1)}) custom-call(bf16[256,256]{1,0:T(8,128)(2,1)S(1)} %get-tuple-element.73.place_ref, bf16[256,256]{1,0:T(8,128)(2,1)S(1)} %get-tuple-element.72.back_ref, f32[16,8192]{1,0:T(8,128)S(1)} %get-tuple-element.33.part_ref, ...), custom_call_target="tpu_custom_call" | custom-call | flops 1 | bytes 1 | tf_op jit(solution)/shard_map/pallas_call | solution.py:128
  38.5 0.3 collective-permute-start.20
  38.8 1.6 %collective-permute-start.24 = (bf16[64,512]{1,0:T(8,128)(2,1)S(1)}, bf16[64,512]{1,0:T(8,128)(2,1)S(1)}, u32[]{:S(2)}, u32[]{:S(2)}) collective-permute-start(bf16[64,512]{1,0:T(8,128)(2,1)S(1)} %slice.179), channel_id=1, source_target_pairs={{0,4},{2,6},{4,0},{6,2},{8,12},{10,14},{12,8},{14,10},{16,20},{18,... | collective-permute-start | bytes 196616 | tf_op jit(solution)/shard_map/ppermute | solution.py:26
  40.5 1.3 %collective-permute-start.21 = (bf16[64,1024]{1,0:T(8,128)(2,1)S(1)}, bf16[64,1024]{1,0:T(8,128)(2,1)S(1)}, u32[]{:S(2)}, u32[]{:S(2)}) collective-permute-start(bf16[64,1024]{1,0:T(8,128)(2,1)S(1)} %slice.178), channel_id=1, source_target_pairs={{0,4},{2,6},{4,0},{6,2},{8,12},{10,14},{12,8},{14,10},{16,20},{18,... | collective-permute-start | bytes 393224 | tf_op jit(solution)/shard_map/ppermute | solution.py:26
  41.8 1.5 %collective-permute-done.24 = bf16[64,512]{1,0:T(8,128)(2,1)S(1)} collective-permute-done((bf16[64,512]{1,0:T(8,128)(2,1)S(1)}, bf16[64,512]{1,0:T(8,128)(2,1)S(1)}, u32[]{:S(2)}, u32[]{:S(2)}) %collective-permute-start.24) | collective-permute-done | bytes 65568 | tf_op jit(solution)/shard_map/ppermute | solution.py:26
  43.3 1.0 %collective-permute-start.25 = (bf16[32,512]{1,0:T(8,128)(2,1)S(1)}, bf16[32,512]{1,0:T(8,128)(2,1)S(1)}, u32[]{:S(2)}, u32[]{:S(2)}) collective-permute-start(bf16[32,512]{1,0:T(8,128)(2,1)S(1)} %slice.181), channel_id=1, source_target_pairs={{0,8},{2,10},{4,12},{6,14},{8,0},{10,2},{12,4},{14,6},{16,24},{18,... | collective-permute-start | bytes 98312 | tf_op jit(solution)/shard_map/ppermute | solution.py:26
  44.3 1.7 %collective-permute-done.21 = bf16[64,1024]{1,0:T(8,128)(2,1)S(1)} collective-permute-done((bf16[64,1024]{1,0:T(8,128)(2,1)S(1)}, bf16[64,1024]{1,0:T(8,128)(2,1)S(1)}, u32[]{:S(2)}, u32[]{:S(2)}) %collective-permute-start.21) | collective-permute-done | bytes 131104 | tf_op jit(solution)/shard_map/ppermute | solution.py:26
  46.1 1.0 %collective-permute-start.22 = (bf16[32,1024]{1,0:T(8,128)(2,1)S(1)}, bf16[32,1024]{1,0:T(8,128)(2,1)S(1)}, u32[]{:S(2)}, u32[]{:S(2)}) collective-permute-start(bf16[32,1024]{1,0:T(8,128)(2,1)S(1)} %slice.180), channel_id=1, source_target_pairs={{0,8},{2,10},{4,12},{6,14},{8,0},{10,2},{12,4},{14,6},{16,24},{18,... | collective-permute-start | bytes 196616 | tf_op jit(solution)/shard_map/ppermute | solution.py:26
  47.0 0.3 collective-permute-done.25
  47.3 0.5 collective-permute-start.26
  47.9 2.5 %collective-permute-done.22 = bf16[32,1024]{1,0:T(8,128)(2,1)S(1)} collective-permute-done((bf16[32,1024]{1,0:T(8,128)(2,1)S(1)}, bf16[32,1024]{1,0:T(8,128)(2,1)S(1)}, u32[]{:S(2)}, u32[]{:S(2)}) %collective-permute-start.22) | collective-permute-done | bytes 65568 | tf_op jit(solution)/shard_map/ppermute | solution.py:26
  50.4 0.9 %collective-permute-done.26 = bf16[32,512]{1,0:T(8,128)(2,1)S(1)} collective-permute-done((bf16[32,512]{1,0:T(8,128)(2,1)S(1)}, bf16[32,512]{1,0:T(8,128)(2,1)S(1)}, u32[]{:S(2)}, u32[]{:S(2)}) %collective-permute-start.26) | collective-permute-done | bytes 32800 | tf_op jit(solution)/shard_map/ppermute | solution.py:26
  51.3 2.4 %collective-permute-start.27 = (bf16[16,1024]{1,0:T(8,128)(2,1)S(1)}, bf16[16,1024]{1,0:T(8,128)(2,1)S(1)}, u32[]{:S(2)}, u32[]{:S(2)}) collective-permute-start(bf16[16,1024]{1,0:T(8,128)(2,1)S(1)} %fusion.5), channel_id=1, source_target_pairs={{0,16},{2,18},{4,20},{6,22},{8,24},{10,26},{12,28},{14,30},{16,0},... | collective-permute-start | bytes 98312 | tf_op jit(solution)/shard_map/ppermute | solution.py:26
  53.7 2.5 %collective-permute-done.27 = bf16[16,1024]{1,0:T(8,128)(2,1)S(1)} collective-permute-done((bf16[16,1024]{1,0:T(8,128)(2,1)S(1)}, bf16[16,1024]{1,0:T(8,128)(2,1)S(1)}, u32[]{:S(2)}, u32[]{:S(2)}) %collective-permute-start.27) | collective-permute-done | bytes 32800 | tf_op jit(solution)/shard_map/ppermute | solution.py:26
  56.2 0.6 %fusion.10 = (f32[1,16,512]{2,1,0:T(8,128)}, f32[1,16,512]{2,1,0:T(8,128)}) fusion(f32[16,1024]{1,0:T(8,128)S(1)} %fusion.3, f32[1,16,512]{2,1,0:T(8,128)S(1)} %copy-done.3, f32[1,16,512]{2,1,0:T(8,128)S(1)} %copy-done.4), kind=kLoop, calls=%fused_computation.51 | loop fusion | flops 73728 | bytes 196608 | tf_op jit(solution)/shard_map/broadcast_in_dim | solution.py:249
  (65 shorter events, 1.1 us)
Async XLA Ops:
  1.4 6.3 %collective-permute-start = (bf16[16,512]{1,0:T(8,128)(2,1)S(1)}, bf16[16,512]{1,0:T(8,128)(2,1)S(1)}, u32[]{:S(2)}, u32[]{:S(2)}) collective-permute-start(bf16[16,512]{1,0:T(8,128)(2,1)S(1)} %bitcast_convert_fusion), channel_id=1, source_target_pairs={{0,16},{2,18},{4,20},{6,22},{8,24},{10,26},{12,28},{14,30},{16,0},... | collective-permute-start | bytes 49160 | tf_op jit(solution)/shard_map/ppermute | solution.py:26
  6.2 3.9 %collective-permute-start.7 = (bf16[16,1024]{1,0:T(8,128)(2,1)S(1)}, bf16[16,1024]{1,0:T(8,128)(2,1)S(1)}, u32[]{:S(2)}, u32[]{:S(2)}) collective-permute-start(bf16[16,1024]{1,0:T(8,128)(2,1)S(1)} %add_convert_fusion), channel_id=1, source_target_pairs={{0,1},{1,0},{2,3},{3,2},{4,5},{5,4},{6,7},{7,6},{8,9},{9,8},{10,11... | collective-permute-start | bytes 98312 | tf_op jit(solution)/shard_map/ppermute | solution.py:26
  7.7 4.8 %collective-permute-start.1 = (bf16[32,512]{1,0:T(8,128)(2,1)S(1)}, bf16[32,512]{1,0:T(8,128)(2,1)S(1)}, u32[]{:S(2)}, u32[]{:S(2)}) collective-permute-start(bf16[32,512]{1,0:T(8,128)(2,1)S(1)} %pad_maximum_fusion.7), channel_id=1, source_target_pairs={{0,8},{2,10},{4,12},{6,14},{8,0},{10,2},{12,4},{14,6},{16,24},{18,... | collective-permute-start | bytes 98312 | tf_op jit(solution)/shard_map/ppermute | solution.py:26
  10.1 8.4 %collective-permute-start.8 = (bf16[16,2560]{1,0:T(8,128)(2,1)S(1)}, bf16[16,2560]{1,0:T(8,128)(2,1)S(1)}, u32[]{:S(2)}, u32[]{:S(2)}) collective-permute-start(bf16[16,2560]{1,0:T(8,128)(2,1)S(1)} %pad_maximum_fusion.3), channel_id=1, source_target_pairs={{0,16},{2,18},{4,20},{6,22},{8,24},{10,26},{12,28},{14,30},{16,0},... | collective-permute-start | bytes 245768 | tf_op jit(solution)/shard_map/ppermute | solution.py:26
  12.6 6.0 %copy-start.5 = (s32[256]{0:T(256)S(1)}, s32[256]{0:T(256)}, u32[]{:S(2)}) copy-start(s32[256]{0:T(256)} %param.10) | copy-start | bytes 3076
  12.6 4.3 %collective-permute-start.2 = (bf16[64,512]{1,0:T(8,128)(2,1)S(1)}, bf16[64,512]{1,0:T(8,128)(2,1)S(1)}, u32[]{:S(2)}, u32[]{:S(2)}) collective-permute-start(bf16[64,512]{1,0:T(8,128)(2,1)S(1)} %pad_maximum_fusion.6), channel_id=1, source_target_pairs={{0,4},{2,6},{4,0},{6,2},{8,12},{10,14},{12,8},{14,10},{16,20},{18,... | collective-permute-start | bytes 196616 | tf_op jit(solution)/shard_map/ppermute | solution.py:26
  16.9 5.9 %collective-permute-start.4 = (bf16[128,512]{1,0:T(8,128)(2,1)S(1)}, bf16[128,512]{1,0:T(8,128)(2,1)S(1)}, u32[]{:S(2)}, u32[]{:S(2)}) collective-permute-start(bf16[128,512]{1,0:T(8,128)(2,1)S(1)} %pad_maximum_fusion.1.w0_ref), channel_id=1, source_target_pairs={{0,1},{1,0},{2,3},{3,2},{4,5},{5,4},{6,7},{7,6},{8,9},{9,8},{10,11... | collective-permute-start | bytes 393224 | tf_op jit(solution)/shard_map/ppermute | solution.py:26
  18.5 1.3 %collective-permute-start.3 = (bf16[128,512]{1,0:T(8,128)(2,1)S(1)}, bf16[128,512]{1,0:T(8,128)(2,1)S(1)}, u32[]{:S(2)}, u32[]{:S(2)}) collective-permute-start(bf16[128,512]{1,0:T(8,128)(2,1)S(1)} %pad_maximum_fusion.1.w0_ref), channel_id=1, source_target_pairs={{0,2},{2,0},{4,6},{6,4},{8,10},{10,8},{12,14},{14,12},{16,18},{18,... | collective-permute-start | bytes 393224 | tf_op jit(solution)/shard_map/ppermute | solution.py:26
  18.8 4.5 %collective-permute-start.12 = (bf16[32,1024]{1,0:T(8,128)(2,1)S(1)}, bf16[32,1024]{1,0:T(8,128)(2,1)S(1)}, u32[]{:S(2)}, u32[]{:S(2)}) collective-permute-start(bf16[32,1024]{1,0:T(8,128)(2,1)S(1)} %slice.114), channel_id=1, source_target_pairs={{0,8},{2,10},{4,12},{6,14},{8,0},{10,2},{12,4},{14,6},{16,24},{18,... | collective-permute-start | bytes 196616 | tf_op jit(solution)/shard_map/ppermute | solution.py:26
  21.1 9.1 %collective-permute-start.11 = (bf16[16,8192]{1,0:T(8,128)(2,1)S(1)}, bf16[16,8192]{1,0:T(8,128)(2,1)S(1)}, u32[]{:S(2)}, u32[]{:S(2)}) collective-permute-start(bf16[16,8192]{1,0:T(8,128)(2,1)S(1)} %get-tuple-element.42), channel_id=1, source_target_pairs={{0,1},{1,0},{2,3},{3,2},{4,5},{5,4},{6,7},{7,6},{8,9},{9,8},{10,11... | collective-permute-start | bytes 786440 | tf_op jit(solution)/shard_map/ppermute | solution.py:26
  21.7 6.2 %collective-permute-start.9 = (bf16[32,1536]{1,0:T(8,128)(2,1)S(1)}, bf16[32,1536]{1,0:T(8,128)(2,1)S(1)}, u32[]{:S(2)}, u32[]{:S(2)}) collective-permute-start(bf16[32,1536]{1,0:T(8,128)(2,1)S(1)} %slice.113), channel_id=1, source_target_pairs={{0,8},{2,10},{4,12},{6,14},{8,0},{10,2},{12,4},{14,6},{16,24},{18,... | collective-permute-start | bytes 294920 | tf_op jit(solution)/shard_map/ppermute | solution.py:26
  22.8 2.6 %collective-permute-start.5 = (bf16[128,512]{1,0:T(8,128)(2,1)S(1)}, bf16[128,512]{1,0:T(8,128)(2,1)S(1)}, u32[]{:S(2)}, u32[]{:S(2)}) collective-permute-start(bf16[128,512]{1,0:T(8,128)(2,1)S(1)} %collective-permute-done.4.w0_ref), channel_id=1, source_target_pairs={{0,2},{2,0},{4,6},{6,4},{8,10},{10,8},{12,14},{14,12},{16,18},{18,... | collective-permute-start | bytes 393224 | tf_op jit(solution)/shard_map/ppermute | solution.py:26
  23.4 6.7 %copy-start.1 = (bf16[2,64,8192]{2,1,0:T(8,128)(2,1)S(1)}, bf16[2,64,8192]{2,1,0:T(8,128)(2,1)}, u32[]{:S(2)}) copy-start(bf16[2,64,8192]{2,1,0:T(8,128)(2,1)} %param.12) | copy-start | bytes 6291460
  23.4 6.1 %collective-permute-start.14 = (bf16[64,512]{1,0:T(8,128)(2,1)S(1)}, bf16[64,512]{1,0:T(8,128)(2,1)S(1)}, u32[]{:S(2)}, u32[]{:S(2)}) collective-permute-start(bf16[64,512]{1,0:T(8,128)(2,1)S(1)} %get-tuple-element.64), channel_id=1, source_target_pairs={{0,4},{2,6},{4,0},{6,2},{8,12},{10,14},{12,8},{14,10},{16,20},{18,... | collective-permute-start | bytes 196616 | tf_op jit(solution)/shard_map/ppermute | solution.py:26
  24.9 4.5 %collective-permute-start.13 = (bf16[64,512]{1,0:T(8,128)(2,1)S(1)}, bf16[64,512]{1,0:T(8,128)(2,1)S(1)}, u32[]{:S(2)}, u32[]{:S(2)}) collective-permute-start(bf16[64,512]{1,0:T(8,128)(2,1)S(1)} %get-tuple-element.65), channel_id=1, source_target_pairs={{0,4},{2,6},{4,0},{6,2},{8,12},{10,14},{12,8},{14,10},{16,20},{18,... | collective-permute-start | bytes 196616 | tf_op jit(solution)/shard_map/ppermute | solution.py:26
  26.7 3.4 %copy-start.2 = (bf16[2,64,8192]{2,1,0:T(8,128)(2,1)S(1)}, bf16[2,64,8192]{2,1,0:T(8,128)(2,1)}, u32[]{:S(2)}) copy-start(bf16[2,64,8192]{2,1,0:T(8,128)(2,1)} %param.13) | copy-start | bytes 6291460
  26.8 8.8 %collective-permute-start.6 = (bf16[16,8192]{1,0:T(8,128)(2,1)S(1)}, bf16[16,8192]{1,0:T(8,128)(2,1)S(1)}, u32[]{:S(2)}, u32[]{:S(2)}) collective-permute-start(bf16[16,8192]{1,0:T(8,128)(2,1)S(1)} %get-tuple-element.34), channel_id=1, source_target_pairs={{0,1},{1,0},{2,3},{3,2},{4,5},{5,4},{6,7},{7,6},{8,9},{9,8},{10,11... | collective-permute-start | bytes 786440 | tf_op jit(solution)/shard_map/ppermute | solution.py:26
  27.9 6.5 %collective-permute-start.10 = (bf16[64,1536]{1,0:T(8,128)(2,1)S(1)}, bf16[64,1536]{1,0:T(8,128)(2,1)S(1)}, u32[]{:S(2)}, u32[]{:S(2)}) collective-permute-start(bf16[64,1536]{1,0:T(8,128)(2,1)S(1)} %get-tuple-element.66), channel_id=1, source_target_pairs={{0,4},{2,6},{4,0},{6,2},{8,12},{10,14},{12,8},{14,10},{16,20},{18,... | collective-permute-start | bytes 589832 | tf_op jit(solution)/shard_map/ppermute | solution.py:26
  29.5 1.4 %collective-permute-start.16 = (bf16[128,512]{1,0:T(8,128)(2,1)S(1)}, bf16[128,512]{1,0:T(8,128)(2,1)S(1)}, u32[]{:S(2)}, u32[]{:S(2)}) collective-permute-start(bf16[128,512]{1,0:T(8,128)(2,1)S(1)} %get-tuple-element.60), channel_id=1, source_target_pairs={{0,2},{2,0},{4,6},{6,4},{8,10},{10,8},{12,14},{14,12},{16,18},{18,... | collective-permute-start | bytes 393224 | tf_op jit(solution)/shard_map/ppermute | solution.py:26
  29.6 1.5 %collective-permute-start.15 = (bf16[128,512]{1,0:T(8,128)(2,1)S(1)}, bf16[128,512]{1,0:T(8,128)(2,1)S(1)}, u32[]{:S(2)}, u32[]{:S(2)}) collective-permute-start(bf16[128,512]{1,0:T(8,128)(2,1)S(1)} %get-tuple-element.61), channel_id=1, source_target_pairs={{0,2},{2,0},{4,6},{6,4},{8,10},{10,8},{12,14},{14,12},{16,18},{18,... | collective-permute-start | bytes 393224 | tf_op jit(solution)/shard_map/ppermute | solution.py:26
  31.1 5.3 %copy-start = (bf16[1,2,8,8192]{3,2,1,0:T(8,128)(2,1)S(1)}, bf16[1,2,8,8192]{3,2,1,0:T(8,128)(2,1)}, u32[]{:S(2)}) copy-start(bf16[1,2,8,8192]{3,2,1,0:T(8,128)(2,1)} %param.11) | copy-start | bytes 786436
  34.5 1.4 %collective-permute-start.19 = (bf16[128,512]{1,0:T(8,128)(2,1)S(1)}, bf16[128,512]{1,0:T(8,128)(2,1)S(1)}, u32[]{:S(2)}, u32[]{:S(2)}) collective-permute-start(bf16[128,512]{1,0:T(8,128)(2,1)S(1)} %get-tuple-element.57), channel_id=1, source_target_pairs={{0,2},{2,0},{4,6},{6,4},{8,10},{10,8},{12,14},{14,12},{16,18},{18,... | collective-permute-start | bytes 393224 | tf_op jit(solution)/shard_map/ppermute | solution.py:26
  34.6 1.5 %collective-permute-start.18 = (bf16[128,512]{1,0:T(8,128)(2,1)S(1)}, bf16[128,512]{1,0:T(8,128)(2,1)S(1)}, u32[]{:S(2)}, u32[]{:S(2)}) collective-permute-start(bf16[128,512]{1,0:T(8,128)(2,1)S(1)} %get-tuple-element.58), channel_id=1, source_target_pairs={{0,2},{2,0},{4,6},{6,4},{8,10},{10,8},{12,14},{14,12},{16,18},{18,... | collective-permute-start | bytes 393224 | tf_op jit(solution)/shard_map/ppermute | solution.py:26
  35.0 1.3 %collective-permute-start.17 = (bf16[128,512]{1,0:T(8,128)(2,1)S(1)}, bf16[128,512]{1,0:T(8,128)(2,1)S(1)}, u32[]{:S(2)}, u32[]{:S(2)}) collective-permute-start(bf16[128,512]{1,0:T(8,128)(2,1)S(1)} %get-tuple-element.59), channel_id=1, source_target_pairs={{0,2},{2,0},{4,6},{6,4},{8,10},{10,8},{12,14},{14,12},{16,18},{18,... | collective-permute-start | bytes 393224 | tf_op jit(solution)/shard_map/ppermute | solution.py:26
  35.1 3.6 %collective-permute-start.23 = (bf16[128,512]{1,0:T(8,128)(2,1)S(1)}, bf16[128,512]{1,0:T(8,128)(2,1)S(1)}, u32[]{:S(2)}, u32[]{:S(2)}) collective-permute-start(bf16[128,512]{1,0:T(8,128)(2,1)S(1)} %get-tuple-element.55), channel_id=1, source_target_pairs={{0,2},{2,0},{4,6},{6,4},{8,10},{10,8},{12,14},{14,12},{16,18},{18,... | collective-permute-start | bytes 393224 | tf_op jit(solution)/shard_map/ppermute | solution.py:26
  38.5 17.7 %copy-start.3 = (f32[1,16,512]{2,1,0:T(8,128)S(1)}, f32[1,16,512]{2,1,0:T(8,128)}, u32[]{:S(2)}) copy-start(f32[1,16,512]{2,1,0:T(8,128)} %param.9) | copy-start | bytes 98308
  38.5 17.7 %copy-start.4 = (f32[1,16,512]{2,1,0:T(8,128)S(1)}, f32[1,16,512]{2,1,0:T(8,128)}, u32[]{:S(2)}) copy-start(f32[1,16,512]{2,1,0:T(8,128)} %param.7) | copy-start | bytes 98308
  38.5 1.9 %collective-permute-start.20 = (bf16[128,1024]{1,0:T(8,128)(2,1)S(1)}, bf16[128,1024]{1,0:T(8,128)(2,1)S(1)}, u32[]{:S(2)}, u32[]{:S(2)}) collective-permute-start(bf16[128,1024]{1,0:T(8,128)(2,1)S(1)} %get-tuple-element.54), channel_id=1, source_target_pairs={{0,2},{2,0},{4,6},{6,4},{8,10},{10,8},{12,14},{14,12},{16,18},{18,... | collective-permute-start | bytes 786440 | tf_op jit(solution)/shard_map/ppermute | solution.py:26
  38.8 4.5 %collective-permute-start.24 = (bf16[64,512]{1,0:T(8,128)(2,1)S(1)}, bf16[64,512]{1,0:T(8,128)(2,1)S(1)}, u32[]{:S(2)}, u32[]{:S(2)}) collective-permute-start(bf16[64,512]{1,0:T(8,128)(2,1)S(1)} %slice.179), channel_id=1, source_target_pairs={{0,4},{2,6},{4,0},{6,2},{8,12},{10,14},{12,8},{14,10},{16,20},{18,... | collective-permute-start | bytes 196616 | tf_op jit(solution)/shard_map/ppermute | solution.py:26
  40.5 5.5 %collective-permute-start.21 = (bf16[64,1024]{1,0:T(8,128)(2,1)S(1)}, bf16[64,1024]{1,0:T(8,128)(2,1)S(1)}, u32[]{:S(2)}, u32[]{:S(2)}) collective-permute-start(bf16[64,1024]{1,0:T(8,128)(2,1)S(1)} %slice.178), channel_id=1, source_target_pairs={{0,4},{2,6},{4,0},{6,2},{8,12},{10,14},{12,8},{14,10},{16,20},{18,... | collective-permute-start | bytes 393224 | tf_op jit(solution)/shard_map/ppermute | solution.py:26
  43.3 4.0 %collective-permute-start.25 = (bf16[32,512]{1,0:T(8,128)(2,1)S(1)}, bf16[32,512]{1,0:T(8,128)(2,1)S(1)}, u32[]{:S(2)}, u32[]{:S(2)}) collective-permute-start(bf16[32,512]{1,0:T(8,128)(2,1)S(1)} %slice.181), channel_id=1, source_target_pairs={{0,8},{2,10},{4,12},{6,14},{8,0},{10,2},{12,4},{14,6},{16,24},{18,... | collective-permute-start | bytes 98312 | tf_op jit(solution)/shard_map/ppermute | solution.py:26
  46.1 4.3 %collective-permute-start.22 = (bf16[32,1024]{1,0:T(8,128)(2,1)S(1)}, bf16[32,1024]{1,0:T(8,128)(2,1)S(1)}, u32[]{:S(2)}, u32[]{:S(2)}) collective-permute-start(bf16[32,1024]{1,0:T(8,128)(2,1)S(1)} %slice.180), channel_id=1, source_target_pairs={{0,8},{2,10},{4,12},{6,14},{8,0},{10,2},{12,4},{14,6},{16,24},{18,... | collective-permute-start | bytes 196616 | tf_op jit(solution)/shard_map/ppermute | solution.py:26
  47.3 4.0 %collective-permute-start.26 = (bf16[32,512]{1,0:T(8,128)(2,1)S(1)}, bf16[32,512]{1,0:T(8,128)(2,1)S(1)}, u32[]{:S(2)}, u32[]{:S(2)}) collective-permute-start(bf16[32,512]{1,0:T(8,128)(2,1)S(1)} %fusion.6), channel_id=1, source_target_pairs={{0,1},{1,0},{2,3},{3,2},{4,5},{5,4},{6,7},{7,6},{8,9},{9,8},{10,11... | collective-permute-start | bytes 98312 | tf_op jit(solution)/shard_map/ppermute | solution.py:26
  51.3 4.9 %collective-permute-start.27 = (bf16[16,1024]{1,0:T(8,128)(2,1)S(1)}, bf16[16,1024]{1,0:T(8,128)(2,1)S(1)}, u32[]{:S(2)}, u32[]{:S(2)}) collective-permute-start(bf16[16,1024]{1,0:T(8,128)(2,1)S(1)} %fusion.5), channel_id=1, source_target_pairs={{0,16},{2,18},{4,20},{6,22},{8,24},{10,26},{12,28},{14,30},{16,0},... | collective-permute-start | bytes 98312 | tf_op jit(solution)/shard_map/ppermute | solution.py:26
